TPU v7x, 32 devices: a whole 2x2x4 slice. The times are simulated.
32 devices in a mesh: groups: 2 (over x), tile: 16 (over z, y, core).
Axes of the slice: x: 2, y: 2, z: 4, core: 2. Of those that a mesh axis runs over, the one named last changes fastest.
Arguments:
- t2_tiles: bfloat16 [3072, 128, 128], P(('groups', 'tile')), parts along dimension 0, may hold values from -6 to 6
- t2_row: int32 [3072], P(('groups', 'tile')), parts along dimension 0, may hold values from 0 to 15
- t2_col: int32 [3072], P(('groups', 'tile')), parts along dimension 0, may hold values from 0 to 63, as said below
- integrals: bfloat16 [128, 128, 1024], P(('groups', 'tile')), parts along dimension 0, may hold values from -0.21875 to 0.21875
Outputs:
- ladder: bfloat16 [512, 128, 1024], P(('groups', 'tile')), parts along dimension 0
There are 2 independent parts, one for each index of `groups`. A program takes and returns all parts, laid end to end along the dimension named above; each array names one. Nothing has to cross between parts.
Inputs may be any that keep to these rules, and one draw needn't show every extreme that they name: `t2_col`: on each device the 96 tiles name exactly 32 distinct integral blocks, each by 3 tiles of distinct row blocks; integral block k belongs to device k // 4; each device names at most 2 blocks of any one device, and exactly 2 of some device.
All inputs are finite; a program needn't handle non-finite values.
Results may differ from a plain program's by a relative error of at most 0.001.
Values may be sent and summed in bfloat16 or wider, within the bound.
No kernel may reach another device: no remote copies, remote signals or barrier semaphores. Data moves between devices by JAX's collectives and lax.ppermute only.
A program may use at most 128 MiB of HBM per device.

v0:
```python
import jax
import jax.numpy as jnp
from jax import lax
from jax.sharding import PartitionSpec as P

W = 32
PPD = 16
REUSE = 3


def swapped(value, axis, bit):
    mask = 2**bit
    pairs = [(source, source ^ mask) for source in range(lax.axis_size(axis))]
    return lax.ppermute(value, axis, pairs)


def flip_pairs(block, width):
    shape = block.shape
    return block.reshape(shape[0], shape[1], width, width).swapaxes(2, 3).reshape(shape)


def per_device(t2_tiles, t2_row, t2_col, integrals):
    peer_count = lax.axis_size("tile")
    local_blocks = integrals.shape[0]
    block_total = peer_count * local_blocks
    tile_count = t2_tiles.shape[0]
    row_width = t2_tiles.shape[1]
    pair_width = t2_tiles.shape[2]
    column_width = integrals.shape[2]
    need_count = tile_count // REUSE
    slot_width = (need_count + peer_count - 1) // peer_count
    block_ids = jnp.arange(block_total, dtype=jnp.int32)
    matches = t2_col[:, None] == block_ids[None, :]
    wanted = jnp.any(matches, axis=0).reshape(peer_count, local_blocks)
    rank_grid = jnp.cumsum(wanted.astype(jnp.int32), axis=1) - 1
    slot_ids = jnp.arange(slot_width, dtype=jnp.int32)
    local_ids = jnp.arange(local_blocks, dtype=jnp.int32)
    hits = wanted[:, None, :] & (rank_grid[:, None, :] == slot_ids[None, :, None])
    request = jnp.sum(jnp.where(hits, local_ids[None, None, :] + 1, 0), axis=2) - 1
    asked = lax.all_to_all(request, "tile", split_axis=0, concat_axis=0, tiled=True)
    picked = jnp.take(integrals, jnp.maximum(asked, 0), axis=0)
    replies = jnp.where(asked[:, :, None, None] >= 0, picked, jnp.zeros((), jnp.bfloat16))
    fetched = lax.all_to_all(replies, "tile", split_axis=0, concat_axis=0, tiled=True).reshape(
        peer_count * slot_width, pair_width, column_width
    )
    owner_of = t2_col // local_blocks
    tile_rank = jnp.sum(jnp.where(matches, rank_grid.reshape(-1)[None, :], 0), axis=1)
    tile_slot = owner_of * slot_width + tile_rank
    group = 8
    turns = tile_count // group
    grouped = (
        t2_tiles.reshape(turns, group, row_width, pair_width),
        tile_slot.reshape(turns, group),
        t2_row.reshape(turns, group),
    )

    def accumulate(running, inputs):
        tile_group, slot_group, row_group = inputs
        blocks = jnp.take(fetched, slot_group, axis=0)
        product = jnp.einsum("tij,tjc->tic", tile_group, blocks, preferred_element_type=jnp.float32)
        return (running.at[row_group].add(product), None)

    initial = jnp.zeros((PPD, row_width, column_width), jnp.float32)
    residual, unused = lax.scan(accumulate, initial, grouped)
    bit_number = peer_count.bit_length() - 2
    partner = swapped(residual, "tile", bit_number)
    return (residual + flip_pairs(partner, W)).astype(jnp.bfloat16)


def solution(mesh):
    in_specs = (
        P(("groups", "tile"), None, None),
        P(("groups", "tile")),
        P(("groups", "tile")),
        P(("groups", "tile"), None, None),
    )
    out_specs = P(("groups", "tile"), None, None)
    return jax.shard_map(
        per_device, mesh=mesh, in_specs=in_specs, out_specs=out_specs, check_vma=False
    )
```

profile of v0, /device:TPU:0, one launch (start us, length us, event | category | flops | bytes accessed | tf_op | source)
XLA Modules:
  0.0 822.2 jit_solution(1358663824167233185)
XLA Ops:
  0.0 0.9 fusion.12
  0.9 0.1 reshape.143
  1.0 0.1 copy.36
  1.1 0.2 reduce_window_sum.11
  1.2 0.1 copy.37
  1.3 0.1 select_reduce_fusion.1
  1.4 0.1 copy.38
  1.5 13.6 %all_to_all.11 = s32[16,1,2]{2,1,0:T(1,128)S(1)} all-to-all(s32[16,1,2]{2,1,0:T(1,128)S(1)} %copy.38), channel_id=1, replica_groups=mesh['groups'=2,'tile'=16] {'tile'}, dimensions={0} | all-to-all | bytes 256 | tf_op jit(solution)/shard_map/all_to_all | solution.py:40
  15.2 0.1 copy.40
  15.3 0.1 copy.42
  15.4 0.1 copy.43
  15.5 0.1 reshape.158
  15.6 5.0 gather_fusion.1
  20.6 7.6 select_select_fusion
  28.2 5.1 all-to-all-start.1
  33.2 0.1 sub.20
  33.3 0.1 select_reduce_fusion
  33.4 0.1 reshape.144
  33.5 0.1 reshape.141
  33.6 150.1 %all-to-all-done.1 = bf16[16,2,128,1024]{3,2,1,0:T(8,128)(2,1)} async-done(((bf16[16,2,128,1024]{3,2,1,0:T(8,128)(2,1)}), bf16[16,2,128,1024]{3,2,1,0:T(8,128)(2,1)}, u32[]{:S(2)}, u32[]{:S(2)}) %all-to-all-start.1) | async-done | bytes 8388640 | tf_op jit(solution)/shard_map/all_to_all | solution.py:43
  183.7 4.3 broadcast_in_dim.66
  187.9 206.7 %while.10 = (s32[]{:T(128)}, f32[16,128,1024]{2,1,0:T(8,128)}, s32[12,8]{1,0:T(8,128)S(1)}, bf16[12,8,128,128]{3,2,1,0:T(8,128)(2,1)}, s32[12,8]{1,0:T(8,128)S(1)}, /*index=5*/bf16[32,128,1024]{2,1,0:T(8,128)(2,1)}, s32[]{:T(128)}) while((s32[]{:T(128)}, f32[16,128,1024]{2,1,0:T(8,128)}, s32[12,8]{1,0:T(8,128)S(1)}, ...), condition=%wide.region_6.7_spmd, body=%wide.region_4.6_spmd.sunk | while | flops 270533728 | bytes 23335280 | solution.py:64
  188.0 4.1 gather_fusion
  192.1 3.7 fusion.21
  195.8 9.3 %scatter_fusion = f32[16,128,1024]{2,1,0:T(8,128)} fusion(f32[16,128,1024]{2,1,0:T(8,128)} %get-tuple-element.103, s32[8]{0:T(128)S(1)} %get-tuple-element.93, f32[8,128,1024]{2,1,0:T(8,128)} %fusion.21), kind=kCustom, calls=%fused_computation.2.clone.1 | custom fusion | flops 1048576 | bytes 12582944 | tf_op jit(solution)/shard_map/while/body/eval_jaxpr/scatter-add | solution.py:61
  205.1 4.1 gather_fusion
  209.2 3.7 fusion.21
  212.9 9.4 %scatter_fusion = f32[16,128,1024]{2,1,0:T(8,128)} fusion(f32[16,128,1024]{2,1,0:T(8,128)} %get-tuple-element.103, s32[8]{0:T(128)S(1)} %get-tuple-element.93, f32[8,128,1024]{2,1,0:T(8,128)} %fusion.21), kind=kCustom, calls=%fused_computation.2.clone.1 | custom fusion | flops 1048576 | bytes 12582944 | tf_op jit(solution)/shard_map/while/body/eval_jaxpr/scatter-add | solution.py:61
  222.4 4.1 gather_fusion
  226.5 3.7 fusion.21
  230.2 9.5 %scatter_fusion = f32[16,128,1024]{2,1,0:T(8,128)} fusion(f32[16,128,1024]{2,1,0:T(8,128)} %get-tuple-element.103, s32[8]{0:T(128)S(1)} %get-tuple-element.93, f32[8,128,1024]{2,1,0:T(8,128)} %fusion.21), kind=kCustom, calls=%fused_computation.2.clone.1 | custom fusion | flops 1048576 | bytes 12582944 | tf_op jit(solution)/shard_map/while/body/eval_jaxpr/scatter-add | solution.py:61
  239.7 4.1 gather_fusion
  243.8 3.7 fusion.21
  247.5 9.3 %scatter_fusion = f32[16,128,1024]{2,1,0:T(8,128)} fusion(f32[16,128,1024]{2,1,0:T(8,128)} %get-tuple-element.103, s32[8]{0:T(128)S(1)} %get-tuple-element.93, f32[8,128,1024]{2,1,0:T(8,128)} %fusion.21), kind=kCustom, calls=%fused_computation.2.clone.1 | custom fusion | flops 1048576 | bytes 12582944 | tf_op jit(solution)/shard_map/while/body/eval_jaxpr/scatter-add | solution.py:61
  256.9 4.1 gather_fusion
  261.0 3.7 fusion.21
  264.7 9.5 %scatter_fusion = f32[16,128,1024]{2,1,0:T(8,128)} fusion(f32[16,128,1024]{2,1,0:T(8,128)} %get-tuple-element.103, s32[8]{0:T(128)S(1)} %get-tuple-element.93, f32[8,128,1024]{2,1,0:T(8,128)} %fusion.21), kind=kCustom, calls=%fused_computation.2.clone.1 | custom fusion | flops 1048576 | bytes 12582944 | tf_op jit(solution)/shard_map/while/body/eval_jaxpr/scatter-add | solution.py:61
  274.3 4.1 gather_fusion
  278.4 3.7 fusion.21
  282.1 9.3 %scatter_fusion = f32[16,128,1024]{2,1,0:T(8,128)} fusion(f32[16,128,1024]{2,1,0:T(8,128)} %get-tuple-element.103, s32[8]{0:T(128)S(1)} %get-tuple-element.93, f32[8,128,1024]{2,1,0:T(8,128)} %fusion.21), kind=kCustom, calls=%fused_computation.2.clone.1 | custom fusion | flops 1048576 | bytes 12582944 | tf_op jit(solution)/shard_map/while/body/eval_jaxpr/scatter-add | solution.py:61
  291.5 4.1 gather_fusion
  295.6 3.7 fusion.21
  299.3 9.2 %scatter_fusion = f32[16,128,1024]{2,1,0:T(8,128)} fusion(f32[16,128,1024]{2,1,0:T(8,128)} %get-tuple-element.103, s32[8]{0:T(128)S(1)} %get-tuple-element.93, f32[8,128,1024]{2,1,0:T(8,128)} %fusion.21), kind=kCustom, calls=%fused_computation.2.clone.1 | custom fusion | flops 1048576 | bytes 12582944 | tf_op jit(solution)/shard_map/while/body/eval_jaxpr/scatter-add | solution.py:61
  308.5 4.1 gather_fusion
  312.6 3.7 fusion.21
  316.3 9.3 %scatter_fusion = f32[16,128,1024]{2,1,0:T(8,128)} fusion(f32[16,128,1024]{2,1,0:T(8,128)} %get-tuple-element.103, s32[8]{0:T(128)S(1)} %get-tuple-element.93, f32[8,128,1024]{2,1,0:T(8,128)} %fusion.21), kind=kCustom, calls=%fused_computation.2.clone.1 | custom fusion | flops 1048576 | bytes 12582944 | tf_op jit(solution)/shard_map/while/body/eval_jaxpr/scatter-add | solution.py:61
  325.7 4.1 gather_fusion
  329.8 3.7 fusion.21
  333.5 9.5 %scatter_fusion = f32[16,128,1024]{2,1,0:T(8,128)} fusion(f32[16,128,1024]{2,1,0:T(8,128)} %get-tuple-element.103, s32[8]{0:T(128)S(1)} %get-tuple-element.93, f32[8,128,1024]{2,1,0:T(8,128)} %fusion.21), kind=kCustom, calls=%fused_computation.2.clone.1 | custom fusion | flops 1048576 | bytes 12582944 | tf_op jit(solution)/shard_map/while/body/eval_jaxpr/scatter-add | solution.py:61
  343.0 4.1 gather_fusion
  347.1 3.7 fusion.21
  350.8 9.5 %scatter_fusion = f32[16,128,1024]{2,1,0:T(8,128)} fusion(f32[16,128,1024]{2,1,0:T(8,128)} %get-tuple-element.103, s32[8]{0:T(128)S(1)} %get-tuple-element.93, f32[8,128,1024]{2,1,0:T(8,128)} %fusion.21), kind=kCustom, calls=%fused_computation.2.clone.1 | custom fusion | flops 1048576 | bytes 12582944 | tf_op jit(solution)/shard_map/while/body/eval_jaxpr/scatter-add | solution.py:61
  360.4 4.1 gather_fusion
  364.5 3.7 fusion.21
  368.2 9.3 %scatter_fusion = f32[16,128,1024]{2,1,0:T(8,128)} fusion(f32[16,128,1024]{2,1,0:T(8,128)} %get-tuple-element.103, s32[8]{0:T(128)S(1)} %get-tuple-element.93, f32[8,128,1024]{2,1,0:T(8,128)} %fusion.21), kind=kCustom, calls=%fused_computation.2.clone.1 | custom fusion | flops 1048576 | bytes 12582944 | tf_op jit(solution)/shard_map/while/body/eval_jaxpr/scatter-add | solution.py:61
  377.5 4.1 gather_fusion
  381.6 3.7 fusion.21
  385.4 9.3 %scatter_fusion = f32[16,128,1024]{2,1,0:T(8,128)} fusion(f32[16,128,1024]{2,1,0:T(8,128)} %get-tuple-element.103, s32[8]{0:T(128)S(1)} %get-tuple-element.93, f32[8,128,1024]{2,1,0:T(8,128)} %fusion.21), kind=kCustom, calls=%fused_computation.2.clone.1 | custom fusion | flops 1048576 | bytes 12582944 | tf_op jit(solution)/shard_map/while/body/eval_jaxpr/scatter-add | solution.py:61
  394.6 9.3 %copy.46 = f32[16,128,1024]{1,2,0:T(8,128)} copy(f32[16,128,1024]{2,1,0:T(8,128)} %get-tuple-element.37) | data formatting | bytes 16777216 | tf_op jit(solution)/shard_map/while | solution.py:64
  403.9 33.5 %collective-permute-start = (f32[16,128,1024]{1,2,0:T(8,128)}, f32[16,128,1024]{1,2,0:T(8,128)S(1)}, u32[]{:S(2)}, u32[]{:S(2)}) collective-permute-start(f32[16,128,1024]{1,2,0:T(8,128)} %copy.46), channel_id=1, source_target_pairs={{0,8},{1,9},{2,10},{3,11},{4,12},{5,13},{6,14},{7,15},{8,0},{9,1},... | collective-permute-start | bytes 25165832 | tf_op jit(solution)/shard_map/ppermute | solution.py:14
  437.4 360.0 %collective-permute-done = f32[16,128,1024]{1,2,0:T(8,128)S(1)} collective-permute-done((f32[16,128,1024]{1,2,0:T(8,128)}, f32[16,128,1024]{1,2,0:T(8,128)S(1)}, u32[]{:S(2)}, u32[]{:S(2)}) %collective-permute-start) | collective-permute-done | bytes 8388640 | tf_op jit(solution)/shard_map/ppermute | solution.py:14
  797.4 9.7 %copy.45 = f32[16,128,32,32]{1,3,2,0:T(8,128)} copy(f32[16,128,32,32]{1,2,3,0:T(8,128)S(1)} %bitcast.44) | data formatting | bytes 16777216 | tf_op jit(solution)/shard_map/transpose | solution.py:19
  807.1 8.7 %fusion.11 = bf16[16,128,1024]{1,2,0:T(8,128)(2,1)} fusion(f32[16,128,1024]{1,2,0:T(8,128)} %copy.46, f32[16,128,32,32]{1,3,2,0:T(8,128)} %copy.45), kind=kLoop, calls=%fused_computation.22 | loop fusion | flops 4194304 | bytes 20971520 | tf_op jit(solution)/shard_map/convert_element_type | solution.py:67
  815.8 6.4 copy.47
  (53 shorter events, 0.5 us)
Async XLA Ops:
  0.0 15.6 %copy-start = (bf16[4,128,1024]{2,1,0:T(8,128)(2,1)S(1)}, bf16[4,128,1024]{2,1,0:T(8,128)(2,1)}, u32[]{:S(2)}) copy-start(bf16[4,128,1024]{2,1,0:T(8,128)(2,1)} %param.9) | copy-start | bytes 3145732
  28.2 5.2 copy-start.3
  28.2 5.3 copy-start.2
  28.2 155.5 %all-to-all-start.1 = ((bf16[16,2,128,1024]{3,2,1,0:T(8,128)(2,1)}), bf16[16,2,128,1024]{3,2,1,0:T(8,128)(2,1)}, u32[]{:S(2)}, u32[]{:S(2)}) async-start(bf16[16,2,128,1024]{3,2,1,0:T(8,128)(2,1)} %select_select_fusion), calls=%async_computation.1 | async-start | bytes 16777216 | tf_op jit(solution)/shard_map/all_to_all | solution.py:43
  403.9 393.5 %collective-permute-start = (f32[16,128,1024]{1,2,0:T(8,128)}, f32[16,128,1024]{1,2,0:T(8,128)S(1)}, u32[]{:S(2)}, u32[]{:S(2)}) collective-permute-start(f32[16,128,1024]{1,2,0:T(8,128)} %copy.46), channel_id=1, source_target_pairs={{0,8},{1,9},{2,10},{3,11},{4,12},{5,13},{6,14},{7,15},{8,0},{9,1},... | collective-permute-start | bytes 25165832 | tf_op jit(solution)/shard_map/ppermute | solution.py:14
  807.1 15.1 %copy-start.1 = (bf16[4,128,1024]{2,1,0:T(8,128)(2,1)S(1)}, bf16[4,128,1024]{2,1,0:T(8,128)(2,1)}, u32[]{:S(2)}) copy-start(bf16[4,128,1024]{2,1,0:T(8,128)(2,1)} %param.9) | copy-start | bytes 3145732
where the time goes:
time: 823 us; the launch traced here: 822 us
  waiting for transfers between devices  510 us (62%)
  other arithmetic  130 us (16%)
  local copies, waits for them, and re-layouts  84.4 us (10%)
  matrix products  44.8 us (5%)
  starting transfers between devices  38.5 us (5%)
  blocking collectives  13.6 us (2%)
    ppermute x1, waiting for transfers between devices, swapped(): return lax.ppermute(value, axis, pairs)  360 us
    all_to_all x1, waiting for transfers between devices, per_device(): lax.all_to_all(replies, 'tile', split_axis=0, concat_axis=0, tiled=True)  150 us
    scatter-add x12, other arithmetic, accumulate(): return (running.at[row_group].add(product), None)  112 us
    gather x12, local copies, waits for them, and re-layouts, accumulate(): blocks = jnp.take(fetched, slot_group, axis=0)  48.8 us
    dot_general x12, matrix products, accumulate(): jnp.einsum('tij,tjc->tic', tile_group, blocks, preferred_element_type=jnp...  44.8 us
    ppermute x1, starting transfers between devices, swapped(): return lax.ppermute(value, axis, pairs)  33.5 us
  transfers between devices with their start and end apart: 2, of which 2 were waited for; matrix products, arithmetic and copies ran while one was open for 0% of the time, Pallas kernels for 0%

commit v1 on v0

v1 whole, which is shorter than its diff:
```python
import functools

import jax
import jax.numpy as jnp
from jax import lax
from jax.experimental import pallas as pl
from jax.experimental.pallas import tpu as pltpu
from jax.sharding import PartitionSpec as P

W = 32
PPD = 16
REUSE = 3
VMEM_LIMIT = 56 * 1024 * 1024


def sorted_order(t2_col):
    count = t2_col.shape[0]
    ids = jnp.arange(count, dtype=jnp.int32)
    before = (t2_col[None, :] < t2_col[:, None]) | (
        (t2_col[None, :] == t2_col[:, None]) & (ids[None, :] < ids[:, None])
    )
    rank = jnp.sum(before.astype(jnp.int32), axis=1)
    return jnp.sum(jnp.where(rank[None, :] == ids[:, None], ids[None, :], 0), axis=1)


def flip_matrix(width):
    columns = jnp.arange(width * width, dtype=jnp.int32)
    source = (columns % width) * width + columns // width
    return (columns[:, None] == source[None, :]).astype(jnp.bfloat16)


def own_kernel(rows, own_ids, far_ids, tiles_ref, block_ref, far_ref, perm_ref, sum_ref, flip_ref):
    step = pl.program_id(0)

    @pl.when(step == 0)
    def _():
        sum_ref[...] = jnp.zeros_like(sum_ref)

    reuse, height, depth = tiles_ref.shape
    product = jnp.dot(
        tiles_ref[...].reshape(reuse * height, depth), block_ref[0], preferred_element_type=jnp.float32
    )
    for part in range(reuse):
        row = rows[step * reuse + part]
        sum_ref[row] += product[part * height : (part + 1) * height]
    flip_ref[0] = jnp.dot(far_ref[0], perm_ref[...], preferred_element_type=jnp.float32).astype(jnp.bfloat16)


def own_part(rows, own_ids, far_ids, tiles, blocks, perm):
    need = own_ids.shape[0]
    height, depth = tiles.shape[1:]
    width = blocks.shape[2]
    return pl.pallas_call(
        own_kernel,
        grid_spec=pltpu.PrefetchScalarGridSpec(
            num_scalar_prefetch=3,
            grid=(need,),
            in_specs=[
                pl.BlockSpec((REUSE, height, depth), lambda j, rows, own, far: (j, 0, 0)),
                pl.BlockSpec((1, depth, width), lambda j, rows, own, far: (own[j], 0, 0)),
                pl.BlockSpec((1, depth, width), lambda j, rows, own, far: (far[j], 0, 0)),
                pl.BlockSpec((width, width), lambda j, rows, own, far: (0, 0)),
            ],
            out_specs=[
                pl.BlockSpec((PPD, height, width), lambda j, rows, own, far: (0, 0, 0)),
                pl.BlockSpec((1, depth, width), lambda j, rows, own, far: (j, 0, 0)),
            ],
        ),
        out_shape=[
            jax.ShapeDtypeStruct((PPD, height, width), jnp.float32),
            jax.ShapeDtypeStruct((need, depth, width), jnp.bfloat16),
        ],
        compiler_params=pltpu.CompilerParams(vmem_limit_bytes=VMEM_LIMIT),
        name="own_part",
    )(rows, own_ids, far_ids, tiles, blocks, blocks, perm)


def far_kernel(rows, tiles_ref, flip_ref, base_ref, out_ref, sum_ref):
    step = pl.program_id(0)

    @pl.when(step == 0)
    def _():
        sum_ref[...] = base_ref[...]

    reuse, height, depth = tiles_ref.shape
    product = jnp.dot(
        tiles_ref[...].reshape(reuse * height, depth), flip_ref[0], preferred_element_type=jnp.float32
    )
    for part in range(reuse):
        row = rows[step * reuse + part]
        sum_ref[row] += product[part * height : (part + 1) * height]

    @pl.when(step == pl.num_programs(0) - 1)
    def _():
        out_ref[...] = sum_ref[...].astype(out_ref.dtype)


def far_part(rows, tiles, flipped, base):
    need, depth, width = flipped.shape
    height = tiles.shape[1]
    whole = (PPD, height, width)
    return pl.pallas_call(
        far_kernel,
        grid_spec=pltpu.PrefetchScalarGridSpec(
            num_scalar_prefetch=1,
            grid=(need,),
            in_specs=[
                pl.BlockSpec((REUSE, height, depth), lambda j, rows: (j, 0, 0)),
                pl.BlockSpec((1, depth, width), lambda j, rows: (j, 0, 0)),
                pl.BlockSpec(whole, lambda j, rows: (0, 0, 0)),
            ],
            out_specs=pl.BlockSpec(whole, lambda j, rows: (0, 0, 0)),
            scratch_shapes=[pltpu.VMEM(whole, jnp.float32)],
        ),
        out_shape=jax.ShapeDtypeStruct(whole, jnp.bfloat16),
        compiler_params=pltpu.CompilerParams(vmem_limit_bytes=VMEM_LIMIT),
        name="far_part",
    )(rows, tiles, flipped, base)


def per_device(t2_tiles, t2_row, t2_col, integrals):
    peers = lax.axis_size("tile")
    opposite = [(source, (source + peers // 2) % peers) for source in range(peers)]
    order = sorted_order(t2_col)
    tiles = jnp.take(t2_tiles, order, axis=0)
    rows = jnp.take(t2_row, order)
    ids = jnp.take(t2_col, order)[::REUSE]
    need = ids.shape[0]
    notes = lax.ppermute(jnp.concatenate([rows, ids]), "tile", opposite)
    far_tiles = lax.ppermute(tiles, "tile", opposite)
    blocks = lax.all_gather(integrals, "tile", axis=0, tiled=True)
    far_rows, far_ids = notes[: REUSE * need], notes[REUSE * need :]
    base, flipped = own_part(rows, ids, far_ids, tiles, blocks, flip_matrix(W))
    return far_part(far_rows, far_tiles, flipped, base)


def solution(mesh):
    in_specs = (
        P(("groups", "tile"), None, None),
        P(("groups", "tile")),
        P(("groups", "tile")),
        P(("groups", "tile"), None, None),
    )
    out_specs = P(("groups", "tile"), None, None)
    return jax.shard_map(
        per_device, mesh=mesh, in_specs=in_specs, out_specs=out_specs, check_vma=False
    )
```

time: 823 us -> 333 us (0.40)
  waiting for transfers between devices: 510 us -> 235 us
  other arithmetic: 130 us -> 7.45 us
  local copies, waits for them, and re-layouts: 84.4 us -> 6.24 us
  Pallas kernels: 0 us -> 65.4 us
  matrix products: 44.8 us -> 0 us
  starting transfers between devices: 38.5 us -> 4.05 us
  blocking collectives: 13.6 us -> 0 us
  between operations: 0.08 us -> 13.5 us
    all_to_all x1 -> x0, waiting for transfers between devices: 150 us -> none  [per_device(): lax.all_to_all(replies, 'tile', split_axis=0, concat_axis=0, tiled=True)]
    ppermute x1 -> x2, waiting for transfers between devices: 360 us -> 234 us  [the longest x1 234 us: per_device(): notes = lax.ppermute(jnp.concatenate([rows, ids]), 'tile', opposite)]
    scatter-add x12 -> x0, other arithmetic: 112 us -> none  [accumulate(): return (running.at[row_group].add(product), None)]
    pallas_call x0 -> x2, Pallas kernels: none -> 65.4 us  [the longest x1 36.4 us: own_part(): pl.pallas_call(own_kernel, grid_spec=pltpu.PrefetchScalarGridSpec(num_sca...]
    gather x13 -> x3, local copies, waits for them, and re-layouts: 53.8 us -> 5.53 us  [the longest x1 2.72 us: per_device(): tiles = jnp.take(t2_tiles, order, axis=0)]
    dot_general x12 -> x0, matrix products: 44.8 us -> none  [accumulate(): jnp.einsum('tij,tjc->tic', tile_group, blocks, preferred_element_type=jnp...]
    ppermute x1 -> x2, starting transfers between devices: 33.5 us -> 4.05 us  [the longest x1 4.04 us: per_device(): far_tiles = lax.ppermute(tiles, 'tile', opposite)]
    all_to_all x1 -> x0, blocking collectives: 13.6 us -> none  [per_device(): lax.all_to_all(request, 'tile', split_axis=0, concat_axis=0, tiled=True)]
  transfers between devices with their start and end apart: 2 -> 3, of which waited for: 2 -> 1; matrix products, arithmetic and copies ran while one was open for 0% -> 4% of each run, Pallas kernels for 0% -> 11%
where the time goes in v1:
time: 333 us; the launch traced here: 331 us
  waiting for transfers between devices  235 us (71%)
  Pallas kernels  65.4 us (20%)
  between operations  13.5 us (4%)
  other arithmetic  7.45 us (2%)
  local copies, waits for them, and re-layouts  6.24 us (2%)
  starting transfers between devices  4.05 us (1%)
    ppermute x1, waiting for transfers between devices, per_device(): notes = lax.ppermute(jnp.concatenate([rows, ids]), 'tile', opposite)  234 us
    pallas_call x1, Pallas kernels, own_part(): pl.pallas_call(own_kernel, grid_spec=pltpu.PrefetchScalarGridSpec(num_sca...  36.4 us
    pallas_call x1, Pallas kernels, far_part(): pl.pallas_call(far_kernel, grid_spec=pltpu.PrefetchScalarGridSpec(num_sca...  29 us
  transfers between devices with their start and end apart: 3, of which 1 were waited for; matrix products, arithmetic and copies ran while one was open for 4% of the time, Pallas kernels for 11%

profile of v1, /device:TPU:0, one launch (start us, length us, event | category | flops | bytes accessed | tf_op | source)
XLA Modules:
  0.0 331.2 jit_solution(12805174165577583436)
XLA Ops:
  6.5 0.0 copy-start
  6.5 0.0 all-gather.2.cloned.1.call-start
  6.5 0.7 all-gather.2.cloned.1.call-update
  7.3 1.1 convert_reduce_fusion
  8.3 0.1 select_reduce_fusion
  8.5 1.6 gather_fusion.1
  10.1 0.0 copy-done
  10.1 2.7 gather_fusion
  12.8 0.0 copy-start.2
  12.8 0.0 copy-start.1
  12.8 3.9 %broadcast_select_fusion.tiles_ref = bf16[96,128,128]{2,1,0:T(8,128)(2,1)} fusion(bf16[96,128,128]{2,1,0:T(8,128)(2,1)} %gather_fusion, pred[96]{0:T(512)(128)(4,1)S(1)} %get-tuple-element.11), kind=kLoop, calls=%fused_computation.5 | loop fusion | flops 1572864 | bytes 6291552 | tf_op jit(solution)/shard_map/jit(_take)/select_n | solution.py:125
  16.7 4.0 %collective-permute-start.1 = (bf16[96,128,128]{2,1,0:T(8,128)(2,1)}, bf16[96,128,128]{2,1,0:T(8,128)(2,1)}, u32[]{:S(2)}, u32[]{:S(2)}) collective-permute-start(bf16[96,128,128]{2,1,0:T(8,128)(2,1)} %broadcast_select_fusion.tiles_ref), channel_id=1, source_target_pairs={{0,8},{1,9},{2,10},{3,11},{4,12},{5,13},{6,14},{7,15},{8,0},{9,1},... | collective-permute-start | bytes 9437192 | tf_op jit(solution)/shard_map/ppermute | solution.py:130
  20.8 0.0 copy-done.1
  20.8 1.2 gather_fusion.2
  22.0 0.1 slice.9.own_ids
  22.2 0.0 copy-start.4
  22.2 0.0 copy-done.2
  22.2 0.1 pad_add_fusion
  22.2 0.0 collective-permute-start
  22.3 2.2 fusion.perm_ref
  24.5 233.8 %collective-permute-done = s32[128]{0:T(128)S(1)} collective-permute-done((s32[128]{0:T(128)S(1)}, s32[128]{0:T(128)S(1)}, u32[]{:S(2)}, u32[]{:S(2)}) %collective-permute-start) | collective-permute-done | bytes 544 | tf_op jit(solution)/shard_map/ppermute | solution.py:129
  258.3 0.0 copy-start.3
  258.3 0.6 slice.11.far_ids
  258.9 0.0 all-gather.2.cloned.1.call-done.block_ref.far_ref
  258.9 0.0 copy-done.4
  258.9 36.4 %own_part.1 = (f32[16,128,1024]{2,1,0:T(8,128)}, bf16[32,128,1024]{2,1,0:T(8,128)(2,1)}) custom-call(s32[96]{0:T(128)} %copy-done.2, s32[32]{0:T(128)} %copy-done.4, s32[32]{0:T(128)} %slice.11.far_ids, bf16[96,128,128]{2,1,0:T(8,128)(2,1)} %broadcast_select_fusion.tiles_ref, bf16[64,128,1024]{2,1,0:T(8,128)(2,1)} %all-gather.2.cloned.1.call-done.block_ref.far_ref, ...), custom_call_target="tpu_custom_call" | custom-call | tf_op jit(solution)/shard_map/own_part/pallas_call | solution.py:53
  295.3 0.0 copy-done.3
  295.3 0.0 collective-permute-done.1.tiles_ref
  295.3 29.0 %far_part.1 = bf16[16,128,1024]{2,1,0:T(8,128)(2,1)} custom-call(s32[96]{0:T(128)} %bitcast.5, bf16[96,128,128]{2,1,0:T(8,128)(2,1)} %collective-permute-done.1.tiles_ref, bf16[32,128,1024]{2,1,0:T(8,128)(2,1)} %get-tuple-element.8.flip_ref, f32[16,128,1024]{2,1,0:T(8,128)} %get-tuple-element.9.base_ref), custom_call_target="tpu_custom_call" | custom-call | tf_op jit(solution)/shard_map/far_part/pallas_call | solution.py:102
  (7 shorter events, 0.0 us)
Async XLA Ops:
  6.5 3.6 %copy-start = (bf16[96,128,128]{2,1,0:T(8,128)(2,1)S(1)}, bf16[96,128,128]{2,1,0:T(8,128)(2,1)}, u32[]{:S(2)}) copy-start(bf16[96,128,128]{2,1,0:T(8,128)(2,1)} %param.6) | copy-start | bytes 9437188
  6.5 252.4 %all-gather.2.cloned.1.call-start = ((), (), s32[]{:S(2)}) async-start(), calls=%async_computation | async-start | bytes 17825792 | tf_op jit(solution)/shard_map/all_gather | solution.py:131
  12.8 9.3 %copy-start.2 = (s32[96]{0:T(128)}, s32[96]{0:T(128)S(1)}, u32[]{:S(2)}) copy-start(s32[96]{0:T(128)S(1)} %get-tuple-element.10.rows) | copy-start | bytes 1156
  12.8 8.0 %copy-start.1 = (s32[96]{0:T(128)S(1)}, s32[96]{0:T(128)}, u32[]{:S(2)}) copy-start(s32[96]{0:T(128)} %param.8) | copy-start | bytes 1156
  16.7 278.6 %collective-permute-start.1 = (bf16[96,128,128]{2,1,0:T(8,128)(2,1)}, bf16[96,128,128]{2,1,0:T(8,128)(2,1)}, u32[]{:S(2)}, u32[]{:S(2)}) collective-permute-start(bf16[96,128,128]{2,1,0:T(8,128)(2,1)} %broadcast_select_fusion.tiles_ref), channel_id=1, source_target_pairs={{0,8},{1,9},{2,10},{3,11},{4,12},{5,13},{6,14},{7,15},{8,0},{9,1},... | collective-permute-start | bytes 9437192 | tf_op jit(solution)/shard_map/ppermute | solution.py:130
  22.2 236.7 %copy-start.4 = (s32[32]{0:T(128)}, s32[32]{0:T(128)S(1)}, u32[]{:S(2)}) copy-start(s32[32]{0:T(128)S(1)} %slice.9.own_ids) | copy-start | bytes 388
  22.2 236.1 %collective-permute-start = (s32[128]{0:T(128)S(1)}, s32[128]{0:T(128)S(1)}, u32[]{:S(2)}, u32[]{:S(2)}) collective-permute-start(s32[128]{0:T(128)S(1)} %pad_add_fusion), channel_id=1, source_target_pairs={{0,8},{1,9},{2,10},{3,11},{4,12},{5,13},{6,14},{7,15},{8,0},{9,1},... | collective-permute-start | bytes 1544 | tf_op jit(solution)/shard_map/ppermute | solution.py:129
  258.3 37.0 %copy-start.3 = (s32[128]{0:T(128)}, s32[128]{0:T(128)S(1)}, u32[]{:S(2)}) copy-start(s32[128]{0:T(128)S(1)} %collective-permute-done) | copy-start | bytes 1540
Sparse Core Ops, SparseCore 0:
  9.5 244.3 all-gather.1

commit v2 on v1

v2 whole, which is shorter than its diff:
```python
import jax
import jax.numpy as jnp
from jax import lax
from jax.experimental import pallas as pl
from jax.experimental.pallas import tpu as pltpu
from jax.sharding import PartitionSpec as P

W = 32
PPD = 16
REUSE = 3
CAP = 2
LAST = 4
VMEM_LIMIT = 56 * 1024 * 1024


def sorted_order(t2_col):
    count = t2_col.shape[0]
    ids = jnp.arange(count, dtype=jnp.int32)
    before = (t2_col[None, :] < t2_col[:, None]) | (
        (t2_col[None, :] == t2_col[:, None]) & (ids[None, :] < ids[:, None])
    )
    rank = jnp.sum(before.astype(jnp.int32), axis=1)
    return jnp.sum(jnp.where(rank[None, :] == ids[:, None], ids[None, :], 0), axis=1)


def flip_matrix(width):
    columns = jnp.arange(width * width, dtype=jnp.int32)
    source = (columns % width) * width + columns // width
    return (columns[:, None] == source[None, :]).astype(jnp.bfloat16)


def tree_gather(shard):
    everyone = range(16)
    centre = [i for i in everyone if i // 4 in (1, 2)]

    def send(value, pairs):
        return lax.ppermute(value, "tile", pairs)

    across = [(i, i ^ 12) for i in centre]
    outward = [(i, i ^ 4) for i in centre]
    me = lax.axis_index("tile")
    z = me // 4
    in_centre = (z == 1) | (z == 2)
    near = send(shard, [(i, i ^ 4) for i in everyone])
    first_centre = send(shard, across)
    second_centre = send(near, across)
    first = jnp.where(in_centre, first_centre, send(first_centre, outward))
    second = jnp.where(in_centre, second_centre, send(second_centre, outward))
    line = [shard, near, first, second]
    other_line = [send(value, [(i, i ^ 2) for i in everyone]) for value in line]
    buffers = []
    for value in line + other_line:
        buffers += [value, send(value, [(i, i ^ 1) for i in everyone])]
    low = z < 2
    zs = [z, z ^ 1, jnp.where(low, 2, 1), jnp.where(low, 3, 0)]
    owners = [4 * zs[k] + ((me & 3) ^ (2 * y + c)) for y in (0, 1) for k in range(4) for c in (0, 1)]
    return buffers, jnp.stack(owners).astype(jnp.int32)


def own_kernel(slots, rows, own_ids, far_ids, owners, tiles_refs, buffer_refs, perm_ref, sum_ref, flip_ref,
               own_blocks, far_blocks, own_sems, far_sems):
    need = own_blocks.shape[0]
    local = buffer_refs[0].shape[0]

    def fetch(buffer_ref, ids, slot, landing, sems):
        offset = lax.rem(ids[slot], local)
        pltpu.make_async_copy(buffer_ref.at[offset], landing.at[slot], sems.at[slot]).start()

    if slots:
        for ids, landing, sems in ((own_ids, own_blocks, own_sems), (far_ids, far_blocks, far_sems)):
            for number, buffer_ref in enumerate(buffer_refs):
                for extra in range(slots):
                    fetch(buffer_ref, ids, owners[number] * slots + extra, landing, sems)
    else:
        for ids, landing, sems in ((own_ids, own_blocks, own_sems), (far_ids, far_blocks, far_sems)):

            @pl.loop(0, need)
            def _(slot):
                fetch(buffer_refs[0], ids, slot, landing, sems)

    sum_ref[...] = jnp.zeros_like(sum_ref)
    base = 0
    for tiles_ref in tiles_refs:
        count, height, depth = tiles_ref.shape

        @pl.loop(0, count // REUSE)
        def _(step, tiles_ref=tiles_ref, base=base):
            slot = base + step
            pltpu.make_async_copy(own_blocks.at[slot], own_blocks.at[slot], own_sems.at[slot]).wait()
            block = own_blocks[slot]
            for part in range(REUSE):
                row = rows[slot * REUSE + part]
                sum_ref[row] += jnp.dot(tiles_ref[step * REUSE + part], block, preferred_element_type=jnp.float32)

        base += count // REUSE

    @pl.loop(0, need)
    def _(slot):
        pltpu.make_async_copy(far_blocks.at[slot], far_blocks.at[slot], far_sems.at[slot]).wait()
        flip_ref[slot] = jnp.dot(
            far_blocks[slot], perm_ref[...], preferred_element_type=jnp.float32
        ).astype(jnp.bfloat16)


def own_part(slots, rows, own_ids, far_ids, owners, tiles, buffers, perm):
    need = own_ids.shape[0]
    height = tiles[0].shape[1]
    depth, width = buffers[0].shape[1:]

    def kernel(rows, own_ids, far_ids, owners, *refs):
        tiles_refs = refs[: len(tiles)]
        buffer_refs = refs[len(tiles) : len(tiles) + len(buffers)]
        own_kernel(slots, rows, own_ids, far_ids, owners, tiles_refs, buffer_refs, *refs[len(tiles) + len(buffers) :])

    vmem = pl.BlockSpec(memory_space=pltpu.VMEM)
    return pl.pallas_call(
        kernel,
        in_specs=[pl.BlockSpec(memory_space=pltpu.SMEM)] * 4
        + [vmem] * len(tiles)
        + [pl.BlockSpec(memory_space=pl.ANY)] * len(buffers)
        + [vmem],
        out_specs=[vmem, vmem],
        out_shape=[
            jax.ShapeDtypeStruct((PPD, height, width), jnp.float32),
            jax.ShapeDtypeStruct((need, depth, width), jnp.bfloat16),
        ],
        scratch_shapes=[
            pltpu.VMEM((need, depth, width), jnp.bfloat16),
            pltpu.VMEM((need, depth, width), jnp.bfloat16),
            pltpu.SemaphoreType.DMA((need,)),
            pltpu.SemaphoreType.DMA((need,)),
        ],
        compiler_params=pltpu.CompilerParams(vmem_limit_bytes=VMEM_LIMIT),
        name="own_part",
    )(rows, own_ids, far_ids, owners, *tiles, *buffers, perm)


def far_kernel(base, rows, tiles_ref, flip_ref, base_ref, out_ref, sum_ref):
    step = pl.program_id(0)

    @pl.when(step == 0)
    def _():
        sum_ref[...] = base_ref[...]

    for part in range(REUSE):
        row = rows[base + step * REUSE + part]
        sum_ref[row] += jnp.dot(tiles_ref[part], flip_ref[0], preferred_element_type=jnp.float32)

    @pl.when(step == pl.num_programs(0) - 1)
    def _():
        out_ref[...] = sum_ref[...].astype(out_ref.dtype)


def far_part(base, rows, tiles, flipped, total, dtype):
    depth, width = flipped.shape[1:]
    count, height = tiles.shape[:2]
    whole = (PPD, height, width)
    first = base // REUSE

    def kernel(*refs):
        far_kernel(base, *refs)

    return pl.pallas_call(
        kernel,
        grid_spec=pltpu.PrefetchScalarGridSpec(
            num_scalar_prefetch=1,
            grid=(count // REUSE,),
            in_specs=[
                pl.BlockSpec((REUSE, height, depth), lambda j, rows: (j, 0, 0)),
                pl.BlockSpec((1, depth, width), lambda j, rows: (first + j, 0, 0)),
                pl.BlockSpec(whole, lambda j, rows: (0, 0, 0), pipeline_mode=pl.Buffered(1)),
            ],
            out_specs=pl.BlockSpec(whole, lambda j, rows: (0, 0, 0), pipeline_mode=pl.Buffered(1)),
            scratch_shapes=[pltpu.VMEM(whole, jnp.float32)],
        ),
        out_shape=jax.ShapeDtypeStruct(whole, dtype),
        compiler_params=pltpu.CompilerParams(vmem_limit_bytes=VMEM_LIMIT),
        name="far_part",
    )(rows, tiles, flipped, total)


def per_device(t2_tiles, t2_row, t2_col, integrals):
    peers = lax.axis_size("tile")
    opposite = [(source, (source + peers // 2) % peers) for source in range(peers)]
    need = t2_col.shape[0] // REUSE
    if peers == 16 and need == CAP * peers:
        slots = CAP
        buffers, owners = tree_gather(integrals)
    else:
        slots = 0
        buffers = [lax.all_gather(integrals, "tile", axis=0, tiled=True)]
        owners = jnp.zeros((1,), jnp.int32)
    order = sorted_order(t2_col)
    rows = jnp.take(t2_row, order)
    ids = jnp.take(t2_col, order)[::REUSE]
    notes = lax.ppermute(jnp.concatenate([rows, ids]), "tile", opposite)
    far_rows, far_ids = notes[: REUSE * need], notes[REUSE * need :]
    cut = REUSE * (need - need // LAST)
    tiles = [jnp.take(t2_tiles, order[:cut], axis=0), jnp.take(t2_tiles, order[cut:], axis=0)]
    far_tiles = [lax.ppermute(part, "tile", opposite) for part in tiles]
    total, flipped = own_part(slots, rows, ids, far_ids, owners, tiles, buffers, flip_matrix(W))
    total = far_part(0, far_rows, far_tiles[0], flipped, total, jnp.float32)
    return far_part(cut, far_rows, far_tiles[1], flipped, total, jnp.bfloat16)


def solution(mesh):
    in_specs = (
        P(("groups", "tile"), None, None),
        P(("groups", "tile")),
        P(("groups", "tile")),
        P(("groups", "tile"), None, None),
    )
    out_specs = P(("groups", "tile"), None, None)
    return jax.shard_map(
        per_device, mesh=mesh, in_specs=in_specs, out_specs=out_specs, check_vma=False
    )
```

time: 333 us -> 241 us (0.72)
  waiting for transfers between devices: 235 us -> 103 us
  starting transfers between devices: 4.05 us -> 39.6 us
  between operations: 13.5 us -> 0.13 us
  Pallas kernels: 65.4 us -> 75.8 us
  other arithmetic: 7.45 us -> 13.6 us
    ppermute x1, waiting for transfers between devices: 234 us -> 1.51 us  [per_device(): notes = lax.ppermute(jnp.concatenate([rows, ids]), 'tile', opposite)]
    ppermute x1 -> x19, waiting for transfers between devices: 0.01 us -> 101 us  [the longest x17 77.2 us: send(): return lax.ppermute(value, 'tile', pairs)]
    ppermute x1, starting transfers between devices: 0.01 us -> 20.9 us  [per_device(): notes = lax.ppermute(jnp.concatenate([rows, ids]), 'tile', opposite)]
    ppermute x1 -> x19, starting transfers between devices: 4.04 us -> 18.7 us  [the longest x17 15.5 us: send(): return lax.ppermute(value, 'tile', pairs)]
    pallas_call x2 -> x3, Pallas kernels: 65.4 us -> 75.8 us  [the longest x1 39.1 us: own_part(): pl.pallas_call(kernel, in_specs=[pl.BlockSpec(memory_space=pltpu.SMEM)] *...]
    select_n x3 -> x4, other arithmetic: 3.92 us -> 10.2 us  [the longest x1 3.35 us: per_device(): jnp.take(t2_tiles, order[:cut], axis=0)]
  transfers between devices with their start and end apart: 3 -> 20, of which waited for: 1 -> 6; matrix products, arithmetic and copies ran while one was open for 4% -> 9% of each run, Pallas kernels for 11% -> 26%
where the time goes in v2:
time: 241 us; the launch traced here: 240 us
  waiting for transfers between devices  103 us (43%)
  Pallas kernels  75.8 us (31%)
  starting transfers between devices  39.6 us (16%)
  other arithmetic  13.6 us (6%)
  local copies, waits for them, and re-layouts  8.51 us (4%)
    ppermute x17, waiting for transfers between devices, send(): return lax.ppermute(value, 'tile', pairs)  77.2 us
    pallas_call x1, Pallas kernels, own_part(): pl.pallas_call(kernel, in_specs=[pl.BlockSpec(memory_space=pltpu.SMEM)] *...  39.1 us
    pallas_call x2, Pallas kernels, far_part(): pl.pallas_call(kernel, grid_spec=pltpu.PrefetchScalarGridSpec(num_scalar_...  36.7 us
    ppermute x2, waiting for transfers between devices, per_device(): far_tiles = [lax.ppermute(part, 'tile', opposite) for part in tiles]  24 us
    ppermute x1, starting transfers between devices, per_device(): notes = lax.ppermute(jnp.concatenate([rows, ids]), 'tile', opposite)  20.9 us
    ppermute x17, starting transfers between devices, send(): return lax.ppermute(value, 'tile', pairs)  15.5 us
  transfers between devices with their start and end apart: 20, of which 6 were waited for; matrix products, arithmetic and copies ran while one was open for 9% of the time, Pallas kernels for 26%

profile of v2, /device:TPU:0, one launch (start us, length us, event | category | flops | bytes accessed | tf_op | source)
XLA Modules:
  0.0 240.3 jit_solution(6991679915714502167)
XLA Ops:
  0.0 0.0 copy-start
  0.0 3.0 %collective-permute-start.3 = (bf16[4,128,1024]{2,1,0:T(8,128)(2,1)}, bf16[4,128,1024]{2,1,0:T(8,128)(2,1)}, u32[]{:S(2)}, u32[]{:S(2)}) collective-permute-start(bf16[4,128,1024]{2,1,0:T(8,128)(2,1)} %refs_2_.1), channel_id=1, source_target_pairs={{0,4},{1,5},{2,6},{3,7},{4,0},{5,1},{6,2},{7,3},{8,12},{9,13},{10,... | collective-permute-start | bytes 3145736 | tf_op jit(solution)/shard_map/ppermute | solution.py:37
  3.0 1.7 collective-permute-start.5
  4.7 21.8 %collective-permute-done.3.refs_4_ = bf16[4,128,1024]{2,1,0:T(8,128)(2,1)} collective-permute-done((bf16[4,128,1024]{2,1,0:T(8,128)(2,1)}, bf16[4,128,1024]{2,1,0:T(8,128)(2,1)}, u32[]{:S(2)}, u32[]{:S(2)}) %collective-permute-start.3) | collective-permute-done | bytes 1048608 | tf_op jit(solution)/shard_map/ppermute | solution.py:37
  26.5 1.7 collective-permute-start.8
  28.2 1.7 collective-permute-start.11
  29.8 0.0 collective-permute-start.2
  29.8 0.9 convert_reduce_fusion
  30.8 0.0 collective-permute-done.5
  30.8 1.3 collective-permute-start.6
  32.1 0.1 select_reduce_fusion
  32.2 1.6 gather_fusion.3
  33.8 1.6 gather_fusion.2
  35.4 0.0 copy-start.2
  35.4 0.1 slice.15.own_ids
  35.5 0.0 collective-permute-done.8
  35.5 1.3 collective-permute-start.9
  36.8 0.1 pad_add_fusion
  36.9 20.9 %collective-permute-start = (s32[128]{0:T(128)S(1)}, s32[128]{0:T(128)S(1)}, u32[]{:S(2)}, u32[]{:S(2)}) collective-permute-start(s32[128]{0:T(128)S(1)} %pad_add_fusion), channel_id=1, source_target_pairs={{0,8},{1,9},{2,10},{3,11},{4,12},{5,13},{6,14},{7,15},{8,0},{9,1},... | collective-permute-start | bytes 1544 | tf_op jit(solution)/shard_map/ppermute | solution.py:196
  57.8 1.5 collective-permute-done
  59.3 1.5 collective-permute-start.13
  60.9 0.0 collective-permute-done.11.refs_10_
  60.9 0.0 collective-permute-start.4
  60.9 0.0 copy-done
  60.9 2.4 %gather_fusion.1 = bf16[72,128,128]{2,1,0:T(8,128)(2,1)} fusion(bf16[96,128,128]{2,1,0:T(8,128)(2,1)S(1)} %copy-done, s32[1024]{0:T(1024)S(1)} %pad_clamp_fusion), kind=kCustom, calls=%fused_computation.3 | custom fusion | bytes 4718880 | tf_op jit(solution)/shard_map/jit(_take)/gather | solution.py:199
  63.3 0.0 copy-done.2
  63.3 0.0 copy-done.3
  63.3 0.0 collective-permute-done.6
  63.3 0.6 collective-permute-start.12
  63.9 3.3 %broadcast_select_fusion.refs_0_ = bf16[72,128,128]{2,1,0:T(8,128)(2,1)} fusion(bf16[72,128,128]{2,1,0:T(8,128)(2,1)} %gather_fusion.1, pred[72]{0:T(512)(128)(4,1)S(1)} %get-tuple-element.10), kind=kLoop, calls=%fused_computation.6 | loop fusion | flops 1179648 | bytes 4718664 | tf_op jit(solution)/shard_map/jit(_take)/select_n | solution.py:199
  67.2 2.3 broadcast_select_fusion.2.refs_6_
  69.6 12.6 %collective-permute-done.9 = bf16[4,128,1024]{2,1,0:T(8,128)(2,1)} collective-permute-done((bf16[4,128,1024]{2,1,0:T(8,128)(2,1)}, bf16[4,128,1024]{2,1,0:T(8,128)(2,1)}, u32[]{:S(2)}, u32[]{:S(2)}) %collective-permute-start.9) | collective-permute-done | bytes 1048608 | tf_op jit(solution)/shard_map/ppermute | solution.py:37
  82.1 0.6 collective-permute-start.19
  82.7 2.4 broadcast_select_fusion.1.refs_8_
  85.1 0.0 collective-permute-done.2.refs_3_
  85.1 0.5 collective-permute-start.15
  85.6 0.0 collective-permute-done.13.refs_12_
  85.6 0.0 collective-permute-start.7
  85.6 0.0 collective-permute-done.4.refs_5_
  85.6 1.6 collective-permute-start.17
  87.2 0.0 collective-permute-done.12.refs_11_
  87.2 0.2 collective-permute-start.14
  87.3 0.1 compare_and_fusion.2
  87.4 1.6 gather_fusion
  89.0 22.5 %collective-permute-done.15.refs_14_ = bf16[4,128,1024]{2,1,0:T(8,128)(2,1)} collective-permute-done((bf16[4,128,1024]{2,1,0:T(8,128)(2,1)}, bf16[4,128,1024]{2,1,0:T(8,128)(2,1)}, u32[]{:S(2)}, u32[]{:S(2)}) %collective-permute-start.15) | collective-permute-done | bytes 1048608 | tf_op jit(solution)/shard_map/ppermute | solution.py:37
  111.5 0.0 collective-permute-start.10
  111.5 0.0 collective-permute-done.7.refs_7_
  111.5 0.5 collective-permute-start.16
  112.0 20.4 %collective-permute-done.17.refs_16_ = bf16[4,128,1024]{2,1,0:T(8,128)(2,1)} collective-permute-done((bf16[4,128,1024]{2,1,0:T(8,128)(2,1)}, bf16[4,128,1024]{2,1,0:T(8,128)(2,1)}, u32[]{:S(2)}, u32[]{:S(2)}) %collective-permute-start.17) | collective-permute-done | bytes 1048608 | tf_op jit(solution)/shard_map/ppermute | solution.py:37
  132.4 0.0 collective-permute-start.18
  132.4 2.2 broadcast_select_fusion.3.refs_1_
  134.6 0.0 collective-permute-done.14.refs_13_
  134.6 2.5 %collective-permute-start.1 = (bf16[24,128,128]{2,1,0:T(8,128)(2,1)}, bf16[24,128,128]{2,1,0:T(8,128)(2,1)}, u32[]{:S(2)}, u32[]{:S(2)}) collective-permute-start(bf16[24,128,128]{2,1,0:T(8,128)(2,1)} %broadcast_select_fusion.3.refs_1_), channel_id=1, source_target_pairs={{0,8},{1,9},{2,10},{3,11},{4,12},{5,13},{6,14},{7,15},{8,0},{9,1},... | collective-permute-start | bytes 2359304 | tf_op jit(solution)/shard_map/ppermute | solution.py:200
  137.1 0.6 stack.67.owners
  137.7 2.2 fusion.refs_18_
  139.9 0.6 slice.18.far_ids
  140.5 0.0 collective-permute-done.10.refs_9_
  140.5 0.0 collective-permute-done.16.refs_15_
  140.5 0.0 collective-permute-done.18.refs_17_
  140.5 39.1 %own_part.1 = (f32[16,128,1024]{2,1,0:T(8,128)}, bf16[32,128,1024]{2,1,0:T(8,128)(2,1)}) custom-call(s32[96]{0:T(128)} %copy-done.2, s32[32]{0:T(128)} %copy-done.3, s32[32]{0:T(128)} %slice.18.far_ids, s32[16]{0:T(128)} %stack.67.owners, bf16[72,128,128]{2,1,0:T(8,128)(2,1)} %broadcast_select_fusion.refs_0_, ...), custom_call_target="tpu_custom_call" | custom-call | tf_op jit(solution)/shard_map/own_part/pallas_call | solution.py:116
  179.6 24.0 %collective-permute-done.19.refs_1_ = bf16[72,128,128]{2,1,0:T(8,128)(2,1)} collective-permute-done((bf16[72,128,128]{2,1,0:T(8,128)(2,1)}, bf16[72,128,128]{2,1,0:T(8,128)(2,1)}, u32[]{:S(2)}, u32[]{:S(2)}) %collective-permute-start.19) | collective-permute-done | bytes 2359328 | tf_op jit(solution)/shard_map/ppermute | solution.py:200
  203.6 24.6 %far_part.2.refs_3_ = f32[16,128,1024]{2,1,0:T(8,128)} custom-call(s32[96]{0:T(128)} %bitcast.17, bf16[72,128,128]{2,1,0:T(8,128)(2,1)} %collective-permute-done.19.refs_1_, bf16[32,128,1024]{2,1,0:T(8,128)(2,1)} %get-tuple-element.8.refs_2_, f32[16,128,1024]{2,1,0:T(8,128)} %get-tuple-element.9.refs_3_), custom_call_target="tpu_custom_call" | custom-call | tf_op jit(solution)/shard_map/far_part/pallas_call | solution.py:163
  228.2 0.0 collective-permute-done.1.refs_1_
  228.2 12.1 %far_part.3 = bf16[16,128,1024]{2,1,0:T(8,128)(2,1)} custom-call(s32[96]{0:T(128)} %bitcast.18, bf16[24,128,128]{2,1,0:T(8,128)(2,1)} %collective-permute-done.1.refs_1_, bf16[32,128,1024]{2,1,0:T(8,128)(2,1)} %get-tuple-element.8.refs_2_, f32[16,128,1024]{2,1,0:T(8,128)} %far_part.2.refs_3_), custom_call_target="tpu_custom_call" | custom-call | tf_op jit(solution)/shard_map/far_part/pallas_call | solution.py:163
  (10 shorter events, 0.0 us)
Async XLA Ops:
  0.0 60.9 %copy-start = (bf16[96,128,128]{2,1,0:T(8,128)(2,1)S(1)}, bf16[96,128,128]{2,1,0:T(8,128)(2,1)}, u32[]{:S(2)}) copy-start(bf16[96,128,128]{2,1,0:T(8,128)(2,1)} %param.6) | copy-start | bytes 9437188
  0.0 26.5 %collective-permute-start.3 = (bf16[4,128,1024]{2,1,0:T(8,128)(2,1)}, bf16[4,128,1024]{2,1,0:T(8,128)(2,1)}, u32[]{:S(2)}, u32[]{:S(2)}) collective-permute-start(bf16[4,128,1024]{2,1,0:T(8,128)(2,1)} %refs_2_.1), channel_id=1, source_target_pairs={{0,4},{1,5},{2,6},{3,7},{4,0},{5,1},{6,2},{7,3},{8,12},{9,13},{10,... | collective-permute-start | bytes 3145736 | tf_op jit(solution)/shard_map/ppermute | solution.py:37
  3.0 27.7 %collective-permute-start.5 = (bf16[4,128,1024]{2,1,0:T(8,128)(2,1)}, bf16[4,128,1024]{2,1,0:T(8,128)(2,1)}, u32[]{:S(2)}, u32[]{:S(2)}) collective-permute-start(bf16[4,128,1024]{2,1,0:T(8,128)(2,1)} %refs_2_.1), channel_id=1, source_target_pairs={{4,8},{5,9},{6,10},{7,11},{8,4},{9,5},{10,6},{11,7},{20,24},{21,25... | collective-permute-start | bytes 3145736 | tf_op jit(solution)/shard_map/ppermute | solution.py:37
  26.5 9.0 %collective-permute-start.8 = (bf16[4,128,1024]{2,1,0:T(8,128)(2,1)}, bf16[4,128,1024]{2,1,0:T(8,128)(2,1)}, u32[]{:S(2)}, u32[]{:S(2)}) collective-permute-start(bf16[4,128,1024]{2,1,0:T(8,128)(2,1)} %collective-permute-done.3.refs_4_), channel_id=1, source_target_pairs={{4,8},{5,9},{6,10},{7,11},{8,4},{9,5},{10,6},{11,7},{20,24},{21,25... | collective-permute-start | bytes 3145736 | tf_op jit(solution)/shard_map/ppermute | solution.py:37
  28.2 32.7 %collective-permute-start.11 = (bf16[4,128,1024]{2,1,0:T(8,128)(2,1)}, bf16[4,128,1024]{2,1,0:T(8,128)(2,1)}, u32[]{:S(2)}, u32[]{:S(2)}) collective-permute-start(bf16[4,128,1024]{2,1,0:T(8,128)(2,1)} %refs_2_.1), channel_id=1, source_target_pairs={{0,2},{1,3},{2,0},{3,1},{4,6},{5,7},{6,4},{7,5},{8,10},{9,11},{10,... | collective-permute-start | bytes 3145736 | tf_op jit(solution)/shard_map/ppermute | solution.py:37
  29.8 55.2 %collective-permute-start.2 = (bf16[4,128,1024]{2,1,0:T(8,128)(2,1)}, bf16[4,128,1024]{2,1,0:T(8,128)(2,1)}, u32[]{:S(2)}, u32[]{:S(2)}) collective-permute-start(bf16[4,128,1024]{2,1,0:T(8,128)(2,1)} %refs_2_.1), channel_id=1, source_target_pairs={{0,1},{1,0},{2,3},{3,2},{4,5},{5,4},{6,7},{7,6},{8,9},{9,8},{10,11... | collective-permute-start | bytes 3145736 | tf_op jit(solution)/shard_map/ppermute | solution.py:37
  30.8 32.6 %collective-permute-start.6 = (bf16[4,128,1024]{2,1,0:T(8,128)(2,1)}, bf16[4,128,1024]{2,1,0:T(8,128)(2,1)}, u32[]{:S(2)}, u32[]{:S(2)}) collective-permute-start(bf16[4,128,1024]{2,1,0:T(8,128)(2,1)} %collective-permute-done.5), channel_id=1, source_target_pairs={{4,0},{5,1},{6,2},{7,3},{8,12},{9,13},{10,14},{11,15},{20,16},{21,... | collective-permute-start | bytes 3145736 | tf_op jit(solution)/shard_map/ppermute | solution.py:37
  35.4 27.9 %copy-start.2 = (s32[96]{0:T(128)}, s32[96]{0:T(128)S(1)}, u32[]{:S(2)}) copy-start(s32[96]{0:T(128)S(1)} %get-tuple-element.14.rows) | copy-start | bytes 1156
  35.5 27.8 %copy-start.3 = (s32[32]{0:T(128)}, s32[32]{0:T(128)S(1)}, u32[]{:S(2)}) copy-start(s32[32]{0:T(128)S(1)} %slice.15.own_ids) | copy-start | bytes 388
  35.5 46.6 %collective-permute-start.9 = (bf16[4,128,1024]{2,1,0:T(8,128)(2,1)}, bf16[4,128,1024]{2,1,0:T(8,128)(2,1)}, u32[]{:S(2)}, u32[]{:S(2)}) collective-permute-start(bf16[4,128,1024]{2,1,0:T(8,128)(2,1)} %collective-permute-done.8), channel_id=1, source_target_pairs={{4,0},{5,1},{6,2},{7,3},{8,12},{9,13},{10,14},{11,15},{20,16},{21,... | collective-permute-start | bytes 3145736 | tf_op jit(solution)/shard_map/ppermute | solution.py:37
  36.9 22.4 %collective-permute-start = (s32[128]{0:T(128)S(1)}, s32[128]{0:T(128)S(1)}, u32[]{:S(2)}, u32[]{:S(2)}) collective-permute-start(s32[128]{0:T(128)S(1)} %pad_add_fusion), channel_id=1, source_target_pairs={{0,8},{1,9},{2,10},{3,11},{4,12},{5,13},{6,14},{7,15},{8,0},{9,1},... | collective-permute-start | bytes 1544 | tf_op jit(solution)/shard_map/ppermute | solution.py:196
  59.3 80.6 %copy-start.1 = (s32[128]{0:T(128)}, s32[128]{0:T(128)S(1)}, u32[]{:S(2)}) copy-start(s32[128]{0:T(128)S(1)} %collective-permute-done) | copy-start | bytes 1540
  59.3 26.2 %collective-permute-start.13 = (bf16[4,128,1024]{2,1,0:T(8,128)(2,1)}, bf16[4,128,1024]{2,1,0:T(8,128)(2,1)}, u32[]{:S(2)}, u32[]{:S(2)}) collective-permute-start(bf16[4,128,1024]{2,1,0:T(8,128)(2,1)} %collective-permute-done.3.refs_4_), channel_id=1, source_target_pairs={{0,2},{1,3},{2,0},{3,1},{4,6},{5,7},{6,4},{7,5},{8,10},{9,11},{10,... | collective-permute-start | bytes 3145736 | tf_op jit(solution)/shard_map/ppermute | solution.py:37
  60.9 24.7 %collective-permute-start.4 = (bf16[4,128,1024]{2,1,0:T(8,128)(2,1)}, bf16[4,128,1024]{2,1,0:T(8,128)(2,1)}, u32[]{:S(2)}, u32[]{:S(2)}) collective-permute-start(bf16[4,128,1024]{2,1,0:T(8,128)(2,1)} %collective-permute-done.3.refs_4_), channel_id=1, source_target_pairs={{0,1},{1,0},{2,3},{3,2},{4,5},{5,4},{6,7},{7,6},{8,9},{9,8},{10,11... | collective-permute-start | bytes 3145736 | tf_op jit(solution)/shard_map/ppermute | solution.py:37
  63.3 23.9 %collective-permute-start.12 = (bf16[4,128,1024]{2,1,0:T(8,128)(2,1)}, bf16[4,128,1024]{2,1,0:T(8,128)(2,1)}, u32[]{:S(2)}, u32[]{:S(2)}) collective-permute-start(bf16[4,128,1024]{2,1,0:T(8,128)(2,1)} %collective-permute-done.11.refs_10_), channel_id=1, source_target_pairs={{0,1},{1,0},{2,3},{3,2},{4,5},{5,4},{6,7},{7,6},{8,9},{9,8},{10,11... | collective-permute-start | bytes 3145736 | tf_op jit(solution)/shard_map/ppermute | solution.py:37
  82.1 121.5 %collective-permute-start.19 = (bf16[72,128,128]{2,1,0:T(8,128)(2,1)}, bf16[72,128,128]{2,1,0:T(8,128)(2,1)}, u32[]{:S(2)}, u32[]{:S(2)}) collective-permute-start(bf16[72,128,128]{2,1,0:T(8,128)(2,1)} %broadcast_select_fusion.refs_0_), channel_id=1, source_target_pairs={{0,8},{1,9},{2,10},{3,11},{4,12},{5,13},{6,14},{7,15},{8,0},{9,1},... | collective-permute-start | bytes 7077896 | tf_op jit(solution)/shard_map/ppermute | solution.py:200
  85.1 26.4 %collective-permute-start.15 = (bf16[4,128,1024]{2,1,0:T(8,128)(2,1)}, bf16[4,128,1024]{2,1,0:T(8,128)(2,1)}, u32[]{:S(2)}, u32[]{:S(2)}) collective-permute-start(bf16[4,128,1024]{2,1,0:T(8,128)(2,1)} %broadcast_select_fusion.2.refs_6_), channel_id=1, source_target_pairs={{0,2},{1,3},{2,0},{3,1},{4,6},{5,7},{6,4},{7,5},{8,10},{9,11},{10,... | collective-permute-start | bytes 3145736 | tf_op jit(solution)/shard_map/ppermute | solution.py:37
  85.6 25.9 %collective-permute-start.7 = (bf16[4,128,1024]{2,1,0:T(8,128)(2,1)}, bf16[4,128,1024]{2,1,0:T(8,128)(2,1)}, u32[]{:S(2)}, u32[]{:S(2)}) collective-permute-start(bf16[4,128,1024]{2,1,0:T(8,128)(2,1)} %broadcast_select_fusion.2.refs_6_), channel_id=1, source_target_pairs={{0,1},{1,0},{2,3},{3,2},{4,5},{5,4},{6,7},{7,6},{8,9},{9,8},{10,11... | collective-permute-start | bytes 3145736 | tf_op jit(solution)/shard_map/ppermute | solution.py:37
  85.6 46.8 %collective-permute-start.17 = (bf16[4,128,1024]{2,1,0:T(8,128)(2,1)}, bf16[4,128,1024]{2,1,0:T(8,128)(2,1)}, u32[]{:S(2)}, u32[]{:S(2)}) collective-permute-start(bf16[4,128,1024]{2,1,0:T(8,128)(2,1)} %broadcast_select_fusion.1.refs_8_), channel_id=1, source_target_pairs={{0,2},{1,3},{2,0},{3,1},{4,6},{5,7},{6,4},{7,5},{8,10},{9,11},{10,... | collective-permute-start | bytes 3145736 | tf_op jit(solution)/shard_map/ppermute | solution.py:37
  87.2 47.4 %collective-permute-start.14 = (bf16[4,128,1024]{2,1,0:T(8,128)(2,1)}, bf16[4,128,1024]{2,1,0:T(8,128)(2,1)}, u32[]{:S(2)}, u32[]{:S(2)}) collective-permute-start(bf16[4,128,1024]{2,1,0:T(8,128)(2,1)} %collective-permute-done.13.refs_12_), channel_id=1, source_target_pairs={{0,1},{1,0},{2,3},{3,2},{4,5},{5,4},{6,7},{7,6},{8,9},{9,8},{10,11... | collective-permute-start | bytes 3145736 | tf_op jit(solution)/shard_map/ppermute | solution.py:37
  111.5 29.0 %collective-permute-start.10 = (bf16[4,128,1024]{2,1,0:T(8,128)(2,1)}, bf16[4,128,1024]{2,1,0:T(8,128)(2,1)}, u32[]{:S(2)}, u32[]{:S(2)}) collective-permute-start(bf16[4,128,1024]{2,1,0:T(8,128)(2,1)} %broadcast_select_fusion.1.refs_8_), channel_id=1, source_target_pairs={{0,1},{1,0},{2,3},{3,2},{4,5},{5,4},{6,7},{7,6},{8,9},{9,8},{10,11... | collective-permute-start | bytes 3145736 | tf_op jit(solution)/shard_map/ppermute | solution.py:37
  111.5 29.0 %collective-permute-start.16 = (bf16[4,128,1024]{2,1,0:T(8,128)(2,1)}, bf16[4,128,1024]{2,1,0:T(8,128)(2,1)}, u32[]{:S(2)}, u32[]{:S(2)}) collective-permute-start(bf16[4,128,1024]{2,1,0:T(8,128)(2,1)} %collective-permute-done.15.refs_14_), channel_id=1, source_target_pairs={{0,1},{1,0},{2,3},{3,2},{4,5},{5,4},{6,7},{7,6},{8,9},{9,8},{10,11... | collective-permute-start | bytes 3145736 | tf_op jit(solution)/shard_map/ppermute | solution.py:37
  132.4 8.2 %collective-permute-start.18 = (bf16[4,128,1024]{2,1,0:T(8,128)(2,1)}, bf16[4,128,1024]{2,1,0:T(8,128)(2,1)}, u32[]{:S(2)}, u32[]{:S(2)}) collective-permute-start(bf16[4,128,1024]{2,1,0:T(8,128)(2,1)} %collective-permute-done.17.refs_16_), channel_id=1, source_target_pairs={{0,1},{1,0},{2,3},{3,2},{4,5},{5,4},{6,7},{7,6},{8,9},{9,8},{10,11... | collective-permute-start | bytes 3145736 | tf_op jit(solution)/shard_map/ppermute | solution.py:37
  134.6 93.6 %collective-permute-start.1 = (bf16[24,128,128]{2,1,0:T(8,128)(2,1)}, bf16[24,128,128]{2,1,0:T(8,128)(2,1)}, u32[]{:S(2)}, u32[]{:S(2)}) collective-permute-start(bf16[24,128,128]{2,1,0:T(8,128)(2,1)} %broadcast_select_fusion.3.refs_1_), channel_id=1, source_target_pairs={{0,8},{1,9},{2,10},{3,11},{4,12},{5,13},{6,14},{7,15},{8,0},{9,1},... | collective-permute-start | bytes 2359304 | tf_op jit(solution)/shard_map/ppermute | solution.py:200

commit v3 on v2

--- a/solution.py
+++ b/solution.py
@@ -29,32 +29,61 @@
     return (columns[:, None] == source[None, :]).astype(jnp.bfloat16)
 
 
-def tree_gather(shard):
-    everyone = range(16)
-    centre = [i for i in everyone if i // 4 in (1, 2)]
-
-    def send(value, pairs):
-        return lax.ppermute(value, "tile", pairs)
-
+def together(*values):
+    return lax.optimization_barrier(values)
+
+
+def send(value, pairs):
+    return lax.ppermute(value, "tile", pairs)
+
+
+def flipped_bit(bit):
+    return [(i, i ^ bit) for i in range(16)]
+
+
+def staged_gather(shard, notes, tiles):
+    centre = [i for i in range(16) if i // 4 in (1, 2)]
     across = [(i, i ^ 12) for i in centre]
     outward = [(i, i ^ 4) for i in centre]
+    other_z, other_y, other_core, opposite = (flipped_bit(bit) for bit in (4, 2, 1, 8))
     me = lax.axis_index("tile")
     z = me // 4
     in_centre = (z == 1) | (z == 2)
-    near = send(shard, [(i, i ^ 4) for i in everyone])
-    first_centre = send(shard, across)
-    second_centre = send(near, across)
-    first = jnp.where(in_centre, first_centre, send(first_centre, outward))
-    second = jnp.where(in_centre, second_centre, send(second_centre, outward))
-    line = [shard, near, first, second]
-    other_line = [send(value, [(i, i ^ 2) for i in everyone]) for value in line]
-    buffers = []
-    for value in line + other_line:
-        buffers += [value, send(value, [(i, i ^ 1) for i in everyone])]
+
+    near = send(shard, other_z)
+    first = send(shard, across)
+    y_own = send(shard, other_y)
+    c_own = send(shard, other_core)
+    far_notes = send(notes, opposite)
+    near, first, y_own, c_own, far_notes, *tiles = together(near, first, y_own, c_own, far_notes, *tiles)
+
+    second = send(near, across)
+    first = jnp.where(in_centre, first, send(first, outward))
+    y_near = send(near, other_y)
+    c_near = send(near, other_core)
+    c_y_own = send(y_own, other_core)
+    second, first, y_near, c_near, c_y_own, *tiles = together(second, first, y_near, c_near, c_y_own, *tiles)
+
+    far_first = send(tiles[0], opposite)
+    second = jnp.where(in_centre, second, send(second, outward))
+    y_first = send(first, other_y)
+    c_first = send(first, other_core)
+    c_y_near = send(y_near, other_core)
+    second, y_first, c_first, c_y_near, *tiles = together(second, y_first, c_first, c_y_near, *tiles)
+
+    y_second = send(second, other_y)
+    c_second = send(second, other_core)
+    c_y_first = send(y_first, other_core)
+    y_second, c_second, c_y_first, *tiles = together(y_second, c_second, c_y_first, *tiles)
+
+    c_y_second = send(y_second, other_core)
+
+    buffers = [shard, c_own, near, c_near, first, c_first, second, c_second]
+    buffers += [y_own, c_y_own, y_near, c_y_near, y_first, c_y_first, y_second, c_y_second]
     low = z < 2
     zs = [z, z ^ 1, jnp.where(low, 2, 1), jnp.where(low, 3, 0)]
     owners = [4 * zs[k] + ((me & 3) ^ (2 * y + c)) for y in (0, 1) for k in range(4) for c in (0, 1)]
-    return buffers, jnp.stack(owners).astype(jnp.int32)
+    return buffers, jnp.stack(owners).astype(jnp.int32), far_notes, tiles, far_first
 
 
 def own_kernel(slots, rows, own_ids, far_ids, owners, tiles_refs, buffer_refs, perm_ref, sum_ref, flip_ref,
@@ -181,26 +210,32 @@
 
 def per_device(t2_tiles, t2_row, t2_col, integrals):
     peers = lax.axis_size("tile")
+    count = t2_col.shape[0]
+    need = count // REUSE
     opposite = [(source, (source + peers // 2) % peers) for source in range(peers)]
-    need = t2_col.shape[0] // REUSE
+    order = sorted_order(t2_col)
+    rows = jnp.take(t2_row, order)
+    ids = jnp.take(t2_col, order)[::REUSE]
+    cut = REUSE * (need - need // LAST)
+    tiles = [jnp.take(t2_tiles, order[:cut], axis=0), jnp.take(t2_tiles, order[cut:], axis=0)]
+    notes = jnp.concatenate([t2_row, t2_col])
     if peers == 16 and need == CAP * peers:
         slots = CAP
-        buffers, owners = tree_gather(integrals)
+        buffers, owners, notes, tiles, far_first = staged_gather(integrals, notes, tiles)
     else:
         slots = 0
         buffers = [lax.all_gather(integrals, "tile", axis=0, tiled=True)]
         owners = jnp.zeros((1,), jnp.int32)
-    order = sorted_order(t2_col)
-    rows = jnp.take(t2_row, order)
-    ids = jnp.take(t2_col, order)[::REUSE]
-    notes = lax.ppermute(jnp.concatenate([rows, ids]), "tile", opposite)
-    far_rows, far_ids = notes[: REUSE * need], notes[REUSE * need :]
-    cut = REUSE * (need - need // LAST)
-    tiles = [jnp.take(t2_tiles, order[:cut], axis=0), jnp.take(t2_tiles, order[cut:], axis=0)]
-    far_tiles = [lax.ppermute(part, "tile", opposite) for part in tiles]
+        notes = send(notes, opposite)
+        far_first = send(tiles[0], opposite)
+    far_order = sorted_order(notes[count:])
+    far_rows = jnp.take(notes[:count], far_order)
+    far_ids = jnp.take(notes[count:], far_order)[::REUSE]
     total, flipped = own_part(slots, rows, ids, far_ids, owners, tiles, buffers, flip_matrix(W))
-    total = far_part(0, far_rows, far_tiles[0], flipped, total, jnp.float32)
-    return far_part(cut, far_rows, far_tiles[1], flipped, total, jnp.bfloat16)
+    total, rest = together(total, tiles[1])
+    far_rest = send(rest, opposite)
+    total = far_part(0, far_rows, far_first, flipped, total, jnp.float32)
+    return far_part(cut, far_rows, far_rest, flipped, total, jnp.bfloat16)
 
 
 def solution(mesh):

time: 241 us -> 253 us (1.050)
  waiting for transfers between devices: 103 us -> 129 us
  starting transfers between devices: 39.6 us -> 21.6 us
  local copies, waits for them, and re-layouts: 8.51 us -> 13.3 us
    ppermute x17 -> x20, waiting for transfers between devices: 77.2 us -> 129 us  [send(): return lax.ppermute(value, 'tile', pairs)]
    ppermute x3 -> x0, waiting for transfers between devices: 25.5 us -> none  [the longest x2 24 us: per_device(): far_tiles = [lax.ppermute(part, 'tile', opposite) for part in tiles]]
    ppermute x3 -> x0, starting transfers between devices: 24 us -> none  [the longest x1 20.9 us: per_device(): notes = lax.ppermute(jnp.concatenate([rows, ids]), 'tile', opposite)]
    ppermute x17 -> x20, starting transfers between devices: 15.5 us -> 21.6 us  [send(): return lax.ppermute(value, 'tile', pairs)]
  transfers between devices with their start and end apart: 20 -> 20, of which waited for: 6 -> 6; matrix products, arithmetic and copies ran while one was open for 9% -> 9% of each run, Pallas kernels for 26% -> 25%
where the time goes in v3:
time: 253 us; the launch traced here: 252 us
  waiting for transfers between devices  129 us (51%)
  Pallas kernels  75.7 us (30%)
  starting transfers between devices  21.6 us (9%)
  local copies, waits for them, and re-layouts  13.3 us (5%)
  other arithmetic  12.4 us (5%)
    ppermute x20, waiting for transfers between devices, send(): return lax.ppermute(value, 'tile', pairs)  129 us
    pallas_call x1, Pallas kernels, own_part(): pl.pallas_call(kernel, in_specs=[pl.BlockSpec(memory_space=pltpu.SMEM)] *...  39 us
    pallas_call x2, Pallas kernels, far_part(): pl.pallas_call(kernel, grid_spec=pltpu.PrefetchScalarGridSpec(num_scalar_...  36.7 us
    ppermute x20, starting transfers between devices, send(): return lax.ppermute(value, 'tile', pairs)  21.6 us
  transfers between devices with their start and end apart: 20, of which 6 were waited for; matrix products, arithmetic and copies ran while one was open for 9% of the time, Pallas kernels for 25%

profile of v3, /device:TPU:0, one launch (start us, length us, event | category | flops | bytes accessed | tf_op | source)
XLA Modules:
  0.0 251.9 jit_solution(17507011552404835685)
XLA Ops:
  0.0 3.0 %collective-permute-start.2 = (bf16[4,128,1024]{2,1,0:T(8,128)(2,1)}, bf16[4,128,1024]{2,1,0:T(8,128)(2,1)}, u32[]{:S(2)}, u32[]{:S(2)}) collective-permute-start(bf16[4,128,1024]{2,1,0:T(8,128)(2,1)} %refs_2_.1), channel_id=1, source_target_pairs={{0,2},{1,3},{2,0},{3,1},{4,6},{5,7},{6,4},{7,5},{8,10},{9,11},{10,... | collective-permute-start | bytes 3145736 | tf_op jit(solution)/shard_map/ppermute | solution.py:37
  3.0 1.7 collective-permute-start.1
  4.6 3.5 %collective-permute-start = (bf16[4,128,1024]{2,1,0:T(8,128)(2,1)}, bf16[4,128,1024]{2,1,0:T(8,128)(2,1)}, u32[]{:S(2)}, u32[]{:S(2)}) collective-permute-start(bf16[4,128,1024]{2,1,0:T(8,128)(2,1)} %refs_2_.1), channel_id=1, source_target_pairs={{0,4},{1,5},{2,6},{3,7},{4,0},{5,1},{6,2},{7,3},{8,12},{9,13},{10,... | collective-permute-start | bytes 3145736 | tf_op jit(solution)/shard_map/ppermute | solution.py:37
  8.1 0.0 collective-permute-start.3
  8.1 0.7 pad_add_fusion
  8.8 0.7 collective-permute-start.4
  9.5 0.9 convert_reduce_fusion.1
  10.5 0.1 select_reduce_fusion.1
  10.6 0.1 compare_and_fusion.2
  10.7 1.6 gather_fusion.1
  12.3 2.4 gather_fusion
  14.7 3.4 %broadcast_select_fusion.refs_0_ = bf16[72,128,128]{2,1,0:T(8,128)(2,1)} fusion(bf16[72,128,128]{2,1,0:T(8,128)(2,1)} %gather_fusion, pred[72]{0:T(512)(128)(4,1)S(1)} %get-tuple-element.66), kind=kLoop, calls=%fused_computation.8 | loop fusion | flops 1179648 | bytes 4718664 | tf_op jit(solution)/shard_map/jit(_take)/select_n | solution.py:220
  18.1 1.0 broadcast_select_fusion.3.refs_1_
  19.2 11.5 %collective-permute-done.4 = s32[192]{0:T(256)S(1)} collective-permute-done((s32[192]{0:T(256)S(1)}, s32[192]{0:T(256)S(1)}, u32[]{:S(2)}, u32[]{:S(2)}) %collective-permute-start.4) | collective-permute-done | bytes 800 | tf_op jit(solution)/shard_map/ppermute | solution.py:37
  30.7 0.0 collective-permute-done.2.refs_10_
  30.7 0.0 collective-permute-done.1
  30.7 0.3 collective-permute-done.refs_4_
  31.0 1.3 collective-permute-start.6
  32.3 0.1 collective-permute-start.9
  32.4 0.5 collective-permute-start.8
  32.9 0.6 collective-permute-start.7
  33.5 1.7 collective-permute-start.5
  35.3 21.7 %collective-permute-done.6 = bf16[4,128,1024]{2,1,0:T(8,128)(2,1)} collective-permute-done((bf16[4,128,1024]{2,1,0:T(8,128)(2,1)}, bf16[4,128,1024]{2,1,0:T(8,128)(2,1)}, u32[]{:S(2)}, u32[]{:S(2)}) %collective-permute-start.6) | collective-permute-done | bytes 1048608 | tf_op jit(solution)/shard_map/ppermute | solution.py:37
  56.9 1.3 broadcast_select_fusion.2.refs_6_
  58.3 0.0 copy-start.1
  58.3 0.0 copy-start.2
  58.3 0.0 collective-permute-done.9.refs_11_
  58.3 0.0 collective-permute-done.7.refs_12_
  58.4 1.4 collective-permute-start.10
  59.8 0.1 collective-permute-start.13
  59.9 0.5 collective-permute-start.12
  60.4 0.6 collective-permute-start.11
  61.0 26.7 %collective-permute-done.10 = bf16[4,128,1024]{2,1,0:T(8,128)(2,1)S(1)} collective-permute-done((bf16[4,128,1024]{2,1,0:T(8,128)(2,1)}, bf16[4,128,1024]{2,1,0:T(8,128)(2,1)S(1)}, u32[]{:S(2)}, u32[]{:S(2)}) %collective-permute-start.10) | collective-permute-done | bytes 1048608 | tf_op jit(solution)/shard_map/ppermute | solution.py:37
  87.7 1.1 broadcast_select_fusion.1.refs_8_
  88.8 0.0 collective-permute-done.13.refs_13_
  88.8 0.0 collective-permute-done.12.refs_7_
  88.9 1.0 copy-done.6
  89.9 0.0 collective-permute-start.16
  89.9 0.4 copy-done.7
  90.2 0.1 collective-permute-start.15
  90.4 1.4 collective-permute-start.14
  91.8 2.1 collective-permute-start.19
  93.9 1.2 gather_fusion.4
  95.2 1.2 gather_fusion.3
  96.4 2.2 fusion.refs_18_
  98.6 17.5 %collective-permute-done.14.refs_16_ = bf16[4,128,1024]{2,1,0:T(8,128)(2,1)} collective-permute-done((bf16[4,128,1024]{2,1,0:T(8,128)(2,1)}, bf16[4,128,1024]{2,1,0:T(8,128)(2,1)}, u32[]{:S(2)}, u32[]{:S(2)}) %collective-permute-start.14) | collective-permute-done | bytes 1048608 | tf_op jit(solution)/shard_map/ppermute | solution.py:37
  116.1 0.5 broadcast_select_fusion.5
  116.6 0.6 slice.23.own_ids
  117.3 0.7 stack.67.owners
  118.0 0.1 fusion.14
  118.0 0.2 convert_reduce_fusion
  118.2 0.1 select_reduce_fusion
  118.3 1.2 gather_fusion.5
  119.6 1.2 gather_fusion.2
  120.8 0.6 broadcast_select_fusion.4
  121.4 0.6 slice.24.far_ids
  122.0 0.0 collective-permute-done.17.refs_17_
  122.0 39.0 %own_part.1 = (f32[16,128,1024]{2,1,0:T(8,128)}, bf16[32,128,1024]{2,1,0:T(8,128)(2,1)}) custom-call(s32[96]{0:T(128)} %get-tuple-element.73.rows, s32[32]{0:T(128)} %slice.23.own_ids, s32[32]{0:T(128)} %slice.24.far_ids, s32[16]{0:T(128)} %stack.67.owners, bf16[72,128,128]{2,1,0:T(8,128)(2,1)} %broadcast_select_fusion.refs_0_, ...), custom_call_target="tpu_custom_call" | custom-call | tf_op jit(solution)/shard_map/own_part/pallas_call | solution.py:145
  161.0 2.3 collective-permute-start.18
  163.3 50.9 %collective-permute-done.19.refs_1_ = bf16[72,128,128]{2,1,0:T(8,128)(2,1)} collective-permute-done((bf16[72,128,128]{2,1,0:T(8,128)(2,1)}, bf16[72,128,128]{2,1,0:T(8,128)(2,1)}, u32[]{:S(2)}, u32[]{:S(2)}) %collective-permute-start.19) | collective-permute-done | bytes 2359328 | tf_op jit(solution)/shard_map/ppermute | solution.py:37
  214.2 24.6 %far_part.2.refs_3_ = f32[16,128,1024]{2,1,0:T(8,128)} custom-call(s32[96]{0:T(128)} %get-tuple-element.71.refs_0_, bf16[72,128,128]{2,1,0:T(8,128)(2,1)} %collective-permute-done.19.refs_1_, bf16[32,128,1024]{2,1,0:T(8,128)(2,1)} %get-tuple-element.62.refs_2_, f32[16,128,1024]{2,1,0:T(8,128)} %get-tuple-element.63.refs_3_), custom_call_target="tpu_custom_call" | custom-call | tf_op jit(solution)/shard_map/far_part/pallas_call | solution.py:192
  238.8 0.0 collective-permute-done.18.refs_1_
  238.8 1.0 copy-done.8
  239.8 12.1 %far_part.3 = bf16[16,128,1024]{2,1,0:T(8,128)(2,1)} custom-call(s32[96]{0:T(128)} %get-tuple-element.71.refs_0_, bf16[24,128,128]{2,1,0:T(8,128)(2,1)} %copy-done.8, bf16[32,128,1024]{2,1,0:T(8,128)(2,1)} %get-tuple-element.62.refs_2_, f32[16,128,1024]{2,1,0:T(8,128)} %far_part.2.refs_3_), custom_call_target="tpu_custom_call" | custom-call | tf_op jit(solution)/shard_map/far_part/pallas_call | solution.py:192
  (28 shorter events, 0.1 us)
Async XLA Ops:
  0.0 10.7 %copy-start = (bf16[96,128,128]{2,1,0:T(8,128)(2,1)S(1)}, bf16[96,128,128]{2,1,0:T(8,128)(2,1)}, u32[]{:S(2)}) copy-start(bf16[96,128,128]{2,1,0:T(8,128)(2,1)} %param.6) | copy-start | bytes 9437188
  0.0 30.7 %collective-permute-start.2 = (bf16[4,128,1024]{2,1,0:T(8,128)(2,1)}, bf16[4,128,1024]{2,1,0:T(8,128)(2,1)}, u32[]{:S(2)}, u32[]{:S(2)}) collective-permute-start(bf16[4,128,1024]{2,1,0:T(8,128)(2,1)} %refs_2_.1), channel_id=1, source_target_pairs={{0,2},{1,3},{2,0},{3,1},{4,6},{5,7},{6,4},{7,5},{8,10},{9,11},{10,... | collective-permute-start | bytes 3145736 | tf_op jit(solution)/shard_map/ppermute | solution.py:37
  3.0 27.8 %collective-permute-start.1 = (bf16[4,128,1024]{2,1,0:T(8,128)(2,1)}, bf16[4,128,1024]{2,1,0:T(8,128)(2,1)}, u32[]{:S(2)}, u32[]{:S(2)}) collective-permute-start(bf16[4,128,1024]{2,1,0:T(8,128)(2,1)} %refs_2_.1), channel_id=1, source_target_pairs={{4,8},{5,9},{6,10},{7,11},{8,4},{9,5},{10,6},{11,7},{20,24},{21,25... | collective-permute-start | bytes 3145736 | tf_op jit(solution)/shard_map/ppermute | solution.py:37
  4.6 26.4 %collective-permute-start = (bf16[4,128,1024]{2,1,0:T(8,128)(2,1)}, bf16[4,128,1024]{2,1,0:T(8,128)(2,1)}, u32[]{:S(2)}, u32[]{:S(2)}) collective-permute-start(bf16[4,128,1024]{2,1,0:T(8,128)(2,1)} %refs_2_.1), channel_id=1, source_target_pairs={{0,4},{1,5},{2,6},{3,7},{4,0},{5,1},{6,2},{7,3},{8,12},{9,13},{10,... | collective-permute-start | bytes 3145736 | tf_op jit(solution)/shard_map/ppermute | solution.py:37
  8.1 22.9 %collective-permute-start.3 = (bf16[4,128,1024]{2,1,0:T(8,128)(2,1)}, bf16[4,128,1024]{2,1,0:T(8,128)(2,1)}, u32[]{:S(2)}, u32[]{:S(2)}) collective-permute-start(bf16[4,128,1024]{2,1,0:T(8,128)(2,1)} %refs_2_.1), channel_id=1, source_target_pairs={{0,1},{1,0},{2,3},{3,2},{4,5},{5,4},{6,7},{7,6},{8,9},{9,8},{10,11... | collective-permute-start | bytes 3145736 | tf_op jit(solution)/shard_map/ppermute | solution.py:37
  8.8 21.9 %collective-permute-start.4 = (s32[192]{0:T(256)S(1)}, s32[192]{0:T(256)S(1)}, u32[]{:S(2)}, u32[]{:S(2)}) collective-permute-start(s32[192]{0:T(256)S(1)} %pad_add_fusion), channel_id=1, source_target_pairs={{0,8},{1,9},{2,10},{3,11},{4,12},{5,13},{6,14},{7,15},{8,0},{9,1},... | collective-permute-start | bytes 2312 | tf_op jit(solution)/shard_map/ppermute | solution.py:37
  14.7 3.4 %copy-start.5 = (bf16[24,128,128]{2,1,0:T(8,128)(2,1)S(1)}, bf16[24,128,128]{2,1,0:T(8,128)(2,1)}, u32[]{:S(2)}) copy-start(bf16[24,128,128]{2,1,0:T(8,128)(2,1)} %gather_fusion.1) | copy-start | bytes 2359300
  31.0 25.9 %collective-permute-start.6 = (bf16[4,128,1024]{2,1,0:T(8,128)(2,1)}, bf16[4,128,1024]{2,1,0:T(8,128)(2,1)}, u32[]{:S(2)}, u32[]{:S(2)}) collective-permute-start(bf16[4,128,1024]{2,1,0:T(8,128)(2,1)} %collective-permute-done.1), channel_id=1, source_target_pairs={{4,0},{5,1},{6,2},{7,3},{8,12},{9,13},{10,14},{11,15},{20,16},{21,... | collective-permute-start | bytes 3145736 | tf_op jit(solution)/shard_map/ppermute | solution.py:37
  32.3 26.0 %collective-permute-start.9 = (bf16[4,128,1024]{2,1,0:T(8,128)(2,1)}, bf16[4,128,1024]{2,1,0:T(8,128)(2,1)}, u32[]{:S(2)}, u32[]{:S(2)}) collective-permute-start(bf16[4,128,1024]{2,1,0:T(8,128)(2,1)} %collective-permute-done.2.refs_10_), channel_id=1, source_target_pairs={{0,1},{1,0},{2,3},{3,2},{4,5},{5,4},{6,7},{7,6},{8,9},{9,8},{10,11... | collective-permute-start | bytes 3145736 | tf_op jit(solution)/shard_map/ppermute | solution.py:37
  32.4 25.9 %collective-permute-start.8 = (bf16[4,128,1024]{2,1,0:T(8,128)(2,1)}, bf16[4,128,1024]{2,1,0:T(8,128)(2,1)}, u32[]{:S(2)}, u32[]{:S(2)}) collective-permute-start(bf16[4,128,1024]{2,1,0:T(8,128)(2,1)} %collective-permute-done.refs_4_), channel_id=1, source_target_pairs={{0,1},{1,0},{2,3},{3,2},{4,5},{5,4},{6,7},{7,6},{8,9},{9,8},{10,11... | collective-permute-start | bytes 3145736 | tf_op jit(solution)/shard_map/ppermute | solution.py:37
  32.9 25.5 %collective-permute-start.7 = (bf16[4,128,1024]{2,1,0:T(8,128)(2,1)}, bf16[4,128,1024]{2,1,0:T(8,128)(2,1)}, u32[]{:S(2)}, u32[]{:S(2)}) collective-permute-start(bf16[4,128,1024]{2,1,0:T(8,128)(2,1)} %collective-permute-done.refs_4_), channel_id=1, source_target_pairs={{0,2},{1,3},{2,0},{3,1},{4,6},{5,7},{6,4},{7,5},{8,10},{9,11},{10,... | collective-permute-start | bytes 3145736 | tf_op jit(solution)/shard_map/ppermute | solution.py:37
  33.5 24.8 %collective-permute-start.5 = (bf16[4,128,1024]{2,1,0:T(8,128)(2,1)}, bf16[4,128,1024]{2,1,0:T(8,128)(2,1)}, u32[]{:S(2)}, u32[]{:S(2)}) collective-permute-start(bf16[4,128,1024]{2,1,0:T(8,128)(2,1)} %collective-permute-done.refs_4_), channel_id=1, source_target_pairs={{4,8},{5,9},{6,10},{7,11},{8,4},{9,5},{10,6},{11,7},{20,24},{21,25... | collective-permute-start | bytes 3145736 | tf_op jit(solution)/shard_map/ppermute | solution.py:37
  58.3 2.1 copy-start.3
  58.3 35.6 %copy-start.1 = (s32[96]{0:T(128)S(1)}, s32[96]{0:T(128)}, u32[]{:S(2)}) copy-start(s32[96]{0:T(128)} %param.8) | copy-start | bytes 1156
  58.3 36.8 %copy-start.2 = (s32[96]{0:T(128)S(1)}, s32[96]{0:T(128)}, u32[]{:S(2)}) copy-start(s32[96]{0:T(128)} %param.7) | copy-start | bytes 1156
  58.4 29.3 %collective-permute-start.10 = (bf16[4,128,1024]{2,1,0:T(8,128)(2,1)}, bf16[4,128,1024]{2,1,0:T(8,128)(2,1)S(1)}, u32[]{:S(2)}, u32[]{:S(2)}) collective-permute-start(bf16[4,128,1024]{2,1,0:T(8,128)(2,1)} %collective-permute-done.5), channel_id=1, source_target_pairs={{4,0},{5,1},{6,2},{7,3},{8,12},{9,13},{10,14},{11,15},{20,16},{21,... | collective-permute-start | bytes 3145736 | tf_op jit(solution)/shard_map/ppermute | solution.py:37
  59.8 29.1 %collective-permute-start.13 = (bf16[4,128,1024]{2,1,0:T(8,128)(2,1)}, bf16[4,128,1024]{2,1,0:T(8,128)(2,1)S(1)}, u32[]{:S(2)}, u32[]{:S(2)}) collective-permute-start(bf16[4,128,1024]{2,1,0:T(8,128)(2,1)} %collective-permute-done.7.refs_12_), channel_id=1, source_target_pairs={{0,1},{1,0},{2,3},{3,2},{4,5},{5,4},{6,7},{7,6},{8,9},{9,8},{10,11... | collective-permute-start | bytes 3145736 | tf_op jit(solution)/shard_map/ppermute | solution.py:37
  59.9 29.0 %collective-permute-start.12 = (bf16[4,128,1024]{2,1,0:T(8,128)(2,1)S(1)}, bf16[4,128,1024]{2,1,0:T(8,128)(2,1)S(1)}, u32[]{:S(2)}, u32[]{:S(2)}) collective-permute-start(bf16[4,128,1024]{2,1,0:T(8,128)(2,1)S(1)} %broadcast_select_fusion.2.refs_6_), channel_id=1, source_target_pairs={{0,1},{1,0},{2,3},{3,2},{4,5},{5,4},{6,7},{7,6},{8,9},{9,8},{10,11... | collective-permute-start | bytes 3145736 | tf_op jit(solution)/shard_map/ppermute | solution.py:37
  60.4 28.5 %collective-permute-start.11 = (bf16[4,128,1024]{2,1,0:T(8,128)(2,1)S(1)}, bf16[4,128,1024]{2,1,0:T(8,128)(2,1)}, u32[]{:S(2)}, u32[]{:S(2)}) collective-permute-start(bf16[4,128,1024]{2,1,0:T(8,128)(2,1)S(1)} %broadcast_select_fusion.2.refs_6_), channel_id=1, source_target_pairs={{0,2},{1,3},{2,0},{3,1},{4,6},{5,7},{6,4},{7,5},{8,10},{9,11},{10,... | collective-permute-start | bytes 3145736 | tf_op jit(solution)/shard_map/ppermute | solution.py:37
  88.8 1.0 copy-start.6
  88.8 1.4 copy-start.7
  89.9 8.8 %collective-permute-start.16 = (bf16[4,128,1024]{2,1,0:T(8,128)(2,1)}, bf16[4,128,1024]{2,1,0:T(8,128)(2,1)}, u32[]{:S(2)}, u32[]{:S(2)}) collective-permute-start(bf16[4,128,1024]{2,1,0:T(8,128)(2,1)} %collective-permute-done.11.refs_14_), channel_id=1, source_target_pairs={{0,1},{1,0},{2,3},{3,2},{4,5},{5,4},{6,7},{7,6},{8,9},{9,8},{10,11... | collective-permute-start | bytes 3145736 | tf_op jit(solution)/shard_map/ppermute | solution.py:37
  90.2 8.4 %collective-permute-start.15 = (bf16[4,128,1024]{2,1,0:T(8,128)(2,1)}, bf16[4,128,1024]{2,1,0:T(8,128)(2,1)}, u32[]{:S(2)}, u32[]{:S(2)}) collective-permute-start(bf16[4,128,1024]{2,1,0:T(8,128)(2,1)} %broadcast_select_fusion.1.refs_8_), channel_id=1, source_target_pairs={{0,1},{1,0},{2,3},{3,2},{4,5},{5,4},{6,7},{7,6},{8,9},{9,8},{10,11... | collective-permute-start | bytes 3145736 | tf_op jit(solution)/shard_map/ppermute | solution.py:37
  90.4 25.7 %collective-permute-start.14 = (bf16[4,128,1024]{2,1,0:T(8,128)(2,1)}, bf16[4,128,1024]{2,1,0:T(8,128)(2,1)}, u32[]{:S(2)}, u32[]{:S(2)}) collective-permute-start(bf16[4,128,1024]{2,1,0:T(8,128)(2,1)} %broadcast_select_fusion.1.refs_8_), channel_id=1, source_target_pairs={{0,2},{1,3},{2,0},{3,1},{4,6},{5,7},{6,4},{7,5},{8,10},{9,11},{10,... | collective-permute-start | bytes 3145736 | tf_op jit(solution)/shard_map/ppermute | solution.py:37
  91.8 122.5 %collective-permute-start.19 = (bf16[72,128,128]{2,1,0:T(8,128)(2,1)}, bf16[72,128,128]{2,1,0:T(8,128)(2,1)}, u32[]{:S(2)}, u32[]{:S(2)}) collective-permute-start(bf16[72,128,128]{2,1,0:T(8,128)(2,1)} %broadcast_select_fusion.refs_0_), channel_id=1, source_target_pairs={{0,8},{1,9},{2,10},{3,11},{4,12},{5,13},{6,14},{7,15},{8,0},{9,1},... | collective-permute-start | bytes 7077896 | tf_op jit(solution)/shard_map/ppermute | solution.py:37
  116.1 5.9 %collective-permute-start.17 = (bf16[4,128,1024]{2,1,0:T(8,128)(2,1)}, bf16[4,128,1024]{2,1,0:T(8,128)(2,1)}, u32[]{:S(2)}, u32[]{:S(2)}) collective-permute-start(bf16[4,128,1024]{2,1,0:T(8,128)(2,1)} %collective-permute-done.14.refs_16_), channel_id=1, source_target_pairs={{0,1},{1,0},{2,3},{3,2},{4,5},{5,4},{6,7},{7,6},{8,9},{9,8},{10,11... | collective-permute-start | bytes 3145736 | tf_op jit(solution)/shard_map/ppermute | solution.py:37
  122.0 39.0 %copy-start.4 = (bf16[24,128,128]{2,1,0:T(8,128)(2,1)S(1)}, bf16[24,128,128]{2,1,0:T(8,128)(2,1)}, u32[]{:S(2)}) copy-start(bf16[24,128,128]{2,1,0:T(8,128)(2,1)} %broadcast_select_fusion.3.refs_1_) | copy-start | bytes 2359300
  161.0 77.8 %collective-permute-start.18 = (bf16[24,128,128]{2,1,0:T(8,128)(2,1)S(1)}, bf16[24,128,128]{2,1,0:T(8,128)(2,1)S(1)}, u32[]{:S(2)}, u32[]{:S(2)}) collective-permute-start(bf16[24,128,128]{2,1,0:T(8,128)(2,1)S(1)} %copy-done.4), channel_id=1, source_target_pairs={{0,8},{1,9},{2,10},{3,11},{4,12},{5,13},{6,14},{7,15},{8,0},{9,1},... | collective-permute-start | bytes 2359304 | tf_op jit(solution)/shard_map/ppermute | solution.py:37
  238.8 1.0 copy-start.8

commit v4 on v0

v4 whole, which is shorter than its diff:
```python
import functools

import jax
import jax.numpy as jnp
from jax import lax
from jax.experimental import pallas as pl
from jax.experimental.pallas import tpu as pltpu
from jax.sharding import PartitionSpec as P

W = 32
PPD = 16
REUSE = 3
QUAD = 4
LAST = 8
COLUMNS = 256
MIB = 1024 * 1024
SMEM = pl.BlockSpec(memory_space=pltpu.SMEM)
VMEM = pl.BlockSpec(memory_space=pltpu.VMEM)
ANY = pl.BlockSpec(memory_space=pl.ANY)


def flip_matrix(width):
    columns = jnp.arange(width * width, dtype=jnp.int32)
    source = (columns % width) * width + columns // width
    return (columns[:, None] == source[None, :]).astype(jnp.bfloat16)


def tables_kernel(rows, cols, starts, tile_at, block_at, slots, cursor):
    count, total = rows.shape[0], slots.shape[0]

    @pl.loop(0, total)
    def _(block):
        slots[block] = 0

    for row in range(PPD):
        cursor[row] = 0

    @pl.loop(0, count)
    def _(tile):
        cursor[rows[tile]] += 1
        slots[cols[tile]] = 1

    place = jnp.int32(0)
    for row in range(PPD):
        size = cursor[row]
        starts[row] = place
        cursor[row] = place
        place += size
    starts[PPD] = place

    def number(block, used):
        named = slots[block]
        slots[block] = jnp.where(named > 0, used, -1)
        return used + named

    lax.fori_loop(0, total, number, jnp.int32(0))

    @pl.loop(0, count)
    def _(tile):
        row = rows[tile]
        position = cursor[row]
        cursor[row] = position + 1
        tile_at[position] = tile
        block_at[position] = slots[cols[tile]]


def tables(rows, cols, total):
    count = rows.shape[0]
    return pl.pallas_call(
        tables_kernel,
        in_specs=[SMEM] * 2,
        out_specs=[SMEM] * 4,
        out_shape=[jax.ShapeDtypeStruct((size,), jnp.int32) for size in (PPD + 1, count, count, total)],
        scratch_shapes=[pltpu.SMEM((PPD,), jnp.int32)],
        name="tables",
    )(rows, cols)


def sort_kernel(tile_at, tiles_ref, first_ref, rest_ref, first_sem, rest_sem):
    cut = first_ref.shape[0]

    @pl.loop(0, cut)
    def _(position):
        pltpu.make_async_copy(tiles_ref.at[tile_at[position]], first_ref.at[position], first_sem).start()

    @pl.loop(0, rest_ref.shape[0])
    def _(position):
        pltpu.make_async_copy(tiles_ref.at[tile_at[cut + position]], rest_ref.at[position], rest_sem).start()

    pltpu.make_async_copy(first_ref, first_ref, first_sem).wait()
    pltpu.make_async_copy(rest_ref, rest_ref, rest_sem).wait()


def sort_tiles(tile_at, tiles, cut):
    count, height, depth = tiles.shape
    return pl.pallas_call(
        sort_kernel,
        in_specs=[SMEM, ANY],
        out_specs=[ANY] * 2,
        out_shape=[jax.ShapeDtypeStruct((size, height, depth), tiles.dtype) for size in (cut, count - cut)],
        scratch_shapes=[pltpu.SemaphoreType.DMA] * 2,
        name="sort_tiles",
    )(tile_at, tiles)


def add_row(sum_ref, fresh, begin, end, tile_of, block_of):
    width = sum_ref.shape[1]

    @pl.loop(0, (end - begin + QUAD - 1) // QUAD)
    def _(turn):
        here = begin + turn * QUAD
        places = [jnp.minimum(here + part, end - 1) for part in range(QUAD)]
        left = [tile_of(places[0])]
        for part in range(1, QUAD):
            tile = tile_of(places[part])
            left.append(jnp.where(here + part < end, tile, jnp.zeros_like(tile)))
        left = jnp.concatenate(left, axis=1)
        for column in range(0, width, COLUMNS):
            window = pl.ds(column, COLUMNS)
            right = jnp.concatenate([block_of(place, window) for place in places], axis=0)
            product = jnp.dot(left, right, preferred_element_type=jnp.float32)
            if fresh:
                sum_ref[:, window] = jnp.where(turn == 0, 0.0, sum_ref[:, window]) + product
            else:
                sum_ref[:, window] += product


def own_kernel(counts, starts, tile_at, block_at, own_slots, far_slots, firsts, tiles_ref, perm_ref, *refs):
    pieces = refs[: len(counts)]
    sum_out, flip_out, own_blocks, far_blocks, sums, own_sems, far_sems, sum_sem, flip_sem = refs[len(counts) :]

    for slots, landing, sems in ((far_slots, far_blocks, far_sems), (own_slots, own_blocks, own_sems)):
        for number, (piece, count) in enumerate(zip(pieces, counts)):

            def fetch(offset, slots=slots, landing=landing, sems=sems, piece=piece, number=number):
                slot = slots[firsts[number] + offset]

                @pl.when(slot >= 0)
                def _():
                    pltpu.make_async_copy(piece.at[offset], landing.at[slot], sems.at[slot]).start()

            if count <= 8:
                for offset in range(count):
                    fetch(offset)
            else:
                pl.loop(0, count)(fetch)

    def arrived(landing, sems, slot):
        pltpu.make_async_copy(landing.at[slot], landing.at[slot], sems.at[slot]).wait()

    need = own_blocks.shape[0]

    @pl.loop(0, need)
    def _(slot):
        arrived(far_blocks, far_sems, slot)
        far_blocks[slot] = jnp.dot(
            far_blocks[slot], perm_ref[...], preferred_element_type=jnp.float32
        ).astype(jnp.bfloat16)
        pltpu.make_async_copy(far_blocks.at[slot], flip_out.at[slot], flip_sem).start()

    @pl.loop(0, need)
    def _(slot):
        arrived(own_blocks, own_sems, slot)

    @pl.loop(0, PPD)
    def _(row):
        begin, end = starts[row], starts[row + 1]

        @pl.when(begin == end)
        def _():
            sums[row] = jnp.zeros(sums.shape[1:], jnp.float32)

        add_row(
            sums.at[row],
            True,
            begin,
            end,
            lambda place: tiles_ref[tile_at[place]],
            lambda place, window: own_blocks[block_at[place], :, window],
        )
        pltpu.make_async_copy(sums.at[row], sum_out.at[row], sum_sem).start()

    pltpu.make_async_copy(far_blocks, flip_out, flip_sem).wait()
    pltpu.make_async_copy(sums, sum_out, sum_sem).wait()


def own_part(own_tables, far_slots, tiles, pieces, firsts):
    starts, tile_at, block_at, own_slots = own_tables
    count, height, _ = tiles.shape
    depth, width = pieces[0].shape[1:]
    need = count // REUSE
    counts = [piece.shape[0] for piece in pieces]
    return pl.pallas_call(
        functools.partial(own_kernel, counts),
        in_specs=[SMEM] * 6 + [VMEM] * 2 + [ANY] * len(pieces),
        out_specs=[ANY] * 2,
        out_shape=[
            jax.ShapeDtypeStruct((PPD, height, width), jnp.float32),
            jax.ShapeDtypeStruct((need, depth, width), jnp.bfloat16),
        ],
        scratch_shapes=[
            pltpu.VMEM((need, depth, width), jnp.bfloat16),
            pltpu.VMEM((need, depth, width), jnp.bfloat16),
            pltpu.VMEM((PPD, height, width), jnp.float32),
            pltpu.SemaphoreType.DMA((need,)),
            pltpu.SemaphoreType.DMA((need,)),
            pltpu.SemaphoreType.DMA,
            pltpu.SemaphoreType.DMA,
        ],
        compiler_params=pltpu.CompilerParams(vmem_limit_bytes=44 * MIB),
        name="own_part",
    )(starts, tile_at, block_at, own_slots, far_slots, firsts, tiles, flip_matrix(W), *pieces)


def far_first_kernel(starts, block_at, tiles_ref, sum_in, flip_in, sum_out, result, blocks, sums, rounded,
                     block_sem, row_sems, back_sem, out_sems):
    cut = tiles_ref.shape[0]
    pltpu.make_async_copy(flip_in, blocks, block_sem).start()
    for row in range(PPD):
        pltpu.make_async_copy(sum_in.at[row], sums.at[row], row_sems.at[row]).start()
    pltpu.make_async_copy(flip_in, blocks, block_sem).wait()

    @pl.loop(0, PPD)
    def _(row):
        pltpu.make_async_copy(sum_in.at[row], sums.at[row], row_sems.at[row]).wait()
        begin, stop = starts[row], starts[row + 1]
        end = jnp.minimum(stop, cut)
        add_row(
            sums.at[row],
            False,
            begin,
            end,
            lambda place: tiles_ref[place],
            lambda place, window: blocks[block_at[place], :, window],
        )

        @pl.when(stop <= cut)
        def _():
            rounded[row] = sums[row].astype(rounded.dtype)
            pltpu.make_async_copy(rounded.at[row], result.at[row], out_sems.at[row]).start()

        @pl.when((begin < cut) & (stop > cut))
        def _():
            copy = pltpu.make_async_copy(sums.at[row], sum_out.at[row], back_sem)
            copy.start()
            copy.wait()

    @pl.loop(0, PPD)
    def _(row):
        @pl.when(starts[row + 1] <= cut)
        def _():
            pltpu.make_async_copy(rounded.at[row], result.at[row], out_sems.at[row]).wait()


def far_first_part(far_tables, tiles, total, flipped):
    starts, _, block_at, _ = far_tables
    whole = total.shape
    return pl.pallas_call(
        far_first_kernel,
        in_specs=[SMEM] * 2 + [VMEM] + [ANY] * 2,
        out_specs=[ANY] * 2,
        out_shape=[jax.ShapeDtypeStruct(whole, jnp.float32), jax.ShapeDtypeStruct(whole, jnp.bfloat16)],
        input_output_aliases={3: 0},
        scratch_shapes=[
            pltpu.VMEM(flipped.shape, jnp.bfloat16),
            pltpu.VMEM(whole, jnp.float32),
            pltpu.VMEM(whole, jnp.bfloat16),
            pltpu.SemaphoreType.DMA,
            pltpu.SemaphoreType.DMA((PPD,)),
            pltpu.SemaphoreType.DMA,
            pltpu.SemaphoreType.DMA((PPD,)),
        ],
        compiler_params=pltpu.CompilerParams(vmem_limit_bytes=36 * MIB),
        name="far_first",
    )(starts, block_at, tiles, total, flipped)


def far_rest_kernel(cut, starts, block_at, tiles_ref, sum_in, flip_in, result_in, result, blocks, sums, rounded,
                    block_sem, row_sems, out_sems):
    del result_in
    count = tiles_ref.shape[0]

    @pl.loop(0, count)
    def _(number):
        pltpu.make_async_copy(flip_in.at[block_at[cut + number]], blocks.at[number], block_sem).start()

    def open_rows(action):
        @pl.loop(0, PPD)
        def _(row):
            @pl.when(starts[row + 1] > cut)
            def _():
                action(row)

    def load(row):
        return pltpu.make_async_copy(sum_in.at[row], sums.at[row], row_sems.at[row])

    def store(row):
        return pltpu.make_async_copy(rounded.at[row], result.at[row], out_sems.at[row])

    open_rows(lambda row: load(row).start())
    pltpu.make_async_copy(blocks, blocks, block_sem).wait()

    def finish(row):
        load(row).wait()
        add_row(
            sums.at[row],
            False,
            jnp.maximum(starts[row], cut),
            starts[row + 1],
            lambda place: tiles_ref[place - cut],
            lambda place, window: blocks[place - cut, :, window],
        )
        rounded[row] = sums[row].astype(rounded.dtype)
        store(row).start()

    open_rows(finish)
    open_rows(lambda row: store(row).wait())


def far_rest_part(far_tables, tiles, total, flipped, result):
    starts, _, block_at, _ = far_tables
    count = block_at.shape[0]
    whole = total.shape
    return pl.pallas_call(
        functools.partial(far_rest_kernel, count - tiles.shape[0]),
        in_specs=[SMEM] * 2 + [VMEM] + [ANY] * 3,
        out_specs=ANY,
        out_shape=jax.ShapeDtypeStruct(whole, result.dtype),
        input_output_aliases={5: 0},
        scratch_shapes=[
            pltpu.VMEM((tiles.shape[0],) + flipped.shape[1:], jnp.bfloat16),
            pltpu.VMEM(whole, jnp.float32),
            pltpu.VMEM(whole, jnp.bfloat16),
            pltpu.SemaphoreType.DMA,
            pltpu.SemaphoreType.DMA((PPD,)),
            pltpu.SemaphoreType.DMA((PPD,)),
        ],
        compiler_params=pltpu.CompilerParams(vmem_limit_bytes=36 * MIB),
        name="far_rest",
    )(starts, block_at, tiles, total, flipped, result)


def together(*values):
    return lax.optimization_barrier(values)


def send(value, pairs):
    return lax.ppermute(value, "tile", pairs)


def flipped_bit(bit):
    return [(i, i ^ bit) for i in range(16)]


def staged_gather(shard, notes, tiles):
    centre = [i for i in range(16) if i // 4 in (1, 2)]
    across = [(i, i ^ 12) for i in centre]
    outward = [(i, i ^ 4) for i in centre]
    other_z, other_y, other_core, opposite = (flipped_bit(bit) for bit in (4, 2, 1, 8))
    me = lax.axis_index("tile")
    z = me // 4
    in_centre = (z == 1) | (z == 2)

    near = send(shard, other_z)
    first = send(shard, across)
    y_own = send(shard, other_y)
    c_own = send(shard, other_core)
    far_notes = send(notes, opposite)
    near, first, y_own, c_own, far_notes, *tiles = together(near, first, y_own, c_own, far_notes, *tiles)

    second = send(near, across)
    first = jnp.where(in_centre, first, send(first, outward))
    y_near = send(near, other_y)
    c_near = send(near, other_core)
    c_y_own = send(y_own, other_core)
    second, first, y_near, c_near, c_y_own, *tiles = together(second, first, y_near, c_near, c_y_own, *tiles)

    far_first = send(tiles[0], opposite)
    second = jnp.where(in_centre, second, send(second, outward))
    y_first = send(first, other_y)
    c_first = send(first, other_core)
    c_y_near = send(y_near, other_core)
    second, y_first, c_first, c_y_near, *tiles = together(second, y_first, c_first, c_y_near, *tiles)

    y_second = send(second, other_y)
    c_second = send(second, other_core)
    c_y_first = send(y_first, other_core)
    y_second, c_second, c_y_first, *tiles = together(y_second, c_second, c_y_first, *tiles)

    half = y_second.shape[0] // 2
    c_y_second = [send(y_second[:half], other_core), send(y_second[half:], other_core)]

    buffers = [shard, c_own, near, c_near, first, c_first, second, c_second]
    buffers += [y_own, c_y_own, y_near, c_y_near, y_first, c_y_first, y_second, *c_y_second]
    low = z < 2
    zs = [z, z ^ 1, jnp.where(low, 2, 1), jnp.where(low, 3, 0)]
    owners = [4 * zs[k] + ((me & 3) ^ (2 * y + c)) for y in (0, 1) for k in range(4) for c in (0, 1)]
    local = shard.shape[0]
    firsts = [owner * local for owner in owners]
    firsts.append(firsts[-1] + half)
    return buffers, jnp.stack(firsts).astype(jnp.int32), far_notes, tiles, far_first


def per_device(t2_tiles, t2_row, t2_col, integrals):
    peers = lax.axis_size("tile")
    count = t2_col.shape[0]
    block_total = peers * integrals.shape[0]
    opposite = [(source, (source + peers // 2) % peers) for source in range(peers)]
    own_tables = tables(t2_row, t2_col, block_total)
    tiles = sort_tiles(own_tables[1], t2_tiles, count - count // LAST)
    notes = jnp.stack([t2_row, t2_col])
    if peers == 16:
        pieces, firsts, notes, tiles, far_first = staged_gather(integrals, notes, tiles)
    else:
        pieces = [lax.all_gather(integrals, "tile", axis=0, tiled=True)]
        firsts = jnp.zeros((1,), jnp.int32)
        notes = send(notes, opposite)
        far_first = send(tiles[0], opposite)
    far_tables = tables(notes[0], notes[1], block_total)
    total, flipped = own_part(own_tables, far_tables[3], t2_tiles, pieces, firsts)
    total, rest = together(total, tiles[1])
    far_rest = send(rest, opposite)
    total, result = far_first_part(far_tables, far_first, total, flipped)
    return far_rest_part(far_tables, far_rest, total, flipped, result)


def solution(mesh):
    in_specs = (
        P(("groups", "tile"), None, None),
        P(("groups", "tile")),
        P(("groups", "tile")),
        P(("groups", "tile"), None, None),
    )
    out_specs = P(("groups", "tile"), None, None)
    return jax.shard_map(
        per_device, mesh=mesh, in_specs=in_specs, out_specs=out_specs, check_vma=False
    )
```

time: 823 us -> 299 us (0.36)
  waiting for transfers between devices: 510 us -> 99.8 us
  Pallas kernels: 0 us -> 154 us
  other arithmetic: 130 us -> 4.4 us
  local copies, waits for them, and re-layouts: 84.4 us -> 14.8 us
  matrix products: 44.8 us -> 0 us
  blocking collectives: 13.6 us -> 0 us
  starting transfers between devices: 38.5 us -> 25.5 us
    ppermute x1 -> x21, waiting for transfers between devices: 360 us -> 99.8 us  [send(): return lax.ppermute(value, 'tile', pairs)]
    pallas_call x0 -> x6, Pallas kernels: none -> 154 us  [the longest x1 97.1 us: sort_tiles(): pl.pallas_call(sort_kernel, in_specs=[SMEM, ANY], out_specs=[ANY] * 2, ou...]
    all_to_all x1 -> x0, waiting for transfers between devices: 150 us -> none  [per_device(): lax.all_to_all(replies, 'tile', split_axis=0, concat_axis=0, tiled=True)]
    scatter-add x12 -> x0, other arithmetic: 112 us -> none  [accumulate(): return (running.at[row_group].add(product), None)]
    gather x13 -> x0, local copies, waits for them, and re-layouts: 53.8 us -> none  [the longest x12 48.8 us: accumulate(): blocks = jnp.take(fetched, slot_group, axis=0)]
    dot_general x12 -> x0, matrix products: 44.8 us -> none  [accumulate(): jnp.einsum('tij,tjc->tic', tile_group, blocks, preferred_element_type=jnp...]
    all_to_all x1 -> x0, blocking collectives: 13.6 us -> none  [per_device(): lax.all_to_all(request, 'tile', split_axis=0, concat_axis=0, tiled=True)]
    unnamed x8 -> x48, local copies, waits for them, and re-layouts: 0.02 us -> 13.1 us
  transfers between devices with their start and end apart: 2 -> 21, of which waited for: 2 -> 6; matrix products, arithmetic and copies ran while one was open for 0% -> 2% of each run, Pallas kernels for 0% -> 50%
where the time goes in v4:
time: 299 us
  Pallas kernels  154 us (52%)
  waiting for transfers between devices  99.8 us (33%)
  starting transfers between devices  25.5 us (9%)
  local copies, waits for them, and re-layouts  14.8 us (5%)
  other arithmetic  4.4 us (1%)
    ppermute x21, waiting for transfers between devices, send(): return lax.ppermute(value, 'tile', pairs)  99.8 us
    pallas_call x1, Pallas kernels, sort_tiles(): pl.pallas_call(sort_kernel, in_specs=[SMEM, ANY], out_specs=[ANY] * 2, ou...  97.1 us
    pallas_call x1, Pallas kernels, own_part(): pl.pallas_call(functools.partial(own_kernel, counts), in_specs=[SMEM] * 6...  30 us
    ppermute x21, starting transfers between devices, send(): return lax.ppermute(value, 'tile', pairs)  25.5 us
    pallas_call x1, Pallas kernels, far_first_part(): pl.pallas_call(far_first_kernel, in_specs=[SMEM] * 2 + [VMEM] + [ANY] * 2...  15.4 us
    unnamed x48, local copies, waits for them, and re-layouts  13.1 us
    pallas_call x2, Pallas kernels, tables(): pl.pallas_call(tables_kernel, in_specs=[SMEM] * 2, out_specs=[SMEM] * 4,...  8.03 us
  transfers between devices with their start and end apart: 21, of which 6 were waited for; matrix products, arithmetic and copies ran while one was open for 2% of the time, Pallas kernels for 50%

profile of v4, /device:TPU:0, one launch (start us, length us, event | category | flops | bytes accessed | tf_op | source)
XLA Modules:
  0.0 299.2 jit_solution(7451798879876152408)
XLA Ops:
  0.0 3.0 collective-permute-start.2
  3.0 0.7 collective-permute-start.1
  3.7 4.4 %collective-permute-start = (bf16[4,128,1024]{2,1,0:T(8,128)(2,1)}, bf16[4,128,1024]{2,1,0:T(8,128)(2,1)S(1)}, u32[]{:S(2)}, u32[]{:S(2)}) collective-permute-start(bf16[4,128,1024]{2,1,0:T(8,128)(2,1)} %refs_0_.1), channel_id=1, source_target_pairs={{0,4},{1,5},{2,6},{3,7},{4,0},{5,1},{6,2},{7,3},{8,12},{9,13},{10,... | collective-permute-start | bytes 3145736 | tf_op jit(solution)/shard_map/ppermute | solution.py:348
  8.1 0.0 collective-permute-start.3
  8.1 0.7 pad_add_fusion
  8.8 0.0 collective-permute-start.4
  8.8 4.0 %tables.2 = (s32[17]{0:T(128)}, s32[96]{0:T(128)}, s32[96]{0:T(128)}, s32[64]{0:T(128)}) custom-call(s32[96]{0:T(128)} %rows.1, s32[96]{0:T(128)} %cols.1), custom_call_target="tpu_custom_call" | custom-call | tf_op jit(solution)/shard_map/tables/pallas_call | solution.py:69
  12.8 97.1 %sort_tiles.1 = (bf16[84,128,128]{2,1,0:T(8,128)(2,1)}, bf16[12,128,128]{2,1,0:T(8,128)(2,1)}) custom-call(s32[96]{0:T(128)} %get-tuple-element.43.tile_at, bf16[96,128,128]{2,1,0:T(8,128)(2,1)} %tiles_ref.3), custom_call_target="tpu_custom_call" | custom-call | tf_op jit(solution)/shard_map/sort_tiles/pallas_call | solution.py:96
  109.9 0.0 collective-permute-done.4
  109.9 0.0 collective-permute-done.2.refs_8_
  109.9 0.0 collective-permute-done.1
  109.9 0.0 collective-permute-done.refs_2_
  109.9 0.0 collective-permute-done.3.refs_1_
  110.0 1.0 copy-done.4
  111.0 1.3 collective-permute-start.6
  112.3 0.6 collective-permute-start.9
  112.9 0.1 collective-permute-start.8
  112.9 0.5 collective-permute-start.7
  113.4 1.6 collective-permute-start.5
  115.1 23.5 %collective-permute-done.6 = bf16[4,128,1024]{2,1,0:T(8,128)(2,1)} collective-permute-done((bf16[4,128,1024]{2,1,0:T(8,128)(2,1)S(1)}, bf16[4,128,1024]{2,1,0:T(8,128)(2,1)}, u32[]{:S(2)}, u32[]{:S(2)}) %collective-permute-start.6) | collective-permute-done | bytes 1048608 | tf_op jit(solution)/shard_map/ppermute | solution.py:348
  138.6 1.3 broadcast_select_fusion.1.refs_4_
  139.9 0.0 copy-start.1
  140.0 0.0 collective-permute-done.9.refs_9_
  140.0 0.0 collective-permute-done.8.refs_3_
  140.0 0.0 collective-permute-done.7.refs_10_
  140.0 0.0 collective-permute-done.5
  140.0 1.4 collective-permute-start.10
  141.4 0.1 collective-permute-start.13
  141.5 0.5 collective-permute-start.12
  142.0 0.5 collective-permute-start.11
  142.5 5.6 %collective-permute-start.20 = (bf16[84,128,128]{2,1,0:T(8,128)(2,1)}, bf16[84,128,128]{2,1,0:T(8,128)(2,1)}, u32[]{:S(2)}, u32[]{:S(2)}) collective-permute-start(bf16[84,128,128]{2,1,0:T(8,128)(2,1)} %get-tuple-element.63), channel_id=1, source_target_pairs={{0,8},{1,9},{2,10},{3,11},{4,12},{5,13},{6,14},{7,15},{8,0},{9,1},... | collective-permute-start | bytes 8257544 | tf_op jit(solution)/shard_map/ppermute | solution.py:348
  148.1 21.1 %collective-permute-done.10 = bf16[4,128,1024]{2,1,0:T(8,128)(2,1)S(1)} collective-permute-done((bf16[4,128,1024]{2,1,0:T(8,128)(2,1)}, bf16[4,128,1024]{2,1,0:T(8,128)(2,1)S(1)}, u32[]{:S(2)}, u32[]{:S(2)}) %collective-permute-start.10) | collective-permute-done | bytes 1048608 | tf_op jit(solution)/shard_map/ppermute | solution.py:348
  169.2 0.1 broadcast_select_fusion.refs_6_
  169.3 0.0 collective-permute-done.13.refs_11_
  169.3 0.0 collective-permute-done.12.refs_5_
  169.3 1.0 copy-done.6
  170.3 0.0 collective-permute-done.11.refs_12_
  170.3 0.0 collective-permute-start.16
  170.3 0.5 collective-permute-start.15
  170.8 1.5 collective-permute-start.14
  172.3 0.6 collective-permute-done.16.refs_13_
  173.0 1.5 collective-permute-done.15.refs_7_
  174.5 1.0 copy-done.8
  175.5 20.5 %collective-permute-done.14.refs_14_ = bf16[4,128,1024]{2,1,0:T(8,128)(2,1)S(1)} collective-permute-done((bf16[4,128,1024]{2,1,0:T(8,128)(2,1)S(1)}, bf16[4,128,1024]{2,1,0:T(8,128)(2,1)S(1)}, u32[]{:S(2)}, u32[]{:S(2)}) %collective-permute-start.14) | collective-permute-done | bytes 1048608 | tf_op jit(solution)/shard_map/ppermute | solution.py:348
  196.0 1.0 copy-done.17
  197.0 1.1 fusion.10
  198.1 0.5 collective-permute-start.17
  198.6 0.1 stack.83.firsts
  198.7 2.3 fusion.perm_ref
  200.9 0.6 slice_bitcast_fusion
  201.5 4.0 %tables.3 = (s32[17]{0:T(128)}, s32[96]{0:T(128)}, s32[96]{0:T(128)}, s32[64]{0:T(128)}) custom-call(s32[96]{0:T(128)} %get-tuple-element.84.rows, s32[96]{0:T(128)} %get-tuple-element.83.cols), custom_call_target="tpu_custom_call" | custom-call | tf_op jit(solution)/shard_map/tables/pallas_call | solution.py:69
  205.5 0.0 collective-permute-done.17.refs_15_
  205.6 1.2 copy-done.3
  206.8 1.2 copy-done.5
  208.1 1.2 copy-done.7
  209.3 1.2 copy-done.9
  210.5 0.6 copy-done.16
  211.1 30.0 %own_part.1 = (f32[16,128,1024]{2,1,0:T(8,128)}, bf16[32,128,1024]{2,1,0:T(8,128)(2,1)}) custom-call(s32[17]{0:T(128)S(1)} %copy-done.13, s32[96]{0:T(128)S(1)} %copy-done.12, s32[96]{0:T(128)S(1)} %copy-done.14, s32[64]{0:T(128)S(1)} %copy-done.15, s32[64]{0:T(128)S(1)} %copy-done.16, s32[17]{0:T(128)S(1)} %stack.83.firsts, ...), custom_call_target="tpu_custom_call" | custom-call | tf_op jit(solution)/shard_map/own_part/pallas_call | solution.py:193
  241.1 2.7 collective-permute-start.19
  243.8 32.6 %collective-permute-done.20.tiles_ref = bf16[84,128,128]{2,1,0:T(8,128)(2,1)} collective-permute-done((bf16[84,128,128]{2,1,0:T(8,128)(2,1)}, bf16[84,128,128]{2,1,0:T(8,128)(2,1)}, u32[]{:S(2)}, u32[]{:S(2)}) %collective-permute-start.20) | collective-permute-done | bytes 2752544 | tf_op jit(solution)/shard_map/ppermute | solution.py:348
  276.4 3.5 %copy-done = f32[16,128,1024]{2,1,0:T(8,128)S(1)} copy-done((f32[16,128,1024]{2,1,0:T(8,128)S(1)}, f32[16,128,1024]{2,1,0:T(8,128)}, u32[]{:S(2)}) %copy-start) | copy-done | bytes 8388632
  279.9 15.4 %far_first.1 = (f32[16,128,1024]{2,1,0:T(8,128)S(1)}, bf16[16,128,1024]{2,1,0:T(8,128)(2,1)}) custom-call(s32[17]{0:T(128)S(1)} %copy-done.10, s32[96]{0:T(128)S(1)} %copy-done.11, bf16[84,128,128]{2,1,0:T(8,128)(2,1)} %collective-permute-done.20.tiles_ref, f32[16,128,1024]{2,1,0:T(8,128)S(1)} %copy-done, ...), custom_call_target="tpu_custom_call", output_to_operand_aliasing={{0}: (3, {})} | custom-call | tf_op jit(solution)/shard_map/far_first/pallas_call | solution.py:258
  295.4 0.0 collective-permute-done.19.tiles_ref
  295.4 3.8 %far_rest.1 = bf16[16,128,1024]{2,1,0:T(8,128)(2,1)} custom-call(s32[17]{0:T(128)S(1)} %copy-done.10, s32[96]{0:T(128)S(1)} %copy-done.11, bf16[12,128,128]{2,1,0:T(8,128)(2,1)S(1)} %collective-permute-done.19.tiles_ref, f32[16,128,1024]{2,1,0:T(8,128)S(1)} %get-tuple-element.79.sum_in, ...), custom_call_target="tpu_custom_call", output_to_operand_aliasing={{}: (5, {})} | custom-call | tf_op jit(solution)/shard_map/far_rest/pallas_call | solution.py:324
  (41 shorter events, 0.1 us)
Async XLA Ops:
  0.0 109.9 %collective-permute-start.2 = (bf16[4,128,1024]{2,1,0:T(8,128)(2,1)}, bf16[4,128,1024]{2,1,0:T(8,128)(2,1)}, u32[]{:S(2)}, u32[]{:S(2)}) collective-permute-start(bf16[4,128,1024]{2,1,0:T(8,128)(2,1)} %refs_0_.1), channel_id=1, source_target_pairs={{0,2},{1,3},{2,0},{3,1},{4,6},{5,7},{6,4},{7,5},{8,10},{9,11},{10,... | collective-permute-start | bytes 3145736 | tf_op jit(solution)/shard_map/ppermute | solution.py:348
  3.0 107.0 %collective-permute-start.1 = (bf16[4,128,1024]{2,1,0:T(8,128)(2,1)}, bf16[4,128,1024]{2,1,0:T(8,128)(2,1)S(1)}, u32[]{:S(2)}, u32[]{:S(2)}) collective-permute-start(bf16[4,128,1024]{2,1,0:T(8,128)(2,1)} %refs_0_.1), channel_id=1, source_target_pairs={{4,8},{5,9},{6,10},{7,11},{8,4},{9,5},{10,6},{11,7},{20,24},{21,25... | collective-permute-start | bytes 3145736 | tf_op jit(solution)/shard_map/ppermute | solution.py:348
  3.7 106.2 %collective-permute-start = (bf16[4,128,1024]{2,1,0:T(8,128)(2,1)}, bf16[4,128,1024]{2,1,0:T(8,128)(2,1)S(1)}, u32[]{:S(2)}, u32[]{:S(2)}) collective-permute-start(bf16[4,128,1024]{2,1,0:T(8,128)(2,1)} %refs_0_.1), channel_id=1, source_target_pairs={{0,4},{1,5},{2,6},{3,7},{4,0},{5,1},{6,2},{7,3},{8,12},{9,13},{10,... | collective-permute-start | bytes 3145736 | tf_op jit(solution)/shard_map/ppermute | solution.py:348
  8.1 101.9 %collective-permute-start.3 = (bf16[4,128,1024]{2,1,0:T(8,128)(2,1)}, bf16[4,128,1024]{2,1,0:T(8,128)(2,1)S(1)}, u32[]{:S(2)}, u32[]{:S(2)}) collective-permute-start(bf16[4,128,1024]{2,1,0:T(8,128)(2,1)} %refs_0_.1), channel_id=1, source_target_pairs={{0,1},{1,0},{2,3},{3,2},{4,5},{5,4},{6,7},{7,6},{8,9},{9,8},{10,11... | collective-permute-start | bytes 3145736 | tf_op jit(solution)/shard_map/ppermute | solution.py:348
  8.8 101.1 %collective-permute-start.4 = (s32[2,96]{1,0:T(2,128)S(1)}, s32[2,96]{1,0:T(2,128)S(1)}, u32[]{:S(2)}, u32[]{:S(2)}) collective-permute-start(s32[2,96]{1,0:T(2,128)S(1)} %pad_add_fusion), channel_id=1, source_target_pairs={{0,8},{1,9},{2,10},{3,11},{4,12},{5,13},{6,14},{7,15},{8,0},{9,1},... | collective-permute-start | bytes 2312 | tf_op jit(solution)/shard_map/ppermute | solution.py:348
  109.9 38.2 %copy-start.2 = (bf16[4,128,1024]{2,1,0:T(8,128)(2,1)}, bf16[4,128,1024]{2,1,0:T(8,128)(2,1)S(1)}, u32[]{:S(2)}) copy-start(bf16[4,128,1024]{2,1,0:T(8,128)(2,1)S(1)} %collective-permute-done.refs_2_) | copy-start | bytes 3145732
  110.0 1.0 copy-start.4
  111.0 27.6 %collective-permute-start.6 = (bf16[4,128,1024]{2,1,0:T(8,128)(2,1)S(1)}, bf16[4,128,1024]{2,1,0:T(8,128)(2,1)}, u32[]{:S(2)}, u32[]{:S(2)}) collective-permute-start(bf16[4,128,1024]{2,1,0:T(8,128)(2,1)S(1)} %collective-permute-done.1), channel_id=1, source_target_pairs={{4,0},{5,1},{6,2},{7,3},{8,12},{9,13},{10,14},{11,15},{20,16},{21,... | collective-permute-start | bytes 3145736 | tf_op jit(solution)/shard_map/ppermute | solution.py:348
  112.3 27.7 %collective-permute-start.9 = (bf16[4,128,1024]{2,1,0:T(8,128)(2,1)}, bf16[4,128,1024]{2,1,0:T(8,128)(2,1)}, u32[]{:S(2)}, u32[]{:S(2)}) collective-permute-start(bf16[4,128,1024]{2,1,0:T(8,128)(2,1)} %collective-permute-done.2.refs_8_), channel_id=1, source_target_pairs={{0,1},{1,0},{2,3},{3,2},{4,5},{5,4},{6,7},{7,6},{8,9},{9,8},{10,11... | collective-permute-start | bytes 3145736 | tf_op jit(solution)/shard_map/ppermute | solution.py:348
  112.9 27.1 %collective-permute-start.8 = (bf16[4,128,1024]{2,1,0:T(8,128)(2,1)S(1)}, bf16[4,128,1024]{2,1,0:T(8,128)(2,1)}, u32[]{:S(2)}, u32[]{:S(2)}) collective-permute-start(bf16[4,128,1024]{2,1,0:T(8,128)(2,1)S(1)} %collective-permute-done.refs_2_), channel_id=1, source_target_pairs={{0,1},{1,0},{2,3},{3,2},{4,5},{5,4},{6,7},{7,6},{8,9},{9,8},{10,11... | collective-permute-start | bytes 3145736 | tf_op jit(solution)/shard_map/ppermute | solution.py:348
  112.9 27.0 %collective-permute-start.7 = (bf16[4,128,1024]{2,1,0:T(8,128)(2,1)S(1)}, bf16[4,128,1024]{2,1,0:T(8,128)(2,1)}, u32[]{:S(2)}, u32[]{:S(2)}) collective-permute-start(bf16[4,128,1024]{2,1,0:T(8,128)(2,1)S(1)} %collective-permute-done.refs_2_), channel_id=1, source_target_pairs={{0,2},{1,3},{2,0},{3,1},{4,6},{5,7},{6,4},{7,5},{8,10},{9,11},{10,... | collective-permute-start | bytes 3145736 | tf_op jit(solution)/shard_map/ppermute | solution.py:348
  113.4 26.5 %collective-permute-start.5 = (bf16[4,128,1024]{2,1,0:T(8,128)(2,1)S(1)}, bf16[4,128,1024]{2,1,0:T(8,128)(2,1)}, u32[]{:S(2)}, u32[]{:S(2)}) collective-permute-start(bf16[4,128,1024]{2,1,0:T(8,128)(2,1)S(1)} %collective-permute-done.refs_2_), channel_id=1, source_target_pairs={{4,8},{5,9},{6,10},{7,11},{8,4},{9,5},{10,6},{11,7},{20,24},{21,25... | collective-permute-start | bytes 3145736 | tf_op jit(solution)/shard_map/ppermute | solution.py:348
  139.9 65.7 %copy-start.1 = (bf16[4,128,1024]{2,1,0:T(8,128)(2,1)S(1)}, bf16[4,128,1024]{2,1,0:T(8,128)(2,1)}, u32[]{:S(2)}) copy-start(bf16[4,128,1024]{2,1,0:T(8,128)(2,1)} %refs_0_.1) | copy-start | bytes 3145732
  139.9 65.6 %copy-start.12 = (s32[96]{0:T(128)S(1)}, s32[96]{0:T(128)}, u32[]{:S(2)}) copy-start(s32[96]{0:T(128)} %get-tuple-element.43.tile_at) | copy-start | bytes 1156
  139.9 65.6 %copy-start.13 = (s32[17]{0:T(128)S(1)}, s32[17]{0:T(128)}, u32[]{:S(2)}) copy-start(s32[17]{0:T(128)} %get-tuple-element.49.starts) | copy-start | bytes 208
  139.9 65.6 %copy-start.14 = (s32[96]{0:T(128)S(1)}, s32[96]{0:T(128)}, u32[]{:S(2)}) copy-start(s32[96]{0:T(128)} %get-tuple-element.50.block_at) | copy-start | bytes 1156
  139.9 65.6 %copy-start.15 = (s32[64]{0:T(128)S(1)}, s32[64]{0:T(128)}, u32[]{:S(2)}) copy-start(s32[64]{0:T(128)} %get-tuple-element.51.own_slots) | copy-start | bytes 772
  140.0 29.2 %collective-permute-start.10 = (bf16[4,128,1024]{2,1,0:T(8,128)(2,1)}, bf16[4,128,1024]{2,1,0:T(8,128)(2,1)S(1)}, u32[]{:S(2)}, u32[]{:S(2)}) collective-permute-start(bf16[4,128,1024]{2,1,0:T(8,128)(2,1)} %collective-permute-done.5), channel_id=1, source_target_pairs={{4,0},{5,1},{6,2},{7,3},{8,12},{9,13},{10,14},{11,15},{20,16},{21,... | collective-permute-start | bytes 3145736 | tf_op jit(solution)/shard_map/ppermute | solution.py:348
  141.4 27.9 %collective-permute-start.13 = (bf16[4,128,1024]{2,1,0:T(8,128)(2,1)}, bf16[4,128,1024]{2,1,0:T(8,128)(2,1)S(1)}, u32[]{:S(2)}, u32[]{:S(2)}) collective-permute-start(bf16[4,128,1024]{2,1,0:T(8,128)(2,1)} %collective-permute-done.7.refs_10_), channel_id=1, source_target_pairs={{0,1},{1,0},{2,3},{3,2},{4,5},{5,4},{6,7},{7,6},{8,9},{9,8},{10,11... | collective-permute-start | bytes 3145736 | tf_op jit(solution)/shard_map/ppermute | solution.py:348
  141.5 27.8 %collective-permute-start.12 = (bf16[4,128,1024]{2,1,0:T(8,128)(2,1)S(1)}, bf16[4,128,1024]{2,1,0:T(8,128)(2,1)S(1)}, u32[]{:S(2)}, u32[]{:S(2)}) collective-permute-start(bf16[4,128,1024]{2,1,0:T(8,128)(2,1)S(1)} %broadcast_select_fusion.1.refs_4_), channel_id=1, source_target_pairs={{0,1},{1,0},{2,3},{3,2},{4,5},{5,4},{6,7},{7,6},{8,9},{9,8},{10,11... | collective-permute-start | bytes 3145736 | tf_op jit(solution)/shard_map/ppermute | solution.py:348
  142.0 28.3 %collective-permute-start.11 = (bf16[4,128,1024]{2,1,0:T(8,128)(2,1)S(1)}, bf16[4,128,1024]{2,1,0:T(8,128)(2,1)S(1)}, u32[]{:S(2)}, u32[]{:S(2)}) collective-permute-start(bf16[4,128,1024]{2,1,0:T(8,128)(2,1)S(1)} %broadcast_select_fusion.1.refs_4_), channel_id=1, source_target_pairs={{0,2},{1,3},{2,0},{3,1},{4,6},{5,7},{6,4},{7,5},{8,10},{9,11},{10,... | collective-permute-start | bytes 3145736 | tf_op jit(solution)/shard_map/ppermute | solution.py:348
  142.5 133.9 %collective-permute-start.20 = (bf16[84,128,128]{2,1,0:T(8,128)(2,1)}, bf16[84,128,128]{2,1,0:T(8,128)(2,1)}, u32[]{:S(2)}, u32[]{:S(2)}) collective-permute-start(bf16[84,128,128]{2,1,0:T(8,128)(2,1)} %get-tuple-element.63), channel_id=1, source_target_pairs={{0,8},{1,9},{2,10},{3,11},{4,12},{5,13},{6,14},{7,15},{8,0},{9,1},... | collective-permute-start | bytes 8257544 | tf_op jit(solution)/shard_map/ppermute | solution.py:348
  169.3 28.8 %copy-start.18 = (bf16[4,128,1024]{2,1,0:T(8,128)(2,1)}, bf16[4,128,1024]{2,1,0:T(8,128)(2,1)S(1)}, u32[]{:S(2)}) copy-start(bf16[4,128,1024]{2,1,0:T(8,128)(2,1)S(1)} %collective-permute-done.13.refs_11_) | copy-start | bytes 3145732
  169.3 1.0 copy-start.6
  170.3 27.7 %copy-start.19 = (bf16[4,128,1024]{2,1,0:T(8,128)(2,1)}, bf16[4,128,1024]{2,1,0:T(8,128)(2,1)S(1)}, u32[]{:S(2)}) copy-start(bf16[4,128,1024]{2,1,0:T(8,128)(2,1)S(1)} %collective-permute-done.11.refs_12_) | copy-start | bytes 3145732
  170.3 2.7 collective-permute-start.16
  170.3 4.2 %collective-permute-start.15 = (bf16[4,128,1024]{2,1,0:T(8,128)(2,1)S(1)}, bf16[4,128,1024]{2,1,0:T(8,128)(2,1)S(1)}, u32[]{:S(2)}, u32[]{:S(2)}) collective-permute-start(bf16[4,128,1024]{2,1,0:T(8,128)(2,1)S(1)} %broadcast_select_fusion.refs_6_), channel_id=1, source_target_pairs={{0,1},{1,0},{2,3},{3,2},{4,5},{5,4},{6,7},{7,6},{8,9},{9,8},{10,11... | collective-permute-start | bytes 3145736 | tf_op jit(solution)/shard_map/ppermute | solution.py:348
  170.8 25.1 %collective-permute-start.14 = (bf16[4,128,1024]{2,1,0:T(8,128)(2,1)S(1)}, bf16[4,128,1024]{2,1,0:T(8,128)(2,1)S(1)}, u32[]{:S(2)}, u32[]{:S(2)}) collective-permute-start(bf16[4,128,1024]{2,1,0:T(8,128)(2,1)S(1)} %broadcast_select_fusion.refs_6_), channel_id=1, source_target_pairs={{0,2},{1,3},{2,0},{3,1},{4,6},{5,7},{6,4},{7,5},{8,10},{9,11},{10,... | collective-permute-start | bytes 3145736 | tf_op jit(solution)/shard_map/ppermute | solution.py:348
  173.0 25.1 %copy-start.20 = (bf16[4,128,1024]{2,1,0:T(8,128)(2,1)}, bf16[4,128,1024]{2,1,0:T(8,128)(2,1)S(1)}, u32[]{:S(2)}) copy-start(bf16[4,128,1024]{2,1,0:T(8,128)(2,1)S(1)} %collective-permute-done.16.refs_13_) | copy-start | bytes 3145732
  174.5 1.0 copy-start.8
  196.0 1.0 copy-start.17
  198.1 7.5 %collective-permute-start.18 = (bf16[2,128,1024]{2,1,0:T(8,128)(2,1)}, bf16[2,128,1024]{2,1,0:T(8,128)(2,1)}, u32[]{:S(2)}, u32[]{:S(2)}) collective-permute-start(bf16[2,128,1024]{2,1,0:T(8,128)(2,1)} %get-tuple-element.81), channel_id=1, source_target_pairs={{0,1},{1,0},{2,3},{3,2},{4,5},{5,4},{6,7},{7,6},{8,9},{9,8},{10,11... | collective-permute-start | bytes 1572872 | tf_op jit(solution)/shard_map/ppermute | solution.py:348
  198.1 7.5 %collective-permute-start.17 = (bf16[2,128,1024]{2,1,0:T(8,128)(2,1)}, bf16[2,128,1024]{2,1,0:T(8,128)(2,1)}, u32[]{:S(2)}, u32[]{:S(2)}) collective-permute-start(bf16[2,128,1024]{2,1,0:T(8,128)(2,1)} %get-tuple-element.82), channel_id=1, source_target_pairs={{0,1},{1,0},{2,3},{3,2},{4,5},{5,4},{6,7},{7,6},{8,9},{9,8},{10,11... | collective-permute-start | bytes 1572872 | tf_op jit(solution)/shard_map/ppermute | solution.py:348
  205.6 1.2 copy-start.3
  206.8 1.2 copy-start.5
  208.1 1.2 copy-start.7
  209.3 1.2 copy-start.9
  210.5 0.6 copy-start.16
  211.1 30.1 %copy-start.21 = (bf16[12,128,128]{2,1,0:T(8,128)(2,1)S(1)}, bf16[12,128,128]{2,1,0:T(8,128)(2,1)}, u32[]{:S(2)}) copy-start(bf16[12,128,128]{2,1,0:T(8,128)(2,1)} %get-tuple-element.76) | copy-start | bytes 1179652
  211.1 65.3 %copy-start.10 = (s32[17]{0:T(128)S(1)}, s32[17]{0:T(128)}, u32[]{:S(2)}) copy-start(s32[17]{0:T(128)} %get-tuple-element.47.starts) | copy-start | bytes 208
  211.1 65.3 %copy-start.11 = (s32[96]{0:T(128)S(1)}, s32[96]{0:T(128)}, u32[]{:S(2)}) copy-start(s32[96]{0:T(128)} %get-tuple-element.48.block_at) | copy-start | bytes 1156
  241.1 54.2 %collective-permute-start.19 = (bf16[12,128,128]{2,1,0:T(8,128)(2,1)S(1)}, bf16[12,128,128]{2,1,0:T(8,128)(2,1)S(1)}, u32[]{:S(2)}, u32[]{:S(2)}) collective-permute-start(bf16[12,128,128]{2,1,0:T(8,128)(2,1)S(1)} %copy-done.21), channel_id=1, source_target_pairs={{0,8},{1,9},{2,10},{3,11},{4,12},{5,13},{6,14},{7,15},{8,0},{9,1},... | collective-permute-start | bytes 1179656 | tf_op jit(solution)/shard_map/ppermute | solution.py:348
  276.4 19.0 %slice-start = ((s8[8388608]{0:T(1024)(128)(4,1)}), s8[4194304]{0:T(1024)(128)(4,1)S(1)}, s32[]{:S(2)}) async-start(s8[8388608]{0:T(1024)(128)(4,1)} %bitcast.23), calls=%async_computation | async-start | bytes 8388608
  276.4 3.5 %copy-start = (f32[16,128,1024]{2,1,0:T(8,128)S(1)}, f32[16,128,1024]{2,1,0:T(8,128)}, u32[]{:S(2)}) copy-start(f32[16,128,1024]{2,1,0:T(8,128)} %get-tuple-element.77.sum_in) | copy-start | bytes 25165828
  279.9 15.4 %slice-start.1 = ((s8[8388608]{0:T(1024)(128)(4,1)}), s8[4194304]{0:T(1024)(128)(4,1)S(1)}, s32[]{:S(2)}) async-start(s8[8388608]{0:T(1024)(128)(4,1)} %bitcast.23), calls=%async_computation.1 | async-start | bytes 8388608

commit v5 on v4

v5 whole, which is shorter than its diff:
```python
import functools

import jax
import jax.numpy as jnp
from jax import lax
from jax.experimental import pallas as pl
from jax.experimental.pallas import tpu as pltpu
from jax.sharding import PartitionSpec as P

W = 32
PPD = 16
REUSE = 3
QUAD = 4
SHARES = (22, 20)
COLUMNS = 256
MIB = 1024 * 1024
SMEM = pl.BlockSpec(memory_space=pltpu.SMEM)
VMEM = pl.BlockSpec(memory_space=pltpu.VMEM)
ANY = pl.BlockSpec(memory_space=pl.ANY)


def flip_matrix(width):
    columns = jnp.arange(width * width, dtype=jnp.int32)
    source = (columns % width) * width + columns // width
    return (columns[:, None] == source[None, :]).astype(jnp.bfloat16)


def tables_kernel(rows, cols, starts, tile_at, block_at, slots, cursor):
    count, total, groups = rows.shape[0], slots.shape[0], cursor.shape[0]

    @pl.loop(0, total)
    def _(block):
        slots[block] = 0

    for row in range(groups):
        cursor[row] = 0

    @pl.loop(0, count)
    def _(tile):
        cursor[rows[tile]] += 1
        slots[cols[tile]] = 1

    place = jnp.int32(0)
    for row in range(groups):
        size = cursor[row]
        starts[row] = place
        cursor[row] = place
        place += size
    starts[groups] = place

    def number(block, used):
        named = slots[block]
        slots[block] = jnp.where(named > 0, used, -1)
        return used + named

    lax.fori_loop(0, total, number, jnp.int32(0))

    @pl.loop(0, count)
    def _(tile):
        row = rows[tile]
        position = cursor[row]
        cursor[row] = position + 1
        tile_at[position] = tile
        block_at[position] = slots[cols[tile]]


def tables(rows, cols, total, groups=PPD):
    count = rows.shape[0]
    return pl.pallas_call(
        tables_kernel,
        in_specs=[SMEM] * 2,
        out_specs=[SMEM] * 4,
        out_shape=[jax.ShapeDtypeStruct((size,), jnp.int32) for size in (groups + 1, count, count, total)],
        scratch_shapes=[pltpu.SMEM((groups,), jnp.int32)],
        name="tables",
    )(rows, cols)


def sort_kernel(tile_at, tiles_ref, *refs):
    parts, sems = refs[: len(refs) // 2], refs[len(refs) // 2 :]
    base = 0
    for part, sem in zip(parts, sems):

        @pl.loop(0, part.shape[0])
        def _(number, part=part, sem=sem, base=base):
            pltpu.make_async_copy(tiles_ref.at[tile_at[base + number]], part.at[number], sem).start()

        base += part.shape[0]
    for part, sem in zip(parts, sems):
        pltpu.make_async_copy(part, part, sem).wait()


def sort_tiles(tile_at, tiles, sizes):
    return pl.pallas_call(
        sort_kernel,
        in_specs=[SMEM, ANY],
        out_specs=[VMEM] * len(sizes),
        out_shape=[jax.ShapeDtypeStruct((size,) + tiles.shape[1:], tiles.dtype) for size in sizes],
        scratch_shapes=[pltpu.SemaphoreType.DMA] * len(sizes),
        compiler_params=pltpu.CompilerParams(vmem_limit_bytes=16 * MIB),
        name="sort_tiles",
    )(tile_at, tiles)


def add_row(sum_ref, begin, end, tile_of, block_of):
    width = sum_ref.shape[1]

    @pl.loop(0, (end - begin + QUAD - 1) // QUAD)
    def _(turn):
        here = begin + turn * QUAD
        places = [jnp.minimum(here + part, end - 1) for part in range(QUAD)]
        left = [tile_of(places[0])]
        for part in range(1, QUAD):
            tile = tile_of(places[part])
            left.append(jnp.where(here + part < end, tile, jnp.zeros_like(tile)))
        left = jnp.concatenate(left, axis=1)
        for column in range(0, width, COLUMNS):
            window = pl.ds(column, COLUMNS)
            right = jnp.concatenate([block_of(place, window) for place in places], axis=0)
            sum_ref[:, window] += jnp.dot(left, right, preferred_element_type=jnp.float32)


def own_kernel(counts, group, fresh, starts, tile_at, block_at, own_slots, far_slots, firsts, tiles_ref, perm_ref, *refs):
    pieces = refs[: len(counts)]
    refs = refs[len(counts) :]
    if not fresh:
        sum_in, refs = refs[0], refs[2:]
    sum_out, flip_out, own_blocks, far_blocks, sums, own_list, far_list, own_sems, far_sems, row_sems = refs

    if not fresh:
        for row in range(PPD):
            pltpu.make_async_copy(sum_in.at[row], sums.at[row], row_sems.at[row]).start()

    def fetch(slots, landing, sems, fetched):
        found = jnp.int32(0)
        for number, (piece, count) in enumerate(zip(pieces, counts)):

            def one(offset, found, piece=piece, number=number):
                slot = slots[firsts[number] + offset]

                @pl.when(slot >= 0)
                def _():
                    fetched[found] = slot
                    pltpu.make_async_copy(piece.at[offset], landing.at[slot], sems.at[slot]).start()

                return found + (slot >= 0).astype(jnp.int32)

            found = lax.fori_loop(0, count, one, found)
        return found

    far_found = fetch(far_slots, far_blocks, far_sems, far_list)
    own_found = fetch(own_slots, own_blocks, own_sems, own_list)

    def arrived(landing, sems, slot):
        pltpu.make_async_copy(landing.at[slot], landing.at[slot], sems.at[slot]).wait()

    def flip_store(slot):
        return pltpu.make_async_copy(far_blocks.at[slot], flip_out.at[slot], far_sems.at[slot])

    @pl.loop(0, far_found)
    def _(number):
        slot = far_list[number]
        arrived(far_blocks, far_sems, slot)
        far_blocks[slot] = jnp.dot(
            far_blocks[slot], perm_ref[...], preferred_element_type=jnp.float32
        ).astype(jnp.bfloat16)
        flip_store(slot).start()

    @pl.loop(0, own_found)
    def _(number):
        arrived(own_blocks, own_sems, own_list[number])

    def store(row):
        return pltpu.make_async_copy(sums.at[row], sum_out.at[row], row_sems.at[row])

    @pl.loop(0, PPD)
    def _(row):
        if fresh:
            sums[row] = jnp.zeros(sums.shape[1:], jnp.float32)
        else:
            arrived(sums, row_sems, row)
        add_row(
            sums.at[row],
            starts[group + row],
            starts[group + row + 1],
            lambda place: tiles_ref[tile_at[place]],
            lambda place, window: own_blocks[block_at[place], :, window],
        )
        store(row).start()

    @pl.loop(0, far_found)
    def _(number):
        flip_store(far_list[number]).wait()

    @pl.loop(0, PPD)
    def _(row):
        store(row).wait()


def own_part(own_tables, far_slots, tiles, pieces, firsts, perm, group=0, earlier=()):
    starts, tile_at, block_at, own_slots = own_tables
    count, height, _ = tiles.shape
    depth, width = pieces[0].shape[1:]
    need = count // REUSE
    counts = [piece.shape[0] for piece in pieces]
    operands = 8 + len(pieces)
    return pl.pallas_call(
        functools.partial(own_kernel, counts, group, not earlier),
        in_specs=[SMEM] * 6 + [VMEM] * 2 + [ANY] * (len(pieces) + len(earlier)),
        out_specs=[ANY] * 2,
        out_shape=[
            jax.ShapeDtypeStruct((PPD, height, width), jnp.float32),
            jax.ShapeDtypeStruct((need, depth, width), jnp.bfloat16),
        ],
        input_output_aliases={operands: 0, operands + 1: 1} if earlier else {},
        scratch_shapes=[
            pltpu.VMEM((need, depth, width), jnp.bfloat16),
            pltpu.VMEM((need, depth, width), jnp.bfloat16),
            pltpu.VMEM((PPD, height, width), jnp.float32),
            pltpu.SMEM((need,), jnp.int32),
            pltpu.SMEM((need,), jnp.int32),
            pltpu.SemaphoreType.DMA((need,)),
            pltpu.SemaphoreType.DMA((need,)),
            pltpu.SemaphoreType.DMA((PPD,)),
        ],
        compiler_params=pltpu.CompilerParams(vmem_limit_bytes=56 * MIB),
        name="own_part",
    )(starts, tile_at, block_at, own_slots, far_slots, firsts, tiles, perm, *pieces, *earlier)


def far_kernel(base, starts, block_at, tiles_ref, sum_in, flip_in, *refs):
    if base:
        refs = refs[1:]
    sum_out, result, blocks, sums, rounded, block_sem, row_sems, out_sems = refs
    count = tiles_ref.shape[0]
    stop = base + count

    @pl.loop(0, count)
    def _(number):
        pltpu.make_async_copy(flip_in.at[block_at[base + number]], blocks.at[number], block_sem).start()

    def each_row(action):
        @pl.loop(0, PPD)
        def _(row):
            first, last = starts[row], starts[row + 1]

            @pl.when(((last > base) if base else True) & ((last <= stop) | (first < stop)))
            def _():
                action(row, last <= stop)

    def load(row):
        return pltpu.make_async_copy(sum_in.at[row], sums.at[row], row_sems.at[row])

    def store(row):
        return pltpu.make_async_copy(rounded.at[row], result.at[row], out_sems.at[row])

    def keep(row):
        return pltpu.make_async_copy(sums.at[row], sum_out.at[row], out_sems.at[row])

    each_row(lambda row, complete: load(row).start())
    pltpu.make_async_copy(blocks, blocks, block_sem).wait()

    def add(row, complete):
        load(row).wait()
        add_row(
            sums.at[row],
            jnp.maximum(starts[row], base),
            jnp.minimum(starts[row + 1], stop),
            lambda place: tiles_ref[place - base],
            lambda place, window: blocks[place - base, :, window],
        )

        @pl.when(complete)
        def _():
            rounded[row] = sums[row].astype(rounded.dtype)
            store(row).start()

        @pl.when(jnp.logical_not(complete))
        def _():
            keep(row).start()

    def finish(row, complete):
        pl.when(complete)(lambda: store(row).wait())
        pl.when(jnp.logical_not(complete))(lambda: keep(row).wait())

    each_row(add)
    each_row(finish)


def far_part(base, far_tables, tiles, flipped, total, result=None):
    starts, _, block_at, _ = far_tables
    whole = total.shape
    count = tiles.shape[0]
    given = [] if result is None else [result]
    aliases = {3: 0, 5: 1} if given else {3: 0}
    return pl.pallas_call(
        functools.partial(far_kernel, base),
        in_specs=[SMEM] * 2 + [VMEM] + [ANY] * (2 + len(given)),
        out_specs=[ANY] * 2,
        out_shape=[jax.ShapeDtypeStruct(whole, jnp.float32), jax.ShapeDtypeStruct(whole, jnp.bfloat16)],
        input_output_aliases=aliases,
        scratch_shapes=[
            pltpu.VMEM((count,) + flipped.shape[1:], jnp.bfloat16),
            pltpu.VMEM(whole, jnp.float32),
            pltpu.VMEM(whole, jnp.bfloat16),
            pltpu.SemaphoreType.DMA,
            pltpu.SemaphoreType.DMA((PPD,)),
            pltpu.SemaphoreType.DMA((PPD,)),
        ],
        compiler_params=pltpu.CompilerParams(vmem_limit_bytes=36 * MIB),
        name="far_part",
    )(starts, block_at, tiles, total, flipped, *given)


def together(*values):
    return lax.optimization_barrier(values)


def send(value, pairs):
    return lax.ppermute(value, "tile", pairs)


def flipped_bit(bit):
    return [(i, i ^ bit) for i in range(16)]


def staged_part(tiles, rows, cols, shard):
    local = shard.shape[0]
    block_total = 16 * local
    centre = [i for i in range(16) if i // 4 in (1, 2)]
    across = [(i, i ^ 12) for i in centre]
    outward = [(i, i ^ 4) for i in centre]
    other_z, other_y, other_core, opposite = (flipped_bit(bit) for bit in (4, 2, 1, 8))
    me = lax.axis_index("tile")
    z = me // 4
    in_centre = (z == 1) | (z == 2)
    zs = [z, z ^ 1, jnp.where(z < 2, 2, 1), jnp.where(z < 2, 3, 0)]

    def owner(k, bits):
        return 4 * zs[k] + ((me & 3) ^ bits)

    def first_blocks(owners):
        return jnp.stack([value * local for value in owners]).astype(jnp.int32)

    col_owner = cols // local
    late = (col_owner // 4 == zs[3]) | (col_owner == owner(2, 3))
    keys = rows + PPD * late.astype(jnp.int32)

    near = send(shard, other_z)
    first = send(shard, across)
    y_own = send(shard, other_y)
    c_own = send(shard, other_core)
    notes = send(jnp.stack([rows, cols]), opposite)
    order = tables(rows, cols, block_total)[1]
    sizes = tile_parts(tiles.shape[0])
    parts = sort_tiles(order, tiles, sizes)
    near, first, y_own, c_own, notes, *parts = together(near, first, y_own, c_own, notes, *parts)

    far_parts = [send(parts[0], opposite)]
    second = send(near, across)
    first = jnp.where(in_centre, first, send(first, outward))
    y_near = send(near, other_y)
    c_near = send(near, other_core)
    c_y_own = send(y_own, other_core)
    own_tables = tables(keys, cols, block_total, 2 * PPD)
    far_tables = tables(notes[0], notes[1], block_total)
    second, first, y_near, c_near, c_y_own, *rest = together(
        second, first, y_near, c_near, c_y_own, *parts[1:], *own_tables, *far_tables
    )
    parts, own_tables, far_tables = rest[: len(parts) - 1], rest[-8:-4], rest[-4:]

    second = jnp.where(in_centre, second, send(second, outward))
    y_first = send(first, other_y)
    c_first = send(first, other_core)
    c_y_near = send(y_near, other_core)
    second, y_first, c_first, c_y_near, far_parts[0] = together(second, y_first, c_first, c_y_near, far_parts[0])

    far_parts.append(send(parts[0], opposite))
    y_second = send(second, other_y)
    c_second = send(second, other_core)
    c_y_first = send(y_first, other_core)
    perm = flip_matrix(W)
    pieces = [shard, c_own, near, c_near, first, c_first, y_own, c_y_own, y_near, c_y_near, y_first]
    owners = [owner(k, y + core) for y in (0, 2) for k in range(3) for core in (0, 1)][:11]
    early = own_part(own_tables, far_tables[3], tiles, pieces, first_blocks(owners), perm)
    y_second, c_second, c_y_first, *early = together(y_second, c_second, c_y_first, *early)

    c_y_second = send(y_second, other_core)
    pieces = [c_y_first, second, c_second, y_second, c_y_second]
    owners = [owner(2, 3)] + [owner(3, bits) for bits in range(4)]
    total, flipped = own_part(own_tables, far_tables[3], tiles, pieces, first_blocks(owners), perm, PPD, early)
    far_parts.append(send(parts[1], opposite))
    return far_products(far_tables, far_parts, flipped, total)


def tile_parts(count):
    sizes = [count * share // 48 for share in SHARES]
    return sizes + [count - sum(sizes)]


def far_products(far_tables, far_parts, flipped, total):
    base, result = 0, None
    for part in far_parts:
        total, result = far_part(base, far_tables, part, flipped, total, result)
        base += part.shape[0]
    return result


def per_device(t2_tiles, t2_row, t2_col, integrals):
    peers = lax.axis_size("tile")
    if peers == 16:
        return staged_part(t2_tiles, t2_row, t2_col, integrals)
    block_total = peers * integrals.shape[0]
    opposite = [(source, (source + peers // 2) % peers) for source in range(peers)]
    own_tables = tables(t2_row, t2_col, block_total)
    parts = sort_tiles(own_tables[1], t2_tiles, tile_parts(t2_tiles.shape[0]))
    notes = send(jnp.stack([t2_row, t2_col]), opposite)
    far_parts = [send(part, opposite) for part in parts]
    blocks = lax.all_gather(integrals, "tile", axis=0, tiled=True)
    far_tables = tables(notes[0], notes[1], block_total)
    firsts = jnp.zeros((1,), jnp.int32)
    total, flipped = own_part(own_tables, far_tables[3], t2_tiles, [blocks], firsts, flip_matrix(W))
    return far_products(far_tables, far_parts, flipped, total)


def solution(mesh):
    in_specs = (
        P(("groups", "tile"), None, None),
        P(("groups", "tile")),
        P(("groups", "tile")),
        P(("groups", "tile"), None, None),
    )
    out_specs = P(("groups", "tile"), None, None)
    return jax.shard_map(
        per_device, mesh=mesh, in_specs=in_specs, out_specs=out_specs, check_vma=False
    )
```

time: 299 us -> 233 us (0.78)
  Pallas kernels: 154 us -> 77.8 us
  waiting for transfers between devices: 99.8 us -> 115 us
  starting transfers between devices: 25.5 us -> 20.4 us
    pallas_call x4 -> x6, Pallas kernels: 146 us -> 65.7 us  [the longest x2 41.2 us: own_part(): pl.pallas_call(functools.partial(own_kernel, counts, group, not earlier),...]
    ppermute x21, waiting for transfers between devices: 99.8 us -> 115 us  [send(): return lax.ppermute(value, 'tile', pairs)]
    ppermute x21, starting transfers between devices: 25.5 us -> 20.4 us  [send(): return lax.ppermute(value, 'tile', pairs)]
    pallas_call x2 -> x3, Pallas kernels: 8.03 us -> 12.1 us  [tables(): pl.pallas_call(tables_kernel, in_specs=[SMEM] * 2, out_specs=[SMEM] * 4,...]
    unnamed x48 -> x20, local copies, waits for them, and re-layouts: 13.1 us -> 11.6 us
  transfers between devices with their start and end apart: 21 -> 21, of which waited for: 6 -> 7; matrix products, arithmetic and copies ran while one was open for 2% -> 4% of each run, Pallas kernels for 50% -> 32%
where the time goes in v5:
time: 233 us
  waiting for transfers between devices  115 us (49%)
  Pallas kernels  77.8 us (33%)
  starting transfers between devices  20.4 us (9%)
  local copies, waits for them, and re-layouts  13.4 us (6%)
  other arithmetic  6.52 us (3%)
    ppermute x21, waiting for transfers between devices, send(): return lax.ppermute(value, 'tile', pairs)  115 us
    pallas_call x2, Pallas kernels, own_part(): pl.pallas_call(functools.partial(own_kernel, counts, group, not earlier),...  41.2 us
    ppermute x21, starting transfers between devices, send(): return lax.ppermute(value, 'tile', pairs)  20.4 us
    pallas_call x3, Pallas kernels, far_part(): pl.pallas_call(functools.partial(far_kernel, base), in_specs=[SMEM] * 2 +...  19 us
    pallas_call x3, Pallas kernels, tables(): pl.pallas_call(tables_kernel, in_specs=[SMEM] * 2, out_specs=[SMEM] * 4,...  12.1 us
    unnamed x20, local copies, waits for them, and re-layouts  11.6 us
    pallas_call x1, Pallas kernels, sort_tiles(): pl.pallas_call(sort_kernel, in_specs=[SMEM, ANY], out_specs=[VMEM] * len(...  5.49 us
  transfers between devices with their start and end apart: 21, of which 7 were waited for; matrix products, arithmetic and copies ran while one was open for 4% of the time, Pallas kernels for 32%

profile of v5, /device:TPU:0, one launch (start us, length us, event | category | flops | bytes accessed | tf_op | source)
XLA Modules:
  0.0 233.0 jit_solution(10116300113207109970)
XLA Ops:
  0.0 3.0 %collective-permute-start.2 = (bf16[4,128,1024]{2,1,0:T(8,128)(2,1)}, bf16[4,128,1024]{2,1,0:T(8,128)(2,1)}, u32[]{:S(2)}, u32[]{:S(2)}) collective-permute-start(bf16[4,128,1024]{2,1,0:T(8,128)(2,1)} %refs_0_.1), channel_id=1, source_target_pairs={{0,2},{1,3},{2,0},{3,1},{4,6},{5,7},{6,4},{7,5},{8,10},{9,11},{10,... | collective-permute-start | bytes 3145736 | tf_op jit(solution)/shard_map/ppermute | solution.py:320
  3.0 1.6 collective-permute-start.1
  4.6 3.5 %collective-permute-start = (bf16[4,128,1024]{2,1,0:T(8,128)(2,1)}, bf16[4,128,1024]{2,1,0:T(8,128)(2,1)}, u32[]{:S(2)}, u32[]{:S(2)}) collective-permute-start(bf16[4,128,1024]{2,1,0:T(8,128)(2,1)} %refs_0_.1), channel_id=1, source_target_pairs={{0,4},{1,5},{2,6},{3,7},{4,0},{5,1},{6,2},{7,3},{8,12},{9,13},{10,... | collective-permute-start | bytes 3145736 | tf_op jit(solution)/shard_map/ppermute | solution.py:320
  8.1 0.0 collective-permute-start.3
  8.1 0.7 pad_add_fusion
  8.8 0.7 collective-permute-start.4
  9.5 4.0 %tables.3 = (s32[17]{0:T(128)}, s32[96]{0:T(128)}, s32[96]{0:T(128)}, s32[64]{0:T(128)}) custom-call(s32[96]{0:T(128)} %rows.1, s32[96]{0:T(128)} %cols.3), custom_call_target="tpu_custom_call" | custom-call | tf_op jit(solution)/shard_map/tables/pallas_call | solution.py:69
  13.5 0.0 copy-start.2
  13.5 1.9 copy-done.2
  15.4 0.7 copy-done.5
  16.0 5.5 %sort_tiles.1 = (bf16[44,128,128]{2,1,0:T(8,128)(2,1)S(1)}, bf16[40,128,128]{2,1,0:T(8,128)(2,1)S(1)}, bf16[12,128,128]{2,1,0:T(8,128)(2,1)S(1)}) custom-call(s32[96]{0:T(128)S(1)} %copy-done.5, bf16[96,128,128]{2,1,0:T(8,128)(2,1)S(1)} %copy-done.2), custom_call_target="tpu_custom_call" | custom-call | tf_op jit(solution)/shard_map/sort_tiles/pallas_call | solution.py:94
  21.5 1.1 copy-done.6
  22.6 8.1 %collective-permute-done.4 = s32[2,96]{1,0:T(2,128)S(1)} collective-permute-done((s32[2,96]{1,0:T(2,128)S(1)}, s32[2,96]{1,0:T(2,128)S(1)}, u32[]{:S(2)}, u32[]{:S(2)}) %collective-permute-start.4) | collective-permute-done | bytes 800 | tf_op jit(solution)/shard_map/ppermute | solution.py:320
  30.7 0.0 collective-permute-done.2.refs_6_
  30.7 0.0 collective-permute-done.1
  30.7 0.3 collective-permute-done.refs_2_
  31.0 0.0 collective-permute-done.3.refs_1_
  31.0 1.3 collective-permute-start.6
  32.3 0.1 collective-permute-start.9
  32.4 0.5 collective-permute-start.8
  32.9 0.5 collective-permute-start.7
  33.4 1.6 collective-permute-start.5
  35.0 1.2 fusion.10.rows
  36.2 4.0 %tables.4 = (s32[33]{0:T(128)}, s32[96]{0:T(128)}, s32[96]{0:T(128)}, s32[64]{0:T(128)}) custom-call(s32[96]{0:T(128)} %fusion.10.rows, s32[96]{0:T(128)} %cols.3), custom_call_target="tpu_custom_call" | custom-call | tf_op jit(solution)/shard_map/tables/pallas_call | solution.py:69
  40.3 0.5 slice_bitcast_fusion
  40.8 4.0 %tables.5 = (s32[17]{0:T(128)}, s32[96]{0:T(128)}, s32[96]{0:T(128)}, s32[64]{0:T(128)}) custom-call(s32[96]{0:T(128)} %get-tuple-element.110.rows, s32[96]{0:T(128)} %get-tuple-element.109.cols), custom_call_target="tpu_custom_call" | custom-call | tf_op jit(solution)/shard_map/tables/pallas_call | solution.py:69
  44.8 12.1 %collective-permute-done.6 = bf16[4,128,1024]{2,1,0:T(8,128)(2,1)} collective-permute-done((bf16[4,128,1024]{2,1,0:T(8,128)(2,1)}, bf16[4,128,1024]{2,1,0:T(8,128)(2,1)}, u32[]{:S(2)}, u32[]{:S(2)}) %collective-permute-start.6) | collective-permute-done | bytes 1048608 | tf_op jit(solution)/shard_map/ppermute | solution.py:320
  56.9 0.2 collective-permute-start.16
  57.1 1.3 broadcast_select_fusion.1.refs_4_
  58.5 0.0 collective-permute-done.9.refs_7_
  58.5 0.0 collective-permute-done.8.refs_3_
  58.5 0.0 collective-permute-done.7.refs_8_
  58.5 0.0 collective-permute-done.5
  58.5 1.3 collective-permute-start.12
  59.8 0.1 collective-permute-start.15
  59.9 0.5 collective-permute-start.14
  60.4 0.5 collective-permute-start.13
  60.9 86.6 %collective-permute-done.12 = bf16[4,128,1024]{2,1,0:T(8,128)(2,1)S(1)} collective-permute-done((bf16[4,128,1024]{2,1,0:T(8,128)(2,1)}, bf16[4,128,1024]{2,1,0:T(8,128)(2,1)S(1)}, u32[]{:S(2)}, u32[]{:S(2)}) %collective-permute-start.12) | collective-permute-done | bytes 1048608 | tf_op jit(solution)/shard_map/ppermute | solution.py:320
  147.5 1.1 broadcast_select_fusion.refs_1_
  148.6 0.0 collective-permute-done.15.refs_9_
  148.7 0.0 collective-permute-done.13.refs_10_
  148.7 0.9 copy-done.8
  149.6 0.0 collective-permute-start.19
  149.6 0.3 copy-done.9
  149.9 0.2 collective-permute-start.18
  150.1 1.5 collective-permute-start.17
  151.7 0.7 stack.83.firsts
  152.3 1.6 collective-permute-start.11
  153.9 2.2 fusion.perm_ref
  156.2 23.1 %own_part.2 = (f32[16,128,1024]{2,1,0:T(8,128)}, bf16[32,128,1024]{2,1,0:T(8,128)(2,1)}) custom-call(s32[33]{0:T(128)} %get-tuple-element.83.starts, s32[96]{0:T(128)} %get-tuple-element.84.tile_at, s32[96]{0:T(128)} %get-tuple-element.85.block_at, s32[64]{0:T(128)} %get-tuple-element.86.own_slots, s32[64]{0:T(128)} %get-tuple-element.87.far_slots, ...), custom_call_target="tpu_custom_call" | custom-call | tf_op jit(solution)/shard_map/own_part/pallas_call | solution.py:207
  179.3 0.0 collective-permute-done.19.refs_0_
  179.3 0.0 collective-permute-done.17.refs_3_
  179.3 0.1 collective-permute-start.20
  179.4 1.7 collective-permute-start.10
  181.1 0.6 stack.71.firsts
  181.7 0.7 collective-permute-done.20.refs_4_
  182.4 18.1 %own_part.3 = (f32[16,128,1024]{2,1,0:T(8,128)}, bf16[32,128,1024]{2,1,0:T(8,128)(2,1)}) custom-call(s32[33]{0:T(128)} %get-tuple-element.83.starts, s32[96]{0:T(128)} %get-tuple-element.84.tile_at, s32[96]{0:T(128)} %get-tuple-element.85.block_at, s32[64]{0:T(128)} %get-tuple-element.86.own_slots, ...), custom_call_target="tpu_custom_call", output_to_operand_aliasing={{0}: (13, {}), {1}: (14, {})} | custom-call | tf_op jit(solution)/shard_map/own_part/pallas_call | solution.py:207
  200.5 3.4 %copy-done = f32[16,128,1024]{2,1,0:T(8,128)S(1)} copy-done((f32[16,128,1024]{2,1,0:T(8,128)S(1)}, f32[16,128,1024]{2,1,0:T(8,128)}, u32[]{:S(2)}) %copy-start) | copy-done | bytes 8388632
  203.9 3.4 %copy-done.1 = bf16[32,128,1024]{2,1,0:T(8,128)(2,1)S(1)} copy-done((bf16[32,128,1024]{2,1,0:T(8,128)(2,1)S(1)}, bf16[32,128,1024]{2,1,0:T(8,128)(2,1)}, u32[]{:S(2)}) %copy-start.1) | copy-done | bytes 8388632
  207.3 7.9 %far_part.3 = (f32[16,128,1024]{2,1,0:T(8,128)S(1)}, bf16[16,128,1024]{2,1,0:T(8,128)(2,1)}) custom-call(s32[17]{0:T(128)S(1)} %copy-done.3, s32[96]{0:T(128)S(1)} %copy-done.4, bf16[44,128,128]{2,1,0:T(8,128)(2,1)S(1)} %collective-permute-done.16.tiles_ref, f32[16,128,1024]{2,1,0:T(8,128)S(1)} %copy-done, ...), custom_call_target="tpu_custom_call", output_to_operand_aliasing={{0}: (3, {})} | custom-call | tf_op jit(solution)/shard_map/far_part/pallas_call | solution.py:296
  215.2 5.9 %collective-permute-done.11.tiles_ref = bf16[40,128,128]{2,1,0:T(8,128)(2,1)S(1)} collective-permute-done((bf16[40,128,128]{2,1,0:T(8,128)(2,1)}, bf16[40,128,128]{2,1,0:T(8,128)(2,1)S(1)}, u32[]{:S(2)}, u32[]{:S(2)}) %collective-permute-start.11) | collective-permute-done | bytes 1310752 | tf_op jit(solution)/shard_map/ppermute | solution.py:320
  221.1 7.3 %far_part.4 = (f32[16,128,1024]{2,1,0:T(8,128)S(1)}, bf16[16,128,1024]{2,1,0:T(8,128)(2,1)}) custom-call(s32[17]{0:T(128)S(1)} %copy-done.3, s32[96]{0:T(128)S(1)} %copy-done.4, bf16[40,128,128]{2,1,0:T(8,128)(2,1)S(1)} %collective-permute-done.11.tiles_ref, ...), custom_call_target="tpu_custom_call", output_to_operand_aliasing={{0}: (3, {}), {1}: (5, {})} | custom-call | tf_op jit(solution)/shard_map/far_part/pallas_call | solution.py:296
  228.3 0.8 collective-permute-done.10.tiles_ref
  229.1 3.9 %far_part.5 = (f32[16,128,1024]{2,1,0:T(8,128)S(1)}, bf16[16,128,1024]{2,1,0:T(8,128)(2,1)}) custom-call(s32[17]{0:T(128)S(1)} %copy-done.3, s32[96]{0:T(128)S(1)} %copy-done.4, bf16[12,128,128]{2,1,0:T(8,128)(2,1)S(1)} %collective-permute-done.10.tiles_ref, ...), custom_call_target="tpu_custom_call", output_to_operand_aliasing={{0}: (3, {}), {1}: (5, {})} | custom-call | tf_op jit(solution)/shard_map/far_part/pallas_call | solution.py:296
  (16 shorter events, 0.0 us)
Async XLA Ops:
  0.0 30.7 %collective-permute-start.2 = (bf16[4,128,1024]{2,1,0:T(8,128)(2,1)}, bf16[4,128,1024]{2,1,0:T(8,128)(2,1)}, u32[]{:S(2)}, u32[]{:S(2)}) collective-permute-start(bf16[4,128,1024]{2,1,0:T(8,128)(2,1)} %refs_0_.1), channel_id=1, source_target_pairs={{0,2},{1,3},{2,0},{3,1},{4,6},{5,7},{6,4},{7,5},{8,10},{9,11},{10,... | collective-permute-start | bytes 3145736 | tf_op jit(solution)/shard_map/ppermute | solution.py:320
  3.0 27.8 %collective-permute-start.1 = (bf16[4,128,1024]{2,1,0:T(8,128)(2,1)}, bf16[4,128,1024]{2,1,0:T(8,128)(2,1)}, u32[]{:S(2)}, u32[]{:S(2)}) collective-permute-start(bf16[4,128,1024]{2,1,0:T(8,128)(2,1)} %refs_0_.1), channel_id=1, source_target_pairs={{4,8},{5,9},{6,10},{7,11},{8,4},{9,5},{10,6},{11,7},{20,24},{21,25... | collective-permute-start | bytes 3145736 | tf_op jit(solution)/shard_map/ppermute | solution.py:320
  4.6 26.4 %collective-permute-start = (bf16[4,128,1024]{2,1,0:T(8,128)(2,1)}, bf16[4,128,1024]{2,1,0:T(8,128)(2,1)}, u32[]{:S(2)}, u32[]{:S(2)}) collective-permute-start(bf16[4,128,1024]{2,1,0:T(8,128)(2,1)} %refs_0_.1), channel_id=1, source_target_pairs={{0,4},{1,5},{2,6},{3,7},{4,0},{5,1},{6,2},{7,3},{8,12},{9,13},{10,... | collective-permute-start | bytes 3145736 | tf_op jit(solution)/shard_map/ppermute | solution.py:320
  8.1 22.9 %collective-permute-start.3 = (bf16[4,128,1024]{2,1,0:T(8,128)(2,1)}, bf16[4,128,1024]{2,1,0:T(8,128)(2,1)}, u32[]{:S(2)}, u32[]{:S(2)}) collective-permute-start(bf16[4,128,1024]{2,1,0:T(8,128)(2,1)} %refs_0_.1), channel_id=1, source_target_pairs={{0,1},{1,0},{2,3},{3,2},{4,5},{5,4},{6,7},{7,6},{8,9},{9,8},{10,11... | collective-permute-start | bytes 3145736 | tf_op jit(solution)/shard_map/ppermute | solution.py:320
  8.8 21.9 %collective-permute-start.4 = (s32[2,96]{1,0:T(2,128)S(1)}, s32[2,96]{1,0:T(2,128)S(1)}, u32[]{:S(2)}, u32[]{:S(2)}) collective-permute-start(s32[2,96]{1,0:T(2,128)S(1)} %pad_add_fusion), channel_id=1, source_target_pairs={{0,8},{1,9},{2,10},{3,11},{4,12},{5,13},{6,14},{7,15},{8,0},{9,1},... | collective-permute-start | bytes 2312 | tf_op jit(solution)/shard_map/ppermute | solution.py:320
  13.5 1.9 copy-start.2
  15.4 0.7 copy-start.5
  21.5 1.1 copy-start.6
  31.0 25.9 %collective-permute-start.6 = (bf16[4,128,1024]{2,1,0:T(8,128)(2,1)}, bf16[4,128,1024]{2,1,0:T(8,128)(2,1)}, u32[]{:S(2)}, u32[]{:S(2)}) collective-permute-start(bf16[4,128,1024]{2,1,0:T(8,128)(2,1)} %collective-permute-done.1), channel_id=1, source_target_pairs={{4,0},{5,1},{6,2},{7,3},{8,12},{9,13},{10,14},{11,15},{20,16},{21,... | collective-permute-start | bytes 3145736 | tf_op jit(solution)/shard_map/ppermute | solution.py:320
  32.3 26.2 %collective-permute-start.9 = (bf16[4,128,1024]{2,1,0:T(8,128)(2,1)}, bf16[4,128,1024]{2,1,0:T(8,128)(2,1)}, u32[]{:S(2)}, u32[]{:S(2)}) collective-permute-start(bf16[4,128,1024]{2,1,0:T(8,128)(2,1)} %collective-permute-done.2.refs_6_), channel_id=1, source_target_pairs={{0,1},{1,0},{2,3},{3,2},{4,5},{5,4},{6,7},{7,6},{8,9},{9,8},{10,11... | collective-permute-start | bytes 3145736 | tf_op jit(solution)/shard_map/ppermute | solution.py:320
  32.4 26.1 %collective-permute-start.8 = (bf16[4,128,1024]{2,1,0:T(8,128)(2,1)}, bf16[4,128,1024]{2,1,0:T(8,128)(2,1)}, u32[]{:S(2)}, u32[]{:S(2)}) collective-permute-start(bf16[4,128,1024]{2,1,0:T(8,128)(2,1)} %collective-permute-done.refs_2_), channel_id=1, source_target_pairs={{0,1},{1,0},{2,3},{3,2},{4,5},{5,4},{6,7},{7,6},{8,9},{9,8},{10,11... | collective-permute-start | bytes 3145736 | tf_op jit(solution)/shard_map/ppermute | solution.py:320
  32.9 25.6 %collective-permute-start.7 = (bf16[4,128,1024]{2,1,0:T(8,128)(2,1)}, bf16[4,128,1024]{2,1,0:T(8,128)(2,1)}, u32[]{:S(2)}, u32[]{:S(2)}) collective-permute-start(bf16[4,128,1024]{2,1,0:T(8,128)(2,1)} %collective-permute-done.refs_2_), channel_id=1, source_target_pairs={{0,2},{1,3},{2,0},{3,1},{4,6},{5,7},{6,4},{7,5},{8,10},{9,11},{10,... | collective-permute-start | bytes 3145736 | tf_op jit(solution)/shard_map/ppermute | solution.py:320
  33.4 25.1 %collective-permute-start.5 = (bf16[4,128,1024]{2,1,0:T(8,128)(2,1)}, bf16[4,128,1024]{2,1,0:T(8,128)(2,1)}, u32[]{:S(2)}, u32[]{:S(2)}) collective-permute-start(bf16[4,128,1024]{2,1,0:T(8,128)(2,1)} %collective-permute-done.refs_2_), channel_id=1, source_target_pairs={{4,8},{5,9},{6,10},{7,11},{8,4},{9,5},{10,6},{11,7},{20,24},{21,25... | collective-permute-start | bytes 3145736 | tf_op jit(solution)/shard_map/ppermute | solution.py:320
  56.9 91.7 %collective-permute-start.16 = (bf16[44,128,128]{2,1,0:T(8,128)(2,1)S(1)}, bf16[44,128,128]{2,1,0:T(8,128)(2,1)S(1)}, u32[]{:S(2)}, u32[]{:S(2)}) collective-permute-start(bf16[44,128,128]{2,1,0:T(8,128)(2,1)S(1)} %get-tuple-element.81), channel_id=1, source_target_pairs={{0,8},{1,9},{2,10},{3,11},{4,12},{5,13},{6,14},{7,15},{8,0},{9,1},... | collective-permute-start | bytes 4325384 | tf_op jit(solution)/shard_map/ppermute | solution.py:320
  58.5 90.2 %copy-start.7 = (bf16[4,128,1024]{2,1,0:T(8,128)(2,1)}, bf16[4,128,1024]{2,1,0:T(8,128)(2,1)S(1)}, u32[]{:S(2)}) copy-start(bf16[4,128,1024]{2,1,0:T(8,128)(2,1)S(1)} %broadcast_select_fusion.1.refs_4_) | copy-start | bytes 3145732
  58.5 89.0 %collective-permute-start.12 = (bf16[4,128,1024]{2,1,0:T(8,128)(2,1)}, bf16[4,128,1024]{2,1,0:T(8,128)(2,1)S(1)}, u32[]{:S(2)}, u32[]{:S(2)}) collective-permute-start(bf16[4,128,1024]{2,1,0:T(8,128)(2,1)} %collective-permute-done.5), channel_id=1, source_target_pairs={{4,0},{5,1},{6,2},{7,3},{8,12},{9,13},{10,14},{11,15},{20,16},{21,... | collective-permute-start | bytes 3145736 | tf_op jit(solution)/shard_map/ppermute | solution.py:320
  59.8 88.8 %collective-permute-start.15 = (bf16[4,128,1024]{2,1,0:T(8,128)(2,1)}, bf16[4,128,1024]{2,1,0:T(8,128)(2,1)S(1)}, u32[]{:S(2)}, u32[]{:S(2)}) collective-permute-start(bf16[4,128,1024]{2,1,0:T(8,128)(2,1)} %collective-permute-done.7.refs_8_), channel_id=1, source_target_pairs={{0,1},{1,0},{2,3},{3,2},{4,5},{5,4},{6,7},{7,6},{8,9},{9,8},{10,11... | collective-permute-start | bytes 3145736 | tf_op jit(solution)/shard_map/ppermute | solution.py:320
  59.9 88.8 %collective-permute-start.14 = (bf16[4,128,1024]{2,1,0:T(8,128)(2,1)S(1)}, bf16[4,128,1024]{2,1,0:T(8,128)(2,1)S(1)}, u32[]{:S(2)}, u32[]{:S(2)}) collective-permute-start(bf16[4,128,1024]{2,1,0:T(8,128)(2,1)S(1)} %broadcast_select_fusion.1.refs_4_), channel_id=1, source_target_pairs={{0,1},{1,0},{2,3},{3,2},{4,5},{5,4},{6,7},{7,6},{8,9},{9,8},{10,11... | collective-permute-start | bytes 3145736 | tf_op jit(solution)/shard_map/ppermute | solution.py:320
  60.4 88.3 %collective-permute-start.13 = (bf16[4,128,1024]{2,1,0:T(8,128)(2,1)S(1)}, bf16[4,128,1024]{2,1,0:T(8,128)(2,1)}, u32[]{:S(2)}, u32[]{:S(2)}) collective-permute-start(bf16[4,128,1024]{2,1,0:T(8,128)(2,1)S(1)} %broadcast_select_fusion.1.refs_4_), channel_id=1, source_target_pairs={{0,2},{1,3},{2,0},{3,1},{4,6},{5,7},{6,4},{7,5},{8,10},{9,11},{10,... | collective-permute-start | bytes 3145736 | tf_op jit(solution)/shard_map/ppermute | solution.py:320
  148.6 1.0 copy-start.8
  148.7 1.3 copy-start.9
  149.6 29.7 %collective-permute-start.19 = (bf16[4,128,1024]{2,1,0:T(8,128)(2,1)}, bf16[4,128,1024]{2,1,0:T(8,128)(2,1)}, u32[]{:S(2)}, u32[]{:S(2)}) collective-permute-start(bf16[4,128,1024]{2,1,0:T(8,128)(2,1)} %collective-permute-done.13.refs_10_), channel_id=1, source_target_pairs={{0,1},{1,0},{2,3},{3,2},{4,5},{5,4},{6,7},{7,6},{8,9},{9,8},{10,11... | collective-permute-start | bytes 3145736 | tf_op jit(solution)/shard_map/ppermute | solution.py:320
  149.9 29.4 %collective-permute-start.18 = (bf16[4,128,1024]{2,1,0:T(8,128)(2,1)}, bf16[4,128,1024]{2,1,0:T(8,128)(2,1)}, u32[]{:S(2)}, u32[]{:S(2)}) collective-permute-start(bf16[4,128,1024]{2,1,0:T(8,128)(2,1)} %broadcast_select_fusion.refs_1_), channel_id=1, source_target_pairs={{0,1},{1,0},{2,3},{3,2},{4,5},{5,4},{6,7},{7,6},{8,9},{9,8},{10,11... | collective-permute-start | bytes 3145736 | tf_op jit(solution)/shard_map/ppermute | solution.py:320
  150.1 29.2 %collective-permute-start.17 = (bf16[4,128,1024]{2,1,0:T(8,128)(2,1)}, bf16[4,128,1024]{2,1,0:T(8,128)(2,1)}, u32[]{:S(2)}, u32[]{:S(2)}) collective-permute-start(bf16[4,128,1024]{2,1,0:T(8,128)(2,1)} %broadcast_select_fusion.refs_1_), channel_id=1, source_target_pairs={{0,2},{1,3},{2,0},{3,1},{4,6},{5,7},{6,4},{7,5},{8,10},{9,11},{10,... | collective-permute-start | bytes 3145736 | tf_op jit(solution)/shard_map/ppermute | solution.py:320
  152.3 68.7 %collective-permute-start.11 = (bf16[40,128,128]{2,1,0:T(8,128)(2,1)}, bf16[40,128,128]{2,1,0:T(8,128)(2,1)S(1)}, u32[]{:S(2)}, u32[]{:S(2)}) collective-permute-start(bf16[40,128,128]{2,1,0:T(8,128)(2,1)} %copy-done.6), channel_id=1, source_target_pairs={{0,8},{1,9},{2,10},{3,11},{4,12},{5,13},{6,14},{7,15},{8,0},{9,1},... | collective-permute-start | bytes 3932168 | tf_op jit(solution)/shard_map/ppermute | solution.py:320
  179.3 3.1 %collective-permute-start.20 = (bf16[4,128,1024]{2,1,0:T(8,128)(2,1)}, bf16[4,128,1024]{2,1,0:T(8,128)(2,1)}, u32[]{:S(2)}, u32[]{:S(2)}) collective-permute-start(bf16[4,128,1024]{2,1,0:T(8,128)(2,1)} %collective-permute-done.17.refs_3_), channel_id=1, source_target_pairs={{0,1},{1,0},{2,3},{3,2},{4,5},{5,4},{6,7},{7,6},{8,9},{9,8},{10,11... | collective-permute-start | bytes 3145736 | tf_op jit(solution)/shard_map/ppermute | solution.py:320
  179.4 49.7 %collective-permute-start.10 = (bf16[12,128,128]{2,1,0:T(8,128)(2,1)S(1)}, bf16[12,128,128]{2,1,0:T(8,128)(2,1)S(1)}, u32[]{:S(2)}, u32[]{:S(2)}) collective-permute-start(bf16[12,128,128]{2,1,0:T(8,128)(2,1)S(1)} %get-tuple-element.76), channel_id=1, source_target_pairs={{0,8},{1,9},{2,10},{3,11},{4,12},{5,13},{6,14},{7,15},{8,0},{9,1},... | collective-permute-start | bytes 1179656 | tf_op jit(solution)/shard_map/ppermute | solution.py:320
  181.7 18.7 %copy-start.3 = (s32[17]{0:T(128)S(1)}, s32[17]{0:T(128)}, u32[]{:S(2)}) copy-start(s32[17]{0:T(128)} %get-tuple-element.74.starts) | copy-start | bytes 208
  181.7 18.8 %copy-start.4 = (s32[96]{0:T(128)S(1)}, s32[96]{0:T(128)}, u32[]{:S(2)}) copy-start(s32[96]{0:T(128)} %get-tuple-element.75.block_at) | copy-start | bytes 1156
  200.5 3.4 %copy-start = (f32[16,128,1024]{2,1,0:T(8,128)S(1)}, f32[16,128,1024]{2,1,0:T(8,128)}, u32[]{:S(2)}) copy-start(f32[16,128,1024]{2,1,0:T(8,128)} %get-tuple-element.102.sum_in) | copy-start | bytes 25165828
  203.9 3.4 %copy-start.1 = (bf16[32,128,1024]{2,1,0:T(8,128)(2,1)S(1)}, bf16[32,128,1024]{2,1,0:T(8,128)(2,1)}, u32[]{:S(2)}) copy-start(bf16[32,128,1024]{2,1,0:T(8,128)(2,1)} %get-tuple-element.103.flip_in) | copy-start | bytes 25165828

commit v6 on v5

--- a/solution.py
+++ b/solution.py
@@ -11,7 +11,7 @@
 PPD = 16
 REUSE = 3
 QUAD = 4
-SHARES = (22, 20)
+SHARES = (24, 18)
 COLUMNS = 256
 MIB = 1024 * 1024
 SMEM = pl.BlockSpec(memory_space=pltpu.SMEM)
@@ -80,6 +80,7 @@
     parts, sems = refs[: len(refs) // 2], refs[len(refs) // 2 :]
     base = 0
     for part, sem in zip(parts, sems):
+        base %= tile_at.shape[0]
 
         @pl.loop(0, part.shape[0])
         def _(number, part=part, sem=sem, base=base):
@@ -228,12 +229,20 @@
     )(starts, tile_at, block_at, own_slots, far_slots, firsts, tiles, perm, *pieces, *earlier)
 
 
-def far_kernel(base, starts, block_at, tiles_ref, sum_in, flip_in, *refs):
-    if base:
-        refs = refs[1:]
-    sum_out, result, blocks, sums, rounded, block_sem, row_sems, out_sems = refs
+def far_kernel(base, sources, starts, block_at, chosen, *refs):
+    tile_refs, refs = refs[:sources], refs[sources:]
+    sum_in, flip_in = refs[:2]
+    refs = refs[3:] if base else refs[2:]
+    sum_out, result, tiles_ref, blocks, sums, rounded, tile_sem, block_sem, row_sems, out_sems = refs
     count = tiles_ref.shape[0]
     stop = base + count
+
+    for number, source in enumerate(tile_refs):
+
+        @pl.when(chosen[0] == number)
+        def _(source=source):
+            begin = base if source.shape[0] > count else 0
+            pltpu.make_async_copy(source.at[pl.ds(begin, count)], tiles_ref, tile_sem).start()
 
     @pl.loop(0, count)
     def _(number):
@@ -258,6 +267,7 @@
         return pltpu.make_async_copy(sums.at[row], sum_out.at[row], out_sems.at[row])
 
     each_row(lambda row, complete: load(row).start())
+    pltpu.make_async_copy(tiles_ref, tiles_ref, tile_sem).wait()
     pltpu.make_async_copy(blocks, blocks, block_sem).wait()
 
     def add(row, complete):
@@ -287,29 +297,32 @@
     each_row(finish)
 
 
-def far_part(base, far_tables, tiles, flipped, total, result=None):
+def far_part(base, far_tables, chosen, sources, flipped, total, result=None):
     starts, _, block_at, _ = far_tables
     whole = total.shape
-    count = tiles.shape[0]
+    tiles_shape = sources[-1].shape
     given = [] if result is None else [result]
-    aliases = {3: 0, 5: 1} if given else {3: 0}
+    operand = 3 + len(sources)
+    aliases = {operand: 0, operand + 2: 1} if given else {operand: 0}
     return pl.pallas_call(
-        functools.partial(far_kernel, base),
-        in_specs=[SMEM] * 2 + [VMEM] + [ANY] * (2 + len(given)),
+        functools.partial(far_kernel, base, len(sources)),
+        in_specs=[SMEM] * 3 + [ANY] * (len(sources) + 2 + len(given)),
         out_specs=[ANY] * 2,
         out_shape=[jax.ShapeDtypeStruct(whole, jnp.float32), jax.ShapeDtypeStruct(whole, jnp.bfloat16)],
         input_output_aliases=aliases,
         scratch_shapes=[
-            pltpu.VMEM((count,) + flipped.shape[1:], jnp.bfloat16),
+            pltpu.VMEM(tiles_shape, jnp.bfloat16),
+            pltpu.VMEM(tiles_shape[:1] + flipped.shape[1:], jnp.bfloat16),
             pltpu.VMEM(whole, jnp.float32),
             pltpu.VMEM(whole, jnp.bfloat16),
+            pltpu.SemaphoreType.DMA,
             pltpu.SemaphoreType.DMA,
             pltpu.SemaphoreType.DMA((PPD,)),
             pltpu.SemaphoreType.DMA((PPD,)),
         ],
         compiler_params=pltpu.CompilerParams(vmem_limit_bytes=36 * MIB),
         name="far_part",
-    )(starts, block_at, tiles, total, flipped, *given)
+    )(starts, block_at, chosen, *sources, total, flipped, *given)
 
 
 def together(*values):
@@ -330,6 +343,8 @@
     centre = [i for i in range(16) if i // 4 in (1, 2)]
     across = [(i, i ^ 12) for i in centre]
     outward = [(i, i ^ 4) for i in centre]
+    from_ends = [(i, i ^ 8) for i in range(16) if i not in centre]
+    from_centre = [(i, i ^ 8) for i in centre]
     other_z, other_y, other_core, opposite = (flipped_bit(bit) for bit in (4, 2, 1, 8))
     me = lax.axis_index("tile")
     z = me // 4
@@ -352,11 +367,10 @@
     c_own = send(shard, other_core)
     notes = send(jnp.stack([rows, cols]), opposite)
     order = tables(rows, cols, block_total)[1]
-    sizes = tile_parts(tiles.shape[0])
-    parts = sort_tiles(order, tiles, sizes)
-    near, first, y_own, c_own, notes, *parts = together(near, first, y_own, c_own, notes, *parts)
-
-    far_parts = [send(parts[0], opposite)]
+    sizes = [tiles.shape[0]] + tile_parts(tiles.shape[0])
+    whole, *parts = sort_tiles(order, tiles, sizes)
+    near, first, y_own, c_own, notes, whole, *parts = together(near, first, y_own, c_own, notes, whole, *parts)
+
     second = send(near, across)
     first = jnp.where(in_centre, first, send(first, outward))
     y_near = send(near, other_y)
@@ -364,18 +378,19 @@
     c_y_own = send(y_own, other_core)
     own_tables = tables(keys, cols, block_total, 2 * PPD)
     far_tables = tables(notes[0], notes[1], block_total)
-    second, first, y_near, c_near, c_y_own, *rest = together(
-        second, first, y_near, c_near, c_y_own, *parts[1:], *own_tables, *far_tables
+    second, first, y_near, c_near, c_y_own, whole, *rest = together(
+        second, first, y_near, c_near, c_y_own, whole, *parts, *own_tables, *far_tables
     )
-    parts, own_tables, far_tables = rest[: len(parts) - 1], rest[-8:-4], rest[-4:]
-
+    parts, own_tables, far_tables = rest[: len(parts)], rest[-8:-4], rest[-4:]
+
+    far_whole = send(whole, from_ends)
+    far_parts = [send(part, from_centre) for part in parts]
     second = jnp.where(in_centre, second, send(second, outward))
     y_first = send(first, other_y)
     c_first = send(first, other_core)
     c_y_near = send(y_near, other_core)
-    second, y_first, c_first, c_y_near, far_parts[0] = together(second, y_first, c_first, c_y_near, far_parts[0])
-
-    far_parts.append(send(parts[0], opposite))
+    second, y_first, c_first, c_y_near = together(second, y_first, c_first, c_y_near)
+
     y_second = send(second, other_y)
     c_second = send(second, other_core)
     c_y_first = send(y_first, other_core)
@@ -389,8 +404,8 @@
     pieces = [c_y_first, second, c_second, y_second, c_y_second]
     owners = [owner(2, 3)] + [owner(3, bits) for bits in range(4)]
     total, flipped = own_part(own_tables, far_tables[3], tiles, pieces, first_blocks(owners), perm, PPD, early)
-    far_parts.append(send(parts[1], opposite))
-    return far_products(far_tables, far_parts, flipped, total)
+    chosen = in_centre.astype(jnp.int32).reshape(1)
+    return far_products(far_tables, 1 - chosen, [[far_whole, part] for part in far_parts], flipped, total)
 
 
 def tile_parts(count):
@@ -398,11 +413,11 @@
     return sizes + [count - sum(sizes)]
 
 
-def far_products(far_tables, far_parts, flipped, total):
+def far_products(far_tables, chosen, far_parts, flipped, total):
     base, result = 0, None
-    for part in far_parts:
-        total, result = far_part(base, far_tables, part, flipped, total, result)
-        base += part.shape[0]
+    for sources in far_parts:
+        total, result = far_part(base, far_tables, chosen, sources, flipped, total, result)
+        base += sources[-1].shape[0]
     return result
 
 
@@ -418,9 +433,9 @@
     far_parts = [send(part, opposite) for part in parts]
     blocks = lax.all_gather(integrals, "tile", axis=0, tiled=True)
     far_tables = tables(notes[0], notes[1], block_total)
-    firsts = jnp.zeros((1,), jnp.int32)
-    total, flipped = own_part(own_tables, far_tables[3], t2_tiles, [blocks], firsts, flip_matrix(W))
-    return far_products(far_tables, far_parts, flipped, total)
+    zero = jnp.zeros((1,), jnp.int32)
+    total, flipped = own_part(own_tables, far_tables[3], t2_tiles, [blocks], zero, flip_matrix(W))
+    return far_products(far_tables, zero, [[part] for part in far_parts], flipped, total)
 
 
 def solution(mesh):

time: 233 us -> 213 us (0.914)
  waiting for transfers between devices: 115 us -> 75.2 us
  Pallas kernels: 77.8 us -> 90.8 us
  starting transfers between devices: 20.4 us -> 29.7 us
    ppermute x21 -> x22, waiting for transfers between devices: 115 us -> 75.2 us  [send(): return lax.ppermute(value, 'tile', pairs)]
    ppermute x21 -> x22, starting transfers between devices: 20.4 us -> 29.7 us  [send(): return lax.ppermute(value, 'tile', pairs)]
    pallas_call x3, Pallas kernels: 19 us -> 26.4 us  [far_part(): pl.pallas_call(functools.partial(far_kernel, base, len(sources)), in_spec...]
    pallas_call x1, Pallas kernels: 5.49 us -> 12.1 us  [sort_tiles(): pl.pallas_call(sort_kernel, in_specs=[SMEM, ANY], out_specs=[VMEM] * len(...]
    unnamed x20 -> x24, local copies, waits for them, and re-layouts: 11.6 us -> 9.29 us
  transfers between devices with their start and end apart: 21 -> 22, of which waited for: 7 -> 8; matrix products, arithmetic and copies ran while one was open for 4% -> 3% of each run, Pallas kernels for 32% -> 40%
where the time goes in v6:
time: 213 us; the launch traced here: 212 us
  Pallas kernels  90.8 us (43%)
  waiting for transfers between devices  75.2 us (35%)
  starting transfers between devices  29.7 us (14%)
  local copies, waits for them, and re-layouts  11.1 us (5%)
  other arithmetic  5.35 us (3%)
    ppermute x22, waiting for transfers between devices, send(): return lax.ppermute(value, 'tile', pairs)  75.2 us
    pallas_call x2, Pallas kernels, own_part(): pl.pallas_call(functools.partial(own_kernel, counts, group, not earlier),...  40.2 us
    ppermute x22, starting transfers between devices, send(): return lax.ppermute(value, 'tile', pairs)  29.7 us
    pallas_call x3, Pallas kernels, far_part(): pl.pallas_call(functools.partial(far_kernel, base, len(sources)), in_spec...  26.4 us
    pallas_call x3, Pallas kernels, tables(): pl.pallas_call(tables_kernel, in_specs=[SMEM] * 2, out_specs=[SMEM] * 4,...  12.1 us
    pallas_call x1, Pallas kernels, sort_tiles(): pl.pallas_call(sort_kernel, in_specs=[SMEM, ANY], out_specs=[VMEM] * len(...  12.1 us
    unnamed x24, local copies, waits for them, and re-layouts  9.29 us
  transfers between devices with their start and end apart: 22, of which 8 were waited for; matrix products, arithmetic and copies ran while one was open for 3% of the time, Pallas kernels for 40%

profile of v6, /device:TPU:0, one launch (start us, length us, event | category | flops | bytes accessed | tf_op | source)
XLA Modules:
  0.0 212.5 jit_solution(14316391329882124780)
XLA Ops:
  0.0 3.0 %collective-permute-start.2 = (bf16[4,128,1024]{2,1,0:T(8,128)(2,1)}, bf16[4,128,1024]{2,1,0:T(8,128)(2,1)}, u32[]{:S(2)}, u32[]{:S(2)}) collective-permute-start(bf16[4,128,1024]{2,1,0:T(8,128)(2,1)} %refs_0_.1), channel_id=1, source_target_pairs={{0,2},{1,3},{2,0},{3,1},{4,6},{5,7},{6,4},{7,5},{8,10},{9,11},{10,... | collective-permute-start | bytes 3145736 | tf_op jit(solution)/shard_map/ppermute | solution.py:333
  3.0 1.6 collective-permute-start.1
  4.6 3.5 %collective-permute-start = (bf16[4,128,1024]{2,1,0:T(8,128)(2,1)}, bf16[4,128,1024]{2,1,0:T(8,128)(2,1)}, u32[]{:S(2)}, u32[]{:S(2)}) collective-permute-start(bf16[4,128,1024]{2,1,0:T(8,128)(2,1)} %refs_0_.1), channel_id=1, source_target_pairs={{0,4},{1,5},{2,6},{3,7},{4,0},{5,1},{6,2},{7,3},{8,12},{9,13},{10,... | collective-permute-start | bytes 3145736 | tf_op jit(solution)/shard_map/ppermute | solution.py:333
  8.1 0.0 collective-permute-start.3
  8.1 0.7 pad_add_fusion
  8.8 0.7 collective-permute-start.4
  9.5 4.0 %tables.3 = (s32[17]{0:T(128)}, s32[96]{0:T(128)}, s32[96]{0:T(128)}, s32[64]{0:T(128)}) custom-call(s32[96]{0:T(128)} %rows.1, s32[96]{0:T(128)} %cols.3), custom_call_target="tpu_custom_call" | custom-call | tf_op jit(solution)/shard_map/tables/pallas_call | solution.py:69
  13.5 0.0 copy-start.1
  13.5 1.9 copy-done.1
  15.4 0.6 copy-done.4
  15.9 12.1 %sort_tiles.1 = (bf16[96,128,128]{2,1,0:T(8,128)(2,1)S(1)}, bf16[48,128,128]{2,1,0:T(8,128)(2,1)}, bf16[36,128,128]{2,1,0:T(8,128)(2,1)}, bf16[12,128,128]{2,1,0:T(8,128)(2,1)}) custom-call(s32[96]{0:T(128)S(1)} %copy-done.4, bf16[96,128,128]{2,1,0:T(8,128)(2,1)S(1)} %copy-done.1), custom_call_target="tpu_custom_call" | custom-call | tf_op jit(solution)/shard_map/sort_tiles/pallas_call | solution.py:95
  28.0 0.0 copy-start.5
  28.0 1.7 copy-done.5
  29.7 1.1 collective-permute-done.4
  30.7 0.0 collective-permute-done.2.refs_6_
  30.7 0.0 collective-permute-done.1
  30.7 0.3 collective-permute-done.refs_2_
  31.0 0.0 collective-permute-done.3.refs_1_
  31.0 1.3 collective-permute-start.6
  32.3 0.1 collective-permute-start.9
  32.4 0.5 collective-permute-start.8
  32.9 0.5 collective-permute-start.7
  33.4 1.6 collective-permute-start.5
  35.0 1.2 fusion.10.rows
  36.3 4.0 %tables.4 = (s32[33]{0:T(128)}, s32[96]{0:T(128)}, s32[96]{0:T(128)}, s32[64]{0:T(128)}) custom-call(s32[96]{0:T(128)} %fusion.10.rows, s32[96]{0:T(128)} %cols.3), custom_call_target="tpu_custom_call" | custom-call | tf_op jit(solution)/shard_map/tables/pallas_call | solution.py:69
  40.3 0.5 slice_bitcast_fusion
  40.8 4.0 %tables.5 = (s32[17]{0:T(128)}, s32[96]{0:T(128)}, s32[96]{0:T(128)}, s32[64]{0:T(128)}) custom-call(s32[96]{0:T(128)} %get-tuple-element.116.rows, s32[96]{0:T(128)} %get-tuple-element.115.cols), custom_call_target="tpu_custom_call" | custom-call | tf_op jit(solution)/shard_map/tables/pallas_call | solution.py:69
  44.9 12.2 %collective-permute-done.6 = bf16[4,128,1024]{2,1,0:T(8,128)(2,1)S(1)} collective-permute-done((bf16[4,128,1024]{2,1,0:T(8,128)(2,1)}, bf16[4,128,1024]{2,1,0:T(8,128)(2,1)S(1)}, u32[]{:S(2)}, u32[]{:S(2)}) %collective-permute-start.6) | collective-permute-done | bytes 1048608 | tf_op jit(solution)/shard_map/ppermute | solution.py:333
  57.1 0.1 broadcast_select_fusion.1.refs_4_
  57.2 0.0 collective-permute-done.9.refs_7_
  57.2 0.0 collective-permute-done.8.refs_3_
  57.3 1.1 collective-permute-done.7.refs_8_
  58.4 1.3 collective-permute-start.14
  59.7 0.1 collective-permute-start.17
  59.7 0.5 collective-permute-start.16
  60.2 0.6 collective-permute-start.15
  60.8 8.7 %collective-permute-start.10 = (bf16[96,128,128]{2,1,0:T(8,128)(2,1)}, bf16[96,128,128]{2,1,0:T(8,128)(2,1)S(1)}, u32[]{:S(2)}, u32[]{:S(2)}) collective-permute-start(bf16[96,128,128]{2,1,0:T(8,128)(2,1)} %copy-done.5), channel_id=1, source_target_pairs={{0,8},{1,9},{2,10},{3,11},{12,4},{13,5},{14,6},{15,7},{16,24},{17,... | collective-permute-start | bytes 9437192 | tf_op jit(solution)/shard_map/ppermute | solution.py:333
  69.5 17.4 %collective-permute-done.14 = bf16[4,128,1024]{2,1,0:T(8,128)(2,1)S(1)} collective-permute-done((bf16[4,128,1024]{2,1,0:T(8,128)(2,1)}, bf16[4,128,1024]{2,1,0:T(8,128)(2,1)S(1)}, u32[]{:S(2)}, u32[]{:S(2)}) %collective-permute-start.14) | collective-permute-done | bytes 1048608 | tf_op jit(solution)/shard_map/ppermute | solution.py:333
  86.9 1.1 broadcast_select_fusion.refs_1_
  88.0 0.0 collective-permute-done.16.refs_5_
  88.0 0.0 collective-permute-done.15.refs_10_
  88.0 0.9 copy-done.9
  88.9 0.4 copy-done.10
  89.3 0.1 collective-permute-start.19
  89.5 0.5 copy-done.11
  89.9 1.5 collective-permute-start.18
  91.4 1.3 collective-permute-start.13
  92.7 0.0 collective-permute-done.20.refs_0_
  92.7 1.3 collective-permute-start.12
  94.0 2.2 %fusion.perm_ref = bf16[1024,1024]{1,0:T(8,128)(2,1)} fusion(s32[1024]{0:T(1024)S(1)} %fusion.7), kind=kLoop, calls=%fused_computation.1 | loop fusion | flops 2097152 | bytes 2101248 | tf_op jit(solution)/shard_map/convert_element_type | solution.py:25
  96.3 0.7 stack.83.firsts
  97.0 23.1 %own_part.2 = (f32[16,128,1024]{2,1,0:T(8,128)}, bf16[32,128,1024]{2,1,0:T(8,128)(2,1)}) custom-call(s32[33]{0:T(128)} %get-tuple-element.86.starts, s32[96]{0:T(128)} %get-tuple-element.87.tile_at, s32[96]{0:T(128)} %get-tuple-element.88.block_at, s32[64]{0:T(128)} %get-tuple-element.89.own_slots, s32[64]{0:T(128)} %get-tuple-element.90.far_slots, ...), custom_call_target="tpu_custom_call" | custom-call | tf_op jit(solution)/shard_map/own_part/pallas_call | solution.py:208
  120.1 0.4 collective-permute-start.21
  120.4 1.3 collective-permute-start.11
  121.8 0.6 stack.71.firsts
  122.4 0.8 collective-permute-done.21.refs_4_
  123.2 17.1 %own_part.3 = (f32[16,128,1024]{2,1,0:T(8,128)}, bf16[32,128,1024]{2,1,0:T(8,128)(2,1)}) custom-call(s32[33]{0:T(128)} %get-tuple-element.86.starts, s32[96]{0:T(128)} %get-tuple-element.87.tile_at, s32[96]{0:T(128)} %get-tuple-element.88.block_at, s32[64]{0:T(128)} %get-tuple-element.89.own_slots, ...), custom_call_target="tpu_custom_call", output_to_operand_aliasing={{0}: (13, {}), {1}: (14, {})} | custom-call | tf_op jit(solution)/shard_map/own_part/pallas_call | solution.py:208
  140.3 32.5 %collective-permute-done.13.refs_1_ = bf16[48,128,128]{2,1,0:T(8,128)(2,1)} collective-permute-done((bf16[48,128,128]{2,1,0:T(8,128)(2,1)}, bf16[48,128,128]{2,1,0:T(8,128)(2,1)}, u32[]{:S(2)}, u32[]{:S(2)}) %collective-permute-start.13) | collective-permute-done | bytes 1572896 | tf_op jit(solution)/shard_map/ppermute | solution.py:333
  172.8 0.0 collective-permute-done.10.refs_0_
  172.8 3.4 %copy-done = f32[16,128,1024]{2,1,0:T(8,128)S(1)} copy-done((f32[16,128,1024]{2,1,0:T(8,128)S(1)}, f32[16,128,1024]{2,1,0:T(8,128)}, u32[]{:S(2)}) %copy-start) | copy-done | bytes 8388632
  176.2 12.0 %far_part.3 = (f32[16,128,1024]{2,1,0:T(8,128)S(1)}, bf16[16,128,1024]{2,1,0:T(8,128)(2,1)}) custom-call(s32[17]{0:T(128)S(1)} %copy-done.2, s32[96]{0:T(128)S(1)} %copy-done.3, s32[1]{0:T(128)} %bitcast.4.chosen, bf16[96,128,128]{2,1,0:T(8,128)(2,1)S(1)} %collective-permute-done.10.refs_0_, ...), custom_call_target="tpu_custom_call", output_to_operand_aliasing={{0}: (5, {})} | custom-call | tf_op jit(solution)/shard_map/far_part/pallas_call | solution.py:307
  188.3 9.8 %collective-permute-done.12.refs_1_ = bf16[36,128,128]{2,1,0:T(8,128)(2,1)} collective-permute-done((bf16[36,128,128]{2,1,0:T(8,128)(2,1)}, bf16[36,128,128]{2,1,0:T(8,128)(2,1)}, u32[]{:S(2)}, u32[]{:S(2)}) %collective-permute-start.12) | collective-permute-done | bytes 1179680 | tf_op jit(solution)/shard_map/ppermute | solution.py:333
  198.1 9.4 %far_part.4 = (f32[16,128,1024]{2,1,0:T(8,128)S(1)}, bf16[16,128,1024]{2,1,0:T(8,128)(2,1)}) custom-call(s32[17]{0:T(128)S(1)} %copy-done.2, s32[96]{0:T(128)S(1)} %copy-done.3, s32[1]{0:T(128)} %bitcast.4.chosen, bf16[96,128,128]{2,1,0:T(8,128)(2,1)S(1)} %collective-permute-done.10.refs_0_, ...), custom_call_target="tpu_custom_call", output_to_operand_aliasing={{0}: (5, {}), {1}: (7, {})} | custom-call | tf_op jit(solution)/shard_map/far_part/pallas_call | solution.py:307
  207.5 4.9 %far_part.5 = (f32[16,128,1024]{2,1,0:T(8,128)S(1)}, bf16[16,128,1024]{2,1,0:T(8,128)(2,1)}) custom-call(s32[17]{0:T(128)S(1)} %copy-done.2, s32[96]{0:T(128)S(1)} %copy-done.3, s32[1]{0:T(128)} %bitcast.4.chosen, bf16[96,128,128]{2,1,0:T(8,128)(2,1)S(1)} %collective-permute-done.10.refs_0_, ...), custom_call_target="tpu_custom_call", output_to_operand_aliasing={{0}: (5, {}), {1}: (7, {})} | custom-call | tf_op jit(solution)/shard_map/far_part/pallas_call | solution.py:307
  (22 shorter events, 0.1 us)
Async XLA Ops:
  0.0 30.7 %collective-permute-start.2 = (bf16[4,128,1024]{2,1,0:T(8,128)(2,1)}, bf16[4,128,1024]{2,1,0:T(8,128)(2,1)}, u32[]{:S(2)}, u32[]{:S(2)}) collective-permute-start(bf16[4,128,1024]{2,1,0:T(8,128)(2,1)} %refs_0_.1), channel_id=1, source_target_pairs={{0,2},{1,3},{2,0},{3,1},{4,6},{5,7},{6,4},{7,5},{8,10},{9,11},{10,... | collective-permute-start | bytes 3145736 | tf_op jit(solution)/shard_map/ppermute | solution.py:333
  3.0 27.8 %collective-permute-start.1 = (bf16[4,128,1024]{2,1,0:T(8,128)(2,1)}, bf16[4,128,1024]{2,1,0:T(8,128)(2,1)}, u32[]{:S(2)}, u32[]{:S(2)}) collective-permute-start(bf16[4,128,1024]{2,1,0:T(8,128)(2,1)} %refs_0_.1), channel_id=1, source_target_pairs={{4,8},{5,9},{6,10},{7,11},{8,4},{9,5},{10,6},{11,7},{20,24},{21,25... | collective-permute-start | bytes 3145736 | tf_op jit(solution)/shard_map/ppermute | solution.py:333
  4.6 26.4 %collective-permute-start = (bf16[4,128,1024]{2,1,0:T(8,128)(2,1)}, bf16[4,128,1024]{2,1,0:T(8,128)(2,1)}, u32[]{:S(2)}, u32[]{:S(2)}) collective-permute-start(bf16[4,128,1024]{2,1,0:T(8,128)(2,1)} %refs_0_.1), channel_id=1, source_target_pairs={{0,4},{1,5},{2,6},{3,7},{4,0},{5,1},{6,2},{7,3},{8,12},{9,13},{10,... | collective-permute-start | bytes 3145736 | tf_op jit(solution)/shard_map/ppermute | solution.py:333
  8.1 22.9 %collective-permute-start.3 = (bf16[4,128,1024]{2,1,0:T(8,128)(2,1)}, bf16[4,128,1024]{2,1,0:T(8,128)(2,1)}, u32[]{:S(2)}, u32[]{:S(2)}) collective-permute-start(bf16[4,128,1024]{2,1,0:T(8,128)(2,1)} %refs_0_.1), channel_id=1, source_target_pairs={{0,1},{1,0},{2,3},{3,2},{4,5},{5,4},{6,7},{7,6},{8,9},{9,8},{10,11... | collective-permute-start | bytes 3145736 | tf_op jit(solution)/shard_map/ppermute | solution.py:333
  8.8 21.9 %collective-permute-start.4 = (s32[2,96]{1,0:T(2,128)S(1)}, s32[2,96]{1,0:T(2,128)S(1)}, u32[]{:S(2)}, u32[]{:S(2)}) collective-permute-start(s32[2,96]{1,0:T(2,128)S(1)} %pad_add_fusion), channel_id=1, source_target_pairs={{0,8},{1,9},{2,10},{3,11},{4,12},{5,13},{6,14},{7,15},{8,0},{9,1},... | collective-permute-start | bytes 2312 | tf_op jit(solution)/shard_map/ppermute | solution.py:333
  13.5 1.9 copy-start.1
  15.4 0.6 copy-start.4
  28.0 1.7 copy-start.5
  31.0 26.1 %collective-permute-start.6 = (bf16[4,128,1024]{2,1,0:T(8,128)(2,1)}, bf16[4,128,1024]{2,1,0:T(8,128)(2,1)S(1)}, u32[]{:S(2)}, u32[]{:S(2)}) collective-permute-start(bf16[4,128,1024]{2,1,0:T(8,128)(2,1)} %collective-permute-done.1), channel_id=1, source_target_pairs={{4,0},{5,1},{6,2},{7,3},{8,12},{9,13},{10,14},{11,15},{20,16},{21,... | collective-permute-start | bytes 3145736 | tf_op jit(solution)/shard_map/ppermute | solution.py:333
  32.3 24.9 %collective-permute-start.9 = (bf16[4,128,1024]{2,1,0:T(8,128)(2,1)}, bf16[4,128,1024]{2,1,0:T(8,128)(2,1)S(1)}, u32[]{:S(2)}, u32[]{:S(2)}) collective-permute-start(bf16[4,128,1024]{2,1,0:T(8,128)(2,1)} %collective-permute-done.2.refs_6_), channel_id=1, source_target_pairs={{0,1},{1,0},{2,3},{3,2},{4,5},{5,4},{6,7},{7,6},{8,9},{9,8},{10,11... | collective-permute-start | bytes 3145736 | tf_op jit(solution)/shard_map/ppermute | solution.py:333
  32.4 24.8 %collective-permute-start.8 = (bf16[4,128,1024]{2,1,0:T(8,128)(2,1)}, bf16[4,128,1024]{2,1,0:T(8,128)(2,1)S(1)}, u32[]{:S(2)}, u32[]{:S(2)}) collective-permute-start(bf16[4,128,1024]{2,1,0:T(8,128)(2,1)} %collective-permute-done.refs_2_), channel_id=1, source_target_pairs={{0,1},{1,0},{2,3},{3,2},{4,5},{5,4},{6,7},{7,6},{8,9},{9,8},{10,11... | collective-permute-start | bytes 3145736 | tf_op jit(solution)/shard_map/ppermute | solution.py:333
  32.9 25.5 %collective-permute-start.7 = (bf16[4,128,1024]{2,1,0:T(8,128)(2,1)}, bf16[4,128,1024]{2,1,0:T(8,128)(2,1)}, u32[]{:S(2)}, u32[]{:S(2)}) collective-permute-start(bf16[4,128,1024]{2,1,0:T(8,128)(2,1)} %collective-permute-done.refs_2_), channel_id=1, source_target_pairs={{0,2},{1,3},{2,0},{3,1},{4,6},{5,7},{6,4},{7,5},{8,10},{9,11},{10,... | collective-permute-start | bytes 3145736 | tf_op jit(solution)/shard_map/ppermute | solution.py:333
  33.4 25.0 %collective-permute-start.5 = (bf16[4,128,1024]{2,1,0:T(8,128)(2,1)}, bf16[4,128,1024]{2,1,0:T(8,128)(2,1)}, u32[]{:S(2)}, u32[]{:S(2)}) collective-permute-start(bf16[4,128,1024]{2,1,0:T(8,128)(2,1)} %collective-permute-done.refs_2_), channel_id=1, source_target_pairs={{4,8},{5,9},{6,10},{7,11},{8,4},{9,5},{10,6},{11,7},{20,24},{21,25... | collective-permute-start | bytes 3145736 | tf_op jit(solution)/shard_map/ppermute | solution.py:333
  57.2 3.0 %copy-start.6 = (bf16[4,128,1024]{2,1,0:T(8,128)(2,1)}, bf16[4,128,1024]{2,1,0:T(8,128)(2,1)S(1)}, u32[]{:S(2)}) copy-start(bf16[4,128,1024]{2,1,0:T(8,128)(2,1)S(1)} %broadcast_select_fusion.1.refs_4_) | copy-start | bytes 3145732
  57.2 3.0 %copy-start.7 = (bf16[4,128,1024]{2,1,0:T(8,128)(2,1)}, bf16[4,128,1024]{2,1,0:T(8,128)(2,1)S(1)}, u32[]{:S(2)}) copy-start(bf16[4,128,1024]{2,1,0:T(8,128)(2,1)S(1)} %collective-permute-done.9.refs_7_) | copy-start | bytes 3145732
  57.3 3.0 %copy-start.8 = (bf16[4,128,1024]{2,1,0:T(8,128)(2,1)}, bf16[4,128,1024]{2,1,0:T(8,128)(2,1)S(1)}, u32[]{:S(2)}) copy-start(bf16[4,128,1024]{2,1,0:T(8,128)(2,1)S(1)} %collective-permute-done.8.refs_3_) | copy-start | bytes 3145732
  58.4 28.5 %collective-permute-start.14 = (bf16[4,128,1024]{2,1,0:T(8,128)(2,1)}, bf16[4,128,1024]{2,1,0:T(8,128)(2,1)S(1)}, u32[]{:S(2)}, u32[]{:S(2)}) collective-permute-start(bf16[4,128,1024]{2,1,0:T(8,128)(2,1)} %collective-permute-done.5), channel_id=1, source_target_pairs={{4,0},{5,1},{6,2},{7,3},{8,12},{9,13},{10,14},{11,15},{20,16},{21,... | collective-permute-start | bytes 3145736 | tf_op jit(solution)/shard_map/ppermute | solution.py:333
  59.7 28.3 %collective-permute-start.17 = (bf16[4,128,1024]{2,1,0:T(8,128)(2,1)}, bf16[4,128,1024]{2,1,0:T(8,128)(2,1)S(1)}, u32[]{:S(2)}, u32[]{:S(2)}) collective-permute-start(bf16[4,128,1024]{2,1,0:T(8,128)(2,1)} %collective-permute-done.7.refs_8_), channel_id=1, source_target_pairs={{0,1},{1,0},{2,3},{3,2},{4,5},{5,4},{6,7},{7,6},{8,9},{9,8},{10,11... | collective-permute-start | bytes 3145736 | tf_op jit(solution)/shard_map/ppermute | solution.py:333
  59.7 28.2 %collective-permute-start.16 = (bf16[4,128,1024]{2,1,0:T(8,128)(2,1)S(1)}, bf16[4,128,1024]{2,1,0:T(8,128)(2,1)S(1)}, u32[]{:S(2)}, u32[]{:S(2)}) collective-permute-start(bf16[4,128,1024]{2,1,0:T(8,128)(2,1)S(1)} %broadcast_select_fusion.1.refs_4_), channel_id=1, source_target_pairs={{0,1},{1,0},{2,3},{3,2},{4,5},{5,4},{6,7},{7,6},{8,9},{9,8},{10,11... | collective-permute-start | bytes 3145736 | tf_op jit(solution)/shard_map/ppermute | solution.py:333
  60.2 27.8 %collective-permute-start.15 = (bf16[4,128,1024]{2,1,0:T(8,128)(2,1)S(1)}, bf16[4,128,1024]{2,1,0:T(8,128)(2,1)S(1)}, u32[]{:S(2)}, u32[]{:S(2)}) collective-permute-start(bf16[4,128,1024]{2,1,0:T(8,128)(2,1)S(1)} %broadcast_select_fusion.1.refs_4_), channel_id=1, source_target_pairs={{0,2},{1,3},{2,0},{3,1},{4,6},{5,7},{6,4},{7,5},{8,10},{9,11},{10,... | collective-permute-start | bytes 3145736 | tf_op jit(solution)/shard_map/ppermute | solution.py:333
  60.8 112.0 %collective-permute-start.10 = (bf16[96,128,128]{2,1,0:T(8,128)(2,1)}, bf16[96,128,128]{2,1,0:T(8,128)(2,1)S(1)}, u32[]{:S(2)}, u32[]{:S(2)}) collective-permute-start(bf16[96,128,128]{2,1,0:T(8,128)(2,1)} %copy-done.5), channel_id=1, source_target_pairs={{0,8},{1,9},{2,10},{3,11},{12,4},{13,5},{14,6},{15,7},{16,24},{17,... | collective-permute-start | bytes 9437192 | tf_op jit(solution)/shard_map/ppermute | solution.py:333
  88.0 1.0 copy-start.9
  88.0 1.3 copy-start.10
  88.9 1.0 copy-start.11
  88.9 3.8 %collective-permute-start.20 = (bf16[4,128,1024]{2,1,0:T(8,128)(2,1)S(1)}, bf16[4,128,1024]{2,1,0:T(8,128)(2,1)}, u32[]{:S(2)}, u32[]{:S(2)}) collective-permute-start(bf16[4,128,1024]{2,1,0:T(8,128)(2,1)S(1)} %collective-permute-done.15.refs_10_), channel_id=1, source_target_pairs={{0,1},{1,0},{2,3},{3,2},{4,5},{5,4},{6,7},{7,6},{8,9},{9,8},{10,11... | collective-permute-start | bytes 3145736 | tf_op jit(solution)/shard_map/ppermute | solution.py:333
  89.3 30.7 %collective-permute-start.19 = (bf16[4,128,1024]{2,1,0:T(8,128)(2,1)}, bf16[4,128,1024]{2,1,0:T(8,128)(2,1)}, u32[]{:S(2)}, u32[]{:S(2)}) collective-permute-start(bf16[4,128,1024]{2,1,0:T(8,128)(2,1)} %broadcast_select_fusion.refs_1_), channel_id=1, source_target_pairs={{0,1},{1,0},{2,3},{3,2},{4,5},{5,4},{6,7},{7,6},{8,9},{9,8},{10,11... | collective-permute-start | bytes 3145736 | tf_op jit(solution)/shard_map/ppermute | solution.py:333
  89.9 30.2 %collective-permute-start.18 = (bf16[4,128,1024]{2,1,0:T(8,128)(2,1)}, bf16[4,128,1024]{2,1,0:T(8,128)(2,1)}, u32[]{:S(2)}, u32[]{:S(2)}) collective-permute-start(bf16[4,128,1024]{2,1,0:T(8,128)(2,1)} %broadcast_select_fusion.refs_1_), channel_id=1, source_target_pairs={{0,2},{1,3},{2,0},{3,1},{4,6},{5,7},{6,4},{7,5},{8,10},{9,11},{10,... | collective-permute-start | bytes 3145736 | tf_op jit(solution)/shard_map/ppermute | solution.py:333
  91.4 81.4 %collective-permute-start.13 = (bf16[48,128,128]{2,1,0:T(8,128)(2,1)}, bf16[48,128,128]{2,1,0:T(8,128)(2,1)}, u32[]{:S(2)}, u32[]{:S(2)}) collective-permute-start(bf16[48,128,128]{2,1,0:T(8,128)(2,1)} %get-tuple-element.85), channel_id=1, source_target_pairs={{4,12},{5,13},{6,14},{7,15},{8,0},{9,1},{10,2},{11,3},{20,28},{21,... | collective-permute-start | bytes 4718600 | tf_op jit(solution)/shard_map/ppermute | solution.py:333
  92.7 105.4 %collective-permute-start.12 = (bf16[36,128,128]{2,1,0:T(8,128)(2,1)}, bf16[36,128,128]{2,1,0:T(8,128)(2,1)}, u32[]{:S(2)}, u32[]{:S(2)}) collective-permute-start(bf16[36,128,128]{2,1,0:T(8,128)(2,1)} %get-tuple-element.84), channel_id=1, source_target_pairs={{4,12},{5,13},{6,14},{7,15},{8,0},{9,1},{10,2},{11,3},{20,28},{21,... | collective-permute-start | bytes 3538952 | tf_op jit(solution)/shard_map/ppermute | solution.py:333
  120.1 3.1 %collective-permute-start.21 = (bf16[4,128,1024]{2,1,0:T(8,128)(2,1)}, bf16[4,128,1024]{2,1,0:T(8,128)(2,1)}, u32[]{:S(2)}, u32[]{:S(2)}) collective-permute-start(bf16[4,128,1024]{2,1,0:T(8,128)(2,1)} %collective-permute-done.18.refs_3_), channel_id=1, source_target_pairs={{0,1},{1,0},{2,3},{3,2},{4,5},{5,4},{6,7},{7,6},{8,9},{9,8},{10,11... | collective-permute-start | bytes 3145736 | tf_op jit(solution)/shard_map/ppermute | solution.py:333
  120.4 87.1 %collective-permute-start.11 = (bf16[12,128,128]{2,1,0:T(8,128)(2,1)}, bf16[12,128,128]{2,1,0:T(8,128)(2,1)S(1)}, u32[]{:S(2)}, u32[]{:S(2)}) collective-permute-start(bf16[12,128,128]{2,1,0:T(8,128)(2,1)} %get-tuple-element.83), channel_id=1, source_target_pairs={{4,12},{5,13},{6,14},{7,15},{8,0},{9,1},{10,2},{11,3},{20,28},{21,... | collective-permute-start | bytes 1179656 | tf_op jit(solution)/shard_map/ppermute | solution.py:333
  122.4 50.4 %copy-start.2 = (s32[17]{0:T(128)S(1)}, s32[17]{0:T(128)}, u32[]{:S(2)}) copy-start(s32[17]{0:T(128)} %get-tuple-element.80.starts) | copy-start | bytes 208
  122.4 50.4 %copy-start.3 = (s32[96]{0:T(128)S(1)}, s32[96]{0:T(128)}, u32[]{:S(2)}) copy-start(s32[96]{0:T(128)} %get-tuple-element.81.block_at) | copy-start | bytes 1156
  172.8 3.4 %copy-start = (f32[16,128,1024]{2,1,0:T(8,128)S(1)}, f32[16,128,1024]{2,1,0:T(8,128)}, u32[]{:S(2)}) copy-start(f32[16,128,1024]{2,1,0:T(8,128)} %get-tuple-element.108.refs_2_) | copy-start | bytes 25165828

commit v7 on v5

--- a/solution.py
+++ b/solution.py
@@ -11,7 +11,7 @@
 PPD = 16
 REUSE = 3
 QUAD = 4
-SHARES = (22, 20)
+SHARES = (24, 18)
 COLUMNS = 256
 MIB = 1024 * 1024
 SMEM = pl.BlockSpec(memory_space=pltpu.SMEM)
@@ -76,30 +76,45 @@
     )(rows, cols)
 
 
-def sort_kernel(tile_at, tiles_ref, *refs):
+def window(ref, tile):
+    depth = ref.shape[1]
+    across = ref.shape[2] // depth
+    if across == 1:
+        return ref.at[tile]
+    return ref.at[lax.div(tile, across), :, pl.ds(pl.multiple_of(lax.rem(tile, across) * depth, depth), depth)]
+
+
+def sort_kernel(choices, tile_at, chosen, tiles_ref, *refs):
     parts, sems = refs[: len(refs) // 2], refs[len(refs) // 2 :]
-    base = 0
-    for part, sem in zip(parts, sems):
-
-        @pl.loop(0, part.shape[0])
-        def _(number, part=part, sem=sem, base=base):
-            pltpu.make_async_copy(tiles_ref.at[tile_at[base + number]], part.at[number], sem).start()
-
-        base += part.shape[0]
-    for part, sem in zip(parts, sems):
-        pltpu.make_async_copy(part, part, sem).wait()
-
-
-def sort_tiles(tile_at, tiles, sizes):
+    begin = {choice: 0 for choice in choices}
+    for choice, part, sem in zip(choices, parts, sems):
+        base = begin[choice]
+        count = part.shape[0] * part.shape[2] // tiles_ref.shape[2]
+        begin[choice] += count
+
+        @pl.when(chosen[0] == choice)
+        def _(part=part, sem=sem, base=base, count=count):
+            @pl.loop(0, count)
+            def _(number):
+                pltpu.make_async_copy(tiles_ref.at[tile_at[base + number]], window(part, number), sem).start()
+
+    for choice, part, sem in zip(choices, parts, sems):
+
+        @pl.when(chosen[0] == choice)
+        def _(part=part, sem=sem):
+            pltpu.make_async_copy(part, part, sem).wait()
+
+
+def sort_tiles(tile_at, chosen, tiles, choices, shapes):
     return pl.pallas_call(
-        sort_kernel,
-        in_specs=[SMEM, ANY],
-        out_specs=[VMEM] * len(sizes),
-        out_shape=[jax.ShapeDtypeStruct((size,) + tiles.shape[1:], tiles.dtype) for size in sizes],
-        scratch_shapes=[pltpu.SemaphoreType.DMA] * len(sizes),
+        functools.partial(sort_kernel, choices),
+        in_specs=[SMEM] * 2 + [ANY],
+        out_specs=[VMEM] * len(shapes),
+        out_shape=[jax.ShapeDtypeStruct(shape, tiles.dtype) for shape in shapes],
+        scratch_shapes=[pltpu.SemaphoreType.DMA] * len(shapes),
         compiler_params=pltpu.CompilerParams(vmem_limit_bytes=16 * MIB),
         name="sort_tiles",
-    )(tile_at, tiles)
+    )(tile_at, chosen, tiles)
 
 
 def add_row(sum_ref, begin, end, tile_of, block_of):
@@ -228,12 +243,28 @@
     )(starts, tile_at, block_at, own_slots, far_slots, firsts, tiles, perm, *pieces, *earlier)
 
 
-def far_kernel(base, starts, block_at, tiles_ref, sum_in, flip_in, *refs):
-    if base:
-        refs = refs[1:]
-    sum_out, result, blocks, sums, rounded, block_sem, row_sems, out_sems = refs
+def far_kernel(base, segments, starts, block_at, chosen, *refs):
+    tile_refs, refs = refs[: len(segments)], refs[len(segments) :]
+    sum_in, flip_in = refs[:2]
+    refs = refs[3:] if base else refs[2:]
+    sum_out, result, tiles_ref, blocks, sums, rounded, tile_sem, block_sem, row_sems, out_sems = refs
     count = tiles_ref.shape[0]
     stop = base + count
+
+    for source, (choice, begin) in zip(tile_refs, segments):
+        held = source.shape[0] * source.shape[2] // tiles_ref.shape[2]
+        low, high = max(begin, base), min(begin + held, stop)
+
+        @pl.when(chosen[0] == choice)
+        def _(source=source, begin=begin, low=low, high=high):
+            if source.shape[2] == tiles_ref.shape[2]:
+                here, there = source.at[pl.ds(low - begin, high - low)], tiles_ref.at[pl.ds(low - base, high - low)]
+                pltpu.make_async_copy(here, there, tile_sem).start()
+            else:
+
+                @pl.loop(low, high)
+                def _(place):
+                    pltpu.make_async_copy(window(source, place - begin), tiles_ref.at[place - base], tile_sem).start()
 
     @pl.loop(0, count)
     def _(number):
@@ -258,6 +289,7 @@
         return pltpu.make_async_copy(sums.at[row], sum_out.at[row], out_sems.at[row])
 
     each_row(lambda row, complete: load(row).start())
+    pltpu.make_async_copy(tiles_ref, tiles_ref, tile_sem).wait()
     pltpu.make_async_copy(blocks, blocks, block_sem).wait()
 
     def add(row, complete):
@@ -287,29 +319,37 @@
     each_row(finish)
 
 
-def far_part(base, far_tables, tiles, flipped, total, result=None):
+def far_part(base, count, far_tables, chosen, sources, flipped, total, result=None):
     starts, _, block_at, _ = far_tables
     whole = total.shape
-    count = tiles.shape[0]
     given = [] if result is None else [result]
-    aliases = {3: 0, 5: 1} if given else {3: 0}
+    held = [array.size // (whole[1] * flipped.shape[1]) for _, _, array in sources]
+    used = [
+        (source[:2], source[2])
+        for source, size in zip(sources, held)
+        if source[1] < base + count and source[1] + size > base
+    ]
+    operand = 3 + len(used)
+    aliases = {operand: 0, operand + 2: 1} if given else {operand: 0}
     return pl.pallas_call(
-        functools.partial(far_kernel, base),
-        in_specs=[SMEM] * 2 + [VMEM] + [ANY] * (2 + len(given)),
+        functools.partial(far_kernel, base, [segment for segment, _ in used]),
+        in_specs=[SMEM] * 3 + [ANY] * (len(used) + 2 + len(given)),
         out_specs=[ANY] * 2,
         out_shape=[jax.ShapeDtypeStruct(whole, jnp.float32), jax.ShapeDtypeStruct(whole, jnp.bfloat16)],
         input_output_aliases=aliases,
         scratch_shapes=[
+            pltpu.VMEM((count, whole[1], flipped.shape[1]), jnp.bfloat16),
             pltpu.VMEM((count,) + flipped.shape[1:], jnp.bfloat16),
             pltpu.VMEM(whole, jnp.float32),
             pltpu.VMEM(whole, jnp.bfloat16),
+            pltpu.SemaphoreType.DMA,
             pltpu.SemaphoreType.DMA,
             pltpu.SemaphoreType.DMA((PPD,)),
             pltpu.SemaphoreType.DMA((PPD,)),
         ],
         compiler_params=pltpu.CompilerParams(vmem_limit_bytes=36 * MIB),
         name="far_part",
-    )(starts, block_at, tiles, total, flipped, *given)
+    )(starts, block_at, chosen, *[array for _, array in used], total, flipped, *given)
 
 
 def together(*values):
@@ -329,18 +369,21 @@
     block_total = 16 * local
     centre = [i for i in range(16) if i // 4 in (1, 2)]
     across = [(i, i ^ 12) for i in centre]
-    outward = [(i, i ^ 4) for i in centre]
+    from_ends = [(i, i ^ 8) for i in range(16) if i not in centre]
+    from_centre = [(i, i ^ 8) for i in centre]
+    around = [(i, i ^ 4) for i in centre] + from_ends
     other_z, other_y, other_core, opposite = (flipped_bit(bit) for bit in (4, 2, 1, 8))
     me = lax.axis_index("tile")
     z = me // 4
     in_centre = (z == 1) | (z == 2)
+    at_end = 1 - in_centre.astype(jnp.int32).reshape(1)
     zs = [z, z ^ 1, jnp.where(z < 2, 2, 1), jnp.where(z < 2, 3, 0)]
 
     def owner(k, bits):
         return 4 * zs[k] + ((me & 3) ^ bits)
 
-    def first_blocks(owners):
-        return jnp.stack([value * local for value in owners]).astype(jnp.int32)
+    def first_blocks(firsts):
+        return jnp.stack(firsts).astype(jnp.int32)
 
     col_owner = cols // local
     late = (col_owner // 4 == zs[3]) | (col_owner == owner(2, 3))
@@ -352,45 +395,54 @@
     c_own = send(shard, other_core)
     notes = send(jnp.stack([rows, cols]), opposite)
     order = tables(rows, cols, block_total)[1]
-    sizes = tile_parts(tiles.shape[0])
-    parts = sort_tiles(order, tiles, sizes)
+    count = tiles.shape[0]
+    step = shard.size // tiles[0].size
+    sizes = tile_parts(count)
+    shapes = [shard.shape] * 2 + [(size,) + tiles.shape[1:] for size in [count - 2 * step] + sizes]
+    parts = sort_tiles(order, at_end, tiles, [1, 1, 1, 0, 0, 0], shapes)
     near, first, y_own, c_own, notes, *parts = together(near, first, y_own, c_own, notes, *parts)
 
-    far_parts = [send(parts[0], opposite)]
+    outer = send(jnp.where(in_centre, first, parts[0]), around)
     second = send(near, across)
-    first = jnp.where(in_centre, first, send(first, outward))
     y_near = send(near, other_y)
     c_near = send(near, other_core)
     c_y_own = send(y_own, other_core)
     own_tables = tables(keys, cols, block_total, 2 * PPD)
     far_tables = tables(notes[0], notes[1], block_total)
+    far_ends = [outer]
+    first = jnp.where(in_centre, first, outer)
     second, first, y_near, c_near, c_y_own, *rest = together(
         second, first, y_near, c_near, c_y_own, *parts[1:], *own_tables, *far_tables
     )
-    parts, own_tables, far_tables = rest[: len(parts) - 1], rest[-8:-4], rest[-4:]
-
-    second = jnp.where(in_centre, second, send(second, outward))
+    parts, own_tables, far_tables = rest[:5], rest[5:9], rest[9:]
+
+    outer = send(jnp.where(in_centre, second, parts[0]), around)
+    far_ends += [outer, send(parts[1], from_ends)]
     y_first = send(first, other_y)
     c_first = send(first, other_core)
     c_y_near = send(y_near, other_core)
-    second, y_first, c_first, c_y_near, far_parts[0] = together(second, y_first, c_first, c_y_near, far_parts[0])
-
-    far_parts.append(send(parts[0], opposite))
-    y_second = send(second, other_y)
-    c_second = send(second, other_core)
-    c_y_first = send(y_first, other_core)
+    halves = (slice(0, local // 2), slice(local // 2, None))
+    second = [jnp.where(in_centre, second[half], outer[half]) for half in halves]
+    *second, y_first, c_first, c_y_near = together(*second, y_first, c_first, c_y_near)
+
+    far_centre = [send(part, from_centre) for part in parts[2:]]
+    y_second = [send(half, other_y) for half in second]
     perm = flip_matrix(W)
     pieces = [shard, c_own, near, c_near, first, c_first, y_own, c_y_own, y_near, c_y_near, y_first]
-    owners = [owner(k, y + core) for y in (0, 2) for k in range(3) for core in (0, 1)][:11]
-    early = own_part(own_tables, far_tables[3], tiles, pieces, first_blocks(owners), perm)
-    y_second, c_second, c_y_first, *early = together(y_second, c_second, c_y_first, *early)
-
-    c_y_second = send(y_second, other_core)
-    pieces = [c_y_first, second, c_second, y_second, c_y_second]
-    owners = [owner(2, 3)] + [owner(3, bits) for bits in range(4)]
-    total, flipped = own_part(own_tables, far_tables[3], tiles, pieces, first_blocks(owners), perm, PPD, early)
-    far_parts.append(send(parts[1], opposite))
-    return far_products(far_tables, far_parts, flipped, total)
+    firsts = [owner(k, y + core) * local for y in (0, 2) for k in range(3) for core in (0, 1)][:11]
+    early = own_part(own_tables, far_tables[3], tiles, pieces, first_blocks(firsts), perm)
+    *y_second, y_first, far_ends[2], total, flipped = together(*y_second, y_first, far_ends[2], *early)
+
+    c_y_first = send(y_first, other_core)
+    c_second = [send(half, other_core) for half in second]
+    c_y_second = [send(half, other_core) for half in y_second]
+    pieces = [c_y_first, *second, *c_second, *y_second, *c_y_second]
+    firsts = [owner(2, 3) * local] + [owner(3, bits) * local + half for bits in range(4) for half in (0, local // 2)]
+    total, flipped = own_part(own_tables, far_tables[3], tiles, pieces, first_blocks(firsts), perm, PPD, (total, flipped))
+
+    sources = [(0, step * number, array) for number, array in enumerate(far_ends)]
+    sources += [(1, sum(sizes[:number]), array) for number, array in enumerate(far_centre)]
+    return far_products(far_tables, at_end, sources, sizes, flipped, total)
 
 
 def tile_parts(count):
@@ -398,11 +450,11 @@
     return sizes + [count - sum(sizes)]
 
 
-def far_products(far_tables, far_parts, flipped, total):
+def far_products(far_tables, chosen, sources, sizes, flipped, total):
     base, result = 0, None
-    for part in far_parts:
-        total, result = far_part(base, far_tables, part, flipped, total, result)
-        base += part.shape[0]
+    for size in sizes:
+        total, result = far_part(base, size, far_tables, chosen, sources, flipped, total, result)
+        base += size
     return result
 
 
@@ -413,14 +465,15 @@
     block_total = peers * integrals.shape[0]
     opposite = [(source, (source + peers // 2) % peers) for source in range(peers)]
     own_tables = tables(t2_row, t2_col, block_total)
-    parts = sort_tiles(own_tables[1], t2_tiles, tile_parts(t2_tiles.shape[0]))
+    sizes = tile_parts(t2_tiles.shape[0])
+    zero = jnp.zeros((1,), jnp.int32)
+    parts = sort_tiles(own_tables[1], zero, t2_tiles, [0] * 3, [(size,) + t2_tiles.shape[1:] for size in sizes])
     notes = send(jnp.stack([t2_row, t2_col]), opposite)
-    far_parts = [send(part, opposite) for part in parts]
+    sources = [(0, sum(sizes[:number]), send(part, opposite)) for number, part in enumerate(parts)]
     blocks = lax.all_gather(integrals, "tile", axis=0, tiled=True)
     far_tables = tables(notes[0], notes[1], block_total)
-    firsts = jnp.zeros((1,), jnp.int32)
-    total, flipped = own_part(own_tables, far_tables[3], t2_tiles, [blocks], firsts, flip_matrix(W))
-    return far_products(far_tables, far_parts, flipped, total)
+    total, flipped = own_part(own_tables, far_tables[3], t2_tiles, [blocks], zero, flip_matrix(W))
+    return far_products(far_tables, zero, sources, sizes, flipped, total)
 
 
 def solution(mesh):

time: 233 us -> 213 us (0.914); the launches traced: 233 us -> 210 us
  waiting for transfers between devices: 115 us -> 64 us
  starting transfers between devices: 20.4 us -> 45.5 us
  Pallas kernels: 77.8 us -> 83.3 us
  local copies, waits for them, and re-layouts: 13.4 us -> 11 us
    ppermute x21 -> x25, waiting for transfers between devices: 115 us -> 64 us  [send(): return lax.ppermute(value, 'tile', pairs)]
    ppermute x21 -> x25, starting transfers between devices: 20.4 us -> 45.5 us  [send(): return lax.ppermute(value, 'tile', pairs)]
    pallas_call x4, Pallas kernels: 24.5 us -> 29.9 us  [the longest x3 24.8 us: far_part(): pl.pallas_call(functools.partial(far_kernel, base, [segment for segment,...]
    unnamed x20 -> x42, local copies, waits for them, and re-layouts: 11.6 us -> 9.13 us
  transfers between devices with their start and end apart: 21 -> 25, of which waited for: 7 -> 9; matrix products, arithmetic and copies ran while one was open for 4% -> 3% of each run, Pallas kernels for 32% -> 38%
where the time goes in v7:
time: 213 us; the launch traced here: 210 us
  Pallas kernels  83.3 us (39%)
  waiting for transfers between devices  64 us (30%)
  starting transfers between devices  45.5 us (21%)
  local copies, waits for them, and re-layouts  11 us (5%)
  other arithmetic  6.04 us (3%)
    ppermute x25, waiting for transfers between devices, send(): return lax.ppermute(value, 'tile', pairs)  64 us
    ppermute x25, starting transfers between devices, send(): return lax.ppermute(value, 'tile', pairs)  45.5 us
    pallas_call x2, Pallas kernels, own_part(): pl.pallas_call(functools.partial(own_kernel, counts, group, not earlier),...  41.3 us
    pallas_call x3, Pallas kernels, far_part(): pl.pallas_call(functools.partial(far_kernel, base, [segment for segment,...  24.8 us
    pallas_call x3, Pallas kernels, tables(): pl.pallas_call(tables_kernel, in_specs=[SMEM] * 2, out_specs=[SMEM] * 4,...  12.1 us
    unnamed x42, local copies, waits for them, and re-layouts  9.13 us
    pallas_call x1, Pallas kernels, sort_tiles(): pl.pallas_call(functools.partial(sort_kernel, choices), in_specs=[SMEM] *...  5.04 us
  transfers between devices with their start and end apart: 25, of which 9 were waited for; matrix products, arithmetic and copies ran while one was open for 3% of the time, Pallas kernels for 38%

profile of v7, /device:TPU:0, one launch (start us, length us, event | category | flops | bytes accessed | tf_op | source)
XLA Modules:
  0.0 210.3 jit_solution(10868769482862034961)
XLA Ops:
  0.0 3.0 %collective-permute-start.2 = (bf16[4,128,1024]{2,1,0:T(8,128)(2,1)}, bf16[4,128,1024]{2,1,0:T(8,128)(2,1)S(1)}, u32[]{:S(2)}, u32[]{:S(2)}) collective-permute-start(bf16[4,128,1024]{2,1,0:T(8,128)(2,1)} %refs_0_.1), channel_id=1, source_target_pairs={{0,2},{1,3},{2,0},{3,1},{4,6},{5,7},{6,4},{7,5},{8,10},{9,11},{10,... | collective-permute-start | bytes 3145736 | tf_op jit(solution)/shard_map/ppermute | solution.py:360
  3.0 0.7 collective-permute-start.1
  3.7 4.4 %collective-permute-start = (bf16[4,128,1024]{2,1,0:T(8,128)(2,1)}, bf16[4,128,1024]{2,1,0:T(8,128)(2,1)}, u32[]{:S(2)}, u32[]{:S(2)}) collective-permute-start(bf16[4,128,1024]{2,1,0:T(8,128)(2,1)} %refs_0_.1), channel_id=1, source_target_pairs={{0,4},{1,5},{2,6},{3,7},{4,0},{5,1},{6,2},{7,3},{8,12},{9,13},{10,... | collective-permute-start | bytes 3145736 | tf_op jit(solution)/shard_map/ppermute | solution.py:360
  8.1 0.0 collective-permute-start.3
  8.1 0.7 pad_add_fusion
  8.8 0.0 collective-permute-start.4
  8.8 4.0 %tables.3 = (s32[17]{0:T(128)}, s32[96]{0:T(128)}, s32[96]{0:T(128)}, s32[64]{0:T(128)}) custom-call(s32[96]{0:T(128)} %rows.1, s32[96]{0:T(128)} %cols.3), custom_call_target="tpu_custom_call" | custom-call | tf_op jit(solution)/shard_map/tables/pallas_call | solution.py:69
  12.8 0.0 copy-start.1
  12.9 1.9 copy-done.1
  14.7 0.6 copy-done.6
  15.3 5.0 %sort_tiles.1 = (bf16[4,128,1024]{2,1,0:T(8,128)(2,1)S(1)}, bf16[4,128,1024]{2,1,0:T(8,128)(2,1)S(1)}, bf16[32,128,128]{2,1,0:T(8,128)(2,1)S(1)}, bf16[48,128,12...) custom-call(s32[96]{0:T(128)S(1)} %copy-done.6, s32[1]{0:T(128)} %bitcast.2.chosen, ...), custom_call_target="tpu_custom_call" | custom-call | tf_op jit(solution)/shard_map/sort_tiles/pallas_call | solution.py:109
  20.4 0.0 copy-start.7
  20.4 10.3 %collective-permute-done.4 = s32[2,96]{1,0:T(2,128)S(1)} collective-permute-done((s32[2,96]{1,0:T(2,128)S(1)}, s32[2,96]{1,0:T(2,128)S(1)}, u32[]{:S(2)}, u32[]{:S(2)}) %collective-permute-start.4) | collective-permute-done | bytes 800 | tf_op jit(solution)/shard_map/ppermute | solution.py:360
  30.7 0.0 collective-permute-done.2.refs_6_
  30.7 0.0 collective-permute-done.1
  30.7 0.3 collective-permute-done.refs_2_
  31.0 0.0 collective-permute-done.3.refs_1_
  31.0 0.7 copy-done.12
  31.7 1.1 broadcast_select_fusion.2
  32.8 2.8 %collective-permute-start.6 = (bf16[4,128,1024]{2,1,0:T(8,128)(2,1)}, bf16[4,128,1024]{2,1,0:T(8,128)(2,1)S(1)}, u32[]{:S(2)}, u32[]{:S(2)}) collective-permute-start(bf16[4,128,1024]{2,1,0:T(8,128)(2,1)} %broadcast_select_fusion.2), channel_id=1, source_target_pairs={{4,0},{5,1},{6,2},{7,3},{8,12},{9,13},{10,14},{11,15},{0,8},{1,9},... | collective-permute-start | bytes 3145736 | tf_op jit(solution)/shard_map/ppermute | solution.py:360
  35.6 0.5 collective-permute-start.8
  36.1 0.5 collective-permute-start.7
  36.6 1.6 collective-permute-start.5
  38.3 0.6 fusion.10.rows
  38.8 4.0 %tables.4 = (s32[33]{0:T(128)}, s32[96]{0:T(128)}, s32[96]{0:T(128)}, s32[64]{0:T(128)}) custom-call(s32[96]{0:T(128)} %fusion.10.rows, s32[96]{0:T(128)} %cols.3), custom_call_target="tpu_custom_call" | custom-call | tf_op jit(solution)/shard_map/tables/pallas_call | solution.py:69
  42.9 0.6 slice_bitcast_fusion
  43.5 4.0 %tables.5 = (s32[17]{0:T(128)}, s32[96]{0:T(128)}, s32[96]{0:T(128)}, s32[64]{0:T(128)}) custom-call(s32[96]{0:T(128)} %get-tuple-element.132.rows, s32[96]{0:T(128)} %get-tuple-element.131.cols), custom_call_target="tpu_custom_call" | custom-call | tf_op jit(solution)/shard_map/tables/pallas_call | solution.py:69
  47.5 0.0 copy-start.8
  47.5 9.1 %collective-permute-done.6.refs_0_ = bf16[4,128,1024]{2,1,0:T(8,128)(2,1)S(1)} collective-permute-done((bf16[4,128,1024]{2,1,0:T(8,128)(2,1)}, bf16[4,128,1024]{2,1,0:T(8,128)(2,1)S(1)}, u32[]{:S(2)}, u32[]{:S(2)}) %collective-permute-start.6) | collective-permute-done | bytes 1048608 | tf_op jit(solution)/shard_map/ppermute | solution.py:360
  56.6 0.1 broadcast_select_fusion.1.refs_4_
  56.8 4.8 %collective-permute-done.7.refs_8_ = bf16[4,128,1024]{2,1,0:T(8,128)(2,1)} collective-permute-done((bf16[4,128,1024]{2,1,0:T(8,128)(2,1)}, bf16[4,128,1024]{2,1,0:T(8,128)(2,1)}, u32[]{:S(2)}, u32[]{:S(2)}) %collective-permute-start.7) | collective-permute-done | bytes 1048608 | tf_op jit(solution)/shard_map/ppermute | solution.py:360
  61.5 0.1 broadcast_select_fusion
  61.6 22.2 %collective-permute-start.10 = (bf16[4,128,1024]{2,1,0:T(8,128)(2,1)S(1)}, bf16[4,128,1024]{2,1,0:T(8,128)(2,1)S(1)}, u32[]{:S(2)}, u32[]{:S(2)}) collective-permute-start(bf16[4,128,1024]{2,1,0:T(8,128)(2,1)S(1)} %broadcast_select_fusion), channel_id=1, source_target_pairs={{4,0},{5,1},{6,2},{7,3},{8,12},{9,13},{10,14},{11,15},{0,8},{1,9},... | collective-permute-start | bytes 3145736 | tf_op jit(solution)/shard_map/ppermute | solution.py:360
  83.8 0.5 collective-permute-start.12
  84.3 0.5 collective-permute-start.11
  84.8 2.0 collective-permute-start.16
  86.9 20.5 %collective-permute-done.10.refs_1_.refs_0_ = bf16[4,128,1024]{2,1,0:T(8,128)(2,1)S(1)} collective-permute-done((bf16[4,128,1024]{2,1,0:T(8,128)(2,1)S(1)}, bf16[4,128,1024]{2,1,0:T(8,128)(2,1)S(1)}, u32[]{:S(2)}, u32[]{:S(2)}) %collective-permute-start.10) | collective-permute-done | bytes 1048608 | tf_op jit(solution)/shard_map/ppermute | solution.py:360
  107.3 1.3 slice_select_fusion
  108.7 0.8 collective-permute-done.11.refs_10_
  109.5 0.5 collective-permute-start.14
  110.0 1.5 collective-permute-start.15
  111.5 1.3 collective-permute-start.19
  112.8 0.1 collective-permute-start.21
  112.9 16.0 %collective-permute-done.16.refs_1_.refs_0_ = bf16[32,128,128]{2,1,0:T(8,128)(2,1)S(1)} collective-permute-done((bf16[32,128,128]{2,1,0:T(8,128)(2,1)S(1)}, bf16[32,128,128]{2,1,0:T(8,128)(2,1)S(1)}, u32[]{:S(2)}, u32[]{:S(2)}) %collective-permute-start.16) | collective-permute-done | bytes 1048608 | tf_op jit(solution)/shard_map/ppermute | solution.py:360
  128.9 1.0 copy-done.2
  129.9 1.3 collective-permute-start.18
  131.2 2.2 %fusion.perm_ref = bf16[1024,1024]{1,0:T(8,128)(2,1)} fusion(s32[1024]{0:T(1024)S(1)} %fusion.7), kind=kLoop, calls=%fused_computation.1 | loop fusion | flops 2097152 | bytes 2101248 | tf_op jit(solution)/shard_map/convert_element_type | solution.py:25
  133.4 0.7 stack.89.firsts
  134.1 23.5 %own_part.2 = (f32[16,128,1024]{2,1,0:T(8,128)}, bf16[32,128,1024]{2,1,0:T(8,128)(2,1)}) custom-call(s32[33]{0:T(128)} %get-tuple-element.101.starts, s32[96]{0:T(128)} %get-tuple-element.102.tile_at, s32[96]{0:T(128)} %get-tuple-element.103.block_at, s32[64]{0:T(128)} %get-tuple-element.104.own_slots, s32[64]{0:T(128)} %get-tuple-element.105.far_slots, ...), custom_call_target="tpu_custom_call" | custom-call | tf_op jit(solution)/shard_map/own_part/pallas_call | solution.py:222
  157.6 0.1 collective-permute-start.22
  157.7 0.5 collective-permute-start.20
  158.2 0.1 collective-permute-start.23
  158.3 1.3 collective-permute-done.22.refs_4_
  159.6 0.1 collective-permute-start.24
  159.7 0.7 copy-done.15
  160.4 0.9 collective-permute-done.23.refs_7_
  161.3 0.8 copy-done.16
  162.1 1.3 collective-permute-start.17
  163.5 0.6 stack.99.firsts
  164.1 17.9 %own_part.3 = (f32[16,128,1024]{2,1,0:T(8,128)}, bf16[32,128,1024]{2,1,0:T(8,128)(2,1)}) custom-call(s32[33]{0:T(128)} %get-tuple-element.101.starts, s32[96]{0:T(128)} %get-tuple-element.102.tile_at, s32[96]{0:T(128)} %get-tuple-element.103.block_at, s32[64]{0:T(128)} %get-tuple-element.104.own_slots, ...), custom_call_target="tpu_custom_call", output_to_operand_aliasing={{0}: (17, {}), {1}: (18, {})} | custom-call | tf_op jit(solution)/shard_map/own_part/pallas_call | solution.py:222
  182.0 3.4 %copy-done = f32[16,128,1024]{2,1,0:T(8,128)S(1)} copy-done((f32[16,128,1024]{2,1,0:T(8,128)S(1)}, f32[16,128,1024]{2,1,0:T(8,128)}, u32[]{:S(2)}) %copy-start) | copy-done | bytes 8388632
  185.4 11.1 %far_part.3 = (f32[16,128,1024]{2,1,0:T(8,128)S(1)}, bf16[16,128,1024]{2,1,0:T(8,128)(2,1)}) custom-call(s32[17]{0:T(128)S(1)} %copy-done.4, s32[96]{0:T(128)S(1)} %copy-done.5, s32[1]{0:T(128)} %bitcast.2.chosen, bf16[4,128,1024]{2,1,0:T(8,128)(2,1)S(1)} %collective-permute-done.6.refs_0_, ...), custom_call_target="tpu_custom_call", output_to_operand_aliasing={{0}: (6, {})} | custom-call | tf_op jit(solution)/shard_map/far_part/pallas_call | solution.py:334
  196.6 9.7 %far_part.4 = (f32[16,128,1024]{2,1,0:T(8,128)S(1)}, bf16[16,128,1024]{2,1,0:T(8,128)(2,1)}) custom-call(s32[17]{0:T(128)S(1)} %copy-done.4, s32[96]{0:T(128)S(1)} %copy-done.5, s32[1]{0:T(128)} %bitcast.2.chosen, bf16[4,128,1024]{2,1,0:T(8,128)(2,1)S(1)} %collective-permute-done.10.refs_1_.refs_0_, ...), custom_call_target="tpu_custom_call", output_to_operand_aliasing={{0}: (6, {}), {1}: (8, {})} | custom-call | tf_op jit(solution)/shard_map/far_part/pallas_call | solution.py:334
  206.3 4.0 %far_part.5 = (f32[16,128,1024]{2,1,0:T(8,128)S(1)}, bf16[16,128,1024]{2,1,0:T(8,128)(2,1)}) custom-call(s32[17]{0:T(128)S(1)} %copy-done.4, s32[96]{0:T(128)S(1)} %copy-done.5, s32[1]{0:T(128)} %bitcast.2.chosen, bf16[32,128,128]{2,1,0:T(8,128)(2,1)S(1)} %copy-done.3, ...), custom_call_target="tpu_custom_call", output_to_operand_aliasing={{0}: (5, {}), {1}: (7, {})} | custom-call | tf_op jit(solution)/shard_map/far_part/pallas_call | solution.py:334
  (49 shorter events, 0.1 us)
Async XLA Ops:
  0.0 38.3 %copy-start.17 = (s32[96]{0:T(128)S(1)}, s32[96]{0:T(128)}, u32[]{:S(2)}) copy-start(s32[96]{0:T(128)} %rows.1) | copy-start | bytes 1156
  0.0 38.3 %copy-start.18 = (s32[96]{0:T(128)S(1)}, s32[96]{0:T(128)}, u32[]{:S(2)}) copy-start(s32[96]{0:T(128)} %cols.3) | copy-start | bytes 1156
  0.0 30.7 %collective-permute-start.2 = (bf16[4,128,1024]{2,1,0:T(8,128)(2,1)}, bf16[4,128,1024]{2,1,0:T(8,128)(2,1)S(1)}, u32[]{:S(2)}, u32[]{:S(2)}) collective-permute-start(bf16[4,128,1024]{2,1,0:T(8,128)(2,1)} %refs_0_.1), channel_id=1, source_target_pairs={{0,2},{1,3},{2,0},{3,1},{4,6},{5,7},{6,4},{7,5},{8,10},{9,11},{10,... | collective-permute-start | bytes 3145736 | tf_op jit(solution)/shard_map/ppermute | solution.py:360
  3.0 27.8 %collective-permute-start.1 = (bf16[4,128,1024]{2,1,0:T(8,128)(2,1)}, bf16[4,128,1024]{2,1,0:T(8,128)(2,1)S(1)}, u32[]{:S(2)}, u32[]{:S(2)}) collective-permute-start(bf16[4,128,1024]{2,1,0:T(8,128)(2,1)} %refs_0_.1), channel_id=1, source_target_pairs={{4,8},{5,9},{6,10},{7,11},{8,4},{9,5},{10,6},{11,7},{20,24},{21,25... | collective-permute-start | bytes 3145736 | tf_op jit(solution)/shard_map/ppermute | solution.py:360
  3.7 27.3 %collective-permute-start = (bf16[4,128,1024]{2,1,0:T(8,128)(2,1)}, bf16[4,128,1024]{2,1,0:T(8,128)(2,1)}, u32[]{:S(2)}, u32[]{:S(2)}) collective-permute-start(bf16[4,128,1024]{2,1,0:T(8,128)(2,1)} %refs_0_.1), channel_id=1, source_target_pairs={{0,4},{1,5},{2,6},{3,7},{4,0},{5,1},{6,2},{7,3},{8,12},{9,13},{10,... | collective-permute-start | bytes 3145736 | tf_op jit(solution)/shard_map/ppermute | solution.py:360
  8.1 22.9 %collective-permute-start.3 = (bf16[4,128,1024]{2,1,0:T(8,128)(2,1)}, bf16[4,128,1024]{2,1,0:T(8,128)(2,1)}, u32[]{:S(2)}, u32[]{:S(2)}) collective-permute-start(bf16[4,128,1024]{2,1,0:T(8,128)(2,1)} %refs_0_.1), channel_id=1, source_target_pairs={{0,1},{1,0},{2,3},{3,2},{4,5},{5,4},{6,7},{7,6},{8,9},{9,8},{10,11... | collective-permute-start | bytes 3145736 | tf_op jit(solution)/shard_map/ppermute | solution.py:360
  8.8 21.9 %collective-permute-start.4 = (s32[2,96]{1,0:T(2,128)S(1)}, s32[2,96]{1,0:T(2,128)S(1)}, u32[]{:S(2)}, u32[]{:S(2)}) collective-permute-start(s32[2,96]{1,0:T(2,128)S(1)} %pad_add_fusion), channel_id=1, source_target_pairs={{0,8},{1,9},{2,10},{3,11},{4,12},{5,13},{6,14},{7,15},{8,0},{9,1},... | collective-permute-start | bytes 2312 | tf_op jit(solution)/shard_map/ppermute | solution.py:360
  12.8 1.9 copy-start.1
  14.7 0.6 copy-start.6
  20.4 12.4 %copy-start.7 = (bf16[32,128,128]{2,1,0:T(8,128)(2,1)}, bf16[32,128,128]{2,1,0:T(8,128)(2,1)S(1)}, u32[]{:S(2)}) copy-start(bf16[32,128,128]{2,1,0:T(8,128)(2,1)S(1)} %get-tuple-element.100) | copy-start | bytes 3145732
  30.7 1.0 copy-start.12
  32.8 23.8 %collective-permute-start.6 = (bf16[4,128,1024]{2,1,0:T(8,128)(2,1)}, bf16[4,128,1024]{2,1,0:T(8,128)(2,1)S(1)}, u32[]{:S(2)}, u32[]{:S(2)}) collective-permute-start(bf16[4,128,1024]{2,1,0:T(8,128)(2,1)} %broadcast_select_fusion.2), channel_id=1, source_target_pairs={{4,0},{5,1},{6,2},{7,3},{8,12},{9,13},{10,14},{11,15},{0,8},{1,9},... | collective-permute-start | bytes 3145736 | tf_op jit(solution)/shard_map/ppermute | solution.py:360
  35.6 21.1 %collective-permute-start.9 = (bf16[4,128,1024]{2,1,0:T(8,128)(2,1)}, bf16[4,128,1024]{2,1,0:T(8,128)(2,1)}, u32[]{:S(2)}, u32[]{:S(2)}) collective-permute-start(bf16[4,128,1024]{2,1,0:T(8,128)(2,1)} %copy-done.12), channel_id=1, source_target_pairs={{0,1},{1,0},{2,3},{3,2},{4,5},{5,4},{6,7},{7,6},{8,9},{9,8},{10,11... | collective-permute-start | bytes 3145736 | tf_op jit(solution)/shard_map/ppermute | solution.py:360
  35.6 21.1 %collective-permute-start.8 = (bf16[4,128,1024]{2,1,0:T(8,128)(2,1)}, bf16[4,128,1024]{2,1,0:T(8,128)(2,1)}, u32[]{:S(2)}, u32[]{:S(2)}) collective-permute-start(bf16[4,128,1024]{2,1,0:T(8,128)(2,1)} %collective-permute-done.refs_2_), channel_id=1, source_target_pairs={{0,1},{1,0},{2,3},{3,2},{4,5},{5,4},{6,7},{7,6},{8,9},{9,8},{10,11... | collective-permute-start | bytes 3145736 | tf_op jit(solution)/shard_map/ppermute | solution.py:360
  36.1 25.4 %collective-permute-start.7 = (bf16[4,128,1024]{2,1,0:T(8,128)(2,1)}, bf16[4,128,1024]{2,1,0:T(8,128)(2,1)}, u32[]{:S(2)}, u32[]{:S(2)}) collective-permute-start(bf16[4,128,1024]{2,1,0:T(8,128)(2,1)} %collective-permute-done.refs_2_), channel_id=1, source_target_pairs={{0,2},{1,3},{2,0},{3,1},{4,6},{5,7},{6,4},{7,5},{8,10},{9,11},{10,... | collective-permute-start | bytes 3145736 | tf_op jit(solution)/shard_map/ppermute | solution.py:360
  36.6 24.9 %collective-permute-start.5 = (bf16[4,128,1024]{2,1,0:T(8,128)(2,1)}, bf16[4,128,1024]{2,1,0:T(8,128)(2,1)}, u32[]{:S(2)}, u32[]{:S(2)}) collective-permute-start(bf16[4,128,1024]{2,1,0:T(8,128)(2,1)} %collective-permute-done.refs_2_), channel_id=1, source_target_pairs={{4,8},{5,9},{6,10},{7,11},{8,4},{9,5},{10,6},{11,7},{20,24},{21,25... | collective-permute-start | bytes 3145736 | tf_op jit(solution)/shard_map/ppermute | solution.py:360
  47.5 37.3 %copy-start.8 = (bf16[32,128,128]{2,1,0:T(8,128)(2,1)S(1)}, bf16[32,128,128]{2,1,0:T(8,128)(2,1)}, u32[]{:S(2)}) copy-start(bf16[32,128,128]{2,1,0:T(8,128)(2,1)} %copy-done.7) | copy-start | bytes 3145732
  56.7 72.2 %copy-start.9 = (bf16[4,128,1024]{2,1,0:T(8,128)(2,1)}, bf16[4,128,1024]{2,1,0:T(8,128)(2,1)S(1)}, u32[]{:S(2)}) copy-start(bf16[4,128,1024]{2,1,0:T(8,128)(2,1)S(1)} %broadcast_select_fusion.1.refs_4_) | copy-start | bytes 3145732
  61.6 45.7 %collective-permute-start.10 = (bf16[4,128,1024]{2,1,0:T(8,128)(2,1)S(1)}, bf16[4,128,1024]{2,1,0:T(8,128)(2,1)S(1)}, u32[]{:S(2)}, u32[]{:S(2)}) collective-permute-start(bf16[4,128,1024]{2,1,0:T(8,128)(2,1)S(1)} %broadcast_select_fusion), channel_id=1, source_target_pairs={{4,0},{5,1},{6,2},{7,3},{8,12},{9,13},{10,14},{11,15},{0,8},{1,9},... | collective-permute-start | bytes 3145736 | tf_op jit(solution)/shard_map/ppermute | solution.py:360
  83.8 24.9 %collective-permute-start.13 = (bf16[4,128,1024]{2,1,0:T(8,128)(2,1)}, bf16[4,128,1024]{2,1,0:T(8,128)(2,1)S(1)}, u32[]{:S(2)}, u32[]{:S(2)}) collective-permute-start(bf16[4,128,1024]{2,1,0:T(8,128)(2,1)} %collective-permute-done.7.refs_8_), channel_id=1, source_target_pairs={{0,1},{1,0},{2,3},{3,2},{4,5},{5,4},{6,7},{7,6},{8,9},{9,8},{10,11... | collective-permute-start | bytes 3145736 | tf_op jit(solution)/shard_map/ppermute | solution.py:360
  83.8 24.9 %collective-permute-start.12 = (bf16[4,128,1024]{2,1,0:T(8,128)(2,1)S(1)}, bf16[4,128,1024]{2,1,0:T(8,128)(2,1)S(1)}, u32[]{:S(2)}, u32[]{:S(2)}) collective-permute-start(bf16[4,128,1024]{2,1,0:T(8,128)(2,1)S(1)} %broadcast_select_fusion.1.refs_4_), channel_id=1, source_target_pairs={{0,1},{1,0},{2,3},{3,2},{4,5},{5,4},{6,7},{7,6},{8,9},{9,8},{10,11... | collective-permute-start | bytes 3145736 | tf_op jit(solution)/shard_map/ppermute | solution.py:360
  84.3 25.2 %collective-permute-start.11 = (bf16[4,128,1024]{2,1,0:T(8,128)(2,1)S(1)}, bf16[4,128,1024]{2,1,0:T(8,128)(2,1)}, u32[]{:S(2)}, u32[]{:S(2)}) collective-permute-start(bf16[4,128,1024]{2,1,0:T(8,128)(2,1)S(1)} %broadcast_select_fusion.1.refs_4_), channel_id=1, source_target_pairs={{0,2},{1,3},{2,0},{3,1},{4,6},{5,7},{6,4},{7,5},{8,10},{9,11},{10,... | collective-permute-start | bytes 3145736 | tf_op jit(solution)/shard_map/ppermute | solution.py:360
  84.8 44.1 %collective-permute-start.16 = (bf16[32,128,128]{2,1,0:T(8,128)(2,1)S(1)}, bf16[32,128,128]{2,1,0:T(8,128)(2,1)S(1)}, u32[]{:S(2)}, u32[]{:S(2)}) collective-permute-start(bf16[32,128,128]{2,1,0:T(8,128)(2,1)S(1)} %copy-done.8), channel_id=1, source_target_pairs={{0,8},{1,9},{2,10},{3,11},{12,4},{13,5},{14,6},{15,7},{16,24},{17,... | collective-permute-start | bytes 3145736 | tf_op jit(solution)/shard_map/ppermute | solution.py:360
  108.7 55.4 %copy-start.10 = (bf16[2,128,1024]{2,1,0:T(8,128)(2,1)}, bf16[2,128,1024]{2,1,0:T(8,128)(2,1)S(1)}, u32[]{:S(2)}) copy-start(bf16[2,128,1024]{2,1,0:T(8,128)(2,1)S(1)} %get-tuple-element.98.refs_2_) | copy-start | bytes 1572868
  108.7 55.4 %copy-start.11 = (bf16[2,128,1024]{2,1,0:T(8,128)(2,1)}, bf16[2,128,1024]{2,1,0:T(8,128)(2,1)S(1)}, u32[]{:S(2)}) copy-start(bf16[2,128,1024]{2,1,0:T(8,128)(2,1)S(1)} %get-tuple-element.97.refs_1_) | copy-start | bytes 1572868
  108.7 22.5 %copy-start.13 = (bf16[4,128,1024]{2,1,0:T(8,128)(2,1)}, bf16[4,128,1024]{2,1,0:T(8,128)(2,1)S(1)}, u32[]{:S(2)}) copy-start(bf16[4,128,1024]{2,1,0:T(8,128)(2,1)S(1)} %collective-permute-done.13.refs_9_) | copy-start | bytes 3145732
  108.7 22.5 %copy-start.14 = (bf16[4,128,1024]{2,1,0:T(8,128)(2,1)}, bf16[4,128,1024]{2,1,0:T(8,128)(2,1)S(1)}, u32[]{:S(2)}) copy-start(bf16[4,128,1024]{2,1,0:T(8,128)(2,1)S(1)} %collective-permute-done.12.refs_5_) | copy-start | bytes 3145732
  109.5 48.1 %collective-permute-start.14 = (bf16[2,128,1024]{2,1,0:T(8,128)(2,1)S(1)}, bf16[2,128,1024]{2,1,0:T(8,128)(2,1)}, u32[]{:S(2)}, u32[]{:S(2)}) collective-permute-start(bf16[2,128,1024]{2,1,0:T(8,128)(2,1)S(1)} %get-tuple-element.97.refs_1_), channel_id=1, source_target_pairs={{0,2},{1,3},{2,0},{3,1},{4,6},{5,7},{6,4},{7,5},{8,10},{9,11},{10,... | collective-permute-start | bytes 1572872 | tf_op jit(solution)/shard_map/ppermute | solution.py:360
  110.0 47.7 %collective-permute-start.15 = (bf16[2,128,1024]{2,1,0:T(8,128)(2,1)S(1)}, bf16[2,128,1024]{2,1,0:T(8,128)(2,1)}, u32[]{:S(2)}, u32[]{:S(2)}) collective-permute-start(bf16[2,128,1024]{2,1,0:T(8,128)(2,1)S(1)} %get-tuple-element.98.refs_2_), channel_id=1, source_target_pairs={{0,2},{1,3},{2,0},{3,1},{4,6},{5,7},{6,4},{7,5},{8,10},{9,11},{10,... | collective-permute-start | bytes 1572872 | tf_op jit(solution)/shard_map/ppermute | solution.py:360
  111.5 70.5 %collective-permute-start.19 = (bf16[48,128,128]{2,1,0:T(8,128)(2,1)}, bf16[48,128,128]{2,1,0:T(8,128)(2,1)}, u32[]{:S(2)}, u32[]{:S(2)}) collective-permute-start(bf16[48,128,128]{2,1,0:T(8,128)(2,1)} %get-tuple-element.116), channel_id=1, source_target_pairs={{4,12},{5,13},{6,14},{7,15},{8,0},{9,1},{10,2},{11,3},{20,28},{21,... | collective-permute-start | bytes 4718600 | tf_op jit(solution)/shard_map/ppermute | solution.py:360
  112.8 45.4 %collective-permute-start.21 = (bf16[2,128,1024]{2,1,0:T(8,128)(2,1)S(1)}, bf16[2,128,1024]{2,1,0:T(8,128)(2,1)}, u32[]{:S(2)}, u32[]{:S(2)}) collective-permute-start(bf16[2,128,1024]{2,1,0:T(8,128)(2,1)S(1)} %get-tuple-element.97.refs_1_), channel_id=1, source_target_pairs={{0,1},{1,0},{2,3},{3,2},{4,5},{5,4},{6,7},{7,6},{8,9},{9,8},{10,11... | collective-permute-start | bytes 1572872 | tf_op jit(solution)/shard_map/ppermute | solution.py:360
  128.9 1.0 copy-start.2
  129.9 66.6 %collective-permute-start.18 = (bf16[36,128,128]{2,1,0:T(8,128)(2,1)}, bf16[36,128,128]{2,1,0:T(8,128)(2,1)}, u32[]{:S(2)}, u32[]{:S(2)}) collective-permute-start(bf16[36,128,128]{2,1,0:T(8,128)(2,1)} %get-tuple-element.115), channel_id=1, source_target_pairs={{4,12},{5,13},{6,14},{7,15},{8,0},{9,1},{10,2},{11,3},{20,28},{21,... | collective-permute-start | bytes 3538952 | tf_op jit(solution)/shard_map/ppermute | solution.py:360
  157.6 2.0 collective-permute-start.22
  157.7 6.4 %collective-permute-start.20 = (bf16[4,128,1024]{2,1,0:T(8,128)(2,1)}, bf16[4,128,1024]{2,1,0:T(8,128)(2,1)}, u32[]{:S(2)}, u32[]{:S(2)}) collective-permute-start(bf16[4,128,1024]{2,1,0:T(8,128)(2,1)} %collective-permute-done.11.refs_10_), channel_id=1, source_target_pairs={{0,1},{1,0},{2,3},{3,2},{4,5},{5,4},{6,7},{7,6},{8,9},{9,8},{10,11... | collective-permute-start | bytes 3145736 | tf_op jit(solution)/shard_map/ppermute | solution.py:360
  158.2 3.1 %collective-permute-start.23 = (bf16[2,128,1024]{2,1,0:T(8,128)(2,1)}, bf16[2,128,1024]{2,1,0:T(8,128)(2,1)S(1)}, u32[]{:S(2)}, u32[]{:S(2)}) collective-permute-start(bf16[2,128,1024]{2,1,0:T(8,128)(2,1)} %collective-permute-done.14.refs_5_), channel_id=1, source_target_pairs={{0,1},{1,0},{2,3},{3,2},{4,5},{5,4},{6,7},{7,6},{8,9},{9,8},{10,11... | collective-permute-start | bytes 1572872 | tf_op jit(solution)/shard_map/ppermute | solution.py:360
  159.6 0.8 copy-start.15
  159.6 4.5 %collective-permute-start.24 = (bf16[2,128,1024]{2,1,0:T(8,128)(2,1)}, bf16[2,128,1024]{2,1,0:T(8,128)(2,1)}, u32[]{:S(2)}, u32[]{:S(2)}) collective-permute-start(bf16[2,128,1024]{2,1,0:T(8,128)(2,1)} %collective-permute-done.15.refs_6_), channel_id=1, source_target_pairs={{0,1},{1,0},{2,3},{3,2},{4,5},{5,4},{6,7},{7,6},{8,9},{9,8},{10,11... | collective-permute-start | bytes 1572872 | tf_op jit(solution)/shard_map/ppermute | solution.py:360
  161.3 0.8 copy-start.16
  162.1 44.2 %collective-permute-start.17 = (bf16[12,128,128]{2,1,0:T(8,128)(2,1)}, bf16[12,128,128]{2,1,0:T(8,128)(2,1)S(1)}, u32[]{:S(2)}, u32[]{:S(2)}) collective-permute-start(bf16[12,128,128]{2,1,0:T(8,128)(2,1)} %get-tuple-element.114), channel_id=1, source_target_pairs={{4,12},{5,13},{6,14},{7,15},{8,0},{9,1},{10,2},{11,3},{20,28},{21,... | collective-permute-start | bytes 1179656 | tf_op jit(solution)/shard_map/ppermute | solution.py:360
  164.1 17.9 %copy-start.4 = (s32[17]{0:T(128)S(1)}, s32[17]{0:T(128)}, u32[]{:S(2)}) copy-start(s32[17]{0:T(128)} %get-tuple-element.91.starts) | copy-start | bytes 208
  164.1 17.9 %copy-start.5 = (s32[96]{0:T(128)S(1)}, s32[96]{0:T(128)}, u32[]{:S(2)}) copy-start(s32[96]{0:T(128)} %get-tuple-element.92.block_at) | copy-start | bytes 1156
  182.0 3.4 %copy-start = (f32[16,128,1024]{2,1,0:T(8,128)S(1)}, f32[16,128,1024]{2,1,0:T(8,128)}, u32[]{:S(2)}) copy-start(f32[16,128,1024]{2,1,0:T(8,128)} %get-tuple-element.122.refs_3_) | copy-start | bytes 25165828
  185.4 11.1 %copy-start.3 = (bf16[32,128,128]{2,1,0:T(8,128)(2,1)S(1)}, bf16[32,128,128]{2,1,0:T(8,128)(2,1)}, u32[]{:S(2)}) copy-start(bf16[32,128,128]{2,1,0:T(8,128)(2,1)} %copy-done.2) | copy-start | bytes 3145732
  196.5 9.8 %slice-start = ((s8[8388608]{0:T(1024)(128)(4,1)}), s8[4194304]{0:T(1024)(128)(4,1)S(1)}, s32[]{:S(2)}) async-start(s8[8388608]{0:T(1024)(128)(4,1)} %bitcast.27), calls=%async_computation | async-start | bytes 8388608
  196.5 9.8 %slice-start.1 = ((s8[8388608]{0:T(1024)(128)(4,1)}), s8[4194304]{0:T(1024)(128)(4,1)S(1)}, s32[]{:S(2)}) async-start(s8[8388608]{0:T(1024)(128)(4,1)} %bitcast.27), calls=%async_computation.1 | async-start | bytes 8388608

commit v8 on v7

--- a/solution.py
+++ b/solution.py
@@ -10,9 +10,8 @@
 W = 32
 PPD = 16
 REUSE = 3
-QUAD = 4
 SHARES = (24, 18)
-COLUMNS = 256
+COLUMNS = 512
 MIB = 1024 * 1024
 SMEM = pl.BlockSpec(memory_space=pltpu.SMEM)
 VMEM = pl.BlockSpec(memory_space=pltpu.VMEM)
@@ -117,17 +116,19 @@
     )(tile_at, chosen, tiles)
 
 
-def add_row(sum_ref, begin, end, tile_of, block_of):
+def add_row(sum_ref, begin, end, depth, ready, tile_of, block_of):
     width = sum_ref.shape[1]
 
-    @pl.loop(0, (end - begin + QUAD - 1) // QUAD)
+    @pl.loop(0, (end - begin + depth - 1) // depth)
     def _(turn):
-        here = begin + turn * QUAD
-        places = [jnp.minimum(here + part, end - 1) for part in range(QUAD)]
-        left = [tile_of(places[0])]
-        for part in range(1, QUAD):
-            tile = tile_of(places[part])
-            left.append(jnp.where(here + part < end, tile, jnp.zeros_like(tile)))
+        here = begin + turn * depth
+        places = [jnp.minimum(here + part, end - 1) for part in range(depth)]
+        left = []
+        for part, place in enumerate(places):
+            inside = here + part < end
+            pl.when(inside)(functools.partial(ready, place))
+            tile = tile_of(place)
+            left.append(jnp.where(inside, tile, jnp.zeros_like(tile)))
         left = jnp.concatenate(left, axis=1)
         for column in range(0, width, COLUMNS):
             window = pl.ds(column, COLUMNS)
@@ -198,6 +199,8 @@
             sums.at[row],
             starts[group + row],
             starts[group + row + 1],
+            4 if fresh else 2,
+            lambda place: None,
             lambda place: tiles_ref[tile_at[place]],
             lambda place, window: own_blocks[block_at[place], :, window],
         )
@@ -247,7 +250,7 @@
     tile_refs, refs = refs[: len(segments)], refs[len(segments) :]
     sum_in, flip_in = refs[:2]
     refs = refs[3:] if base else refs[2:]
-    sum_out, result, tiles_ref, blocks, sums, rounded, tile_sem, block_sem, row_sems, out_sems = refs
+    sum_out, result, tiles_ref, blocks, sums, rounded, tile_sem, block_sems, row_sems, out_sems = refs
     count = tiles_ref.shape[0]
     stop = base + count
 
@@ -268,7 +271,7 @@
 
     @pl.loop(0, count)
     def _(number):
-        pltpu.make_async_copy(flip_in.at[block_at[base + number]], blocks.at[number], block_sem).start()
+        pltpu.make_async_copy(flip_in.at[block_at[base + number]], blocks.at[number], block_sems.at[number]).start()
 
     def each_row(action):
         @pl.loop(0, PPD)
@@ -290,7 +293,10 @@
 
     each_row(lambda row, complete: load(row).start())
     pltpu.make_async_copy(tiles_ref, tiles_ref, tile_sem).wait()
-    pltpu.make_async_copy(blocks, blocks, block_sem).wait()
+
+    def ready(place):
+        block = blocks.at[place - base]
+        pltpu.make_async_copy(block, block, block_sems.at[place - base]).wait()
 
     def add(row, complete):
         load(row).wait()
@@ -298,6 +304,8 @@
             sums.at[row],
             jnp.maximum(starts[row], base),
             jnp.minimum(starts[row + 1], stop),
+            4,
+            ready,
             lambda place: tiles_ref[place - base],
             lambda place, window: blocks[place - base, :, window],
         )
@@ -343,11 +351,11 @@
             pltpu.VMEM(whole, jnp.float32),
             pltpu.VMEM(whole, jnp.bfloat16),
             pltpu.SemaphoreType.DMA,
-            pltpu.SemaphoreType.DMA,
+            pltpu.SemaphoreType.DMA((count,)),
             pltpu.SemaphoreType.DMA((PPD,)),
             pltpu.SemaphoreType.DMA((PPD,)),
         ],
-        compiler_params=pltpu.CompilerParams(vmem_limit_bytes=36 * MIB),
+        compiler_params=pltpu.CompilerParams(vmem_limit_bytes=56 * MIB),
         name="far_part",
     )(starts, block_at, chosen, *[array for _, array in used], total, flipped, *given)
 
@@ -391,9 +399,10 @@
 
     near = send(shard, other_z)
     first = send(shard, across)
-    y_own = send(shard, other_y)
-    c_own = send(shard, other_core)
-    notes = send(jnp.stack([rows, cols]), opposite)
+    notes, later = together(jnp.stack([rows, cols]), shard)
+    y_own = send(later, other_y)
+    c_own = send(later, other_core)
+    notes = send(notes, opposite)
     order = tables(rows, cols, block_total)[1]
     count = tiles.shape[0]
     step = shard.size // tiles[0].size
@@ -425,13 +434,17 @@
     second = [jnp.where(in_centre, second[half], outer[half]) for half in halves]
     *second, y_first, c_first, c_y_near = together(*second, y_first, c_first, c_y_near)
 
-    far_centre = [send(part, from_centre) for part in parts[2:]]
+    far_centre = [send(parts[2], from_centre)]
     y_second = [send(half, other_y) for half in second]
     perm = flip_matrix(W)
     pieces = [shard, c_own, near, c_near, first, c_first, y_own, c_y_own, y_near, c_y_near, y_first]
     firsts = [owner(k, y + core) * local for y in (0, 2) for k in range(3) for core in (0, 1)][:11]
     early = own_part(own_tables, far_tables[3], tiles, pieces, first_blocks(firsts), perm)
-    *y_second, y_first, far_ends[2], total, flipped = together(*y_second, y_first, far_ends[2], *early)
+    y_second[0], y_second[1], second[0], second[1], y_first, total, flipped, *parts = together(
+        *y_second, *second, y_first, *early, *parts[3:]
+    )
+    far_centre += [send(part, from_centre) for part in parts]
+    *y_second, far_ends[2] = together(*y_second, far_ends[2])
 
     c_y_first = send(y_first, other_core)
     c_second = [send(half, other_core) for half in second]

time: 213 us -> 210 us (0.986)
  waiting for transfers between devices: 64 us -> 58 us
  local copies, waits for them, and re-layouts: 11 us -> 6.22 us
  starting transfers between devices: 45.5 us -> 49.4 us
  Pallas kernels: 83.3 us -> 86.9 us
  other arithmetic: 6.04 us -> 8.57 us
    ppermute x25, waiting for transfers between devices: 64 us -> 58 us  [send(): return lax.ppermute(value, 'tile', pairs)]
    pallas_call x3, Pallas kernels: 24.8 us -> 29.9 us  [far_part(): pl.pallas_call(functools.partial(far_kernel, base, [segment for segment,...]
    unnamed x42 -> x26, local copies, waits for them, and re-layouts: 9.13 us -> 4.41 us
    ppermute x25, starting transfers between devices: 45.5 us -> 49.4 us  [send(): return lax.ppermute(value, 'tile', pairs)]
  transfers between devices with their start and end apart: 25 -> 25, of which waited for: 9 -> 9; matrix products, arithmetic and copies ran while one was open for 3% -> 4% of each run, Pallas kernels for 38% -> 39%
where the time goes in v8:
time: 210 us; the launch traced here: 209 us
  Pallas kernels  86.9 us (41%)
  waiting for transfers between devices  58 us (28%)
  starting transfers between devices  49.4 us (24%)
  other arithmetic  8.57 us (4%)
  local copies, waits for them, and re-layouts  6.22 us (3%)
    ppermute x25, waiting for transfers between devices, send(): return lax.ppermute(value, 'tile', pairs)  58 us
    ppermute x25, starting transfers between devices, send(): return lax.ppermute(value, 'tile', pairs)  49.4 us
    pallas_call x2, Pallas kernels, own_part(): pl.pallas_call(functools.partial(own_kernel, counts, group, not earlier),...  40.1 us
    pallas_call x3, Pallas kernels, far_part(): pl.pallas_call(functools.partial(far_kernel, base, [segment for segment,...  29.9 us
    pallas_call x3, Pallas kernels, tables(): pl.pallas_call(tables_kernel, in_specs=[SMEM] * 2, out_specs=[SMEM] * 4,...  12.1 us
    pallas_call x1, Pallas kernels, sort_tiles(): pl.pallas_call(functools.partial(sort_kernel, choices), in_specs=[SMEM] *...  4.73 us
    unnamed x26, local copies, waits for them, and re-layouts  4.41 us
  transfers between devices with their start and end apart: 25, of which 9 were waited for; matrix products, arithmetic and copies ran while one was open for 4% of the time, Pallas kernels for 39%

profile of v8, /device:TPU:0, one launch (start us, length us, event | category | flops | bytes accessed | tf_op | source)
XLA Modules:
  0.0 209.4 jit_solution(3595462760909483061)
XLA Ops:
  0.0 0.7 pad_add_fusion
  0.7 0.5 collective-permute-start.3
  1.2 2.6 %collective-permute-start.2 = (bf16[4,128,1024]{2,1,0:T(8,128)(2,1)}, bf16[4,128,1024]{2,1,0:T(8,128)(2,1)}, u32[]{:S(2)}, u32[]{:S(2)}) collective-permute-start(bf16[4,128,1024]{2,1,0:T(8,128)(2,1)} %refs_0_.1), channel_id=1, source_target_pairs={{0,2},{1,3},{2,0},{3,1},{4,6},{5,7},{6,4},{7,5},{8,10},{9,11},{10,... | collective-permute-start | bytes 3145736 | tf_op jit(solution)/shard_map/ppermute | solution.py:368
  3.8 1.6 collective-permute-start.1
  5.4 3.5 %collective-permute-start = (bf16[4,128,1024]{2,1,0:T(8,128)(2,1)}, bf16[4,128,1024]{2,1,0:T(8,128)(2,1)}, u32[]{:S(2)}, u32[]{:S(2)}) collective-permute-start(bf16[4,128,1024]{2,1,0:T(8,128)(2,1)} %refs_0_.1), channel_id=1, source_target_pairs={{0,4},{1,5},{2,6},{3,7},{4,0},{5,1},{6,2},{7,3},{8,12},{9,13},{10,... | collective-permute-start | bytes 3145736 | tf_op jit(solution)/shard_map/ppermute | solution.py:368
  8.9 0.7 collective-permute-start.4
  9.6 4.0 %tables.3 = (s32[17]{0:T(128)}, s32[96]{0:T(128)}, s32[96]{0:T(128)}, s32[64]{0:T(128)}) custom-call(s32[96]{0:T(128)} %rows.1, s32[96]{0:T(128)} %cols.3), custom_call_target="tpu_custom_call" | custom-call | tf_op jit(solution)/shard_map/tables/pallas_call | solution.py:68
  13.6 0.0 copy-start
  13.6 1.9 copy-done
  15.5 0.7 copy-done.1
  16.2 4.7 %sort_tiles.1 = (bf16[4,128,1024]{2,1,0:T(8,128)(2,1)S(1)}, bf16[4,128,1024]{2,1,0:T(8,128)(2,1)S(1)}, bf16[32,128,128]{2,1,0:T(8,128)(2,1)}, bf16[48,128,128]{2...) custom-call(s32[96]{0:T(128)S(1)} %copy-done.1, s32[1]{0:T(128)} %bitcast.2.chosen, ...), custom_call_target="tpu_custom_call" | custom-call | tf_op jit(solution)/shard_map/sort_tiles/pallas_call | solution.py:108
  20.9 11.2 %collective-permute-done.4 = s32[2,96]{1,0:T(2,128)S(1)} collective-permute-done((s32[2,96]{1,0:T(2,128)S(1)}, s32[2,96]{1,0:T(2,128)S(1)}, u32[]{:S(2)}, u32[]{:S(2)}) %collective-permute-start.4) | collective-permute-done | bytes 800 | tf_op jit(solution)/shard_map/ppermute | solution.py:368
  32.1 0.0 collective-permute-done.3.refs_1_
  32.1 0.0 collective-permute-done.2.refs_6_
  32.2 0.0 collective-permute-done.1
  32.2 0.3 collective-permute-done.refs_2_
  32.5 1.1 broadcast_select_fusion.2
  33.6 3.8 %collective-permute-start.6 = (bf16[4,128,1024]{2,1,0:T(8,128)(2,1)}, bf16[4,128,1024]{2,1,0:T(8,128)(2,1)}, u32[]{:S(2)}, u32[]{:S(2)}) collective-permute-start(bf16[4,128,1024]{2,1,0:T(8,128)(2,1)} %broadcast_select_fusion.2), channel_id=1, source_target_pairs={{4,0},{5,1},{6,2},{7,3},{8,12},{9,13},{10,14},{11,15},{0,8},{1,9},... | collective-permute-start | bytes 3145736 | tf_op jit(solution)/shard_map/ppermute | solution.py:368
  37.4 0.5 collective-permute-start.8
  37.9 0.5 collective-permute-start.7
  38.4 1.7 collective-permute-start.5
  40.0 0.6 fusion.10.rows
  40.6 4.0 %tables.4 = (s32[33]{0:T(128)}, s32[96]{0:T(128)}, s32[96]{0:T(128)}, s32[64]{0:T(128)}) custom-call(s32[96]{0:T(128)} %fusion.10.rows, s32[96]{0:T(128)} %cols.3), custom_call_target="tpu_custom_call" | custom-call | tf_op jit(solution)/shard_map/tables/pallas_call | solution.py:68
  44.7 0.6 slice_bitcast_fusion
  45.2 4.0 %tables.5 = (s32[17]{0:T(128)}, s32[96]{0:T(128)}, s32[96]{0:T(128)}, s32[64]{0:T(128)}) custom-call(s32[96]{0:T(128)} %get-tuple-element.148.rows, s32[96]{0:T(128)} %get-tuple-element.147.cols), custom_call_target="tpu_custom_call" | custom-call | tf_op jit(solution)/shard_map/tables/pallas_call | solution.py:68
  49.3 9.9 %collective-permute-done.6.refs_0_ = bf16[4,128,1024]{2,1,0:T(8,128)(2,1)} collective-permute-done((bf16[4,128,1024]{2,1,0:T(8,128)(2,1)}, bf16[4,128,1024]{2,1,0:T(8,128)(2,1)}, u32[]{:S(2)}, u32[]{:S(2)}) %collective-permute-start.6) | collective-permute-done | bytes 1048608 | tf_op jit(solution)/shard_map/ppermute | solution.py:368
  59.2 1.3 broadcast_select_fusion.1.refs_4_
  60.5 0.0 collective-permute-done.8.refs_3_
  60.5 2.7 %collective-permute-done.7.refs_8_ = bf16[4,128,1024]{2,1,0:T(8,128)(2,1)} collective-permute-done((bf16[4,128,1024]{2,1,0:T(8,128)(2,1)}, bf16[4,128,1024]{2,1,0:T(8,128)(2,1)}, u32[]{:S(2)}, u32[]{:S(2)}) %collective-permute-start.7) | collective-permute-done | bytes 1048608 | tf_op jit(solution)/shard_map/ppermute | solution.py:368
  63.3 0.0 collective-permute-done.5
  63.3 0.1 broadcast_select_fusion
  63.4 22.8 %collective-permute-start.10 = (bf16[4,128,1024]{2,1,0:T(8,128)(2,1)S(1)}, bf16[4,128,1024]{2,1,0:T(8,128)(2,1)S(1)}, u32[]{:S(2)}, u32[]{:S(2)}) collective-permute-start(bf16[4,128,1024]{2,1,0:T(8,128)(2,1)S(1)} %broadcast_select_fusion), channel_id=1, source_target_pairs={{4,0},{5,1},{6,2},{7,3},{8,12},{9,13},{10,14},{11,15},{0,8},{1,9},... | collective-permute-start | bytes 3145736 | tf_op jit(solution)/shard_map/ppermute | solution.py:368
  86.2 0.5 collective-permute-start.12
  86.7 0.5 collective-permute-start.11
  87.2 3.0 %collective-permute-start.16 = (bf16[32,128,128]{2,1,0:T(8,128)(2,1)}, bf16[32,128,128]{2,1,0:T(8,128)(2,1)}, u32[]{:S(2)}, u32[]{:S(2)}) collective-permute-start(bf16[32,128,128]{2,1,0:T(8,128)(2,1)} %get-tuple-element.126), channel_id=1, source_target_pairs={{0,8},{1,9},{2,10},{3,11},{12,4},{13,5},{14,6},{15,7},{16,24},{17,... | collective-permute-start | bytes 3145736 | tf_op jit(solution)/shard_map/ppermute | solution.py:368
  90.2 19.6 %collective-permute-done.10.refs_1_.refs_0_ = bf16[4,128,1024]{2,1,0:T(8,128)(2,1)S(1)} collective-permute-done((bf16[4,128,1024]{2,1,0:T(8,128)(2,1)S(1)}, bf16[4,128,1024]{2,1,0:T(8,128)(2,1)S(1)}, u32[]{:S(2)}, u32[]{:S(2)}) %collective-permute-start.10) | collective-permute-done | bytes 1048608 | tf_op jit(solution)/shard_map/ppermute | solution.py:368
  109.8 2.5 %slice_select_fusion = (bf16[2,128,1024]{2,1,0:T(8,128)(2,1)S(1)}, bf16[2,128,1024]{2,1,0:T(8,128)(2,1)}) fusion(bf16[4,128,1024]{2,1,0:T(8,128)(2,1)S(1)} %collective-permute-done.10.refs_1_.refs_0_, bf16[4,128,1024]{2,1,0:T(8,128)(2,1)} %collective-permute-done.5, pred[]{:T(512)S(6)} %or.6), kind=kLoop, calls=%fused_computation.5 | loop fusion | flops 524288 | bytes 3145729 | tf_op jit(solution)/shard_map/jit(_where)/select_n | solution.py:434
  112.3 0.0 collective-permute-done.12.refs_5_
  112.3 0.6 collective-permute-start.14
  112.9 1.5 collective-permute-start.15
  114.4 1.3 collective-permute-start.19
  115.7 2.2 %fusion.perm_ref = bf16[1024,1024]{1,0:T(8,128)(2,1)} fusion(s32[1024]{0:T(1024)S(1)} %fusion.7), kind=kLoop, calls=%fused_computation.1 | loop fusion | flops 2097152 | bytes 2101248 | tf_op jit(solution)/shard_map/convert_element_type | solution.py:24
  117.9 0.6 stack.89.firsts
  118.5 22.9 %own_part.2 = (f32[16,128,1024]{2,1,0:T(8,128)}, bf16[32,128,1024]{2,1,0:T(8,128)(2,1)}) custom-call(s32[33]{0:T(128)} %get-tuple-element.110.starts, s32[96]{0:T(128)} %get-tuple-element.111.tile_at, s32[96]{0:T(128)} %get-tuple-element.112.block_at, s32[64]{0:T(128)} %get-tuple-element.113.own_slots, s32[64]{0:T(128)} %get-tuple-element.114.far_slots, ...), custom_call_target="tpu_custom_call" | custom-call | tf_op jit(solution)/shard_map/own_part/pallas_call | solution.py:225
  141.5 0.0 collective-permute-done.15.refs_6_
  141.5 0.0 collective-permute-done.16.refs_1_.refs_0_
  141.5 0.1 collective-permute-start.23
  141.6 1.3 collective-permute-start.18
  142.9 0.6 collective-permute-start.24
  143.4 0.1 collective-permute-start.20
  143.5 0.2 collective-permute-done.23.refs_7_
  143.7 0.3 collective-permute-start.21
  143.9 1.2 collective-permute-done.24.refs_8_
  145.2 0.4 collective-permute-start.22
  145.5 2.6 %collective-permute-done.21.refs_3_ = bf16[2,128,1024]{2,1,0:T(8,128)(2,1)S(1)} collective-permute-done((bf16[2,128,1024]{2,1,0:T(8,128)(2,1)}, bf16[2,128,1024]{2,1,0:T(8,128)(2,1)S(1)}, u32[]{:S(2)}, u32[]{:S(2)}) %collective-permute-start.21) | collective-permute-done | bytes 524320 | tf_op jit(solution)/shard_map/ppermute | solution.py:368
  148.2 0.8 copy-done.10
  148.9 1.3 collective-permute-start.17
  150.3 0.6 stack.99.firsts
  150.9 1.0 copy-done.7
  151.9 17.2 %own_part.3 = (f32[16,128,1024]{2,1,0:T(8,128)}, bf16[32,128,1024]{2,1,0:T(8,128)(2,1)}) custom-call(s32[33]{0:T(128)} %get-tuple-element.110.starts, s32[96]{0:T(128)} %get-tuple-element.111.tile_at, s32[96]{0:T(128)} %get-tuple-element.112.block_at, s32[64]{0:T(128)} %get-tuple-element.113.own_slots, ...), custom_call_target="tpu_custom_call", output_to_operand_aliasing={{0}: (17, {}), {1}: (18, {})} | custom-call | tf_op jit(solution)/shard_map/own_part/pallas_call | solution.py:225
  169.2 13.3 %far_part.3 = (f32[16,128,1024]{2,1,0:T(8,128)}, bf16[16,128,1024]{2,1,0:T(8,128)(2,1)}) custom-call(s32[17]{0:T(128)} %get-tuple-element.101.starts, s32[96]{0:T(128)} %get-tuple-element.102.block_at, s32[1]{0:T(128)} %bitcast.2.chosen, bf16[4,128,1024]{2,1,0:T(8,128)(2,1)} %collective-permute-done.6.refs_0_, ...), custom_call_target="tpu_custom_call", output_to_operand_aliasing={{0}: (6, {})} | custom-call | tf_op jit(solution)/shard_map/far_part/pallas_call | solution.py:342
  182.5 10.3 %collective-permute-done.18.refs_2_ = bf16[36,128,128]{2,1,0:T(8,128)(2,1)} collective-permute-done((bf16[36,128,128]{2,1,0:T(8,128)(2,1)}, bf16[36,128,128]{2,1,0:T(8,128)(2,1)}, u32[]{:S(2)}, u32[]{:S(2)}) %collective-permute-start.18) | collective-permute-done | bytes 1179680 | tf_op jit(solution)/shard_map/ppermute | solution.py:368
  192.7 11.2 %far_part.4 = (f32[16,128,1024]{2,1,0:T(8,128)}, bf16[16,128,1024]{2,1,0:T(8,128)(2,1)}) custom-call(s32[17]{0:T(128)} %get-tuple-element.101.starts, s32[96]{0:T(128)} %get-tuple-element.102.block_at, s32[1]{0:T(128)} %bitcast.2.chosen, bf16[4,128,1024]{2,1,0:T(8,128)(2,1)} %copy-done.2, ...), custom_call_target="tpu_custom_call", output_to_operand_aliasing={{0}: (6, {}), {1}: (8, {})} | custom-call | tf_op jit(solution)/shard_map/far_part/pallas_call | solution.py:342
  203.9 5.4 %far_part.5 = (f32[16,128,1024]{2,1,0:T(8,128)}, bf16[16,128,1024]{2,1,0:T(8,128)(2,1)}) custom-call(s32[17]{0:T(128)} %get-tuple-element.101.starts, s32[96]{0:T(128)} %get-tuple-element.102.block_at, s32[1]{0:T(128)} %bitcast.2.chosen, bf16[32,128,128]{2,1,0:T(8,128)(2,1)} %collective-permute-done.16.refs_1_.refs_0_, ...), custom_call_target="tpu_custom_call", output_to_operand_aliasing={{0}: (5, {}), {1}: (7, {})} | custom-call | tf_op jit(solution)/shard_map/far_part/pallas_call | solution.py:342
  (32 shorter events, 0.1 us)
Async XLA Ops:
  0.0 40.0 %copy-start.11 = (s32[96]{0:T(128)S(1)}, s32[96]{0:T(128)}, u32[]{:S(2)}) copy-start(s32[96]{0:T(128)} %rows.1) | copy-start | bytes 1156
  0.0 40.0 %copy-start.12 = (s32[96]{0:T(128)S(1)}, s32[96]{0:T(128)}, u32[]{:S(2)}) copy-start(s32[96]{0:T(128)} %cols.3) | copy-start | bytes 1156
  0.7 31.4 %collective-permute-start.3 = (bf16[4,128,1024]{2,1,0:T(8,128)(2,1)}, bf16[4,128,1024]{2,1,0:T(8,128)(2,1)}, u32[]{:S(2)}, u32[]{:S(2)}) collective-permute-start(bf16[4,128,1024]{2,1,0:T(8,128)(2,1)} %refs_0_.1), channel_id=1, source_target_pairs={{0,1},{1,0},{2,3},{3,2},{4,5},{5,4},{6,7},{7,6},{8,9},{9,8},{10,11... | collective-permute-start | bytes 3145736 | tf_op jit(solution)/shard_map/ppermute | solution.py:368
  1.2 31.0 %collective-permute-start.2 = (bf16[4,128,1024]{2,1,0:T(8,128)(2,1)}, bf16[4,128,1024]{2,1,0:T(8,128)(2,1)}, u32[]{:S(2)}, u32[]{:S(2)}) collective-permute-start(bf16[4,128,1024]{2,1,0:T(8,128)(2,1)} %refs_0_.1), channel_id=1, source_target_pairs={{0,2},{1,3},{2,0},{3,1},{4,6},{5,7},{6,4},{7,5},{8,10},{9,11},{10,... | collective-permute-start | bytes 3145736 | tf_op jit(solution)/shard_map/ppermute | solution.py:368
  3.8 28.4 %collective-permute-start.1 = (bf16[4,128,1024]{2,1,0:T(8,128)(2,1)}, bf16[4,128,1024]{2,1,0:T(8,128)(2,1)}, u32[]{:S(2)}, u32[]{:S(2)}) collective-permute-start(bf16[4,128,1024]{2,1,0:T(8,128)(2,1)} %refs_0_.1), channel_id=1, source_target_pairs={{4,8},{5,9},{6,10},{7,11},{8,4},{9,5},{10,6},{11,7},{20,24},{21,25... | collective-permute-start | bytes 3145736 | tf_op jit(solution)/shard_map/ppermute | solution.py:368
  5.4 27.0 %collective-permute-start = (bf16[4,128,1024]{2,1,0:T(8,128)(2,1)}, bf16[4,128,1024]{2,1,0:T(8,128)(2,1)}, u32[]{:S(2)}, u32[]{:S(2)}) collective-permute-start(bf16[4,128,1024]{2,1,0:T(8,128)(2,1)} %refs_0_.1), channel_id=1, source_target_pairs={{0,4},{1,5},{2,6},{3,7},{4,0},{5,1},{6,2},{7,3},{8,12},{9,13},{10,... | collective-permute-start | bytes 3145736 | tf_op jit(solution)/shard_map/ppermute | solution.py:368
  8.9 23.2 %collective-permute-start.4 = (s32[2,96]{1,0:T(2,128)S(1)}, s32[2,96]{1,0:T(2,128)S(1)}, u32[]{:S(2)}, u32[]{:S(2)}) collective-permute-start(s32[2,96]{1,0:T(2,128)S(1)} %pad_add_fusion), channel_id=1, source_target_pairs={{0,8},{1,9},{2,10},{3,11},{4,12},{5,13},{6,14},{7,15},{8,0},{9,1},... | collective-permute-start | bytes 2312 | tf_op jit(solution)/shard_map/ppermute | solution.py:368
  13.6 1.9 copy-start
  15.5 0.7 copy-start.1
  33.6 25.6 %collective-permute-start.6 = (bf16[4,128,1024]{2,1,0:T(8,128)(2,1)}, bf16[4,128,1024]{2,1,0:T(8,128)(2,1)}, u32[]{:S(2)}, u32[]{:S(2)}) collective-permute-start(bf16[4,128,1024]{2,1,0:T(8,128)(2,1)} %broadcast_select_fusion.2), channel_id=1, source_target_pairs={{4,0},{5,1},{6,2},{7,3},{8,12},{9,13},{10,14},{11,15},{0,8},{1,9},... | collective-permute-start | bytes 3145736 | tf_op jit(solution)/shard_map/ppermute | solution.py:368
  37.4 23.2 %collective-permute-start.9 = (bf16[4,128,1024]{2,1,0:T(8,128)(2,1)}, bf16[4,128,1024]{2,1,0:T(8,128)(2,1)}, u32[]{:S(2)}, u32[]{:S(2)}) collective-permute-start(bf16[4,128,1024]{2,1,0:T(8,128)(2,1)} %collective-permute-done.2.refs_6_), channel_id=1, source_target_pairs={{0,1},{1,0},{2,3},{3,2},{4,5},{5,4},{6,7},{7,6},{8,9},{9,8},{10,11... | collective-permute-start | bytes 3145736 | tf_op jit(solution)/shard_map/ppermute | solution.py:368
  37.4 23.2 %collective-permute-start.8 = (bf16[4,128,1024]{2,1,0:T(8,128)(2,1)}, bf16[4,128,1024]{2,1,0:T(8,128)(2,1)}, u32[]{:S(2)}, u32[]{:S(2)}) collective-permute-start(bf16[4,128,1024]{2,1,0:T(8,128)(2,1)} %collective-permute-done.refs_2_), channel_id=1, source_target_pairs={{0,1},{1,0},{2,3},{3,2},{4,5},{5,4},{6,7},{7,6},{8,9},{9,8},{10,11... | collective-permute-start | bytes 3145736 | tf_op jit(solution)/shard_map/ppermute | solution.py:368
  37.9 25.4 %collective-permute-start.7 = (bf16[4,128,1024]{2,1,0:T(8,128)(2,1)}, bf16[4,128,1024]{2,1,0:T(8,128)(2,1)}, u32[]{:S(2)}, u32[]{:S(2)}) collective-permute-start(bf16[4,128,1024]{2,1,0:T(8,128)(2,1)} %collective-permute-done.refs_2_), channel_id=1, source_target_pairs={{0,2},{1,3},{2,0},{3,1},{4,6},{5,7},{6,4},{7,5},{8,10},{9,11},{10,... | collective-permute-start | bytes 3145736 | tf_op jit(solution)/shard_map/ppermute | solution.py:368
  38.4 24.9 %collective-permute-start.5 = (bf16[4,128,1024]{2,1,0:T(8,128)(2,1)}, bf16[4,128,1024]{2,1,0:T(8,128)(2,1)}, u32[]{:S(2)}, u32[]{:S(2)}) collective-permute-start(bf16[4,128,1024]{2,1,0:T(8,128)(2,1)} %collective-permute-done.refs_2_), channel_id=1, source_target_pairs={{4,8},{5,9},{6,10},{7,11},{8,4},{9,5},{10,6},{11,7},{20,24},{21,25... | collective-permute-start | bytes 3145736 | tf_op jit(solution)/shard_map/ppermute | solution.py:368
  60.5 55.2 %copy-start.3 = (bf16[4,128,1024]{2,1,0:T(8,128)(2,1)}, bf16[4,128,1024]{2,1,0:T(8,128)(2,1)S(1)}, u32[]{:S(2)}) copy-start(bf16[4,128,1024]{2,1,0:T(8,128)(2,1)S(1)} %broadcast_select_fusion.1.refs_4_) | copy-start | bytes 3145732
  63.4 46.4 %collective-permute-start.10 = (bf16[4,128,1024]{2,1,0:T(8,128)(2,1)S(1)}, bf16[4,128,1024]{2,1,0:T(8,128)(2,1)S(1)}, u32[]{:S(2)}, u32[]{:S(2)}) collective-permute-start(bf16[4,128,1024]{2,1,0:T(8,128)(2,1)S(1)} %broadcast_select_fusion), channel_id=1, source_target_pairs={{4,0},{5,1},{6,2},{7,3},{8,12},{9,13},{10,14},{11,15},{0,8},{1,9},... | collective-permute-start | bytes 3145736 | tf_op jit(solution)/shard_map/ppermute | solution.py:368
  86.2 26.0 %collective-permute-start.13 = (bf16[4,128,1024]{2,1,0:T(8,128)(2,1)}, bf16[4,128,1024]{2,1,0:T(8,128)(2,1)S(1)}, u32[]{:S(2)}, u32[]{:S(2)}) collective-permute-start(bf16[4,128,1024]{2,1,0:T(8,128)(2,1)} %collective-permute-done.7.refs_8_), channel_id=1, source_target_pairs={{0,1},{1,0},{2,3},{3,2},{4,5},{5,4},{6,7},{7,6},{8,9},{9,8},{10,11... | collective-permute-start | bytes 3145736 | tf_op jit(solution)/shard_map/ppermute | solution.py:368
  86.2 26.1 %collective-permute-start.12 = (bf16[4,128,1024]{2,1,0:T(8,128)(2,1)S(1)}, bf16[4,128,1024]{2,1,0:T(8,128)(2,1)S(1)}, u32[]{:S(2)}, u32[]{:S(2)}) collective-permute-start(bf16[4,128,1024]{2,1,0:T(8,128)(2,1)S(1)} %broadcast_select_fusion.1.refs_4_), channel_id=1, source_target_pairs={{0,1},{1,0},{2,3},{3,2},{4,5},{5,4},{6,7},{7,6},{8,9},{9,8},{10,11... | collective-permute-start | bytes 3145736 | tf_op jit(solution)/shard_map/ppermute | solution.py:368
  86.7 25.6 %collective-permute-start.11 = (bf16[4,128,1024]{2,1,0:T(8,128)(2,1)S(1)}, bf16[4,128,1024]{2,1,0:T(8,128)(2,1)}, u32[]{:S(2)}, u32[]{:S(2)}) collective-permute-start(bf16[4,128,1024]{2,1,0:T(8,128)(2,1)S(1)} %broadcast_select_fusion.1.refs_4_), channel_id=1, source_target_pairs={{0,2},{1,3},{2,0},{3,1},{4,6},{5,7},{6,4},{7,5},{8,10},{9,11},{10,... | collective-permute-start | bytes 3145736 | tf_op jit(solution)/shard_map/ppermute | solution.py:368
  87.2 54.2 %collective-permute-start.16 = (bf16[32,128,128]{2,1,0:T(8,128)(2,1)}, bf16[32,128,128]{2,1,0:T(8,128)(2,1)}, u32[]{:S(2)}, u32[]{:S(2)}) collective-permute-start(bf16[32,128,128]{2,1,0:T(8,128)(2,1)} %get-tuple-element.126), channel_id=1, source_target_pairs={{0,8},{1,9},{2,10},{3,11},{12,4},{13,5},{14,6},{15,7},{16,24},{17,... | collective-permute-start | bytes 3145736 | tf_op jit(solution)/shard_map/ppermute | solution.py:368
  109.8 31.7 %copy-start.2 = (bf16[4,128,1024]{2,1,0:T(8,128)(2,1)}, bf16[4,128,1024]{2,1,0:T(8,128)(2,1)S(1)}, u32[]{:S(2)}) copy-start(bf16[4,128,1024]{2,1,0:T(8,128)(2,1)S(1)} %collective-permute-done.10.refs_1_.refs_0_) | copy-start | bytes 3145732
  112.3 32.9 %copy-start.4 = (bf16[2,128,1024]{2,1,0:T(8,128)(2,1)}, bf16[2,128,1024]{2,1,0:T(8,128)(2,1)S(1)}, u32[]{:S(2)}) copy-start(bf16[2,128,1024]{2,1,0:T(8,128)(2,1)S(1)} %get-tuple-element.133.refs_2_) | copy-start | bytes 1572868
  112.3 2.1 %copy-start.5 = (bf16[4,128,1024]{2,1,0:T(8,128)(2,1)}, bf16[4,128,1024]{2,1,0:T(8,128)(2,1)S(1)}, u32[]{:S(2)}) copy-start(bf16[4,128,1024]{2,1,0:T(8,128)(2,1)S(1)} %collective-permute-done.13.refs_9_) | copy-start | bytes 3145732
  112.3 3.4 %copy-start.6 = (bf16[4,128,1024]{2,1,0:T(8,128)(2,1)}, bf16[4,128,1024]{2,1,0:T(8,128)(2,1)S(1)}, u32[]{:S(2)}) copy-start(bf16[4,128,1024]{2,1,0:T(8,128)(2,1)S(1)} %collective-permute-done.12.refs_5_) | copy-start | bytes 3145732
  112.3 29.1 %collective-permute-start.14 = (bf16[2,128,1024]{2,1,0:T(8,128)(2,1)}, bf16[2,128,1024]{2,1,0:T(8,128)(2,1)}, u32[]{:S(2)}, u32[]{:S(2)}) collective-permute-start(bf16[2,128,1024]{2,1,0:T(8,128)(2,1)} %get-tuple-element.132.refs_1_), channel_id=1, source_target_pairs={{0,2},{1,3},{2,0},{3,1},{4,6},{5,7},{6,4},{7,5},{8,10},{9,11},{10,... | collective-permute-start | bytes 1572872 | tf_op jit(solution)/shard_map/ppermute | solution.py:368
  112.9 28.6 %collective-permute-start.15 = (bf16[2,128,1024]{2,1,0:T(8,128)(2,1)S(1)}, bf16[2,128,1024]{2,1,0:T(8,128)(2,1)}, u32[]{:S(2)}, u32[]{:S(2)}) collective-permute-start(bf16[2,128,1024]{2,1,0:T(8,128)(2,1)S(1)} %get-tuple-element.133.refs_2_), channel_id=1, source_target_pairs={{0,2},{1,3},{2,0},{3,1},{4,6},{5,7},{6,4},{7,5},{8,10},{9,11},{10,... | collective-permute-start | bytes 1572872 | tf_op jit(solution)/shard_map/ppermute | solution.py:368
  114.4 54.8 %collective-permute-start.19 = (bf16[48,128,128]{2,1,0:T(8,128)(2,1)S(1)}, bf16[48,128,128]{2,1,0:T(8,128)(2,1)}, u32[]{:S(2)}, u32[]{:S(2)}) collective-permute-start(bf16[48,128,128]{2,1,0:T(8,128)(2,1)S(1)} %get-tuple-element.130), channel_id=1, source_target_pairs={{4,12},{5,13},{6,14},{7,15},{8,0},{9,1},{10,2},{11,3},{20,28},{21,... | collective-permute-start | bytes 4718600 | tf_op jit(solution)/shard_map/ppermute | solution.py:368
  141.5 2.2 %collective-permute-start.23 = (bf16[2,128,1024]{2,1,0:T(8,128)(2,1)}, bf16[2,128,1024]{2,1,0:T(8,128)(2,1)S(1)}, u32[]{:S(2)}, u32[]{:S(2)}) collective-permute-start(bf16[2,128,1024]{2,1,0:T(8,128)(2,1)} %collective-permute-done.14.refs_5_), channel_id=1, source_target_pairs={{0,1},{1,0},{2,3},{3,2},{4,5},{5,4},{6,7},{7,6},{8,9},{9,8},{10,11... | collective-permute-start | bytes 1572872 | tf_op jit(solution)/shard_map/ppermute | solution.py:368
  141.6 51.2 %collective-permute-start.18 = (bf16[36,128,128]{2,1,0:T(8,128)(2,1)}, bf16[36,128,128]{2,1,0:T(8,128)(2,1)}, u32[]{:S(2)}, u32[]{:S(2)}) collective-permute-start(bf16[36,128,128]{2,1,0:T(8,128)(2,1)} %get-tuple-element.129), channel_id=1, source_target_pairs={{4,12},{5,13},{6,14},{7,15},{8,0},{9,1},{10,2},{11,3},{20,28},{21,... | collective-permute-start | bytes 3538952 | tf_op jit(solution)/shard_map/ppermute | solution.py:368
  142.9 2.3 %collective-permute-start.24 = (bf16[2,128,1024]{2,1,0:T(8,128)(2,1)}, bf16[2,128,1024]{2,1,0:T(8,128)(2,1)S(1)}, u32[]{:S(2)}, u32[]{:S(2)}) collective-permute-start(bf16[2,128,1024]{2,1,0:T(8,128)(2,1)} %collective-permute-done.15.refs_6_), channel_id=1, source_target_pairs={{0,1},{1,0},{2,3},{3,2},{4,5},{5,4},{6,7},{7,6},{8,9},{9,8},{10,11... | collective-permute-start | bytes 1572872 | tf_op jit(solution)/shard_map/ppermute | solution.py:368
  143.4 7.5 %collective-permute-start.20 = (bf16[4,128,1024]{2,1,0:T(8,128)(2,1)}, bf16[4,128,1024]{2,1,0:T(8,128)(2,1)S(1)}, u32[]{:S(2)}, u32[]{:S(2)}) collective-permute-start(bf16[4,128,1024]{2,1,0:T(8,128)(2,1)} %collective-permute-done.11.refs_10_), channel_id=1, source_target_pairs={{0,1},{1,0},{2,3},{3,2},{4,5},{5,4},{6,7},{7,6},{8,9},{9,8},{10,11... | collective-permute-start | bytes 3145736 | tf_op jit(solution)/shard_map/ppermute | solution.py:368
  143.7 1.9 copy-start.8
  143.7 4.5 %collective-permute-start.21 = (bf16[2,128,1024]{2,1,0:T(8,128)(2,1)}, bf16[2,128,1024]{2,1,0:T(8,128)(2,1)S(1)}, u32[]{:S(2)}, u32[]{:S(2)}) collective-permute-start(bf16[2,128,1024]{2,1,0:T(8,128)(2,1)} %get-tuple-element.132.refs_1_), channel_id=1, source_target_pairs={{0,1},{1,0},{2,3},{3,2},{4,5},{5,4},{6,7},{7,6},{8,9},{9,8},{10,11... | collective-permute-start | bytes 1572872 | tf_op jit(solution)/shard_map/ppermute | solution.py:368
  145.2 3.0 %copy-start.9 = (bf16[2,128,1024]{2,1,0:T(8,128)(2,1)}, bf16[2,128,1024]{2,1,0:T(8,128)(2,1)S(1)}, u32[]{:S(2)}) copy-start(bf16[2,128,1024]{2,1,0:T(8,128)(2,1)S(1)} %collective-permute-done.24.refs_8_) | copy-start | bytes 1572868
  145.2 5.7 %collective-permute-start.22 = (bf16[2,128,1024]{2,1,0:T(8,128)(2,1)S(1)}, bf16[2,128,1024]{2,1,0:T(8,128)(2,1)}, u32[]{:S(2)}, u32[]{:S(2)}) collective-permute-start(bf16[2,128,1024]{2,1,0:T(8,128)(2,1)S(1)} %get-tuple-element.133.refs_2_), channel_id=1, source_target_pairs={{0,1},{1,0},{2,3},{3,2},{4,5},{5,4},{6,7},{7,6},{8,9},{9,8},{10,11... | collective-permute-start | bytes 1572872 | tf_op jit(solution)/shard_map/ppermute | solution.py:368
  148.2 0.8 copy-start.10
  148.9 55.0 %collective-permute-start.17 = (bf16[12,128,128]{2,1,0:T(8,128)(2,1)S(1)}, bf16[12,128,128]{2,1,0:T(8,128)(2,1)}, u32[]{:S(2)}, u32[]{:S(2)}) collective-permute-start(bf16[12,128,128]{2,1,0:T(8,128)(2,1)S(1)} %get-tuple-element.128), channel_id=1, source_target_pairs={{4,12},{5,13},{6,14},{7,15},{8,0},{9,1},{10,2},{11,3},{20,28},{21,... | collective-permute-start | bytes 1179656 | tf_op jit(solution)/shard_map/ppermute | solution.py:368
  150.9 1.0 copy-start.7

commit v9 on v8

--- a/solution.py
+++ b/solution.py
@@ -11,7 +11,7 @@
 PPD = 16
 REUSE = 3
 SHARES = (24, 18)
-COLUMNS = 512
+COLUMNS = 256
 MIB = 1024 * 1024
 SMEM = pl.BlockSpec(memory_space=pltpu.SMEM)
 VMEM = pl.BlockSpec(memory_space=pltpu.VMEM)
@@ -116,19 +116,17 @@
     )(tile_at, chosen, tiles)
 
 
-def add_row(sum_ref, begin, end, depth, ready, tile_of, block_of):
+def add_row(sum_ref, begin, end, depth, tile_of, block_of):
     width = sum_ref.shape[1]
 
     @pl.loop(0, (end - begin + depth - 1) // depth)
     def _(turn):
         here = begin + turn * depth
         places = [jnp.minimum(here + part, end - 1) for part in range(depth)]
-        left = []
-        for part, place in enumerate(places):
-            inside = here + part < end
-            pl.when(inside)(functools.partial(ready, place))
-            tile = tile_of(place)
-            left.append(jnp.where(inside, tile, jnp.zeros_like(tile)))
+        left = [tile_of(places[0])]
+        for part in range(1, depth):
+            tile = tile_of(places[part])
+            left.append(jnp.where(here + part < end, tile, jnp.zeros_like(tile)))
         left = jnp.concatenate(left, axis=1)
         for column in range(0, width, COLUMNS):
             window = pl.ds(column, COLUMNS)
@@ -143,10 +141,6 @@
         sum_in, refs = refs[0], refs[2:]
     sum_out, flip_out, own_blocks, far_blocks, sums, own_list, far_list, own_sems, far_sems, row_sems = refs
 
-    if not fresh:
-        for row in range(PPD):
-            pltpu.make_async_copy(sum_in.at[row], sums.at[row], row_sems.at[row]).start()
-
     def fetch(slots, landing, sems, fetched):
         found = jnp.int32(0)
         for number, (piece, count) in enumerate(zip(pieces, counts)):
@@ -166,6 +160,9 @@
 
     far_found = fetch(far_slots, far_blocks, far_sems, far_list)
     own_found = fetch(own_slots, own_blocks, own_sems, own_list)
+    if not fresh:
+        for row in range(PPD):
+            pltpu.make_async_copy(sum_in.at[row], sums.at[row], row_sems.at[row]).start()
 
     def arrived(landing, sems, slot):
         pltpu.make_async_copy(landing.at[slot], landing.at[slot], sems.at[slot]).wait()
@@ -200,7 +197,6 @@
             starts[group + row],
             starts[group + row + 1],
             4 if fresh else 2,
-            lambda place: None,
             lambda place: tiles_ref[tile_at[place]],
             lambda place, window: own_blocks[block_at[place], :, window],
         )
@@ -294,18 +290,21 @@
     each_row(lambda row, complete: load(row).start())
     pltpu.make_async_copy(tiles_ref, tiles_ref, tile_sem).wait()
 
-    def ready(place):
-        block = blocks.at[place - base]
-        pltpu.make_async_copy(block, block, block_sems.at[place - base]).wait()
 
     def add(row, complete):
+        begin, end = jnp.maximum(starts[row], base), jnp.minimum(starts[row + 1], stop)
         load(row).wait()
+
+        @pl.loop(0, end - begin)
+        def _(number):
+            block = blocks.at[begin - base + number]
+            pltpu.make_async_copy(block, block, block_sems.at[begin - base + number]).wait()
+
         add_row(
             sums.at[row],
-            jnp.maximum(starts[row], base),
-            jnp.minimum(starts[row + 1], stop),
+            begin,
+            end,
             4,
-            ready,
             lambda place: tiles_ref[place - base],
             lambda place, window: blocks[place - base, :, window],
         )
@@ -380,6 +379,7 @@
     from_ends = [(i, i ^ 8) for i in range(16) if i not in centre]
     from_centre = [(i, i ^ 8) for i in centre]
     around = [(i, i ^ 4) for i in centre] + from_ends
+    around_crossed = [(i, i ^ 4) for i in centre] + [(i, i ^ 9) for i, _ in from_ends]
     other_z, other_y, other_core, opposite = (flipped_bit(bit) for bit in (4, 2, 1, 8))
     me = lax.axis_index("tile")
     z = me // 4
@@ -399,49 +399,49 @@
 
     near = send(shard, other_z)
     first = send(shard, across)
-    notes, later = together(jnp.stack([rows, cols]), shard)
-    y_own = send(later, other_y)
-    c_own = send(later, other_core)
-    notes = send(notes, opposite)
+    notes = send(jnp.stack([rows, cols]), opposite)
     order = tables(rows, cols, block_total)[1]
+    c_own = send(shard, other_core)
     count = tiles.shape[0]
     step = shard.size // tiles[0].size
     sizes = tile_parts(count)
     shapes = [shard.shape] * 2 + [(size,) + tiles.shape[1:] for size in [count - 2 * step] + sizes]
     parts = sort_tiles(order, at_end, tiles, [1, 1, 1, 0, 0, 0], shapes)
-    near, first, y_own, c_own, notes, *parts = together(near, first, y_own, c_own, notes, *parts)
+    near, first, c_own, notes, *parts = together(near, first, c_own, notes, *parts)
 
     outer = send(jnp.where(in_centre, first, parts[0]), around)
-    second = send(near, across)
+    second = send(jnp.where(in_centre, near, parts[1]), across + [(i, i ^ 1) for i, _ in from_ends])
+    y_own = send(shard, other_y)
     y_near = send(near, other_y)
     c_near = send(near, other_core)
-    c_y_own = send(y_own, other_core)
     own_tables = tables(keys, cols, block_total, 2 * PPD)
     far_tables = tables(notes[0], notes[1], block_total)
+    perm = flip_matrix(W)
     far_ends = [outer]
     first = jnp.where(in_centre, first, outer)
-    second, first, y_near, c_near, c_y_own, *rest = together(
-        second, first, y_near, c_near, c_y_own, *parts[1:], *own_tables, *far_tables
+    second, first, y_own, y_near, c_near, perm, *rest = together(
+        second, first, y_own, y_near, c_near, perm, *parts[2:], *own_tables, *far_tables
     )
-    parts, own_tables, far_tables = rest[:5], rest[5:9], rest[9:]
-
-    outer = send(jnp.where(in_centre, second, parts[0]), around)
-    far_ends += [outer, send(parts[1], from_ends)]
+    parts, own_tables, far_tables = rest[:4], rest[4:8], rest[8:]
+
+    outer = send(second, around_crossed)
     y_first = send(first, other_y)
     c_first = send(first, other_core)
+    c_y_own = send(y_own, other_core)
     c_y_near = send(y_near, other_core)
+    tiles_last, c_first = together(parts[0], c_first)
+    far_ends += [outer, send(tiles_last, from_ends)]
     halves = (slice(0, local // 2), slice(local // 2, None))
     second = [jnp.where(in_centre, second[half], outer[half]) for half in halves]
-    *second, y_first, c_first, c_y_near = together(*second, y_first, c_first, c_y_near)
-
-    far_centre = [send(parts[2], from_centre)]
+    *second, y_first, c_first, c_y_own, c_y_near = together(*second, y_first, c_first, c_y_own, c_y_near)
+
+    far_centre = [send(parts[1], from_centre)]
     y_second = [send(half, other_y) for half in second]
-    perm = flip_matrix(W)
     pieces = [shard, c_own, near, c_near, first, c_first, y_own, c_y_own, y_near, c_y_near, y_first]
     firsts = [owner(k, y + core) * local for y in (0, 2) for k in range(3) for core in (0, 1)][:11]
     early = own_part(own_tables, far_tables[3], tiles, pieces, first_blocks(firsts), perm)
     y_second[0], y_second[1], second[0], second[1], y_first, total, flipped, *parts = together(
-        *y_second, *second, y_first, *early, *parts[3:]
+        *y_second, *second, y_first, *early, *parts[2:]
     )
     far_centre += [send(part, from_centre) for part in parts]
     *y_second, far_ends[2] = together(*y_second, far_ends[2])

time: 210 us -> 210 us (level)
  Pallas kernels: 86.9 us -> 82.8 us
  starting transfers between devices: 49.4 us -> 51.5 us
    unnamed x26 -> x28, local copies, waits for them, and re-layouts: 4.41 us -> 6.11 us
  transfers between devices with their start and end apart: 25 -> 25, of which waited for: 9 -> 9; matrix products, arithmetic and copies ran while one was open for 4% -> 5% of each run, Pallas kernels for 39% -> 37%
where the time goes in v9:
time: 210 us
  Pallas kernels  82.8 us (39%)
  waiting for transfers between devices  57.4 us (27%)
  starting transfers between devices  51.5 us (25%)
  other arithmetic  9.66 us (5%)
  local copies, waits for them, and re-layouts  7.9 us (4%)
    ppermute x25, waiting for transfers between devices, send(): return lax.ppermute(value, 'tile', pairs)  57.4 us
    ppermute x25, starting transfers between devices, send(): return lax.ppermute(value, 'tile', pairs)  51.5 us
    pallas_call x2, Pallas kernels, own_part(): pl.pallas_call(functools.partial(own_kernel, counts, group, not earlier),...  38.2 us
    pallas_call x3, Pallas kernels, far_part(): pl.pallas_call(functools.partial(far_kernel, base, [segment for segment,...  29.2 us
    pallas_call x3, Pallas kernels, tables(): pl.pallas_call(tables_kernel, in_specs=[SMEM] * 2, out_specs=[SMEM] * 4,...  12.1 us
    unnamed x28, local copies, waits for them, and re-layouts  6.11 us
  transfers between devices with their start and end apart: 25, of which 9 were waited for; matrix products, arithmetic and copies ran while one was open for 5% of the time, Pallas kernels for 37%

profile of v9, /device:TPU:0, one launch (start us, length us, event | category | flops | bytes accessed | tf_op | source)
XLA Modules:
  0.0 209.6 jit_solution(7722436325296205728)
XLA Ops:
  0.0 0.5 collective-permute-start.2
  0.5 1.6 collective-permute-start.1
  2.1 4.5 %collective-permute-start = (bf16[4,128,1024]{2,1,0:T(8,128)(2,1)}, bf16[4,128,1024]{2,1,0:T(8,128)(2,1)}, u32[]{:S(2)}, u32[]{:S(2)}) collective-permute-start(bf16[4,128,1024]{2,1,0:T(8,128)(2,1)} %refs_0_.1), channel_id=1, source_target_pairs={{0,4},{1,5},{2,6},{3,7},{4,0},{5,1},{6,2},{7,3},{8,12},{9,13},{10,... | collective-permute-start | bytes 3145736 | tf_op jit(solution)/shard_map/ppermute | solution.py:367
  6.6 1.5 collective-permute-start.6
  8.1 0.7 pad_add_fusion
  8.8 0.7 collective-permute-start.3
  9.5 4.0 %tables.3 = (s32[17]{0:T(128)}, s32[96]{0:T(128)}, s32[96]{0:T(128)}, s32[64]{0:T(128)}) custom-call(s32[96]{0:T(128)} %rows.1, s32[96]{0:T(128)} %cols.3), custom_call_target="tpu_custom_call" | custom-call | tf_op jit(solution)/shard_map/tables/pallas_call | solution.py:68
  13.5 0.0 copy-start
  13.5 1.9 copy-done
  15.4 0.7 copy-done.1
  16.1 3.3 %sort_tiles.1 = (bf16[4,128,1024]{2,1,0:T(8,128)(2,1)S(1)}, bf16[4,128,1024]{2,1,0:T(8,128)(2,1)S(1)}, bf16[32,128,128]{2,1,0:T(8,128)(2,1)S(1)}, bf16[48,128,12...) custom-call(s32[96]{0:T(128)S(1)} %copy-done.1, s32[1]{0:T(128)} %bitcast.2.chosen, ...), custom_call_target="tpu_custom_call" | custom-call | tf_op jit(solution)/shard_map/sort_tiles/pallas_call | solution.py:108
  19.4 1.0 copy-done.2
  20.4 9.8 %collective-permute-done.3 = s32[2,96]{1,0:T(2,128)S(1)} collective-permute-done((s32[2,96]{1,0:T(2,128)S(1)}, s32[2,96]{1,0:T(2,128)S(1)}, u32[]{:S(2)}, u32[]{:S(2)}) %collective-permute-start.3) | collective-permute-done | bytes 800 | tf_op jit(solution)/shard_map/ppermute | solution.py:367
  30.2 0.3 collective-permute-done.refs_2_
  30.5 0.0 collective-permute-start.8
  30.5 1.5 collective-permute-start.7
  32.0 1.1 broadcast_select_fusion.1
  33.1 3.9 %collective-permute-start.5 = (bf16[4,128,1024]{2,1,0:T(8,128)(2,1)}, bf16[4,128,1024]{2,1,0:T(8,128)(2,1)}, u32[]{:S(2)}, u32[]{:S(2)}) collective-permute-start(bf16[4,128,1024]{2,1,0:T(8,128)(2,1)} %broadcast_select_fusion.1), channel_id=1, source_target_pairs={{4,0},{5,1},{6,2},{7,3},{8,12},{9,13},{10,14},{11,15},{0,8},{1,9},... | collective-permute-start | bytes 3145736 | tf_op jit(solution)/shard_map/ppermute | solution.py:367
  37.0 1.1 broadcast_select_fusion.2
  38.1 0.0 collective-permute-start.4
  38.1 0.5 fusion.10.rows
  38.6 4.0 %tables.4 = (s32[33]{0:T(128)}, s32[96]{0:T(128)}, s32[96]{0:T(128)}, s32[64]{0:T(128)}) custom-call(s32[96]{0:T(128)} %fusion.10.rows, s32[96]{0:T(128)} %cols.3), custom_call_target="tpu_custom_call" | custom-call | tf_op jit(solution)/shard_map/tables/pallas_call | solution.py:68
  42.7 2.2 %fusion.perm_ref = bf16[1024,1024]{1,0:T(8,128)(2,1)} fusion(s32[1024]{0:T(1024)S(1)} %fusion.7), kind=kLoop, calls=%fused_computation.1 | loop fusion | flops 2097152 | bytes 2101248 | tf_op jit(solution)/shard_map/convert_element_type | solution.py:24
  44.9 0.5 slice_bitcast_fusion
  45.4 4.0 %tables.5 = (s32[17]{0:T(128)}, s32[96]{0:T(128)}, s32[96]{0:T(128)}, s32[64]{0:T(128)}) custom-call(s32[96]{0:T(128)} %get-tuple-element.148.rows, s32[96]{0:T(128)} %get-tuple-element.147.cols), custom_call_target="tpu_custom_call" | custom-call | tf_op jit(solution)/shard_map/tables/pallas_call | solution.py:68
  49.5 10.7 %collective-permute-done.5.refs_0_ = bf16[4,128,1024]{2,1,0:T(8,128)(2,1)} collective-permute-done((bf16[4,128,1024]{2,1,0:T(8,128)(2,1)}, bf16[4,128,1024]{2,1,0:T(8,128)(2,1)}, u32[]{:S(2)}, u32[]{:S(2)}) %collective-permute-start.5) | collective-permute-done | bytes 1048608 | tf_op jit(solution)/shard_map/ppermute | solution.py:367
  60.1 1.3 broadcast_select_fusion.refs_4_
  61.5 0.0 collective-permute-done.6.refs_6_
  61.5 0.0 collective-permute-done.8.refs_3_
  61.5 0.0 collective-permute-done.7.refs_8_
  61.5 0.1 collective-permute-start.11
  61.6 24.5 %collective-permute-start.9 = (bf16[4,128,1024]{2,1,0:T(8,128)(2,1)}, bf16[4,128,1024]{2,1,0:T(8,128)(2,1)S(1)}, u32[]{:S(2)}, u32[]{:S(2)}) collective-permute-start(bf16[4,128,1024]{2,1,0:T(8,128)(2,1)} %collective-permute-done.4), channel_id=1, source_target_pairs={{4,0},{5,1},{6,2},{7,3},{8,12},{9,13},{10,14},{11,15},{0,9},{1,8},... | collective-permute-start | bytes 3145736 | tf_op jit(solution)/shard_map/ppermute | solution.py:367
  86.0 0.1 collective-permute-start.12
  86.1 0.4 collective-permute-start.13
  86.6 0.5 collective-permute-start.10
  87.1 0.0 collective-permute-done.11.refs_5_
  87.1 1.0 copy-done.5
  88.1 4.4 %collective-permute-start.16 = (bf16[32,128,128]{2,1,0:T(8,128)(2,1)}, bf16[32,128,128]{2,1,0:T(8,128)(2,1)}, u32[]{:S(2)}, u32[]{:S(2)}) collective-permute-start(bf16[32,128,128]{2,1,0:T(8,128)(2,1)} %copy-done.2), channel_id=1, source_target_pairs={{0,8},{1,9},{2,10},{3,11},{12,4},{13,5},{14,6},{15,7},{16,24},{17,... | collective-permute-start | bytes 3145736 | tf_op jit(solution)/shard_map/ppermute | solution.py:367
  92.5 17.4 %collective-permute-done.9.refs_1_.refs_0_ = bf16[4,128,1024]{2,1,0:T(8,128)(2,1)S(1)} collective-permute-done((bf16[4,128,1024]{2,1,0:T(8,128)(2,1)}, bf16[4,128,1024]{2,1,0:T(8,128)(2,1)S(1)}, u32[]{:S(2)}, u32[]{:S(2)}) %collective-permute-start.9) | collective-permute-done | bytes 1048608 | tf_op jit(solution)/shard_map/ppermute | solution.py:367
  109.9 2.7 %slice_select_fusion = (bf16[2,128,1024]{2,1,0:T(8,128)(2,1)}, bf16[2,128,1024]{2,1,0:T(8,128)(2,1)}) fusion(bf16[4,128,1024]{2,1,0:T(8,128)(2,1)S(1)} %collective-permute-done.9.refs_1_.refs_0_, bf16[4,128,1024]{2,1,0:T(8,128)(2,1)} %collective-permute-done.4, pred[]{:T(512)S(6)} %or.6), kind=kLoop, calls=%fused_computation.5 | loop fusion | flops 524288 | bytes 3145729 | tf_op jit(solution)/shard_map/jit(_where)/select_n | solution.py:435
  112.6 0.6 collective-permute-start.14
  113.2 1.5 collective-permute-start.15
  114.7 1.3 collective-permute-start.19
  116.0 0.6 stack.89.firsts
  116.6 23.4 %own_part.2 = (f32[16,128,1024]{2,1,0:T(8,128)}, bf16[32,128,1024]{2,1,0:T(8,128)(2,1)}) custom-call(s32[33]{0:T(128)} %get-tuple-element.109.starts, s32[96]{0:T(128)} %get-tuple-element.110.tile_at, s32[96]{0:T(128)} %get-tuple-element.111.block_at, s32[64]{0:T(128)} %get-tuple-element.112.own_slots, s32[64]{0:T(128)} %get-tuple-element.113.far_slots, ...), custom_call_target="tpu_custom_call" | custom-call | tf_op jit(solution)/shard_map/own_part/pallas_call | solution.py:221
  140.1 0.1 collective-permute-start.21
  140.2 1.3 collective-permute-start.18
  141.5 0.6 collective-permute-start.22
  142.0 0.1 collective-permute-start.20
  142.1 0.2 collective-permute-done.21.refs_3_
  142.3 0.3 collective-permute-start.23
  142.5 1.2 collective-permute-done.22.refs_4_
  143.8 0.4 collective-permute-start.24
  144.1 1.1 collective-permute-done.23.refs_7_
  145.3 0.8 copy-done.10
  146.1 1.3 collective-permute-start.17
  147.4 0.7 stack.99.firsts
  148.0 14.8 %own_part.3 = (f32[16,128,1024]{2,1,0:T(8,128)}, bf16[32,128,1024]{2,1,0:T(8,128)(2,1)}) custom-call(s32[33]{0:T(128)} %get-tuple-element.109.starts, s32[96]{0:T(128)} %get-tuple-element.110.tile_at, s32[96]{0:T(128)} %get-tuple-element.111.block_at, s32[64]{0:T(128)} %get-tuple-element.112.own_slots, ...), custom_call_target="tpu_custom_call", output_to_operand_aliasing={{0}: (17, {}), {1}: (18, {})} | custom-call | tf_op jit(solution)/shard_map/own_part/pallas_call | solution.py:221
  162.9 4.6 %collective-permute-done.19.refs_2_ = bf16[48,128,128]{2,1,0:T(8,128)(2,1)} collective-permute-done((bf16[48,128,128]{2,1,0:T(8,128)(2,1)S(1)}, bf16[48,128,128]{2,1,0:T(8,128)(2,1)}, u32[]{:S(2)}, u32[]{:S(2)}) %collective-permute-start.19) | collective-permute-done | bytes 1572896 | tf_op jit(solution)/shard_map/ppermute | solution.py:367
  167.5 13.1 %far_part.3 = (f32[16,128,1024]{2,1,0:T(8,128)}, bf16[16,128,1024]{2,1,0:T(8,128)(2,1)}) custom-call(s32[17]{0:T(128)} %get-tuple-element.98.starts, s32[96]{0:T(128)} %get-tuple-element.99.block_at, s32[1]{0:T(128)} %bitcast.2.chosen, bf16[4,128,1024]{2,1,0:T(8,128)(2,1)} %collective-permute-done.5.refs_0_, ...), custom_call_target="tpu_custom_call", output_to_operand_aliasing={{0}: (6, {})} | custom-call | tf_op jit(solution)/shard_map/far_part/pallas_call | solution.py:341
  180.6 12.2 %collective-permute-done.18.refs_2_ = bf16[36,128,128]{2,1,0:T(8,128)(2,1)} collective-permute-done((bf16[36,128,128]{2,1,0:T(8,128)(2,1)S(1)}, bf16[36,128,128]{2,1,0:T(8,128)(2,1)}, u32[]{:S(2)}, u32[]{:S(2)}) %collective-permute-start.18) | collective-permute-done | bytes 1179680 | tf_op jit(solution)/shard_map/ppermute | solution.py:367
  192.8 10.8 %far_part.4 = (f32[16,128,1024]{2,1,0:T(8,128)}, bf16[16,128,1024]{2,1,0:T(8,128)(2,1)}) custom-call(s32[17]{0:T(128)} %get-tuple-element.98.starts, s32[96]{0:T(128)} %get-tuple-element.99.block_at, s32[1]{0:T(128)} %bitcast.2.chosen, bf16[4,128,1024]{2,1,0:T(8,128)(2,1)} %copy-done.3, ...), custom_call_target="tpu_custom_call", output_to_operand_aliasing={{0}: (6, {}), {1}: (8, {})} | custom-call | tf_op jit(solution)/shard_map/far_part/pallas_call | solution.py:341
  203.5 0.7 copy-done.11
  204.3 5.3 %far_part.5 = (f32[16,128,1024]{2,1,0:T(8,128)}, bf16[16,128,1024]{2,1,0:T(8,128)(2,1)}) custom-call(s32[17]{0:T(128)} %get-tuple-element.98.starts, s32[96]{0:T(128)} %get-tuple-element.99.block_at, s32[1]{0:T(128)} %bitcast.2.chosen, bf16[32,128,128]{2,1,0:T(8,128)(2,1)} %collective-permute-done.16.refs_1_.refs_0_, ...), custom_call_target="tpu_custom_call", output_to_operand_aliasing={{0}: (5, {}), {1}: (7, {})} | custom-call | tf_op jit(solution)/shard_map/far_part/pallas_call | solution.py:341
  (34 shorter events, 0.1 us)
Async XLA Ops:
  0.0 30.2 %collective-permute-start.2 = (bf16[4,128,1024]{2,1,0:T(8,128)(2,1)}, bf16[4,128,1024]{2,1,0:T(8,128)(2,1)}, u32[]{:S(2)}, u32[]{:S(2)}) collective-permute-start(bf16[4,128,1024]{2,1,0:T(8,128)(2,1)} %refs_0_.1), channel_id=1, source_target_pairs={{0,1},{1,0},{2,3},{3,2},{4,5},{5,4},{6,7},{7,6},{8,9},{9,8},{10,11... | collective-permute-start | bytes 3145736 | tf_op jit(solution)/shard_map/ppermute | solution.py:367
  0.5 29.7 %collective-permute-start.1 = (bf16[4,128,1024]{2,1,0:T(8,128)(2,1)}, bf16[4,128,1024]{2,1,0:T(8,128)(2,1)}, u32[]{:S(2)}, u32[]{:S(2)}) collective-permute-start(bf16[4,128,1024]{2,1,0:T(8,128)(2,1)} %refs_0_.1), channel_id=1, source_target_pairs={{4,8},{5,9},{6,10},{7,11},{8,4},{9,5},{10,6},{11,7},{20,24},{21,25... | collective-permute-start | bytes 3145736 | tf_op jit(solution)/shard_map/ppermute | solution.py:367
  2.1 28.4 %collective-permute-start = (bf16[4,128,1024]{2,1,0:T(8,128)(2,1)}, bf16[4,128,1024]{2,1,0:T(8,128)(2,1)}, u32[]{:S(2)}, u32[]{:S(2)}) collective-permute-start(bf16[4,128,1024]{2,1,0:T(8,128)(2,1)} %refs_0_.1), channel_id=1, source_target_pairs={{0,4},{1,5},{2,6},{3,7},{4,0},{5,1},{6,2},{7,3},{8,12},{9,13},{10,... | collective-permute-start | bytes 3145736 | tf_op jit(solution)/shard_map/ppermute | solution.py:367
  6.6 54.9 %collective-permute-start.6 = (bf16[4,128,1024]{2,1,0:T(8,128)(2,1)}, bf16[4,128,1024]{2,1,0:T(8,128)(2,1)}, u32[]{:S(2)}, u32[]{:S(2)}) collective-permute-start(bf16[4,128,1024]{2,1,0:T(8,128)(2,1)} %refs_0_.1), channel_id=1, source_target_pairs={{0,2},{1,3},{2,0},{3,1},{4,6},{5,7},{6,4},{7,5},{8,10},{9,11},{10,... | collective-permute-start | bytes 3145736 | tf_op jit(solution)/shard_map/ppermute | solution.py:367
  8.8 21.4 %collective-permute-start.3 = (s32[2,96]{1,0:T(2,128)S(1)}, s32[2,96]{1,0:T(2,128)S(1)}, u32[]{:S(2)}, u32[]{:S(2)}) collective-permute-start(s32[2,96]{1,0:T(2,128)S(1)} %pad_add_fusion), channel_id=1, source_target_pairs={{0,8},{1,9},{2,10},{3,11},{4,12},{5,13},{6,14},{7,15},{8,0},{9,1},... | collective-permute-start | bytes 2312 | tf_op jit(solution)/shard_map/ppermute | solution.py:367
  13.5 1.9 copy-start
  15.4 0.7 copy-start.1
  16.1 22.0 %copy-start.12 = (s32[96]{0:T(128)S(1)}, s32[96]{0:T(128)}, u32[]{:S(2)}) copy-start(s32[96]{0:T(128)} %rows.1) | copy-start | bytes 1156
  16.1 22.0 %copy-start.13 = (s32[96]{0:T(128)S(1)}, s32[96]{0:T(128)}, u32[]{:S(2)}) copy-start(s32[96]{0:T(128)} %cols.3) | copy-start | bytes 1156
  19.4 1.0 copy-start.2
  30.5 31.0 %collective-permute-start.8 = (bf16[4,128,1024]{2,1,0:T(8,128)(2,1)}, bf16[4,128,1024]{2,1,0:T(8,128)(2,1)}, u32[]{:S(2)}, u32[]{:S(2)}) collective-permute-start(bf16[4,128,1024]{2,1,0:T(8,128)(2,1)} %collective-permute-done.refs_2_), channel_id=1, source_target_pairs={{0,1},{1,0},{2,3},{3,2},{4,5},{5,4},{6,7},{7,6},{8,9},{9,8},{10,11... | collective-permute-start | bytes 3145736 | tf_op jit(solution)/shard_map/ppermute | solution.py:367
  30.5 31.0 %collective-permute-start.7 = (bf16[4,128,1024]{2,1,0:T(8,128)(2,1)}, bf16[4,128,1024]{2,1,0:T(8,128)(2,1)}, u32[]{:S(2)}, u32[]{:S(2)}) collective-permute-start(bf16[4,128,1024]{2,1,0:T(8,128)(2,1)} %collective-permute-done.refs_2_), channel_id=1, source_target_pairs={{0,2},{1,3},{2,0},{3,1},{4,6},{5,7},{6,4},{7,5},{8,10},{9,11},{10,... | collective-permute-start | bytes 3145736 | tf_op jit(solution)/shard_map/ppermute | solution.py:367
  33.1 27.0 %collective-permute-start.5 = (bf16[4,128,1024]{2,1,0:T(8,128)(2,1)}, bf16[4,128,1024]{2,1,0:T(8,128)(2,1)}, u32[]{:S(2)}, u32[]{:S(2)}) collective-permute-start(bf16[4,128,1024]{2,1,0:T(8,128)(2,1)} %broadcast_select_fusion.1), channel_id=1, source_target_pairs={{4,0},{5,1},{6,2},{7,3},{8,12},{9,13},{10,14},{11,15},{0,8},{1,9},... | collective-permute-start | bytes 3145736 | tf_op jit(solution)/shard_map/ppermute | solution.py:367
  38.1 23.4 %collective-permute-start.4 = (bf16[4,128,1024]{2,1,0:T(8,128)(2,1)}, bf16[4,128,1024]{2,1,0:T(8,128)(2,1)}, u32[]{:S(2)}, u32[]{:S(2)}) collective-permute-start(bf16[4,128,1024]{2,1,0:T(8,128)(2,1)} %broadcast_select_fusion.2), channel_id=1, source_target_pairs={{4,8},{5,9},{6,10},{7,11},{8,4},{9,5},{10,6},{11,7},{0,1},{1,0},{2... | collective-permute-start | bytes 3145736 | tf_op jit(solution)/shard_map/ppermute | solution.py:367
  61.5 53.2 %copy-start.4 = (bf16[4,128,1024]{2,1,0:T(8,128)(2,1)}, bf16[4,128,1024]{2,1,0:T(8,128)(2,1)S(1)}, u32[]{:S(2)}) copy-start(bf16[4,128,1024]{2,1,0:T(8,128)(2,1)S(1)} %broadcast_select_fusion.refs_4_) | copy-start | bytes 3145732
  61.5 25.6 %collective-permute-start.11 = (bf16[4,128,1024]{2,1,0:T(8,128)(2,1)S(1)}, bf16[4,128,1024]{2,1,0:T(8,128)(2,1)S(1)}, u32[]{:S(2)}, u32[]{:S(2)}) collective-permute-start(bf16[4,128,1024]{2,1,0:T(8,128)(2,1)S(1)} %broadcast_select_fusion.refs_4_), channel_id=1, source_target_pairs={{0,1},{1,0},{2,3},{3,2},{4,5},{5,4},{6,7},{7,6},{8,9},{9,8},{10,11... | collective-permute-start | bytes 3145736 | tf_op jit(solution)/shard_map/ppermute | solution.py:367
  61.6 48.3 %collective-permute-start.9 = (bf16[4,128,1024]{2,1,0:T(8,128)(2,1)}, bf16[4,128,1024]{2,1,0:T(8,128)(2,1)S(1)}, u32[]{:S(2)}, u32[]{:S(2)}) collective-permute-start(bf16[4,128,1024]{2,1,0:T(8,128)(2,1)} %collective-permute-done.4), channel_id=1, source_target_pairs={{4,0},{5,1},{6,2},{7,3},{8,12},{9,13},{10,14},{11,15},{0,9},{1,8},... | collective-permute-start | bytes 3145736 | tf_op jit(solution)/shard_map/ppermute | solution.py:367
  86.0 26.5 %collective-permute-start.12 = (bf16[4,128,1024]{2,1,0:T(8,128)(2,1)}, bf16[4,128,1024]{2,1,0:T(8,128)(2,1)S(1)}, u32[]{:S(2)}, u32[]{:S(2)}) collective-permute-start(bf16[4,128,1024]{2,1,0:T(8,128)(2,1)} %collective-permute-done.6.refs_6_), channel_id=1, source_target_pairs={{0,1},{1,0},{2,3},{3,2},{4,5},{5,4},{6,7},{7,6},{8,9},{9,8},{10,11... | collective-permute-start | bytes 3145736 | tf_op jit(solution)/shard_map/ppermute | solution.py:367
  86.1 26.5 %collective-permute-start.13 = (bf16[4,128,1024]{2,1,0:T(8,128)(2,1)}, bf16[4,128,1024]{2,1,0:T(8,128)(2,1)S(1)}, u32[]{:S(2)}, u32[]{:S(2)}) collective-permute-start(bf16[4,128,1024]{2,1,0:T(8,128)(2,1)} %collective-permute-done.7.refs_8_), channel_id=1, source_target_pairs={{0,1},{1,0},{2,3},{3,2},{4,5},{5,4},{6,7},{7,6},{8,9},{9,8},{10,11... | collective-permute-start | bytes 3145736 | tf_op jit(solution)/shard_map/ppermute | solution.py:367
  86.6 26.0 %collective-permute-start.10 = (bf16[4,128,1024]{2,1,0:T(8,128)(2,1)S(1)}, bf16[4,128,1024]{2,1,0:T(8,128)(2,1)}, u32[]{:S(2)}, u32[]{:S(2)}) collective-permute-start(bf16[4,128,1024]{2,1,0:T(8,128)(2,1)S(1)} %broadcast_select_fusion.refs_4_), channel_id=1, source_target_pairs={{0,2},{1,3},{2,0},{3,1},{4,6},{5,7},{6,4},{7,5},{8,10},{9,11},{10,... | collective-permute-start | bytes 3145736 | tf_op jit(solution)/shard_map/ppermute | solution.py:367
  87.1 1.0 copy-start.5
  88.1 53.9 %collective-permute-start.16 = (bf16[32,128,128]{2,1,0:T(8,128)(2,1)}, bf16[32,128,128]{2,1,0:T(8,128)(2,1)}, u32[]{:S(2)}, u32[]{:S(2)}) collective-permute-start(bf16[32,128,128]{2,1,0:T(8,128)(2,1)} %copy-done.2), channel_id=1, source_target_pairs={{0,8},{1,9},{2,10},{3,11},{12,4},{13,5},{14,6},{15,7},{16,24},{17,... | collective-permute-start | bytes 3145736 | tf_op jit(solution)/shard_map/ppermute | solution.py:367
  109.9 3.3 %copy-start.3 = (bf16[4,128,1024]{2,1,0:T(8,128)(2,1)}, bf16[4,128,1024]{2,1,0:T(8,128)(2,1)S(1)}, u32[]{:S(2)}) copy-start(bf16[4,128,1024]{2,1,0:T(8,128)(2,1)S(1)} %collective-permute-done.9.refs_1_.refs_0_) | copy-start | bytes 3145732
  112.6 2.1 %copy-start.6 = (bf16[4,128,1024]{2,1,0:T(8,128)(2,1)}, bf16[4,128,1024]{2,1,0:T(8,128)(2,1)S(1)}, u32[]{:S(2)}) copy-start(bf16[4,128,1024]{2,1,0:T(8,128)(2,1)S(1)} %collective-permute-done.12.refs_7_) | copy-start | bytes 3145732
  112.6 2.1 %copy-start.7 = (bf16[4,128,1024]{2,1,0:T(8,128)(2,1)}, bf16[4,128,1024]{2,1,0:T(8,128)(2,1)S(1)}, u32[]{:S(2)}) copy-start(bf16[4,128,1024]{2,1,0:T(8,128)(2,1)S(1)} %collective-permute-done.13.refs_9_) | copy-start | bytes 3145732
  112.6 27.5 %collective-permute-start.14 = (bf16[2,128,1024]{2,1,0:T(8,128)(2,1)}, bf16[2,128,1024]{2,1,0:T(8,128)(2,1)}, u32[]{:S(2)}, u32[]{:S(2)}) collective-permute-start(bf16[2,128,1024]{2,1,0:T(8,128)(2,1)} %get-tuple-element.132.refs_1_), channel_id=1, source_target_pairs={{0,2},{1,3},{2,0},{3,1},{4,6},{5,7},{6,4},{7,5},{8,10},{9,11},{10,... | collective-permute-start | bytes 1572872 | tf_op jit(solution)/shard_map/ppermute | solution.py:367
  113.2 26.9 %collective-permute-start.15 = (bf16[2,128,1024]{2,1,0:T(8,128)(2,1)}, bf16[2,128,1024]{2,1,0:T(8,128)(2,1)}, u32[]{:S(2)}, u32[]{:S(2)}) collective-permute-start(bf16[2,128,1024]{2,1,0:T(8,128)(2,1)} %get-tuple-element.133.refs_2_), channel_id=1, source_target_pairs={{0,2},{1,3},{2,0},{3,1},{4,6},{5,7},{6,4},{7,5},{8,10},{9,11},{10,... | collective-permute-start | bytes 1572872 | tf_op jit(solution)/shard_map/ppermute | solution.py:367
  114.7 52.8 %collective-permute-start.19 = (bf16[48,128,128]{2,1,0:T(8,128)(2,1)S(1)}, bf16[48,128,128]{2,1,0:T(8,128)(2,1)}, u32[]{:S(2)}, u32[]{:S(2)}) collective-permute-start(bf16[48,128,128]{2,1,0:T(8,128)(2,1)S(1)} %get-tuple-element.130), channel_id=1, source_target_pairs={{4,12},{5,13},{6,14},{7,15},{8,0},{9,1},{10,2},{11,3},{20,28},{21,... | collective-permute-start | bytes 4718600 | tf_op jit(solution)/shard_map/ppermute | solution.py:367
  140.1 2.2 %collective-permute-start.21 = (bf16[2,128,1024]{2,1,0:T(8,128)(2,1)}, bf16[2,128,1024]{2,1,0:T(8,128)(2,1)S(1)}, u32[]{:S(2)}, u32[]{:S(2)}) collective-permute-start(bf16[2,128,1024]{2,1,0:T(8,128)(2,1)} %get-tuple-element.132.refs_1_), channel_id=1, source_target_pairs={{0,1},{1,0},{2,3},{3,2},{4,5},{5,4},{6,7},{7,6},{8,9},{9,8},{10,11... | collective-permute-start | bytes 1572872 | tf_op jit(solution)/shard_map/ppermute | solution.py:367
  140.2 52.6 %collective-permute-start.18 = (bf16[36,128,128]{2,1,0:T(8,128)(2,1)S(1)}, bf16[36,128,128]{2,1,0:T(8,128)(2,1)}, u32[]{:S(2)}, u32[]{:S(2)}) collective-permute-start(bf16[36,128,128]{2,1,0:T(8,128)(2,1)S(1)} %get-tuple-element.129), channel_id=1, source_target_pairs={{4,12},{5,13},{6,14},{7,15},{8,0},{9,1},{10,2},{11,3},{20,28},{21,... | collective-permute-start | bytes 3538952 | tf_op jit(solution)/shard_map/ppermute | solution.py:367
  141.5 2.3 %collective-permute-start.22 = (bf16[2,128,1024]{2,1,0:T(8,128)(2,1)}, bf16[2,128,1024]{2,1,0:T(8,128)(2,1)S(1)}, u32[]{:S(2)}, u32[]{:S(2)}) collective-permute-start(bf16[2,128,1024]{2,1,0:T(8,128)(2,1)} %get-tuple-element.133.refs_2_), channel_id=1, source_target_pairs={{0,1},{1,0},{2,3},{3,2},{4,5},{5,4},{6,7},{7,6},{8,9},{9,8},{10,11... | collective-permute-start | bytes 1572872 | tf_op jit(solution)/shard_map/ppermute | solution.py:367
  142.0 6.0 %collective-permute-start.20 = (bf16[4,128,1024]{2,1,0:T(8,128)(2,1)}, bf16[4,128,1024]{2,1,0:T(8,128)(2,1)}, u32[]{:S(2)}, u32[]{:S(2)}) collective-permute-start(bf16[4,128,1024]{2,1,0:T(8,128)(2,1)} %collective-permute-done.10.refs_10_), channel_id=1, source_target_pairs={{0,1},{1,0},{2,3},{3,2},{4,5},{5,4},{6,7},{7,6},{8,9},{9,8},{10,11... | collective-permute-start | bytes 3145736 | tf_op jit(solution)/shard_map/ppermute | solution.py:367
  142.3 1.9 copy-start.8
  142.3 3.0 %collective-permute-start.23 = (bf16[2,128,1024]{2,1,0:T(8,128)(2,1)}, bf16[2,128,1024]{2,1,0:T(8,128)(2,1)S(1)}, u32[]{:S(2)}, u32[]{:S(2)}) collective-permute-start(bf16[2,128,1024]{2,1,0:T(8,128)(2,1)} %collective-permute-done.14.refs_5_), channel_id=1, source_target_pairs={{0,1},{1,0},{2,3},{3,2},{4,5},{5,4},{6,7},{7,6},{8,9},{9,8},{10,11... | collective-permute-start | bytes 1572872 | tf_op jit(solution)/shard_map/ppermute | solution.py:367
  143.8 1.5 copy-start.9
  143.8 4.3 %collective-permute-start.24 = (bf16[2,128,1024]{2,1,0:T(8,128)(2,1)}, bf16[2,128,1024]{2,1,0:T(8,128)(2,1)}, u32[]{:S(2)}, u32[]{:S(2)}) collective-permute-start(bf16[2,128,1024]{2,1,0:T(8,128)(2,1)} %collective-permute-done.15.refs_6_), channel_id=1, source_target_pairs={{0,1},{1,0},{2,3},{3,2},{4,5},{5,4},{6,7},{7,6},{8,9},{9,8},{10,11... | collective-permute-start | bytes 1572872 | tf_op jit(solution)/shard_map/ppermute | solution.py:367
  145.3 0.8 copy-start.10
  146.1 57.5 %collective-permute-start.17 = (bf16[12,128,128]{2,1,0:T(8,128)(2,1)S(1)}, bf16[12,128,128]{2,1,0:T(8,128)(2,1)S(1)}, u32[]{:S(2)}, u32[]{:S(2)}) collective-permute-start(bf16[12,128,128]{2,1,0:T(8,128)(2,1)S(1)} %get-tuple-element.128), channel_id=1, source_target_pairs={{4,12},{5,13},{6,14},{7,15},{8,0},{9,1},{10,2},{11,3},{20,28},{21,... | collective-permute-start | bytes 1179656 | tf_op jit(solution)/shard_map/ppermute | solution.py:367
  203.5 0.7 copy-start.11

commit v10 on v9

--- a/solution.py
+++ b/solution.py
@@ -10,7 +10,7 @@
 W = 32
 PPD = 16
 REUSE = 3
-SHARES = (24, 18)
+SHARES = (30, 12)
 COLUMNS = 256
 MIB = 1024 * 1024
 SMEM = pl.BlockSpec(memory_space=pltpu.SMEM)
@@ -354,7 +354,7 @@
             pltpu.SemaphoreType.DMA((PPD,)),
             pltpu.SemaphoreType.DMA((PPD,)),
         ],
-        compiler_params=pltpu.CompilerParams(vmem_limit_bytes=56 * MIB),
+        compiler_params=pltpu.CompilerParams(vmem_limit_bytes=40 * MIB),
         name="far_part",
     )(starts, block_at, chosen, *[array for _, array in used], total, flipped, *given)
 
@@ -407,9 +407,10 @@
     sizes = tile_parts(count)
     shapes = [shard.shape] * 2 + [(size,) + tiles.shape[1:] for size in [count - 2 * step] + sizes]
     parts = sort_tiles(order, at_end, tiles, [1, 1, 1, 0, 0, 0], shapes)
-    near, first, c_own, notes, *parts = together(near, first, c_own, notes, *parts)
+    first, *parts = together(first, *parts)
 
     outer = send(jnp.where(in_centre, first, parts[0]), around)
+    near, c_own, notes, *parts = together(near, c_own, notes, *parts)
     second = send(jnp.where(in_centre, near, parts[1]), across + [(i, i ^ 1) for i, _ in from_ends])
     y_own = send(shard, other_y)
     y_near = send(near, other_y)

time: 210 us -> 206 us (0.981)
  Pallas kernels: 82.8 us -> 77.7 us
  local copies, waits for them, and re-layouts: 7.9 us -> 10.8 us
    pallas_call x3, Pallas kernels: 29.2 us -> 23.2 us  [far_part(): pl.pallas_call(functools.partial(far_kernel, base, [segment for segment,...]
    unnamed x28 -> x32, local copies, waits for them, and re-layouts: 6.11 us -> 9.03 us
  transfers between devices with their start and end apart: 25 -> 25, of which waited for: 9 -> 10; matrix products, arithmetic and copies ran while one was open for 5% -> 5% of each run, Pallas kernels for 37% -> 35%
where the time goes in v10:
time: 206 us
  Pallas kernels  77.7 us (38%)
  waiting for transfers between devices  56.3 us (27%)
  starting transfers between devices  52.8 us (26%)
  local copies, waits for them, and re-layouts  10.8 us (5%)
  other arithmetic  8.05 us (4%)
    ppermute x25, waiting for transfers between devices, send(): return lax.ppermute(value, 'tile', pairs)  56.3 us
    ppermute x25, starting transfers between devices, send(): return lax.ppermute(value, 'tile', pairs)  52.8 us
    pallas_call x2, Pallas kernels, own_part(): pl.pallas_call(functools.partial(own_kernel, counts, group, not earlier),...  38.1 us
    pallas_call x3, Pallas kernels, far_part(): pl.pallas_call(functools.partial(far_kernel, base, [segment for segment,...  23.2 us
    pallas_call x3, Pallas kernels, tables(): pl.pallas_call(tables_kernel, in_specs=[SMEM] * 2, out_specs=[SMEM] * 4,...  12.1 us
    unnamed x32, local copies, waits for them, and re-layouts  9.03 us
    pallas_call x1, Pallas kernels, sort_tiles(): pl.pallas_call(functools.partial(sort_kernel, choices), in_specs=[SMEM] *...  4.37 us
  transfers between devices with their start and end apart: 25, of which 10 were waited for; matrix products, arithmetic and copies ran while one was open for 5% of the time, Pallas kernels for 35%

profile of v10, /device:TPU:0, one launch (start us, length us, event | category | flops | bytes accessed | tf_op | source)
XLA Modules:
  0.0 206.0 jit_solution(3162101929463973939)
XLA Ops:
  0.0 1.6 collective-permute-start.3
  1.6 0.5 collective-permute-start.1
  2.1 4.6 %collective-permute-start = (bf16[4,128,1024]{2,1,0:T(8,128)(2,1)}, bf16[4,128,1024]{2,1,0:T(8,128)(2,1)}, u32[]{:S(2)}, u32[]{:S(2)}) collective-permute-start(bf16[4,128,1024]{2,1,0:T(8,128)(2,1)} %refs_0_.1), channel_id=1, source_target_pairs={{0,4},{1,5},{2,6},{3,7},{4,0},{5,1},{6,2},{7,3},{8,12},{9,13},{10,... | collective-permute-start | bytes 3145736 | tf_op jit(solution)/shard_map/ppermute | solution.py:367
  6.7 1.5 collective-permute-start.6
  8.2 0.7 pad_add_fusion
  8.9 0.6 collective-permute-start.2
  9.5 4.0 %tables.3 = (s32[17]{0:T(128)}, s32[96]{0:T(128)}, s32[96]{0:T(128)}, s32[64]{0:T(128)}) custom-call(s32[96]{0:T(128)} %rows.1, s32[96]{0:T(128)} %cols.3), custom_call_target="tpu_custom_call" | custom-call | tf_op jit(solution)/shard_map/tables/pallas_call | solution.py:68
  13.5 0.0 copy-start.1
  13.5 1.9 copy-done.1
  15.4 0.6 copy-done.4
  16.0 4.4 %sort_tiles.1 = (bf16[4,128,1024]{2,1,0:T(8,128)(2,1)S(1)}, bf16[4,128,1024]{2,1,0:T(8,128)(2,1)S(1)}, bf16[32,128,128]{2,1,0:T(8,128)(2,1)S(1)}, bf16[60,128,12...) custom-call(s32[96]{0:T(128)S(1)} %copy-done.4, s32[1]{0:T(128)} %bitcast.2.chosen, ...), custom_call_target="tpu_custom_call" | custom-call | tf_op jit(solution)/shard_map/sort_tiles/pallas_call | solution.py:108
  20.4 1.0 copy-done.6
  21.4 8.6 %collective-permute-done.2 = s32[2,96]{1,0:T(2,128)S(1)} collective-permute-done((s32[2,96]{1,0:T(2,128)S(1)}, s32[2,96]{1,0:T(2,128)S(1)}, u32[]{:S(2)}, u32[]{:S(2)}) %collective-permute-start.2) | collective-permute-done | bytes 800 | tf_op jit(solution)/shard_map/ppermute | solution.py:367
  30.0 0.0 collective-permute-done.1.refs_1_
  30.0 0.7 collective-permute-done.refs_2_
  30.7 0.0 collective-permute-start.8
  30.7 1.5 collective-permute-start.7
  32.3 1.1 broadcast_select_fusion.1
  33.4 3.8 %collective-permute-start.5 = (bf16[4,128,1024]{2,1,0:T(8,128)(2,1)}, bf16[4,128,1024]{2,1,0:T(8,128)(2,1)S(1)}, u32[]{:S(2)}, u32[]{:S(2)}) collective-permute-start(bf16[4,128,1024]{2,1,0:T(8,128)(2,1)} %broadcast_select_fusion.1), channel_id=1, source_target_pairs={{4,0},{5,1},{6,2},{7,3},{8,12},{9,13},{10,14},{11,15},{0,8},{1,9},... | collective-permute-start | bytes 3145736 | tf_op jit(solution)/shard_map/ppermute | solution.py:367
  37.2 1.1 broadcast_select_fusion.2
  38.3 0.5 fusion.10.rows
  38.9 4.0 %tables.4 = (s32[33]{0:T(128)}, s32[96]{0:T(128)}, s32[96]{0:T(128)}, s32[64]{0:T(128)}) custom-call(s32[96]{0:T(128)} %fusion.10.rows, s32[96]{0:T(128)} %cols.3), custom_call_target="tpu_custom_call" | custom-call | tf_op jit(solution)/shard_map/tables/pallas_call | solution.py:68
  42.9 2.2 %fusion.perm_ref = bf16[1024,1024]{1,0:T(8,128)(2,1)} fusion(s32[1024]{0:T(1024)S(1)} %fusion.7), kind=kLoop, calls=%fused_computation.1 | loop fusion | flops 2097152 | bytes 2101248 | tf_op jit(solution)/shard_map/convert_element_type | solution.py:24
  45.1 0.5 slice_bitcast_fusion
  45.7 4.0 %tables.5 = (s32[17]{0:T(128)}, s32[96]{0:T(128)}, s32[96]{0:T(128)}, s32[64]{0:T(128)}) custom-call(s32[96]{0:T(128)} %get-tuple-element.158.rows, s32[96]{0:T(128)} %get-tuple-element.157.cols), custom_call_target="tpu_custom_call" | custom-call | tf_op jit(solution)/shard_map/tables/pallas_call | solution.py:68
  49.7 10.6 %collective-permute-done.5.refs_0_ = bf16[4,128,1024]{2,1,0:T(8,128)(2,1)S(1)} collective-permute-done((bf16[4,128,1024]{2,1,0:T(8,128)(2,1)}, bf16[4,128,1024]{2,1,0:T(8,128)(2,1)S(1)}, u32[]{:S(2)}, u32[]{:S(2)}) %collective-permute-start.5) | collective-permute-done | bytes 1048608 | tf_op jit(solution)/shard_map/ppermute | solution.py:367
  60.3 0.1 broadcast_select_fusion.refs_4_
  60.4 0.0 collective-permute-done.6.refs_6_
  60.5 0.0 collective-permute-done.8.refs_3_
  60.5 0.1 collective-permute-start.11
  60.6 25.7 %collective-permute-start.9 = (bf16[4,128,1024]{2,1,0:T(8,128)(2,1)}, bf16[4,128,1024]{2,1,0:T(8,128)(2,1)S(1)}, u32[]{:S(2)}, u32[]{:S(2)}) collective-permute-start(bf16[4,128,1024]{2,1,0:T(8,128)(2,1)} %collective-permute-done.4), channel_id=1, source_target_pairs={{4,0},{5,1},{6,2},{7,3},{8,12},{9,13},{10,14},{11,15},{0,9},{1,8},... | collective-permute-start | bytes 3145736 | tf_op jit(solution)/shard_map/ppermute | solution.py:367
  86.2 0.1 collective-permute-start.12
  86.3 0.4 collective-permute-start.13
  86.8 0.5 collective-permute-start.10
  87.3 1.3 collective-permute-start.19
  88.6 21.0 %collective-permute-done.9.refs_1_.refs_0_ = bf16[4,128,1024]{2,1,0:T(8,128)(2,1)S(1)} collective-permute-done((bf16[4,128,1024]{2,1,0:T(8,128)(2,1)}, bf16[4,128,1024]{2,1,0:T(8,128)(2,1)S(1)}, u32[]{:S(2)}, u32[]{:S(2)}) %collective-permute-start.9) | collective-permute-done | bytes 1048608 | tf_op jit(solution)/shard_map/ppermute | solution.py:367
  109.5 4.7 %collective-permute-start.16 = (bf16[32,128,128]{2,1,0:T(8,128)(2,1)}, bf16[32,128,128]{2,1,0:T(8,128)(2,1)S(1)}, u32[]{:S(2)}, u32[]{:S(2)}) collective-permute-start(bf16[32,128,128]{2,1,0:T(8,128)(2,1)} %copy-done.6), channel_id=1, source_target_pairs={{0,8},{1,9},{2,10},{3,11},{12,4},{13,5},{14,6},{15,7},{16,24},{17,... | collective-permute-start | bytes 3145736 | tf_op jit(solution)/shard_map/ppermute | solution.py:367
  114.3 2.3 %slice_select_fusion = (bf16[2,128,1024]{2,1,0:T(8,128)(2,1)}, bf16[2,128,1024]{2,1,0:T(8,128)(2,1)}) fusion(bf16[4,128,1024]{2,1,0:T(8,128)(2,1)S(1)} %collective-permute-done.9.refs_1_.refs_0_, bf16[4,128,1024]{2,1,0:T(8,128)(2,1)} %collective-permute-done.4, pred[]{:T(512)S(6)} %or.6), kind=kLoop, calls=%fused_computation.5 | loop fusion | flops 524288 | bytes 3145729 | tf_op jit(solution)/shard_map/jit(_where)/select_n | solution.py:436
  116.6 0.9 copy-done.9
  117.6 0.3 copy-done.10
  117.9 0.5 collective-permute-start.14
  118.4 1.5 collective-permute-start.15
  119.9 0.6 stack.89.firsts
  120.5 23.5 %own_part.2 = (f32[16,128,1024]{2,1,0:T(8,128)}, bf16[32,128,1024]{2,1,0:T(8,128)(2,1)}) custom-call(s32[33]{0:T(128)} %get-tuple-element.119.starts, s32[96]{0:T(128)} %get-tuple-element.120.tile_at, s32[96]{0:T(128)} %get-tuple-element.121.block_at, s32[64]{0:T(128)} %get-tuple-element.122.own_slots, s32[64]{0:T(128)} %get-tuple-element.123.far_slots, ...), custom_call_target="tpu_custom_call" | custom-call | tf_op jit(solution)/shard_map/own_part/pallas_call | solution.py:221
  144.0 0.1 collective-permute-start.21
  144.1 0.5 collective-permute-start.22
  144.6 0.1 collective-permute-start.20
  144.7 0.4 collective-permute-start.23
  145.1 1.1 collective-permute-done.21.refs_3_
  146.2 1.3 collective-permute-start.18
  147.5 0.2 collective-permute-done.22.refs_4_
  147.7 0.1 collective-permute-start.24
  147.9 1.4 collective-permute-done.23.refs_7_
  149.2 0.8 copy-done.13
  150.1 1.3 collective-permute-start.17
  151.4 0.6 stack.99.firsts
  152.0 14.6 %own_part.3 = (f32[16,128,1024]{2,1,0:T(8,128)}, bf16[32,128,1024]{2,1,0:T(8,128)(2,1)}) custom-call(s32[33]{0:T(128)} %get-tuple-element.119.starts, s32[96]{0:T(128)} %get-tuple-element.120.tile_at, s32[96]{0:T(128)} %get-tuple-element.121.block_at, s32[64]{0:T(128)} %get-tuple-element.122.own_slots, ...), custom_call_target="tpu_custom_call", output_to_operand_aliasing={{0}: (17, {}), {1}: (18, {})} | custom-call | tf_op jit(solution)/shard_map/own_part/pallas_call | solution.py:221
  166.6 9.6 %collective-permute-done.19.refs_2_ = bf16[60,128,128]{2,1,0:T(8,128)(2,1)} collective-permute-done((bf16[60,128,128]{2,1,0:T(8,128)(2,1)}, bf16[60,128,128]{2,1,0:T(8,128)(2,1)}, u32[]{:S(2)}, u32[]{:S(2)}) %collective-permute-start.19) | collective-permute-done | bytes 1966112 | tf_op jit(solution)/shard_map/ppermute | solution.py:367
  176.2 3.4 %copy-done = f32[16,128,1024]{2,1,0:T(8,128)S(1)} copy-done((f32[16,128,1024]{2,1,0:T(8,128)S(1)}, f32[16,128,1024]{2,1,0:T(8,128)}, u32[]{:S(2)}) %copy-start) | copy-done | bytes 8388632
  179.6 12.2 %far_part.3 = (f32[16,128,1024]{2,1,0:T(8,128)S(1)}, bf16[16,128,1024]{2,1,0:T(8,128)(2,1)}) custom-call(s32[17]{0:T(128)S(1)} %copy-done.2, s32[96]{0:T(128)S(1)} %copy-done.3, s32[1]{0:T(128)} %bitcast.2.chosen, bf16[4,128,1024]{2,1,0:T(8,128)(2,1)S(1)} %collective-permute-done.5.refs_0_, ...), custom_call_target="tpu_custom_call", output_to_operand_aliasing={{0}: (6, {})} | custom-call | tf_op jit(solution)/shard_map/far_part/pallas_call | solution.py:341
  191.8 1.3 collective-permute-done.18.refs_2_
  193.1 6.3 %far_part.4 = (f32[16,128,1024]{2,1,0:T(8,128)S(1)}, bf16[16,128,1024]{2,1,0:T(8,128)(2,1)}) custom-call(s32[17]{0:T(128)S(1)} %copy-done.2, s32[96]{0:T(128)S(1)} %copy-done.3, s32[1]{0:T(128)} %bitcast.2.chosen, bf16[4,128,1024]{2,1,0:T(8,128)(2,1)S(1)} %collective-permute-done.9.refs_1_.refs_0_, ...), custom_call_target="tpu_custom_call", output_to_operand_aliasing={{0}: (6, {}), {1}: (8, {})} | custom-call | tf_op jit(solution)/shard_map/far_part/pallas_call | solution.py:341
  199.4 1.9 collective-permute-done.17.refs_1_
  201.3 4.7 %far_part.5 = (f32[16,128,1024]{2,1,0:T(8,128)S(1)}, bf16[16,128,1024]{2,1,0:T(8,128)(2,1)}) custom-call(s32[17]{0:T(128)S(1)} %copy-done.2, s32[96]{0:T(128)S(1)} %copy-done.3, s32[1]{0:T(128)} %bitcast.2.chosen, bf16[32,128,128]{2,1,0:T(8,128)(2,1)S(1)} %collective-permute-done.16.refs_1_.refs_0_, ...), custom_call_target="tpu_custom_call", output_to_operand_aliasing={{0}: (5, {}), {1}: (7, {})} | custom-call | tf_op jit(solution)/shard_map/far_part/pallas_call | solution.py:341
  (38 shorter events, 0.1 us)
Async XLA Ops:
  0.0 21.4 %collective-permute-start.3 = (bf16[4,128,1024]{2,1,0:T(8,128)(2,1)}, bf16[4,128,1024]{2,1,0:T(8,128)(2,1)}, u32[]{:S(2)}, u32[]{:S(2)}) collective-permute-start(bf16[4,128,1024]{2,1,0:T(8,128)(2,1)} %refs_0_.1), channel_id=1, source_target_pairs={{4,8},{5,9},{6,10},{7,11},{8,4},{9,5},{10,6},{11,7},{20,24},{21,25... | collective-permute-start | bytes 3145736 | tf_op jit(solution)/shard_map/ppermute | solution.py:367
  1.6 28.4 %collective-permute-start.1 = (bf16[4,128,1024]{2,1,0:T(8,128)(2,1)}, bf16[4,128,1024]{2,1,0:T(8,128)(2,1)}, u32[]{:S(2)}, u32[]{:S(2)}) collective-permute-start(bf16[4,128,1024]{2,1,0:T(8,128)(2,1)} %refs_0_.1), channel_id=1, source_target_pairs={{0,1},{1,0},{2,3},{3,2},{4,5},{5,4},{6,7},{7,6},{8,9},{9,8},{10,11... | collective-permute-start | bytes 3145736 | tf_op jit(solution)/shard_map/ppermute | solution.py:367
  2.1 28.6 %collective-permute-start = (bf16[4,128,1024]{2,1,0:T(8,128)(2,1)}, bf16[4,128,1024]{2,1,0:T(8,128)(2,1)}, u32[]{:S(2)}, u32[]{:S(2)}) collective-permute-start(bf16[4,128,1024]{2,1,0:T(8,128)(2,1)} %refs_0_.1), channel_id=1, source_target_pairs={{0,4},{1,5},{2,6},{3,7},{4,0},{5,1},{6,2},{7,3},{8,12},{9,13},{10,... | collective-permute-start | bytes 3145736 | tf_op jit(solution)/shard_map/ppermute | solution.py:367
  6.7 53.8 %collective-permute-start.6 = (bf16[4,128,1024]{2,1,0:T(8,128)(2,1)}, bf16[4,128,1024]{2,1,0:T(8,128)(2,1)}, u32[]{:S(2)}, u32[]{:S(2)}) collective-permute-start(bf16[4,128,1024]{2,1,0:T(8,128)(2,1)} %refs_0_.1), channel_id=1, source_target_pairs={{0,2},{1,3},{2,0},{3,1},{4,6},{5,7},{6,4},{7,5},{8,10},{9,11},{10,... | collective-permute-start | bytes 3145736 | tf_op jit(solution)/shard_map/ppermute | solution.py:367
  8.9 21.2 %collective-permute-start.2 = (s32[2,96]{1,0:T(2,128)S(1)}, s32[2,96]{1,0:T(2,128)S(1)}, u32[]{:S(2)}, u32[]{:S(2)}) collective-permute-start(s32[2,96]{1,0:T(2,128)S(1)} %pad_add_fusion), channel_id=1, source_target_pairs={{0,8},{1,9},{2,10},{3,11},{4,12},{5,13},{6,14},{7,15},{8,0},{9,1},... | collective-permute-start | bytes 2312 | tf_op jit(solution)/shard_map/ppermute | solution.py:367
  13.5 1.9 copy-start.1
  15.4 0.6 copy-start.4
  16.0 22.4 %copy-start.14 = (s32[96]{0:T(128)S(1)}, s32[96]{0:T(128)}, u32[]{:S(2)}) copy-start(s32[96]{0:T(128)} %rows.1) | copy-start | bytes 1156
  16.0 22.4 %copy-start.15 = (s32[96]{0:T(128)S(1)}, s32[96]{0:T(128)}, u32[]{:S(2)}) copy-start(s32[96]{0:T(128)} %cols.3) | copy-start | bytes 1156
  20.4 1.0 copy-start.6
  21.4 16.9 %copy-start.5 = (bf16[60,128,128]{2,1,0:T(8,128)(2,1)}, bf16[60,128,128]{2,1,0:T(8,128)(2,1)S(1)}, u32[]{:S(2)}) copy-start(bf16[60,128,128]{2,1,0:T(8,128)(2,1)S(1)} %get-tuple-element.140) | copy-start | bytes 5898244
  30.7 29.7 %collective-permute-start.8 = (bf16[4,128,1024]{2,1,0:T(8,128)(2,1)}, bf16[4,128,1024]{2,1,0:T(8,128)(2,1)}, u32[]{:S(2)}, u32[]{:S(2)}) collective-permute-start(bf16[4,128,1024]{2,1,0:T(8,128)(2,1)} %collective-permute-done.refs_2_), channel_id=1, source_target_pairs={{0,1},{1,0},{2,3},{3,2},{4,5},{5,4},{6,7},{7,6},{8,9},{9,8},{10,11... | collective-permute-start | bytes 3145736 | tf_op jit(solution)/shard_map/ppermute | solution.py:367
  30.7 29.7 %collective-permute-start.7 = (bf16[4,128,1024]{2,1,0:T(8,128)(2,1)}, bf16[4,128,1024]{2,1,0:T(8,128)(2,1)}, u32[]{:S(2)}, u32[]{:S(2)}) collective-permute-start(bf16[4,128,1024]{2,1,0:T(8,128)(2,1)} %collective-permute-done.refs_2_), channel_id=1, source_target_pairs={{0,2},{1,3},{2,0},{3,1},{4,6},{5,7},{6,4},{7,5},{8,10},{9,11},{10,... | collective-permute-start | bytes 3145736 | tf_op jit(solution)/shard_map/ppermute | solution.py:367
  33.4 26.9 %collective-permute-start.5 = (bf16[4,128,1024]{2,1,0:T(8,128)(2,1)}, bf16[4,128,1024]{2,1,0:T(8,128)(2,1)S(1)}, u32[]{:S(2)}, u32[]{:S(2)}) collective-permute-start(bf16[4,128,1024]{2,1,0:T(8,128)(2,1)} %broadcast_select_fusion.1), channel_id=1, source_target_pairs={{4,0},{5,1},{6,2},{7,3},{8,12},{9,13},{10,14},{11,15},{0,8},{1,9},... | collective-permute-start | bytes 3145736 | tf_op jit(solution)/shard_map/ppermute | solution.py:367
  38.3 22.1 %collective-permute-start.4 = (bf16[4,128,1024]{2,1,0:T(8,128)(2,1)}, bf16[4,128,1024]{2,1,0:T(8,128)(2,1)}, u32[]{:S(2)}, u32[]{:S(2)}) collective-permute-start(bf16[4,128,1024]{2,1,0:T(8,128)(2,1)} %broadcast_select_fusion.2), channel_id=1, source_target_pairs={{4,8},{5,9},{6,10},{7,11},{8,4},{9,5},{10,6},{11,7},{0,1},{1,0},{2... | collective-permute-start | bytes 3145736 | tf_op jit(solution)/shard_map/ppermute | solution.py:367
  60.4 49.1 %copy-start.7 = (bf16[4,128,1024]{2,1,0:T(8,128)(2,1)}, bf16[4,128,1024]{2,1,0:T(8,128)(2,1)S(1)}, u32[]{:S(2)}) copy-start(bf16[4,128,1024]{2,1,0:T(8,128)(2,1)S(1)} %broadcast_select_fusion.refs_4_) | copy-start | bytes 3145732
  60.5 26.8 %collective-permute-start.11 = (bf16[4,128,1024]{2,1,0:T(8,128)(2,1)S(1)}, bf16[4,128,1024]{2,1,0:T(8,128)(2,1)S(1)}, u32[]{:S(2)}, u32[]{:S(2)}) collective-permute-start(bf16[4,128,1024]{2,1,0:T(8,128)(2,1)S(1)} %broadcast_select_fusion.refs_4_), channel_id=1, source_target_pairs={{0,1},{1,0},{2,3},{3,2},{4,5},{5,4},{6,7},{7,6},{8,9},{9,8},{10,11... | collective-permute-start | bytes 3145736 | tf_op jit(solution)/shard_map/ppermute | solution.py:367
  60.6 49.0 %collective-permute-start.9 = (bf16[4,128,1024]{2,1,0:T(8,128)(2,1)}, bf16[4,128,1024]{2,1,0:T(8,128)(2,1)S(1)}, u32[]{:S(2)}, u32[]{:S(2)}) collective-permute-start(bf16[4,128,1024]{2,1,0:T(8,128)(2,1)} %collective-permute-done.4), channel_id=1, source_target_pairs={{4,0},{5,1},{6,2},{7,3},{8,12},{9,13},{10,14},{11,15},{0,9},{1,8},... | collective-permute-start | bytes 3145736 | tf_op jit(solution)/shard_map/ppermute | solution.py:367
  86.2 30.4 %collective-permute-start.12 = (bf16[4,128,1024]{2,1,0:T(8,128)(2,1)}, bf16[4,128,1024]{2,1,0:T(8,128)(2,1)S(1)}, u32[]{:S(2)}, u32[]{:S(2)}) collective-permute-start(bf16[4,128,1024]{2,1,0:T(8,128)(2,1)} %collective-permute-done.6.refs_6_), channel_id=1, source_target_pairs={{0,1},{1,0},{2,3},{3,2},{4,5},{5,4},{6,7},{7,6},{8,9},{9,8},{10,11... | collective-permute-start | bytes 3145736 | tf_op jit(solution)/shard_map/ppermute | solution.py:367
  86.3 30.3 %collective-permute-start.13 = (bf16[4,128,1024]{2,1,0:T(8,128)(2,1)}, bf16[4,128,1024]{2,1,0:T(8,128)(2,1)S(1)}, u32[]{:S(2)}, u32[]{:S(2)}) collective-permute-start(bf16[4,128,1024]{2,1,0:T(8,128)(2,1)} %collective-permute-done.7.refs_8_), channel_id=1, source_target_pairs={{0,1},{1,0},{2,3},{3,2},{4,5},{5,4},{6,7},{7,6},{8,9},{9,8},{10,11... | collective-permute-start | bytes 3145736 | tf_op jit(solution)/shard_map/ppermute | solution.py:367
  86.8 29.9 %collective-permute-start.10 = (bf16[4,128,1024]{2,1,0:T(8,128)(2,1)S(1)}, bf16[4,128,1024]{2,1,0:T(8,128)(2,1)}, u32[]{:S(2)}, u32[]{:S(2)}) collective-permute-start(bf16[4,128,1024]{2,1,0:T(8,128)(2,1)S(1)} %broadcast_select_fusion.refs_4_), channel_id=1, source_target_pairs={{0,2},{1,3},{2,0},{3,1},{4,6},{5,7},{6,4},{7,5},{8,10},{9,11},{10,... | collective-permute-start | bytes 3145736 | tf_op jit(solution)/shard_map/ppermute | solution.py:367
  87.3 1.3 copy-start.8
  87.3 88.9 %collective-permute-start.19 = (bf16[60,128,128]{2,1,0:T(8,128)(2,1)}, bf16[60,128,128]{2,1,0:T(8,128)(2,1)}, u32[]{:S(2)}, u32[]{:S(2)}) collective-permute-start(bf16[60,128,128]{2,1,0:T(8,128)(2,1)} %copy-done.5), channel_id=1, source_target_pairs={{4,12},{5,13},{6,14},{7,15},{8,0},{9,1},{10,2},{11,3},{20,28},{21,... | collective-permute-start | bytes 5898248 | tf_op jit(solution)/shard_map/ppermute | solution.py:367
  109.5 35.2 %collective-permute-start.16 = (bf16[32,128,128]{2,1,0:T(8,128)(2,1)}, bf16[32,128,128]{2,1,0:T(8,128)(2,1)S(1)}, u32[]{:S(2)}, u32[]{:S(2)}) collective-permute-start(bf16[32,128,128]{2,1,0:T(8,128)(2,1)} %copy-done.6), channel_id=1, source_target_pairs={{0,8},{1,9},{2,10},{3,11},{12,4},{13,5},{14,6},{15,7},{16,24},{17,... | collective-permute-start | bytes 3145736 | tf_op jit(solution)/shard_map/ppermute | solution.py:367
  116.6 1.0 copy-start.9
  116.6 1.3 copy-start.10
  117.9 26.1 %collective-permute-start.14 = (bf16[2,128,1024]{2,1,0:T(8,128)(2,1)}, bf16[2,128,1024]{2,1,0:T(8,128)(2,1)}, u32[]{:S(2)}, u32[]{:S(2)}) collective-permute-start(bf16[2,128,1024]{2,1,0:T(8,128)(2,1)} %get-tuple-element.142.refs_1_), channel_id=1, source_target_pairs={{0,2},{1,3},{2,0},{3,1},{4,6},{5,7},{6,4},{7,5},{8,10},{9,11},{10,... | collective-permute-start | bytes 1572872 | tf_op jit(solution)/shard_map/ppermute | solution.py:367
  118.4 25.6 %collective-permute-start.15 = (bf16[2,128,1024]{2,1,0:T(8,128)(2,1)}, bf16[2,128,1024]{2,1,0:T(8,128)(2,1)}, u32[]{:S(2)}, u32[]{:S(2)}) collective-permute-start(bf16[2,128,1024]{2,1,0:T(8,128)(2,1)} %get-tuple-element.143.refs_2_), channel_id=1, source_target_pairs={{0,2},{1,3},{2,0},{3,1},{4,6},{5,7},{6,4},{7,5},{8,10},{9,11},{10,... | collective-permute-start | bytes 1572872 | tf_op jit(solution)/shard_map/ppermute | solution.py:367
  144.0 2.2 %collective-permute-start.21 = (bf16[2,128,1024]{2,1,0:T(8,128)(2,1)}, bf16[2,128,1024]{2,1,0:T(8,128)(2,1)S(1)}, u32[]{:S(2)}, u32[]{:S(2)}) collective-permute-start(bf16[2,128,1024]{2,1,0:T(8,128)(2,1)} %get-tuple-element.142.refs_1_), channel_id=1, source_target_pairs={{0,1},{1,0},{2,3},{3,2},{4,5},{5,4},{6,7},{7,6},{8,9},{9,8},{10,11... | collective-permute-start | bytes 1572872 | tf_op jit(solution)/shard_map/ppermute | solution.py:367
  144.1 3.6 %collective-permute-start.22 = (bf16[2,128,1024]{2,1,0:T(8,128)(2,1)}, bf16[2,128,1024]{2,1,0:T(8,128)(2,1)S(1)}, u32[]{:S(2)}, u32[]{:S(2)}) collective-permute-start(bf16[2,128,1024]{2,1,0:T(8,128)(2,1)} %get-tuple-element.143.refs_2_), channel_id=1, source_target_pairs={{0,1},{1,0},{2,3},{3,2},{4,5},{5,4},{6,7},{7,6},{8,9},{9,8},{10,11... | collective-permute-start | bytes 1572872 | tf_op jit(solution)/shard_map/ppermute | solution.py:367
  144.6 7.4 %collective-permute-start.20 = (bf16[4,128,1024]{2,1,0:T(8,128)(2,1)}, bf16[4,128,1024]{2,1,0:T(8,128)(2,1)}, u32[]{:S(2)}, u32[]{:S(2)}) collective-permute-start(bf16[4,128,1024]{2,1,0:T(8,128)(2,1)} %collective-permute-done.10.refs_10_), channel_id=1, source_target_pairs={{0,1},{1,0},{2,3},{3,2},{4,5},{5,4},{6,7},{7,6},{8,9},{9,8},{10,11... | collective-permute-start | bytes 3145736 | tf_op jit(solution)/shard_map/ppermute | solution.py:367
  144.7 4.5 %collective-permute-start.23 = (bf16[2,128,1024]{2,1,0:T(8,128)(2,1)}, bf16[2,128,1024]{2,1,0:T(8,128)(2,1)S(1)}, u32[]{:S(2)}, u32[]{:S(2)}) collective-permute-start(bf16[2,128,1024]{2,1,0:T(8,128)(2,1)} %collective-permute-done.14.refs_5_), channel_id=1, source_target_pairs={{0,1},{1,0},{2,3},{3,2},{4,5},{5,4},{6,7},{7,6},{8,9},{9,8},{10,11... | collective-permute-start | bytes 1572872 | tf_op jit(solution)/shard_map/ppermute | solution.py:367
  146.2 1.6 copy-start.11
  146.2 46.8 %collective-permute-start.18 = (bf16[24,128,128]{2,1,0:T(8,128)(2,1)}, bf16[24,128,128]{2,1,0:T(8,128)(2,1)}, u32[]{:S(2)}, u32[]{:S(2)}) collective-permute-start(bf16[24,128,128]{2,1,0:T(8,128)(2,1)} %get-tuple-element.139), channel_id=1, source_target_pairs={{4,12},{5,13},{6,14},{7,15},{8,0},{9,1},{10,2},{11,3},{20,28},{21,... | collective-permute-start | bytes 2359304 | tf_op jit(solution)/shard_map/ppermute | solution.py:367
  147.7 1.5 copy-start.12
  147.7 4.3 %collective-permute-start.24 = (bf16[2,128,1024]{2,1,0:T(8,128)(2,1)}, bf16[2,128,1024]{2,1,0:T(8,128)(2,1)}, u32[]{:S(2)}, u32[]{:S(2)}) collective-permute-start(bf16[2,128,1024]{2,1,0:T(8,128)(2,1)} %collective-permute-done.15.refs_6_), channel_id=1, source_target_pairs={{0,1},{1,0},{2,3},{3,2},{4,5},{5,4},{6,7},{7,6},{8,9},{9,8},{10,11... | collective-permute-start | bytes 1572872 | tf_op jit(solution)/shard_map/ppermute | solution.py:367
  149.2 0.8 copy-start.13
  150.1 51.2 %collective-permute-start.17 = (bf16[12,128,128]{2,1,0:T(8,128)(2,1)}, bf16[12,128,128]{2,1,0:T(8,128)(2,1)S(1)}, u32[]{:S(2)}, u32[]{:S(2)}) collective-permute-start(bf16[12,128,128]{2,1,0:T(8,128)(2,1)} %get-tuple-element.138), channel_id=1, source_target_pairs={{4,12},{5,13},{6,14},{7,15},{8,0},{9,1},{10,2},{11,3},{20,28},{21,... | collective-permute-start | bytes 1179656 | tf_op jit(solution)/shard_map/ppermute | solution.py:367
  152.0 24.2 %copy-start.2 = (s32[17]{0:T(128)S(1)}, s32[17]{0:T(128)}, u32[]{:S(2)}) copy-start(s32[17]{0:T(128)} %get-tuple-element.108.starts) | copy-start | bytes 208
  152.0 24.2 %copy-start.3 = (s32[96]{0:T(128)S(1)}, s32[96]{0:T(128)}, u32[]{:S(2)}) copy-start(s32[96]{0:T(128)} %get-tuple-element.109.block_at) | copy-start | bytes 1156
  176.2 3.4 %copy-start = (f32[16,128,1024]{2,1,0:T(8,128)S(1)}, f32[16,128,1024]{2,1,0:T(8,128)}, u32[]{:S(2)}) copy-start(f32[16,128,1024]{2,1,0:T(8,128)} %get-tuple-element.148.refs_3_) | copy-start | bytes 25165828

commit v11 on v10

--- a/solution.py
+++ b/solution.py
@@ -114,6 +114,29 @@
         compiler_params=pltpu.CompilerParams(vmem_limit_bytes=16 * MIB),
         name="sort_tiles",
     )(tile_at, chosen, tiles)
+
+
+def payload_kernel(at_end, tiles_ref, received, payload, sem):
+    del received
+
+    @pl.when(at_end[0] == 1)
+    def _():
+        copy = pltpu.make_async_copy(tiles_ref, payload, sem)
+        copy.start()
+        copy.wait()
+
+
+def payload_of(at_end, tiles, received):
+    return pl.pallas_call(
+        payload_kernel,
+        in_specs=[SMEM, VMEM, ANY],
+        out_specs=ANY,
+        out_shape=jax.ShapeDtypeStruct(received.shape, received.dtype),
+        input_output_aliases={2: 0},
+        scratch_shapes=[pltpu.SemaphoreType.DMA],
+        compiler_params=pltpu.CompilerParams(vmem_limit_bytes=4 * MIB),
+        name="payload",
+    )(at_end, tiles, received)
 
 
 def add_row(sum_ref, begin, end, depth, tile_of, block_of):
@@ -379,7 +402,6 @@
     from_ends = [(i, i ^ 8) for i in range(16) if i not in centre]
     from_centre = [(i, i ^ 8) for i in centre]
     around = [(i, i ^ 4) for i in centre] + from_ends
-    around_crossed = [(i, i ^ 4) for i in centre] + [(i, i ^ 9) for i, _ in from_ends]
     other_z, other_y, other_core, opposite = (flipped_bit(bit) for bit in (4, 2, 1, 8))
     me = lax.axis_index("tile")
     z = me // 4
@@ -409,23 +431,24 @@
     parts = sort_tiles(order, at_end, tiles, [1, 1, 1, 0, 0, 0], shapes)
     first, *parts = together(first, *parts)
 
-    outer = send(jnp.where(in_centre, first, parts[0]), around)
-    near, c_own, notes, *parts = together(near, c_own, notes, *parts)
-    second = send(jnp.where(in_centre, near, parts[1]), across + [(i, i ^ 1) for i, _ in from_ends])
+    first = payload_of(at_end, parts[0], first)
+    outer = send(first, around)
+    near, c_own, *parts = together(near, c_own, *parts)
+    second = send(near, across)
     y_own = send(shard, other_y)
     y_near = send(near, other_y)
     c_near = send(near, other_core)
     own_tables = tables(keys, cols, block_total, 2 * PPD)
-    far_tables = tables(notes[0], notes[1], block_total)
     perm = flip_matrix(W)
     far_ends = [outer]
     first = jnp.where(in_centre, first, outer)
-    second, first, y_own, y_near, c_near, perm, *rest = together(
-        second, first, y_own, y_near, c_near, perm, *parts[2:], *own_tables, *far_tables
+    second, first, y_own, y_near, c_near, perm, notes, *rest = together(
+        second, first, y_own, y_near, c_near, perm, notes, *parts[1:], *own_tables
     )
-    parts, own_tables, far_tables = rest[:4], rest[4:8], rest[8:]
-
-    outer = send(second, around_crossed)
+    parts, own_tables = rest[1:5], rest[5:]
+
+    second = payload_of(at_end, rest[0], second)
+    outer = send(second, around)
     y_first = send(first, other_y)
     c_first = send(first, other_core)
     c_y_own = send(y_own, other_core)
@@ -434,7 +457,10 @@
     far_ends += [outer, send(tiles_last, from_ends)]
     halves = (slice(0, local // 2), slice(local // 2, None))
     second = [jnp.where(in_centre, second[half], outer[half]) for half in halves]
-    *second, y_first, c_first, c_y_own, c_y_near = together(*second, y_first, c_first, c_y_own, c_y_near)
+    far_tables = tables(notes[0], notes[1], block_total)
+    second[0], second[1], y_first, c_first, c_y_own, c_y_near, *far_tables = together(
+        *second, y_first, c_first, c_y_own, c_y_near, *far_tables
+    )
 
     far_centre = [send(parts[1], from_centre)]
     y_second = [send(half, other_y) for half in second]

time: 206 us -> 199 us (0.966)
  starting transfers between devices: 52.8 us -> 40 us
  waiting for transfers between devices: 56.3 us -> 65.7 us
  other arithmetic: 8.05 us -> 4.91 us
    ppermute x25, starting transfers between devices: 52.8 us -> 40 us  [send(): return lax.ppermute(value, 'tile', pairs)]
    ppermute x25, waiting for transfers between devices: 56.3 us -> 65.7 us  [send(): return lax.ppermute(value, 'tile', pairs)]
    select_n x2 -> x0, other arithmetic: 2.21 us -> none  [the longest x1 1.11 us: staged_part(): jnp.where(in_centre, near, parts[1])]
    unnamed x32 -> x36, local copies, waits for them, and re-layouts: 9.03 us -> 9.17 us
  transfers between devices with their start and end apart: 25 -> 25, of which waited for: 10 -> 9; matrix products, arithmetic and copies ran while one was open for 5% -> 3% of each run, Pallas kernels for 35% -> 36%
where the time goes in v11:
time: 199 us; the launch traced here: 198 us
  Pallas kernels  76.2 us (38%)
  waiting for transfers between devices  65.7 us (33%)
  starting transfers between devices  40 us (20%)
  local copies, waits for them, and re-layouts  11 us (6%)
  other arithmetic  4.91 us (2%)
    ppermute x25, waiting for transfers between devices, send(): return lax.ppermute(value, 'tile', pairs)  65.7 us
    ppermute x25, starting transfers between devices, send(): return lax.ppermute(value, 'tile', pairs)  40 us
    pallas_call x2, Pallas kernels, own_part(): pl.pallas_call(functools.partial(own_kernel, counts, group, not earlier),...  37.3 us
    pallas_call x3, Pallas kernels, far_part(): pl.pallas_call(functools.partial(far_kernel, base, [segment for segment,...  22.4 us
    pallas_call x3, Pallas kernels, tables(): pl.pallas_call(tables_kernel, in_specs=[SMEM] * 2, out_specs=[SMEM] * 4,...  12.1 us
    unnamed x36, local copies, waits for them, and re-layouts  9.17 us
    pallas_call x1, Pallas kernels, sort_tiles(): pl.pallas_call(functools.partial(sort_kernel, choices), in_specs=[SMEM] *...  4.36 us
  transfers between devices with their start and end apart: 25, of which 9 were waited for; matrix products, arithmetic and copies ran while one was open for 3% of the time, Pallas kernels for 36%

profile of v11, /device:TPU:0, one launch (start us, length us, event | category | flops | bytes accessed | tf_op | source)
XLA Modules:
  0.0 198.2 jit_solution(7822777594555697407)
XLA Ops:
  0.0 0.8 collective-permute-start.2
  0.9 0.5 collective-permute-start.1
  1.4 5.4 %collective-permute-start = (bf16[4,128,1024]{2,1,0:T(8,128)(2,1)}, bf16[4,128,1024]{2,1,0:T(8,128)(2,1)}, u32[]{:S(2)}, u32[]{:S(2)}) collective-permute-start(bf16[4,128,1024]{2,1,0:T(8,128)(2,1)} %refs_0_.1), channel_id=1, source_target_pairs={{0,4},{1,5},{2,6},{3,7},{4,0},{5,1},{6,2},{7,3},{8,12},{9,13},{10,... | collective-permute-start | bytes 3145736 | tf_op jit(solution)/shard_map/ppermute | solution.py:390
  6.8 4.0 %tables.3 = (s32[17]{0:T(128)}, s32[96]{0:T(128)}, s32[96]{0:T(128)}, s32[64]{0:T(128)}) custom-call(s32[96]{0:T(128)} %rows.1, s32[96]{0:T(128)} %cols.3), custom_call_target="tpu_custom_call" | custom-call | tf_op jit(solution)/shard_map/tables/pallas_call | solution.py:68
  10.8 0.0 copy-start.1
  10.8 1.9 copy-done.1
  12.7 0.6 copy-done.6
  13.3 4.4 %sort_tiles.1 = (bf16[4,128,1024]{2,1,0:T(8,128)(2,1)S(1)}, bf16[4,128,1024]{2,1,0:T(8,128)(2,1)S(1)}, bf16[32,128,128]{2,1,0:T(8,128)(2,1)S(1)}, bf16[60,128,12...) custom-call(s32[96]{0:T(128)S(1)} %copy-done.6, s32[1]{0:T(128)} %bitcast.chosen.at_end, ...), custom_call_target="tpu_custom_call" | custom-call | tf_op jit(solution)/shard_map/sort_tiles/pallas_call | solution.py:108
  17.7 0.9 copy-done.8
  18.7 0.0 collective-permute-done.2.received
  18.7 0.1 payload.2
  18.8 12.5 %collective-permute-start.4 = (bf16[4,128,1024]{2,1,0:T(8,128)(2,1)S(1)}, bf16[4,128,1024]{2,1,0:T(8,128)(2,1)S(1)}, u32[]{:S(2)}, u32[]{:S(2)}) collective-permute-start(bf16[4,128,1024]{2,1,0:T(8,128)(2,1)S(1)} %payload.2), channel_id=1, source_target_pairs={{4,0},{5,1},{6,2},{7,3},{8,12},{9,13},{10,14},{11,15},{0,8},{1,9},... | collective-permute-start | bytes 3145736 | tf_op jit(solution)/shard_map/ppermute | solution.py:390
  31.3 1.5 collective-permute-start.5
  32.8 0.0 collective-permute-done.1.refs_1_
  32.8 0.0 collective-permute-done.refs_2_
  32.8 0.1 collective-permute-start.7
  32.9 0.9 copy-done.9
  33.8 0.5 collective-permute-start.6
  34.3 0.7 collective-permute-start.3
  35.1 0.5 fusion.10.rows
  35.6 4.0 %tables.4 = (s32[33]{0:T(128)}, s32[96]{0:T(128)}, s32[96]{0:T(128)}, s32[64]{0:T(128)}) custom-call(s32[96]{0:T(128)} %fusion.10.rows, s32[96]{0:T(128)} %cols.3), custom_call_target="tpu_custom_call" | custom-call | tf_op jit(solution)/shard_map/tables/pallas_call | solution.py:68
  39.7 2.2 %fusion.perm_ref = bf16[1024,1024]{1,0:T(8,128)(2,1)} fusion(s32[1024]{0:T(1024)S(1)} %fusion.7), kind=kLoop, calls=%fused_computation.1 | loop fusion | flops 2097152 | bytes 2101248 | tf_op jit(solution)/shard_map/convert_element_type | solution.py:24
  41.9 11.3 %collective-permute-done.4.refs_0_ = bf16[4,128,1024]{2,1,0:T(8,128)(2,1)S(1)} collective-permute-done((bf16[4,128,1024]{2,1,0:T(8,128)(2,1)S(1)}, bf16[4,128,1024]{2,1,0:T(8,128)(2,1)S(1)}, u32[]{:S(2)}, u32[]{:S(2)}) %collective-permute-start.4) | collective-permute-done | bytes 1048608 | tf_op jit(solution)/shard_map/ppermute | solution.py:390
  53.2 3.2 %collective-permute-start.8 = (s32[2,96]{1,0:T(2,128)S(1)}, s32[2,96]{1,0:T(2,128)S(1)}, u32[]{:S(2)}, u32[]{:S(2)}) collective-permute-start(s32[2,96]{1,0:T(2,128)S(1)} %pad_add_fusion), channel_id=1, source_target_pairs={{0,8},{1,9},{2,10},{3,11},{4,12},{5,13},{6,14},{7,15},{8,0},{9,1},... | collective-permute-start | bytes 2312 | tf_op jit(solution)/shard_map/ppermute | solution.py:390
  56.4 1.1 broadcast_select_fusion.refs_4_
  57.5 19.7 %collective-permute-done.8 = s32[2,96]{1,0:T(2,128)S(1)} collective-permute-done((s32[2,96]{1,0:T(2,128)S(1)}, s32[2,96]{1,0:T(2,128)S(1)}, u32[]{:S(2)}, u32[]{:S(2)}) %collective-permute-start.8) | collective-permute-done | bytes 800 | tf_op jit(solution)/shard_map/ppermute | solution.py:390
  77.2 0.0 collective-permute-done.5.refs_6_
  77.2 0.7 collective-permute-done.6.refs_8_
  77.9 0.1 payload.3
  78.0 0.9 collective-permute-start.9
  78.9 0.2 collective-permute-start.12
  79.1 0.3 collective-permute-start.13
  79.4 1.5 collective-permute-start.10
  80.9 0.6 slice_bitcast_fusion
  81.5 4.0 %tables.5 = (s32[17]{0:T(128)}, s32[96]{0:T(128)}, s32[96]{0:T(128)}, s32[64]{0:T(128)}) custom-call(s32[96]{0:T(128)} %get-tuple-element.160.rows, s32[96]{0:T(128)} %get-tuple-element.159.cols), custom_call_target="tpu_custom_call" | custom-call | tf_op jit(solution)/shard_map/tables/pallas_call | solution.py:68
  85.5 1.3 collective-permute-start.19
  86.8 16.9 %collective-permute-done.9.refs_1_.refs_0_ = bf16[4,128,1024]{2,1,0:T(8,128)(2,1)S(1)} collective-permute-done((bf16[4,128,1024]{2,1,0:T(8,128)(2,1)S(1)}, bf16[4,128,1024]{2,1,0:T(8,128)(2,1)S(1)}, u32[]{:S(2)}, u32[]{:S(2)}) %collective-permute-start.9) | collective-permute-done | bytes 1048608 | tf_op jit(solution)/shard_map/ppermute | solution.py:390
  103.7 4.6 %collective-permute-start.16 = (bf16[32,128,128]{2,1,0:T(8,128)(2,1)}, bf16[32,128,128]{2,1,0:T(8,128)(2,1)}, u32[]{:S(2)}, u32[]{:S(2)}) collective-permute-start(bf16[32,128,128]{2,1,0:T(8,128)(2,1)} %copy-done.8), channel_id=1, source_target_pairs={{0,8},{1,9},{2,10},{3,11},{12,4},{13,5},{14,6},{15,7},{16,24},{17,... | collective-permute-start | bytes 3145736 | tf_op jit(solution)/shard_map/ppermute | solution.py:390
  108.4 1.1 slice_select_fusion
  109.5 1.6 collective-permute-start.14
  111.0 0.5 collective-permute-start.15
  111.5 0.7 stack.89.firsts
  112.2 22.8 %own_part.2 = (f32[16,128,1024]{2,1,0:T(8,128)}, bf16[32,128,1024]{2,1,0:T(8,128)(2,1)}) custom-call(s32[33]{0:T(128)} %get-tuple-element.121.starts, s32[96]{0:T(128)} %get-tuple-element.122.tile_at, s32[96]{0:T(128)} %get-tuple-element.123.block_at, s32[64]{0:T(128)} %get-tuple-element.124.own_slots, s32[64]{0:T(128)} %get-tuple-element.125.far_slots, ...), custom_call_target="tpu_custom_call" | custom-call | tf_op jit(solution)/shard_map/own_part/pallas_call | solution.py:244
  135.1 0.1 collective-permute-start.21
  135.2 0.5 collective-permute-start.22
  135.7 0.1 collective-permute-start.20
  135.7 0.4 collective-permute-start.23
  136.2 1.1 collective-permute-done.21.refs_3_
  137.3 1.3 collective-permute-start.18
  138.6 1.0 collective-permute-done.22.refs_4_
  139.5 0.1 collective-permute-start.24
  139.7 0.0 collective-permute-done.23.refs_7_
  139.7 0.6 copy-done.13
  140.3 0.8 copy-done.14
  141.1 1.3 collective-permute-start.17
  142.4 0.6 stack.99.firsts
  143.0 14.5 %own_part.3 = (f32[16,128,1024]{2,1,0:T(8,128)}, bf16[32,128,1024]{2,1,0:T(8,128)(2,1)}) custom-call(s32[33]{0:T(128)} %get-tuple-element.121.starts, s32[96]{0:T(128)} %get-tuple-element.122.tile_at, s32[96]{0:T(128)} %get-tuple-element.123.block_at, s32[64]{0:T(128)} %get-tuple-element.124.own_slots, ...), custom_call_target="tpu_custom_call", output_to_operand_aliasing={{0}: (17, {}), {1}: (18, {})} | custom-call | tf_op jit(solution)/shard_map/own_part/pallas_call | solution.py:244
  157.5 11.1 %collective-permute-done.19.refs_2_ = bf16[60,128,128]{2,1,0:T(8,128)(2,1)} collective-permute-done((bf16[60,128,128]{2,1,0:T(8,128)(2,1)}, bf16[60,128,128]{2,1,0:T(8,128)(2,1)}, u32[]{:S(2)}, u32[]{:S(2)}) %collective-permute-start.19) | collective-permute-done | bytes 1966112 | tf_op jit(solution)/shard_map/ppermute | solution.py:390
  168.6 3.4 %copy-done = f32[16,128,1024]{2,1,0:T(8,128)S(1)} copy-done((f32[16,128,1024]{2,1,0:T(8,128)S(1)}, f32[16,128,1024]{2,1,0:T(8,128)}, u32[]{:S(2)}) %copy-start) | copy-done | bytes 8388632
  172.0 11.8 %far_part.3 = (f32[16,128,1024]{2,1,0:T(8,128)S(1)}, bf16[16,128,1024]{2,1,0:T(8,128)(2,1)}) custom-call(s32[17]{0:T(128)S(1)} %copy-done.4, s32[96]{0:T(128)S(1)} %copy-done.5, s32[1]{0:T(128)} %bitcast.chosen.at_end, bf16[4,128,1024]{2,1,0:T(8,128)(2,1)S(1)} %collective-permute-done.4.refs_0_, ...), custom_call_target="tpu_custom_call", output_to_operand_aliasing={{0}: (6, {})} | custom-call | tf_op jit(solution)/shard_map/far_part/pallas_call | solution.py:364
  183.8 1.5 collective-permute-done.18.refs_2_
  185.3 6.0 %far_part.4 = (f32[16,128,1024]{2,1,0:T(8,128)S(1)}, bf16[16,128,1024]{2,1,0:T(8,128)(2,1)}) custom-call(s32[17]{0:T(128)S(1)} %copy-done.4, s32[96]{0:T(128)S(1)} %copy-done.5, s32[1]{0:T(128)} %bitcast.chosen.at_end, bf16[4,128,1024]{2,1,0:T(8,128)(2,1)S(1)} %collective-permute-done.9.refs_1_.refs_0_, ...), custom_call_target="tpu_custom_call", output_to_operand_aliasing={{0}: (6, {}), {1}: (8, {})} | custom-call | tf_op jit(solution)/shard_map/far_part/pallas_call | solution.py:364
  191.3 2.3 %collective-permute-done.17.refs_1_ = bf16[12,128,128]{2,1,0:T(8,128)(2,1)S(1)} collective-permute-done((bf16[12,128,128]{2,1,0:T(8,128)(2,1)}, bf16[12,128,128]{2,1,0:T(8,128)(2,1)S(1)}, u32[]{:S(2)}, u32[]{:S(2)}) %collective-permute-start.17) | collective-permute-done | bytes 393248 | tf_op jit(solution)/shard_map/ppermute | solution.py:390
  193.6 4.5 %far_part.5 = (f32[16,128,1024]{2,1,0:T(8,128)S(1)}, bf16[16,128,1024]{2,1,0:T(8,128)(2,1)}) custom-call(s32[17]{0:T(128)S(1)} %copy-done.4, s32[96]{0:T(128)S(1)} %copy-done.5, s32[1]{0:T(128)} %bitcast.chosen.at_end, bf16[32,128,128]{2,1,0:T(8,128)(2,1)} %collective-permute-done.16.refs_1_.refs_0_, ...), custom_call_target="tpu_custom_call", output_to_operand_aliasing={{0}: (5, {}), {1}: (7, {})} | custom-call | tf_op jit(solution)/shard_map/far_part/pallas_call | solution.py:364
  (42 shorter events, 0.1 us)
Async XLA Ops:
  0.0 35.0 %copy-start.15 = (s32[96]{0:T(128)S(1)}, s32[96]{0:T(128)}, u32[]{:S(2)}) copy-start(s32[96]{0:T(128)} %cols.3) | copy-start | bytes 1156
  0.0 39.6 %copy-start.16 = (s32[96]{0:T(128)S(1)}, s32[96]{0:T(128)}, u32[]{:S(2)}) copy-start(s32[96]{0:T(128)} %cols.3) | copy-start | bytes 1156
  0.0 35.0 %copy-start.17 = (s32[96]{0:T(128)S(1)}, s32[96]{0:T(128)}, u32[]{:S(2)}) copy-start(s32[96]{0:T(128)} %rows.1) | copy-start | bytes 1156
  0.0 18.7 %collective-permute-start.2 = (bf16[4,128,1024]{2,1,0:T(8,128)(2,1)}, bf16[4,128,1024]{2,1,0:T(8,128)(2,1)S(1)}, u32[]{:S(2)}, u32[]{:S(2)}) collective-permute-start(bf16[4,128,1024]{2,1,0:T(8,128)(2,1)} %refs_0_.1), channel_id=1, source_target_pairs={{4,8},{5,9},{6,10},{7,11},{8,4},{9,5},{10,6},{11,7},{20,24},{21,25... | collective-permute-start | bytes 3145736 | tf_op jit(solution)/shard_map/ppermute | solution.py:390
  0.9 31.9 %collective-permute-start.1 = (bf16[4,128,1024]{2,1,0:T(8,128)(2,1)}, bf16[4,128,1024]{2,1,0:T(8,128)(2,1)S(1)}, u32[]{:S(2)}, u32[]{:S(2)}) collective-permute-start(bf16[4,128,1024]{2,1,0:T(8,128)(2,1)} %refs_0_.1), channel_id=1, source_target_pairs={{0,1},{1,0},{2,3},{3,2},{4,5},{5,4},{6,7},{7,6},{8,9},{9,8},{10,11... | collective-permute-start | bytes 3145736 | tf_op jit(solution)/shard_map/ppermute | solution.py:390
  1.4 31.4 %collective-permute-start = (bf16[4,128,1024]{2,1,0:T(8,128)(2,1)}, bf16[4,128,1024]{2,1,0:T(8,128)(2,1)}, u32[]{:S(2)}, u32[]{:S(2)}) collective-permute-start(bf16[4,128,1024]{2,1,0:T(8,128)(2,1)} %refs_0_.1), channel_id=1, source_target_pairs={{0,4},{1,5},{2,6},{3,7},{4,0},{5,1},{6,2},{7,3},{8,12},{9,13},{10,... | collective-permute-start | bytes 3145736 | tf_op jit(solution)/shard_map/ppermute | solution.py:390
  10.8 1.9 copy-start.1
  12.7 0.6 copy-start.6
  17.7 1.0 copy-start.8
  18.7 14.2 %copy-start.2 = (bf16[4,128,1024]{2,1,0:T(8,128)(2,1)}, bf16[4,128,1024]{2,1,0:T(8,128)(2,1)S(1)}, u32[]{:S(2)}) copy-start(bf16[4,128,1024]{2,1,0:T(8,128)(2,1)S(1)} %get-tuple-element.105.tiles_ref) | copy-start | bytes 3145732
  18.7 15.6 %copy-start.7 = (bf16[60,128,128]{2,1,0:T(8,128)(2,1)}, bf16[60,128,128]{2,1,0:T(8,128)(2,1)S(1)}, u32[]{:S(2)}) copy-start(bf16[60,128,128]{2,1,0:T(8,128)(2,1)S(1)} %get-tuple-element.142) | copy-start | bytes 5898244
  18.8 34.5 %collective-permute-start.4 = (bf16[4,128,1024]{2,1,0:T(8,128)(2,1)S(1)}, bf16[4,128,1024]{2,1,0:T(8,128)(2,1)S(1)}, u32[]{:S(2)}, u32[]{:S(2)}) collective-permute-start(bf16[4,128,1024]{2,1,0:T(8,128)(2,1)S(1)} %payload.2), channel_id=1, source_target_pairs={{4,0},{5,1},{6,2},{7,3},{8,12},{9,13},{10,14},{11,15},{0,8},{1,9},... | collective-permute-start | bytes 3145736 | tf_op jit(solution)/shard_map/ppermute | solution.py:390
  31.3 46.0 %collective-permute-start.5 = (bf16[4,128,1024]{2,1,0:T(8,128)(2,1)}, bf16[4,128,1024]{2,1,0:T(8,128)(2,1)}, u32[]{:S(2)}, u32[]{:S(2)}) collective-permute-start(bf16[4,128,1024]{2,1,0:T(8,128)(2,1)} %refs_0_.1), channel_id=1, source_target_pairs={{0,2},{1,3},{2,0},{3,1},{4,6},{5,7},{6,4},{7,5},{8,10},{9,11},{10,... | collective-permute-start | bytes 3145736 | tf_op jit(solution)/shard_map/ppermute | solution.py:390
  32.8 1.0 copy-start.9
  32.8 44.4 %collective-permute-start.7 = (bf16[4,128,1024]{2,1,0:T(8,128)(2,1)}, bf16[4,128,1024]{2,1,0:T(8,128)(2,1)}, u32[]{:S(2)}, u32[]{:S(2)}) collective-permute-start(bf16[4,128,1024]{2,1,0:T(8,128)(2,1)} %collective-permute-done.refs_2_), channel_id=1, source_target_pairs={{0,1},{1,0},{2,3},{3,2},{4,5},{5,4},{6,7},{7,6},{8,9},{9,8},{10,11... | collective-permute-start | bytes 3145736 | tf_op jit(solution)/shard_map/ppermute | solution.py:390
  33.8 44.1 %collective-permute-start.6 = (bf16[4,128,1024]{2,1,0:T(8,128)(2,1)}, bf16[4,128,1024]{2,1,0:T(8,128)(2,1)}, u32[]{:S(2)}, u32[]{:S(2)}) collective-permute-start(bf16[4,128,1024]{2,1,0:T(8,128)(2,1)} %collective-permute-done.refs_2_), channel_id=1, source_target_pairs={{0,2},{1,3},{2,0},{3,1},{4,6},{5,7},{6,4},{7,5},{8,10},{9,11},{10,... | collective-permute-start | bytes 3145736 | tf_op jit(solution)/shard_map/ppermute | solution.py:390
  34.3 43.6 %collective-permute-start.3 = (bf16[4,128,1024]{2,1,0:T(8,128)(2,1)}, bf16[4,128,1024]{2,1,0:T(8,128)(2,1)S(1)}, u32[]{:S(2)}, u32[]{:S(2)}) collective-permute-start(bf16[4,128,1024]{2,1,0:T(8,128)(2,1)} %collective-permute-done.refs_2_), channel_id=1, source_target_pairs={{4,8},{5,9},{6,10},{7,11},{8,4},{9,5},{10,6},{11,7},{20,24},{21,25... | collective-permute-start | bytes 3145736 | tf_op jit(solution)/shard_map/ppermute | solution.py:390
  39.6 38.3 %copy-start.3 = (bf16[4,128,1024]{2,1,0:T(8,128)(2,1)S(1)}, bf16[4,128,1024]{2,1,0:T(8,128)(2,1)}, u32[]{:S(2)}) copy-start(bf16[4,128,1024]{2,1,0:T(8,128)(2,1)} %copy-done.2) | copy-start | bytes 3145732
  53.2 24.0 %collective-permute-start.8 = (s32[2,96]{1,0:T(2,128)S(1)}, s32[2,96]{1,0:T(2,128)S(1)}, u32[]{:S(2)}, u32[]{:S(2)}) collective-permute-start(s32[2,96]{1,0:T(2,128)S(1)} %pad_add_fusion), channel_id=1, source_target_pairs={{0,8},{1,9},{2,10},{3,11},{4,12},{5,13},{6,14},{7,15},{8,0},{9,1},... | collective-permute-start | bytes 2312 | tf_op jit(solution)/shard_map/ppermute | solution.py:390
  77.9 7.6 %collective-permute-start.11 = (bf16[4,128,1024]{2,1,0:T(8,128)(2,1)}, bf16[4,128,1024]{2,1,0:T(8,128)(2,1)}, u32[]{:S(2)}, u32[]{:S(2)}) collective-permute-start(bf16[4,128,1024]{2,1,0:T(8,128)(2,1)} %broadcast_select_fusion.refs_4_), channel_id=1, source_target_pairs={{0,1},{1,0},{2,3},{3,2},{4,5},{5,4},{6,7},{7,6},{8,9},{9,8},{10,11... | collective-permute-start | bytes 3145736 | tf_op jit(solution)/shard_map/ppermute | solution.py:390
  78.0 25.7 %collective-permute-start.9 = (bf16[4,128,1024]{2,1,0:T(8,128)(2,1)S(1)}, bf16[4,128,1024]{2,1,0:T(8,128)(2,1)S(1)}, u32[]{:S(2)}, u32[]{:S(2)}) collective-permute-start(bf16[4,128,1024]{2,1,0:T(8,128)(2,1)S(1)} %payload.3), channel_id=1, source_target_pairs={{4,0},{5,1},{6,2},{7,3},{8,12},{9,13},{10,14},{11,15},{0,8},{1,9},... | collective-permute-start | bytes 3145736 | tf_op jit(solution)/shard_map/ppermute | solution.py:390
  78.9 30.6 %collective-permute-start.12 = (bf16[4,128,1024]{2,1,0:T(8,128)(2,1)}, bf16[4,128,1024]{2,1,0:T(8,128)(2,1)}, u32[]{:S(2)}, u32[]{:S(2)}) collective-permute-start(bf16[4,128,1024]{2,1,0:T(8,128)(2,1)} %collective-permute-done.5.refs_6_), channel_id=1, source_target_pairs={{0,1},{1,0},{2,3},{3,2},{4,5},{5,4},{6,7},{7,6},{8,9},{9,8},{10,11... | collective-permute-start | bytes 3145736 | tf_op jit(solution)/shard_map/ppermute | solution.py:390
  79.1 30.4 %collective-permute-start.13 = (bf16[4,128,1024]{2,1,0:T(8,128)(2,1)}, bf16[4,128,1024]{2,1,0:T(8,128)(2,1)}, u32[]{:S(2)}, u32[]{:S(2)}) collective-permute-start(bf16[4,128,1024]{2,1,0:T(8,128)(2,1)} %collective-permute-done.6.refs_8_), channel_id=1, source_target_pairs={{0,1},{1,0},{2,3},{3,2},{4,5},{5,4},{6,7},{7,6},{8,9},{9,8},{10,11... | collective-permute-start | bytes 3145736 | tf_op jit(solution)/shard_map/ppermute | solution.py:390
  79.4 30.1 %collective-permute-start.10 = (bf16[4,128,1024]{2,1,0:T(8,128)(2,1)}, bf16[4,128,1024]{2,1,0:T(8,128)(2,1)}, u32[]{:S(2)}, u32[]{:S(2)}) collective-permute-start(bf16[4,128,1024]{2,1,0:T(8,128)(2,1)} %broadcast_select_fusion.refs_4_), channel_id=1, source_target_pairs={{0,2},{1,3},{2,0},{3,1},{4,6},{5,7},{6,4},{7,5},{8,10},{9,11},{10,... | collective-permute-start | bytes 3145736 | tf_op jit(solution)/shard_map/ppermute | solution.py:390
  85.5 83.0 %collective-permute-start.19 = (bf16[60,128,128]{2,1,0:T(8,128)(2,1)}, bf16[60,128,128]{2,1,0:T(8,128)(2,1)}, u32[]{:S(2)}, u32[]{:S(2)}) collective-permute-start(bf16[60,128,128]{2,1,0:T(8,128)(2,1)} %copy-done.7), channel_id=1, source_target_pairs={{4,12},{5,13},{6,14},{7,15},{8,0},{9,1},{10,2},{11,3},{20,28},{21,... | collective-permute-start | bytes 5898248 | tf_op jit(solution)/shard_map/ppermute | solution.py:390
  103.7 32.0 %collective-permute-start.16 = (bf16[32,128,128]{2,1,0:T(8,128)(2,1)}, bf16[32,128,128]{2,1,0:T(8,128)(2,1)}, u32[]{:S(2)}, u32[]{:S(2)}) collective-permute-start(bf16[32,128,128]{2,1,0:T(8,128)(2,1)} %copy-done.8), channel_id=1, source_target_pairs={{0,8},{1,9},{2,10},{3,11},{12,4},{13,5},{14,6},{15,7},{16,24},{17,... | collective-permute-start | bytes 3145736 | tf_op jit(solution)/shard_map/ppermute | solution.py:390
  109.5 25.6 %collective-permute-start.14 = (bf16[2,128,1024]{2,1,0:T(8,128)(2,1)}, bf16[2,128,1024]{2,1,0:T(8,128)(2,1)S(1)}, u32[]{:S(2)}, u32[]{:S(2)}) collective-permute-start(bf16[2,128,1024]{2,1,0:T(8,128)(2,1)} %get-tuple-element.144.refs_1_), channel_id=1, source_target_pairs={{0,2},{1,3},{2,0},{3,1},{4,6},{5,7},{6,4},{7,5},{8,10},{9,11},{10,... | collective-permute-start | bytes 1572872 | tf_op jit(solution)/shard_map/ppermute | solution.py:390
  111.0 24.0 %collective-permute-start.15 = (bf16[2,128,1024]{2,1,0:T(8,128)(2,1)}, bf16[2,128,1024]{2,1,0:T(8,128)(2,1)S(1)}, u32[]{:S(2)}, u32[]{:S(2)}) collective-permute-start(bf16[2,128,1024]{2,1,0:T(8,128)(2,1)} %get-tuple-element.145.refs_2_), channel_id=1, source_target_pairs={{0,2},{1,3},{2,0},{3,1},{4,6},{5,7},{6,4},{7,5},{8,10},{9,11},{10,... | collective-permute-start | bytes 1572872 | tf_op jit(solution)/shard_map/ppermute | solution.py:390
  135.1 4.6 %copy-start.10 = (bf16[2,128,1024]{2,1,0:T(8,128)(2,1)}, bf16[2,128,1024]{2,1,0:T(8,128)(2,1)S(1)}, u32[]{:S(2)}) copy-start(bf16[2,128,1024]{2,1,0:T(8,128)(2,1)S(1)} %collective-permute-done.14.refs_5_) | copy-start | bytes 1572868
  135.1 1.1 copy-start.11
  135.1 2.2 %collective-permute-start.21 = (bf16[2,128,1024]{2,1,0:T(8,128)(2,1)}, bf16[2,128,1024]{2,1,0:T(8,128)(2,1)S(1)}, u32[]{:S(2)}, u32[]{:S(2)}) collective-permute-start(bf16[2,128,1024]{2,1,0:T(8,128)(2,1)} %get-tuple-element.144.refs_1_), channel_id=1, source_target_pairs={{0,1},{1,0},{2,3},{3,2},{4,5},{5,4},{6,7},{7,6},{8,9},{9,8},{10,11... | collective-permute-start | bytes 1572872 | tf_op jit(solution)/shard_map/ppermute | solution.py:390
  135.2 4.4 %collective-permute-start.22 = (bf16[2,128,1024]{2,1,0:T(8,128)(2,1)}, bf16[2,128,1024]{2,1,0:T(8,128)(2,1)S(1)}, u32[]{:S(2)}, u32[]{:S(2)}) collective-permute-start(bf16[2,128,1024]{2,1,0:T(8,128)(2,1)} %get-tuple-element.145.refs_2_), channel_id=1, source_target_pairs={{0,1},{1,0},{2,3},{3,2},{4,5},{5,4},{6,7},{7,6},{8,9},{9,8},{10,11... | collective-permute-start | bytes 1572872 | tf_op jit(solution)/shard_map/ppermute | solution.py:390
  135.7 7.4 %collective-permute-start.20 = (bf16[4,128,1024]{2,1,0:T(8,128)(2,1)}, bf16[4,128,1024]{2,1,0:T(8,128)(2,1)}, u32[]{:S(2)}, u32[]{:S(2)}) collective-permute-start(bf16[4,128,1024]{2,1,0:T(8,128)(2,1)} %collective-permute-done.10.refs_10_), channel_id=1, source_target_pairs={{0,1},{1,0},{2,3},{3,2},{4,5},{5,4},{6,7},{7,6},{8,9},{9,8},{10,11... | collective-permute-start | bytes 3145736 | tf_op jit(solution)/shard_map/ppermute | solution.py:390
  135.7 3.9 %collective-permute-start.23 = (bf16[2,128,1024]{2,1,0:T(8,128)(2,1)S(1)}, bf16[2,128,1024]{2,1,0:T(8,128)(2,1)S(1)}, u32[]{:S(2)}, u32[]{:S(2)}) collective-permute-start(bf16[2,128,1024]{2,1,0:T(8,128)(2,1)S(1)} %collective-permute-done.14.refs_5_), channel_id=1, source_target_pairs={{0,1},{1,0},{2,3},{3,2},{4,5},{5,4},{6,7},{7,6},{8,9},{9,8},{10,11... | collective-permute-start | bytes 1572872 | tf_op jit(solution)/shard_map/ppermute | solution.py:390
  137.3 2.4 %copy-start.12 = (bf16[2,128,1024]{2,1,0:T(8,128)(2,1)}, bf16[2,128,1024]{2,1,0:T(8,128)(2,1)S(1)}, u32[]{:S(2)}) copy-start(bf16[2,128,1024]{2,1,0:T(8,128)(2,1)S(1)} %collective-permute-done.21.refs_3_) | copy-start | bytes 1572868
  137.3 48.0 %collective-permute-start.18 = (bf16[24,128,128]{2,1,0:T(8,128)(2,1)}, bf16[24,128,128]{2,1,0:T(8,128)(2,1)S(1)}, u32[]{:S(2)}, u32[]{:S(2)}) collective-permute-start(bf16[24,128,128]{2,1,0:T(8,128)(2,1)} %get-tuple-element.141), channel_id=1, source_target_pairs={{4,12},{5,13},{6,14},{7,15},{8,0},{9,1},{10,2},{11,3},{20,28},{21,... | collective-permute-start | bytes 2359304 | tf_op jit(solution)/shard_map/ppermute | solution.py:390
  139.5 0.8 copy-start.13
  139.5 3.5 %collective-permute-start.24 = (bf16[2,128,1024]{2,1,0:T(8,128)(2,1)}, bf16[2,128,1024]{2,1,0:T(8,128)(2,1)}, u32[]{:S(2)}, u32[]{:S(2)}) collective-permute-start(bf16[2,128,1024]{2,1,0:T(8,128)(2,1)} %copy-done.11), channel_id=1, source_target_pairs={{0,1},{1,0},{2,3},{3,2},{4,5},{5,4},{6,7},{7,6},{8,9},{9,8},{10,11... | collective-permute-start | bytes 1572872 | tf_op jit(solution)/shard_map/ppermute | solution.py:390
  140.3 0.8 copy-start.14
  141.1 52.6 %collective-permute-start.17 = (bf16[12,128,128]{2,1,0:T(8,128)(2,1)}, bf16[12,128,128]{2,1,0:T(8,128)(2,1)S(1)}, u32[]{:S(2)}, u32[]{:S(2)}) collective-permute-start(bf16[12,128,128]{2,1,0:T(8,128)(2,1)} %get-tuple-element.140), channel_id=1, source_target_pairs={{4,12},{5,13},{6,14},{7,15},{8,0},{9,1},{10,2},{11,3},{20,28},{21,... | collective-permute-start | bytes 1179656 | tf_op jit(solution)/shard_map/ppermute | solution.py:390
  143.0 25.6 %copy-start.4 = (s32[17]{0:T(128)S(1)}, s32[17]{0:T(128)}, u32[]{:S(2)}) copy-start(s32[17]{0:T(128)} %get-tuple-element.116.starts) | copy-start | bytes 208
  143.0 25.6 %copy-start.5 = (s32[96]{0:T(128)S(1)}, s32[96]{0:T(128)}, u32[]{:S(2)}) copy-start(s32[96]{0:T(128)} %get-tuple-element.117.block_at) | copy-start | bytes 1156
  168.6 3.4 %copy-start = (f32[16,128,1024]{2,1,0:T(8,128)S(1)}, f32[16,128,1024]{2,1,0:T(8,128)}, u32[]{:S(2)}) copy-start(f32[16,128,1024]{2,1,0:T(8,128)} %get-tuple-element.150.refs_3_) | copy-start | bytes 25165828

commit v12 on v11

--- a/solution.py
+++ b/solution.py
@@ -402,7 +402,7 @@
     from_ends = [(i, i ^ 8) for i in range(16) if i not in centre]
     from_centre = [(i, i ^ 8) for i in centre]
     around = [(i, i ^ 4) for i in centre] + from_ends
-    other_z, other_y, other_core, opposite = (flipped_bit(bit) for bit in (4, 2, 1, 8))
+    other_z, other_y, other_core = (flipped_bit(bit) for bit in (4, 2, 1))
     me = lax.axis_index("tile")
     z = me // 4
     in_centre = (z == 1) | (z == 2)
@@ -421,9 +421,10 @@
 
     near = send(shard, other_z)
     first = send(shard, across)
-    notes = send(jnp.stack([rows, cols]), opposite)
+    notes = lax.all_gather(jnp.stack([rows, cols]), "tile")
     order = tables(rows, cols, block_total)[1]
     c_own = send(shard, other_core)
+    y_own = send(shard, other_y)
     count = tiles.shape[0]
     step = shard.size // tiles[0].size
     sizes = tile_parts(count)
@@ -433,22 +434,21 @@
 
     first = payload_of(at_end, parts[0], first)
     outer = send(first, around)
-    near, c_own, *parts = together(near, c_own, *parts)
+    near, c_own, y_own, *parts = together(near, c_own, y_own, *parts)
     second = send(near, across)
-    y_own = send(shard, other_y)
     y_near = send(near, other_y)
     c_near = send(near, other_core)
     own_tables = tables(keys, cols, block_total, 2 * PPD)
     perm = flip_matrix(W)
     far_ends = [outer]
     first = jnp.where(in_centre, first, outer)
-    second, first, y_own, y_near, c_near, perm, notes, *rest = together(
-        second, first, y_own, y_near, c_near, perm, notes, *parts[1:], *own_tables
+    second, tiles_next = together(second, parts[1])
+    second = payload_of(at_end, tiles_next, second)
+    outer = send(second, around)
+    first, y_own, y_near, c_near, perm, notes, *rest = together(
+        first, y_own, y_near, c_near, perm, notes, *parts[2:], *own_tables
     )
-    parts, own_tables = rest[1:5], rest[5:]
-
-    second = payload_of(at_end, rest[0], second)
-    outer = send(second, around)
+    parts, own_tables = rest[:4], rest[4:]
     y_first = send(first, other_y)
     c_first = send(first, other_core)
     c_y_own = send(y_own, other_core)
@@ -457,6 +457,7 @@
     far_ends += [outer, send(tiles_last, from_ends)]
     halves = (slice(0, local // 2), slice(local // 2, None))
     second = [jnp.where(in_centre, second[half], outer[half]) for half in halves]
+    notes = lax.dynamic_index_in_dim(notes, me ^ 8, keepdims=False)
     far_tables = tables(notes[0], notes[1], block_total)
     second[0], second[1], y_first, c_first, c_y_own, c_y_near, *far_tables = together(
         *second, y_first, c_first, c_y_own, c_y_near, *far_tables

time: 199 us -> 213 us (1.070)
  waiting for transfers between devices: 65.7 us -> 31.8 us
  blocking collectives: 0 us -> 30.7 us
  starting transfers between devices: 40 us -> 55.9 us
  Pallas kernels: 76.2 us -> 78.9 us
    ppermute x25 -> x24, waiting for transfers between devices: 65.7 us -> 31.8 us  [send(): return lax.ppermute(value, 'tile', pairs)]
    all_gather x0 -> x1, blocking collectives: none -> 30.7 us  [staged_part(): notes = lax.all_gather(jnp.stack([rows, cols]), 'tile')]
    ppermute x25 -> x24, starting transfers between devices: 40 us -> 55.9 us  [send(): return lax.ppermute(value, 'tile', pairs)]
  transfers between devices with their start and end apart: 25 -> 24, of which waited for: 9 -> 7; matrix products, arithmetic and copies ran while one was open for 3% -> 3% of each run, Pallas kernels for 36% -> 35%
where the time goes in v12:
time: 213 us
  Pallas kernels  78.9 us (37%)
  starting transfers between devices  55.9 us (26%)
  waiting for transfers between devices  31.8 us (15%)
  blocking collectives  30.7 us (14%)
  local copies, waits for them, and re-layouts  10.1 us (5%)
  other arithmetic  4.94 us (2%)
    ppermute x24, starting transfers between devices, send(): return lax.ppermute(value, 'tile', pairs)  55.9 us
    pallas_call x2, Pallas kernels, own_part(): pl.pallas_call(functools.partial(own_kernel, counts, group, not earlier),...  38.7 us
    ppermute x24, waiting for transfers between devices, send(): return lax.ppermute(value, 'tile', pairs)  31.8 us
    all_gather x1, blocking collectives, staged_part(): notes = lax.all_gather(jnp.stack([rows, cols]), 'tile')  30.7 us
    pallas_call x3, Pallas kernels, far_part(): pl.pallas_call(functools.partial(far_kernel, base, [segment for segment,...  23.6 us
    pallas_call x3, Pallas kernels, tables(): pl.pallas_call(tables_kernel, in_specs=[SMEM] * 2, out_specs=[SMEM] * 4,...  12.1 us
    unnamed x36, local copies, waits for them, and re-layouts  8.31 us
    pallas_call x1, Pallas kernels, sort_tiles(): pl.pallas_call(functools.partial(sort_kernel, choices), in_specs=[SMEM] *...  4.36 us
  transfers between devices with their start and end apart: 24, of which 7 were waited for; matrix products, arithmetic and copies ran while one was open for 3% of the time, Pallas kernels for 35%

profile of v12, /device:TPU:0, one launch (start us, length us, event | category | flops | bytes accessed | tf_op | source)
XLA Modules:
  0.0 212.6 jit_solution(9680314832600452702)
XLA Ops:
  0.0 0.8 collective-permute-start.3
  0.9 3.0 %collective-permute-start.2 = (bf16[4,128,1024]{2,1,0:T(8,128)(2,1)}, bf16[4,128,1024]{2,1,0:T(8,128)(2,1)}, u32[]{:S(2)}, u32[]{:S(2)}) collective-permute-start(bf16[4,128,1024]{2,1,0:T(8,128)(2,1)} %refs_0_.1), channel_id=1, source_target_pairs={{0,2},{1,3},{2,0},{3,1},{4,6},{5,7},{6,4},{7,5},{8,10},{9,11},{10,... | collective-permute-start | bytes 3145736 | tf_op jit(solution)/shard_map/ppermute | solution.py:390
  3.9 0.0 collective-permute-start.1
  3.9 4.3 %collective-permute-start = (bf16[4,128,1024]{2,1,0:T(8,128)(2,1)}, bf16[4,128,1024]{2,1,0:T(8,128)(2,1)}, u32[]{:S(2)}, u32[]{:S(2)}) collective-permute-start(bf16[4,128,1024]{2,1,0:T(8,128)(2,1)} %refs_0_.1), channel_id=1, source_target_pairs={{0,4},{1,5},{2,6},{3,7},{4,0},{5,1},{6,2},{7,3},{8,12},{9,13},{10,... | collective-permute-start | bytes 3145736 | tf_op jit(solution)/shard_map/ppermute | solution.py:390
  8.2 4.0 %tables.3 = (s32[17]{0:T(128)}, s32[96]{0:T(128)}, s32[96]{0:T(128)}, s32[64]{0:T(128)}) custom-call(s32[96]{0:T(128)} %rows.1, s32[96]{0:T(128)} %cols.3), custom_call_target="tpu_custom_call" | custom-call | tf_op jit(solution)/shard_map/tables/pallas_call | solution.py:68
  12.3 0.0 copy-start.1
  12.3 1.9 copy-done.1
  14.2 0.7 copy-done.6
  14.8 4.4 %sort_tiles.1 = (bf16[4,128,1024]{2,1,0:T(8,128)(2,1)S(1)}, bf16[4,128,1024]{2,1,0:T(8,128)(2,1)S(1)}, bf16[32,128,128]{2,1,0:T(8,128)(2,1)S(1)}, bf16[60,128,12...) custom-call(s32[96]{0:T(128)S(1)} %copy-done.6, s32[1]{0:T(128)} %bitcast.chosen.at_end, ...), custom_call_target="tpu_custom_call" | custom-call | tf_op jit(solution)/shard_map/sort_tiles/pallas_call | solution.py:108
  19.2 1.0 copy-done.8
  20.2 0.1 payload.3
  20.3 11.0 %collective-permute-start.6 = (bf16[4,128,1024]{2,1,0:T(8,128)(2,1)S(1)}, bf16[4,128,1024]{2,1,0:T(8,128)(2,1)S(1)}, u32[]{:S(2)}, u32[]{:S(2)}) collective-permute-start(bf16[4,128,1024]{2,1,0:T(8,128)(2,1)S(1)} %payload.3), channel_id=1, source_target_pairs={{4,0},{5,1},{6,2},{7,3},{8,12},{9,13},{10,14},{11,15},{0,8},{1,9},... | collective-permute-start | bytes 3145736 | tf_op jit(solution)/shard_map/ppermute | solution.py:390
  31.3 0.0 collective-permute-done.2.refs_6_
  31.3 0.0 collective-permute-done.1.refs_1_
  31.3 1.3 collective-permute-done.refs_2_
  32.6 1.2 collective-permute-start.7
  33.8 0.7 collective-permute-start.4
  34.5 0.5 fusion.10.rows
  35.1 4.0 %tables.4 = (s32[33]{0:T(128)}, s32[96]{0:T(128)}, s32[96]{0:T(128)}, s32[64]{0:T(128)}) custom-call(s32[96]{0:T(128)} %fusion.10.rows, s32[96]{0:T(128)} %cols.3), custom_call_target="tpu_custom_call" | custom-call | tf_op jit(solution)/shard_map/tables/pallas_call | solution.py:68
  39.2 30.7 %all-gather.1 = s32[16,2,96]{2,1,0:T(2,128)S(1)} all-gather(s32[1,2,96]{2,1,0:T(2,128)S(1)} %add_bitcast_fusion), channel_id=2, replica_groups=mesh['groups'=2,'tile'=16] {'tile'}, dimensions={0}, use_global_device_ids=true | all-gather | bytes 13056 | tf_op jit(solution)/shard_map/all_gather | solution.py:424
  69.8 2.2 %fusion.perm_ref = bf16[1024,1024]{1,0:T(8,128)(2,1)} fusion(s32[1024]{0:T(1024)S(1)} %fusion.7), kind=kLoop, calls=%fused_computation.1 | loop fusion | flops 2097152 | bytes 2101248 | tf_op jit(solution)/shard_map/convert_element_type | solution.py:24
  72.0 0.0 collective-permute-done.6.refs_0_
  72.0 1.1 broadcast_select_fusion.refs_4_
  73.1 0.0 collective-permute-done.8.refs_3_
  73.1 0.0 collective-permute-done.7.refs_8_
  73.1 0.3 collective-permute-start.10
  73.5 0.0 collective-permute-done.4.received
  73.5 0.1 payload.2
  73.6 19.8 %collective-permute-start.5 = (bf16[4,128,1024]{2,1,0:T(8,128)(2,1)S(1)}, bf16[4,128,1024]{2,1,0:T(8,128)(2,1)S(1)}, u32[]{:S(2)}, u32[]{:S(2)}) collective-permute-start(bf16[4,128,1024]{2,1,0:T(8,128)(2,1)S(1)} %payload.2), channel_id=1, source_target_pairs={{4,0},{5,1},{6,2},{7,3},{8,12},{9,13},{10,14},{11,15},{0,8},{1,9},... | collective-permute-start | bytes 3145736 | tf_op jit(solution)/shard_map/ppermute | solution.py:390
  93.3 0.0 collective-permute-start.11
  93.4 0.5 collective-permute-start.12
  93.9 0.6 collective-permute-start.9
  94.5 0.5 slice_bitcast_fusion
  95.0 4.0 %tables.5 = (s32[17]{0:T(128)}, s32[96]{0:T(128)}, s32[96]{0:T(128)}, s32[64]{0:T(128)}) custom-call(s32[96]{0:T(128)} %get-tuple-element.162.rows, s32[96]{0:T(128)} %get-tuple-element.161.cols), custom_call_target="tpu_custom_call" | custom-call | tf_op jit(solution)/shard_map/tables/pallas_call | solution.py:68
  99.1 0.0 collective-permute-done.10.refs_5_
  99.1 1.3 collective-permute-start.18
  100.4 15.8 %collective-permute-done.5.refs_1_.refs_0_ = bf16[4,128,1024]{2,1,0:T(8,128)(2,1)S(1)} collective-permute-done((bf16[4,128,1024]{2,1,0:T(8,128)(2,1)S(1)}, bf16[4,128,1024]{2,1,0:T(8,128)(2,1)S(1)}, u32[]{:S(2)}, u32[]{:S(2)}) %collective-permute-start.5) | collective-permute-done | bytes 1048608 | tf_op jit(solution)/shard_map/ppermute | solution.py:390
  116.2 6.4 %collective-permute-start.15 = (bf16[32,128,128]{2,1,0:T(8,128)(2,1)}, bf16[32,128,128]{2,1,0:T(8,128)(2,1)}, u32[]{:S(2)}, u32[]{:S(2)}) collective-permute-start(bf16[32,128,128]{2,1,0:T(8,128)(2,1)} %copy-done.8), channel_id=1, source_target_pairs={{0,8},{1,9},{2,10},{3,11},{12,4},{13,5},{14,6},{15,7},{16,24},{17,... | collective-permute-start | bytes 3145736 | tf_op jit(solution)/shard_map/ppermute | solution.py:390
  122.5 1.1 slice_select_fusion
  123.6 0.7 collective-permute-start.13
  124.3 1.4 collective-permute-start.14
  125.7 0.6 stack.89.firsts
  126.3 23.8 %own_part.2 = (f32[16,128,1024]{2,1,0:T(8,128)}, bf16[32,128,1024]{2,1,0:T(8,128)(2,1)}) custom-call(s32[33]{0:T(128)} %get-tuple-element.123.starts, s32[96]{0:T(128)} %get-tuple-element.124.tile_at, s32[96]{0:T(128)} %get-tuple-element.125.block_at, s32[64]{0:T(128)} %get-tuple-element.126.own_slots, s32[64]{0:T(128)} %get-tuple-element.127.far_slots, ...), custom_call_target="tpu_custom_call" | custom-call | tf_op jit(solution)/shard_map/own_part/pallas_call | solution.py:244
  150.2 0.1 collective-permute-start.20
  150.2 0.5 collective-permute-start.21
  150.7 0.1 collective-permute-start.19
  150.8 0.4 collective-permute-start.22
  151.3 1.1 collective-permute-done.20.refs_3_
  152.3 1.3 collective-permute-start.17
  153.6 1.0 collective-permute-done.21.refs_4_
  154.6 0.1 collective-permute-start.23
  154.7 0.0 collective-permute-done.22.refs_7_
  154.8 0.6 copy-done.13
  155.4 0.8 copy-done.14
  156.2 1.3 collective-permute-start.16
  157.5 0.6 stack.99.firsts
  158.1 14.9 %own_part.3 = (f32[16,128,1024]{2,1,0:T(8,128)}, bf16[32,128,1024]{2,1,0:T(8,128)(2,1)}) custom-call(s32[33]{0:T(128)} %get-tuple-element.123.starts, s32[96]{0:T(128)} %get-tuple-element.124.tile_at, s32[96]{0:T(128)} %get-tuple-element.125.block_at, s32[64]{0:T(128)} %get-tuple-element.126.own_slots, ...), custom_call_target="tpu_custom_call", output_to_operand_aliasing={{0}: (17, {}), {1}: (18, {})} | custom-call | tf_op jit(solution)/shard_map/own_part/pallas_call | solution.py:244
  173.1 9.8 %collective-permute-done.18.refs_2_ = bf16[60,128,128]{2,1,0:T(8,128)(2,1)} collective-permute-done((bf16[60,128,128]{2,1,0:T(8,128)(2,1)}, bf16[60,128,128]{2,1,0:T(8,128)(2,1)}, u32[]{:S(2)}, u32[]{:S(2)}) %collective-permute-start.18) | collective-permute-done | bytes 1966112 | tf_op jit(solution)/shard_map/ppermute | solution.py:390
  182.8 3.4 %copy-done = f32[16,128,1024]{2,1,0:T(8,128)S(1)} copy-done((f32[16,128,1024]{2,1,0:T(8,128)S(1)}, f32[16,128,1024]{2,1,0:T(8,128)}, u32[]{:S(2)}) %copy-start) | copy-done | bytes 8388632
  186.2 12.4 %far_part.3 = (f32[16,128,1024]{2,1,0:T(8,128)S(1)}, bf16[16,128,1024]{2,1,0:T(8,128)(2,1)}) custom-call(s32[17]{0:T(128)S(1)} %copy-done.4, s32[96]{0:T(128)S(1)} %copy-done.5, s32[1]{0:T(128)} %bitcast.chosen.at_end, bf16[4,128,1024]{2,1,0:T(8,128)(2,1)S(1)} %collective-permute-done.6.refs_0_, ...), custom_call_target="tpu_custom_call", output_to_operand_aliasing={{0}: (6, {})} | custom-call | tf_op jit(solution)/shard_map/far_part/pallas_call | solution.py:364
  198.6 1.0 collective-permute-done.17.refs_2_
  199.6 6.5 %far_part.4 = (f32[16,128,1024]{2,1,0:T(8,128)S(1)}, bf16[16,128,1024]{2,1,0:T(8,128)(2,1)}) custom-call(s32[17]{0:T(128)S(1)} %copy-done.4, s32[96]{0:T(128)S(1)} %copy-done.5, s32[1]{0:T(128)} %bitcast.chosen.at_end, bf16[4,128,1024]{2,1,0:T(8,128)(2,1)S(1)} %collective-permute-done.5.refs_1_.refs_0_, ...), custom_call_target="tpu_custom_call", output_to_operand_aliasing={{0}: (6, {}), {1}: (8, {})} | custom-call | tf_op jit(solution)/shard_map/far_part/pallas_call | solution.py:364
  206.1 1.8 collective-permute-done.16.refs_1_
  207.9 4.7 %far_part.5 = (f32[16,128,1024]{2,1,0:T(8,128)S(1)}, bf16[16,128,1024]{2,1,0:T(8,128)(2,1)}) custom-call(s32[17]{0:T(128)S(1)} %copy-done.4, s32[96]{0:T(128)S(1)} %copy-done.5, s32[1]{0:T(128)} %bitcast.chosen.at_end, bf16[32,128,128]{2,1,0:T(8,128)(2,1)} %collective-permute-done.15.refs_1_.refs_0_, ...), custom_call_target="tpu_custom_call", output_to_operand_aliasing={{0}: (5, {}), {1}: (7, {})} | custom-call | tf_op jit(solution)/shard_map/far_part/pallas_call | solution.py:364
  (42 shorter events, 0.1 us)
Async XLA Ops:
  0.0 34.5 %copy-start.15 = (s32[96]{0:T(128)S(1)}, s32[96]{0:T(128)}, u32[]{:S(2)}) copy-start(s32[96]{0:T(128)} %cols.3) | copy-start | bytes 1156
  0.0 39.1 %copy-start.16 = (s32[96]{0:T(128)S(1)}, s32[96]{0:T(128)}, u32[]{:S(2)}) copy-start(s32[96]{0:T(128)} %cols.3) | copy-start | bytes 1156
  0.0 34.5 %copy-start.17 = (s32[96]{0:T(128)S(1)}, s32[96]{0:T(128)}, u32[]{:S(2)}) copy-start(s32[96]{0:T(128)} %rows.1) | copy-start | bytes 1156
  0.0 20.2 %collective-permute-start.3 = (bf16[4,128,1024]{2,1,0:T(8,128)(2,1)}, bf16[4,128,1024]{2,1,0:T(8,128)(2,1)S(1)}, u32[]{:S(2)}, u32[]{:S(2)}) collective-permute-start(bf16[4,128,1024]{2,1,0:T(8,128)(2,1)} %refs_0_.1), channel_id=1, source_target_pairs={{4,8},{5,9},{6,10},{7,11},{8,4},{9,5},{10,6},{11,7},{20,24},{21,25... | collective-permute-start | bytes 3145736 | tf_op jit(solution)/shard_map/ppermute | solution.py:390
  0.9 30.4 %collective-permute-start.2 = (bf16[4,128,1024]{2,1,0:T(8,128)(2,1)}, bf16[4,128,1024]{2,1,0:T(8,128)(2,1)}, u32[]{:S(2)}, u32[]{:S(2)}) collective-permute-start(bf16[4,128,1024]{2,1,0:T(8,128)(2,1)} %refs_0_.1), channel_id=1, source_target_pairs={{0,2},{1,3},{2,0},{3,1},{4,6},{5,7},{6,4},{7,5},{8,10},{9,11},{10,... | collective-permute-start | bytes 3145736 | tf_op jit(solution)/shard_map/ppermute | solution.py:390
  3.9 27.4 %collective-permute-start.1 = (bf16[4,128,1024]{2,1,0:T(8,128)(2,1)}, bf16[4,128,1024]{2,1,0:T(8,128)(2,1)S(1)}, u32[]{:S(2)}, u32[]{:S(2)}) collective-permute-start(bf16[4,128,1024]{2,1,0:T(8,128)(2,1)} %refs_0_.1), channel_id=1, source_target_pairs={{0,1},{1,0},{2,3},{3,2},{4,5},{5,4},{6,7},{7,6},{8,9},{9,8},{10,11... | collective-permute-start | bytes 3145736 | tf_op jit(solution)/shard_map/ppermute | solution.py:390
  3.9 28.7 %collective-permute-start = (bf16[4,128,1024]{2,1,0:T(8,128)(2,1)}, bf16[4,128,1024]{2,1,0:T(8,128)(2,1)}, u32[]{:S(2)}, u32[]{:S(2)}) collective-permute-start(bf16[4,128,1024]{2,1,0:T(8,128)(2,1)} %refs_0_.1), channel_id=1, source_target_pairs={{0,4},{1,5},{2,6},{3,7},{4,0},{5,1},{6,2},{7,3},{8,12},{9,13},{10,... | collective-permute-start | bytes 3145736 | tf_op jit(solution)/shard_map/ppermute | solution.py:390
  12.3 1.9 copy-start.1
  14.2 0.7 copy-start.6
  19.2 1.0 copy-start.8
  20.2 12.4 %copy-start.2 = (bf16[4,128,1024]{2,1,0:T(8,128)(2,1)}, bf16[4,128,1024]{2,1,0:T(8,128)(2,1)S(1)}, u32[]{:S(2)}) copy-start(bf16[4,128,1024]{2,1,0:T(8,128)(2,1)S(1)} %get-tuple-element.97.tiles_ref) | copy-start | bytes 3145732
  20.2 13.6 %copy-start.7 = (bf16[60,128,128]{2,1,0:T(8,128)(2,1)}, bf16[60,128,128]{2,1,0:T(8,128)(2,1)S(1)}, u32[]{:S(2)}) copy-start(bf16[60,128,128]{2,1,0:T(8,128)(2,1)S(1)} %get-tuple-element.144) | copy-start | bytes 5898244
  20.3 51.8 %collective-permute-start.6 = (bf16[4,128,1024]{2,1,0:T(8,128)(2,1)S(1)}, bf16[4,128,1024]{2,1,0:T(8,128)(2,1)S(1)}, u32[]{:S(2)}, u32[]{:S(2)}) collective-permute-start(bf16[4,128,1024]{2,1,0:T(8,128)(2,1)S(1)} %payload.3), channel_id=1, source_target_pairs={{4,0},{5,1},{6,2},{7,3},{8,12},{9,13},{10,14},{11,15},{0,8},{1,9},... | collective-permute-start | bytes 3145736 | tf_op jit(solution)/shard_map/ppermute | solution.py:390
  31.3 1.3 copy-start.9
  32.6 40.5 %collective-permute-start.8 = (bf16[4,128,1024]{2,1,0:T(8,128)(2,1)}, bf16[4,128,1024]{2,1,0:T(8,128)(2,1)}, u32[]{:S(2)}, u32[]{:S(2)}) collective-permute-start(bf16[4,128,1024]{2,1,0:T(8,128)(2,1)} %collective-permute-done.refs_2_), channel_id=1, source_target_pairs={{0,1},{1,0},{2,3},{3,2},{4,5},{5,4},{6,7},{7,6},{8,9},{9,8},{10,11... | collective-permute-start | bytes 3145736 | tf_op jit(solution)/shard_map/ppermute | solution.py:390
  32.6 40.5 %collective-permute-start.7 = (bf16[4,128,1024]{2,1,0:T(8,128)(2,1)}, bf16[4,128,1024]{2,1,0:T(8,128)(2,1)}, u32[]{:S(2)}, u32[]{:S(2)}) collective-permute-start(bf16[4,128,1024]{2,1,0:T(8,128)(2,1)} %collective-permute-done.refs_2_), channel_id=1, source_target_pairs={{0,2},{1,3},{2,0},{3,1},{4,6},{5,7},{6,4},{7,5},{8,10},{9,11},{10,... | collective-permute-start | bytes 3145736 | tf_op jit(solution)/shard_map/ppermute | solution.py:390
  33.8 39.7 %collective-permute-start.4 = (bf16[4,128,1024]{2,1,0:T(8,128)(2,1)}, bf16[4,128,1024]{2,1,0:T(8,128)(2,1)S(1)}, u32[]{:S(2)}, u32[]{:S(2)}) collective-permute-start(bf16[4,128,1024]{2,1,0:T(8,128)(2,1)} %collective-permute-done.refs_2_), channel_id=1, source_target_pairs={{4,8},{5,9},{6,10},{7,11},{8,4},{9,5},{10,6},{11,7},{20,24},{21,25... | collective-permute-start | bytes 3145736 | tf_op jit(solution)/shard_map/ppermute | solution.py:390
  39.1 34.3 %copy-start.3 = (bf16[4,128,1024]{2,1,0:T(8,128)(2,1)S(1)}, bf16[4,128,1024]{2,1,0:T(8,128)(2,1)}, u32[]{:S(2)}) copy-start(bf16[4,128,1024]{2,1,0:T(8,128)(2,1)} %copy-done.2) | copy-start | bytes 3145732
  73.1 25.9 %collective-permute-start.10 = (bf16[4,128,1024]{2,1,0:T(8,128)(2,1)}, bf16[4,128,1024]{2,1,0:T(8,128)(2,1)}, u32[]{:S(2)}, u32[]{:S(2)}) collective-permute-start(bf16[4,128,1024]{2,1,0:T(8,128)(2,1)} %broadcast_select_fusion.refs_4_), channel_id=1, source_target_pairs={{0,1},{1,0},{2,3},{3,2},{4,5},{5,4},{6,7},{7,6},{8,9},{9,8},{10,11... | collective-permute-start | bytes 3145736 | tf_op jit(solution)/shard_map/ppermute | solution.py:390
  73.6 42.6 %collective-permute-start.5 = (bf16[4,128,1024]{2,1,0:T(8,128)(2,1)S(1)}, bf16[4,128,1024]{2,1,0:T(8,128)(2,1)S(1)}, u32[]{:S(2)}, u32[]{:S(2)}) collective-permute-start(bf16[4,128,1024]{2,1,0:T(8,128)(2,1)S(1)} %payload.2), channel_id=1, source_target_pairs={{4,0},{5,1},{6,2},{7,3},{8,12},{9,13},{10,14},{11,15},{0,8},{1,9},... | collective-permute-start | bytes 3145736 | tf_op jit(solution)/shard_map/ppermute | solution.py:390
  93.3 30.3 %collective-permute-start.11 = (bf16[4,128,1024]{2,1,0:T(8,128)(2,1)}, bf16[4,128,1024]{2,1,0:T(8,128)(2,1)}, u32[]{:S(2)}, u32[]{:S(2)}) collective-permute-start(bf16[4,128,1024]{2,1,0:T(8,128)(2,1)} %collective-permute-done.2.refs_6_), channel_id=1, source_target_pairs={{0,1},{1,0},{2,3},{3,2},{4,5},{5,4},{6,7},{7,6},{8,9},{9,8},{10,11... | collective-permute-start | bytes 3145736 | tf_op jit(solution)/shard_map/ppermute | solution.py:390
  93.4 30.3 %collective-permute-start.12 = (bf16[4,128,1024]{2,1,0:T(8,128)(2,1)}, bf16[4,128,1024]{2,1,0:T(8,128)(2,1)}, u32[]{:S(2)}, u32[]{:S(2)}) collective-permute-start(bf16[4,128,1024]{2,1,0:T(8,128)(2,1)} %collective-permute-done.7.refs_8_), channel_id=1, source_target_pairs={{0,1},{1,0},{2,3},{3,2},{4,5},{5,4},{6,7},{7,6},{8,9},{9,8},{10,11... | collective-permute-start | bytes 3145736 | tf_op jit(solution)/shard_map/ppermute | solution.py:390
  93.9 29.8 %collective-permute-start.9 = (bf16[4,128,1024]{2,1,0:T(8,128)(2,1)}, bf16[4,128,1024]{2,1,0:T(8,128)(2,1)}, u32[]{:S(2)}, u32[]{:S(2)}) collective-permute-start(bf16[4,128,1024]{2,1,0:T(8,128)(2,1)} %broadcast_select_fusion.refs_4_), channel_id=1, source_target_pairs={{0,2},{1,3},{2,0},{3,1},{4,6},{5,7},{6,4},{7,5},{8,10},{9,11},{10,... | collective-permute-start | bytes 3145736 | tf_op jit(solution)/shard_map/ppermute | solution.py:390
  99.1 83.8 %collective-permute-start.18 = (bf16[60,128,128]{2,1,0:T(8,128)(2,1)}, bf16[60,128,128]{2,1,0:T(8,128)(2,1)}, u32[]{:S(2)}, u32[]{:S(2)}) collective-permute-start(bf16[60,128,128]{2,1,0:T(8,128)(2,1)} %copy-done.7), channel_id=1, source_target_pairs={{4,12},{5,13},{6,14},{7,15},{8,0},{9,1},{10,2},{11,3},{20,28},{21,... | collective-permute-start | bytes 5898248 | tf_op jit(solution)/shard_map/ppermute | solution.py:390
  116.2 34.7 %collective-permute-start.15 = (bf16[32,128,128]{2,1,0:T(8,128)(2,1)}, bf16[32,128,128]{2,1,0:T(8,128)(2,1)}, u32[]{:S(2)}, u32[]{:S(2)}) collective-permute-start(bf16[32,128,128]{2,1,0:T(8,128)(2,1)} %copy-done.8), channel_id=1, source_target_pairs={{0,8},{1,9},{2,10},{3,11},{12,4},{13,5},{14,6},{15,7},{16,24},{17,... | collective-permute-start | bytes 3145736 | tf_op jit(solution)/shard_map/ppermute | solution.py:390
  123.6 26.5 %collective-permute-start.13 = (bf16[2,128,1024]{2,1,0:T(8,128)(2,1)}, bf16[2,128,1024]{2,1,0:T(8,128)(2,1)S(1)}, u32[]{:S(2)}, u32[]{:S(2)}) collective-permute-start(bf16[2,128,1024]{2,1,0:T(8,128)(2,1)} %get-tuple-element.146.refs_1_), channel_id=1, source_target_pairs={{0,2},{1,3},{2,0},{3,1},{4,6},{5,7},{6,4},{7,5},{8,10},{9,11},{10,... | collective-permute-start | bytes 1572872 | tf_op jit(solution)/shard_map/ppermute | solution.py:390
  124.3 25.8 %collective-permute-start.14 = (bf16[2,128,1024]{2,1,0:T(8,128)(2,1)}, bf16[2,128,1024]{2,1,0:T(8,128)(2,1)S(1)}, u32[]{:S(2)}, u32[]{:S(2)}) collective-permute-start(bf16[2,128,1024]{2,1,0:T(8,128)(2,1)} %get-tuple-element.147.refs_2_), channel_id=1, source_target_pairs={{0,2},{1,3},{2,0},{3,1},{4,6},{5,7},{6,4},{7,5},{8,10},{9,11},{10,... | collective-permute-start | bytes 1572872 | tf_op jit(solution)/shard_map/ppermute | solution.py:390
  150.1 4.6 %copy-start.10 = (bf16[2,128,1024]{2,1,0:T(8,128)(2,1)}, bf16[2,128,1024]{2,1,0:T(8,128)(2,1)S(1)}, u32[]{:S(2)}) copy-start(bf16[2,128,1024]{2,1,0:T(8,128)(2,1)S(1)} %collective-permute-done.13.refs_5_) | copy-start | bytes 1572868
  150.2 1.1 copy-start.11
  150.2 2.2 %collective-permute-start.20 = (bf16[2,128,1024]{2,1,0:T(8,128)(2,1)}, bf16[2,128,1024]{2,1,0:T(8,128)(2,1)S(1)}, u32[]{:S(2)}, u32[]{:S(2)}) collective-permute-start(bf16[2,128,1024]{2,1,0:T(8,128)(2,1)} %get-tuple-element.146.refs_1_), channel_id=1, source_target_pairs={{0,1},{1,0},{2,3},{3,2},{4,5},{5,4},{6,7},{7,6},{8,9},{9,8},{10,11... | collective-permute-start | bytes 1572872 | tf_op jit(solution)/shard_map/ppermute | solution.py:390
  150.2 4.4 %collective-permute-start.21 = (bf16[2,128,1024]{2,1,0:T(8,128)(2,1)}, bf16[2,128,1024]{2,1,0:T(8,128)(2,1)S(1)}, u32[]{:S(2)}, u32[]{:S(2)}) collective-permute-start(bf16[2,128,1024]{2,1,0:T(8,128)(2,1)} %get-tuple-element.147.refs_2_), channel_id=1, source_target_pairs={{0,1},{1,0},{2,3},{3,2},{4,5},{5,4},{6,7},{7,6},{8,9},{9,8},{10,11... | collective-permute-start | bytes 1572872 | tf_op jit(solution)/shard_map/ppermute | solution.py:390
  150.7 7.4 %collective-permute-start.19 = (bf16[4,128,1024]{2,1,0:T(8,128)(2,1)}, bf16[4,128,1024]{2,1,0:T(8,128)(2,1)}, u32[]{:S(2)}, u32[]{:S(2)}) collective-permute-start(bf16[4,128,1024]{2,1,0:T(8,128)(2,1)} %collective-permute-done.9.refs_10_), channel_id=1, source_target_pairs={{0,1},{1,0},{2,3},{3,2},{4,5},{5,4},{6,7},{7,6},{8,9},{9,8},{10,11... | collective-permute-start | bytes 3145736 | tf_op jit(solution)/shard_map/ppermute | solution.py:390
  150.8 3.9 %collective-permute-start.22 = (bf16[2,128,1024]{2,1,0:T(8,128)(2,1)S(1)}, bf16[2,128,1024]{2,1,0:T(8,128)(2,1)S(1)}, u32[]{:S(2)}, u32[]{:S(2)}) collective-permute-start(bf16[2,128,1024]{2,1,0:T(8,128)(2,1)S(1)} %collective-permute-done.13.refs_5_), channel_id=1, source_target_pairs={{0,1},{1,0},{2,3},{3,2},{4,5},{5,4},{6,7},{7,6},{8,9},{9,8},{10,11... | collective-permute-start | bytes 1572872 | tf_op jit(solution)/shard_map/ppermute | solution.py:390
  152.3 2.4 %copy-start.12 = (bf16[2,128,1024]{2,1,0:T(8,128)(2,1)}, bf16[2,128,1024]{2,1,0:T(8,128)(2,1)S(1)}, u32[]{:S(2)}) copy-start(bf16[2,128,1024]{2,1,0:T(8,128)(2,1)S(1)} %collective-permute-done.20.refs_3_) | copy-start | bytes 1572868
  152.3 47.2 %collective-permute-start.17 = (bf16[24,128,128]{2,1,0:T(8,128)(2,1)}, bf16[24,128,128]{2,1,0:T(8,128)(2,1)S(1)}, u32[]{:S(2)}, u32[]{:S(2)}) collective-permute-start(bf16[24,128,128]{2,1,0:T(8,128)(2,1)} %get-tuple-element.143), channel_id=1, source_target_pairs={{4,12},{5,13},{6,14},{7,15},{8,0},{9,1},{10,2},{11,3},{20,28},{21,... | collective-permute-start | bytes 2359304 | tf_op jit(solution)/shard_map/ppermute | solution.py:390
  154.6 0.8 copy-start.13
  154.6 3.5 %collective-permute-start.23 = (bf16[2,128,1024]{2,1,0:T(8,128)(2,1)}, bf16[2,128,1024]{2,1,0:T(8,128)(2,1)}, u32[]{:S(2)}, u32[]{:S(2)}) collective-permute-start(bf16[2,128,1024]{2,1,0:T(8,128)(2,1)} %copy-done.11), channel_id=1, source_target_pairs={{0,1},{1,0},{2,3},{3,2},{4,5},{5,4},{6,7},{7,6},{8,9},{9,8},{10,11... | collective-permute-start | bytes 1572872 | tf_op jit(solution)/shard_map/ppermute | solution.py:390
  155.4 0.8 copy-start.14
  156.2 51.8 %collective-permute-start.16 = (bf16[12,128,128]{2,1,0:T(8,128)(2,1)}, bf16[12,128,128]{2,1,0:T(8,128)(2,1)S(1)}, u32[]{:S(2)}, u32[]{:S(2)}) collective-permute-start(bf16[12,128,128]{2,1,0:T(8,128)(2,1)} %get-tuple-element.142), channel_id=1, source_target_pairs={{4,12},{5,13},{6,14},{7,15},{8,0},{9,1},{10,2},{11,3},{20,28},{21,... | collective-permute-start | bytes 1179656 | tf_op jit(solution)/shard_map/ppermute | solution.py:390
  158.1 24.7 %copy-start.4 = (s32[17]{0:T(128)S(1)}, s32[17]{0:T(128)}, u32[]{:S(2)}) copy-start(s32[17]{0:T(128)} %get-tuple-element.118.starts) | copy-start | bytes 208
  158.1 24.7 %copy-start.5 = (s32[96]{0:T(128)S(1)}, s32[96]{0:T(128)}, u32[]{:S(2)}) copy-start(s32[96]{0:T(128)} %get-tuple-element.119.block_at) | copy-start | bytes 1156
  182.8 3.4 %copy-start = (f32[16,128,1024]{2,1,0:T(8,128)S(1)}, f32[16,128,1024]{2,1,0:T(8,128)}, u32[]{:S(2)}) copy-start(f32[16,128,1024]{2,1,0:T(8,128)} %get-tuple-element.152.refs_3_) | copy-start | bytes 25165828

commit v13 on v12

--- a/solution.py
+++ b/solution.py
@@ -13,6 +13,7 @@
 SHARES = (30, 12)
 COLUMNS = 256
 MIB = 1024 * 1024
+FAR_COST = 10**10
 SMEM = pl.BlockSpec(memory_space=pltpu.SMEM)
 VMEM = pl.BlockSpec(memory_space=pltpu.VMEM)
 ANY = pl.BlockSpec(memory_space=pl.ANY)
@@ -63,7 +64,7 @@
         block_at[position] = slots[cols[tile]]
 
 
-def tables(rows, cols, total, groups=PPD):
+def tables(rows, cols, total, groups=PPD, cost=0):
     count = rows.shape[0]
     return pl.pallas_call(
         tables_kernel,
@@ -71,6 +72,7 @@
         out_specs=[SMEM] * 4,
         out_shape=[jax.ShapeDtypeStruct((size,), jnp.int32) for size in (groups + 1, count, count, total)],
         scratch_shapes=[pltpu.SMEM((groups,), jnp.int32)],
+        cost_estimate=pl.CostEstimate(flops=cost, bytes_accessed=0, transcendentals=0) if cost else None,
         name="tables",
     )(rows, cols)
 
@@ -402,7 +404,7 @@
     from_ends = [(i, i ^ 8) for i in range(16) if i not in centre]
     from_centre = [(i, i ^ 8) for i in centre]
     around = [(i, i ^ 4) for i in centre] + from_ends
-    other_z, other_y, other_core = (flipped_bit(bit) for bit in (4, 2, 1))
+    other_z, other_y, other_core, opposite = (flipped_bit(bit) for bit in (4, 2, 1, 8))
     me = lax.axis_index("tile")
     z = me // 4
     in_centre = (z == 1) | (z == 2)
@@ -421,7 +423,7 @@
 
     near = send(shard, other_z)
     first = send(shard, across)
-    notes = lax.all_gather(jnp.stack([rows, cols]), "tile")
+    notes = send(jnp.stack([rows, cols]), opposite)
     order = tables(rows, cols, block_total)[1]
     c_own = send(shard, other_core)
     y_own = send(shard, other_y)
@@ -439,16 +441,17 @@
     y_near = send(near, other_y)
     c_near = send(near, other_core)
     own_tables = tables(keys, cols, block_total, 2 * PPD)
+    far_tables = tables(notes[0], notes[1], block_total, cost=FAR_COST)
     perm = flip_matrix(W)
     far_ends = [outer]
     first = jnp.where(in_centre, first, outer)
     second, tiles_next = together(second, parts[1])
     second = payload_of(at_end, tiles_next, second)
     outer = send(second, around)
-    first, y_own, y_near, c_near, perm, notes, *rest = together(
-        first, y_own, y_near, c_near, perm, notes, *parts[2:], *own_tables
+    first, y_own, y_near, c_near, perm, *rest = together(
+        first, y_own, y_near, c_near, perm, *parts[2:], *own_tables, *far_tables
     )
-    parts, own_tables = rest[:4], rest[4:]
+    parts, own_tables, far_tables = rest[:4], rest[4:8], rest[8:]
     y_first = send(first, other_y)
     c_first = send(first, other_core)
     c_y_own = send(y_own, other_core)
@@ -457,11 +460,7 @@
     far_ends += [outer, send(tiles_last, from_ends)]
     halves = (slice(0, local // 2), slice(local // 2, None))
     second = [jnp.where(in_centre, second[half], outer[half]) for half in halves]
-    notes = lax.dynamic_index_in_dim(notes, me ^ 8, keepdims=False)
-    far_tables = tables(notes[0], notes[1], block_total)
-    second[0], second[1], y_first, c_first, c_y_own, c_y_near, *far_tables = together(
-        *second, y_first, c_first, c_y_own, c_y_near, *far_tables
-    )
+    *second, y_first, c_first, c_y_own, c_y_near = together(*second, y_first, c_first, c_y_own, c_y_near)
 
     far_centre = [send(parts[1], from_centre)]
     y_second = [send(half, other_y) for half in second]

time: 213 us -> 202 us (0.948)
  blocking collectives: 30.7 us -> 0 us
  waiting for transfers between devices: 31.8 us -> 56.4 us
  starting transfers between devices: 55.9 us -> 48.8 us
  local copies, waits for them, and re-layouts: 10.1 us -> 12.6 us
    all_gather x1 -> x0, blocking collectives: 30.7 us -> none  [staged_part(): notes = lax.all_gather(jnp.stack([rows, cols]), 'tile')]
    ppermute x24 -> x25, waiting for transfers between devices: 31.8 us -> 56.4 us  [send(): return lax.ppermute(value, 'tile', pairs)]
    ppermute x24 -> x25, starting transfers between devices: 55.9 us -> 48.8 us  [send(): return lax.ppermute(value, 'tile', pairs)]
    unnamed x36 -> x34, local copies, waits for them, and re-layouts: 8.31 us -> 10.8 us
  transfers between devices with their start and end apart: 24 -> 25, of which waited for: 7 -> 8; matrix products, arithmetic and copies ran while one was open for 3% -> 3% of each run, Pallas kernels for 35% -> 36%
where the time goes in v13:
time: 202 us
  Pallas kernels  78.4 us (39%)
  waiting for transfers between devices  56.4 us (28%)
  starting transfers between devices  48.8 us (24%)
  local copies, waits for them, and re-layouts  12.6 us (6%)
  other arithmetic  5.28 us (3%)
    ppermute x25, waiting for transfers between devices, send(): return lax.ppermute(value, 'tile', pairs)  56.4 us
    ppermute x25, starting transfers between devices, send(): return lax.ppermute(value, 'tile', pairs)  48.8 us
    pallas_call x2, Pallas kernels, own_part(): pl.pallas_call(functools.partial(own_kernel, counts, group, not earlier),...  37.4 us
    pallas_call x3, Pallas kernels, far_part(): pl.pallas_call(functools.partial(far_kernel, base, [segment for segment,...  23.5 us
    pallas_call x3, Pallas kernels, tables(): pl.pallas_call(tables_kernel, in_specs=[SMEM] * 2, out_specs=[SMEM] * 4,...  12.1 us
    unnamed x34, local copies, waits for them, and re-layouts  10.8 us
    pallas_call x1, Pallas kernels, sort_tiles(): pl.pallas_call(functools.partial(sort_kernel, choices), in_specs=[SMEM] *...  5.31 us
  transfers between devices with their start and end apart: 25, of which 8 were waited for; matrix products, arithmetic and copies ran while one was open for 3% of the time, Pallas kernels for 36%

profile of v13, /device:TPU:0, one launch (start us, length us, event | category | flops | bytes accessed | tf_op | source)
XLA Modules:
  0.0 201.9 jit_solution(12998914741545616674)
XLA Ops:
  0.0 0.7 collective-permute-start
  0.7 0.5 collective-permute-start.3
  1.2 5.4 %collective-permute-start.2 = (bf16[4,128,1024]{2,1,0:T(8,128)(2,1)}, bf16[4,128,1024]{2,1,0:T(8,128)(2,1)}, u32[]{:S(2)}, u32[]{:S(2)}) collective-permute-start(bf16[4,128,1024]{2,1,0:T(8,128)(2,1)} %refs_0_.1), channel_id=1, source_target_pairs={{0,4},{1,5},{2,6},{3,7},{4,0},{5,1},{6,2},{7,3},{8,12},{9,13},{10,... | collective-permute-start | bytes 3145736 | tf_op jit(solution)/shard_map/ppermute | solution.py:392
  6.7 1.5 collective-permute-start.4
  8.2 0.7 pad_add_fusion
  8.9 4.0 %tables.3 = (s32[17]{0:T(128)}, s32[96]{0:T(128)}, s32[96]{0:T(128)}, s32[64]{0:T(128)}) custom-call(s32[96]{0:T(128)} %rows.1, s32[96]{0:T(128)} %cols.3), custom_call_target="tpu_custom_call" | custom-call | tf_op jit(solution)/shard_map/tables/pallas_call | solution.py:69
  12.9 1.2 fusion.10.rows
  14.1 4.0 %tables.4 = (s32[33]{0:T(128)}, s32[96]{0:T(128)}, s32[96]{0:T(128)}, s32[64]{0:T(128)}) custom-call(s32[96]{0:T(128)} %fusion.10.rows, s32[96]{0:T(128)} %cols.3), custom_call_target="tpu_custom_call" | custom-call | tf_op jit(solution)/shard_map/tables/pallas_call | solution.py:69
  18.2 2.2 %fusion.perm_ref = bf16[1024,1024]{1,0:T(8,128)(2,1)} fusion(s32[1024]{0:T(1024)S(1)} %fusion.7), kind=kLoop, calls=%fused_computation.1 | loop fusion | flops 2097152 | bytes 2101248 | tf_op jit(solution)/shard_map/convert_element_type | solution.py:25
  20.4 1.9 copy-done.1
  22.3 0.6 copy-done.6
  22.9 5.3 %sort_tiles.1 = (bf16[4,128,1024]{2,1,0:T(8,128)(2,1)S(1)}, bf16[4,128,1024]{2,1,0:T(8,128)(2,1)S(1)}, bf16[32,128,128]{2,1,0:T(8,128)(2,1)}, bf16[60,128,128]{2...) custom-call(s32[96]{0:T(128)S(1)} %copy-done.6, s32[1]{0:T(128)} %bitcast.chosen.at_end, ...), custom_call_target="tpu_custom_call" | custom-call | tf_op jit(solution)/shard_map/sort_tiles/pallas_call | solution.py:110
  28.3 0.1 payload.2
  28.4 5.1 %collective-permute-start.1 = (bf16[4,128,1024]{2,1,0:T(8,128)(2,1)S(1)}, bf16[4,128,1024]{2,1,0:T(8,128)(2,1)S(1)}, u32[]{:S(2)}, u32[]{:S(2)}) collective-permute-start(bf16[4,128,1024]{2,1,0:T(8,128)(2,1)S(1)} %payload.2), channel_id=1, source_target_pairs={{4,0},{5,1},{6,2},{7,3},{8,12},{9,13},{10,14},{11,15},{0,8},{1,9},... | collective-permute-start | bytes 3145736 | tf_op jit(solution)/shard_map/ppermute | solution.py:392
  33.4 0.5 slice_bitcast_fusion
  34.0 1.0 copy-done.8
  35.0 0.7 collective-permute-start.8
  35.7 0.1 collective-permute-start.6
  35.8 0.6 collective-permute-start.5
  36.4 4.0 %tables.5 = (s32[17]{0:T(128)}, s32[96]{0:T(128)}, s32[96]{0:T(128)}, s32[64]{0:T(128)}) custom-call(s32[96]{0:T(128)} %get-tuple-element.160.rows, s32[96]{0:T(128)} %get-tuple-element.159.cols), custom_call_target="tpu_custom_call" | custom-call | flops 10000000000 | tf_op jit(solution)/shard_map/tables/pallas_call | solution.py:69
  40.4 15.3 %collective-permute-done.1.refs_0_ = bf16[4,128,1024]{2,1,0:T(8,128)(2,1)S(1)} collective-permute-done((bf16[4,128,1024]{2,1,0:T(8,128)(2,1)S(1)}, bf16[4,128,1024]{2,1,0:T(8,128)(2,1)S(1)}, u32[]{:S(2)}, u32[]{:S(2)}) %collective-permute-start.1) | collective-permute-done | bytes 1048608 | tf_op jit(solution)/shard_map/ppermute | solution.py:392
  55.7 0.1 broadcast_select_fusion.refs_4_
  55.8 5.9 %collective-permute-done.5.refs_8_ = bf16[4,128,1024]{2,1,0:T(8,128)(2,1)} collective-permute-done((bf16[4,128,1024]{2,1,0:T(8,128)(2,1)}, bf16[4,128,1024]{2,1,0:T(8,128)(2,1)}, u32[]{:S(2)}, u32[]{:S(2)}) %collective-permute-start.5) | collective-permute-done | bytes 1048608 | tf_op jit(solution)/shard_map/ppermute | solution.py:392
  61.7 1.2 copy-done.3
  62.9 0.1 payload.3
  63.0 19.8 %collective-permute-start.9 = (bf16[4,128,1024]{2,1,0:T(8,128)(2,1)S(1)}, bf16[4,128,1024]{2,1,0:T(8,128)(2,1)S(1)}, u32[]{:S(2)}, u32[]{:S(2)}) collective-permute-start(bf16[4,128,1024]{2,1,0:T(8,128)(2,1)S(1)} %payload.3), channel_id=1, source_target_pairs={{4,0},{5,1},{6,2},{7,3},{8,12},{9,13},{10,14},{11,15},{0,8},{1,9},... | collective-permute-start | bytes 3145736 | tf_op jit(solution)/shard_map/ppermute | solution.py:392
  82.8 0.5 collective-permute-start.13
  83.3 0.5 collective-permute-start.10
  83.8 0.0 collective-permute-done.11.refs_5_
  83.8 1.3 collective-permute-start.19
  85.1 20.3 %collective-permute-done.9.refs_1_.refs_0_ = bf16[4,128,1024]{2,1,0:T(8,128)(2,1)S(1)} collective-permute-done((bf16[4,128,1024]{2,1,0:T(8,128)(2,1)S(1)}, bf16[4,128,1024]{2,1,0:T(8,128)(2,1)S(1)}, u32[]{:S(2)}, u32[]{:S(2)}) %collective-permute-start.9) | collective-permute-done | bytes 1048608 | tf_op jit(solution)/shard_map/ppermute | solution.py:392
  105.4 6.4 %collective-permute-start.16 = (bf16[32,128,128]{2,1,0:T(8,128)(2,1)}, bf16[32,128,128]{2,1,0:T(8,128)(2,1)}, u32[]{:S(2)}, u32[]{:S(2)}) collective-permute-start(bf16[32,128,128]{2,1,0:T(8,128)(2,1)} %get-tuple-element.138), channel_id=1, source_target_pairs={{0,8},{1,9},{2,10},{3,11},{12,4},{13,5},{14,6},{15,7},{16,24},{17,... | collective-permute-start | bytes 3145736 | tf_op jit(solution)/shard_map/ppermute | solution.py:392
  111.8 1.1 slice_select_fusion
  112.9 0.0 collective-permute-done.13.refs_9_
  112.9 1.0 copy-done.10
  113.9 0.3 copy-done.11
  114.2 0.5 collective-permute-start.14
  114.7 1.5 collective-permute-start.15
  116.2 0.6 stack.89.firsts
  116.8 23.1 %own_part.2 = (f32[16,128,1024]{2,1,0:T(8,128)}, bf16[32,128,1024]{2,1,0:T(8,128)(2,1)}) custom-call(s32[33]{0:T(128)} %get-tuple-element.121.starts, s32[96]{0:T(128)} %get-tuple-element.122.tile_at, s32[96]{0:T(128)} %get-tuple-element.123.block_at, s32[64]{0:T(128)} %get-tuple-element.124.own_slots, s32[64]{0:T(128)} %get-tuple-element.125.far_slots, ...), custom_call_target="tpu_custom_call" | custom-call | tf_op jit(solution)/shard_map/own_part/pallas_call | solution.py:246
  140.0 0.0 collective-permute-done.15.refs_6_
  140.0 0.1 collective-permute-start.21
  140.1 0.5 collective-permute-start.22
  140.6 0.1 collective-permute-start.20
  140.7 0.0 collective-permute-done.16.refs_1_.refs_0_
  140.7 0.4 collective-permute-start.23
  141.1 1.1 collective-permute-done.21.refs_3_
  142.2 1.3 collective-permute-start.18
  143.5 1.0 collective-permute-done.22.refs_4_
  144.5 0.1 collective-permute-start.24
  144.6 0.0 collective-permute-done.23.refs_7_
  144.6 0.6 copy-done.15
  145.2 0.8 copy-done.16
  146.0 1.3 collective-permute-start.17
  147.3 0.6 stack.99.firsts
  148.0 0.0 collective-permute-done.24.refs_8_
  148.0 14.2 %own_part.3 = (f32[16,128,1024]{2,1,0:T(8,128)}, bf16[32,128,1024]{2,1,0:T(8,128)(2,1)}) custom-call(s32[33]{0:T(128)} %get-tuple-element.121.starts, s32[96]{0:T(128)} %get-tuple-element.122.tile_at, s32[96]{0:T(128)} %get-tuple-element.123.block_at, s32[64]{0:T(128)} %get-tuple-element.124.own_slots, ...), custom_call_target="tpu_custom_call", output_to_operand_aliasing={{0}: (17, {}), {1}: (18, {})} | custom-call | tf_op jit(solution)/shard_map/own_part/pallas_call | solution.py:246
  162.2 9.8 %collective-permute-done.19.refs_2_ = bf16[60,128,128]{2,1,0:T(8,128)(2,1)} collective-permute-done((bf16[60,128,128]{2,1,0:T(8,128)(2,1)}, bf16[60,128,128]{2,1,0:T(8,128)(2,1)}, u32[]{:S(2)}, u32[]{:S(2)}) %collective-permute-start.19) | collective-permute-done | bytes 1966112 | tf_op jit(solution)/shard_map/ppermute | solution.py:392
  172.0 3.4 %copy-done = f32[16,128,1024]{2,1,0:T(8,128)S(1)} copy-done((f32[16,128,1024]{2,1,0:T(8,128)S(1)}, f32[16,128,1024]{2,1,0:T(8,128)}, u32[]{:S(2)}) %copy-start) | copy-done | bytes 8388632
  175.4 12.2 %far_part.3 = (f32[16,128,1024]{2,1,0:T(8,128)S(1)}, bf16[16,128,1024]{2,1,0:T(8,128)(2,1)}) custom-call(s32[17]{0:T(128)S(1)} %copy-done.4, s32[96]{0:T(128)S(1)} %copy-done.5, s32[1]{0:T(128)} %bitcast.chosen.at_end, bf16[4,128,1024]{2,1,0:T(8,128)(2,1)S(1)} %collective-permute-done.1.refs_0_, ...), custom_call_target="tpu_custom_call", output_to_operand_aliasing={{0}: (6, {})} | custom-call | tf_op jit(solution)/shard_map/far_part/pallas_call | solution.py:366
  187.5 1.2 collective-permute-done.18.refs_2_
  188.7 6.5 %far_part.4 = (f32[16,128,1024]{2,1,0:T(8,128)S(1)}, bf16[16,128,1024]{2,1,0:T(8,128)(2,1)}) custom-call(s32[17]{0:T(128)S(1)} %copy-done.4, s32[96]{0:T(128)S(1)} %copy-done.5, s32[1]{0:T(128)} %bitcast.chosen.at_end, bf16[4,128,1024]{2,1,0:T(8,128)(2,1)S(1)} %collective-permute-done.9.refs_1_.refs_0_, ...), custom_call_target="tpu_custom_call", output_to_operand_aliasing={{0}: (6, {}), {1}: (8, {})} | custom-call | tf_op jit(solution)/shard_map/far_part/pallas_call | solution.py:366
  195.3 1.8 collective-permute-done.17.refs_1_
  197.1 4.8 %far_part.5 = (f32[16,128,1024]{2,1,0:T(8,128)S(1)}, bf16[16,128,1024]{2,1,0:T(8,128)(2,1)}) custom-call(s32[17]{0:T(128)S(1)} %copy-done.4, s32[96]{0:T(128)S(1)} %copy-done.5, s32[1]{0:T(128)} %bitcast.chosen.at_end, bf16[32,128,128]{2,1,0:T(8,128)(2,1)} %collective-permute-done.16.refs_1_.refs_0_, ...), custom_call_target="tpu_custom_call", output_to_operand_aliasing={{0}: (5, {}), {1}: (7, {})} | custom-call | tf_op jit(solution)/shard_map/far_part/pallas_call | solution.py:366
  (40 shorter events, 0.1 us)
Async XLA Ops:
  0.0 28.3 %collective-permute-start = (bf16[4,128,1024]{2,1,0:T(8,128)(2,1)}, bf16[4,128,1024]{2,1,0:T(8,128)(2,1)S(1)}, u32[]{:S(2)}, u32[]{:S(2)}) collective-permute-start(bf16[4,128,1024]{2,1,0:T(8,128)(2,1)} %refs_0_.1), channel_id=1, source_target_pairs={{4,8},{5,9},{6,10},{7,11},{8,4},{9,5},{10,6},{11,7},{20,24},{21,25... | collective-permute-start | bytes 3145736 | tf_op jit(solution)/shard_map/ppermute | solution.py:392
  0.7 33.3 %collective-permute-start.3 = (bf16[4,128,1024]{2,1,0:T(8,128)(2,1)}, bf16[4,128,1024]{2,1,0:T(8,128)(2,1)S(1)}, u32[]{:S(2)}, u32[]{:S(2)}) collective-permute-start(bf16[4,128,1024]{2,1,0:T(8,128)(2,1)} %refs_0_.1), channel_id=1, source_target_pairs={{0,1},{1,0},{2,3},{3,2},{4,5},{5,4},{6,7},{7,6},{8,9},{9,8},{10,11... | collective-permute-start | bytes 3145736 | tf_op jit(solution)/shard_map/ppermute | solution.py:392
  1.2 32.8 %collective-permute-start.2 = (bf16[4,128,1024]{2,1,0:T(8,128)(2,1)}, bf16[4,128,1024]{2,1,0:T(8,128)(2,1)}, u32[]{:S(2)}, u32[]{:S(2)}) collective-permute-start(bf16[4,128,1024]{2,1,0:T(8,128)(2,1)} %refs_0_.1), channel_id=1, source_target_pairs={{0,4},{1,5},{2,6},{3,7},{4,0},{5,1},{6,2},{7,3},{8,12},{9,13},{10,... | collective-permute-start | bytes 3145736 | tf_op jit(solution)/shard_map/ppermute | solution.py:392
  6.7 28.3 %collective-permute-start.4 = (bf16[4,128,1024]{2,1,0:T(8,128)(2,1)}, bf16[4,128,1024]{2,1,0:T(8,128)(2,1)}, u32[]{:S(2)}, u32[]{:S(2)}) collective-permute-start(bf16[4,128,1024]{2,1,0:T(8,128)(2,1)} %refs_0_.1), channel_id=1, source_target_pairs={{0,2},{1,3},{2,0},{3,1},{4,6},{5,7},{6,4},{7,5},{8,10},{9,11},{10,... | collective-permute-start | bytes 3145736 | tf_op jit(solution)/shard_map/ppermute | solution.py:392
  8.9 24.6 %collective-permute-start.7 = (s32[2,96]{1,0:T(2,128)S(1)}, s32[2,96]{1,0:T(2,128)S(1)}, u32[]{:S(2)}, u32[]{:S(2)}) collective-permute-start(s32[2,96]{1,0:T(2,128)S(1)} %pad_add_fusion), channel_id=1, source_target_pairs={{0,8},{1,9},{2,10},{3,11},{4,12},{5,13},{6,14},{7,15},{8,0},{9,1},... | collective-permute-start | bytes 2312 | tf_op jit(solution)/shard_map/ppermute | solution.py:392
  20.4 1.9 copy-start.1
  22.3 0.6 copy-start.6
  28.2 5.8 %copy-start.2 = (bf16[4,128,1024]{2,1,0:T(8,128)(2,1)}, bf16[4,128,1024]{2,1,0:T(8,128)(2,1)S(1)}, u32[]{:S(2)}) copy-start(bf16[4,128,1024]{2,1,0:T(8,128)(2,1)S(1)} %get-tuple-element.111.tiles_ref) | copy-start | bytes 3145732
  28.4 27.3 %collective-permute-start.1 = (bf16[4,128,1024]{2,1,0:T(8,128)(2,1)S(1)}, bf16[4,128,1024]{2,1,0:T(8,128)(2,1)S(1)}, u32[]{:S(2)}, u32[]{:S(2)}) collective-permute-start(bf16[4,128,1024]{2,1,0:T(8,128)(2,1)S(1)} %payload.2), channel_id=1, source_target_pairs={{4,0},{5,1},{6,2},{7,3},{8,12},{9,13},{10,14},{11,15},{0,8},{1,9},... | collective-permute-start | bytes 3145736 | tf_op jit(solution)/shard_map/ppermute | solution.py:392
  34.0 1.0 copy-start.8
  35.0 26.7 %collective-permute-start.8 = (bf16[4,128,1024]{2,1,0:T(8,128)(2,1)}, bf16[4,128,1024]{2,1,0:T(8,128)(2,1)S(1)}, u32[]{:S(2)}, u32[]{:S(2)}) collective-permute-start(bf16[4,128,1024]{2,1,0:T(8,128)(2,1)} %collective-permute-done.2.refs_2_), channel_id=1, source_target_pairs={{4,8},{5,9},{6,10},{7,11},{8,4},{9,5},{10,6},{11,7},{20,24},{21,25... | collective-permute-start | bytes 3145736 | tf_op jit(solution)/shard_map/ppermute | solution.py:392
  35.7 20.1 %collective-permute-start.6 = (bf16[4,128,1024]{2,1,0:T(8,128)(2,1)}, bf16[4,128,1024]{2,1,0:T(8,128)(2,1)}, u32[]{:S(2)}, u32[]{:S(2)}) collective-permute-start(bf16[4,128,1024]{2,1,0:T(8,128)(2,1)} %collective-permute-done.2.refs_2_), channel_id=1, source_target_pairs={{0,1},{1,0},{2,3},{3,2},{4,5},{5,4},{6,7},{7,6},{8,9},{9,8},{10,11... | collective-permute-start | bytes 3145736 | tf_op jit(solution)/shard_map/ppermute | solution.py:392
  35.8 25.9 %collective-permute-start.5 = (bf16[4,128,1024]{2,1,0:T(8,128)(2,1)}, bf16[4,128,1024]{2,1,0:T(8,128)(2,1)}, u32[]{:S(2)}, u32[]{:S(2)}) collective-permute-start(bf16[4,128,1024]{2,1,0:T(8,128)(2,1)} %collective-permute-done.2.refs_2_), channel_id=1, source_target_pairs={{0,2},{1,3},{2,0},{3,1},{4,6},{5,7},{6,4},{7,5},{8,10},{9,11},{10,... | collective-permute-start | bytes 3145736 | tf_op jit(solution)/shard_map/ppermute | solution.py:392
  55.8 57.1 %copy-start.7 = (bf16[4,128,1024]{2,1,0:T(8,128)(2,1)}, bf16[4,128,1024]{2,1,0:T(8,128)(2,1)S(1)}, u32[]{:S(2)}) copy-start(bf16[4,128,1024]{2,1,0:T(8,128)(2,1)S(1)} %broadcast_select_fusion.refs_4_) | copy-start | bytes 3145732
  61.7 22.1 %collective-permute-start.11 = (bf16[4,128,1024]{2,1,0:T(8,128)(2,1)S(1)}, bf16[4,128,1024]{2,1,0:T(8,128)(2,1)S(1)}, u32[]{:S(2)}, u32[]{:S(2)}) collective-permute-start(bf16[4,128,1024]{2,1,0:T(8,128)(2,1)S(1)} %broadcast_select_fusion.refs_4_), channel_id=1, source_target_pairs={{0,1},{1,0},{2,3},{3,2},{4,5},{5,4},{6,7},{7,6},{8,9},{9,8},{10,11... | collective-permute-start | bytes 3145736 | tf_op jit(solution)/shard_map/ppermute | solution.py:392
  61.7 1.2 copy-start.3
  63.0 42.4 %collective-permute-start.9 = (bf16[4,128,1024]{2,1,0:T(8,128)(2,1)S(1)}, bf16[4,128,1024]{2,1,0:T(8,128)(2,1)S(1)}, u32[]{:S(2)}, u32[]{:S(2)}) collective-permute-start(bf16[4,128,1024]{2,1,0:T(8,128)(2,1)S(1)} %payload.3), channel_id=1, source_target_pairs={{4,0},{5,1},{6,2},{7,3},{8,12},{9,13},{10,14},{11,15},{0,8},{1,9},... | collective-permute-start | bytes 3145736 | tf_op jit(solution)/shard_map/ppermute | solution.py:392
  82.8 30.1 %collective-permute-start.12 = (bf16[4,128,1024]{2,1,0:T(8,128)(2,1)}, bf16[4,128,1024]{2,1,0:T(8,128)(2,1)S(1)}, u32[]{:S(2)}, u32[]{:S(2)}) collective-permute-start(bf16[4,128,1024]{2,1,0:T(8,128)(2,1)} %collective-permute-done.4.refs_6_), channel_id=1, source_target_pairs={{0,1},{1,0},{2,3},{3,2},{4,5},{5,4},{6,7},{7,6},{8,9},{9,8},{10,11... | collective-permute-start | bytes 3145736 | tf_op jit(solution)/shard_map/ppermute | solution.py:392
  82.8 30.1 %collective-permute-start.13 = (bf16[4,128,1024]{2,1,0:T(8,128)(2,1)}, bf16[4,128,1024]{2,1,0:T(8,128)(2,1)S(1)}, u32[]{:S(2)}, u32[]{:S(2)}) collective-permute-start(bf16[4,128,1024]{2,1,0:T(8,128)(2,1)} %collective-permute-done.5.refs_8_), channel_id=1, source_target_pairs={{0,1},{1,0},{2,3},{3,2},{4,5},{5,4},{6,7},{7,6},{8,9},{9,8},{10,11... | collective-permute-start | bytes 3145736 | tf_op jit(solution)/shard_map/ppermute | solution.py:392
  83.3 29.6 %collective-permute-start.10 = (bf16[4,128,1024]{2,1,0:T(8,128)(2,1)S(1)}, bf16[4,128,1024]{2,1,0:T(8,128)(2,1)}, u32[]{:S(2)}, u32[]{:S(2)}) collective-permute-start(bf16[4,128,1024]{2,1,0:T(8,128)(2,1)S(1)} %broadcast_select_fusion.refs_4_), channel_id=1, source_target_pairs={{0,2},{1,3},{2,0},{3,1},{4,6},{5,7},{6,4},{7,5},{8,10},{9,11},{10,... | collective-permute-start | bytes 3145736 | tf_op jit(solution)/shard_map/ppermute | solution.py:392
  83.8 21.6 %copy-start.9 = (bf16[4,128,1024]{2,1,0:T(8,128)(2,1)}, bf16[4,128,1024]{2,1,0:T(8,128)(2,1)S(1)}, u32[]{:S(2)}) copy-start(bf16[4,128,1024]{2,1,0:T(8,128)(2,1)S(1)} %collective-permute-done.11.refs_5_) | copy-start | bytes 3145732
  83.8 88.2 %collective-permute-start.19 = (bf16[60,128,128]{2,1,0:T(8,128)(2,1)}, bf16[60,128,128]{2,1,0:T(8,128)(2,1)}, u32[]{:S(2)}, u32[]{:S(2)}) collective-permute-start(bf16[60,128,128]{2,1,0:T(8,128)(2,1)} %get-tuple-element.142), channel_id=1, source_target_pairs={{4,12},{5,13},{6,14},{7,15},{8,0},{9,1},{10,2},{11,3},{20,28},{21,... | collective-permute-start | bytes 5898248 | tf_op jit(solution)/shard_map/ppermute | solution.py:392
  105.4 35.3 %collective-permute-start.16 = (bf16[32,128,128]{2,1,0:T(8,128)(2,1)}, bf16[32,128,128]{2,1,0:T(8,128)(2,1)}, u32[]{:S(2)}, u32[]{:S(2)}) collective-permute-start(bf16[32,128,128]{2,1,0:T(8,128)(2,1)} %get-tuple-element.138), channel_id=1, source_target_pairs={{0,8},{1,9},{2,10},{3,11},{12,4},{13,5},{14,6},{15,7},{16,24},{17,... | collective-permute-start | bytes 3145736 | tf_op jit(solution)/shard_map/ppermute | solution.py:392
  112.9 1.0 copy-start.10
  112.9 1.3 copy-start.11
  114.2 25.8 %collective-permute-start.14 = (bf16[2,128,1024]{2,1,0:T(8,128)(2,1)}, bf16[2,128,1024]{2,1,0:T(8,128)(2,1)S(1)}, u32[]{:S(2)}, u32[]{:S(2)}) collective-permute-start(bf16[2,128,1024]{2,1,0:T(8,128)(2,1)} %get-tuple-element.144.refs_1_), channel_id=1, source_target_pairs={{0,2},{1,3},{2,0},{3,1},{4,6},{5,7},{6,4},{7,5},{8,10},{9,11},{10,... | collective-permute-start | bytes 1572872 | tf_op jit(solution)/shard_map/ppermute | solution.py:392
  114.7 25.3 %collective-permute-start.15 = (bf16[2,128,1024]{2,1,0:T(8,128)(2,1)}, bf16[2,128,1024]{2,1,0:T(8,128)(2,1)S(1)}, u32[]{:S(2)}, u32[]{:S(2)}) collective-permute-start(bf16[2,128,1024]{2,1,0:T(8,128)(2,1)} %get-tuple-element.145.refs_2_), channel_id=1, source_target_pairs={{0,2},{1,3},{2,0},{3,1},{4,6},{5,7},{6,4},{7,5},{8,10},{9,11},{10,... | collective-permute-start | bytes 1572872 | tf_op jit(solution)/shard_map/ppermute | solution.py:392
  140.0 4.6 %copy-start.12 = (bf16[2,128,1024]{2,1,0:T(8,128)(2,1)}, bf16[2,128,1024]{2,1,0:T(8,128)(2,1)S(1)}, u32[]{:S(2)}) copy-start(bf16[2,128,1024]{2,1,0:T(8,128)(2,1)S(1)} %collective-permute-done.14.refs_5_) | copy-start | bytes 1572868
  140.0 1.1 copy-start.13
  140.0 2.2 %collective-permute-start.21 = (bf16[2,128,1024]{2,1,0:T(8,128)(2,1)}, bf16[2,128,1024]{2,1,0:T(8,128)(2,1)S(1)}, u32[]{:S(2)}, u32[]{:S(2)}) collective-permute-start(bf16[2,128,1024]{2,1,0:T(8,128)(2,1)} %get-tuple-element.144.refs_1_), channel_id=1, source_target_pairs={{0,1},{1,0},{2,3},{3,2},{4,5},{5,4},{6,7},{7,6},{8,9},{9,8},{10,11... | collective-permute-start | bytes 1572872 | tf_op jit(solution)/shard_map/ppermute | solution.py:392
  140.1 4.4 %collective-permute-start.22 = (bf16[2,128,1024]{2,1,0:T(8,128)(2,1)}, bf16[2,128,1024]{2,1,0:T(8,128)(2,1)S(1)}, u32[]{:S(2)}, u32[]{:S(2)}) collective-permute-start(bf16[2,128,1024]{2,1,0:T(8,128)(2,1)} %get-tuple-element.145.refs_2_), channel_id=1, source_target_pairs={{0,1},{1,0},{2,3},{3,2},{4,5},{5,4},{6,7},{7,6},{8,9},{9,8},{10,11... | collective-permute-start | bytes 1572872 | tf_op jit(solution)/shard_map/ppermute | solution.py:392
  140.6 7.4 %collective-permute-start.20 = (bf16[4,128,1024]{2,1,0:T(8,128)(2,1)}, bf16[4,128,1024]{2,1,0:T(8,128)(2,1)}, u32[]{:S(2)}, u32[]{:S(2)}) collective-permute-start(bf16[4,128,1024]{2,1,0:T(8,128)(2,1)} %collective-permute-done.10.refs_10_), channel_id=1, source_target_pairs={{0,1},{1,0},{2,3},{3,2},{4,5},{5,4},{6,7},{7,6},{8,9},{9,8},{10,11... | collective-permute-start | bytes 3145736 | tf_op jit(solution)/shard_map/ppermute | solution.py:392
  140.7 3.9 %collective-permute-start.23 = (bf16[2,128,1024]{2,1,0:T(8,128)(2,1)S(1)}, bf16[2,128,1024]{2,1,0:T(8,128)(2,1)S(1)}, u32[]{:S(2)}, u32[]{:S(2)}) collective-permute-start(bf16[2,128,1024]{2,1,0:T(8,128)(2,1)S(1)} %collective-permute-done.14.refs_5_), channel_id=1, source_target_pairs={{0,1},{1,0},{2,3},{3,2},{4,5},{5,4},{6,7},{7,6},{8,9},{9,8},{10,11... | collective-permute-start | bytes 1572872 | tf_op jit(solution)/shard_map/ppermute | solution.py:392
  142.2 2.4 %copy-start.14 = (bf16[2,128,1024]{2,1,0:T(8,128)(2,1)}, bf16[2,128,1024]{2,1,0:T(8,128)(2,1)S(1)}, u32[]{:S(2)}) copy-start(bf16[2,128,1024]{2,1,0:T(8,128)(2,1)S(1)} %collective-permute-done.21.refs_3_) | copy-start | bytes 1572868
  142.2 46.5 %collective-permute-start.18 = (bf16[24,128,128]{2,1,0:T(8,128)(2,1)}, bf16[24,128,128]{2,1,0:T(8,128)(2,1)S(1)}, u32[]{:S(2)}, u32[]{:S(2)}) collective-permute-start(bf16[24,128,128]{2,1,0:T(8,128)(2,1)} %get-tuple-element.141), channel_id=1, source_target_pairs={{4,12},{5,13},{6,14},{7,15},{8,0},{9,1},{10,2},{11,3},{20,28},{21,... | collective-permute-start | bytes 2359304 | tf_op jit(solution)/shard_map/ppermute | solution.py:392
  144.5 0.8 copy-start.15
  144.5 3.5 %collective-permute-start.24 = (bf16[2,128,1024]{2,1,0:T(8,128)(2,1)}, bf16[2,128,1024]{2,1,0:T(8,128)(2,1)}, u32[]{:S(2)}, u32[]{:S(2)}) collective-permute-start(bf16[2,128,1024]{2,1,0:T(8,128)(2,1)} %copy-done.13), channel_id=1, source_target_pairs={{0,1},{1,0},{2,3},{3,2},{4,5},{5,4},{6,7},{7,6},{8,9},{9,8},{10,11... | collective-permute-start | bytes 1572872 | tf_op jit(solution)/shard_map/ppermute | solution.py:392
  145.2 0.8 copy-start.16
  146.0 51.0 %collective-permute-start.17 = (bf16[12,128,128]{2,1,0:T(8,128)(2,1)}, bf16[12,128,128]{2,1,0:T(8,128)(2,1)S(1)}, u32[]{:S(2)}, u32[]{:S(2)}) collective-permute-start(bf16[12,128,128]{2,1,0:T(8,128)(2,1)} %get-tuple-element.140), channel_id=1, source_target_pairs={{4,12},{5,13},{6,14},{7,15},{8,0},{9,1},{10,2},{11,3},{20,28},{21,... | collective-permute-start | bytes 1179656 | tf_op jit(solution)/shard_map/ppermute | solution.py:392
  148.0 24.0 %copy-start.4 = (s32[17]{0:T(128)S(1)}, s32[17]{0:T(128)}, u32[]{:S(2)}) copy-start(s32[17]{0:T(128)} %get-tuple-element.108.starts) | copy-start | bytes 208
  148.0 24.0 %copy-start.5 = (s32[96]{0:T(128)S(1)}, s32[96]{0:T(128)}, u32[]{:S(2)}) copy-start(s32[96]{0:T(128)} %get-tuple-element.109.block_at) | copy-start | bytes 1156
  172.0 3.4 %copy-start = (f32[16,128,1024]{2,1,0:T(8,128)S(1)}, f32[16,128,1024]{2,1,0:T(8,128)}, u32[]{:S(2)}) copy-start(f32[16,128,1024]{2,1,0:T(8,128)} %get-tuple-element.150.refs_3_) | copy-start | bytes 25165828

commit v14 on v13

--- a/solution.py
+++ b/solution.py
@@ -13,15 +13,14 @@
 SHARES = (30, 12)
 COLUMNS = 256
 MIB = 1024 * 1024
-FAR_COST = 10**10
+FAR_COST = 4 * 10**9
 SMEM = pl.BlockSpec(memory_space=pltpu.SMEM)
 VMEM = pl.BlockSpec(memory_space=pltpu.VMEM)
 ANY = pl.BlockSpec(memory_space=pl.ANY)
 
 
-def flip_matrix(width):
-    columns = jnp.arange(width * width, dtype=jnp.int32)
-    source = (columns % width) * width + columns // width
+def flip_matrix(columns):
+    source = (columns % W) * W + columns // W
     return (columns[:, None] == source[None, :]).astype(jnp.bfloat16)
 
 
@@ -131,7 +130,7 @@
 def payload_of(at_end, tiles, received):
     return pl.pallas_call(
         payload_kernel,
-        in_specs=[SMEM, VMEM, ANY],
+        in_specs=[SMEM, ANY, ANY],
         out_specs=ANY,
         out_shape=jax.ShapeDtypeStruct(received.shape, received.dtype),
         input_output_aliases={2: 0},
@@ -420,6 +419,7 @@
     col_owner = cols // local
     late = (col_owner // 4 == zs[3]) | (col_owner == owner(2, 3))
     keys = rows + PPD * late.astype(jnp.int32)
+    columns = jnp.arange(shard.shape[2], dtype=jnp.int32)
 
     near = send(shard, other_z)
     first = send(shard, across)
@@ -436,17 +436,16 @@
 
     first = payload_of(at_end, parts[0], first)
     outer = send(first, around)
-    near, c_own, y_own, *parts = together(near, c_own, y_own, *parts)
+    near, c_own, y_own, keys, columns, *parts = together(near, c_own, y_own, keys, columns, *parts)
     second = send(near, across)
     y_near = send(near, other_y)
     c_near = send(near, other_core)
     own_tables = tables(keys, cols, block_total, 2 * PPD)
     far_tables = tables(notes[0], notes[1], block_total, cost=FAR_COST)
-    perm = flip_matrix(W)
+    perm = flip_matrix(columns)
     far_ends = [outer]
     first = jnp.where(in_centre, first, outer)
-    second, tiles_next = together(second, parts[1])
-    second = payload_of(at_end, tiles_next, second)
+    second = payload_of(at_end, parts[1], second)
     outer = send(second, around)
     first, y_own, y_near, c_near, perm, *rest = together(
         first, y_own, y_near, c_near, perm, *parts[2:], *own_tables, *far_tables
@@ -512,7 +511,8 @@
     sources = [(0, sum(sizes[:number]), send(part, opposite)) for number, part in enumerate(parts)]
     blocks = lax.all_gather(integrals, "tile", axis=0, tiled=True)
     far_tables = tables(notes[0], notes[1], block_total)
-    total, flipped = own_part(own_tables, far_tables[3], t2_tiles, [blocks], zero, flip_matrix(W))
+    columns = jnp.arange(integrals.shape[2], dtype=jnp.int32)
+    total, flipped = own_part(own_tables, far_tables[3], t2_tiles, [blocks], zero, flip_matrix(columns))
     return far_products(far_tables, zero, sources, sizes, flipped, total)
 
 

time: 202 us -> 198 us (0.980)
  waiting for transfers between devices: 56.4 us -> 48.9 us
  starting transfers between devices: 48.8 us -> 54.3 us
    ppermute x25, waiting for transfers between devices: 56.4 us -> 48.9 us  [send(): return lax.ppermute(value, 'tile', pairs)]
    ppermute x25, starting transfers between devices: 48.8 us -> 54.3 us  [send(): return lax.ppermute(value, 'tile', pairs)]
  transfers between devices with their start and end apart: 25 -> 25, of which waited for: 8 -> 9; matrix products, arithmetic and copies ran while one was open for 3% -> 3% of each run, Pallas kernels for 36% -> 37%
where the time goes in v14:
time: 198 us
  Pallas kernels  78.4 us (40%)
  starting transfers between devices  54.3 us (27%)
  waiting for transfers between devices  48.9 us (25%)
  local copies, waits for them, and re-layouts  10.9 us (6%)
  other arithmetic  4.8 us (2%)
    ppermute x25, starting transfers between devices, send(): return lax.ppermute(value, 'tile', pairs)  54.3 us
    ppermute x25, waiting for transfers between devices, send(): return lax.ppermute(value, 'tile', pairs)  48.9 us
    pallas_call x2, Pallas kernels, own_part(): pl.pallas_call(functools.partial(own_kernel, counts, group, not earlier),...  38.1 us
    pallas_call x3, Pallas kernels, far_part(): pl.pallas_call(functools.partial(far_kernel, base, [segment for segment,...  22.7 us
    pallas_call x3, Pallas kernels, tables(): pl.pallas_call(tables_kernel, in_specs=[SMEM] * 2, out_specs=[SMEM] * 4,...  12.1 us
    unnamed x34, local copies, waits for them, and re-layouts  9.08 us
    pallas_call x1, Pallas kernels, sort_tiles(): pl.pallas_call(functools.partial(sort_kernel, choices), in_specs=[SMEM] *...  5.31 us
  transfers between devices with their start and end apart: 25, of which 9 were waited for; matrix products, arithmetic and copies ran while one was open for 3% of the time, Pallas kernels for 37%

profile of v14, /device:TPU:0, one launch (start us, length us, event | category | flops | bytes accessed | tf_op | source)
XLA Modules:
  0.0 197.6 jit_solution(2134349429689960431)
XLA Ops:
  0.0 0.7 collective-permute-start
  0.7 0.5 collective-permute-start.3
  1.2 5.4 %collective-permute-start.2 = (bf16[4,128,1024]{2,1,0:T(8,128)(2,1)}, bf16[4,128,1024]{2,1,0:T(8,128)(2,1)}, u32[]{:S(2)}, u32[]{:S(2)}) collective-permute-start(bf16[4,128,1024]{2,1,0:T(8,128)(2,1)} %refs_0_.1), channel_id=1, source_target_pairs={{0,4},{1,5},{2,6},{3,7},{4,0},{5,1},{6,2},{7,3},{8,12},{9,13},{10,... | collective-permute-start | bytes 3145736 | tf_op jit(solution)/shard_map/ppermute | solution.py:391
  6.7 1.5 collective-permute-start.4
  8.2 0.7 pad_add_fusion
  8.9 4.0 %tables.3 = (s32[17]{0:T(128)}, s32[96]{0:T(128)}, s32[96]{0:T(128)}, s32[64]{0:T(128)}) custom-call(s32[96]{0:T(128)} %rows.1, s32[96]{0:T(128)} %cols.3), custom_call_target="tpu_custom_call" | custom-call | tf_op jit(solution)/shard_map/tables/pallas_call | solution.py:68
  12.9 1.2 fusion.6.rows
  14.1 1.9 copy-done.1
  16.0 0.6 copy-done.6
  16.7 5.3 %sort_tiles.1 = (bf16[4,128,1024]{2,1,0:T(8,128)(2,1)S(1)}, bf16[4,128,1024]{2,1,0:T(8,128)(2,1)S(1)}, bf16[32,128,128]{2,1,0:T(8,128)(2,1)}, bf16[60,128,128]{2...) custom-call(s32[96]{0:T(128)S(1)} %copy-done.6, s32[1]{0:T(128)} %bitcast.chosen.at_end, ...), custom_call_target="tpu_custom_call" | custom-call | tf_op jit(solution)/shard_map/sort_tiles/pallas_call | solution.py:109
  22.0 0.0 collective-permute-done.received
  22.0 0.1 payload.2
  22.1 9.0 %collective-permute-start.1 = (bf16[4,128,1024]{2,1,0:T(8,128)(2,1)S(1)}, bf16[4,128,1024]{2,1,0:T(8,128)(2,1)S(1)}, u32[]{:S(2)}, u32[]{:S(2)}) collective-permute-start(bf16[4,128,1024]{2,1,0:T(8,128)(2,1)S(1)} %payload.2), channel_id=1, source_target_pairs={{4,0},{5,1},{6,2},{7,3},{8,12},{9,13},{10,14},{11,15},{0,8},{1,9},... | collective-permute-start | bytes 3145736 | tf_op jit(solution)/shard_map/ppermute | solution.py:391
  31.1 0.5 slice_bitcast_fusion
  31.7 0.5 collective-permute-done.4.refs_6_
  32.2 0.5 copy-done.8
  32.7 0.7 collective-permute-start.8
  33.4 0.1 collective-permute-start.6
  33.5 1.6 collective-permute-start.5
  35.1 4.0 %tables.5 = (s32[17]{0:T(128)}, s32[96]{0:T(128)}, s32[96]{0:T(128)}, s32[64]{0:T(128)}) custom-call(s32[96]{0:T(128)} %get-tuple-element.160.rows, s32[96]{0:T(128)} %get-tuple-element.159.cols), custom_call_target="tpu_custom_call" | custom-call | flops 4000000000 | tf_op jit(solution)/shard_map/tables/pallas_call | solution.py:68
  39.1 4.0 %tables.4 = (s32[33]{0:T(128)}, s32[96]{0:T(128)}, s32[96]{0:T(128)}, s32[64]{0:T(128)}) custom-call(s32[96]{0:T(128)} %fusion.6.rows, s32[96]{0:T(128)} %cols.3), custom_call_target="tpu_custom_call" | custom-call | tf_op jit(solution)/shard_map/tables/pallas_call | solution.py:68
  43.2 1.7 compare_convert_fusion.perm_ref
  44.9 8.2 %collective-permute-done.1.refs_0_ = bf16[4,128,1024]{2,1,0:T(8,128)(2,1)S(1)} collective-permute-done((bf16[4,128,1024]{2,1,0:T(8,128)(2,1)S(1)}, bf16[4,128,1024]{2,1,0:T(8,128)(2,1)S(1)}, u32[]{:S(2)}, u32[]{:S(2)}) %collective-permute-start.1) | collective-permute-done | bytes 1048608 | tf_op jit(solution)/shard_map/ppermute | solution.py:391
  53.1 0.1 broadcast_select_fusion.refs_4_
  53.2 0.0 collective-permute-done.6.refs_3_
  53.2 6.1 %collective-permute-done.5.refs_8_ = bf16[4,128,1024]{2,1,0:T(8,128)(2,1)} collective-permute-done((bf16[4,128,1024]{2,1,0:T(8,128)(2,1)}, bf16[4,128,1024]{2,1,0:T(8,128)(2,1)}, u32[]{:S(2)}, u32[]{:S(2)}) %collective-permute-start.5) | collective-permute-done | bytes 1048608 | tf_op jit(solution)/shard_map/ppermute | solution.py:391
  59.4 0.1 payload.3
  59.5 19.2 %collective-permute-start.9 = (bf16[4,128,1024]{2,1,0:T(8,128)(2,1)S(1)}, bf16[4,128,1024]{2,1,0:T(8,128)(2,1)S(1)}, u32[]{:S(2)}, u32[]{:S(2)}) collective-permute-start(bf16[4,128,1024]{2,1,0:T(8,128)(2,1)S(1)} %payload.3), channel_id=1, source_target_pairs={{4,0},{5,1},{6,2},{7,3},{8,12},{9,13},{10,14},{11,15},{0,8},{1,9},... | collective-permute-start | bytes 3145736 | tf_op jit(solution)/shard_map/ppermute | solution.py:391
  78.7 0.0 collective-permute-start.12
  78.7 0.5 collective-permute-start.13
  79.2 1.5 collective-permute-start.10
  80.7 0.0 collective-permute-done.11.refs_5_
  80.7 1.3 collective-permute-start.19
  82.0 19.3 %collective-permute-done.9.refs_1_.refs_0_ = bf16[4,128,1024]{2,1,0:T(8,128)(2,1)S(1)} collective-permute-done((bf16[4,128,1024]{2,1,0:T(8,128)(2,1)S(1)}, bf16[4,128,1024]{2,1,0:T(8,128)(2,1)S(1)}, u32[]{:S(2)}, u32[]{:S(2)}) %collective-permute-start.9) | collective-permute-done | bytes 1048608 | tf_op jit(solution)/shard_map/ppermute | solution.py:391
  101.3 6.4 %collective-permute-start.16 = (bf16[32,128,128]{2,1,0:T(8,128)(2,1)}, bf16[32,128,128]{2,1,0:T(8,128)(2,1)}, u32[]{:S(2)}, u32[]{:S(2)}) collective-permute-start(bf16[32,128,128]{2,1,0:T(8,128)(2,1)} %get-tuple-element.138), channel_id=1, source_target_pairs={{0,8},{1,9},{2,10},{3,11},{12,4},{13,5},{14,6},{15,7},{16,24},{17,... | collective-permute-start | bytes 3145736 | tf_op jit(solution)/shard_map/ppermute | solution.py:391
  107.7 1.1 slice_select_fusion
  108.8 0.0 collective-permute-done.12.refs_7_
  108.8 1.0 copy-done.10
  109.8 0.3 copy-done.11
  110.1 1.5 collective-permute-start.14
  111.6 0.5 collective-permute-start.15
  112.1 0.6 stack.89.firsts
  112.7 23.2 %own_part.2 = (f32[16,128,1024]{2,1,0:T(8,128)}, bf16[32,128,1024]{2,1,0:T(8,128)(2,1)}) custom-call(s32[33]{0:T(128)} %get-tuple-element.121.starts, s32[96]{0:T(128)} %get-tuple-element.122.tile_at, s32[96]{0:T(128)} %get-tuple-element.123.block_at, s32[64]{0:T(128)} %get-tuple-element.124.own_slots, s32[64]{0:T(128)} %get-tuple-element.125.far_slots, ...), custom_call_target="tpu_custom_call" | custom-call | tf_op jit(solution)/shard_map/own_part/pallas_call | solution.py:245
  135.9 0.1 collective-permute-start.21
  136.0 0.5 collective-permute-start.22
  136.5 0.1 collective-permute-start.20
  136.6 0.4 collective-permute-start.23
  137.0 1.1 collective-permute-done.21.refs_3_
  138.1 1.3 collective-permute-start.18
  139.4 1.0 collective-permute-done.22.refs_4_
  140.4 0.1 collective-permute-start.24
  140.5 0.0 collective-permute-done.23.refs_7_
  140.5 0.6 copy-done.15
  141.2 0.8 copy-done.16
  141.9 1.3 collective-permute-start.17
  143.2 0.6 stack.99.firsts
  143.9 15.0 %own_part.3 = (f32[16,128,1024]{2,1,0:T(8,128)}, bf16[32,128,1024]{2,1,0:T(8,128)(2,1)}) custom-call(s32[33]{0:T(128)} %get-tuple-element.121.starts, s32[96]{0:T(128)} %get-tuple-element.122.tile_at, s32[96]{0:T(128)} %get-tuple-element.123.block_at, s32[64]{0:T(128)} %get-tuple-element.124.own_slots, ...), custom_call_target="tpu_custom_call", output_to_operand_aliasing={{0}: (17, {}), {1}: (18, {})} | custom-call | tf_op jit(solution)/shard_map/own_part/pallas_call | solution.py:245
  158.9 9.0 %collective-permute-done.19.refs_2_ = bf16[60,128,128]{2,1,0:T(8,128)(2,1)} collective-permute-done((bf16[60,128,128]{2,1,0:T(8,128)(2,1)}, bf16[60,128,128]{2,1,0:T(8,128)(2,1)}, u32[]{:S(2)}, u32[]{:S(2)}) %collective-permute-start.19) | collective-permute-done | bytes 1966112 | tf_op jit(solution)/shard_map/ppermute | solution.py:391
  167.9 3.4 %copy-done = f32[16,128,1024]{2,1,0:T(8,128)S(1)} copy-done((f32[16,128,1024]{2,1,0:T(8,128)S(1)}, f32[16,128,1024]{2,1,0:T(8,128)}, u32[]{:S(2)}) %copy-start) | copy-done | bytes 8388632
  171.3 12.3 %far_part.3 = (f32[16,128,1024]{2,1,0:T(8,128)S(1)}, bf16[16,128,1024]{2,1,0:T(8,128)(2,1)}) custom-call(s32[17]{0:T(128)S(1)} %copy-done.4, s32[96]{0:T(128)S(1)} %copy-done.5, s32[1]{0:T(128)} %bitcast.chosen.at_end, bf16[4,128,1024]{2,1,0:T(8,128)(2,1)S(1)} %collective-permute-done.1.refs_0_, ...), custom_call_target="tpu_custom_call", output_to_operand_aliasing={{0}: (6, {})} | custom-call | tf_op jit(solution)/shard_map/far_part/pallas_call | solution.py:365
  183.6 1.0 collective-permute-done.18.refs_2_
  184.6 5.8 %far_part.4 = (f32[16,128,1024]{2,1,0:T(8,128)S(1)}, bf16[16,128,1024]{2,1,0:T(8,128)(2,1)}) custom-call(s32[17]{0:T(128)S(1)} %copy-done.4, s32[96]{0:T(128)S(1)} %copy-done.5, s32[1]{0:T(128)} %bitcast.chosen.at_end, bf16[4,128,1024]{2,1,0:T(8,128)(2,1)S(1)} %collective-permute-done.9.refs_1_.refs_0_, ...), custom_call_target="tpu_custom_call", output_to_operand_aliasing={{0}: (6, {}), {1}: (8, {})} | custom-call | tf_op jit(solution)/shard_map/far_part/pallas_call | solution.py:365
  190.5 2.5 %collective-permute-done.17.refs_1_ = bf16[12,128,128]{2,1,0:T(8,128)(2,1)S(1)} collective-permute-done((bf16[12,128,128]{2,1,0:T(8,128)(2,1)}, bf16[12,128,128]{2,1,0:T(8,128)(2,1)S(1)}, u32[]{:S(2)}, u32[]{:S(2)}) %collective-permute-start.17) | collective-permute-done | bytes 393248 | tf_op jit(solution)/shard_map/ppermute | solution.py:391
  193.0 4.6 %far_part.5 = (f32[16,128,1024]{2,1,0:T(8,128)S(1)}, bf16[16,128,1024]{2,1,0:T(8,128)(2,1)}) custom-call(s32[17]{0:T(128)S(1)} %copy-done.4, s32[96]{0:T(128)S(1)} %copy-done.5, s32[1]{0:T(128)} %bitcast.chosen.at_end, bf16[32,128,128]{2,1,0:T(8,128)(2,1)} %collective-permute-done.16.refs_1_.refs_0_, ...), custom_call_target="tpu_custom_call", output_to_operand_aliasing={{0}: (5, {}), {1}: (7, {})} | custom-call | tf_op jit(solution)/shard_map/far_part/pallas_call | solution.py:365
  (41 shorter events, 0.1 us)
Async XLA Ops:
  0.0 22.0 %collective-permute-start = (bf16[4,128,1024]{2,1,0:T(8,128)(2,1)}, bf16[4,128,1024]{2,1,0:T(8,128)(2,1)S(1)}, u32[]{:S(2)}, u32[]{:S(2)}) collective-permute-start(bf16[4,128,1024]{2,1,0:T(8,128)(2,1)} %refs_0_.1), channel_id=1, source_target_pairs={{4,8},{5,9},{6,10},{7,11},{8,4},{9,5},{10,6},{11,7},{20,24},{21,25... | collective-permute-start | bytes 3145736 | tf_op jit(solution)/shard_map/ppermute | solution.py:391
  0.7 30.9 %collective-permute-start.3 = (bf16[4,128,1024]{2,1,0:T(8,128)(2,1)}, bf16[4,128,1024]{2,1,0:T(8,128)(2,1)S(1)}, u32[]{:S(2)}, u32[]{:S(2)}) collective-permute-start(bf16[4,128,1024]{2,1,0:T(8,128)(2,1)} %refs_0_.1), channel_id=1, source_target_pairs={{0,1},{1,0},{2,3},{3,2},{4,5},{5,4},{6,7},{7,6},{8,9},{9,8},{10,11... | collective-permute-start | bytes 3145736 | tf_op jit(solution)/shard_map/ppermute | solution.py:391
  1.2 30.4 %collective-permute-start.2 = (bf16[4,128,1024]{2,1,0:T(8,128)(2,1)}, bf16[4,128,1024]{2,1,0:T(8,128)(2,1)}, u32[]{:S(2)}, u32[]{:S(2)}) collective-permute-start(bf16[4,128,1024]{2,1,0:T(8,128)(2,1)} %refs_0_.1), channel_id=1, source_target_pairs={{0,4},{1,5},{2,6},{3,7},{4,0},{5,1},{6,2},{7,3},{8,12},{9,13},{10,... | collective-permute-start | bytes 3145736 | tf_op jit(solution)/shard_map/ppermute | solution.py:391
  6.7 25.5 %collective-permute-start.4 = (bf16[4,128,1024]{2,1,0:T(8,128)(2,1)}, bf16[4,128,1024]{2,1,0:T(8,128)(2,1)}, u32[]{:S(2)}, u32[]{:S(2)}) collective-permute-start(bf16[4,128,1024]{2,1,0:T(8,128)(2,1)} %refs_0_.1), channel_id=1, source_target_pairs={{0,2},{1,3},{2,0},{3,1},{4,6},{5,7},{6,4},{7,5},{8,10},{9,11},{10,... | collective-permute-start | bytes 3145736 | tf_op jit(solution)/shard_map/ppermute | solution.py:391
  8.9 22.3 %collective-permute-start.7 = (s32[2,96]{1,0:T(2,128)S(1)}, s32[2,96]{1,0:T(2,128)S(1)}, u32[]{:S(2)}, u32[]{:S(2)}) collective-permute-start(s32[2,96]{1,0:T(2,128)S(1)} %pad_add_fusion), channel_id=1, source_target_pairs={{0,8},{1,9},{2,10},{3,11},{4,12},{5,13},{6,14},{7,15},{8,0},{9,1},... | collective-permute-start | bytes 2312 | tf_op jit(solution)/shard_map/ppermute | solution.py:391
  14.1 1.9 copy-start.1
  16.0 0.6 copy-start.6
  22.0 10.2 %copy-start.2 = (bf16[4,128,1024]{2,1,0:T(8,128)(2,1)}, bf16[4,128,1024]{2,1,0:T(8,128)(2,1)S(1)}, u32[]{:S(2)}) copy-start(bf16[4,128,1024]{2,1,0:T(8,128)(2,1)S(1)} %get-tuple-element.112.tiles_ref) | copy-start | bytes 3145732
  22.1 31.0 %collective-permute-start.1 = (bf16[4,128,1024]{2,1,0:T(8,128)(2,1)S(1)}, bf16[4,128,1024]{2,1,0:T(8,128)(2,1)S(1)}, u32[]{:S(2)}, u32[]{:S(2)}) collective-permute-start(bf16[4,128,1024]{2,1,0:T(8,128)(2,1)S(1)} %payload.2), channel_id=1, source_target_pairs={{4,0},{5,1},{6,2},{7,3},{8,12},{9,13},{10,14},{11,15},{0,8},{1,9},... | collective-permute-start | bytes 3145736 | tf_op jit(solution)/shard_map/ppermute | solution.py:391
  31.7 1.0 copy-start.8
  32.7 26.7 %collective-permute-start.8 = (bf16[4,128,1024]{2,1,0:T(8,128)(2,1)}, bf16[4,128,1024]{2,1,0:T(8,128)(2,1)S(1)}, u32[]{:S(2)}, u32[]{:S(2)}) collective-permute-start(bf16[4,128,1024]{2,1,0:T(8,128)(2,1)} %collective-permute-done.2.refs_2_), channel_id=1, source_target_pairs={{4,8},{5,9},{6,10},{7,11},{8,4},{9,5},{10,6},{11,7},{20,24},{21,25... | collective-permute-start | bytes 3145736 | tf_op jit(solution)/shard_map/ppermute | solution.py:391
  33.4 19.8 %collective-permute-start.6 = (bf16[4,128,1024]{2,1,0:T(8,128)(2,1)}, bf16[4,128,1024]{2,1,0:T(8,128)(2,1)}, u32[]{:S(2)}, u32[]{:S(2)}) collective-permute-start(bf16[4,128,1024]{2,1,0:T(8,128)(2,1)} %collective-permute-done.2.refs_2_), channel_id=1, source_target_pairs={{0,1},{1,0},{2,3},{3,2},{4,5},{5,4},{6,7},{7,6},{8,9},{9,8},{10,11... | collective-permute-start | bytes 3145736 | tf_op jit(solution)/shard_map/ppermute | solution.py:391
  33.5 25.9 %collective-permute-start.5 = (bf16[4,128,1024]{2,1,0:T(8,128)(2,1)}, bf16[4,128,1024]{2,1,0:T(8,128)(2,1)}, u32[]{:S(2)}, u32[]{:S(2)}) collective-permute-start(bf16[4,128,1024]{2,1,0:T(8,128)(2,1)} %collective-permute-done.2.refs_2_), channel_id=1, source_target_pairs={{0,2},{1,3},{2,0},{3,1},{4,6},{5,7},{6,4},{7,5},{8,10},{9,11},{10,... | collective-permute-start | bytes 3145736 | tf_op jit(solution)/shard_map/ppermute | solution.py:391
  43.1 16.2 %copy-start.3 = (bf16[4,128,1024]{2,1,0:T(8,128)(2,1)S(1)}, bf16[4,128,1024]{2,1,0:T(8,128)(2,1)}, u32[]{:S(2)}) copy-start(bf16[4,128,1024]{2,1,0:T(8,128)(2,1)} %copy-done.2) | copy-start | bytes 3145732
  53.2 55.6 %copy-start.7 = (bf16[4,128,1024]{2,1,0:T(8,128)(2,1)}, bf16[4,128,1024]{2,1,0:T(8,128)(2,1)S(1)}, u32[]{:S(2)}) copy-start(bf16[4,128,1024]{2,1,0:T(8,128)(2,1)S(1)} %broadcast_select_fusion.refs_4_) | copy-start | bytes 3145732
  59.4 21.4 %collective-permute-start.11 = (bf16[4,128,1024]{2,1,0:T(8,128)(2,1)S(1)}, bf16[4,128,1024]{2,1,0:T(8,128)(2,1)S(1)}, u32[]{:S(2)}, u32[]{:S(2)}) collective-permute-start(bf16[4,128,1024]{2,1,0:T(8,128)(2,1)S(1)} %broadcast_select_fusion.refs_4_), channel_id=1, source_target_pairs={{0,1},{1,0},{2,3},{3,2},{4,5},{5,4},{6,7},{7,6},{8,9},{9,8},{10,11... | collective-permute-start | bytes 3145736 | tf_op jit(solution)/shard_map/ppermute | solution.py:391
  59.5 41.9 %collective-permute-start.9 = (bf16[4,128,1024]{2,1,0:T(8,128)(2,1)S(1)}, bf16[4,128,1024]{2,1,0:T(8,128)(2,1)S(1)}, u32[]{:S(2)}, u32[]{:S(2)}) collective-permute-start(bf16[4,128,1024]{2,1,0:T(8,128)(2,1)S(1)} %payload.3), channel_id=1, source_target_pairs={{4,0},{5,1},{6,2},{7,3},{8,12},{9,13},{10,14},{11,15},{0,8},{1,9},... | collective-permute-start | bytes 3145736 | tf_op jit(solution)/shard_map/ppermute | solution.py:391
  78.7 30.1 %collective-permute-start.12 = (bf16[4,128,1024]{2,1,0:T(8,128)(2,1)}, bf16[4,128,1024]{2,1,0:T(8,128)(2,1)S(1)}, u32[]{:S(2)}, u32[]{:S(2)}) collective-permute-start(bf16[4,128,1024]{2,1,0:T(8,128)(2,1)} %collective-permute-done.4.refs_6_), channel_id=1, source_target_pairs={{0,1},{1,0},{2,3},{3,2},{4,5},{5,4},{6,7},{7,6},{8,9},{9,8},{10,11... | collective-permute-start | bytes 3145736 | tf_op jit(solution)/shard_map/ppermute | solution.py:391
  78.7 30.1 %collective-permute-start.13 = (bf16[4,128,1024]{2,1,0:T(8,128)(2,1)}, bf16[4,128,1024]{2,1,0:T(8,128)(2,1)S(1)}, u32[]{:S(2)}, u32[]{:S(2)}) collective-permute-start(bf16[4,128,1024]{2,1,0:T(8,128)(2,1)} %collective-permute-done.5.refs_8_), channel_id=1, source_target_pairs={{0,1},{1,0},{2,3},{3,2},{4,5},{5,4},{6,7},{7,6},{8,9},{9,8},{10,11... | collective-permute-start | bytes 3145736 | tf_op jit(solution)/shard_map/ppermute | solution.py:391
  79.2 29.6 %collective-permute-start.10 = (bf16[4,128,1024]{2,1,0:T(8,128)(2,1)S(1)}, bf16[4,128,1024]{2,1,0:T(8,128)(2,1)}, u32[]{:S(2)}, u32[]{:S(2)}) collective-permute-start(bf16[4,128,1024]{2,1,0:T(8,128)(2,1)S(1)} %broadcast_select_fusion.refs_4_), channel_id=1, source_target_pairs={{0,2},{1,3},{2,0},{3,1},{4,6},{5,7},{6,4},{7,5},{8,10},{9,11},{10,... | collective-permute-start | bytes 3145736 | tf_op jit(solution)/shard_map/ppermute | solution.py:391
  80.7 20.6 %copy-start.9 = (bf16[4,128,1024]{2,1,0:T(8,128)(2,1)}, bf16[4,128,1024]{2,1,0:T(8,128)(2,1)S(1)}, u32[]{:S(2)}) copy-start(bf16[4,128,1024]{2,1,0:T(8,128)(2,1)S(1)} %collective-permute-done.11.refs_5_) | copy-start | bytes 3145732
  80.7 87.2 %collective-permute-start.19 = (bf16[60,128,128]{2,1,0:T(8,128)(2,1)}, bf16[60,128,128]{2,1,0:T(8,128)(2,1)}, u32[]{:S(2)}, u32[]{:S(2)}) collective-permute-start(bf16[60,128,128]{2,1,0:T(8,128)(2,1)} %get-tuple-element.142), channel_id=1, source_target_pairs={{4,12},{5,13},{6,14},{7,15},{8,0},{9,1},{10,2},{11,3},{20,28},{21,... | collective-permute-start | bytes 5898248 | tf_op jit(solution)/shard_map/ppermute | solution.py:391
  101.3 35.3 %collective-permute-start.16 = (bf16[32,128,128]{2,1,0:T(8,128)(2,1)}, bf16[32,128,128]{2,1,0:T(8,128)(2,1)}, u32[]{:S(2)}, u32[]{:S(2)}) collective-permute-start(bf16[32,128,128]{2,1,0:T(8,128)(2,1)} %get-tuple-element.138), channel_id=1, source_target_pairs={{0,8},{1,9},{2,10},{3,11},{12,4},{13,5},{14,6},{15,7},{16,24},{17,... | collective-permute-start | bytes 3145736 | tf_op jit(solution)/shard_map/ppermute | solution.py:391
  108.8 1.0 copy-start.10
  108.8 1.3 copy-start.11
  110.1 25.8 %collective-permute-start.14 = (bf16[2,128,1024]{2,1,0:T(8,128)(2,1)}, bf16[2,128,1024]{2,1,0:T(8,128)(2,1)S(1)}, u32[]{:S(2)}, u32[]{:S(2)}) collective-permute-start(bf16[2,128,1024]{2,1,0:T(8,128)(2,1)} %get-tuple-element.144.refs_1_), channel_id=1, source_target_pairs={{0,2},{1,3},{2,0},{3,1},{4,6},{5,7},{6,4},{7,5},{8,10},{9,11},{10,... | collective-permute-start | bytes 1572872 | tf_op jit(solution)/shard_map/ppermute | solution.py:391
  111.6 24.3 %collective-permute-start.15 = (bf16[2,128,1024]{2,1,0:T(8,128)(2,1)}, bf16[2,128,1024]{2,1,0:T(8,128)(2,1)S(1)}, u32[]{:S(2)}, u32[]{:S(2)}) collective-permute-start(bf16[2,128,1024]{2,1,0:T(8,128)(2,1)} %get-tuple-element.145.refs_2_), channel_id=1, source_target_pairs={{0,2},{1,3},{2,0},{3,1},{4,6},{5,7},{6,4},{7,5},{8,10},{9,11},{10,... | collective-permute-start | bytes 1572872 | tf_op jit(solution)/shard_map/ppermute | solution.py:391
  135.9 4.6 %copy-start.12 = (bf16[2,128,1024]{2,1,0:T(8,128)(2,1)}, bf16[2,128,1024]{2,1,0:T(8,128)(2,1)S(1)}, u32[]{:S(2)}) copy-start(bf16[2,128,1024]{2,1,0:T(8,128)(2,1)S(1)} %collective-permute-done.14.refs_5_) | copy-start | bytes 1572868
  135.9 1.1 copy-start.13
  135.9 2.2 %collective-permute-start.21 = (bf16[2,128,1024]{2,1,0:T(8,128)(2,1)}, bf16[2,128,1024]{2,1,0:T(8,128)(2,1)S(1)}, u32[]{:S(2)}, u32[]{:S(2)}) collective-permute-start(bf16[2,128,1024]{2,1,0:T(8,128)(2,1)} %get-tuple-element.144.refs_1_), channel_id=1, source_target_pairs={{0,1},{1,0},{2,3},{3,2},{4,5},{5,4},{6,7},{7,6},{8,9},{9,8},{10,11... | collective-permute-start | bytes 1572872 | tf_op jit(solution)/shard_map/ppermute | solution.py:391
  136.0 4.4 %collective-permute-start.22 = (bf16[2,128,1024]{2,1,0:T(8,128)(2,1)}, bf16[2,128,1024]{2,1,0:T(8,128)(2,1)S(1)}, u32[]{:S(2)}, u32[]{:S(2)}) collective-permute-start(bf16[2,128,1024]{2,1,0:T(8,128)(2,1)} %get-tuple-element.145.refs_2_), channel_id=1, source_target_pairs={{0,1},{1,0},{2,3},{3,2},{4,5},{5,4},{6,7},{7,6},{8,9},{9,8},{10,11... | collective-permute-start | bytes 1572872 | tf_op jit(solution)/shard_map/ppermute | solution.py:391
  136.5 7.4 %collective-permute-start.20 = (bf16[4,128,1024]{2,1,0:T(8,128)(2,1)}, bf16[4,128,1024]{2,1,0:T(8,128)(2,1)}, u32[]{:S(2)}, u32[]{:S(2)}) collective-permute-start(bf16[4,128,1024]{2,1,0:T(8,128)(2,1)} %collective-permute-done.10.refs_10_), channel_id=1, source_target_pairs={{0,1},{1,0},{2,3},{3,2},{4,5},{5,4},{6,7},{7,6},{8,9},{9,8},{10,11... | collective-permute-start | bytes 3145736 | tf_op jit(solution)/shard_map/ppermute | solution.py:391
  136.6 3.9 %collective-permute-start.23 = (bf16[2,128,1024]{2,1,0:T(8,128)(2,1)S(1)}, bf16[2,128,1024]{2,1,0:T(8,128)(2,1)S(1)}, u32[]{:S(2)}, u32[]{:S(2)}) collective-permute-start(bf16[2,128,1024]{2,1,0:T(8,128)(2,1)S(1)} %collective-permute-done.14.refs_5_), channel_id=1, source_target_pairs={{0,1},{1,0},{2,3},{3,2},{4,5},{5,4},{6,7},{7,6},{8,9},{9,8},{10,11... | collective-permute-start | bytes 1572872 | tf_op jit(solution)/shard_map/ppermute | solution.py:391
  138.1 2.4 %copy-start.14 = (bf16[2,128,1024]{2,1,0:T(8,128)(2,1)}, bf16[2,128,1024]{2,1,0:T(8,128)(2,1)S(1)}, u32[]{:S(2)}) copy-start(bf16[2,128,1024]{2,1,0:T(8,128)(2,1)S(1)} %collective-permute-done.21.refs_3_) | copy-start | bytes 1572868
  138.1 46.5 %collective-permute-start.18 = (bf16[24,128,128]{2,1,0:T(8,128)(2,1)}, bf16[24,128,128]{2,1,0:T(8,128)(2,1)S(1)}, u32[]{:S(2)}, u32[]{:S(2)}) collective-permute-start(bf16[24,128,128]{2,1,0:T(8,128)(2,1)} %get-tuple-element.141), channel_id=1, source_target_pairs={{4,12},{5,13},{6,14},{7,15},{8,0},{9,1},{10,2},{11,3},{20,28},{21,... | collective-permute-start | bytes 2359304 | tf_op jit(solution)/shard_map/ppermute | solution.py:391
  140.4 0.8 copy-start.15
  140.4 3.5 %collective-permute-start.24 = (bf16[2,128,1024]{2,1,0:T(8,128)(2,1)}, bf16[2,128,1024]{2,1,0:T(8,128)(2,1)}, u32[]{:S(2)}, u32[]{:S(2)}) collective-permute-start(bf16[2,128,1024]{2,1,0:T(8,128)(2,1)} %copy-done.13), channel_id=1, source_target_pairs={{0,1},{1,0},{2,3},{3,2},{4,5},{5,4},{6,7},{7,6},{8,9},{9,8},{10,11... | collective-permute-start | bytes 1572872 | tf_op jit(solution)/shard_map/ppermute | solution.py:391
  141.2 0.8 copy-start.16
  141.9 51.0 %collective-permute-start.17 = (bf16[12,128,128]{2,1,0:T(8,128)(2,1)}, bf16[12,128,128]{2,1,0:T(8,128)(2,1)S(1)}, u32[]{:S(2)}, u32[]{:S(2)}) collective-permute-start(bf16[12,128,128]{2,1,0:T(8,128)(2,1)} %get-tuple-element.140), channel_id=1, source_target_pairs={{4,12},{5,13},{6,14},{7,15},{8,0},{9,1},{10,2},{11,3},{20,28},{21,... | collective-permute-start | bytes 1179656 | tf_op jit(solution)/shard_map/ppermute | solution.py:391
  143.9 24.0 %copy-start.4 = (s32[17]{0:T(128)S(1)}, s32[17]{0:T(128)}, u32[]{:S(2)}) copy-start(s32[17]{0:T(128)} %get-tuple-element.110.starts) | copy-start | bytes 208
  143.9 24.0 %copy-start.5 = (s32[96]{0:T(128)S(1)}, s32[96]{0:T(128)}, u32[]{:S(2)}) copy-start(s32[96]{0:T(128)} %get-tuple-element.111.block_at) | copy-start | bytes 1156
  167.9 3.4 %copy-start = (f32[16,128,1024]{2,1,0:T(8,128)S(1)}, f32[16,128,1024]{2,1,0:T(8,128)}, u32[]{:S(2)}) copy-start(f32[16,128,1024]{2,1,0:T(8,128)} %get-tuple-element.150.refs_3_) | copy-start | bytes 25165828

commit v15 on v14

--- a/solution.py
+++ b/solution.py
@@ -10,7 +10,7 @@
 W = 32
 PPD = 16
 REUSE = 3
-SHARES = (30, 12)
+SHARES = (30, 9, 6)
 COLUMNS = 256
 MIB = 1024 * 1024
 FAR_COST = 4 * 10**9
@@ -24,8 +24,26 @@
     return (columns[:, None] == source[None, :]).astype(jnp.bfloat16)
 
 
-def tables_kernel(rows, cols, starts, tile_at, block_at, slots, cursor):
-    count, total, groups = rows.shape[0], slots.shape[0], cursor.shape[0]
+class View:
+    def __init__(self, ref, offset):
+        self.ref, self.offset = ref, offset
+
+    def __getitem__(self, index):
+        return self.ref[self.offset + index]
+
+    def __setitem__(self, index, value):
+        self.ref[self.offset + index] = value
+
+
+def table_views(table, count, groups):
+    places = [0, groups + 1, groups + 1 + count, groups + 1 + 2 * count]
+    return [View(table, place) for place in places]
+
+
+def tables_kernel(rows, cols, table, cursor):
+    count, groups = rows.shape[0], cursor.shape[0]
+    total = table.shape[0] - (groups + 1 + 2 * count)
+    starts, tile_at, block_at, slots = table_views(table, count, groups)
 
     @pl.loop(0, total)
     def _(block):
@@ -68,8 +86,8 @@
     return pl.pallas_call(
         tables_kernel,
         in_specs=[SMEM] * 2,
-        out_specs=[SMEM] * 4,
-        out_shape=[jax.ShapeDtypeStruct((size,), jnp.int32) for size in (groups + 1, count, count, total)],
+        out_specs=SMEM,
+        out_shape=jax.ShapeDtypeStruct((groups + 1 + 2 * count + total,), jnp.int32),
         scratch_shapes=[pltpu.SMEM((groups,), jnp.int32)],
         cost_estimate=pl.CostEstimate(flops=cost, bytes_accessed=0, transcendentals=0) if cost else None,
         name="tables",
@@ -84,7 +102,8 @@
     return ref.at[lax.div(tile, across), :, pl.ds(pl.multiple_of(lax.rem(tile, across) * depth, depth), depth)]
 
 
-def sort_kernel(choices, tile_at, chosen, tiles_ref, *refs):
+def sort_kernel(choices, table, chosen, tiles_ref, *refs):
+    tile_at = table_views(table, tiles_ref.shape[0], PPD)[1]
     parts, sems = refs[: len(refs) // 2], refs[len(refs) // 2 :]
     begin = {choice: 0 for choice in choices}
     for choice, part, sem in zip(choices, parts, sems):
@@ -105,7 +124,7 @@
             pltpu.make_async_copy(part, part, sem).wait()
 
 
-def sort_tiles(tile_at, chosen, tiles, choices, shapes):
+def sort_tiles(table, chosen, tiles, choices, shapes):
     return pl.pallas_call(
         functools.partial(sort_kernel, choices),
         in_specs=[SMEM] * 2 + [ANY],
@@ -114,7 +133,7 @@
         scratch_shapes=[pltpu.SemaphoreType.DMA] * len(shapes),
         compiler_params=pltpu.CompilerParams(vmem_limit_bytes=16 * MIB),
         name="sort_tiles",
-    )(tile_at, chosen, tiles)
+    )(table, chosen, tiles)
 
 
 def payload_kernel(at_end, tiles_ref, received, payload, sem):
@@ -158,7 +177,9 @@
             sum_ref[:, window] += jnp.dot(left, right, preferred_element_type=jnp.float32)
 
 
-def own_kernel(counts, group, fresh, starts, tile_at, block_at, own_slots, far_slots, firsts, tiles_ref, perm_ref, *refs):
+def own_kernel(counts, groups, group, fresh, own_table, far_table, firsts, tiles_ref, perm_ref, *refs):
+    starts, tile_at, block_at, own_slots = table_views(own_table, tiles_ref.shape[0], groups)
+    far_slots = table_views(far_table, tiles_ref.shape[0], PPD)[3]
     pieces = refs[: len(counts)]
     refs = refs[len(counts) :]
     if not fresh:
@@ -235,16 +256,15 @@
         store(row).wait()
 
 
-def own_part(own_tables, far_slots, tiles, pieces, firsts, perm, group=0, earlier=()):
-    starts, tile_at, block_at, own_slots = own_tables
+def own_part(own_table, far_table, tiles, pieces, firsts, perm, groups=PPD, group=0, earlier=()):
     count, height, _ = tiles.shape
     depth, width = pieces[0].shape[1:]
     need = count // REUSE
     counts = [piece.shape[0] for piece in pieces]
-    operands = 8 + len(pieces)
+    operands = 5 + len(pieces)
     return pl.pallas_call(
-        functools.partial(own_kernel, counts, group, not earlier),
-        in_specs=[SMEM] * 6 + [VMEM] * 2 + [ANY] * (len(pieces) + len(earlier)),
+        functools.partial(own_kernel, counts, groups, group, not earlier),
+        in_specs=[SMEM] * 3 + [VMEM] * 2 + [ANY] * (len(pieces) + len(earlier)),
         out_specs=[ANY] * 2,
         out_shape=[
             jax.ShapeDtypeStruct((PPD, height, width), jnp.float32),
@@ -263,10 +283,11 @@
         ],
         compiler_params=pltpu.CompilerParams(vmem_limit_bytes=56 * MIB),
         name="own_part",
-    )(starts, tile_at, block_at, own_slots, far_slots, firsts, tiles, perm, *pieces, *earlier)
-
-
-def far_kernel(base, segments, starts, block_at, chosen, *refs):
+    )(own_table, far_table, firsts, tiles, perm, *pieces, *earlier)
+
+
+def far_kernel(base, total_count, segments, table, chosen, *refs):
+    starts, _, block_at, _ = table_views(table, total_count, PPD)
     tile_refs, refs = refs[: len(segments)], refs[len(segments) :]
     sum_in, flip_in = refs[:2]
     refs = refs[3:] if base else refs[2:]
@@ -350,8 +371,7 @@
     each_row(finish)
 
 
-def far_part(base, count, far_tables, chosen, sources, flipped, total, result=None):
-    starts, _, block_at, _ = far_tables
+def far_part(base, count, total_count, far_table, chosen, sources, flipped, total, result=None):
     whole = total.shape
     given = [] if result is None else [result]
     held = [array.size // (whole[1] * flipped.shape[1]) for _, _, array in sources]
@@ -360,11 +380,11 @@
         for source, size in zip(sources, held)
         if source[1] < base + count and source[1] + size > base
     ]
-    operand = 3 + len(used)
+    operand = 2 + len(used)
     aliases = {operand: 0, operand + 2: 1} if given else {operand: 0}
     return pl.pallas_call(
-        functools.partial(far_kernel, base, [segment for segment, _ in used]),
-        in_specs=[SMEM] * 3 + [ANY] * (len(used) + 2 + len(given)),
+        functools.partial(far_kernel, base, total_count, [segment for segment, _ in used]),
+        in_specs=[SMEM] * 2 + [ANY] * (len(used) + 2 + len(given)),
         out_specs=[ANY] * 2,
         out_shape=[jax.ShapeDtypeStruct(whole, jnp.float32), jax.ShapeDtypeStruct(whole, jnp.bfloat16)],
         input_output_aliases=aliases,
@@ -380,7 +400,7 @@
         ],
         compiler_params=pltpu.CompilerParams(vmem_limit_bytes=40 * MIB),
         name="far_part",
-    )(starts, block_at, chosen, *[array for _, array in used], total, flipped, *given)
+    )(far_table, chosen, *[array for _, array in used], total, flipped, *given)
 
 
 def together(*values):
@@ -424,14 +444,14 @@
     near = send(shard, other_z)
     first = send(shard, across)
     notes = send(jnp.stack([rows, cols]), opposite)
-    order = tables(rows, cols, block_total)[1]
+    order = tables(rows, cols, block_total)
     c_own = send(shard, other_core)
     y_own = send(shard, other_y)
     count = tiles.shape[0]
     step = shard.size // tiles[0].size
     sizes = tile_parts(count)
     shapes = [shard.shape] * 2 + [(size,) + tiles.shape[1:] for size in [count - 2 * step] + sizes]
-    parts = sort_tiles(order, at_end, tiles, [1, 1, 1, 0, 0, 0], shapes)
+    parts = sort_tiles(order, at_end, tiles, [1] * 3 + [0] * len(sizes), shapes)
     first, *parts = together(first, *parts)
 
     first = payload_of(at_end, parts[0], first)
@@ -440,32 +460,32 @@
     second = send(near, across)
     y_near = send(near, other_y)
     c_near = send(near, other_core)
-    own_tables = tables(keys, cols, block_total, 2 * PPD)
-    far_tables = tables(notes[0], notes[1], block_total, cost=FAR_COST)
+    c_y_own = send(y_own, other_core)
+    own_table = tables(keys, cols, block_total, 2 * PPD)
+    far_table = tables(notes[0], notes[1], block_total, cost=FAR_COST)
     perm = flip_matrix(columns)
     far_ends = [outer]
     first = jnp.where(in_centre, first, outer)
     second = payload_of(at_end, parts[1], second)
     outer = send(second, around)
-    first, y_own, y_near, c_near, perm, *rest = together(
-        first, y_own, y_near, c_near, perm, *parts[2:], *own_tables, *far_tables
+    first, c_y_own, y_near, c_near, perm, *rest = together(
+        first, c_y_own, y_near, c_near, perm, own_table, far_table, *parts[2:]
     )
-    parts, own_tables, far_tables = rest[:4], rest[4:8], rest[8:]
+    own_table, far_table, *parts = rest
     y_first = send(first, other_y)
     c_first = send(first, other_core)
-    c_y_own = send(y_own, other_core)
     c_y_near = send(y_near, other_core)
     tiles_last, c_first = together(parts[0], c_first)
     far_ends += [outer, send(tiles_last, from_ends)]
     halves = (slice(0, local // 2), slice(local // 2, None))
     second = [jnp.where(in_centre, second[half], outer[half]) for half in halves]
-    *second, y_first, c_first, c_y_own, c_y_near = together(*second, y_first, c_first, c_y_own, c_y_near)
+    *second, y_first, c_first, c_y_near = together(*second, y_first, c_first, c_y_near)
 
     far_centre = [send(parts[1], from_centre)]
     y_second = [send(half, other_y) for half in second]
     pieces = [shard, c_own, near, c_near, first, c_first, y_own, c_y_own, y_near, c_y_near, y_first]
     firsts = [owner(k, y + core) * local for y in (0, 2) for k in range(3) for core in (0, 1)][:11]
-    early = own_part(own_tables, far_tables[3], tiles, pieces, first_blocks(firsts), perm)
+    early = own_part(own_table, far_table, tiles, pieces, first_blocks(firsts), perm, 2 * PPD)
     y_second[0], y_second[1], second[0], second[1], y_first, total, flipped, *parts = together(
         *y_second, *second, y_first, *early, *parts[2:]
     )
@@ -477,11 +497,12 @@
     c_y_second = [send(half, other_core) for half in y_second]
     pieces = [c_y_first, *second, *c_second, *y_second, *c_y_second]
     firsts = [owner(2, 3) * local] + [owner(3, bits) * local + half for bits in range(4) for half in (0, local // 2)]
-    total, flipped = own_part(own_tables, far_tables[3], tiles, pieces, first_blocks(firsts), perm, PPD, (total, flipped))
+    earlier = (total, flipped)
+    total, flipped = own_part(own_table, far_table, tiles, pieces, first_blocks(firsts), perm, 2 * PPD, PPD, earlier)
 
     sources = [(0, step * number, array) for number, array in enumerate(far_ends)]
     sources += [(1, sum(sizes[:number]), array) for number, array in enumerate(far_centre)]
-    return far_products(far_tables, at_end, sources, sizes, flipped, total)
+    return far_products(far_table, at_end, sources, sizes, flipped, total)
 
 
 def tile_parts(count):
@@ -489,10 +510,10 @@
     return sizes + [count - sum(sizes)]
 
 
-def far_products(far_tables, chosen, sources, sizes, flipped, total):
+def far_products(far_table, chosen, sources, sizes, flipped, total):
     base, result = 0, None
     for size in sizes:
-        total, result = far_part(base, size, far_tables, chosen, sources, flipped, total, result)
+        total, result = far_part(base, size, sum(sizes), far_table, chosen, sources, flipped, total, result)
         base += size
     return result
 
@@ -503,17 +524,17 @@
         return staged_part(t2_tiles, t2_row, t2_col, integrals)
     block_total = peers * integrals.shape[0]
     opposite = [(source, (source + peers // 2) % peers) for source in range(peers)]
-    own_tables = tables(t2_row, t2_col, block_total)
+    own_table = tables(t2_row, t2_col, block_total)
     sizes = tile_parts(t2_tiles.shape[0])
     zero = jnp.zeros((1,), jnp.int32)
-    parts = sort_tiles(own_tables[1], zero, t2_tiles, [0] * 3, [(size,) + t2_tiles.shape[1:] for size in sizes])
+    parts = sort_tiles(own_table, zero, t2_tiles, [0] * len(sizes), [(size,) + t2_tiles.shape[1:] for size in sizes])
     notes = send(jnp.stack([t2_row, t2_col]), opposite)
     sources = [(0, sum(sizes[:number]), send(part, opposite)) for number, part in enumerate(parts)]
     blocks = lax.all_gather(integrals, "tile", axis=0, tiled=True)
-    far_tables = tables(notes[0], notes[1], block_total)
+    far_table = tables(notes[0], notes[1], block_total)
     columns = jnp.arange(integrals.shape[2], dtype=jnp.int32)
-    total, flipped = own_part(own_tables, far_tables[3], t2_tiles, [blocks], zero, flip_matrix(columns))
-    return far_products(far_tables, zero, sources, sizes, flipped, total)
+    total, flipped = own_part(own_table, far_table, t2_tiles, [blocks], zero, flip_matrix(columns))
+    return far_products(far_table, zero, sources, sizes, flipped, total)
 
 
 def solution(mesh):

time: 198 us -> 199 us (level)
  waiting for transfers between devices: 48.9 us -> 43.4 us
  Pallas kernels: 78.4 us -> 81.6 us
    ppermute x25 -> x26, waiting for transfers between devices: 48.9 us -> 43.4 us  [send(): return lax.ppermute(value, 'tile', pairs)]
    pallas_call x8 -> x9, Pallas kernels: 72.9 us -> 76.1 us  [the longest x2 38.3 us: own_part(): pl.pallas_call(functools.partial(own_kernel, counts, groups, group, not e...]
    unnamed x34 -> x26, local copies, waits for them, and re-layouts: 9.08 us -> 9.73 us
    ppermute x25 -> x26, starting transfers between devices: 54.3 us -> 54.8 us  [send(): return lax.ppermute(value, 'tile', pairs)]
  transfers between devices with their start and end apart: 25 -> 26, of which waited for: 9 -> 8; matrix products, arithmetic and copies ran while one was open for 3% -> 4% of each run, Pallas kernels for 37% -> 39%
where the time goes in v15:
time: 199 us; the launch traced here: 198 us
  Pallas kernels  81.6 us (41%)
  starting transfers between devices  54.8 us (28%)
  waiting for transfers between devices  43.4 us (22%)
  local copies, waits for them, and re-layouts  11.6 us (6%)
  other arithmetic  6.02 us (3%)
    ppermute x26, starting transfers between devices, send(): return lax.ppermute(value, 'tile', pairs)  54.8 us
    ppermute x26, waiting for transfers between devices, send(): return lax.ppermute(value, 'tile', pairs)  43.4 us
    pallas_call x2, Pallas kernels, own_part(): pl.pallas_call(functools.partial(own_kernel, counts, groups, group, not e...  38.3 us
    pallas_call x4, Pallas kernels, far_part(): pl.pallas_call(functools.partial(far_kernel, base, total_count, [segment...  25.4 us
    pallas_call x3, Pallas kernels, tables(): pl.pallas_call(tables_kernel, in_specs=[SMEM] * 2, out_specs=SMEM, out_sh...  12.4 us
    unnamed x26, local copies, waits for them, and re-layouts  9.73 us
    pallas_call x1, Pallas kernels, sort_tiles(): pl.pallas_call(functools.partial(sort_kernel, choices), in_specs=[SMEM] *...  5.37 us
  transfers between devices with their start and end apart: 26, of which 8 were waited for; matrix products, arithmetic and copies ran while one was open for 4% of the time, Pallas kernels for 39%

profile of v15, /device:TPU:0, one launch (start us, length us, event | category | flops | bytes accessed | tf_op | source)
XLA Modules:
  0.0 197.9 jit_solution(13240463904465314267)
XLA Ops:
  0.0 0.7 collective-permute-start
  0.7 0.5 collective-permute-start.3
  1.2 5.4 %collective-permute-start.2 = (bf16[4,128,1024]{2,1,0:T(8,128)(2,1)}, bf16[4,128,1024]{2,1,0:T(8,128)(2,1)}, u32[]{:S(2)}, u32[]{:S(2)}) collective-permute-start(bf16[4,128,1024]{2,1,0:T(8,128)(2,1)} %refs_0_.1), channel_id=1, source_target_pairs={{0,4},{1,5},{2,6},{3,7},{4,0},{5,1},{6,2},{7,3},{8,12},{9,13},{10,... | collective-permute-start | bytes 3145736 | tf_op jit(solution)/shard_map/ppermute | solution.py:411
  6.7 1.5 collective-permute-start.4
  8.2 0.7 pad_add_fusion
  8.9 4.1 %tables.3.table = s32[273]{0:T(512)} custom-call(s32[96]{0:T(128)} %rows.1, s32[96]{0:T(128)} %cols.3), custom_call_target="tpu_custom_call" | custom-call | tf_op jit(solution)/shard_map/tables/pallas_call | solution.py:86
  13.0 1.2 fusion.6.rows
  14.3 1.9 copy-done.1
  16.2 0.7 copy-done.6
  16.8 5.4 %sort_tiles.1 = (bf16[4,128,1024]{2,1,0:T(8,128)(2,1)S(1)}, bf16[4,128,1024]{2,1,0:T(8,128)(2,1)S(1)}, bf16[32,128,128]{2,1,0:T(8,128)(2,1)}, bf16[60,128,128]{2...) custom-call(s32[273]{0:T(512)S(1)} %copy-done.6, ...), custom_call_target="tpu_custom_call" | custom-call | tf_op jit(solution)/shard_map/sort_tiles/pallas_call | solution.py:128
  22.2 1.0 copy-done.3
  23.2 0.0 collective-permute-done.received
  23.2 0.1 payload.2
  23.3 7.8 %collective-permute-start.1 = (bf16[4,128,1024]{2,1,0:T(8,128)(2,1)S(1)}, bf16[4,128,1024]{2,1,0:T(8,128)(2,1)S(1)}, u32[]{:S(2)}, u32[]{:S(2)}) collective-permute-start(bf16[4,128,1024]{2,1,0:T(8,128)(2,1)S(1)} %payload.2), channel_id=1, source_target_pairs={{4,0},{5,1},{6,2},{7,3},{8,12},{9,13},{10,14},{11,15},{0,8},{1,9},... | collective-permute-start | bytes 3145736 | tf_op jit(solution)/shard_map/ppermute | solution.py:411
  31.1 0.0 collective-permute-done.8
  31.1 0.5 slice_bitcast_fusion
  31.6 0.0 collective-permute-done.3.refs_1_
  31.6 0.0 collective-permute-done.2.refs_2_
  31.6 0.6 collective-permute-done.4.refs_6_
  32.2 0.7 collective-permute-start.9
  32.9 0.1 collective-permute-start.7
  33.0 1.6 collective-permute-start.6
  34.6 0.2 collective-permute-start.5
  34.8 4.1 %tables.5.far_table.table = s32[273]{0:T(512)} custom-call(s32[96]{0:T(128)} %get-tuple-element.146.rows, s32[96]{0:T(128)} %get-tuple-element.145.cols), custom_call_target="tpu_custom_call" | custom-call | flops 4000000000 | tf_op jit(solution)/shard_map/tables/pallas_call | solution.py:86
  38.9 4.2 %tables.4.own_table = s32[289]{0:T(512)} custom-call(s32[96]{0:T(128)} %fusion.6.rows, s32[96]{0:T(128)} %cols.3), custom_call_target="tpu_custom_call" | custom-call | tf_op jit(solution)/shard_map/tables/pallas_call | solution.py:86
  43.1 1.7 compare_convert_fusion.perm_ref
  44.8 8.3 %collective-permute-done.1.refs_0_ = bf16[4,128,1024]{2,1,0:T(8,128)(2,1)S(1)} collective-permute-done((bf16[4,128,1024]{2,1,0:T(8,128)(2,1)S(1)}, bf16[4,128,1024]{2,1,0:T(8,128)(2,1)S(1)}, u32[]{:S(2)}, u32[]{:S(2)}) %collective-permute-start.1) | collective-permute-done | bytes 1048608 | tf_op jit(solution)/shard_map/ppermute | solution.py:411
  53.1 0.1 broadcast_select_fusion.refs_4_
  53.2 0.0 collective-permute-done.5.refs_7_
  53.3 5.6 %collective-permute-done.6.refs_8_ = bf16[4,128,1024]{2,1,0:T(8,128)(2,1)} collective-permute-done((bf16[4,128,1024]{2,1,0:T(8,128)(2,1)}, bf16[4,128,1024]{2,1,0:T(8,128)(2,1)}, u32[]{:S(2)}, u32[]{:S(2)}) %collective-permute-start.6) | collective-permute-done | bytes 1048608 | tf_op jit(solution)/shard_map/ppermute | solution.py:411
  58.9 0.1 payload.3
  59.0 1.0 copy-done.2
  60.0 19.6 %collective-permute-start.10 = (bf16[4,128,1024]{2,1,0:T(8,128)(2,1)}, bf16[4,128,1024]{2,1,0:T(8,128)(2,1)S(1)}, u32[]{:S(2)}, u32[]{:S(2)}) collective-permute-start(bf16[4,128,1024]{2,1,0:T(8,128)(2,1)} %copy-done.2), channel_id=1, source_target_pairs={{4,0},{5,1},{6,2},{7,3},{8,12},{9,13},{10,14},{11,15},{0,8},{1,9},... | collective-permute-start | bytes 3145736 | tf_op jit(solution)/shard_map/ppermute | solution.py:411
  79.6 1.5 collective-permute-start.11
  81.2 1.3 collective-permute-start.20
  82.4 0.0 collective-permute-done.12.refs_5_
  82.5 6.8 %collective-permute-start.16 = (bf16[32,128,128]{2,1,0:T(8,128)(2,1)}, bf16[32,128,128]{2,1,0:T(8,128)(2,1)S(1)}, u32[]{:S(2)}, u32[]{:S(2)}) collective-permute-start(bf16[32,128,128]{2,1,0:T(8,128)(2,1)} %get-tuple-element.121), channel_id=1, source_target_pairs={{0,8},{1,9},{2,10},{3,11},{12,4},{13,5},{14,6},{15,7},{16,24},{17,... | collective-permute-start | bytes 3145736 | tf_op jit(solution)/shard_map/ppermute | solution.py:411
  89.2 14.3 %collective-permute-done.10.refs_1_.refs_0_ = bf16[4,128,1024]{2,1,0:T(8,128)(2,1)S(1)} collective-permute-done((bf16[4,128,1024]{2,1,0:T(8,128)(2,1)}, bf16[4,128,1024]{2,1,0:T(8,128)(2,1)S(1)}, u32[]{:S(2)}, u32[]{:S(2)}) %collective-permute-start.10) | collective-permute-done | bytes 1048608 | tf_op jit(solution)/shard_map/ppermute | solution.py:411
  103.5 2.3 %slice_select_fusion = (bf16[2,128,1024]{2,1,0:T(8,128)(2,1)}, bf16[2,128,1024]{2,1,0:T(8,128)(2,1)}) fusion(bf16[4,128,1024]{2,1,0:T(8,128)(2,1)S(1)} %collective-permute-done.10.refs_1_.refs_0_, bf16[4,128,1024]{2,1,0:T(8,128)(2,1)} %copy-done.2, pred[]{:T(512)S(6)} %or.6), kind=kLoop, calls=%fused_computation.2 | loop fusion | flops 524288 | bytes 3145729 | tf_op jit(solution)/shard_map/jit(_where)/select_n | solution.py:481
  105.8 1.0 copy-done.8
  106.8 1.5 collective-permute-start.14
  108.3 0.5 collective-permute-start.15
  108.9 0.7 stack.89.firsts
  109.5 23.6 %own_part.2 = (f32[16,128,1024]{2,1,0:T(8,128)}, bf16[32,128,1024]{2,1,0:T(8,128)(2,1)}) custom-call(s32[289]{0:T(512)} %tables.4.own_table, s32[273]{0:T(512)} %tables.5.far_table.table, s32[11]{0:T(128)} %stack.89.firsts, bf16[96,128,128]{2,1,0:T(8,128)(2,1)} %tiles_ref.5, bf16[1024,1024]{1,0:T(8,128)(2,1)} %compare_convert_fusion.perm_ref, ...), custom_call_target="tpu_custom_call" | custom-call | tf_op jit(solution)/shard_map/own_part/pallas_call | solution.py:265
  133.1 0.1 collective-permute-start.22
  133.2 0.5 collective-permute-start.23
  133.7 0.1 collective-permute-start.21
  133.8 0.4 collective-permute-start.24
  134.2 1.1 collective-permute-done.22.refs_3_
  135.3 0.1 collective-permute-start.25
  135.4 1.4 collective-permute-done.23.refs_4_
  136.8 1.3 collective-permute-start.19
  138.1 0.2 collective-permute-done.24.refs_7_
  138.3 1.3 collective-permute-start.18
  139.6 0.8 copy-done.12
  140.4 1.3 collective-permute-start.17
  141.7 0.7 stack.99.firsts
  142.4 14.7 %own_part.3 = (f32[16,128,1024]{2,1,0:T(8,128)}, bf16[32,128,1024]{2,1,0:T(8,128)(2,1)}) custom-call(s32[289]{0:T(512)} %tables.4.own_table, s32[273]{0:T(512)} %tables.5.far_table.table, s32[9]{0:T(128)} %stack.99.firsts, bf16[96,128,128]{2,1,0:T(8,128)(2,1)} %tiles_ref.5, ...), custom_call_target="tpu_custom_call", output_to_operand_aliasing={{0}: (14, {}), {1}: (15, {})} | custom-call | tf_op jit(solution)/shard_map/own_part/pallas_call | solution.py:265
  157.1 11.9 %collective-permute-done.20.refs_2_ = bf16[60,128,128]{2,1,0:T(8,128)(2,1)} collective-permute-done((bf16[60,128,128]{2,1,0:T(8,128)(2,1)}, bf16[60,128,128]{2,1,0:T(8,128)(2,1)}, u32[]{:S(2)}, u32[]{:S(2)}) %collective-permute-start.20) | collective-permute-done | bytes 1966112 | tf_op jit(solution)/shard_map/ppermute | solution.py:411
  169.0 3.4 %copy-done = f32[16,128,1024]{2,1,0:T(8,128)S(1)} copy-done((f32[16,128,1024]{2,1,0:T(8,128)S(1)}, f32[16,128,1024]{2,1,0:T(8,128)}, u32[]{:S(2)}) %copy-start) | copy-done | bytes 8388632
  172.4 12.3 %far_part.4 = (f32[16,128,1024]{2,1,0:T(8,128)S(1)}, bf16[16,128,1024]{2,1,0:T(8,128)(2,1)}) custom-call(s32[273]{0:T(512)S(1)} %copy-done.5, s32[1]{0:T(128)} %bitcast.chosen.at_end, bf16[4,128,1024]{2,1,0:T(8,128)(2,1)S(1)} %collective-permute-done.1.refs_0_, ...), custom_call_target="tpu_custom_call", output_to_operand_aliasing={{0}: (5, {})} | custom-call | tf_op jit(solution)/shard_map/far_part/pallas_call | solution.py:385
  184.8 5.3 %far_part.5 = (f32[16,128,1024]{2,1,0:T(8,128)S(1)}, bf16[16,128,1024]{2,1,0:T(8,128)(2,1)}) custom-call(s32[273]{0:T(512)S(1)} %copy-done.5, s32[1]{0:T(128)} %bitcast.chosen.at_end, bf16[4,128,1024]{2,1,0:T(8,128)(2,1)S(1)} %collective-permute-done.10.refs_1_.refs_0_, ...), custom_call_target="tpu_custom_call", output_to_operand_aliasing={{0}: (5, {}), {1}: (7, {})} | custom-call | tf_op jit(solution)/shard_map/far_part/pallas_call | solution.py:385
  190.1 4.3 %far_part.6 = (f32[16,128,1024]{2,1,0:T(8,128)S(1)}, bf16[16,128,1024]{2,1,0:T(8,128)(2,1)}) custom-call(s32[273]{0:T(512)S(1)} %copy-done.5, s32[1]{0:T(128)} %bitcast.chosen.at_end, bf16[32,128,128]{2,1,0:T(8,128)(2,1)S(1)} %collective-permute-done.16.refs_1_.refs_0_, ...), custom_call_target="tpu_custom_call", output_to_operand_aliasing={{0}: (4, {}), {1}: (6, {})} | custom-call | tf_op jit(solution)/shard_map/far_part/pallas_call | solution.py:385
  194.4 3.5 %far_part.7 = (f32[16,128,1024]{2,1,0:T(8,128)S(1)}, bf16[16,128,1024]{2,1,0:T(8,128)(2,1)}) custom-call(s32[273]{0:T(512)S(1)} %copy-done.5, s32[1]{0:T(128)} %bitcast.chosen.at_end, bf16[32,128,128]{2,1,0:T(8,128)(2,1)S(1)} %collective-permute-done.16.refs_1_.refs_0_, ...), custom_call_target="tpu_custom_call", output_to_operand_aliasing={{0}: (4, {}), {1}: (6, {})} | custom-call | tf_op jit(solution)/shard_map/far_part/pallas_call | solution.py:385
  (36 shorter events, 0.1 us)
Async XLA Ops:
  0.0 23.2 %collective-permute-start = (bf16[4,128,1024]{2,1,0:T(8,128)(2,1)}, bf16[4,128,1024]{2,1,0:T(8,128)(2,1)S(1)}, u32[]{:S(2)}, u32[]{:S(2)}) collective-permute-start(bf16[4,128,1024]{2,1,0:T(8,128)(2,1)} %refs_0_.1), channel_id=1, source_target_pairs={{4,8},{5,9},{6,10},{7,11},{8,4},{9,5},{10,6},{11,7},{20,24},{21,25... | collective-permute-start | bytes 3145736 | tf_op jit(solution)/shard_map/ppermute | solution.py:411
  0.7 30.9 %collective-permute-start.3 = (bf16[4,128,1024]{2,1,0:T(8,128)(2,1)}, bf16[4,128,1024]{2,1,0:T(8,128)(2,1)}, u32[]{:S(2)}, u32[]{:S(2)}) collective-permute-start(bf16[4,128,1024]{2,1,0:T(8,128)(2,1)} %refs_0_.1), channel_id=1, source_target_pairs={{0,1},{1,0},{2,3},{3,2},{4,5},{5,4},{6,7},{7,6},{8,9},{9,8},{10,11... | collective-permute-start | bytes 3145736 | tf_op jit(solution)/shard_map/ppermute | solution.py:411
  1.2 30.4 %collective-permute-start.2 = (bf16[4,128,1024]{2,1,0:T(8,128)(2,1)}, bf16[4,128,1024]{2,1,0:T(8,128)(2,1)}, u32[]{:S(2)}, u32[]{:S(2)}) collective-permute-start(bf16[4,128,1024]{2,1,0:T(8,128)(2,1)} %refs_0_.1), channel_id=1, source_target_pairs={{0,4},{1,5},{2,6},{3,7},{4,0},{5,1},{6,2},{7,3},{8,12},{9,13},{10,... | collective-permute-start | bytes 3145736 | tf_op jit(solution)/shard_map/ppermute | solution.py:411
  6.7 25.5 %collective-permute-start.4 = (bf16[4,128,1024]{2,1,0:T(8,128)(2,1)}, bf16[4,128,1024]{2,1,0:T(8,128)(2,1)}, u32[]{:S(2)}, u32[]{:S(2)}) collective-permute-start(bf16[4,128,1024]{2,1,0:T(8,128)(2,1)} %refs_0_.1), channel_id=1, source_target_pairs={{0,2},{1,3},{2,0},{3,1},{4,6},{5,7},{6,4},{7,5},{8,10},{9,11},{10,... | collective-permute-start | bytes 3145736 | tf_op jit(solution)/shard_map/ppermute | solution.py:411
  8.9 22.3 %collective-permute-start.8 = (s32[2,96]{1,0:T(2,128)S(1)}, s32[2,96]{1,0:T(2,128)S(1)}, u32[]{:S(2)}, u32[]{:S(2)}) collective-permute-start(s32[2,96]{1,0:T(2,128)S(1)} %pad_add_fusion), channel_id=1, source_target_pairs={{0,8},{1,9},{2,10},{3,11},{4,12},{5,13},{6,14},{7,15},{8,0},{9,1},... | collective-permute-start | bytes 2312 | tf_op jit(solution)/shard_map/ppermute | solution.py:411
  14.3 1.9 copy-start.1
  16.2 0.7 copy-start.6
  22.2 1.0 copy-start.3
  23.3 29.8 %collective-permute-start.1 = (bf16[4,128,1024]{2,1,0:T(8,128)(2,1)S(1)}, bf16[4,128,1024]{2,1,0:T(8,128)(2,1)S(1)}, u32[]{:S(2)}, u32[]{:S(2)}) collective-permute-start(bf16[4,128,1024]{2,1,0:T(8,128)(2,1)S(1)} %payload.2), channel_id=1, source_target_pairs={{4,0},{5,1},{6,2},{7,3},{8,12},{9,13},{10,14},{11,15},{0,8},{1,9},... | collective-permute-start | bytes 3145736 | tf_op jit(solution)/shard_map/ppermute | solution.py:411
  32.2 26.7 %collective-permute-start.9 = (bf16[4,128,1024]{2,1,0:T(8,128)(2,1)}, bf16[4,128,1024]{2,1,0:T(8,128)(2,1)S(1)}, u32[]{:S(2)}, u32[]{:S(2)}) collective-permute-start(bf16[4,128,1024]{2,1,0:T(8,128)(2,1)} %collective-permute-done.2.refs_2_), channel_id=1, source_target_pairs={{4,8},{5,9},{6,10},{7,11},{8,4},{9,5},{10,6},{11,7},{20,24},{21,25... | collective-permute-start | bytes 3145736 | tf_op jit(solution)/shard_map/ppermute | solution.py:411
  32.9 20.3 %collective-permute-start.7 = (bf16[4,128,1024]{2,1,0:T(8,128)(2,1)}, bf16[4,128,1024]{2,1,0:T(8,128)(2,1)}, u32[]{:S(2)}, u32[]{:S(2)}) collective-permute-start(bf16[4,128,1024]{2,1,0:T(8,128)(2,1)} %collective-permute-done.2.refs_2_), channel_id=1, source_target_pairs={{0,1},{1,0},{2,3},{3,2},{4,5},{5,4},{6,7},{7,6},{8,9},{9,8},{10,11... | collective-permute-start | bytes 3145736 | tf_op jit(solution)/shard_map/ppermute | solution.py:411
  33.0 25.9 %collective-permute-start.6 = (bf16[4,128,1024]{2,1,0:T(8,128)(2,1)}, bf16[4,128,1024]{2,1,0:T(8,128)(2,1)}, u32[]{:S(2)}, u32[]{:S(2)}) collective-permute-start(bf16[4,128,1024]{2,1,0:T(8,128)(2,1)} %collective-permute-done.2.refs_2_), channel_id=1, source_target_pairs={{0,2},{1,3},{2,0},{3,1},{4,6},{5,7},{6,4},{7,5},{8,10},{9,11},{10,... | collective-permute-start | bytes 3145736 | tf_op jit(solution)/shard_map/ppermute | solution.py:411
  34.6 18.6 %collective-permute-start.5 = (bf16[4,128,1024]{2,1,0:T(8,128)(2,1)}, bf16[4,128,1024]{2,1,0:T(8,128)(2,1)}, u32[]{:S(2)}, u32[]{:S(2)}) collective-permute-start(bf16[4,128,1024]{2,1,0:T(8,128)(2,1)} %collective-permute-done.4.refs_6_), channel_id=1, source_target_pairs={{0,1},{1,0},{2,3},{3,2},{4,5},{5,4},{6,7},{7,6},{8,9},{9,8},{10,11... | collective-permute-start | bytes 3145736 | tf_op jit(solution)/shard_map/ppermute | solution.py:411
  43.0 15.9 %copy-start.4 = (bf16[4,128,1024]{2,1,0:T(8,128)(2,1)S(1)}, bf16[4,128,1024]{2,1,0:T(8,128)(2,1)}, u32[]{:S(2)}) copy-start(bf16[4,128,1024]{2,1,0:T(8,128)(2,1)} %copy-done.3) | copy-start | bytes 3145732
  53.2 50.3 %copy-start.7 = (bf16[4,128,1024]{2,1,0:T(8,128)(2,1)}, bf16[4,128,1024]{2,1,0:T(8,128)(2,1)S(1)}, u32[]{:S(2)}) copy-start(bf16[4,128,1024]{2,1,0:T(8,128)(2,1)S(1)} %broadcast_select_fusion.refs_4_) | copy-start | bytes 3145732
  58.9 23.6 %collective-permute-start.12 = (bf16[4,128,1024]{2,1,0:T(8,128)(2,1)S(1)}, bf16[4,128,1024]{2,1,0:T(8,128)(2,1)}, u32[]{:S(2)}, u32[]{:S(2)}) collective-permute-start(bf16[4,128,1024]{2,1,0:T(8,128)(2,1)S(1)} %broadcast_select_fusion.refs_4_), channel_id=1, source_target_pairs={{0,1},{1,0},{2,3},{3,2},{4,5},{5,4},{6,7},{7,6},{8,9},{9,8},{10,11... | collective-permute-start | bytes 3145736 | tf_op jit(solution)/shard_map/ppermute | solution.py:411
  59.0 1.0 copy-start.2
  60.0 43.5 %collective-permute-start.10 = (bf16[4,128,1024]{2,1,0:T(8,128)(2,1)}, bf16[4,128,1024]{2,1,0:T(8,128)(2,1)S(1)}, u32[]{:S(2)}, u32[]{:S(2)}) collective-permute-start(bf16[4,128,1024]{2,1,0:T(8,128)(2,1)} %copy-done.2), channel_id=1, source_target_pairs={{4,0},{5,1},{6,2},{7,3},{8,12},{9,13},{10,14},{11,15},{0,8},{1,9},... | collective-permute-start | bytes 3145736 | tf_op jit(solution)/shard_map/ppermute | solution.py:411
  79.6 26.2 %collective-permute-start.13 = (bf16[4,128,1024]{2,1,0:T(8,128)(2,1)}, bf16[4,128,1024]{2,1,0:T(8,128)(2,1)S(1)}, u32[]{:S(2)}, u32[]{:S(2)}) collective-permute-start(bf16[4,128,1024]{2,1,0:T(8,128)(2,1)} %collective-permute-done.6.refs_8_), channel_id=1, source_target_pairs={{0,1},{1,0},{2,3},{3,2},{4,5},{5,4},{6,7},{7,6},{8,9},{9,8},{10,11... | collective-permute-start | bytes 3145736 | tf_op jit(solution)/shard_map/ppermute | solution.py:411
  79.6 26.2 %collective-permute-start.11 = (bf16[4,128,1024]{2,1,0:T(8,128)(2,1)S(1)}, bf16[4,128,1024]{2,1,0:T(8,128)(2,1)}, u32[]{:S(2)}, u32[]{:S(2)}) collective-permute-start(bf16[4,128,1024]{2,1,0:T(8,128)(2,1)S(1)} %broadcast_select_fusion.refs_4_), channel_id=1, source_target_pairs={{0,2},{1,3},{2,0},{3,1},{4,6},{5,7},{6,4},{7,5},{8,10},{9,11},{10,... | collective-permute-start | bytes 3145736 | tf_op jit(solution)/shard_map/ppermute | solution.py:411
  81.2 87.9 %collective-permute-start.20 = (bf16[60,128,128]{2,1,0:T(8,128)(2,1)}, bf16[60,128,128]{2,1,0:T(8,128)(2,1)}, u32[]{:S(2)}, u32[]{:S(2)}) collective-permute-start(bf16[60,128,128]{2,1,0:T(8,128)(2,1)} %get-tuple-element.126), channel_id=1, source_target_pairs={{4,12},{5,13},{6,14},{7,15},{8,0},{9,1},{10,2},{11,3},{20,28},{21,... | collective-permute-start | bytes 5898248 | tf_op jit(solution)/shard_map/ppermute | solution.py:411
  82.5 51.3 %collective-permute-start.16 = (bf16[32,128,128]{2,1,0:T(8,128)(2,1)}, bf16[32,128,128]{2,1,0:T(8,128)(2,1)S(1)}, u32[]{:S(2)}, u32[]{:S(2)}) collective-permute-start(bf16[32,128,128]{2,1,0:T(8,128)(2,1)} %get-tuple-element.121), channel_id=1, source_target_pairs={{0,8},{1,9},{2,10},{3,11},{12,4},{13,5},{14,6},{15,7},{16,24},{17,... | collective-permute-start | bytes 3145736 | tf_op jit(solution)/shard_map/ppermute | solution.py:411
  105.8 1.0 copy-start.8
  106.8 26.3 %collective-permute-start.14 = (bf16[2,128,1024]{2,1,0:T(8,128)(2,1)}, bf16[2,128,1024]{2,1,0:T(8,128)(2,1)}, u32[]{:S(2)}, u32[]{:S(2)}) collective-permute-start(bf16[2,128,1024]{2,1,0:T(8,128)(2,1)} %get-tuple-element.128.refs_1_), channel_id=1, source_target_pairs={{0,2},{1,3},{2,0},{3,1},{4,6},{5,7},{6,4},{7,5},{8,10},{9,11},{10,... | collective-permute-start | bytes 1572872 | tf_op jit(solution)/shard_map/ppermute | solution.py:411
  108.3 24.8 %collective-permute-start.15 = (bf16[2,128,1024]{2,1,0:T(8,128)(2,1)}, bf16[2,128,1024]{2,1,0:T(8,128)(2,1)}, u32[]{:S(2)}, u32[]{:S(2)}) collective-permute-start(bf16[2,128,1024]{2,1,0:T(8,128)(2,1)} %get-tuple-element.129.refs_2_), channel_id=1, source_target_pairs={{0,2},{1,3},{2,0},{3,1},{4,6},{5,7},{6,4},{7,5},{8,10},{9,11},{10,... | collective-permute-start | bytes 1572872 | tf_op jit(solution)/shard_map/ppermute | solution.py:411
  133.1 2.2 %collective-permute-start.22 = (bf16[2,128,1024]{2,1,0:T(8,128)(2,1)}, bf16[2,128,1024]{2,1,0:T(8,128)(2,1)S(1)}, u32[]{:S(2)}, u32[]{:S(2)}) collective-permute-start(bf16[2,128,1024]{2,1,0:T(8,128)(2,1)} %get-tuple-element.128.refs_1_), channel_id=1, source_target_pairs={{0,1},{1,0},{2,3},{3,2},{4,5},{5,4},{6,7},{7,6},{8,9},{9,8},{10,11... | collective-permute-start | bytes 1572872 | tf_op jit(solution)/shard_map/ppermute | solution.py:411
  133.2 3.6 %collective-permute-start.23 = (bf16[2,128,1024]{2,1,0:T(8,128)(2,1)}, bf16[2,128,1024]{2,1,0:T(8,128)(2,1)S(1)}, u32[]{:S(2)}, u32[]{:S(2)}) collective-permute-start(bf16[2,128,1024]{2,1,0:T(8,128)(2,1)} %get-tuple-element.129.refs_2_), channel_id=1, source_target_pairs={{0,1},{1,0},{2,3},{3,2},{4,5},{5,4},{6,7},{7,6},{8,9},{9,8},{10,11... | collective-permute-start | bytes 1572872 | tf_op jit(solution)/shard_map/ppermute | solution.py:411
  133.7 8.7 %collective-permute-start.21 = (bf16[4,128,1024]{2,1,0:T(8,128)(2,1)}, bf16[4,128,1024]{2,1,0:T(8,128)(2,1)}, u32[]{:S(2)}, u32[]{:S(2)}) collective-permute-start(bf16[4,128,1024]{2,1,0:T(8,128)(2,1)} %collective-permute-done.11.refs_10_), channel_id=1, source_target_pairs={{0,1},{1,0},{2,3},{3,2},{4,5},{5,4},{6,7},{7,6},{8,9},{9,8},{10,11... | collective-permute-start | bytes 3145736 | tf_op jit(solution)/shard_map/ppermute | solution.py:411
  133.8 4.5 %collective-permute-start.24 = (bf16[2,128,1024]{2,1,0:T(8,128)(2,1)}, bf16[2,128,1024]{2,1,0:T(8,128)(2,1)S(1)}, u32[]{:S(2)}, u32[]{:S(2)}) collective-permute-start(bf16[2,128,1024]{2,1,0:T(8,128)(2,1)} %collective-permute-done.14.refs_5_), channel_id=1, source_target_pairs={{0,1},{1,0},{2,3},{3,2},{4,5},{5,4},{6,7},{7,6},{8,9},{9,8},{10,11... | collective-permute-start | bytes 1572872 | tf_op jit(solution)/shard_map/ppermute | solution.py:411
  135.3 2.8 %copy-start.9 = (bf16[2,128,1024]{2,1,0:T(8,128)(2,1)}, bf16[2,128,1024]{2,1,0:T(8,128)(2,1)S(1)}, u32[]{:S(2)}) copy-start(bf16[2,128,1024]{2,1,0:T(8,128)(2,1)S(1)} %collective-permute-done.22.refs_3_) | copy-start | bytes 1572868
  135.3 4.3 %collective-permute-start.25 = (bf16[2,128,1024]{2,1,0:T(8,128)(2,1)}, bf16[2,128,1024]{2,1,0:T(8,128)(2,1)S(1)}, u32[]{:S(2)}, u32[]{:S(2)}) collective-permute-start(bf16[2,128,1024]{2,1,0:T(8,128)(2,1)} %collective-permute-done.15.refs_6_), channel_id=1, source_target_pairs={{0,1},{1,0},{2,3},{3,2},{4,5},{5,4},{6,7},{7,6},{8,9},{9,8},{10,11... | collective-permute-start | bytes 1572872 | tf_op jit(solution)/shard_map/ppermute | solution.py:411
  136.8 1.5 copy-start.10
  136.8 47.9 %collective-permute-start.19 = (bf16[18,128,128]{2,1,0:T(8,128)(2,1)}, bf16[18,128,128]{2,1,0:T(8,128)(2,1)}, u32[]{:S(2)}, u32[]{:S(2)}) collective-permute-start(bf16[18,128,128]{2,1,0:T(8,128)(2,1)} %get-tuple-element.125), channel_id=1, source_target_pairs={{4,12},{5,13},{6,14},{7,15},{8,0},{9,1},{10,2},{11,3},{20,28},{21,... | collective-permute-start | bytes 1769480 | tf_op jit(solution)/shard_map/ppermute | solution.py:411
  138.3 1.3 copy-start.11
  138.3 51.8 %collective-permute-start.18 = (bf16[12,128,128]{2,1,0:T(8,128)(2,1)}, bf16[12,128,128]{2,1,0:T(8,128)(2,1)S(1)}, u32[]{:S(2)}, u32[]{:S(2)}) collective-permute-start(bf16[12,128,128]{2,1,0:T(8,128)(2,1)} %get-tuple-element.124), channel_id=1, source_target_pairs={{4,12},{5,13},{6,14},{7,15},{8,0},{9,1},{10,2},{11,3},{20,28},{21,... | collective-permute-start | bytes 1179656 | tf_op jit(solution)/shard_map/ppermute | solution.py:411
  139.6 0.8 copy-start.12
  140.4 54.0 %collective-permute-start.17 = (bf16[6,128,128]{2,1,0:T(8,128)(2,1)}, bf16[6,128,128]{2,1,0:T(8,128)(2,1)}, u32[]{:S(2)}, u32[]{:S(2)}) collective-permute-start(bf16[6,128,128]{2,1,0:T(8,128)(2,1)} %get-tuple-element.123), channel_id=1, source_target_pairs={{4,12},{5,13},{6,14},{7,15},{8,0},{9,1},{10,2},{11,3},{20,28},{21,... | collective-permute-start | bytes 589832 | tf_op jit(solution)/shard_map/ppermute | solution.py:411
  142.4 26.6 %copy-start.5 = (s32[273]{0:T(512)S(1)}, s32[273]{0:T(512)}, u32[]{:S(2)}) copy-start(s32[273]{0:T(512)} %tables.5.far_table.table) | copy-start | bytes 3280
  169.0 3.4 %copy-start = (f32[16,128,1024]{2,1,0:T(8,128)S(1)}, f32[16,128,1024]{2,1,0:T(8,128)}, u32[]{:S(2)}) copy-start(f32[16,128,1024]{2,1,0:T(8,128)} %get-tuple-element.134.refs_3_) | copy-start | bytes 25165828

commit v16 on v15

--- a/solution.py
+++ b/solution.py
@@ -281,7 +281,7 @@
             pltpu.SemaphoreType.DMA((need,)),
             pltpu.SemaphoreType.DMA((PPD,)),
         ],
-        compiler_params=pltpu.CompilerParams(vmem_limit_bytes=56 * MIB),
+        compiler_params=pltpu.CompilerParams(vmem_limit_bytes=36 * MIB),
         name="own_part",
     )(own_table, far_table, firsts, tiles, perm, *pieces, *earlier)
 
@@ -291,7 +291,7 @@
     tile_refs, refs = refs[: len(segments)], refs[len(segments) :]
     sum_in, flip_in = refs[:2]
     refs = refs[3:] if base else refs[2:]
-    sum_out, result, tiles_ref, blocks, sums, rounded, tile_sem, block_sems, row_sems, out_sems = refs
+    sum_out, result, tiles_ref, sums, rounded, tile_sem, row_sems, out_sems = refs
     count = tiles_ref.shape[0]
     stop = base + count
 
@@ -310,10 +310,6 @@
                 def _(place):
                     pltpu.make_async_copy(window(source, place - begin), tiles_ref.at[place - base], tile_sem).start()
 
-    @pl.loop(0, count)
-    def _(number):
-        pltpu.make_async_copy(flip_in.at[block_at[base + number]], blocks.at[number], block_sems.at[number]).start()
-
     def each_row(action):
         @pl.loop(0, PPD)
         def _(row):
@@ -335,15 +331,9 @@
     each_row(lambda row, complete: load(row).start())
     pltpu.make_async_copy(tiles_ref, tiles_ref, tile_sem).wait()
 
-
     def add(row, complete):
         begin, end = jnp.maximum(starts[row], base), jnp.minimum(starts[row + 1], stop)
         load(row).wait()
-
-        @pl.loop(0, end - begin)
-        def _(number):
-            block = blocks.at[begin - base + number]
-            pltpu.make_async_copy(block, block, block_sems.at[begin - base + number]).wait()
 
         add_row(
             sums.at[row],
@@ -351,7 +341,7 @@
             end,
             4,
             lambda place: tiles_ref[place - base],
-            lambda place, window: blocks[place - base, :, window],
+            lambda place, window: flip_in[block_at[place], :, window],
         )
 
         @pl.when(complete)
@@ -384,21 +374,19 @@
     aliases = {operand: 0, operand + 2: 1} if given else {operand: 0}
     return pl.pallas_call(
         functools.partial(far_kernel, base, total_count, [segment for segment, _ in used]),
-        in_specs=[SMEM] * 2 + [ANY] * (len(used) + 2 + len(given)),
+        in_specs=[SMEM] * 2 + [ANY] * (len(used) + 1) + [VMEM] + [ANY] * len(given),
         out_specs=[ANY] * 2,
         out_shape=[jax.ShapeDtypeStruct(whole, jnp.float32), jax.ShapeDtypeStruct(whole, jnp.bfloat16)],
         input_output_aliases=aliases,
         scratch_shapes=[
             pltpu.VMEM((count, whole[1], flipped.shape[1]), jnp.bfloat16),
-            pltpu.VMEM((count,) + flipped.shape[1:], jnp.bfloat16),
             pltpu.VMEM(whole, jnp.float32),
             pltpu.VMEM(whole, jnp.bfloat16),
             pltpu.SemaphoreType.DMA,
-            pltpu.SemaphoreType.DMA((count,)),
             pltpu.SemaphoreType.DMA((PPD,)),
             pltpu.SemaphoreType.DMA((PPD,)),
         ],
-        compiler_params=pltpu.CompilerParams(vmem_limit_bytes=40 * MIB),
+        compiler_params=pltpu.CompilerParams(vmem_limit_bytes=26 * MIB),
         name="far_part",
     )(far_table, chosen, *[array for _, array in used], total, flipped, *given)
 

time: 199 us -> 199 us (level)
  local copies, waits for them, and re-layouts: 11.6 us -> 29.7 us
  waiting for transfers between devices: 43.4 us -> 28.2 us
  Pallas kernels: 81.6 us -> 75.8 us
    unnamed x26 -> x60, local copies, waits for them, and re-layouts: 9.73 us -> 29 us
    ppermute x26, waiting for transfers between devices: 43.4 us -> 28.2 us  [send(): return lax.ppermute(value, 'tile', pairs)]
    pallas_call x4, Pallas kernels: 25.4 us -> 20.7 us  [far_part(): pl.pallas_call(functools.partial(far_kernel, base, total_count, [segment...]
    pallas_call x2, Pallas kernels: 38.3 us -> 35.3 us  [own_part(): pl.pallas_call(functools.partial(own_kernel, counts, groups, group, not e...]
  transfers between devices with their start and end apart: 26 -> 26, of which waited for: 8 -> 8; matrix products, arithmetic and copies ran while one was open for 4% -> 4% of each run, Pallas kernels for 39% -> 37%
where the time goes in v16:
time: 199 us; the launch traced here: 197 us
  Pallas kernels  75.8 us (38%)
  starting transfers between devices  55.3 us (28%)
  local copies, waits for them, and re-layouts  29.7 us (15%)
  waiting for transfers between devices  28.2 us (14%)
  other arithmetic  7.36 us (4%)
    ppermute x26, starting transfers between devices, send(): return lax.ppermute(value, 'tile', pairs)  55.3 us
    pallas_call x2, Pallas kernels, own_part(): pl.pallas_call(functools.partial(own_kernel, counts, groups, group, not e...  35.3 us
    unnamed x60, local copies, waits for them, and re-layouts  29 us
    ppermute x26, waiting for transfers between devices, send(): return lax.ppermute(value, 'tile', pairs)  28.2 us
    pallas_call x4, Pallas kernels, far_part(): pl.pallas_call(functools.partial(far_kernel, base, total_count, [segment...  20.7 us
    pallas_call x3, Pallas kernels, tables(): pl.pallas_call(tables_kernel, in_specs=[SMEM] * 2, out_specs=SMEM, out_sh...  12.4 us
    pallas_call x1, Pallas kernels, sort_tiles(): pl.pallas_call(functools.partial(sort_kernel, choices), in_specs=[SMEM] *...  5.37 us
  transfers between devices with their start and end apart: 26, of which 8 were waited for; matrix products, arithmetic and copies ran while one was open for 4% of the time, Pallas kernels for 37%

profile of v16, /device:TPU:0, one launch (start us, length us, event | category | flops | bytes accessed | tf_op | source)
XLA Modules:
  0.0 196.8 jit_solution(17574274811061743858)
XLA Ops:
  0.0 1.6 collective-permute-start
  1.6 0.5 collective-permute-start.3
  2.1 4.6 %collective-permute-start.2 = (bf16[4,128,1024]{2,1,0:T(8,128)(2,1)}, bf16[4,128,1024]{2,1,0:T(8,128)(2,1)}, u32[]{:S(2)}, u32[]{:S(2)}) collective-permute-start(bf16[4,128,1024]{2,1,0:T(8,128)(2,1)} %refs_0_.1), channel_id=1, source_target_pairs={{0,4},{1,5},{2,6},{3,7},{4,0},{5,1},{6,2},{7,3},{8,12},{9,13},{10,... | collective-permute-start | bytes 3145736 | tf_op jit(solution)/shard_map/ppermute | solution.py:399
  6.7 1.5 collective-permute-start.4
  8.2 0.7 pad_add_fusion
  8.9 0.6 collective-permute-start.8
  9.4 4.1 %tables.3.table = s32[273]{0:T(512)} custom-call(s32[96]{0:T(128)} %rows.1, s32[96]{0:T(128)} %cols.3), custom_call_target="tpu_custom_call" | custom-call | tf_op jit(solution)/shard_map/tables/pallas_call | solution.py:86
  13.6 1.3 fusion.6.rows
  14.9 1.9 copy-done.2
  16.8 0.7 copy-done.29
  17.4 5.4 %sort_tiles.1 = (bf16[4,128,1024]{2,1,0:T(8,128)(2,1)S(1)}, bf16[4,128,1024]{2,1,0:T(8,128)(2,1)S(1)}, bf16[32,128,128]{2,1,0:T(8,128)(2,1)}, bf16[60,128,128]{2...) custom-call(s32[273]{0:T(512)S(1)} %copy-done.29, ...), custom_call_target="tpu_custom_call" | custom-call | tf_op jit(solution)/shard_map/sort_tiles/pallas_call | solution.py:128
  22.8 1.1 payload.2
  23.9 7.3 %collective-permute-start.1 = (bf16[4,128,1024]{2,1,0:T(8,128)(2,1)}, bf16[4,128,1024]{2,1,0:T(8,128)(2,1)}, u32[]{:S(2)}, u32[]{:S(2)}) collective-permute-start(bf16[4,128,1024]{2,1,0:T(8,128)(2,1)} %payload.2), channel_id=1, source_target_pairs={{4,0},{5,1},{6,2},{7,3},{8,12},{9,13},{10,14},{11,15},{0,8},{1,9},... | collective-permute-start | bytes 3145736 | tf_op jit(solution)/shard_map/ppermute | solution.py:399
  31.2 0.6 slice_bitcast_fusion
  32.2 1.6 collective-permute-start.9
  33.8 1.5 collective-permute-start.6
  35.6 4.1 %tables.5.far_table.table = s32[273]{0:T(512)} custom-call(s32[96]{0:T(128)} %get-tuple-element.146.rows, s32[96]{0:T(128)} %get-tuple-element.145.cols), custom_call_target="tpu_custom_call" | custom-call | flops 4000000000 | tf_op jit(solution)/shard_map/tables/pallas_call | solution.py:86
  39.7 4.2 %tables.4.own_table = s32[289]{0:T(512)} custom-call(s32[96]{0:T(128)} %fusion.6.rows, s32[96]{0:T(128)} %cols.3), custom_call_target="tpu_custom_call" | custom-call | tf_op jit(solution)/shard_map/tables/pallas_call | solution.py:86
  43.9 1.7 compare_convert_fusion.perm_ref
  45.7 7.6 %collective-permute-done.1.refs_0_ = bf16[4,128,1024]{2,1,0:T(8,128)(2,1)} collective-permute-done((bf16[4,128,1024]{2,1,0:T(8,128)(2,1)}, bf16[4,128,1024]{2,1,0:T(8,128)(2,1)}, u32[]{:S(2)}, u32[]{:S(2)}) %collective-permute-start.1) | collective-permute-done | bytes 1048608 | tf_op jit(solution)/shard_map/ppermute | solution.py:399
  53.2 1.3 broadcast_select_fusion.refs_4_
  54.6 5.1 %collective-permute-done.6.refs_8_ = bf16[4,128,1024]{2,1,0:T(8,128)(2,1)} collective-permute-done((bf16[4,128,1024]{2,1,0:T(8,128)(2,1)}, bf16[4,128,1024]{2,1,0:T(8,128)(2,1)}, u32[]{:S(2)}, u32[]{:S(2)}) %collective-permute-start.6) | collective-permute-done | bytes 1048608 | tf_op jit(solution)/shard_map/ppermute | solution.py:399
  59.7 1.0 payload.3
  60.7 18.3 %collective-permute-start.10 = (bf16[4,128,1024]{2,1,0:T(8,128)(2,1)}, bf16[4,128,1024]{2,1,0:T(8,128)(2,1)S(1)}, u32[]{:S(2)}, u32[]{:S(2)}) collective-permute-start(bf16[4,128,1024]{2,1,0:T(8,128)(2,1)} %payload.3), channel_id=1, source_target_pairs={{4,0},{5,1},{6,2},{7,3},{8,12},{9,13},{10,14},{11,15},{0,8},{1,9},... | collective-permute-start | bytes 3145736 | tf_op jit(solution)/shard_map/ppermute | solution.py:399
  79.0 1.5 collective-permute-start.11
  80.5 1.3 collective-permute-start.20
  81.8 1.0 copy-done.13
  82.8 7.7 %collective-permute-start.16 = (bf16[32,128,128]{2,1,0:T(8,128)(2,1)}, bf16[32,128,128]{2,1,0:T(8,128)(2,1)}, u32[]{:S(2)}, u32[]{:S(2)}) collective-permute-start(bf16[32,128,128]{2,1,0:T(8,128)(2,1)} %get-tuple-element.121), channel_id=1, source_target_pairs={{0,8},{1,9},{2,10},{3,11},{12,4},{13,5},{14,6},{15,7},{16,24},{17,... | collective-permute-start | bytes 3145736 | tf_op jit(solution)/shard_map/ppermute | solution.py:399
  90.5 12.4 %collective-permute-done.10.refs_1_.refs_0_ = bf16[4,128,1024]{2,1,0:T(8,128)(2,1)S(1)} collective-permute-done((bf16[4,128,1024]{2,1,0:T(8,128)(2,1)}, bf16[4,128,1024]{2,1,0:T(8,128)(2,1)S(1)}, u32[]{:S(2)}, u32[]{:S(2)}) %collective-permute-start.10) | collective-permute-done | bytes 1048608 | tf_op jit(solution)/shard_map/ppermute | solution.py:399
  102.9 2.3 %slice_select_fusion = (bf16[2,128,1024]{2,1,0:T(8,128)(2,1)}, bf16[2,128,1024]{2,1,0:T(8,128)(2,1)}) fusion(bf16[4,128,1024]{2,1,0:T(8,128)(2,1)S(1)} %collective-permute-done.10.refs_1_.refs_0_, bf16[4,128,1024]{2,1,0:T(8,128)(2,1)} %payload.3, pred[]{:T(512)S(6)} %or.6), kind=kLoop, calls=%fused_computation.2 | loop fusion | flops 524288 | bytes 3145729 | tf_op jit(solution)/shard_map/jit(_where)/select_n | solution.py:469
  105.2 1.0 copy-done.6
  106.2 1.0 copy-done.15
  107.2 1.5 collective-permute-start.14
  108.7 0.5 collective-permute-start.15
  109.3 1.6 copy-done.4
  110.9 1.2 copy-done.9
  112.1 1.2 copy-done.10
  113.4 1.2 copy-done.12
  114.6 1.2 copy-done.14
  115.8 1.2 copy-done.16
  117.0 22.5 %own_part.2 = (f32[16,128,1024]{2,1,0:T(8,128)}, bf16[32,128,1024]{2,1,0:T(8,128)(2,1)}) custom-call(s32[289]{0:T(512)S(1)} %copy-done.28, s32[273]{0:T(512)S(1)} %copy-done.27, s32[11]{0:T(128)S(1)} %stack.89.firsts, bf16[96,128,128]{2,1,0:T(8,128)(2,1)S(1)} %copy-done.3, bf16[1024,1024]{1,0:T(8,128)(2,1)S(1)} %copy-done.4, ...), custom_call_target="tpu_custom_call" | custom-call | tf_op jit(solution)/shard_map/own_part/pallas_call | solution.py:265
  139.6 0.5 collective-permute-start.23
  140.6 1.1 collective-permute-done.22.refs_3_
  141.7 0.8 copy-done.19
  142.6 0.6 collective-permute-done.23.refs_4_
  143.2 0.8 copy-done.21
  144.0 1.3 collective-permute-start.19
  145.3 0.8 copy-done.23
  146.1 1.3 collective-permute-start.18
  147.4 0.8 copy-done.25
  148.3 1.3 collective-permute-start.17
  149.7 1.6 copy-done.5
  151.3 1.0 copy-done.20
  152.3 1.0 copy-done.22
  153.3 1.0 copy-done.24
  154.4 1.0 copy-done.26
  155.4 12.8 %own_part.3 = (f32[16,128,1024]{2,1,0:T(8,128)}, bf16[32,128,1024]{2,1,0:T(8,128)(2,1)}) custom-call(s32[289]{0:T(512)S(1)} %copy-done.28, s32[273]{0:T(512)S(1)} %copy-done.27, s32[9]{0:T(128)S(1)} %stack.99.firsts, bf16[96,128,128]{2,1,0:T(8,128)(2,1)S(1)} %copy-done.3, ...), custom_call_target="tpu_custom_call", output_to_operand_aliasing={{0}: (14, {}), {1}: (15, {})} | custom-call | tf_op jit(solution)/shard_map/own_part/pallas_call | solution.py:265
  168.4 3.4 %copy-done = f32[16,128,1024]{2,1,0:T(8,128)S(1)} copy-done((f32[16,128,1024]{2,1,0:T(8,128)S(1)}, f32[16,128,1024]{2,1,0:T(8,128)}, u32[]{:S(2)}) %copy-start) | copy-done | bytes 8388632
  171.8 3.4 %copy-done.1 = bf16[32,128,1024]{2,1,0:T(8,128)(2,1)S(1)} copy-done((bf16[32,128,1024]{2,1,0:T(8,128)(2,1)S(1)}, bf16[32,128,1024]{2,1,0:T(8,128)(2,1)}, u32[]{:S(2)}) %copy-start.1) | copy-done | bytes 8388632
  175.2 9.4 %far_part.4 = (f32[16,128,1024]{2,1,0:T(8,128)S(1)}, bf16[16,128,1024]{2,1,0:T(8,128)(2,1)}) custom-call(s32[273]{0:T(512)S(1)} %copy-done.27, s32[1]{0:T(128)} %bitcast.chosen.at_end, bf16[4,128,1024]{2,1,0:T(8,128)(2,1)} %collective-permute-done.1.refs_0_, bf16[4,128,1024]{2,1,0:T(8,128)(2,1)S(1)} %copy-done.7, ...), custom_call_target="tpu_custom_call", output_to_operand_aliasing={{0}: (5, {})} | custom-call | tf_op jit(solution)/shard_map/far_part/pallas_call | solution.py:375
  184.6 4.8 %far_part.5 = (f32[16,128,1024]{2,1,0:T(8,128)S(1)}, bf16[16,128,1024]{2,1,0:T(8,128)(2,1)}) custom-call(s32[273]{0:T(512)S(1)} %copy-done.27, s32[1]{0:T(128)} %bitcast.chosen.at_end, bf16[4,128,1024]{2,1,0:T(8,128)(2,1)S(1)} %copy-done.7, ...), custom_call_target="tpu_custom_call", output_to_operand_aliasing={{0}: (5, {}), {1}: (7, {})} | custom-call | tf_op jit(solution)/shard_map/far_part/pallas_call | solution.py:375
  189.4 3.4 %far_part.6 = (f32[16,128,1024]{2,1,0:T(8,128)S(1)}, bf16[16,128,1024]{2,1,0:T(8,128)(2,1)}) custom-call(s32[273]{0:T(512)S(1)} %copy-done.27, s32[1]{0:T(128)} %bitcast.chosen.at_end, bf16[32,128,128]{2,1,0:T(8,128)(2,1)} %collective-permute-done.16.refs_1_.refs_0_, ...), custom_call_target="tpu_custom_call", output_to_operand_aliasing={{0}: (4, {}), {1}: (6, {})} | custom-call | tf_op jit(solution)/shard_map/far_part/pallas_call | solution.py:375
  192.7 0.8 collective-permute-done.17.refs_1_
  193.6 3.2 %far_part.7 = (f32[16,128,1024]{2,1,0:T(8,128)S(1)}, bf16[16,128,1024]{2,1,0:T(8,128)(2,1)}) custom-call(s32[273]{0:T(512)S(1)} %copy-done.27, s32[1]{0:T(128)} %bitcast.chosen.at_end, bf16[32,128,128]{2,1,0:T(8,128)(2,1)} %collective-permute-done.16.refs_1_.refs_0_, ...), custom_call_target="tpu_custom_call", output_to_operand_aliasing={{0}: (4, {}), {1}: (6, {})} | custom-call | tf_op jit(solution)/shard_map/far_part/pallas_call | solution.py:375
  (70 shorter events, 1.8 us)
Async XLA Ops:
  0.0 22.8 %collective-permute-start = (bf16[4,128,1024]{2,1,0:T(8,128)(2,1)}, bf16[4,128,1024]{2,1,0:T(8,128)(2,1)}, u32[]{:S(2)}, u32[]{:S(2)}) collective-permute-start(bf16[4,128,1024]{2,1,0:T(8,128)(2,1)} %refs_0_.1), channel_id=1, source_target_pairs={{4,8},{5,9},{6,10},{7,11},{8,4},{9,5},{10,6},{11,7},{20,24},{21,25... | collective-permute-start | bytes 3145736 | tf_op jit(solution)/shard_map/ppermute | solution.py:399
  1.6 30.2 %collective-permute-start.3 = (bf16[4,128,1024]{2,1,0:T(8,128)(2,1)}, bf16[4,128,1024]{2,1,0:T(8,128)(2,1)S(1)}, u32[]{:S(2)}, u32[]{:S(2)}) collective-permute-start(bf16[4,128,1024]{2,1,0:T(8,128)(2,1)} %refs_0_.1), channel_id=1, source_target_pairs={{0,1},{1,0},{2,3},{3,2},{4,5},{5,4},{6,7},{7,6},{8,9},{9,8},{10,11... | collective-permute-start | bytes 3145736 | tf_op jit(solution)/shard_map/ppermute | solution.py:399
  2.1 29.7 %collective-permute-start.2 = (bf16[4,128,1024]{2,1,0:T(8,128)(2,1)}, bf16[4,128,1024]{2,1,0:T(8,128)(2,1)}, u32[]{:S(2)}, u32[]{:S(2)}) collective-permute-start(bf16[4,128,1024]{2,1,0:T(8,128)(2,1)} %refs_0_.1), channel_id=1, source_target_pairs={{0,4},{1,5},{2,6},{3,7},{4,0},{5,1},{6,2},{7,3},{8,12},{9,13},{10,... | collective-permute-start | bytes 3145736 | tf_op jit(solution)/shard_map/ppermute | solution.py:399
  6.7 25.5 %collective-permute-start.4 = (bf16[4,128,1024]{2,1,0:T(8,128)(2,1)}, bf16[4,128,1024]{2,1,0:T(8,128)(2,1)}, u32[]{:S(2)}, u32[]{:S(2)}) collective-permute-start(bf16[4,128,1024]{2,1,0:T(8,128)(2,1)} %refs_0_.1), channel_id=1, source_target_pairs={{0,2},{1,3},{2,0},{3,1},{4,6},{5,7},{6,4},{7,5},{8,10},{9,11},{10,... | collective-permute-start | bytes 3145736 | tf_op jit(solution)/shard_map/ppermute | solution.py:399
  8.9 22.4 %collective-permute-start.8 = (s32[2,96]{1,0:T(2,128)S(1)}, s32[2,96]{1,0:T(2,128)S(1)}, u32[]{:S(2)}, u32[]{:S(2)}) collective-permute-start(s32[2,96]{1,0:T(2,128)S(1)} %pad_add_fusion), channel_id=1, source_target_pairs={{0,8},{1,9},{2,10},{3,11},{4,12},{5,13},{6,14},{7,15},{8,0},{9,1},... | collective-permute-start | bytes 2312 | tf_op jit(solution)/shard_map/ppermute | solution.py:399
  14.9 1.9 copy-start.2
  16.8 0.7 copy-start.29
  22.8 9.0 %copy-start.17 = (bf16[4,128,1024]{2,1,0:T(8,128)(2,1)}, bf16[4,128,1024]{2,1,0:T(8,128)(2,1)S(1)}, u32[]{:S(2)}) copy-start(bf16[4,128,1024]{2,1,0:T(8,128)(2,1)S(1)} %get-tuple-element.99.tiles_ref) | copy-start | bytes 3145732
  23.9 29.3 %collective-permute-start.1 = (bf16[4,128,1024]{2,1,0:T(8,128)(2,1)}, bf16[4,128,1024]{2,1,0:T(8,128)(2,1)}, u32[]{:S(2)}, u32[]{:S(2)}) collective-permute-start(bf16[4,128,1024]{2,1,0:T(8,128)(2,1)} %payload.2), channel_id=1, source_target_pairs={{4,0},{5,1},{6,2},{7,3},{8,12},{9,13},{10,14},{11,15},{0,8},{1,9},... | collective-permute-start | bytes 3145736 | tf_op jit(solution)/shard_map/ppermute | solution.py:399
  31.8 7.9 %copy-start.11 = (bf16[4,128,1024]{2,1,0:T(8,128)(2,1)}, bf16[4,128,1024]{2,1,0:T(8,128)(2,1)S(1)}, u32[]{:S(2)}) copy-start(bf16[4,128,1024]{2,1,0:T(8,128)(2,1)S(1)} %collective-permute-done.3.refs_1_) | copy-start | bytes 3145732
  32.2 27.5 %collective-permute-start.9 = (bf16[4,128,1024]{2,1,0:T(8,128)(2,1)}, bf16[4,128,1024]{2,1,0:T(8,128)(2,1)}, u32[]{:S(2)}, u32[]{:S(2)}) collective-permute-start(bf16[4,128,1024]{2,1,0:T(8,128)(2,1)} %collective-permute-done.2.refs_2_), channel_id=1, source_target_pairs={{4,8},{5,9},{6,10},{7,11},{8,4},{9,5},{10,6},{11,7},{20,24},{21,25... | collective-permute-start | bytes 3145736 | tf_op jit(solution)/shard_map/ppermute | solution.py:399
  33.8 20.7 %collective-permute-start.7 = (bf16[4,128,1024]{2,1,0:T(8,128)(2,1)}, bf16[4,128,1024]{2,1,0:T(8,128)(2,1)}, u32[]{:S(2)}, u32[]{:S(2)}) collective-permute-start(bf16[4,128,1024]{2,1,0:T(8,128)(2,1)} %collective-permute-done.2.refs_2_), channel_id=1, source_target_pairs={{0,1},{1,0},{2,3},{3,2},{4,5},{5,4},{6,7},{7,6},{8,9},{9,8},{10,11... | collective-permute-start | bytes 3145736 | tf_op jit(solution)/shard_map/ppermute | solution.py:399
  33.8 25.9 %collective-permute-start.6 = (bf16[4,128,1024]{2,1,0:T(8,128)(2,1)}, bf16[4,128,1024]{2,1,0:T(8,128)(2,1)}, u32[]{:S(2)}, u32[]{:S(2)}) collective-permute-start(bf16[4,128,1024]{2,1,0:T(8,128)(2,1)} %collective-permute-done.2.refs_2_), channel_id=1, source_target_pairs={{0,2},{1,3},{2,0},{3,1},{4,6},{5,7},{6,4},{7,5},{8,10},{9,11},{10,... | collective-permute-start | bytes 3145736 | tf_op jit(solution)/shard_map/ppermute | solution.py:399
  35.4 19.2 %collective-permute-start.5 = (bf16[4,128,1024]{2,1,0:T(8,128)(2,1)}, bf16[4,128,1024]{2,1,0:T(8,128)(2,1)}, u32[]{:S(2)}, u32[]{:S(2)}) collective-permute-start(bf16[4,128,1024]{2,1,0:T(8,128)(2,1)} %collective-permute-done.4.refs_6_), channel_id=1, source_target_pairs={{0,1},{1,0},{2,3},{3,2},{4,5},{5,4},{6,7},{7,6},{8,9},{9,8},{10,11... | collective-permute-start | bytes 3145736 | tf_op jit(solution)/shard_map/ppermute | solution.py:399
  43.9 15.8 %copy-start.18 = (bf16[4,128,1024]{2,1,0:T(8,128)(2,1)S(1)}, bf16[4,128,1024]{2,1,0:T(8,128)(2,1)}, u32[]{:S(2)}) copy-start(bf16[4,128,1024]{2,1,0:T(8,128)(2,1)} %copy-done.17) | copy-start | bytes 3145732
  45.6 63.6 %copy-start.3 = (bf16[96,128,128]{2,1,0:T(8,128)(2,1)S(1)}, bf16[96,128,128]{2,1,0:T(8,128)(2,1)}, u32[]{:S(2)}) copy-start(bf16[96,128,128]{2,1,0:T(8,128)(2,1)} %tiles_ref.5) | copy-start | bytes 9437188
  45.6 63.7 %copy-start.27 = (s32[273]{0:T(512)S(1)}, s32[273]{0:T(512)}, u32[]{:S(2)}) copy-start(s32[273]{0:T(512)} %tables.5.far_table.table) | copy-start | bytes 3280
  45.6 63.7 %copy-start.28 = (s32[289]{0:T(512)S(1)}, s32[289]{0:T(512)}, u32[]{:S(2)}) copy-start(s32[289]{0:T(512)} %tables.4.own_table) | copy-start | bytes 3472
  54.6 50.7 %copy-start.8 = (bf16[4,128,1024]{2,1,0:T(8,128)(2,1)}, bf16[4,128,1024]{2,1,0:T(8,128)(2,1)S(1)}, u32[]{:S(2)}) copy-start(bf16[4,128,1024]{2,1,0:T(8,128)(2,1)S(1)} %broadcast_select_fusion.refs_4_) | copy-start | bytes 3145732
  59.7 22.1 %collective-permute-start.12 = (bf16[4,128,1024]{2,1,0:T(8,128)(2,1)S(1)}, bf16[4,128,1024]{2,1,0:T(8,128)(2,1)S(1)}, u32[]{:S(2)}, u32[]{:S(2)}) collective-permute-start(bf16[4,128,1024]{2,1,0:T(8,128)(2,1)S(1)} %broadcast_select_fusion.refs_4_), channel_id=1, source_target_pairs={{0,1},{1,0},{2,3},{3,2},{4,5},{5,4},{6,7},{7,6},{8,9},{9,8},{10,11... | collective-permute-start | bytes 3145736 | tf_op jit(solution)/shard_map/ppermute | solution.py:399
  60.7 42.2 %collective-permute-start.10 = (bf16[4,128,1024]{2,1,0:T(8,128)(2,1)}, bf16[4,128,1024]{2,1,0:T(8,128)(2,1)S(1)}, u32[]{:S(2)}, u32[]{:S(2)}) collective-permute-start(bf16[4,128,1024]{2,1,0:T(8,128)(2,1)} %payload.3), channel_id=1, source_target_pairs={{4,0},{5,1},{6,2},{7,3},{8,12},{9,13},{10,14},{11,15},{0,8},{1,9},... | collective-permute-start | bytes 3145736 | tf_op jit(solution)/shard_map/ppermute | solution.py:399
  79.0 27.2 %collective-permute-start.13 = (bf16[4,128,1024]{2,1,0:T(8,128)(2,1)}, bf16[4,128,1024]{2,1,0:T(8,128)(2,1)S(1)}, u32[]{:S(2)}, u32[]{:S(2)}) collective-permute-start(bf16[4,128,1024]{2,1,0:T(8,128)(2,1)} %collective-permute-done.6.refs_8_), channel_id=1, source_target_pairs={{0,1},{1,0},{2,3},{3,2},{4,5},{5,4},{6,7},{7,6},{8,9},{9,8},{10,11... | collective-permute-start | bytes 3145736 | tf_op jit(solution)/shard_map/ppermute | solution.py:399
  79.0 28.2 %collective-permute-start.11 = (bf16[4,128,1024]{2,1,0:T(8,128)(2,1)S(1)}, bf16[4,128,1024]{2,1,0:T(8,128)(2,1)}, u32[]{:S(2)}, u32[]{:S(2)}) collective-permute-start(bf16[4,128,1024]{2,1,0:T(8,128)(2,1)S(1)} %broadcast_select_fusion.refs_4_), channel_id=1, source_target_pairs={{0,2},{1,3},{2,0},{3,1},{4,6},{5,7},{6,4},{7,5},{8,10},{9,11},{10,... | collective-permute-start | bytes 3145736 | tf_op jit(solution)/shard_map/ppermute | solution.py:399
  80.5 87.9 %collective-permute-start.20 = (bf16[60,128,128]{2,1,0:T(8,128)(2,1)}, bf16[60,128,128]{2,1,0:T(8,128)(2,1)}, u32[]{:S(2)}, u32[]{:S(2)}) collective-permute-start(bf16[60,128,128]{2,1,0:T(8,128)(2,1)} %get-tuple-element.126), channel_id=1, source_target_pairs={{4,12},{5,13},{6,14},{7,15},{8,0},{9,1},{10,2},{11,3},{20,28},{21,... | collective-permute-start | bytes 5898248 | tf_op jit(solution)/shard_map/ppermute | solution.py:399
  81.8 1.0 copy-start.13
  82.8 57.4 %collective-permute-start.16 = (bf16[32,128,128]{2,1,0:T(8,128)(2,1)}, bf16[32,128,128]{2,1,0:T(8,128)(2,1)}, u32[]{:S(2)}, u32[]{:S(2)}) collective-permute-start(bf16[32,128,128]{2,1,0:T(8,128)(2,1)} %get-tuple-element.121), channel_id=1, source_target_pairs={{0,8},{1,9},{2,10},{3,11},{12,4},{13,5},{14,6},{15,7},{16,24},{17,... | collective-permute-start | bytes 3145736 | tf_op jit(solution)/shard_map/ppermute | solution.py:399
  105.2 1.0 copy-start.6
  106.2 1.0 copy-start.15
  107.2 32.3 %collective-permute-start.14 = (bf16[2,128,1024]{2,1,0:T(8,128)(2,1)}, bf16[2,128,1024]{2,1,0:T(8,128)(2,1)}, u32[]{:S(2)}, u32[]{:S(2)}) collective-permute-start(bf16[2,128,1024]{2,1,0:T(8,128)(2,1)} %get-tuple-element.128.refs_1_), channel_id=1, source_target_pairs={{0,2},{1,3},{2,0},{3,1},{4,6},{5,7},{6,4},{7,5},{8,10},{9,11},{10,... | collective-permute-start | bytes 1572872 | tf_op jit(solution)/shard_map/ppermute | solution.py:399
  108.7 30.8 %collective-permute-start.15 = (bf16[2,128,1024]{2,1,0:T(8,128)(2,1)}, bf16[2,128,1024]{2,1,0:T(8,128)(2,1)}, u32[]{:S(2)}, u32[]{:S(2)}) collective-permute-start(bf16[2,128,1024]{2,1,0:T(8,128)(2,1)} %get-tuple-element.129.refs_2_), channel_id=1, source_target_pairs={{0,2},{1,3},{2,0},{3,1},{4,6},{5,7},{6,4},{7,5},{8,10},{9,11},{10,... | collective-permute-start | bytes 1572872 | tf_op jit(solution)/shard_map/ppermute | solution.py:399
  109.3 1.6 copy-start.4
  110.9 1.2 copy-start.9
  112.1 1.2 copy-start.10
  113.4 1.2 copy-start.12
  114.6 1.2 copy-start.14
  115.8 1.2 copy-start.16
  139.5 2.2 %collective-permute-start.22 = (bf16[2,128,1024]{2,1,0:T(8,128)(2,1)}, bf16[2,128,1024]{2,1,0:T(8,128)(2,1)S(1)}, u32[]{:S(2)}, u32[]{:S(2)}) collective-permute-start(bf16[2,128,1024]{2,1,0:T(8,128)(2,1)} %get-tuple-element.128.refs_1_), channel_id=1, source_target_pairs={{0,1},{1,0},{2,3},{3,2},{4,5},{5,4},{6,7},{7,6},{8,9},{9,8},{10,11... | collective-permute-start | bytes 1572872 | tf_op jit(solution)/shard_map/ppermute | solution.py:399
  139.6 3.6 %collective-permute-start.23 = (bf16[2,128,1024]{2,1,0:T(8,128)(2,1)}, bf16[2,128,1024]{2,1,0:T(8,128)(2,1)S(1)}, u32[]{:S(2)}, u32[]{:S(2)}) collective-permute-start(bf16[2,128,1024]{2,1,0:T(8,128)(2,1)} %get-tuple-element.129.refs_2_), channel_id=1, source_target_pairs={{0,1},{1,0},{2,3},{3,2},{4,5},{5,4},{6,7},{7,6},{8,9},{9,8},{10,11... | collective-permute-start | bytes 1572872 | tf_op jit(solution)/shard_map/ppermute | solution.py:399
  140.1 9.6 %collective-permute-start.21 = (bf16[4,128,1024]{2,1,0:T(8,128)(2,1)}, bf16[4,128,1024]{2,1,0:T(8,128)(2,1)}, u32[]{:S(2)}, u32[]{:S(2)}) collective-permute-start(bf16[4,128,1024]{2,1,0:T(8,128)(2,1)} %collective-permute-done.11.refs_10_), channel_id=1, source_target_pairs={{0,1},{1,0},{2,3},{3,2},{4,5},{5,4},{6,7},{7,6},{8,9},{9,8},{10,11... | collective-permute-start | bytes 3145736 | tf_op jit(solution)/shard_map/ppermute | solution.py:399
  140.2 5.1 %collective-permute-start.24 = (bf16[2,128,1024]{2,1,0:T(8,128)(2,1)}, bf16[2,128,1024]{2,1,0:T(8,128)(2,1)S(1)}, u32[]{:S(2)}, u32[]{:S(2)}) collective-permute-start(bf16[2,128,1024]{2,1,0:T(8,128)(2,1)} %collective-permute-done.14.refs_5_), channel_id=1, source_target_pairs={{0,1},{1,0},{2,3},{3,2},{4,5},{5,4},{6,7},{7,6},{8,9},{9,8},{10,11... | collective-permute-start | bytes 1572872 | tf_op jit(solution)/shard_map/ppermute | solution.py:399
  141.7 0.8 copy-start.19
  142.5 4.9 %collective-permute-start.25 = (bf16[2,128,1024]{2,1,0:T(8,128)(2,1)}, bf16[2,128,1024]{2,1,0:T(8,128)(2,1)S(1)}, u32[]{:S(2)}, u32[]{:S(2)}) collective-permute-start(bf16[2,128,1024]{2,1,0:T(8,128)(2,1)} %collective-permute-done.15.refs_6_), channel_id=1, source_target_pairs={{0,1},{1,0},{2,3},{3,2},{4,5},{5,4},{6,7},{7,6},{8,9},{9,8},{10,11... | collective-permute-start | bytes 1572872 | tf_op jit(solution)/shard_map/ppermute | solution.py:399
  143.2 0.8 copy-start.21
  144.0 40.6 %collective-permute-start.19 = (bf16[18,128,128]{2,1,0:T(8,128)(2,1)}, bf16[18,128,128]{2,1,0:T(8,128)(2,1)}, u32[]{:S(2)}, u32[]{:S(2)}) collective-permute-start(bf16[18,128,128]{2,1,0:T(8,128)(2,1)} %get-tuple-element.125), channel_id=1, source_target_pairs={{4,12},{5,13},{6,14},{7,15},{8,0},{9,1},{10,2},{11,3},{20,28},{21,... | collective-permute-start | bytes 1769480 | tf_op jit(solution)/shard_map/ppermute | solution.py:399
  145.3 0.8 copy-start.23
  146.1 43.3 %collective-permute-start.18 = (bf16[12,128,128]{2,1,0:T(8,128)(2,1)}, bf16[12,128,128]{2,1,0:T(8,128)(2,1)S(1)}, u32[]{:S(2)}, u32[]{:S(2)}) collective-permute-start(bf16[12,128,128]{2,1,0:T(8,128)(2,1)} %get-tuple-element.124), channel_id=1, source_target_pairs={{4,12},{5,13},{6,14},{7,15},{8,0},{9,1},{10,2},{11,3},{20,28},{21,... | collective-permute-start | bytes 1179656 | tf_op jit(solution)/shard_map/ppermute | solution.py:399
  147.4 0.8 copy-start.25
  148.3 45.3 %collective-permute-start.17 = (bf16[6,128,128]{2,1,0:T(8,128)(2,1)}, bf16[6,128,128]{2,1,0:T(8,128)(2,1)}, u32[]{:S(2)}, u32[]{:S(2)}) collective-permute-start(bf16[6,128,128]{2,1,0:T(8,128)(2,1)} %get-tuple-element.123), channel_id=1, source_target_pairs={{4,12},{5,13},{6,14},{7,15},{8,0},{9,1},{10,2},{11,3},{20,28},{21,... | collective-permute-start | bytes 589832 | tf_op jit(solution)/shard_map/ppermute | solution.py:399
  149.7 1.6 copy-start.5
  151.3 1.0 copy-start.20
  152.3 1.0 copy-start.22
  153.3 1.0 copy-start.24
  154.4 1.0 copy-start.26
  155.4 13.0 %copy-start.7 = (bf16[4,128,1024]{2,1,0:T(8,128)(2,1)S(1)}, bf16[4,128,1024]{2,1,0:T(8,128)(2,1)}, u32[]{:S(2)}) copy-start(bf16[4,128,1024]{2,1,0:T(8,128)(2,1)} %copy-done.6) | copy-start | bytes 3145732
  168.4 3.4 %copy-start = (f32[16,128,1024]{2,1,0:T(8,128)S(1)}, f32[16,128,1024]{2,1,0:T(8,128)}, u32[]{:S(2)}) copy-start(f32[16,128,1024]{2,1,0:T(8,128)} %get-tuple-element.134.refs_3_) | copy-start | bytes 25165828
  171.8 3.4 %copy-start.1 = (bf16[32,128,1024]{2,1,0:T(8,128)(2,1)S(1)}, bf16[32,128,1024]{2,1,0:T(8,128)(2,1)}, u32[]{:S(2)}) copy-start(bf16[32,128,1024]{2,1,0:T(8,128)(2,1)} %get-tuple-element.135.refs_4_.refs_3_) | copy-start | bytes 25165828

commit v17 on v16

--- a/solution.py
+++ b/solution.py
@@ -281,7 +281,7 @@
             pltpu.SemaphoreType.DMA((need,)),
             pltpu.SemaphoreType.DMA((PPD,)),
         ],
-        compiler_params=pltpu.CompilerParams(vmem_limit_bytes=36 * MIB),
+        compiler_params=pltpu.CompilerParams(vmem_limit_bytes=56 * MIB),
         name="own_part",
     )(own_table, far_table, firsts, tiles, perm, *pieces, *earlier)
 

time: 199 us -> 198 us (level)
  waiting for transfers between devices: 28.2 us -> 44.8 us
  local copies, waits for them, and re-layouts: 29.7 us -> 15 us
    ppermute x26, waiting for transfers between devices: 28.2 us -> 44.8 us  [send(): return lax.ppermute(value, 'tile', pairs)]
    unnamed x60 -> x28, local copies, waits for them, and re-layouts: 29 us -> 13.1 us
    pallas_call x2, Pallas kernels: 35.3 us -> 37.9 us  [own_part(): pl.pallas_call(functools.partial(own_kernel, counts, groups, group, not e...]
  transfers between devices with their start and end apart: 26 -> 26, of which waited for: 8 -> 10; matrix products, arithmetic and copies ran while one was open for 4% -> 4% of each run, Pallas kernels for 37% -> 37%
where the time goes in v17:
time: 198 us; the launch traced here: 197 us
  Pallas kernels  76.4 us (39%)
  starting transfers between devices  54.8 us (28%)
  waiting for transfers between devices  44.8 us (23%)
  local copies, waits for them, and re-layouts  15 us (8%)
  other arithmetic  6.06 us (3%)
    ppermute x26, starting transfers between devices, send(): return lax.ppermute(value, 'tile', pairs)  54.8 us
    ppermute x26, waiting for transfers between devices, send(): return lax.ppermute(value, 'tile', pairs)  44.8 us
    pallas_call x2, Pallas kernels, own_part(): pl.pallas_call(functools.partial(own_kernel, counts, groups, group, not e...  37.9 us
    pallas_call x4, Pallas kernels, far_part(): pl.pallas_call(functools.partial(far_kernel, base, total_count, [segment...  20.6 us
    unnamed x28, local copies, waits for them, and re-layouts  13.1 us
    pallas_call x3, Pallas kernels, tables(): pl.pallas_call(tables_kernel, in_specs=[SMEM] * 2, out_specs=SMEM, out_sh...  12.4 us
    pallas_call x1, Pallas kernels, sort_tiles(): pl.pallas_call(functools.partial(sort_kernel, choices), in_specs=[SMEM] *...  5.38 us
  transfers between devices with their start and end apart: 26, of which 10 were waited for; matrix products, arithmetic and copies ran while one was open for 4% of the time, Pallas kernels for 37%

profile of v17, /device:TPU:0, one launch (start us, length us, event | category | flops | bytes accessed | tf_op | source)
XLA Modules:
  0.0 197.4 jit_solution(10835143377097732563)
XLA Ops:
  0.0 0.7 collective-permute-start
  0.7 0.5 collective-permute-start.3
  1.2 5.4 %collective-permute-start.2 = (bf16[4,128,1024]{2,1,0:T(8,128)(2,1)}, bf16[4,128,1024]{2,1,0:T(8,128)(2,1)}, u32[]{:S(2)}, u32[]{:S(2)}) collective-permute-start(bf16[4,128,1024]{2,1,0:T(8,128)(2,1)} %refs_0_.1), channel_id=1, source_target_pairs={{0,4},{1,5},{2,6},{3,7},{4,0},{5,1},{6,2},{7,3},{8,12},{9,13},{10,... | collective-permute-start | bytes 3145736 | tf_op jit(solution)/shard_map/ppermute | solution.py:399
  6.7 1.5 collective-permute-start.4
  8.2 0.7 pad_add_fusion
  8.9 4.1 %tables.3.table = s32[273]{0:T(512)} custom-call(s32[96]{0:T(128)} %rows.1, s32[96]{0:T(128)} %cols.3), custom_call_target="tpu_custom_call" | custom-call | tf_op jit(solution)/shard_map/tables/pallas_call | solution.py:86
  13.0 1.3 fusion.6.rows
  14.3 1.9 copy-done.2
  16.2 0.7 copy-done.7
  16.9 5.4 %sort_tiles.1 = (bf16[4,128,1024]{2,1,0:T(8,128)(2,1)S(1)}, bf16[4,128,1024]{2,1,0:T(8,128)(2,1)S(1)}, bf16[32,128,128]{2,1,0:T(8,128)(2,1)}, bf16[60,128,128]{2...) custom-call(s32[273]{0:T(512)S(1)} %copy-done.7, ...), custom_call_target="tpu_custom_call" | custom-call | tf_op jit(solution)/shard_map/sort_tiles/pallas_call | solution.py:128
  22.3 1.0 copy-done.4
  23.2 0.1 payload.2
  23.3 7.8 %collective-permute-start.1 = (bf16[4,128,1024]{2,1,0:T(8,128)(2,1)S(1)}, bf16[4,128,1024]{2,1,0:T(8,128)(2,1)S(1)}, u32[]{:S(2)}, u32[]{:S(2)}) collective-permute-start(bf16[4,128,1024]{2,1,0:T(8,128)(2,1)S(1)} %payload.2), channel_id=1, source_target_pairs={{4,0},{5,1},{6,2},{7,3},{8,12},{9,13},{10,14},{11,15},{0,8},{1,9},... | collective-permute-start | bytes 3145736 | tf_op jit(solution)/shard_map/ppermute | solution.py:399
  31.1 0.0 collective-permute-done.8
  31.1 0.6 slice_bitcast_fusion
  31.7 0.0 collective-permute-done.2.refs_2_
  31.7 0.5 collective-permute-done.4.refs_6_
  32.2 0.7 collective-permute-start.9
  32.9 0.1 collective-permute-start.7
  33.0 1.6 collective-permute-start.6
  34.6 0.2 collective-permute-start.5
  34.8 4.1 %tables.5.far_table.table = s32[273]{0:T(512)} custom-call(s32[96]{0:T(128)} %get-tuple-element.146.rows, s32[96]{0:T(128)} %get-tuple-element.145.cols), custom_call_target="tpu_custom_call" | custom-call | flops 4000000000 | tf_op jit(solution)/shard_map/tables/pallas_call | solution.py:86
  38.9 4.2 %tables.4.own_table = s32[289]{0:T(512)} custom-call(s32[96]{0:T(128)} %fusion.6.rows, s32[96]{0:T(128)} %cols.3), custom_call_target="tpu_custom_call" | custom-call | tf_op jit(solution)/shard_map/tables/pallas_call | solution.py:86
  43.1 1.7 compare_convert_fusion.perm_ref
  44.8 8.3 %collective-permute-done.1.refs_0_ = bf16[4,128,1024]{2,1,0:T(8,128)(2,1)S(1)} collective-permute-done((bf16[4,128,1024]{2,1,0:T(8,128)(2,1)S(1)}, bf16[4,128,1024]{2,1,0:T(8,128)(2,1)S(1)}, u32[]{:S(2)}, u32[]{:S(2)}) %collective-permute-start.1) | collective-permute-done | bytes 1048608 | tf_op jit(solution)/shard_map/ppermute | solution.py:399
  53.1 0.1 broadcast_select_fusion.refs_4_
  53.3 5.6 %collective-permute-done.6.refs_8_ = bf16[4,128,1024]{2,1,0:T(8,128)(2,1)} collective-permute-done((bf16[4,128,1024]{2,1,0:T(8,128)(2,1)}, bf16[4,128,1024]{2,1,0:T(8,128)(2,1)}, u32[]{:S(2)}, u32[]{:S(2)}) %collective-permute-start.6) | collective-permute-done | bytes 1048608 | tf_op jit(solution)/shard_map/ppermute | solution.py:399
  58.9 0.0 collective-permute-start.12
  58.9 0.1 payload.3
  59.0 1.0 copy-done.3
  60.0 19.6 %collective-permute-start.10 = (bf16[4,128,1024]{2,1,0:T(8,128)(2,1)}, bf16[4,128,1024]{2,1,0:T(8,128)(2,1)S(1)}, u32[]{:S(2)}, u32[]{:S(2)}) collective-permute-start(bf16[4,128,1024]{2,1,0:T(8,128)(2,1)} %copy-done.3), channel_id=1, source_target_pairs={{4,0},{5,1},{6,2},{7,3},{8,12},{9,13},{10,14},{11,15},{0,8},{1,9},... | collective-permute-start | bytes 3145736 | tf_op jit(solution)/shard_map/ppermute | solution.py:399
  79.6 1.5 collective-permute-start.11
  81.2 1.3 collective-permute-start.20
  82.5 6.8 %collective-permute-start.16 = (bf16[32,128,128]{2,1,0:T(8,128)(2,1)}, bf16[32,128,128]{2,1,0:T(8,128)(2,1)S(1)}, u32[]{:S(2)}, u32[]{:S(2)}) collective-permute-start(bf16[32,128,128]{2,1,0:T(8,128)(2,1)} %get-tuple-element.121), channel_id=1, source_target_pairs={{0,8},{1,9},{2,10},{3,11},{12,4},{13,5},{14,6},{15,7},{16,24},{17,... | collective-permute-start | bytes 3145736 | tf_op jit(solution)/shard_map/ppermute | solution.py:399
  89.2 14.3 %collective-permute-done.10.refs_1_.refs_0_ = bf16[4,128,1024]{2,1,0:T(8,128)(2,1)S(1)} collective-permute-done((bf16[4,128,1024]{2,1,0:T(8,128)(2,1)}, bf16[4,128,1024]{2,1,0:T(8,128)(2,1)S(1)}, u32[]{:S(2)}, u32[]{:S(2)}) %collective-permute-start.10) | collective-permute-done | bytes 1048608 | tf_op jit(solution)/shard_map/ppermute | solution.py:399
  103.5 2.3 %slice_select_fusion = (bf16[2,128,1024]{2,1,0:T(8,128)(2,1)}, bf16[2,128,1024]{2,1,0:T(8,128)(2,1)}) fusion(bf16[4,128,1024]{2,1,0:T(8,128)(2,1)S(1)} %collective-permute-done.10.refs_1_.refs_0_, bf16[4,128,1024]{2,1,0:T(8,128)(2,1)} %copy-done.3, pred[]{:T(512)S(6)} %or.6), kind=kLoop, calls=%fused_computation.2 | loop fusion | flops 524288 | bytes 3145729 | tf_op jit(solution)/shard_map/jit(_where)/select_n | solution.py:469
  105.8 1.0 copy-done.9
  106.8 1.5 collective-permute-start.14
  108.3 0.5 collective-permute-start.15
  108.8 0.7 stack.89.firsts
  109.5 23.2 %own_part.2 = (f32[16,128,1024]{2,1,0:T(8,128)}, bf16[32,128,1024]{2,1,0:T(8,128)(2,1)}) custom-call(s32[289]{0:T(512)} %tables.4.own_table, s32[273]{0:T(512)} %tables.5.far_table.table, s32[11]{0:T(128)} %stack.89.firsts, bf16[96,128,128]{2,1,0:T(8,128)(2,1)} %tiles_ref.5, bf16[1024,1024]{1,0:T(8,128)(2,1)} %compare_convert_fusion.perm_ref, ...), custom_call_target="tpu_custom_call" | custom-call | tf_op jit(solution)/shard_map/own_part/pallas_call | solution.py:265
  132.8 0.1 collective-permute-start.22
  132.8 0.5 collective-permute-start.23
  133.3 0.1 collective-permute-start.21
  133.4 0.4 collective-permute-start.24
  133.8 1.1 collective-permute-done.22.refs_3_
  134.9 0.1 collective-permute-start.25
  135.1 1.4 collective-permute-done.23.refs_4_
  136.4 1.3 collective-permute-start.19
  137.7 0.2 collective-permute-done.24.refs_7_
  137.9 1.3 collective-permute-start.18
  139.3 0.8 copy-done.13
  140.1 1.3 collective-permute-start.17
  141.4 0.6 stack.99.firsts
  142.0 14.7 %own_part.3 = (f32[16,128,1024]{2,1,0:T(8,128)}, bf16[32,128,1024]{2,1,0:T(8,128)(2,1)}) custom-call(s32[289]{0:T(512)} %tables.4.own_table, s32[273]{0:T(512)} %tables.5.far_table.table, s32[9]{0:T(128)} %stack.99.firsts, bf16[96,128,128]{2,1,0:T(8,128)(2,1)} %tiles_ref.5, ...), custom_call_target="tpu_custom_call", output_to_operand_aliasing={{0}: (14, {}), {1}: (15, {})} | custom-call | tf_op jit(solution)/shard_map/own_part/pallas_call | solution.py:265
  156.7 12.3 %collective-permute-done.20.refs_2_ = bf16[60,128,128]{2,1,0:T(8,128)(2,1)} collective-permute-done((bf16[60,128,128]{2,1,0:T(8,128)(2,1)}, bf16[60,128,128]{2,1,0:T(8,128)(2,1)}, u32[]{:S(2)}, u32[]{:S(2)}) %collective-permute-start.20) | collective-permute-done | bytes 1966112 | tf_op jit(solution)/shard_map/ppermute | solution.py:399
  169.0 3.4 %copy-done = f32[16,128,1024]{2,1,0:T(8,128)S(1)} copy-done((f32[16,128,1024]{2,1,0:T(8,128)S(1)}, f32[16,128,1024]{2,1,0:T(8,128)}, u32[]{:S(2)}) %copy-start) | copy-done | bytes 8388632
  172.4 3.4 %copy-done.1 = bf16[32,128,1024]{2,1,0:T(8,128)(2,1)S(1)} copy-done((bf16[32,128,1024]{2,1,0:T(8,128)(2,1)S(1)}, bf16[32,128,1024]{2,1,0:T(8,128)(2,1)}, u32[]{:S(2)}) %copy-start.1) | copy-done | bytes 8388632
  175.8 9.7 %far_part.4 = (f32[16,128,1024]{2,1,0:T(8,128)S(1)}, bf16[16,128,1024]{2,1,0:T(8,128)(2,1)}) custom-call(s32[273]{0:T(512)S(1)} %copy-done.6, s32[1]{0:T(128)} %bitcast.chosen.at_end, bf16[4,128,1024]{2,1,0:T(8,128)(2,1)S(1)} %collective-permute-done.1.refs_0_, ...), custom_call_target="tpu_custom_call", output_to_operand_aliasing={{0}: (5, {})} | custom-call | tf_op jit(solution)/shard_map/far_part/pallas_call | solution.py:375
  185.5 4.3 %far_part.5 = (f32[16,128,1024]{2,1,0:T(8,128)S(1)}, bf16[16,128,1024]{2,1,0:T(8,128)(2,1)}) custom-call(s32[273]{0:T(512)S(1)} %copy-done.6, s32[1]{0:T(128)} %bitcast.chosen.at_end, bf16[4,128,1024]{2,1,0:T(8,128)(2,1)S(1)} %collective-permute-done.10.refs_1_.refs_0_, ...), custom_call_target="tpu_custom_call", output_to_operand_aliasing={{0}: (5, {}), {1}: (7, {})} | custom-call | tf_op jit(solution)/shard_map/far_part/pallas_call | solution.py:375
  189.8 0.2 collective-permute-done.18.refs_1_
  190.0 3.4 %far_part.6 = (f32[16,128,1024]{2,1,0:T(8,128)S(1)}, bf16[16,128,1024]{2,1,0:T(8,128)(2,1)}) custom-call(s32[273]{0:T(512)S(1)} %copy-done.6, s32[1]{0:T(128)} %bitcast.chosen.at_end, bf16[32,128,128]{2,1,0:T(8,128)(2,1)S(1)} %collective-permute-done.16.refs_1_.refs_0_, ...), custom_call_target="tpu_custom_call", output_to_operand_aliasing={{0}: (4, {}), {1}: (6, {})} | custom-call | tf_op jit(solution)/shard_map/far_part/pallas_call | solution.py:375
  193.4 0.8 collective-permute-done.17.refs_1_
  194.2 3.1 %far_part.7 = (f32[16,128,1024]{2,1,0:T(8,128)S(1)}, bf16[16,128,1024]{2,1,0:T(8,128)(2,1)}) custom-call(s32[273]{0:T(512)S(1)} %copy-done.6, s32[1]{0:T(128)} %bitcast.chosen.at_end, bf16[32,128,128]{2,1,0:T(8,128)(2,1)S(1)} %collective-permute-done.16.refs_1_.refs_0_, ...), custom_call_target="tpu_custom_call", output_to_operand_aliasing={{0}: (4, {}), {1}: (6, {})} | custom-call | tf_op jit(solution)/shard_map/far_part/pallas_call | solution.py:375
  (38 shorter events, 0.1 us)
Async XLA Ops:
  0.0 23.2 %collective-permute-start = (bf16[4,128,1024]{2,1,0:T(8,128)(2,1)}, bf16[4,128,1024]{2,1,0:T(8,128)(2,1)S(1)}, u32[]{:S(2)}, u32[]{:S(2)}) collective-permute-start(bf16[4,128,1024]{2,1,0:T(8,128)(2,1)} %refs_0_.1), channel_id=1, source_target_pairs={{4,8},{5,9},{6,10},{7,11},{8,4},{9,5},{10,6},{11,7},{20,24},{21,25... | collective-permute-start | bytes 3145736 | tf_op jit(solution)/shard_map/ppermute | solution.py:399
  0.7 31.0 %collective-permute-start.3 = (bf16[4,128,1024]{2,1,0:T(8,128)(2,1)}, bf16[4,128,1024]{2,1,0:T(8,128)(2,1)}, u32[]{:S(2)}, u32[]{:S(2)}) collective-permute-start(bf16[4,128,1024]{2,1,0:T(8,128)(2,1)} %refs_0_.1), channel_id=1, source_target_pairs={{0,1},{1,0},{2,3},{3,2},{4,5},{5,4},{6,7},{7,6},{8,9},{9,8},{10,11... | collective-permute-start | bytes 3145736 | tf_op jit(solution)/shard_map/ppermute | solution.py:399
  1.2 30.5 %collective-permute-start.2 = (bf16[4,128,1024]{2,1,0:T(8,128)(2,1)}, bf16[4,128,1024]{2,1,0:T(8,128)(2,1)}, u32[]{:S(2)}, u32[]{:S(2)}) collective-permute-start(bf16[4,128,1024]{2,1,0:T(8,128)(2,1)} %refs_0_.1), channel_id=1, source_target_pairs={{0,4},{1,5},{2,6},{3,7},{4,0},{5,1},{6,2},{7,3},{8,12},{9,13},{10,... | collective-permute-start | bytes 3145736 | tf_op jit(solution)/shard_map/ppermute | solution.py:399
  6.7 25.5 %collective-permute-start.4 = (bf16[4,128,1024]{2,1,0:T(8,128)(2,1)}, bf16[4,128,1024]{2,1,0:T(8,128)(2,1)}, u32[]{:S(2)}, u32[]{:S(2)}) collective-permute-start(bf16[4,128,1024]{2,1,0:T(8,128)(2,1)} %refs_0_.1), channel_id=1, source_target_pairs={{0,2},{1,3},{2,0},{3,1},{4,6},{5,7},{6,4},{7,5},{8,10},{9,11},{10,... | collective-permute-start | bytes 3145736 | tf_op jit(solution)/shard_map/ppermute | solution.py:399
  8.9 22.3 %collective-permute-start.8 = (s32[2,96]{1,0:T(2,128)S(1)}, s32[2,96]{1,0:T(2,128)S(1)}, u32[]{:S(2)}, u32[]{:S(2)}) collective-permute-start(s32[2,96]{1,0:T(2,128)S(1)} %pad_add_fusion), channel_id=1, source_target_pairs={{0,8},{1,9},{2,10},{3,11},{4,12},{5,13},{6,14},{7,15},{8,0},{9,1},... | collective-permute-start | bytes 2312 | tf_op jit(solution)/shard_map/ppermute | solution.py:399
  14.3 1.9 copy-start.2
  16.2 0.7 copy-start.7
  22.3 1.0 copy-start.4
  23.3 29.8 %collective-permute-start.1 = (bf16[4,128,1024]{2,1,0:T(8,128)(2,1)S(1)}, bf16[4,128,1024]{2,1,0:T(8,128)(2,1)S(1)}, u32[]{:S(2)}, u32[]{:S(2)}) collective-permute-start(bf16[4,128,1024]{2,1,0:T(8,128)(2,1)S(1)} %payload.2), channel_id=1, source_target_pairs={{4,0},{5,1},{6,2},{7,3},{8,12},{9,13},{10,14},{11,15},{0,8},{1,9},... | collective-permute-start | bytes 3145736 | tf_op jit(solution)/shard_map/ppermute | solution.py:399
  32.2 26.7 %collective-permute-start.9 = (bf16[4,128,1024]{2,1,0:T(8,128)(2,1)}, bf16[4,128,1024]{2,1,0:T(8,128)(2,1)S(1)}, u32[]{:S(2)}, u32[]{:S(2)}) collective-permute-start(bf16[4,128,1024]{2,1,0:T(8,128)(2,1)} %collective-permute-done.2.refs_2_), channel_id=1, source_target_pairs={{4,8},{5,9},{6,10},{7,11},{8,4},{9,5},{10,6},{11,7},{20,24},{21,25... | collective-permute-start | bytes 3145736 | tf_op jit(solution)/shard_map/ppermute | solution.py:399
  32.9 20.3 %collective-permute-start.7 = (bf16[4,128,1024]{2,1,0:T(8,128)(2,1)}, bf16[4,128,1024]{2,1,0:T(8,128)(2,1)}, u32[]{:S(2)}, u32[]{:S(2)}) collective-permute-start(bf16[4,128,1024]{2,1,0:T(8,128)(2,1)} %collective-permute-done.2.refs_2_), channel_id=1, source_target_pairs={{0,1},{1,0},{2,3},{3,2},{4,5},{5,4},{6,7},{7,6},{8,9},{9,8},{10,11... | collective-permute-start | bytes 3145736 | tf_op jit(solution)/shard_map/ppermute | solution.py:399
  33.0 25.9 %collective-permute-start.6 = (bf16[4,128,1024]{2,1,0:T(8,128)(2,1)}, bf16[4,128,1024]{2,1,0:T(8,128)(2,1)}, u32[]{:S(2)}, u32[]{:S(2)}) collective-permute-start(bf16[4,128,1024]{2,1,0:T(8,128)(2,1)} %collective-permute-done.2.refs_2_), channel_id=1, source_target_pairs={{0,2},{1,3},{2,0},{3,1},{4,6},{5,7},{6,4},{7,5},{8,10},{9,11},{10,... | collective-permute-start | bytes 3145736 | tf_op jit(solution)/shard_map/ppermute | solution.py:399
  34.6 18.6 %collective-permute-start.5 = (bf16[4,128,1024]{2,1,0:T(8,128)(2,1)}, bf16[4,128,1024]{2,1,0:T(8,128)(2,1)}, u32[]{:S(2)}, u32[]{:S(2)}) collective-permute-start(bf16[4,128,1024]{2,1,0:T(8,128)(2,1)} %collective-permute-done.4.refs_6_), channel_id=1, source_target_pairs={{0,1},{1,0},{2,3},{3,2},{4,5},{5,4},{6,7},{7,6},{8,9},{9,8},{10,11... | collective-permute-start | bytes 3145736 | tf_op jit(solution)/shard_map/ppermute | solution.py:399
  43.0 15.9 %copy-start.5 = (bf16[4,128,1024]{2,1,0:T(8,128)(2,1)S(1)}, bf16[4,128,1024]{2,1,0:T(8,128)(2,1)}, u32[]{:S(2)}) copy-start(bf16[4,128,1024]{2,1,0:T(8,128)(2,1)} %copy-done.4) | copy-start | bytes 3145732
  53.2 50.3 %copy-start.8 = (bf16[4,128,1024]{2,1,0:T(8,128)(2,1)}, bf16[4,128,1024]{2,1,0:T(8,128)(2,1)S(1)}, u32[]{:S(2)}) copy-start(bf16[4,128,1024]{2,1,0:T(8,128)(2,1)S(1)} %broadcast_select_fusion.refs_4_) | copy-start | bytes 3145732
  58.9 23.5 %collective-permute-start.12 = (bf16[4,128,1024]{2,1,0:T(8,128)(2,1)S(1)}, bf16[4,128,1024]{2,1,0:T(8,128)(2,1)}, u32[]{:S(2)}, u32[]{:S(2)}) collective-permute-start(bf16[4,128,1024]{2,1,0:T(8,128)(2,1)S(1)} %broadcast_select_fusion.refs_4_), channel_id=1, source_target_pairs={{0,1},{1,0},{2,3},{3,2},{4,5},{5,4},{6,7},{7,6},{8,9},{9,8},{10,11... | collective-permute-start | bytes 3145736 | tf_op jit(solution)/shard_map/ppermute | solution.py:399
  59.0 1.0 copy-start.3
  60.0 43.5 %collective-permute-start.10 = (bf16[4,128,1024]{2,1,0:T(8,128)(2,1)}, bf16[4,128,1024]{2,1,0:T(8,128)(2,1)S(1)}, u32[]{:S(2)}, u32[]{:S(2)}) collective-permute-start(bf16[4,128,1024]{2,1,0:T(8,128)(2,1)} %copy-done.3), channel_id=1, source_target_pairs={{4,0},{5,1},{6,2},{7,3},{8,12},{9,13},{10,14},{11,15},{0,8},{1,9},... | collective-permute-start | bytes 3145736 | tf_op jit(solution)/shard_map/ppermute | solution.py:399
  79.6 26.2 %collective-permute-start.13 = (bf16[4,128,1024]{2,1,0:T(8,128)(2,1)}, bf16[4,128,1024]{2,1,0:T(8,128)(2,1)S(1)}, u32[]{:S(2)}, u32[]{:S(2)}) collective-permute-start(bf16[4,128,1024]{2,1,0:T(8,128)(2,1)} %collective-permute-done.6.refs_8_), channel_id=1, source_target_pairs={{0,1},{1,0},{2,3},{3,2},{4,5},{5,4},{6,7},{7,6},{8,9},{9,8},{10,11... | collective-permute-start | bytes 3145736 | tf_op jit(solution)/shard_map/ppermute | solution.py:399
  79.6 26.2 %collective-permute-start.11 = (bf16[4,128,1024]{2,1,0:T(8,128)(2,1)S(1)}, bf16[4,128,1024]{2,1,0:T(8,128)(2,1)}, u32[]{:S(2)}, u32[]{:S(2)}) collective-permute-start(bf16[4,128,1024]{2,1,0:T(8,128)(2,1)S(1)} %broadcast_select_fusion.refs_4_), channel_id=1, source_target_pairs={{0,2},{1,3},{2,0},{3,1},{4,6},{5,7},{6,4},{7,5},{8,10},{9,11},{10,... | collective-permute-start | bytes 3145736 | tf_op jit(solution)/shard_map/ppermute | solution.py:399
  81.2 87.9 %collective-permute-start.20 = (bf16[60,128,128]{2,1,0:T(8,128)(2,1)}, bf16[60,128,128]{2,1,0:T(8,128)(2,1)}, u32[]{:S(2)}, u32[]{:S(2)}) collective-permute-start(bf16[60,128,128]{2,1,0:T(8,128)(2,1)} %get-tuple-element.126), channel_id=1, source_target_pairs={{4,12},{5,13},{6,14},{7,15},{8,0},{9,1},{10,2},{11,3},{20,28},{21,... | collective-permute-start | bytes 5898248 | tf_op jit(solution)/shard_map/ppermute | solution.py:399
  82.5 51.0 %collective-permute-start.16 = (bf16[32,128,128]{2,1,0:T(8,128)(2,1)}, bf16[32,128,128]{2,1,0:T(8,128)(2,1)S(1)}, u32[]{:S(2)}, u32[]{:S(2)}) collective-permute-start(bf16[32,128,128]{2,1,0:T(8,128)(2,1)} %get-tuple-element.121), channel_id=1, source_target_pairs={{0,8},{1,9},{2,10},{3,11},{12,4},{13,5},{14,6},{15,7},{16,24},{17,... | collective-permute-start | bytes 3145736 | tf_op jit(solution)/shard_map/ppermute | solution.py:399
  105.8 1.0 copy-start.9
  106.8 25.9 %collective-permute-start.14 = (bf16[2,128,1024]{2,1,0:T(8,128)(2,1)}, bf16[2,128,1024]{2,1,0:T(8,128)(2,1)}, u32[]{:S(2)}, u32[]{:S(2)}) collective-permute-start(bf16[2,128,1024]{2,1,0:T(8,128)(2,1)} %get-tuple-element.128.refs_1_), channel_id=1, source_target_pairs={{0,2},{1,3},{2,0},{3,1},{4,6},{5,7},{6,4},{7,5},{8,10},{9,11},{10,... | collective-permute-start | bytes 1572872 | tf_op jit(solution)/shard_map/ppermute | solution.py:399
  108.3 24.4 %collective-permute-start.15 = (bf16[2,128,1024]{2,1,0:T(8,128)(2,1)}, bf16[2,128,1024]{2,1,0:T(8,128)(2,1)}, u32[]{:S(2)}, u32[]{:S(2)}) collective-permute-start(bf16[2,128,1024]{2,1,0:T(8,128)(2,1)} %get-tuple-element.129.refs_2_), channel_id=1, source_target_pairs={{0,2},{1,3},{2,0},{3,1},{4,6},{5,7},{6,4},{7,5},{8,10},{9,11},{10,... | collective-permute-start | bytes 1572872 | tf_op jit(solution)/shard_map/ppermute | solution.py:399
  132.8 2.2 %collective-permute-start.22 = (bf16[2,128,1024]{2,1,0:T(8,128)(2,1)}, bf16[2,128,1024]{2,1,0:T(8,128)(2,1)S(1)}, u32[]{:S(2)}, u32[]{:S(2)}) collective-permute-start(bf16[2,128,1024]{2,1,0:T(8,128)(2,1)} %get-tuple-element.128.refs_1_), channel_id=1, source_target_pairs={{0,1},{1,0},{2,3},{3,2},{4,5},{5,4},{6,7},{7,6},{8,9},{9,8},{10,11... | collective-permute-start | bytes 1572872 | tf_op jit(solution)/shard_map/ppermute | solution.py:399
  132.8 3.6 %collective-permute-start.23 = (bf16[2,128,1024]{2,1,0:T(8,128)(2,1)}, bf16[2,128,1024]{2,1,0:T(8,128)(2,1)S(1)}, u32[]{:S(2)}, u32[]{:S(2)}) collective-permute-start(bf16[2,128,1024]{2,1,0:T(8,128)(2,1)} %get-tuple-element.129.refs_2_), channel_id=1, source_target_pairs={{0,1},{1,0},{2,3},{3,2},{4,5},{5,4},{6,7},{7,6},{8,9},{9,8},{10,11... | collective-permute-start | bytes 1572872 | tf_op jit(solution)/shard_map/ppermute | solution.py:399
  133.3 8.7 %collective-permute-start.21 = (bf16[4,128,1024]{2,1,0:T(8,128)(2,1)}, bf16[4,128,1024]{2,1,0:T(8,128)(2,1)}, u32[]{:S(2)}, u32[]{:S(2)}) collective-permute-start(bf16[4,128,1024]{2,1,0:T(8,128)(2,1)} %collective-permute-done.11.refs_10_), channel_id=1, source_target_pairs={{0,1},{1,0},{2,3},{3,2},{4,5},{5,4},{6,7},{7,6},{8,9},{9,8},{10,11... | collective-permute-start | bytes 3145736 | tf_op jit(solution)/shard_map/ppermute | solution.py:399
  133.4 4.5 %collective-permute-start.24 = (bf16[2,128,1024]{2,1,0:T(8,128)(2,1)}, bf16[2,128,1024]{2,1,0:T(8,128)(2,1)S(1)}, u32[]{:S(2)}, u32[]{:S(2)}) collective-permute-start(bf16[2,128,1024]{2,1,0:T(8,128)(2,1)} %collective-permute-done.14.refs_5_), channel_id=1, source_target_pairs={{0,1},{1,0},{2,3},{3,2},{4,5},{5,4},{6,7},{7,6},{8,9},{9,8},{10,11... | collective-permute-start | bytes 1572872 | tf_op jit(solution)/shard_map/ppermute | solution.py:399
  134.9 2.8 %copy-start.10 = (bf16[2,128,1024]{2,1,0:T(8,128)(2,1)}, bf16[2,128,1024]{2,1,0:T(8,128)(2,1)S(1)}, u32[]{:S(2)}) copy-start(bf16[2,128,1024]{2,1,0:T(8,128)(2,1)S(1)} %collective-permute-done.22.refs_3_) | copy-start | bytes 1572868
  134.9 4.3 %collective-permute-start.25 = (bf16[2,128,1024]{2,1,0:T(8,128)(2,1)}, bf16[2,128,1024]{2,1,0:T(8,128)(2,1)S(1)}, u32[]{:S(2)}, u32[]{:S(2)}) collective-permute-start(bf16[2,128,1024]{2,1,0:T(8,128)(2,1)} %collective-permute-done.15.refs_6_), channel_id=1, source_target_pairs={{0,1},{1,0},{2,3},{3,2},{4,5},{5,4},{6,7},{7,6},{8,9},{9,8},{10,11... | collective-permute-start | bytes 1572872 | tf_op jit(solution)/shard_map/ppermute | solution.py:399
  136.4 1.5 copy-start.11
  136.4 49.0 %collective-permute-start.19 = (bf16[18,128,128]{2,1,0:T(8,128)(2,1)}, bf16[18,128,128]{2,1,0:T(8,128)(2,1)}, u32[]{:S(2)}, u32[]{:S(2)}) collective-permute-start(bf16[18,128,128]{2,1,0:T(8,128)(2,1)} %get-tuple-element.125), channel_id=1, source_target_pairs={{4,12},{5,13},{6,14},{7,15},{8,0},{9,1},{10,2},{11,3},{20,28},{21,... | collective-permute-start | bytes 1769480 | tf_op jit(solution)/shard_map/ppermute | solution.py:399
  137.9 1.3 copy-start.12
  137.9 52.0 %collective-permute-start.18 = (bf16[12,128,128]{2,1,0:T(8,128)(2,1)}, bf16[12,128,128]{2,1,0:T(8,128)(2,1)S(1)}, u32[]{:S(2)}, u32[]{:S(2)}) collective-permute-start(bf16[12,128,128]{2,1,0:T(8,128)(2,1)} %get-tuple-element.124), channel_id=1, source_target_pairs={{4,12},{5,13},{6,14},{7,15},{8,0},{9,1},{10,2},{11,3},{20,28},{21,... | collective-permute-start | bytes 1179656 | tf_op jit(solution)/shard_map/ppermute | solution.py:399
  139.3 0.8 copy-start.13
  140.1 54.2 %collective-permute-start.17 = (bf16[6,128,128]{2,1,0:T(8,128)(2,1)}, bf16[6,128,128]{2,1,0:T(8,128)(2,1)}, u32[]{:S(2)}, u32[]{:S(2)}) collective-permute-start(bf16[6,128,128]{2,1,0:T(8,128)(2,1)} %get-tuple-element.123), channel_id=1, source_target_pairs={{4,12},{5,13},{6,14},{7,15},{8,0},{9,1},{10,2},{11,3},{20,28},{21,... | collective-permute-start | bytes 589832 | tf_op jit(solution)/shard_map/ppermute | solution.py:399
  142.0 27.0 %copy-start.6 = (s32[273]{0:T(512)S(1)}, s32[273]{0:T(512)}, u32[]{:S(2)}) copy-start(s32[273]{0:T(512)} %tables.5.far_table.table) | copy-start | bytes 3280
  169.0 3.4 %copy-start = (f32[16,128,1024]{2,1,0:T(8,128)S(1)}, f32[16,128,1024]{2,1,0:T(8,128)}, u32[]{:S(2)}) copy-start(f32[16,128,1024]{2,1,0:T(8,128)} %get-tuple-element.134.refs_3_) | copy-start | bytes 25165828
  172.4 3.4 %copy-start.1 = (bf16[32,128,1024]{2,1,0:T(8,128)(2,1)S(1)}, bf16[32,128,1024]{2,1,0:T(8,128)(2,1)}, u32[]{:S(2)}) copy-start(bf16[32,128,1024]{2,1,0:T(8,128)(2,1)} %get-tuple-element.135.refs_4_.refs_3_) | copy-start | bytes 25165828

commit v18 on v17

--- a/solution.py
+++ b/solution.py
@@ -448,7 +448,6 @@
     second = send(near, across)
     y_near = send(near, other_y)
     c_near = send(near, other_core)
-    c_y_own = send(y_own, other_core)
     own_table = tables(keys, cols, block_total, 2 * PPD)
     far_table = tables(notes[0], notes[1], block_total, cost=FAR_COST)
     perm = flip_matrix(columns)
@@ -456,18 +455,19 @@
     first = jnp.where(in_centre, first, outer)
     second = payload_of(at_end, parts[1], second)
     outer = send(second, around)
-    first, c_y_own, y_near, c_near, perm, *rest = together(
-        first, c_y_own, y_near, c_near, perm, own_table, far_table, *parts[2:]
+    first, y_own, y_near, c_near, perm, *rest = together(
+        first, y_own, y_near, c_near, perm, own_table, far_table, *parts[2:]
     )
     own_table, far_table, *parts = rest
     y_first = send(first, other_y)
     c_first = send(first, other_core)
+    c_y_own = send(y_own, other_core)
     c_y_near = send(y_near, other_core)
     tiles_last, c_first = together(parts[0], c_first)
     far_ends += [outer, send(tiles_last, from_ends)]
     halves = (slice(0, local // 2), slice(local // 2, None))
     second = [jnp.where(in_centre, second[half], outer[half]) for half in halves]
-    *second, y_first, c_first, c_y_near = together(*second, y_first, c_first, c_y_near)
+    *second, y_first, c_first, c_y_own, c_y_near = together(*second, y_first, c_first, c_y_own, c_y_near)
 
     far_centre = [send(parts[1], from_centre)]
     y_second = [send(half, other_y) for half in second]

time: 198 us -> 198 us (level)
    unnamed x28 -> x32, local copies, waits for them, and re-layouts: 13.1 us -> 13.4 us
  transfers between devices with their start and end apart: 26 -> 26, of which waited for: 10 -> 9; matrix products, arithmetic and copies ran while one was open for 4% -> 4% of each run, Pallas kernels for 37% -> 37%
where the time goes in v18:
time: 198 us
  Pallas kernels  76.8 us (39%)
  starting transfers between devices  53.6 us (27%)
  waiting for transfers between devices  45.6 us (23%)
  local copies, waits for them, and re-layouts  15.2 us (8%)
  other arithmetic  6.1 us (3%)
    ppermute x26, starting transfers between devices, send(): return lax.ppermute(value, 'tile', pairs)  53.6 us
    ppermute x26, waiting for transfers between devices, send(): return lax.ppermute(value, 'tile', pairs)  45.6 us
    pallas_call x2, Pallas kernels, own_part(): pl.pallas_call(functools.partial(own_kernel, counts, groups, group, not e...  37.7 us
    pallas_call x4, Pallas kernels, far_part(): pl.pallas_call(functools.partial(far_kernel, base, total_count, [segment...  21.1 us
    unnamed x32, local copies, waits for them, and re-layouts  13.4 us
    pallas_call x3, Pallas kernels, tables(): pl.pallas_call(tables_kernel, in_specs=[SMEM] * 2, out_specs=SMEM, out_sh...  12.4 us
    pallas_call x1, Pallas kernels, sort_tiles(): pl.pallas_call(functools.partial(sort_kernel, choices), in_specs=[SMEM] *...  5.38 us
  transfers between devices with their start and end apart: 26, of which 9 were waited for; matrix products, arithmetic and copies ran while one was open for 4% of the time, Pallas kernels for 37%

profile of v18, /device:TPU:0, one launch (start us, length us, event | category | flops | bytes accessed | tf_op | source)
XLA Modules:
  0.0 197.7 jit_solution(15487077103813260524)
XLA Ops:
  0.0 0.7 collective-permute-start
  0.7 0.5 collective-permute-start.3
  1.2 5.4 %collective-permute-start.2 = (bf16[4,128,1024]{2,1,0:T(8,128)(2,1)}, bf16[4,128,1024]{2,1,0:T(8,128)(2,1)}, u32[]{:S(2)}, u32[]{:S(2)}) collective-permute-start(bf16[4,128,1024]{2,1,0:T(8,128)(2,1)} %refs_0_.1), channel_id=1, source_target_pairs={{0,4},{1,5},{2,6},{3,7},{4,0},{5,1},{6,2},{7,3},{8,12},{9,13},{10,... | collective-permute-start | bytes 3145736 | tf_op jit(solution)/shard_map/ppermute | solution.py:399
  6.7 1.5 collective-permute-start.4
  8.2 0.7 pad_add_fusion
  8.9 0.0 collective-permute-start.7
  8.9 4.1 %tables.3.table = s32[273]{0:T(512)} custom-call(s32[96]{0:T(128)} %rows.1, s32[96]{0:T(128)} %cols.3), custom_call_target="tpu_custom_call" | custom-call | tf_op jit(solution)/shard_map/tables/pallas_call | solution.py:86
  13.0 1.3 fusion.6.rows
  14.3 1.9 copy-done.2
  16.2 0.7 copy-done.7
  16.9 5.4 %sort_tiles.1 = (bf16[4,128,1024]{2,1,0:T(8,128)(2,1)S(1)}, bf16[4,128,1024]{2,1,0:T(8,128)(2,1)S(1)}, bf16[32,128,128]{2,1,0:T(8,128)(2,1)}, bf16[60,128,128]{2...) custom-call(s32[273]{0:T(512)S(1)} %copy-done.7, ...), custom_call_target="tpu_custom_call" | custom-call | tf_op jit(solution)/shard_map/sort_tiles/pallas_call | solution.py:128
  22.3 1.0 copy-done.4
  23.3 0.1 payload.2
  23.4 7.7 %collective-permute-start.1 = (bf16[4,128,1024]{2,1,0:T(8,128)(2,1)S(1)}, bf16[4,128,1024]{2,1,0:T(8,128)(2,1)S(1)}, u32[]{:S(2)}, u32[]{:S(2)}) collective-permute-start(bf16[4,128,1024]{2,1,0:T(8,128)(2,1)S(1)} %payload.2), channel_id=1, source_target_pairs={{4,0},{5,1},{6,2},{7,3},{8,12},{9,13},{10,14},{11,15},{0,8},{1,9},... | collective-permute-start | bytes 3145736 | tf_op jit(solution)/shard_map/ppermute | solution.py:399
  31.1 0.6 slice_bitcast_fusion
  31.7 0.0 collective-permute-done.3.refs_1_
  31.7 0.0 collective-permute-done.2.refs_2_
  31.7 0.5 collective-permute-done.4.refs_6_
  32.2 0.7 collective-permute-start.8
  32.9 0.1 collective-permute-start.6
  33.0 1.6 collective-permute-start.5
  34.6 4.1 %tables.5.far_table.table = s32[273]{0:T(512)} custom-call(s32[96]{0:T(128)} %get-tuple-element.148.rows, s32[96]{0:T(128)} %get-tuple-element.147.cols), custom_call_target="tpu_custom_call" | custom-call | flops 4000000000 | tf_op jit(solution)/shard_map/tables/pallas_call | solution.py:86
  38.7 4.2 %tables.4.own_table = s32[289]{0:T(512)} custom-call(s32[96]{0:T(128)} %fusion.6.rows, s32[96]{0:T(128)} %cols.3), custom_call_target="tpu_custom_call" | custom-call | tf_op jit(solution)/shard_map/tables/pallas_call | solution.py:86
  42.9 1.7 compare_convert_fusion.perm_ref
  44.6 8.5 %collective-permute-done.1.refs_0_ = bf16[4,128,1024]{2,1,0:T(8,128)(2,1)S(1)} collective-permute-done((bf16[4,128,1024]{2,1,0:T(8,128)(2,1)S(1)}, bf16[4,128,1024]{2,1,0:T(8,128)(2,1)S(1)}, u32[]{:S(2)}, u32[]{:S(2)}) %collective-permute-start.1) | collective-permute-done | bytes 1048608 | tf_op jit(solution)/shard_map/ppermute | solution.py:399
  53.1 0.1 broadcast_select_fusion.refs_4_
  53.2 5.7 %collective-permute-done.5.refs_8_ = bf16[4,128,1024]{2,1,0:T(8,128)(2,1)} collective-permute-done((bf16[4,128,1024]{2,1,0:T(8,128)(2,1)}, bf16[4,128,1024]{2,1,0:T(8,128)(2,1)}, u32[]{:S(2)}, u32[]{:S(2)}) %collective-permute-start.5) | collective-permute-done | bytes 1048608 | tf_op jit(solution)/shard_map/ppermute | solution.py:399
  58.9 0.1 payload.3
  59.0 1.0 copy-done.3
  60.0 19.6 %collective-permute-start.9 = (bf16[4,128,1024]{2,1,0:T(8,128)(2,1)}, bf16[4,128,1024]{2,1,0:T(8,128)(2,1)S(1)}, u32[]{:S(2)}, u32[]{:S(2)}) collective-permute-start(bf16[4,128,1024]{2,1,0:T(8,128)(2,1)} %copy-done.3), channel_id=1, source_target_pairs={{4,0},{5,1},{6,2},{7,3},{8,12},{9,13},{10,14},{11,15},{0,8},{1,9},... | collective-permute-start | bytes 3145736 | tf_op jit(solution)/shard_map/ppermute | solution.py:399
  79.6 0.5 collective-permute-start.13
  80.1 1.5 collective-permute-start.10
  81.7 1.3 collective-permute-start.20
  83.0 19.6 %collective-permute-done.9.refs_1_.refs_0_ = bf16[4,128,1024]{2,1,0:T(8,128)(2,1)S(1)} collective-permute-done((bf16[4,128,1024]{2,1,0:T(8,128)(2,1)}, bf16[4,128,1024]{2,1,0:T(8,128)(2,1)S(1)}, u32[]{:S(2)}, u32[]{:S(2)}) %collective-permute-start.9) | collective-permute-done | bytes 1048608 | tf_op jit(solution)/shard_map/ppermute | solution.py:399
  102.6 5.3 %collective-permute-start.16 = (bf16[32,128,128]{2,1,0:T(8,128)(2,1)}, bf16[32,128,128]{2,1,0:T(8,128)(2,1)S(1)}, u32[]{:S(2)}, u32[]{:S(2)}) collective-permute-start(bf16[32,128,128]{2,1,0:T(8,128)(2,1)} %get-tuple-element.123), channel_id=1, source_target_pairs={{0,8},{1,9},{2,10},{3,11},{12,4},{13,5},{14,6},{15,7},{16,24},{17,... | collective-permute-start | bytes 3145736 | tf_op jit(solution)/shard_map/ppermute | solution.py:399
  107.9 2.3 %slice_select_fusion = (bf16[2,128,1024]{2,1,0:T(8,128)(2,1)}, bf16[2,128,1024]{2,1,0:T(8,128)(2,1)}) fusion(bf16[4,128,1024]{2,1,0:T(8,128)(2,1)S(1)} %collective-permute-done.9.refs_1_.refs_0_, bf16[4,128,1024]{2,1,0:T(8,128)(2,1)} %copy-done.3, pred[]{:T(512)S(6)} %or.6), kind=kLoop, calls=%fused_computation.2 | loop fusion | flops 524288 | bytes 3145729 | tf_op jit(solution)/shard_map/jit(_where)/select_n | solution.py:469
  110.2 1.0 copy-done.10
  111.1 0.3 copy-done.11
  111.5 1.5 collective-permute-start.14
  113.0 0.5 collective-permute-start.15
  113.5 0.6 stack.89.firsts
  114.2 23.3 %own_part.2 = (f32[16,128,1024]{2,1,0:T(8,128)}, bf16[32,128,1024]{2,1,0:T(8,128)(2,1)}) custom-call(s32[289]{0:T(512)} %tables.4.own_table, s32[273]{0:T(512)} %tables.5.far_table.table, s32[11]{0:T(128)} %stack.89.firsts, bf16[96,128,128]{2,1,0:T(8,128)(2,1)} %tiles_ref.5, bf16[1024,1024]{1,0:T(8,128)(2,1)} %compare_convert_fusion.perm_ref, ...), custom_call_target="tpu_custom_call" | custom-call | tf_op jit(solution)/shard_map/own_part/pallas_call | solution.py:265
  137.4 0.1 collective-permute-start.22
  137.5 0.5 collective-permute-start.23
  138.0 0.1 collective-permute-start.21
  138.1 0.4 collective-permute-start.24
  138.5 1.1 collective-permute-done.22.refs_3_
  139.6 0.1 collective-permute-start.25
  139.8 1.4 collective-permute-done.23.refs_4_
  141.1 1.3 collective-permute-start.19
  142.4 0.2 collective-permute-done.24.refs_7_
  142.6 1.3 collective-permute-start.18
  144.0 0.8 copy-done.15
  144.7 1.3 collective-permute-start.17
  146.0 0.6 stack.99.firsts
  146.7 14.4 %own_part.3 = (f32[16,128,1024]{2,1,0:T(8,128)}, bf16[32,128,1024]{2,1,0:T(8,128)(2,1)}) custom-call(s32[289]{0:T(512)} %tables.4.own_table, s32[273]{0:T(512)} %tables.5.far_table.table, s32[9]{0:T(128)} %stack.99.firsts, bf16[96,128,128]{2,1,0:T(8,128)(2,1)} %tiles_ref.5, ...), custom_call_target="tpu_custom_call", output_to_operand_aliasing={{0}: (14, {}), {1}: (15, {})} | custom-call | tf_op jit(solution)/shard_map/own_part/pallas_call | solution.py:265
  161.1 7.9 %collective-permute-done.20.refs_2_ = bf16[60,128,128]{2,1,0:T(8,128)(2,1)} collective-permute-done((bf16[60,128,128]{2,1,0:T(8,128)(2,1)}, bf16[60,128,128]{2,1,0:T(8,128)(2,1)}, u32[]{:S(2)}, u32[]{:S(2)}) %collective-permute-start.20) | collective-permute-done | bytes 1966112 | tf_op jit(solution)/shard_map/ppermute | solution.py:399
  169.0 3.4 %copy-done = f32[16,128,1024]{2,1,0:T(8,128)S(1)} copy-done((f32[16,128,1024]{2,1,0:T(8,128)S(1)}, f32[16,128,1024]{2,1,0:T(8,128)}, u32[]{:S(2)}) %copy-start) | copy-done | bytes 8388632
  172.4 3.4 %copy-done.1 = bf16[32,128,1024]{2,1,0:T(8,128)(2,1)S(1)} copy-done((bf16[32,128,1024]{2,1,0:T(8,128)(2,1)S(1)}, bf16[32,128,1024]{2,1,0:T(8,128)(2,1)}, u32[]{:S(2)}) %copy-start.1) | copy-done | bytes 8388632
  175.8 9.6 %far_part.4 = (f32[16,128,1024]{2,1,0:T(8,128)S(1)}, bf16[16,128,1024]{2,1,0:T(8,128)(2,1)}) custom-call(s32[273]{0:T(512)S(1)} %copy-done.6, s32[1]{0:T(128)} %bitcast.chosen.at_end, bf16[4,128,1024]{2,1,0:T(8,128)(2,1)S(1)} %collective-permute-done.1.refs_0_, ...), custom_call_target="tpu_custom_call", output_to_operand_aliasing={{0}: (5, {})} | custom-call | tf_op jit(solution)/shard_map/far_part/pallas_call | solution.py:375
  185.4 4.7 %far_part.5 = (f32[16,128,1024]{2,1,0:T(8,128)S(1)}, bf16[16,128,1024]{2,1,0:T(8,128)(2,1)}) custom-call(s32[273]{0:T(512)S(1)} %copy-done.6, s32[1]{0:T(128)} %bitcast.chosen.at_end, bf16[4,128,1024]{2,1,0:T(8,128)(2,1)S(1)} %collective-permute-done.9.refs_1_.refs_0_, ...), custom_call_target="tpu_custom_call", output_to_operand_aliasing={{0}: (5, {}), {1}: (7, {})} | custom-call | tf_op jit(solution)/shard_map/far_part/pallas_call | solution.py:375
  190.1 3.3 %far_part.6 = (f32[16,128,1024]{2,1,0:T(8,128)S(1)}, bf16[16,128,1024]{2,1,0:T(8,128)(2,1)}) custom-call(s32[273]{0:T(512)S(1)} %copy-done.6, s32[1]{0:T(128)} %bitcast.chosen.at_end, bf16[32,128,128]{2,1,0:T(8,128)(2,1)S(1)} %collective-permute-done.16.refs_1_.refs_0_, ...), custom_call_target="tpu_custom_call", output_to_operand_aliasing={{0}: (4, {}), {1}: (6, {})} | custom-call | tf_op jit(solution)/shard_map/far_part/pallas_call | solution.py:375
  193.5 0.7 collective-permute-done.17.refs_1_
  194.2 3.5 %far_part.7 = (f32[16,128,1024]{2,1,0:T(8,128)S(1)}, bf16[16,128,1024]{2,1,0:T(8,128)(2,1)}) custom-call(s32[273]{0:T(512)S(1)} %copy-done.6, s32[1]{0:T(128)} %bitcast.chosen.at_end, bf16[32,128,128]{2,1,0:T(8,128)(2,1)S(1)} %collective-permute-done.16.refs_1_.refs_0_, ...), custom_call_target="tpu_custom_call", output_to_operand_aliasing={{0}: (4, {}), {1}: (6, {})} | custom-call | tf_op jit(solution)/shard_map/far_part/pallas_call | solution.py:375
  (42 shorter events, 0.1 us)
Async XLA Ops:
  0.0 23.3 %collective-permute-start = (bf16[4,128,1024]{2,1,0:T(8,128)(2,1)}, bf16[4,128,1024]{2,1,0:T(8,128)(2,1)S(1)}, u32[]{:S(2)}, u32[]{:S(2)}) collective-permute-start(bf16[4,128,1024]{2,1,0:T(8,128)(2,1)} %refs_0_.1), channel_id=1, source_target_pairs={{4,8},{5,9},{6,10},{7,11},{8,4},{9,5},{10,6},{11,7},{20,24},{21,25... | collective-permute-start | bytes 3145736 | tf_op jit(solution)/shard_map/ppermute | solution.py:399
  0.7 31.0 %collective-permute-start.3 = (bf16[4,128,1024]{2,1,0:T(8,128)(2,1)}, bf16[4,128,1024]{2,1,0:T(8,128)(2,1)}, u32[]{:S(2)}, u32[]{:S(2)}) collective-permute-start(bf16[4,128,1024]{2,1,0:T(8,128)(2,1)} %refs_0_.1), channel_id=1, source_target_pairs={{0,1},{1,0},{2,3},{3,2},{4,5},{5,4},{6,7},{7,6},{8,9},{9,8},{10,11... | collective-permute-start | bytes 3145736 | tf_op jit(solution)/shard_map/ppermute | solution.py:399
  1.2 30.4 %collective-permute-start.2 = (bf16[4,128,1024]{2,1,0:T(8,128)(2,1)}, bf16[4,128,1024]{2,1,0:T(8,128)(2,1)}, u32[]{:S(2)}, u32[]{:S(2)}) collective-permute-start(bf16[4,128,1024]{2,1,0:T(8,128)(2,1)} %refs_0_.1), channel_id=1, source_target_pairs={{0,4},{1,5},{2,6},{3,7},{4,0},{5,1},{6,2},{7,3},{8,12},{9,13},{10,... | collective-permute-start | bytes 3145736 | tf_op jit(solution)/shard_map/ppermute | solution.py:399
  6.7 25.5 %collective-permute-start.4 = (bf16[4,128,1024]{2,1,0:T(8,128)(2,1)}, bf16[4,128,1024]{2,1,0:T(8,128)(2,1)}, u32[]{:S(2)}, u32[]{:S(2)}) collective-permute-start(bf16[4,128,1024]{2,1,0:T(8,128)(2,1)} %refs_0_.1), channel_id=1, source_target_pairs={{0,2},{1,3},{2,0},{3,1},{4,6},{5,7},{6,4},{7,5},{8,10},{9,11},{10,... | collective-permute-start | bytes 3145736 | tf_op jit(solution)/shard_map/ppermute | solution.py:399
  8.9 22.3 %collective-permute-start.7 = (s32[2,96]{1,0:T(2,128)S(1)}, s32[2,96]{1,0:T(2,128)S(1)}, u32[]{:S(2)}, u32[]{:S(2)}) collective-permute-start(s32[2,96]{1,0:T(2,128)S(1)} %pad_add_fusion), channel_id=1, source_target_pairs={{0,8},{1,9},{2,10},{3,11},{4,12},{5,13},{6,14},{7,15},{8,0},{9,1},... | collective-permute-start | bytes 2312 | tf_op jit(solution)/shard_map/ppermute | solution.py:399
  14.3 1.9 copy-start.2
  16.2 0.7 copy-start.7
  22.3 1.0 copy-start.4
  23.4 29.7 %collective-permute-start.1 = (bf16[4,128,1024]{2,1,0:T(8,128)(2,1)S(1)}, bf16[4,128,1024]{2,1,0:T(8,128)(2,1)S(1)}, u32[]{:S(2)}, u32[]{:S(2)}) collective-permute-start(bf16[4,128,1024]{2,1,0:T(8,128)(2,1)S(1)} %payload.2), channel_id=1, source_target_pairs={{4,0},{5,1},{6,2},{7,3},{8,12},{9,13},{10,14},{11,15},{0,8},{1,9},... | collective-permute-start | bytes 3145736 | tf_op jit(solution)/shard_map/ppermute | solution.py:399
  32.2 26.7 %collective-permute-start.8 = (bf16[4,128,1024]{2,1,0:T(8,128)(2,1)}, bf16[4,128,1024]{2,1,0:T(8,128)(2,1)S(1)}, u32[]{:S(2)}, u32[]{:S(2)}) collective-permute-start(bf16[4,128,1024]{2,1,0:T(8,128)(2,1)} %collective-permute-done.2.refs_2_), channel_id=1, source_target_pairs={{4,8},{5,9},{6,10},{7,11},{8,4},{9,5},{10,6},{11,7},{20,24},{21,25... | collective-permute-start | bytes 3145736 | tf_op jit(solution)/shard_map/ppermute | solution.py:399
  32.9 20.3 %collective-permute-start.6 = (bf16[4,128,1024]{2,1,0:T(8,128)(2,1)}, bf16[4,128,1024]{2,1,0:T(8,128)(2,1)}, u32[]{:S(2)}, u32[]{:S(2)}) collective-permute-start(bf16[4,128,1024]{2,1,0:T(8,128)(2,1)} %collective-permute-done.2.refs_2_), channel_id=1, source_target_pairs={{0,1},{1,0},{2,3},{3,2},{4,5},{5,4},{6,7},{7,6},{8,9},{9,8},{10,11... | collective-permute-start | bytes 3145736 | tf_op jit(solution)/shard_map/ppermute | solution.py:399
  33.0 25.9 %collective-permute-start.5 = (bf16[4,128,1024]{2,1,0:T(8,128)(2,1)}, bf16[4,128,1024]{2,1,0:T(8,128)(2,1)}, u32[]{:S(2)}, u32[]{:S(2)}) collective-permute-start(bf16[4,128,1024]{2,1,0:T(8,128)(2,1)} %collective-permute-done.2.refs_2_), channel_id=1, source_target_pairs={{0,2},{1,3},{2,0},{3,1},{4,6},{5,7},{6,4},{7,5},{8,10},{9,11},{10,... | collective-permute-start | bytes 3145736 | tf_op jit(solution)/shard_map/ppermute | solution.py:399
  42.9 16.0 %copy-start.5 = (bf16[4,128,1024]{2,1,0:T(8,128)(2,1)S(1)}, bf16[4,128,1024]{2,1,0:T(8,128)(2,1)}, u32[]{:S(2)}) copy-start(bf16[4,128,1024]{2,1,0:T(8,128)(2,1)} %copy-done.4) | copy-start | bytes 3145732
  53.2 49.4 %copy-start.8 = (bf16[4,128,1024]{2,1,0:T(8,128)(2,1)}, bf16[4,128,1024]{2,1,0:T(8,128)(2,1)S(1)}, u32[]{:S(2)}) copy-start(bf16[4,128,1024]{2,1,0:T(8,128)(2,1)S(1)} %broadcast_select_fusion.refs_4_) | copy-start | bytes 3145732
  58.9 22.8 %collective-permute-start.11 = (bf16[4,128,1024]{2,1,0:T(8,128)(2,1)S(1)}, bf16[4,128,1024]{2,1,0:T(8,128)(2,1)S(1)}, u32[]{:S(2)}, u32[]{:S(2)}) collective-permute-start(bf16[4,128,1024]{2,1,0:T(8,128)(2,1)S(1)} %broadcast_select_fusion.refs_4_), channel_id=1, source_target_pairs={{0,1},{1,0},{2,3},{3,2},{4,5},{5,4},{6,7},{7,6},{8,9},{9,8},{10,11... | collective-permute-start | bytes 3145736 | tf_op jit(solution)/shard_map/ppermute | solution.py:399
  59.0 1.0 copy-start.3
  60.0 42.6 %collective-permute-start.9 = (bf16[4,128,1024]{2,1,0:T(8,128)(2,1)}, bf16[4,128,1024]{2,1,0:T(8,128)(2,1)S(1)}, u32[]{:S(2)}, u32[]{:S(2)}) collective-permute-start(bf16[4,128,1024]{2,1,0:T(8,128)(2,1)} %copy-done.3), channel_id=1, source_target_pairs={{4,0},{5,1},{6,2},{7,3},{8,12},{9,13},{10,14},{11,15},{0,8},{1,9},... | collective-permute-start | bytes 3145736 | tf_op jit(solution)/shard_map/ppermute | solution.py:399
  79.6 30.5 %collective-permute-start.12 = (bf16[4,128,1024]{2,1,0:T(8,128)(2,1)}, bf16[4,128,1024]{2,1,0:T(8,128)(2,1)S(1)}, u32[]{:S(2)}, u32[]{:S(2)}) collective-permute-start(bf16[4,128,1024]{2,1,0:T(8,128)(2,1)} %collective-permute-done.4.refs_6_), channel_id=1, source_target_pairs={{0,1},{1,0},{2,3},{3,2},{4,5},{5,4},{6,7},{7,6},{8,9},{9,8},{10,11... | collective-permute-start | bytes 3145736 | tf_op jit(solution)/shard_map/ppermute | solution.py:399
  79.6 30.6 %collective-permute-start.13 = (bf16[4,128,1024]{2,1,0:T(8,128)(2,1)}, bf16[4,128,1024]{2,1,0:T(8,128)(2,1)S(1)}, u32[]{:S(2)}, u32[]{:S(2)}) collective-permute-start(bf16[4,128,1024]{2,1,0:T(8,128)(2,1)} %collective-permute-done.5.refs_8_), channel_id=1, source_target_pairs={{0,1},{1,0},{2,3},{3,2},{4,5},{5,4},{6,7},{7,6},{8,9},{9,8},{10,11... | collective-permute-start | bytes 3145736 | tf_op jit(solution)/shard_map/ppermute | solution.py:399
  80.1 30.1 %collective-permute-start.10 = (bf16[4,128,1024]{2,1,0:T(8,128)(2,1)S(1)}, bf16[4,128,1024]{2,1,0:T(8,128)(2,1)}, u32[]{:S(2)}, u32[]{:S(2)}) collective-permute-start(bf16[4,128,1024]{2,1,0:T(8,128)(2,1)S(1)} %broadcast_select_fusion.refs_4_), channel_id=1, source_target_pairs={{0,2},{1,3},{2,0},{3,1},{4,6},{5,7},{6,4},{7,5},{8,10},{9,11},{10,... | collective-permute-start | bytes 3145736 | tf_op jit(solution)/shard_map/ppermute | solution.py:399
  81.7 1.3 copy-start.9
  81.7 87.4 %collective-permute-start.20 = (bf16[60,128,128]{2,1,0:T(8,128)(2,1)}, bf16[60,128,128]{2,1,0:T(8,128)(2,1)}, u32[]{:S(2)}, u32[]{:S(2)}) collective-permute-start(bf16[60,128,128]{2,1,0:T(8,128)(2,1)} %get-tuple-element.128), channel_id=1, source_target_pairs={{4,12},{5,13},{6,14},{7,15},{8,0},{9,1},{10,2},{11,3},{20,28},{21,... | collective-permute-start | bytes 5898248 | tf_op jit(solution)/shard_map/ppermute | solution.py:399
  102.6 35.5 %collective-permute-start.16 = (bf16[32,128,128]{2,1,0:T(8,128)(2,1)}, bf16[32,128,128]{2,1,0:T(8,128)(2,1)S(1)}, u32[]{:S(2)}, u32[]{:S(2)}) collective-permute-start(bf16[32,128,128]{2,1,0:T(8,128)(2,1)} %get-tuple-element.123), channel_id=1, source_target_pairs={{0,8},{1,9},{2,10},{3,11},{12,4},{13,5},{14,6},{15,7},{16,24},{17,... | collective-permute-start | bytes 3145736 | tf_op jit(solution)/shard_map/ppermute | solution.py:399
  110.2 1.0 copy-start.10
  110.2 1.3 copy-start.11
  111.5 25.9 %collective-permute-start.14 = (bf16[2,128,1024]{2,1,0:T(8,128)(2,1)}, bf16[2,128,1024]{2,1,0:T(8,128)(2,1)}, u32[]{:S(2)}, u32[]{:S(2)}) collective-permute-start(bf16[2,128,1024]{2,1,0:T(8,128)(2,1)} %get-tuple-element.130.refs_1_), channel_id=1, source_target_pairs={{0,2},{1,3},{2,0},{3,1},{4,6},{5,7},{6,4},{7,5},{8,10},{9,11},{10,... | collective-permute-start | bytes 1572872 | tf_op jit(solution)/shard_map/ppermute | solution.py:399
  113.0 24.4 %collective-permute-start.15 = (bf16[2,128,1024]{2,1,0:T(8,128)(2,1)}, bf16[2,128,1024]{2,1,0:T(8,128)(2,1)}, u32[]{:S(2)}, u32[]{:S(2)}) collective-permute-start(bf16[2,128,1024]{2,1,0:T(8,128)(2,1)} %get-tuple-element.131.refs_2_), channel_id=1, source_target_pairs={{0,2},{1,3},{2,0},{3,1},{4,6},{5,7},{6,4},{7,5},{8,10},{9,11},{10,... | collective-permute-start | bytes 1572872 | tf_op jit(solution)/shard_map/ppermute | solution.py:399
  137.4 2.2 %collective-permute-start.22 = (bf16[2,128,1024]{2,1,0:T(8,128)(2,1)}, bf16[2,128,1024]{2,1,0:T(8,128)(2,1)S(1)}, u32[]{:S(2)}, u32[]{:S(2)}) collective-permute-start(bf16[2,128,1024]{2,1,0:T(8,128)(2,1)} %get-tuple-element.130.refs_1_), channel_id=1, source_target_pairs={{0,1},{1,0},{2,3},{3,2},{4,5},{5,4},{6,7},{7,6},{8,9},{9,8},{10,11... | collective-permute-start | bytes 1572872 | tf_op jit(solution)/shard_map/ppermute | solution.py:399
  137.5 3.6 %collective-permute-start.23 = (bf16[2,128,1024]{2,1,0:T(8,128)(2,1)}, bf16[2,128,1024]{2,1,0:T(8,128)(2,1)S(1)}, u32[]{:S(2)}, u32[]{:S(2)}) collective-permute-start(bf16[2,128,1024]{2,1,0:T(8,128)(2,1)} %get-tuple-element.131.refs_2_), channel_id=1, source_target_pairs={{0,1},{1,0},{2,3},{3,2},{4,5},{5,4},{6,7},{7,6},{8,9},{9,8},{10,11... | collective-permute-start | bytes 1572872 | tf_op jit(solution)/shard_map/ppermute | solution.py:399
  138.0 8.6 %collective-permute-start.21 = (bf16[4,128,1024]{2,1,0:T(8,128)(2,1)}, bf16[4,128,1024]{2,1,0:T(8,128)(2,1)}, u32[]{:S(2)}, u32[]{:S(2)}) collective-permute-start(bf16[4,128,1024]{2,1,0:T(8,128)(2,1)} %collective-permute-done.10.refs_10_), channel_id=1, source_target_pairs={{0,1},{1,0},{2,3},{3,2},{4,5},{5,4},{6,7},{7,6},{8,9},{9,8},{10,11... | collective-permute-start | bytes 3145736 | tf_op jit(solution)/shard_map/ppermute | solution.py:399
  138.1 4.5 %collective-permute-start.24 = (bf16[2,128,1024]{2,1,0:T(8,128)(2,1)}, bf16[2,128,1024]{2,1,0:T(8,128)(2,1)S(1)}, u32[]{:S(2)}, u32[]{:S(2)}) collective-permute-start(bf16[2,128,1024]{2,1,0:T(8,128)(2,1)} %collective-permute-done.14.refs_5_), channel_id=1, source_target_pairs={{0,1},{1,0},{2,3},{3,2},{4,5},{5,4},{6,7},{7,6},{8,9},{9,8},{10,11... | collective-permute-start | bytes 1572872 | tf_op jit(solution)/shard_map/ppermute | solution.py:399
  139.6 2.8 %copy-start.12 = (bf16[2,128,1024]{2,1,0:T(8,128)(2,1)}, bf16[2,128,1024]{2,1,0:T(8,128)(2,1)S(1)}, u32[]{:S(2)}) copy-start(bf16[2,128,1024]{2,1,0:T(8,128)(2,1)S(1)} %collective-permute-done.22.refs_3_) | copy-start | bytes 1572868
  139.6 4.3 %collective-permute-start.25 = (bf16[2,128,1024]{2,1,0:T(8,128)(2,1)}, bf16[2,128,1024]{2,1,0:T(8,128)(2,1)S(1)}, u32[]{:S(2)}, u32[]{:S(2)}) collective-permute-start(bf16[2,128,1024]{2,1,0:T(8,128)(2,1)} %collective-permute-done.15.refs_6_), channel_id=1, source_target_pairs={{0,1},{1,0},{2,3},{3,2},{4,5},{5,4},{6,7},{7,6},{8,9},{9,8},{10,11... | collective-permute-start | bytes 1572872 | tf_op jit(solution)/shard_map/ppermute | solution.py:399
  141.1 1.5 copy-start.13
  141.1 44.3 %collective-permute-start.19 = (bf16[18,128,128]{2,1,0:T(8,128)(2,1)}, bf16[18,128,128]{2,1,0:T(8,128)(2,1)}, u32[]{:S(2)}, u32[]{:S(2)}) collective-permute-start(bf16[18,128,128]{2,1,0:T(8,128)(2,1)} %get-tuple-element.127), channel_id=1, source_target_pairs={{4,12},{5,13},{6,14},{7,15},{8,0},{9,1},{10,2},{11,3},{20,28},{21,... | collective-permute-start | bytes 1769480 | tf_op jit(solution)/shard_map/ppermute | solution.py:399
  142.6 1.3 copy-start.14
  142.6 47.5 %collective-permute-start.18 = (bf16[12,128,128]{2,1,0:T(8,128)(2,1)}, bf16[12,128,128]{2,1,0:T(8,128)(2,1)S(1)}, u32[]{:S(2)}, u32[]{:S(2)}) collective-permute-start(bf16[12,128,128]{2,1,0:T(8,128)(2,1)} %get-tuple-element.126), channel_id=1, source_target_pairs={{4,12},{5,13},{6,14},{7,15},{8,0},{9,1},{10,2},{11,3},{20,28},{21,... | collective-permute-start | bytes 1179656 | tf_op jit(solution)/shard_map/ppermute | solution.py:399
  143.9 0.8 copy-start.15
  144.7 49.5 %collective-permute-start.17 = (bf16[6,128,128]{2,1,0:T(8,128)(2,1)}, bf16[6,128,128]{2,1,0:T(8,128)(2,1)}, u32[]{:S(2)}, u32[]{:S(2)}) collective-permute-start(bf16[6,128,128]{2,1,0:T(8,128)(2,1)} %get-tuple-element.125), channel_id=1, source_target_pairs={{4,12},{5,13},{6,14},{7,15},{8,0},{9,1},{10,2},{11,3},{20,28},{21,... | collective-permute-start | bytes 589832 | tf_op jit(solution)/shard_map/ppermute | solution.py:399
  146.6 22.4 %copy-start.6 = (s32[273]{0:T(512)S(1)}, s32[273]{0:T(512)}, u32[]{:S(2)}) copy-start(s32[273]{0:T(512)} %tables.5.far_table.table) | copy-start | bytes 3280
  169.0 3.4 %copy-start = (f32[16,128,1024]{2,1,0:T(8,128)S(1)}, f32[16,128,1024]{2,1,0:T(8,128)}, u32[]{:S(2)}) copy-start(f32[16,128,1024]{2,1,0:T(8,128)} %get-tuple-element.136.refs_3_) | copy-start | bytes 25165828
  172.4 3.4 %copy-start.1 = (bf16[32,128,1024]{2,1,0:T(8,128)(2,1)S(1)}, bf16[32,128,1024]{2,1,0:T(8,128)(2,1)}, u32[]{:S(2)}) copy-start(bf16[32,128,1024]{2,1,0:T(8,128)(2,1)} %get-tuple-element.137.refs_4_.refs_3_) | copy-start | bytes 25165828

commit v19 on v18

--- a/solution.py
+++ b/solution.py
@@ -13,10 +13,12 @@
 SHARES = (30, 9, 6)
 COLUMNS = 256
 MIB = 1024 * 1024
+GRANT = 36
 FAR_COST = 4 * 10**9
 SMEM = pl.BlockSpec(memory_space=pltpu.SMEM)
 VMEM = pl.BlockSpec(memory_space=pltpu.VMEM)
 ANY = pl.BlockSpec(memory_space=pl.ANY)
+HBM = pl.BlockSpec(memory_space=pltpu.HBM)
 
 
 def flip_matrix(columns):
@@ -149,7 +151,7 @@
 def payload_of(at_end, tiles, received):
     return pl.pallas_call(
         payload_kernel,
-        in_specs=[SMEM, ANY, ANY],
+        in_specs=[SMEM, HBM, ANY],
         out_specs=ANY,
         out_shape=jax.ShapeDtypeStruct(received.shape, received.dtype),
         input_output_aliases={2: 0},
@@ -182,9 +184,11 @@
     far_slots = table_views(far_table, tiles_ref.shape[0], PPD)[3]
     pieces = refs[: len(counts)]
     refs = refs[len(counts) :]
-    if not fresh:
-        sum_in, refs = refs[0], refs[2:]
-    sum_out, flip_out, own_blocks, far_blocks, sums, own_list, far_list, own_sems, far_sems, row_sems = refs
+    if fresh:
+        sum_out, flip_out, sums, *refs = refs
+    else:
+        sum_in, flip_in, sums, flip_out, flip_sem, *refs = refs
+    own_blocks, far_blocks, own_list, far_list, own_sems, far_sems, row_sems = refs
 
     def fetch(slots, landing, sems, fetched):
         found = jnp.int32(0)
@@ -206,8 +210,10 @@
     far_found = fetch(far_slots, far_blocks, far_sems, far_list)
     own_found = fetch(own_slots, own_blocks, own_sems, own_list)
     if not fresh:
+        pltpu.make_async_copy(flip_in, flip_out, flip_sem).start()
         for row in range(PPD):
             pltpu.make_async_copy(sum_in.at[row], sums.at[row], row_sems.at[row]).start()
+        pltpu.make_async_copy(flip_in, flip_out, flip_sem).wait()
 
     def arrived(landing, sems, slot):
         pltpu.make_async_copy(landing.at[slot], landing.at[slot], sems.at[slot]).wait()
@@ -219,10 +225,12 @@
     def _(number):
         slot = far_list[number]
         arrived(far_blocks, far_sems, slot)
-        far_blocks[slot] = jnp.dot(
-            far_blocks[slot], perm_ref[...], preferred_element_type=jnp.float32
-        ).astype(jnp.bfloat16)
-        flip_store(slot).start()
+        turned = jnp.dot(far_blocks[slot], perm_ref[...], preferred_element_type=jnp.float32).astype(jnp.bfloat16)
+        if fresh:
+            far_blocks[slot] = turned
+            flip_store(slot).start()
+        else:
+            flip_out[slot] = turned
 
     @pl.loop(0, own_found)
     def _(number):
@@ -245,15 +253,18 @@
             lambda place: tiles_ref[tile_at[place]],
             lambda place, window: own_blocks[block_at[place], :, window],
         )
-        store(row).start()
-
-    @pl.loop(0, far_found)
-    def _(number):
-        flip_store(far_list[number]).wait()
-
-    @pl.loop(0, PPD)
-    def _(row):
-        store(row).wait()
+        if fresh:
+            store(row).start()
+
+    if fresh:
+
+        @pl.loop(0, far_found)
+        def _(number):
+            flip_store(far_list[number]).wait()
+
+        @pl.loop(0, PPD)
+        def _(row):
+            store(row).wait()
 
 
 def own_part(own_table, far_table, tiles, pieces, firsts, perm, groups=PPD, group=0, earlier=()):
@@ -261,27 +272,32 @@
     depth, width = pieces[0].shape[1:]
     need = count // REUSE
     counts = [piece.shape[0] for piece in pieces]
-    operands = 5 + len(pieces)
+    whole = (PPD, height, width)
+    flips = (need, depth, width)
+    if earlier:
+        out_specs = [VMEM] * 2
+        out_shape = [pltpu.VMEM(whole, jnp.float32), pltpu.VMEM(flips, jnp.bfloat16)]
+        first_scratch = pltpu.SemaphoreType.DMA
+    else:
+        out_specs = [ANY] * 2
+        out_shape = [jax.ShapeDtypeStruct(whole, jnp.float32), jax.ShapeDtypeStruct(flips, jnp.bfloat16)]
+        first_scratch = pltpu.VMEM(whole, jnp.float32)
     return pl.pallas_call(
         functools.partial(own_kernel, counts, groups, group, not earlier),
         in_specs=[SMEM] * 3 + [VMEM] * 2 + [ANY] * (len(pieces) + len(earlier)),
-        out_specs=[ANY] * 2,
-        out_shape=[
-            jax.ShapeDtypeStruct((PPD, height, width), jnp.float32),
-            jax.ShapeDtypeStruct((need, depth, width), jnp.bfloat16),
-        ],
-        input_output_aliases={operands: 0, operands + 1: 1} if earlier else {},
+        out_specs=out_specs,
+        out_shape=out_shape,
         scratch_shapes=[
-            pltpu.VMEM((need, depth, width), jnp.bfloat16),
-            pltpu.VMEM((need, depth, width), jnp.bfloat16),
-            pltpu.VMEM((PPD, height, width), jnp.float32),
+            first_scratch,
+            pltpu.VMEM(flips, jnp.bfloat16),
+            pltpu.VMEM(flips, jnp.bfloat16),
             pltpu.SMEM((need,), jnp.int32),
             pltpu.SMEM((need,), jnp.int32),
             pltpu.SemaphoreType.DMA((need,)),
             pltpu.SemaphoreType.DMA((need,)),
             pltpu.SemaphoreType.DMA((PPD,)),
         ],
-        compiler_params=pltpu.CompilerParams(vmem_limit_bytes=56 * MIB),
+        compiler_params=pltpu.CompilerParams(vmem_limit_bytes=(GRANT if earlier else 56) * MIB),
         name="own_part",
     )(own_table, far_table, firsts, tiles, perm, *pieces, *earlier)
 
@@ -290,8 +306,8 @@
     starts, _, block_at, _ = table_views(table, total_count, PPD)
     tile_refs, refs = refs[: len(segments)], refs[len(segments) :]
     sum_in, flip_in = refs[:2]
-    refs = refs[3:] if base else refs[2:]
-    sum_out, result, tiles_ref, sums, rounded, tile_sem, row_sems, out_sems = refs
+    carry_in = refs[2] if base else None
+    carry_out, result, tiles_ref, sums, rounded, tile_sem, row_sems, out_sems = refs[4:] if base else refs[2:]
     count = tiles_ref.shape[0]
     stop = base + count
 
@@ -320,20 +336,31 @@
                 action(row, last <= stop)
 
     def load(row):
-        return pltpu.make_async_copy(sum_in.at[row], sums.at[row], row_sems.at[row])
+        if base:
+            goes_on = starts[row] < base
+
+            @pl.when(goes_on)
+            def _():
+                pltpu.make_async_copy(carry_in, sums.at[row], row_sems.at[row]).start()
+
+            @pl.when(jnp.logical_not(goes_on))
+            def _():
+                pltpu.make_async_copy(sum_in.at[row], sums.at[row], row_sems.at[row]).start()
+        else:
+            pltpu.make_async_copy(sum_in.at[row], sums.at[row], row_sems.at[row]).start()
 
     def store(row):
         return pltpu.make_async_copy(rounded.at[row], result.at[row], out_sems.at[row])
 
     def keep(row):
-        return pltpu.make_async_copy(sums.at[row], sum_out.at[row], out_sems.at[row])
-
-    each_row(lambda row, complete: load(row).start())
+        return pltpu.make_async_copy(sums.at[row], carry_out, out_sems.at[row])
+
+    each_row(lambda row, complete: load(row))
     pltpu.make_async_copy(tiles_ref, tiles_ref, tile_sem).wait()
 
     def add(row, complete):
         begin, end = jnp.maximum(starts[row], base), jnp.minimum(starts[row + 1], stop)
-        load(row).wait()
+        pltpu.make_async_copy(sums.at[row], sums.at[row], row_sems.at[row]).wait()
 
         add_row(
             sums.at[row],
@@ -361,23 +388,20 @@
     each_row(finish)
 
 
-def far_part(base, count, total_count, far_table, chosen, sources, flipped, total, result=None):
+def far_part(base, count, total_count, far_table, chosen, sources, flipped, total, earlier=()):
     whole = total.shape
-    given = [] if result is None else [result]
     held = [array.size // (whole[1] * flipped.shape[1]) for _, _, array in sources]
     used = [
         (source[:2], source[2])
         for source, size in zip(sources, held)
         if source[1] < base + count and source[1] + size > base
     ]
-    operand = 2 + len(used)
-    aliases = {operand: 0, operand + 2: 1} if given else {operand: 0}
     return pl.pallas_call(
         functools.partial(far_kernel, base, total_count, [segment for segment, _ in used]),
-        in_specs=[SMEM] * 2 + [ANY] * (len(used) + 1) + [VMEM] + [ANY] * len(given),
+        in_specs=[SMEM] * 2 + [ANY] * len(used) + [VMEM] * 2 + [ANY] * len(earlier),
         out_specs=[ANY] * 2,
-        out_shape=[jax.ShapeDtypeStruct(whole, jnp.float32), jax.ShapeDtypeStruct(whole, jnp.bfloat16)],
-        input_output_aliases=aliases,
+        out_shape=[jax.ShapeDtypeStruct(whole[1:], jnp.float32), jax.ShapeDtypeStruct(whole, jnp.bfloat16)],
+        input_output_aliases={5 + len(used): 1} if earlier else {},
         scratch_shapes=[
             pltpu.VMEM((count, whole[1], flipped.shape[1]), jnp.bfloat16),
             pltpu.VMEM(whole, jnp.float32),
@@ -386,9 +410,9 @@
             pltpu.SemaphoreType.DMA((PPD,)),
             pltpu.SemaphoreType.DMA((PPD,)),
         ],
-        compiler_params=pltpu.CompilerParams(vmem_limit_bytes=26 * MIB),
+        compiler_params=pltpu.CompilerParams(vmem_limit_bytes=24 * MIB),
         name="far_part",
-    )(far_table, chosen, *[array for _, array in used], total, flipped, *given)
+    )(far_table, chosen, *[array for _, array in used], total, flipped, *earlier)
 
 
 def together(*values):
@@ -499,11 +523,11 @@
 
 
 def far_products(far_table, chosen, sources, sizes, flipped, total):
-    base, result = 0, None
+    base, earlier = 0, ()
     for size in sizes:
-        total, result = far_part(base, size, sum(sizes), far_table, chosen, sources, flipped, total, result)
+        earlier = far_part(base, size, sum(sizes), far_table, chosen, sources, flipped, total, earlier)
         base += size
-    return result
+    return earlier[1]
 
 
 def per_device(t2_tiles, t2_row, t2_col, integrals):

time: 198 us -> 196 us (0.990)
  local copies, waits for them, and re-layouts: 15.2 us -> 6.46 us
  Pallas kernels: 76.8 us -> 82.6 us
    unnamed x32, local copies, waits for them, and re-layouts: 13.4 us -> 5.18 us
    pallas_call x2, Pallas kernels: 37.7 us -> 44.1 us  [own_part(): pl.pallas_call(functools.partial(own_kernel, counts, groups, group, not e...]
  transfers between devices with their start and end apart: 26 -> 26, of which waited for: 9 -> 11; matrix products, arithmetic and copies ran while one was open for 4% -> 3% of each run, Pallas kernels for 37% -> 41%
where the time goes in v19:
time: 196 us
  Pallas kernels  82.6 us (42%)
  starting transfers between devices  54.3 us (28%)
  waiting for transfers between devices  47.3 us (24%)
  local copies, waits for them, and re-layouts  6.46 us (3%)
  other arithmetic  4.88 us (2%)
    ppermute x26, starting transfers between devices, send(): return lax.ppermute(value, 'tile', pairs)  54.3 us
    ppermute x26, waiting for transfers between devices, send(): return lax.ppermute(value, 'tile', pairs)  47.3 us
    pallas_call x2, Pallas kernels, own_part(): pl.pallas_call(functools.partial(own_kernel, counts, groups, group, not e...  44.1 us
    pallas_call x4, Pallas kernels, far_part(): pl.pallas_call(functools.partial(far_kernel, base, total_count, [segment...  20.5 us
    pallas_call x3, Pallas kernels, tables(): pl.pallas_call(tables_kernel, in_specs=[SMEM] * 2, out_specs=SMEM, out_sh...  12.4 us
    pallas_call x1, Pallas kernels, sort_tiles(): pl.pallas_call(functools.partial(sort_kernel, choices), in_specs=[SMEM] *...  5.35 us
    unnamed x32, local copies, waits for them, and re-layouts  5.18 us
  transfers between devices with their start and end apart: 26, of which 11 were waited for; matrix products, arithmetic and copies ran while one was open for 3% of the time, Pallas kernels for 41%

profile of v19, /device:TPU:0, one launch (start us, length us, event | category | flops | bytes accessed | tf_op | source)
XLA Modules:
  0.0 196.0 jit_solution(15514382747228268886)
XLA Ops:
  0.0 0.7 collective-permute-start
  0.7 0.5 collective-permute-start.3
  1.2 5.4 %collective-permute-start.2 = (bf16[4,128,1024]{2,1,0:T(8,128)(2,1)}, bf16[4,128,1024]{2,1,0:T(8,128)(2,1)}, u32[]{:S(2)}, u32[]{:S(2)}) collective-permute-start(bf16[4,128,1024]{2,1,0:T(8,128)(2,1)} %refs_0_.1), channel_id=1, source_target_pairs={{0,4},{1,5},{2,6},{3,7},{4,0},{5,1},{6,2},{7,3},{8,12},{9,13},{10,... | collective-permute-start | bytes 3145736 | tf_op jit(solution)/shard_map/ppermute | solution.py:423
  6.7 1.5 collective-permute-start.4
  8.2 0.7 pad_add_fusion
  8.9 4.1 %tables.3.table = s32[273]{0:T(512)} custom-call(s32[96]{0:T(128)} %rows.1, s32[96]{0:T(128)} %cols.3), custom_call_target="tpu_custom_call" | custom-call | tf_op jit(solution)/shard_map/tables/pallas_call | solution.py:88
  13.0 1.2 fusion.6.rows
  14.3 1.9 copy-done
  16.2 0.7 copy-done.7
  16.8 5.4 %sort_tiles.1 = (bf16[4,128,1024]{2,1,0:T(8,128)(2,1)S(1)}, bf16[4,128,1024]{2,1,0:T(8,128)(2,1)S(1)}, bf16[32,128,128]{2,1,0:T(8,128)(2,1)}, bf16[60,128,128]{2...) custom-call(s32[273]{0:T(512)S(1)} %copy-done.7, ...), custom_call_target="tpu_custom_call" | custom-call | tf_op jit(solution)/shard_map/sort_tiles/pallas_call | solution.py:130
  22.2 0.0 collective-permute-done.received
  22.2 0.1 payload.2
  22.3 8.8 %collective-permute-start.1 = (bf16[4,128,1024]{2,1,0:T(8,128)(2,1)S(1)}, bf16[4,128,1024]{2,1,0:T(8,128)(2,1)S(1)}, u32[]{:S(2)}, u32[]{:S(2)}) collective-permute-start(bf16[4,128,1024]{2,1,0:T(8,128)(2,1)S(1)} %payload.2), channel_id=1, source_target_pairs={{4,0},{5,1},{6,2},{7,3},{8,12},{9,13},{10,14},{11,15},{0,8},{1,9},... | collective-permute-start | bytes 3145736 | tf_op jit(solution)/shard_map/ppermute | solution.py:423
  31.1 0.5 slice_bitcast_fusion
  31.6 0.0 collective-permute-done.2.refs_2_
  31.6 0.6 collective-permute-done.4.refs_6_
  32.2 0.4 copy-done.9
  32.6 0.7 collective-permute-start.8
  33.4 0.1 collective-permute-start.6
  33.4 1.6 collective-permute-start.5
  35.0 4.1 %tables.5.far_table.table = s32[273]{0:T(512)} custom-call(s32[96]{0:T(128)} %get-tuple-element.148.rows, s32[96]{0:T(128)} %get-tuple-element.147.cols), custom_call_target="tpu_custom_call" | custom-call | flops 4000000000 | tf_op jit(solution)/shard_map/tables/pallas_call | solution.py:88
  39.2 4.2 %tables.4.own_table = s32[289]{0:T(512)} custom-call(s32[96]{0:T(128)} %fusion.6.rows, s32[96]{0:T(128)} %cols.3), custom_call_target="tpu_custom_call" | custom-call | tf_op jit(solution)/shard_map/tables/pallas_call | solution.py:88
  43.4 1.7 compare_convert_fusion.perm_ref
  45.1 8.0 %collective-permute-done.1.refs_0_ = bf16[4,128,1024]{2,1,0:T(8,128)(2,1)S(1)} collective-permute-done((bf16[4,128,1024]{2,1,0:T(8,128)(2,1)S(1)}, bf16[4,128,1024]{2,1,0:T(8,128)(2,1)S(1)}, u32[]{:S(2)}, u32[]{:S(2)}) %collective-permute-start.1) | collective-permute-done | bytes 1048608 | tf_op jit(solution)/shard_map/ppermute | solution.py:423
  53.1 0.1 broadcast_select_fusion.refs_4_
  53.2 0.0 collective-permute-done.6.refs_3_
  53.2 6.1 %collective-permute-done.5.refs_8_ = bf16[4,128,1024]{2,1,0:T(8,128)(2,1)} collective-permute-done((bf16[4,128,1024]{2,1,0:T(8,128)(2,1)}, bf16[4,128,1024]{2,1,0:T(8,128)(2,1)}, u32[]{:S(2)}, u32[]{:S(2)}) %collective-permute-start.5) | collective-permute-done | bytes 1048608 | tf_op jit(solution)/shard_map/ppermute | solution.py:423
  59.3 0.0 collective-permute-start.11
  59.4 0.1 payload.3
  59.5 19.2 %collective-permute-start.9 = (bf16[4,128,1024]{2,1,0:T(8,128)(2,1)S(1)}, bf16[4,128,1024]{2,1,0:T(8,128)(2,1)S(1)}, u32[]{:S(2)}, u32[]{:S(2)}) collective-permute-start(bf16[4,128,1024]{2,1,0:T(8,128)(2,1)S(1)} %payload.3), channel_id=1, source_target_pairs={{4,0},{5,1},{6,2},{7,3},{8,12},{9,13},{10,14},{11,15},{0,8},{1,9},... | collective-permute-start | bytes 3145736 | tf_op jit(solution)/shard_map/ppermute | solution.py:423
  78.7 0.5 collective-permute-start.13
  79.2 1.5 collective-permute-start.10
  80.7 1.3 collective-permute-start.25
  82.0 19.3 %collective-permute-done.9.refs_1_.refs_0_ = bf16[4,128,1024]{2,1,0:T(8,128)(2,1)S(1)} collective-permute-done((bf16[4,128,1024]{2,1,0:T(8,128)(2,1)S(1)}, bf16[4,128,1024]{2,1,0:T(8,128)(2,1)S(1)}, u32[]{:S(2)}, u32[]{:S(2)}) %collective-permute-start.9) | collective-permute-done | bytes 1048608 | tf_op jit(solution)/shard_map/ppermute | solution.py:423
  101.3 5.4 %collective-permute-start.16 = (bf16[32,128,128]{2,1,0:T(8,128)(2,1)}, bf16[32,128,128]{2,1,0:T(8,128)(2,1)S(1)}, u32[]{:S(2)}, u32[]{:S(2)}) collective-permute-start(bf16[32,128,128]{2,1,0:T(8,128)(2,1)} %get-tuple-element.123), channel_id=1, source_target_pairs={{0,8},{1,9},{2,10},{3,11},{12,4},{13,5},{14,6},{15,7},{16,24},{17,... | collective-permute-start | bytes 3145736 | tf_op jit(solution)/shard_map/ppermute | solution.py:423
  106.7 1.1 slice_select_fusion
  107.9 1.0 copy-done.11
  108.8 0.3 copy-done.12
  109.2 1.5 collective-permute-start.14
  110.7 0.5 collective-permute-start.15
  111.2 0.7 stack.89.firsts
  111.9 23.6 %own_part.2 = (f32[16,128,1024]{2,1,0:T(8,128)}, bf16[32,128,1024]{2,1,0:T(8,128)(2,1)}) custom-call(s32[289]{0:T(512)} %tables.4.own_table, s32[273]{0:T(512)} %tables.5.far_table.table, s32[11]{0:T(128)} %stack.89.firsts, bf16[96,128,128]{2,1,0:T(8,128)(2,1)} %tiles_ref.5, bf16[1024,1024]{1,0:T(8,128)(2,1)} %compare_convert_fusion.perm_ref, ...), custom_call_target="tpu_custom_call" | custom-call | tf_op jit(solution)/shard_map/own_part/pallas_call | solution.py:285
  135.5 0.1 collective-permute-start.19
  135.5 0.5 collective-permute-start.20
  136.0 0.1 collective-permute-start.18
  136.1 0.4 collective-permute-start.21
  136.6 1.1 collective-permute-done.19.refs_3_
  137.7 0.1 collective-permute-start.22
  137.8 1.4 collective-permute-done.20.refs_4_
  139.2 1.3 collective-permute-start.24
  140.4 0.2 collective-permute-done.21.refs_7_
  140.7 1.3 collective-permute-start.23
  142.0 0.8 copy-done.15
  142.8 1.3 collective-permute-start.17
  144.1 0.1 stack.99.firsts
  144.3 20.6 %own_part.3 = (f32[16,128,1024]{2,1,0:T(8,128)S(1)}, bf16[32,128,1024]{2,1,0:T(8,128)(2,1)S(1)}) custom-call(s32[289]{0:T(512)S(1)} %copy-done.6, s32[273]{0:T(512)S(1)} %copy-done.5, s32[9]{0:T(128)S(1)} %stack.99.firsts, bf16[96,128,128]{2,1,0:T(8,128)(2,1)} %tiles_ref.5, bf16[1024,1024]{1,0:T(8,128)(2,1)} %compare_convert_fusion.perm_ref, ...), custom_call_target="tpu_custom_call" | custom-call | tf_op jit(solution)/shard_map/own_part/pallas_call | solution.py:285
  164.8 3.1 %collective-permute-done.25.refs_2_ = bf16[60,128,128]{2,1,0:T(8,128)(2,1)} collective-permute-done((bf16[60,128,128]{2,1,0:T(8,128)(2,1)}, bf16[60,128,128]{2,1,0:T(8,128)(2,1)}, u32[]{:S(2)}, u32[]{:S(2)}) %collective-permute-start.25) | collective-permute-done | bytes 1966112 | tf_op jit(solution)/shard_map/ppermute | solution.py:423
  167.9 9.7 %far_part.4 = (f32[128,1024]{1,0:T(8,128)S(1)}, bf16[16,128,1024]{2,1,0:T(8,128)(2,1)}) custom-call(s32[273]{0:T(512)S(1)} %copy-done.5, s32[1]{0:T(128)} %bitcast.chosen.at_end, bf16[4,128,1024]{2,1,0:T(8,128)(2,1)S(1)} %copy-done.2, bf16[4,128,1024]{2,1,0:T(8,128)(2,1)S(1)} %collective-permute-done.9.refs_1_.refs_0_, ...), custom_call_target="tpu_custom_call" | custom-call | tf_op jit(solution)/shard_map/far_part/pallas_call | solution.py:399
  177.6 2.8 %collective-permute-done.24.refs_2_ = bf16[18,128,128]{2,1,0:T(8,128)(2,1)S(1)} collective-permute-done((bf16[18,128,128]{2,1,0:T(8,128)(2,1)}, bf16[18,128,128]{2,1,0:T(8,128)(2,1)S(1)}, u32[]{:S(2)}, u32[]{:S(2)}) %collective-permute-start.24) | collective-permute-done | bytes 589856 | tf_op jit(solution)/shard_map/ppermute | solution.py:423
  180.4 3.8 %far_part.5 = (f32[128,1024]{1,0:T(8,128)S(1)}, bf16[16,128,1024]{2,1,0:T(8,128)(2,1)}) custom-call(s32[273]{0:T(512)S(1)} %copy-done.5, s32[1]{0:T(128)} %bitcast.chosen.at_end, bf16[4,128,1024]{2,1,0:T(8,128)(2,1)S(1)} %collective-permute-done.9.refs_1_.refs_0_, ...), custom_call_target="tpu_custom_call", output_to_operand_aliasing={{1}: (8, {})} | custom-call | tf_op jit(solution)/shard_map/far_part/pallas_call | solution.py:399
  184.3 4.7 %collective-permute-done.23.refs_1_ = bf16[12,128,128]{2,1,0:T(8,128)(2,1)} collective-permute-done((bf16[12,128,128]{2,1,0:T(8,128)(2,1)}, bf16[12,128,128]{2,1,0:T(8,128)(2,1)}, u32[]{:S(2)}, u32[]{:S(2)}) %collective-permute-start.23) | collective-permute-done | bytes 393248 | tf_op jit(solution)/shard_map/ppermute | solution.py:423
  189.0 3.9 %far_part.6 = (f32[128,1024]{1,0:T(8,128)S(1)}, bf16[16,128,1024]{2,1,0:T(8,128)(2,1)}) custom-call(s32[273]{0:T(512)S(1)} %copy-done.5, s32[1]{0:T(128)} %bitcast.chosen.at_end, bf16[32,128,128]{2,1,0:T(8,128)(2,1)S(1)} %collective-permute-done.16.refs_1_.refs_0_, ...), custom_call_target="tpu_custom_call", output_to_operand_aliasing={{1}: (7, {})} | custom-call | tf_op jit(solution)/shard_map/far_part/pallas_call | solution.py:399
  192.9 0.1 collective-permute-done.17.refs_1_
  193.0 3.0 %far_part.7 = (f32[128,1024]{1,0:T(8,128)}, bf16[16,128,1024]{2,1,0:T(8,128)(2,1)}) custom-call(s32[273]{0:T(512)S(1)} %copy-done.5, s32[1]{0:T(128)} %bitcast.chosen.at_end, bf16[32,128,128]{2,1,0:T(8,128)(2,1)S(1)} %collective-permute-done.16.refs_1_.refs_0_, ...), custom_call_target="tpu_custom_call", output_to_operand_aliasing={{1}: (7, {})} | custom-call | tf_op jit(solution)/shard_map/far_part/pallas_call | solution.py:399
  (42 shorter events, 0.1 us)
Async XLA Ops:
  0.0 22.2 %collective-permute-start = (bf16[4,128,1024]{2,1,0:T(8,128)(2,1)}, bf16[4,128,1024]{2,1,0:T(8,128)(2,1)S(1)}, u32[]{:S(2)}, u32[]{:S(2)}) collective-permute-start(bf16[4,128,1024]{2,1,0:T(8,128)(2,1)} %refs_0_.1), channel_id=1, source_target_pairs={{4,8},{5,9},{6,10},{7,11},{8,4},{9,5},{10,6},{11,7},{20,24},{21,25... | collective-permute-start | bytes 3145736 | tf_op jit(solution)/shard_map/ppermute | solution.py:423
  0.7 30.9 %collective-permute-start.3 = (bf16[4,128,1024]{2,1,0:T(8,128)(2,1)}, bf16[4,128,1024]{2,1,0:T(8,128)(2,1)S(1)}, u32[]{:S(2)}, u32[]{:S(2)}) collective-permute-start(bf16[4,128,1024]{2,1,0:T(8,128)(2,1)} %refs_0_.1), channel_id=1, source_target_pairs={{0,1},{1,0},{2,3},{3,2},{4,5},{5,4},{6,7},{7,6},{8,9},{9,8},{10,11... | collective-permute-start | bytes 3145736 | tf_op jit(solution)/shard_map/ppermute | solution.py:423
  1.2 30.4 %collective-permute-start.2 = (bf16[4,128,1024]{2,1,0:T(8,128)(2,1)}, bf16[4,128,1024]{2,1,0:T(8,128)(2,1)}, u32[]{:S(2)}, u32[]{:S(2)}) collective-permute-start(bf16[4,128,1024]{2,1,0:T(8,128)(2,1)} %refs_0_.1), channel_id=1, source_target_pairs={{0,4},{1,5},{2,6},{3,7},{4,0},{5,1},{6,2},{7,3},{8,12},{9,13},{10,... | collective-permute-start | bytes 3145736 | tf_op jit(solution)/shard_map/ppermute | solution.py:423
  6.7 25.5 %collective-permute-start.4 = (bf16[4,128,1024]{2,1,0:T(8,128)(2,1)}, bf16[4,128,1024]{2,1,0:T(8,128)(2,1)}, u32[]{:S(2)}, u32[]{:S(2)}) collective-permute-start(bf16[4,128,1024]{2,1,0:T(8,128)(2,1)} %refs_0_.1), channel_id=1, source_target_pairs={{0,2},{1,3},{2,0},{3,1},{4,6},{5,7},{6,4},{7,5},{8,10},{9,11},{10,... | collective-permute-start | bytes 3145736 | tf_op jit(solution)/shard_map/ppermute | solution.py:423
  8.9 22.3 %collective-permute-start.7 = (s32[2,96]{1,0:T(2,128)S(1)}, s32[2,96]{1,0:T(2,128)S(1)}, u32[]{:S(2)}, u32[]{:S(2)}) collective-permute-start(s32[2,96]{1,0:T(2,128)S(1)} %pad_add_fusion), channel_id=1, source_target_pairs={{0,8},{1,9},{2,10},{3,11},{4,12},{5,13},{6,14},{7,15},{8,0},{9,1},... | collective-permute-start | bytes 2312 | tf_op jit(solution)/shard_map/ppermute | solution.py:423
  14.3 1.9 copy-start
  16.2 0.7 copy-start.7
  22.2 10.0 %copy-start.3 = (bf16[4,128,1024]{2,1,0:T(8,128)(2,1)}, bf16[4,128,1024]{2,1,0:T(8,128)(2,1)S(1)}, u32[]{:S(2)}) copy-start(bf16[4,128,1024]{2,1,0:T(8,128)(2,1)S(1)} %get-tuple-element.100.tiles_ref) | copy-start | bytes 3145732
  22.3 30.8 %collective-permute-start.1 = (bf16[4,128,1024]{2,1,0:T(8,128)(2,1)S(1)}, bf16[4,128,1024]{2,1,0:T(8,128)(2,1)S(1)}, u32[]{:S(2)}, u32[]{:S(2)}) collective-permute-start(bf16[4,128,1024]{2,1,0:T(8,128)(2,1)S(1)} %payload.2), channel_id=1, source_target_pairs={{4,0},{5,1},{6,2},{7,3},{8,12},{9,13},{10,14},{11,15},{0,8},{1,9},... | collective-permute-start | bytes 3145736 | tf_op jit(solution)/shard_map/ppermute | solution.py:423
  31.6 1.0 copy-start.9
  32.6 26.7 %collective-permute-start.8 = (bf16[4,128,1024]{2,1,0:T(8,128)(2,1)}, bf16[4,128,1024]{2,1,0:T(8,128)(2,1)S(1)}, u32[]{:S(2)}, u32[]{:S(2)}) collective-permute-start(bf16[4,128,1024]{2,1,0:T(8,128)(2,1)} %collective-permute-done.2.refs_2_), channel_id=1, source_target_pairs={{4,8},{5,9},{6,10},{7,11},{8,4},{9,5},{10,6},{11,7},{20,24},{21,25... | collective-permute-start | bytes 3145736 | tf_op jit(solution)/shard_map/ppermute | solution.py:423
  33.4 19.9 %collective-permute-start.6 = (bf16[4,128,1024]{2,1,0:T(8,128)(2,1)}, bf16[4,128,1024]{2,1,0:T(8,128)(2,1)}, u32[]{:S(2)}, u32[]{:S(2)}) collective-permute-start(bf16[4,128,1024]{2,1,0:T(8,128)(2,1)} %collective-permute-done.2.refs_2_), channel_id=1, source_target_pairs={{0,1},{1,0},{2,3},{3,2},{4,5},{5,4},{6,7},{7,6},{8,9},{9,8},{10,11... | collective-permute-start | bytes 3145736 | tf_op jit(solution)/shard_map/ppermute | solution.py:423
  33.4 25.9 %collective-permute-start.5 = (bf16[4,128,1024]{2,1,0:T(8,128)(2,1)}, bf16[4,128,1024]{2,1,0:T(8,128)(2,1)}, u32[]{:S(2)}, u32[]{:S(2)}) collective-permute-start(bf16[4,128,1024]{2,1,0:T(8,128)(2,1)} %collective-permute-done.2.refs_2_), channel_id=1, source_target_pairs={{0,2},{1,3},{2,0},{3,1},{4,6},{5,7},{6,4},{7,5},{8,10},{9,11},{10,... | collective-permute-start | bytes 3145736 | tf_op jit(solution)/shard_map/ppermute | solution.py:423
  43.3 16.0 %copy-start.4 = (bf16[4,128,1024]{2,1,0:T(8,128)(2,1)S(1)}, bf16[4,128,1024]{2,1,0:T(8,128)(2,1)}, u32[]{:S(2)}) copy-start(bf16[4,128,1024]{2,1,0:T(8,128)(2,1)} %copy-done.3) | copy-start | bytes 3145732
  53.1 6.2 %copy-start.1 = (bf16[4,128,1024]{2,1,0:T(8,128)(2,1)}, bf16[4,128,1024]{2,1,0:T(8,128)(2,1)S(1)}, u32[]{:S(2)}) copy-start(bf16[4,128,1024]{2,1,0:T(8,128)(2,1)S(1)} %collective-permute-done.1.refs_0_) | copy-start | bytes 3145732
  53.2 54.6 %copy-start.8 = (bf16[4,128,1024]{2,1,0:T(8,128)(2,1)}, bf16[4,128,1024]{2,1,0:T(8,128)(2,1)S(1)}, u32[]{:S(2)}) copy-start(bf16[4,128,1024]{2,1,0:T(8,128)(2,1)S(1)} %broadcast_select_fusion.refs_4_) | copy-start | bytes 3145732
  59.3 21.4 %collective-permute-start.11 = (bf16[4,128,1024]{2,1,0:T(8,128)(2,1)S(1)}, bf16[4,128,1024]{2,1,0:T(8,128)(2,1)S(1)}, u32[]{:S(2)}, u32[]{:S(2)}) collective-permute-start(bf16[4,128,1024]{2,1,0:T(8,128)(2,1)S(1)} %broadcast_select_fusion.refs_4_), channel_id=1, source_target_pairs={{0,1},{1,0},{2,3},{3,2},{4,5},{5,4},{6,7},{7,6},{8,9},{9,8},{10,11... | collective-permute-start | bytes 3145736 | tf_op jit(solution)/shard_map/ppermute | solution.py:423
  59.5 41.9 %collective-permute-start.9 = (bf16[4,128,1024]{2,1,0:T(8,128)(2,1)S(1)}, bf16[4,128,1024]{2,1,0:T(8,128)(2,1)S(1)}, u32[]{:S(2)}, u32[]{:S(2)}) collective-permute-start(bf16[4,128,1024]{2,1,0:T(8,128)(2,1)S(1)} %payload.3), channel_id=1, source_target_pairs={{4,0},{5,1},{6,2},{7,3},{8,12},{9,13},{10,14},{11,15},{0,8},{1,9},... | collective-permute-start | bytes 3145736 | tf_op jit(solution)/shard_map/ppermute | solution.py:423
  78.7 29.2 %collective-permute-start.12 = (bf16[4,128,1024]{2,1,0:T(8,128)(2,1)}, bf16[4,128,1024]{2,1,0:T(8,128)(2,1)S(1)}, u32[]{:S(2)}, u32[]{:S(2)}) collective-permute-start(bf16[4,128,1024]{2,1,0:T(8,128)(2,1)} %collective-permute-done.4.refs_6_), channel_id=1, source_target_pairs={{0,1},{1,0},{2,3},{3,2},{4,5},{5,4},{6,7},{7,6},{8,9},{9,8},{10,11... | collective-permute-start | bytes 3145736 | tf_op jit(solution)/shard_map/ppermute | solution.py:423
  78.7 29.2 %collective-permute-start.13 = (bf16[4,128,1024]{2,1,0:T(8,128)(2,1)}, bf16[4,128,1024]{2,1,0:T(8,128)(2,1)S(1)}, u32[]{:S(2)}, u32[]{:S(2)}) collective-permute-start(bf16[4,128,1024]{2,1,0:T(8,128)(2,1)} %collective-permute-done.5.refs_8_), channel_id=1, source_target_pairs={{0,1},{1,0},{2,3},{3,2},{4,5},{5,4},{6,7},{7,6},{8,9},{9,8},{10,11... | collective-permute-start | bytes 3145736 | tf_op jit(solution)/shard_map/ppermute | solution.py:423
  79.2 28.7 %collective-permute-start.10 = (bf16[4,128,1024]{2,1,0:T(8,128)(2,1)S(1)}, bf16[4,128,1024]{2,1,0:T(8,128)(2,1)}, u32[]{:S(2)}, u32[]{:S(2)}) collective-permute-start(bf16[4,128,1024]{2,1,0:T(8,128)(2,1)S(1)} %broadcast_select_fusion.refs_4_), channel_id=1, source_target_pairs={{0,2},{1,3},{2,0},{3,1},{4,6},{5,7},{6,4},{7,5},{8,10},{9,11},{10,... | collective-permute-start | bytes 3145736 | tf_op jit(solution)/shard_map/ppermute | solution.py:423
  80.7 1.3 copy-start.10
  80.7 87.2 %collective-permute-start.25 = (bf16[60,128,128]{2,1,0:T(8,128)(2,1)}, bf16[60,128,128]{2,1,0:T(8,128)(2,1)}, u32[]{:S(2)}, u32[]{:S(2)}) collective-permute-start(bf16[60,128,128]{2,1,0:T(8,128)(2,1)} %get-tuple-element.137), channel_id=1, source_target_pairs={{4,12},{5,13},{6,14},{7,15},{8,0},{9,1},{10,2},{11,3},{20,28},{21,... | collective-permute-start | bytes 5898248 | tf_op jit(solution)/shard_map/ppermute | solution.py:423
  101.3 34.8 %collective-permute-start.16 = (bf16[32,128,128]{2,1,0:T(8,128)(2,1)}, bf16[32,128,128]{2,1,0:T(8,128)(2,1)S(1)}, u32[]{:S(2)}, u32[]{:S(2)}) collective-permute-start(bf16[32,128,128]{2,1,0:T(8,128)(2,1)} %get-tuple-element.123), channel_id=1, source_target_pairs={{0,8},{1,9},{2,10},{3,11},{12,4},{13,5},{14,6},{15,7},{16,24},{17,... | collective-permute-start | bytes 3145736 | tf_op jit(solution)/shard_map/ppermute | solution.py:423
  107.9 1.0 copy-start.11
  107.9 1.3 copy-start.12
  109.2 26.3 %collective-permute-start.14 = (bf16[2,128,1024]{2,1,0:T(8,128)(2,1)}, bf16[2,128,1024]{2,1,0:T(8,128)(2,1)}, u32[]{:S(2)}, u32[]{:S(2)}) collective-permute-start(bf16[2,128,1024]{2,1,0:T(8,128)(2,1)} %get-tuple-element.127.refs_1_), channel_id=1, source_target_pairs={{0,2},{1,3},{2,0},{3,1},{4,6},{5,7},{6,4},{7,5},{8,10},{9,11},{10,... | collective-permute-start | bytes 1572872 | tf_op jit(solution)/shard_map/ppermute | solution.py:423
  110.7 24.8 %collective-permute-start.15 = (bf16[2,128,1024]{2,1,0:T(8,128)(2,1)}, bf16[2,128,1024]{2,1,0:T(8,128)(2,1)}, u32[]{:S(2)}, u32[]{:S(2)}) collective-permute-start(bf16[2,128,1024]{2,1,0:T(8,128)(2,1)} %get-tuple-element.128.refs_2_), channel_id=1, source_target_pairs={{0,2},{1,3},{2,0},{3,1},{4,6},{5,7},{6,4},{7,5},{8,10},{9,11},{10,... | collective-permute-start | bytes 1572872 | tf_op jit(solution)/shard_map/ppermute | solution.py:423
  111.9 32.4 %copy-start.5 = (s32[273]{0:T(512)S(1)}, s32[273]{0:T(512)}, u32[]{:S(2)}) copy-start(s32[273]{0:T(512)} %tables.5.far_table.table) | copy-start | bytes 3280
  111.9 32.4 %copy-start.6 = (s32[289]{0:T(512)S(1)}, s32[289]{0:T(512)}, u32[]{:S(2)}) copy-start(s32[289]{0:T(512)} %tables.4.own_table) | copy-start | bytes 3472
  135.5 2.2 %collective-permute-start.19 = (bf16[2,128,1024]{2,1,0:T(8,128)(2,1)}, bf16[2,128,1024]{2,1,0:T(8,128)(2,1)S(1)}, u32[]{:S(2)}, u32[]{:S(2)}) collective-permute-start(bf16[2,128,1024]{2,1,0:T(8,128)(2,1)} %get-tuple-element.127.refs_1_), channel_id=1, source_target_pairs={{0,1},{1,0},{2,3},{3,2},{4,5},{5,4},{6,7},{7,6},{8,9},{9,8},{10,11... | collective-permute-start | bytes 1572872 | tf_op jit(solution)/shard_map/ppermute | solution.py:423
  135.5 3.6 %collective-permute-start.20 = (bf16[2,128,1024]{2,1,0:T(8,128)(2,1)}, bf16[2,128,1024]{2,1,0:T(8,128)(2,1)S(1)}, u32[]{:S(2)}, u32[]{:S(2)}) collective-permute-start(bf16[2,128,1024]{2,1,0:T(8,128)(2,1)} %get-tuple-element.128.refs_2_), channel_id=1, source_target_pairs={{0,1},{1,0},{2,3},{3,2},{4,5},{5,4},{6,7},{7,6},{8,9},{9,8},{10,11... | collective-permute-start | bytes 1572872 | tf_op jit(solution)/shard_map/ppermute | solution.py:423
  136.0 8.2 %collective-permute-start.18 = (bf16[4,128,1024]{2,1,0:T(8,128)(2,1)}, bf16[4,128,1024]{2,1,0:T(8,128)(2,1)}, u32[]{:S(2)}, u32[]{:S(2)}) collective-permute-start(bf16[4,128,1024]{2,1,0:T(8,128)(2,1)} %collective-permute-done.10.refs_10_), channel_id=1, source_target_pairs={{0,1},{1,0},{2,3},{3,2},{4,5},{5,4},{6,7},{7,6},{8,9},{9,8},{10,11... | collective-permute-start | bytes 3145736 | tf_op jit(solution)/shard_map/ppermute | solution.py:423
  136.1 4.5 %collective-permute-start.21 = (bf16[2,128,1024]{2,1,0:T(8,128)(2,1)}, bf16[2,128,1024]{2,1,0:T(8,128)(2,1)S(1)}, u32[]{:S(2)}, u32[]{:S(2)}) collective-permute-start(bf16[2,128,1024]{2,1,0:T(8,128)(2,1)} %collective-permute-done.14.refs_5_), channel_id=1, source_target_pairs={{0,1},{1,0},{2,3},{3,2},{4,5},{5,4},{6,7},{7,6},{8,9},{9,8},{10,11... | collective-permute-start | bytes 1572872 | tf_op jit(solution)/shard_map/ppermute | solution.py:423
  137.7 4.3 %collective-permute-start.22 = (bf16[2,128,1024]{2,1,0:T(8,128)(2,1)}, bf16[2,128,1024]{2,1,0:T(8,128)(2,1)S(1)}, u32[]{:S(2)}, u32[]{:S(2)}) collective-permute-start(bf16[2,128,1024]{2,1,0:T(8,128)(2,1)} %collective-permute-done.15.refs_6_), channel_id=1, source_target_pairs={{0,1},{1,0},{2,3},{3,2},{4,5},{5,4},{6,7},{7,6},{8,9},{9,8},{10,11... | collective-permute-start | bytes 1572872 | tf_op jit(solution)/shard_map/ppermute | solution.py:423
  139.2 2.8 %copy-start.13 = (bf16[2,128,1024]{2,1,0:T(8,128)(2,1)}, bf16[2,128,1024]{2,1,0:T(8,128)(2,1)S(1)}, u32[]{:S(2)}) copy-start(bf16[2,128,1024]{2,1,0:T(8,128)(2,1)S(1)} %collective-permute-done.20.refs_4_) | copy-start | bytes 1572868
  139.2 41.3 %collective-permute-start.24 = (bf16[18,128,128]{2,1,0:T(8,128)(2,1)}, bf16[18,128,128]{2,1,0:T(8,128)(2,1)S(1)}, u32[]{:S(2)}, u32[]{:S(2)}) collective-permute-start(bf16[18,128,128]{2,1,0:T(8,128)(2,1)} %get-tuple-element.136), channel_id=1, source_target_pairs={{4,12},{5,13},{6,14},{7,15},{8,0},{9,1},{10,2},{11,3},{20,28},{21,... | collective-permute-start | bytes 1769480 | tf_op jit(solution)/shard_map/ppermute | solution.py:423
  140.7 1.3 copy-start.14
  140.7 48.3 %collective-permute-start.23 = (bf16[12,128,128]{2,1,0:T(8,128)(2,1)}, bf16[12,128,128]{2,1,0:T(8,128)(2,1)}, u32[]{:S(2)}, u32[]{:S(2)}) collective-permute-start(bf16[12,128,128]{2,1,0:T(8,128)(2,1)} %get-tuple-element.135), channel_id=1, source_target_pairs={{4,12},{5,13},{6,14},{7,15},{8,0},{9,1},{10,2},{11,3},{20,28},{21,... | collective-permute-start | bytes 1179656 | tf_op jit(solution)/shard_map/ppermute | solution.py:423
  142.0 0.9 copy-start.15
  142.8 50.1 %collective-permute-start.17 = (bf16[6,128,128]{2,1,0:T(8,128)(2,1)}, bf16[6,128,128]{2,1,0:T(8,128)(2,1)S(1)}, u32[]{:S(2)}, u32[]{:S(2)}) collective-permute-start(bf16[6,128,128]{2,1,0:T(8,128)(2,1)} %get-tuple-element.125), channel_id=1, source_target_pairs={{4,12},{5,13},{6,14},{7,15},{8,0},{9,1},{10,2},{11,3},{20,28},{21,... | collective-permute-start | bytes 589832 | tf_op jit(solution)/shard_map/ppermute | solution.py:423
  144.2 23.7 %copy-start.2 = (bf16[4,128,1024]{2,1,0:T(8,128)(2,1)S(1)}, bf16[4,128,1024]{2,1,0:T(8,128)(2,1)}, u32[]{:S(2)}) copy-start(bf16[4,128,1024]{2,1,0:T(8,128)(2,1)} %copy-done.1) | copy-start | bytes 3145732

commit v20 on v19

--- a/solution.py
+++ b/solution.py
@@ -311,7 +311,9 @@
     count = tiles_ref.shape[0]
     stop = base + count
 
-    for source, (choice, begin) in zip(tile_refs, segments):
+    direct, direct_choice = tile_refs[-1], segments[-1][0]
+    copied = list(zip(tile_refs, segments))[:-1]
+    for source, (choice, begin) in copied:
         held = source.shape[0] * source.shape[2] // tiles_ref.shape[2]
         low, high = max(begin, base), min(begin + held, stop)
 
@@ -356,7 +358,16 @@
         return pltpu.make_async_copy(sums.at[row], carry_out, out_sems.at[row])
 
     each_row(lambda row, complete: load(row))
-    pltpu.make_async_copy(tiles_ref, tiles_ref, tile_sem).wait()
+    if copied:
+
+        @pl.when(chosen[0] != direct_choice)
+        def _():
+            pltpu.make_async_copy(tiles_ref, tiles_ref, tile_sem).wait()
+
+    def tile_of(place):
+        if not copied:
+            return direct[place - base]
+        return jnp.where(chosen[0] == direct_choice, direct[place - base], tiles_ref[place - base])
 
     def add(row, complete):
         begin, end = jnp.maximum(starts[row], base), jnp.minimum(starts[row + 1], stop)
@@ -367,7 +378,7 @@
             begin,
             end,
             4,
-            lambda place: tiles_ref[place - base],
+            tile_of,
             lambda place, window: flip_in[block_at[place], :, window],
         )
 
@@ -398,7 +409,7 @@
     ]
     return pl.pallas_call(
         functools.partial(far_kernel, base, total_count, [segment for segment, _ in used]),
-        in_specs=[SMEM] * 2 + [ANY] * len(used) + [VMEM] * 2 + [ANY] * len(earlier),
+        in_specs=[SMEM] * 2 + [ANY] * (len(used) - 1) + [VMEM] * 3 + [ANY] * len(earlier),
         out_specs=[ANY] * 2,
         out_shape=[jax.ShapeDtypeStruct(whole[1:], jnp.float32), jax.ShapeDtypeStruct(whole, jnp.bfloat16)],
         input_output_aliases={5 + len(used): 1} if earlier else {},

time: 196 us -> 196 us (level)
  transfers between devices with their start and end apart: 26 -> 26, of which waited for: 11 -> 11; matrix products, arithmetic and copies ran while one was open for 3% -> 3% of each run, Pallas kernels for 41% -> 40%
where the time goes in v20:
time: 196 us
  Pallas kernels  81.4 us (42%)
  starting transfers between devices  54.3 us (28%)
  waiting for transfers between devices  48.6 us (25%)
  local copies, waits for them, and re-layouts  6.46 us (3%)
  other arithmetic  4.88 us (2%)
    ppermute x26, starting transfers between devices, send(): return lax.ppermute(value, 'tile', pairs)  54.3 us
    ppermute x26, waiting for transfers between devices, send(): return lax.ppermute(value, 'tile', pairs)  48.6 us
    pallas_call x2, Pallas kernels, own_part(): pl.pallas_call(functools.partial(own_kernel, counts, groups, group, not e...  43.5 us
    pallas_call x4, Pallas kernels, far_part(): pl.pallas_call(functools.partial(far_kernel, base, total_count, [segment...  20 us
    pallas_call x3, Pallas kernels, tables(): pl.pallas_call(tables_kernel, in_specs=[SMEM] * 2, out_specs=SMEM, out_sh...  12.4 us
    pallas_call x1, Pallas kernels, sort_tiles(): pl.pallas_call(functools.partial(sort_kernel, choices), in_specs=[SMEM] *...  5.35 us
    unnamed x32, local copies, waits for them, and re-layouts  5.18 us
  transfers between devices with their start and end apart: 26, of which 11 were waited for; matrix products, arithmetic and copies ran while one was open for 3% of the time, Pallas kernels for 40%

profile of v20, /device:TPU:0, one launch (start us, length us, event | category | flops | bytes accessed | tf_op | source)
XLA Modules:
  0.0 196.1 jit_solution(16758196347921976066)
XLA Ops:
  0.0 0.7 collective-permute-start
  0.7 0.5 collective-permute-start.3
  1.2 5.4 %collective-permute-start.2 = (bf16[4,128,1024]{2,1,0:T(8,128)(2,1)}, bf16[4,128,1024]{2,1,0:T(8,128)(2,1)}, u32[]{:S(2)}, u32[]{:S(2)}) collective-permute-start(bf16[4,128,1024]{2,1,0:T(8,128)(2,1)} %refs_0_.1), channel_id=1, source_target_pairs={{0,4},{1,5},{2,6},{3,7},{4,0},{5,1},{6,2},{7,3},{8,12},{9,13},{10,... | collective-permute-start | bytes 3145736 | tf_op jit(solution)/shard_map/ppermute | solution.py:434
  6.7 1.5 collective-permute-start.4
  8.2 0.7 pad_add_fusion
  8.9 0.0 collective-permute-start.7
  8.9 4.1 %tables.3.table = s32[273]{0:T(512)} custom-call(s32[96]{0:T(128)} %rows.1, s32[96]{0:T(128)} %cols.3), custom_call_target="tpu_custom_call" | custom-call | tf_op jit(solution)/shard_map/tables/pallas_call | solution.py:88
  13.0 1.2 fusion.6.rows
  14.3 1.9 copy-done
  16.2 0.7 copy-done.7
  16.8 5.4 %sort_tiles.1 = (bf16[4,128,1024]{2,1,0:T(8,128)(2,1)S(1)}, bf16[4,128,1024]{2,1,0:T(8,128)(2,1)S(1)}, bf16[32,128,128]{2,1,0:T(8,128)(2,1)}, bf16[60,128,128]{2...) custom-call(s32[273]{0:T(512)S(1)} %copy-done.7, ...), custom_call_target="tpu_custom_call" | custom-call | tf_op jit(solution)/shard_map/sort_tiles/pallas_call | solution.py:130
  22.2 0.0 collective-permute-done.received
  22.2 0.1 payload.2
  22.3 8.8 %collective-permute-start.1 = (bf16[4,128,1024]{2,1,0:T(8,128)(2,1)S(1)}, bf16[4,128,1024]{2,1,0:T(8,128)(2,1)S(1)}, u32[]{:S(2)}, u32[]{:S(2)}) collective-permute-start(bf16[4,128,1024]{2,1,0:T(8,128)(2,1)S(1)} %payload.2), channel_id=1, source_target_pairs={{4,0},{5,1},{6,2},{7,3},{8,12},{9,13},{10,14},{11,15},{0,8},{1,9},... | collective-permute-start | bytes 3145736 | tf_op jit(solution)/shard_map/ppermute | solution.py:434
  31.1 0.0 collective-permute-done.7
  31.1 0.5 slice_bitcast_fusion
  31.6 0.6 collective-permute-done.4.refs_6_
  32.2 0.4 copy-done.9
  32.6 0.7 collective-permute-start.8
  33.4 0.1 collective-permute-start.6
  33.4 1.6 collective-permute-start.5
  35.0 4.1 %tables.5.far_table.table = s32[273]{0:T(512)} custom-call(s32[96]{0:T(128)} %get-tuple-element.148.rows, s32[96]{0:T(128)} %get-tuple-element.147.cols), custom_call_target="tpu_custom_call" | custom-call | flops 4000000000 | tf_op jit(solution)/shard_map/tables/pallas_call | solution.py:88
  39.2 4.2 %tables.4.own_table = s32[289]{0:T(512)} custom-call(s32[96]{0:T(128)} %fusion.6.rows, s32[96]{0:T(128)} %cols.3), custom_call_target="tpu_custom_call" | custom-call | tf_op jit(solution)/shard_map/tables/pallas_call | solution.py:88
  43.4 1.7 compare_convert_fusion.perm_ref
  45.1 8.0 %collective-permute-done.1.refs_0_ = bf16[4,128,1024]{2,1,0:T(8,128)(2,1)S(1)} collective-permute-done((bf16[4,128,1024]{2,1,0:T(8,128)(2,1)S(1)}, bf16[4,128,1024]{2,1,0:T(8,128)(2,1)S(1)}, u32[]{:S(2)}, u32[]{:S(2)}) %collective-permute-start.1) | collective-permute-done | bytes 1048608 | tf_op jit(solution)/shard_map/ppermute | solution.py:434
  53.1 0.1 broadcast_select_fusion.refs_4_
  53.2 0.0 collective-permute-done.6.refs_3_
  53.2 6.1 %collective-permute-done.5.refs_8_ = bf16[4,128,1024]{2,1,0:T(8,128)(2,1)} collective-permute-done((bf16[4,128,1024]{2,1,0:T(8,128)(2,1)}, bf16[4,128,1024]{2,1,0:T(8,128)(2,1)}, u32[]{:S(2)}, u32[]{:S(2)}) %collective-permute-start.5) | collective-permute-done | bytes 1048608 | tf_op jit(solution)/shard_map/ppermute | solution.py:434
  59.4 0.1 payload.3
  59.5 19.2 %collective-permute-start.9 = (bf16[4,128,1024]{2,1,0:T(8,128)(2,1)S(1)}, bf16[4,128,1024]{2,1,0:T(8,128)(2,1)S(1)}, u32[]{:S(2)}, u32[]{:S(2)}) collective-permute-start(bf16[4,128,1024]{2,1,0:T(8,128)(2,1)S(1)} %payload.3), channel_id=1, source_target_pairs={{4,0},{5,1},{6,2},{7,3},{8,12},{9,13},{10,14},{11,15},{0,8},{1,9},... | collective-permute-start | bytes 3145736 | tf_op jit(solution)/shard_map/ppermute | solution.py:434
  78.7 0.5 collective-permute-start.13
  79.2 1.5 collective-permute-start.10
  80.7 1.3 collective-permute-start.25
  82.0 19.3 %collective-permute-done.9.refs_1_.refs_0_ = bf16[4,128,1024]{2,1,0:T(8,128)(2,1)S(1)} collective-permute-done((bf16[4,128,1024]{2,1,0:T(8,128)(2,1)S(1)}, bf16[4,128,1024]{2,1,0:T(8,128)(2,1)S(1)}, u32[]{:S(2)}, u32[]{:S(2)}) %collective-permute-start.9) | collective-permute-done | bytes 1048608 | tf_op jit(solution)/shard_map/ppermute | solution.py:434
  101.3 5.4 %collective-permute-start.16 = (bf16[32,128,128]{2,1,0:T(8,128)(2,1)}, bf16[32,128,128]{2,1,0:T(8,128)(2,1)S(1)}, u32[]{:S(2)}, u32[]{:S(2)}) collective-permute-start(bf16[32,128,128]{2,1,0:T(8,128)(2,1)} %get-tuple-element.123), channel_id=1, source_target_pairs={{0,8},{1,9},{2,10},{3,11},{12,4},{13,5},{14,6},{15,7},{16,24},{17,... | collective-permute-start | bytes 3145736 | tf_op jit(solution)/shard_map/ppermute | solution.py:434
  106.7 1.1 slice_select_fusion
  107.9 1.0 copy-done.11
  108.8 0.3 copy-done.12
  109.2 1.5 collective-permute-start.14
  110.7 0.5 collective-permute-start.15
  111.2 0.7 stack.89.firsts
  111.9 23.4 %own_part.2 = (f32[16,128,1024]{2,1,0:T(8,128)}, bf16[32,128,1024]{2,1,0:T(8,128)(2,1)}) custom-call(s32[289]{0:T(512)} %tables.4.own_table, s32[273]{0:T(512)} %tables.5.far_table.table, s32[11]{0:T(128)} %stack.89.firsts, bf16[96,128,128]{2,1,0:T(8,128)(2,1)} %tiles_ref.5, bf16[1024,1024]{1,0:T(8,128)(2,1)} %compare_convert_fusion.perm_ref, ...), custom_call_target="tpu_custom_call" | custom-call | tf_op jit(solution)/shard_map/own_part/pallas_call | solution.py:285
  135.3 0.1 collective-permute-start.19
  135.4 0.5 collective-permute-start.20
  135.9 0.1 collective-permute-start.18
  136.0 0.4 collective-permute-start.21
  136.4 1.1 collective-permute-done.19.refs_3_
  137.5 0.1 collective-permute-start.22
  137.6 1.4 collective-permute-done.20.refs_4_
  139.0 1.3 collective-permute-start.24
  140.3 0.2 collective-permute-done.21.refs_7_
  140.5 1.3 collective-permute-start.23
  141.8 0.8 copy-done.15
  142.7 1.3 collective-permute-start.17
  144.0 0.1 stack.99.firsts
  144.1 20.1 %own_part.3 = (f32[16,128,1024]{2,1,0:T(8,128)S(1)}, bf16[32,128,1024]{2,1,0:T(8,128)(2,1)S(1)}) custom-call(s32[289]{0:T(512)S(1)} %copy-done.6, s32[273]{0:T(512)S(1)} %copy-done.5, s32[9]{0:T(128)S(1)} %stack.99.firsts, bf16[96,128,128]{2,1,0:T(8,128)(2,1)} %tiles_ref.5, bf16[1024,1024]{1,0:T(8,128)(2,1)} %compare_convert_fusion.perm_ref, ...), custom_call_target="tpu_custom_call" | custom-call | tf_op jit(solution)/shard_map/own_part/pallas_call | solution.py:285
  164.2 3.7 %collective-permute-done.25.refs_2_ = bf16[60,128,128]{2,1,0:T(8,128)(2,1)} collective-permute-done((bf16[60,128,128]{2,1,0:T(8,128)(2,1)}, bf16[60,128,128]{2,1,0:T(8,128)(2,1)}, u32[]{:S(2)}, u32[]{:S(2)}) %collective-permute-start.25) | collective-permute-done | bytes 1966112 | tf_op jit(solution)/shard_map/ppermute | solution.py:434
  167.9 9.4 %far_part.4 = (f32[128,1024]{1,0:T(8,128)S(1)}, bf16[16,128,1024]{2,1,0:T(8,128)(2,1)}) custom-call(s32[273]{0:T(512)S(1)} %copy-done.5, s32[1]{0:T(128)} %bitcast.chosen.at_end, bf16[4,128,1024]{2,1,0:T(8,128)(2,1)S(1)} %copy-done.2, bf16[4,128,1024]{2,1,0:T(8,128)(2,1)S(1)} %collective-permute-done.9.refs_1_.refs_0_, ...), custom_call_target="tpu_custom_call" | custom-call | tf_op jit(solution)/shard_map/far_part/pallas_call | solution.py:410
  177.2 3.2 %collective-permute-done.24.refs_2_ = bf16[18,128,128]{2,1,0:T(8,128)(2,1)S(1)} collective-permute-done((bf16[18,128,128]{2,1,0:T(8,128)(2,1)}, bf16[18,128,128]{2,1,0:T(8,128)(2,1)S(1)}, u32[]{:S(2)}, u32[]{:S(2)}) %collective-permute-start.24) | collective-permute-done | bytes 589856 | tf_op jit(solution)/shard_map/ppermute | solution.py:434
  180.4 3.9 %far_part.5 = (f32[128,1024]{1,0:T(8,128)S(1)}, bf16[16,128,1024]{2,1,0:T(8,128)(2,1)}) custom-call(s32[273]{0:T(512)S(1)} %copy-done.5, s32[1]{0:T(128)} %bitcast.chosen.at_end, bf16[4,128,1024]{2,1,0:T(8,128)(2,1)S(1)} %collective-permute-done.9.refs_1_.refs_0_, ...), custom_call_target="tpu_custom_call", output_to_operand_aliasing={{1}: (8, {})} | custom-call | tf_op jit(solution)/shard_map/far_part/pallas_call | solution.py:410
  184.3 4.6 %collective-permute-done.23.refs_1_ = bf16[12,128,128]{2,1,0:T(8,128)(2,1)} collective-permute-done((bf16[12,128,128]{2,1,0:T(8,128)(2,1)}, bf16[12,128,128]{2,1,0:T(8,128)(2,1)}, u32[]{:S(2)}, u32[]{:S(2)}) %collective-permute-start.23) | collective-permute-done | bytes 393248 | tf_op jit(solution)/shard_map/ppermute | solution.py:434
  189.0 3.6 %far_part.6 = (f32[128,1024]{1,0:T(8,128)S(1)}, bf16[16,128,1024]{2,1,0:T(8,128)(2,1)}) custom-call(s32[273]{0:T(512)S(1)} %copy-done.5, s32[1]{0:T(128)} %bitcast.chosen.at_end, bf16[32,128,128]{2,1,0:T(8,128)(2,1)S(1)} %collective-permute-done.16.refs_1_.refs_0_, ...), custom_call_target="tpu_custom_call", output_to_operand_aliasing={{1}: (7, {})} | custom-call | tf_op jit(solution)/shard_map/far_part/pallas_call | solution.py:410
  192.6 0.4 collective-permute-done.17.refs_1_
  193.0 3.2 %far_part.7 = (f32[128,1024]{1,0:T(8,128)}, bf16[16,128,1024]{2,1,0:T(8,128)(2,1)}) custom-call(s32[273]{0:T(512)S(1)} %copy-done.5, s32[1]{0:T(128)} %bitcast.chosen.at_end, bf16[32,128,128]{2,1,0:T(8,128)(2,1)S(1)} %collective-permute-done.16.refs_1_.refs_0_, ...), custom_call_target="tpu_custom_call", output_to_operand_aliasing={{1}: (7, {})} | custom-call | tf_op jit(solution)/shard_map/far_part/pallas_call | solution.py:410
  (42 shorter events, 0.1 us)
Async XLA Ops:
  0.0 22.2 %collective-permute-start = (bf16[4,128,1024]{2,1,0:T(8,128)(2,1)}, bf16[4,128,1024]{2,1,0:T(8,128)(2,1)S(1)}, u32[]{:S(2)}, u32[]{:S(2)}) collective-permute-start(bf16[4,128,1024]{2,1,0:T(8,128)(2,1)} %refs_0_.1), channel_id=1, source_target_pairs={{4,8},{5,9},{6,10},{7,11},{8,4},{9,5},{10,6},{11,7},{20,24},{21,25... | collective-permute-start | bytes 3145736 | tf_op jit(solution)/shard_map/ppermute | solution.py:434
  0.7 30.9 %collective-permute-start.3 = (bf16[4,128,1024]{2,1,0:T(8,128)(2,1)}, bf16[4,128,1024]{2,1,0:T(8,128)(2,1)S(1)}, u32[]{:S(2)}, u32[]{:S(2)}) collective-permute-start(bf16[4,128,1024]{2,1,0:T(8,128)(2,1)} %refs_0_.1), channel_id=1, source_target_pairs={{0,1},{1,0},{2,3},{3,2},{4,5},{5,4},{6,7},{7,6},{8,9},{9,8},{10,11... | collective-permute-start | bytes 3145736 | tf_op jit(solution)/shard_map/ppermute | solution.py:434
  1.2 30.4 %collective-permute-start.2 = (bf16[4,128,1024]{2,1,0:T(8,128)(2,1)}, bf16[4,128,1024]{2,1,0:T(8,128)(2,1)}, u32[]{:S(2)}, u32[]{:S(2)}) collective-permute-start(bf16[4,128,1024]{2,1,0:T(8,128)(2,1)} %refs_0_.1), channel_id=1, source_target_pairs={{0,4},{1,5},{2,6},{3,7},{4,0},{5,1},{6,2},{7,3},{8,12},{9,13},{10,... | collective-permute-start | bytes 3145736 | tf_op jit(solution)/shard_map/ppermute | solution.py:434
  6.7 25.5 %collective-permute-start.4 = (bf16[4,128,1024]{2,1,0:T(8,128)(2,1)}, bf16[4,128,1024]{2,1,0:T(8,128)(2,1)}, u32[]{:S(2)}, u32[]{:S(2)}) collective-permute-start(bf16[4,128,1024]{2,1,0:T(8,128)(2,1)} %refs_0_.1), channel_id=1, source_target_pairs={{0,2},{1,3},{2,0},{3,1},{4,6},{5,7},{6,4},{7,5},{8,10},{9,11},{10,... | collective-permute-start | bytes 3145736 | tf_op jit(solution)/shard_map/ppermute | solution.py:434
  8.9 22.3 %collective-permute-start.7 = (s32[2,96]{1,0:T(2,128)S(1)}, s32[2,96]{1,0:T(2,128)S(1)}, u32[]{:S(2)}, u32[]{:S(2)}) collective-permute-start(s32[2,96]{1,0:T(2,128)S(1)} %pad_add_fusion), channel_id=1, source_target_pairs={{0,8},{1,9},{2,10},{3,11},{4,12},{5,13},{6,14},{7,15},{8,0},{9,1},... | collective-permute-start | bytes 2312 | tf_op jit(solution)/shard_map/ppermute | solution.py:434
  14.3 1.9 copy-start
  16.2 0.7 copy-start.7
  22.2 10.0 %copy-start.3 = (bf16[4,128,1024]{2,1,0:T(8,128)(2,1)}, bf16[4,128,1024]{2,1,0:T(8,128)(2,1)S(1)}, u32[]{:S(2)}) copy-start(bf16[4,128,1024]{2,1,0:T(8,128)(2,1)S(1)} %get-tuple-element.100.tiles_ref) | copy-start | bytes 3145732
  22.3 30.8 %collective-permute-start.1 = (bf16[4,128,1024]{2,1,0:T(8,128)(2,1)S(1)}, bf16[4,128,1024]{2,1,0:T(8,128)(2,1)S(1)}, u32[]{:S(2)}, u32[]{:S(2)}) collective-permute-start(bf16[4,128,1024]{2,1,0:T(8,128)(2,1)S(1)} %payload.2), channel_id=1, source_target_pairs={{4,0},{5,1},{6,2},{7,3},{8,12},{9,13},{10,14},{11,15},{0,8},{1,9},... | collective-permute-start | bytes 3145736 | tf_op jit(solution)/shard_map/ppermute | solution.py:434
  31.6 1.0 copy-start.9
  32.6 26.7 %collective-permute-start.8 = (bf16[4,128,1024]{2,1,0:T(8,128)(2,1)}, bf16[4,128,1024]{2,1,0:T(8,128)(2,1)S(1)}, u32[]{:S(2)}, u32[]{:S(2)}) collective-permute-start(bf16[4,128,1024]{2,1,0:T(8,128)(2,1)} %collective-permute-done.2.refs_2_), channel_id=1, source_target_pairs={{4,8},{5,9},{6,10},{7,11},{8,4},{9,5},{10,6},{11,7},{20,24},{21,25... | collective-permute-start | bytes 3145736 | tf_op jit(solution)/shard_map/ppermute | solution.py:434
  33.4 19.9 %collective-permute-start.6 = (bf16[4,128,1024]{2,1,0:T(8,128)(2,1)}, bf16[4,128,1024]{2,1,0:T(8,128)(2,1)}, u32[]{:S(2)}, u32[]{:S(2)}) collective-permute-start(bf16[4,128,1024]{2,1,0:T(8,128)(2,1)} %collective-permute-done.2.refs_2_), channel_id=1, source_target_pairs={{0,1},{1,0},{2,3},{3,2},{4,5},{5,4},{6,7},{7,6},{8,9},{9,8},{10,11... | collective-permute-start | bytes 3145736 | tf_op jit(solution)/shard_map/ppermute | solution.py:434
  33.4 25.9 %collective-permute-start.5 = (bf16[4,128,1024]{2,1,0:T(8,128)(2,1)}, bf16[4,128,1024]{2,1,0:T(8,128)(2,1)}, u32[]{:S(2)}, u32[]{:S(2)}) collective-permute-start(bf16[4,128,1024]{2,1,0:T(8,128)(2,1)} %collective-permute-done.2.refs_2_), channel_id=1, source_target_pairs={{0,2},{1,3},{2,0},{3,1},{4,6},{5,7},{6,4},{7,5},{8,10},{9,11},{10,... | collective-permute-start | bytes 3145736 | tf_op jit(solution)/shard_map/ppermute | solution.py:434
  43.3 16.0 %copy-start.4 = (bf16[4,128,1024]{2,1,0:T(8,128)(2,1)S(1)}, bf16[4,128,1024]{2,1,0:T(8,128)(2,1)}, u32[]{:S(2)}) copy-start(bf16[4,128,1024]{2,1,0:T(8,128)(2,1)} %copy-done.3) | copy-start | bytes 3145732
  53.1 6.2 %copy-start.1 = (bf16[4,128,1024]{2,1,0:T(8,128)(2,1)}, bf16[4,128,1024]{2,1,0:T(8,128)(2,1)S(1)}, u32[]{:S(2)}) copy-start(bf16[4,128,1024]{2,1,0:T(8,128)(2,1)S(1)} %collective-permute-done.1.refs_0_) | copy-start | bytes 3145732
  53.2 54.6 %copy-start.8 = (bf16[4,128,1024]{2,1,0:T(8,128)(2,1)}, bf16[4,128,1024]{2,1,0:T(8,128)(2,1)S(1)}, u32[]{:S(2)}) copy-start(bf16[4,128,1024]{2,1,0:T(8,128)(2,1)S(1)} %broadcast_select_fusion.refs_4_) | copy-start | bytes 3145732
  59.3 21.4 %collective-permute-start.11 = (bf16[4,128,1024]{2,1,0:T(8,128)(2,1)S(1)}, bf16[4,128,1024]{2,1,0:T(8,128)(2,1)S(1)}, u32[]{:S(2)}, u32[]{:S(2)}) collective-permute-start(bf16[4,128,1024]{2,1,0:T(8,128)(2,1)S(1)} %broadcast_select_fusion.refs_4_), channel_id=1, source_target_pairs={{0,1},{1,0},{2,3},{3,2},{4,5},{5,4},{6,7},{7,6},{8,9},{9,8},{10,11... | collective-permute-start | bytes 3145736 | tf_op jit(solution)/shard_map/ppermute | solution.py:434
  59.5 41.9 %collective-permute-start.9 = (bf16[4,128,1024]{2,1,0:T(8,128)(2,1)S(1)}, bf16[4,128,1024]{2,1,0:T(8,128)(2,1)S(1)}, u32[]{:S(2)}, u32[]{:S(2)}) collective-permute-start(bf16[4,128,1024]{2,1,0:T(8,128)(2,1)S(1)} %payload.3), channel_id=1, source_target_pairs={{4,0},{5,1},{6,2},{7,3},{8,12},{9,13},{10,14},{11,15},{0,8},{1,9},... | collective-permute-start | bytes 3145736 | tf_op jit(solution)/shard_map/ppermute | solution.py:434
  78.7 29.2 %collective-permute-start.12 = (bf16[4,128,1024]{2,1,0:T(8,128)(2,1)}, bf16[4,128,1024]{2,1,0:T(8,128)(2,1)S(1)}, u32[]{:S(2)}, u32[]{:S(2)}) collective-permute-start(bf16[4,128,1024]{2,1,0:T(8,128)(2,1)} %collective-permute-done.4.refs_6_), channel_id=1, source_target_pairs={{0,1},{1,0},{2,3},{3,2},{4,5},{5,4},{6,7},{7,6},{8,9},{9,8},{10,11... | collective-permute-start | bytes 3145736 | tf_op jit(solution)/shard_map/ppermute | solution.py:434
  78.7 29.2 %collective-permute-start.13 = (bf16[4,128,1024]{2,1,0:T(8,128)(2,1)}, bf16[4,128,1024]{2,1,0:T(8,128)(2,1)S(1)}, u32[]{:S(2)}, u32[]{:S(2)}) collective-permute-start(bf16[4,128,1024]{2,1,0:T(8,128)(2,1)} %collective-permute-done.5.refs_8_), channel_id=1, source_target_pairs={{0,1},{1,0},{2,3},{3,2},{4,5},{5,4},{6,7},{7,6},{8,9},{9,8},{10,11... | collective-permute-start | bytes 3145736 | tf_op jit(solution)/shard_map/ppermute | solution.py:434
  79.2 28.7 %collective-permute-start.10 = (bf16[4,128,1024]{2,1,0:T(8,128)(2,1)S(1)}, bf16[4,128,1024]{2,1,0:T(8,128)(2,1)}, u32[]{:S(2)}, u32[]{:S(2)}) collective-permute-start(bf16[4,128,1024]{2,1,0:T(8,128)(2,1)S(1)} %broadcast_select_fusion.refs_4_), channel_id=1, source_target_pairs={{0,2},{1,3},{2,0},{3,1},{4,6},{5,7},{6,4},{7,5},{8,10},{9,11},{10,... | collective-permute-start | bytes 3145736 | tf_op jit(solution)/shard_map/ppermute | solution.py:434
  80.7 1.3 copy-start.10
  80.7 87.2 %collective-permute-start.25 = (bf16[60,128,128]{2,1,0:T(8,128)(2,1)}, bf16[60,128,128]{2,1,0:T(8,128)(2,1)}, u32[]{:S(2)}, u32[]{:S(2)}) collective-permute-start(bf16[60,128,128]{2,1,0:T(8,128)(2,1)} %get-tuple-element.137), channel_id=1, source_target_pairs={{4,12},{5,13},{6,14},{7,15},{8,0},{9,1},{10,2},{11,3},{20,28},{21,... | collective-permute-start | bytes 5898248 | tf_op jit(solution)/shard_map/ppermute | solution.py:434
  101.3 34.6 %collective-permute-start.16 = (bf16[32,128,128]{2,1,0:T(8,128)(2,1)}, bf16[32,128,128]{2,1,0:T(8,128)(2,1)S(1)}, u32[]{:S(2)}, u32[]{:S(2)}) collective-permute-start(bf16[32,128,128]{2,1,0:T(8,128)(2,1)} %get-tuple-element.123), channel_id=1, source_target_pairs={{0,8},{1,9},{2,10},{3,11},{12,4},{13,5},{14,6},{15,7},{16,24},{17,... | collective-permute-start | bytes 3145736 | tf_op jit(solution)/shard_map/ppermute | solution.py:434
  107.9 1.0 copy-start.11
  107.9 1.3 copy-start.12
  109.2 26.1 %collective-permute-start.14 = (bf16[2,128,1024]{2,1,0:T(8,128)(2,1)}, bf16[2,128,1024]{2,1,0:T(8,128)(2,1)}, u32[]{:S(2)}, u32[]{:S(2)}) collective-permute-start(bf16[2,128,1024]{2,1,0:T(8,128)(2,1)} %get-tuple-element.127.refs_1_), channel_id=1, source_target_pairs={{0,2},{1,3},{2,0},{3,1},{4,6},{5,7},{6,4},{7,5},{8,10},{9,11},{10,... | collective-permute-start | bytes 1572872 | tf_op jit(solution)/shard_map/ppermute | solution.py:434
  110.7 24.6 %collective-permute-start.15 = (bf16[2,128,1024]{2,1,0:T(8,128)(2,1)}, bf16[2,128,1024]{2,1,0:T(8,128)(2,1)}, u32[]{:S(2)}, u32[]{:S(2)}) collective-permute-start(bf16[2,128,1024]{2,1,0:T(8,128)(2,1)} %get-tuple-element.128.refs_2_), channel_id=1, source_target_pairs={{0,2},{1,3},{2,0},{3,1},{4,6},{5,7},{6,4},{7,5},{8,10},{9,11},{10,... | collective-permute-start | bytes 1572872 | tf_op jit(solution)/shard_map/ppermute | solution.py:434
  111.9 32.2 %copy-start.5 = (s32[273]{0:T(512)S(1)}, s32[273]{0:T(512)}, u32[]{:S(2)}) copy-start(s32[273]{0:T(512)} %tables.5.far_table.table) | copy-start | bytes 3280
  111.9 32.2 %copy-start.6 = (s32[289]{0:T(512)S(1)}, s32[289]{0:T(512)}, u32[]{:S(2)}) copy-start(s32[289]{0:T(512)} %tables.4.own_table) | copy-start | bytes 3472
  135.3 2.2 %collective-permute-start.19 = (bf16[2,128,1024]{2,1,0:T(8,128)(2,1)}, bf16[2,128,1024]{2,1,0:T(8,128)(2,1)S(1)}, u32[]{:S(2)}, u32[]{:S(2)}) collective-permute-start(bf16[2,128,1024]{2,1,0:T(8,128)(2,1)} %get-tuple-element.127.refs_1_), channel_id=1, source_target_pairs={{0,1},{1,0},{2,3},{3,2},{4,5},{5,4},{6,7},{7,6},{8,9},{9,8},{10,11... | collective-permute-start | bytes 1572872 | tf_op jit(solution)/shard_map/ppermute | solution.py:434
  135.4 3.6 %collective-permute-start.20 = (bf16[2,128,1024]{2,1,0:T(8,128)(2,1)}, bf16[2,128,1024]{2,1,0:T(8,128)(2,1)S(1)}, u32[]{:S(2)}, u32[]{:S(2)}) collective-permute-start(bf16[2,128,1024]{2,1,0:T(8,128)(2,1)} %get-tuple-element.128.refs_2_), channel_id=1, source_target_pairs={{0,1},{1,0},{2,3},{3,2},{4,5},{5,4},{6,7},{7,6},{8,9},{9,8},{10,11... | collective-permute-start | bytes 1572872 | tf_op jit(solution)/shard_map/ppermute | solution.py:434
  135.9 8.2 %collective-permute-start.18 = (bf16[4,128,1024]{2,1,0:T(8,128)(2,1)}, bf16[4,128,1024]{2,1,0:T(8,128)(2,1)}, u32[]{:S(2)}, u32[]{:S(2)}) collective-permute-start(bf16[4,128,1024]{2,1,0:T(8,128)(2,1)} %collective-permute-done.10.refs_10_), channel_id=1, source_target_pairs={{0,1},{1,0},{2,3},{3,2},{4,5},{5,4},{6,7},{7,6},{8,9},{9,8},{10,11... | collective-permute-start | bytes 3145736 | tf_op jit(solution)/shard_map/ppermute | solution.py:434
  136.0 4.5 %collective-permute-start.21 = (bf16[2,128,1024]{2,1,0:T(8,128)(2,1)}, bf16[2,128,1024]{2,1,0:T(8,128)(2,1)S(1)}, u32[]{:S(2)}, u32[]{:S(2)}) collective-permute-start(bf16[2,128,1024]{2,1,0:T(8,128)(2,1)} %collective-permute-done.14.refs_5_), channel_id=1, source_target_pairs={{0,1},{1,0},{2,3},{3,2},{4,5},{5,4},{6,7},{7,6},{8,9},{9,8},{10,11... | collective-permute-start | bytes 1572872 | tf_op jit(solution)/shard_map/ppermute | solution.py:434
  137.5 4.3 %collective-permute-start.22 = (bf16[2,128,1024]{2,1,0:T(8,128)(2,1)}, bf16[2,128,1024]{2,1,0:T(8,128)(2,1)S(1)}, u32[]{:S(2)}, u32[]{:S(2)}) collective-permute-start(bf16[2,128,1024]{2,1,0:T(8,128)(2,1)} %collective-permute-done.15.refs_6_), channel_id=1, source_target_pairs={{0,1},{1,0},{2,3},{3,2},{4,5},{5,4},{6,7},{7,6},{8,9},{9,8},{10,11... | collective-permute-start | bytes 1572872 | tf_op jit(solution)/shard_map/ppermute | solution.py:434
  139.0 2.8 %copy-start.13 = (bf16[2,128,1024]{2,1,0:T(8,128)(2,1)}, bf16[2,128,1024]{2,1,0:T(8,128)(2,1)S(1)}, u32[]{:S(2)}) copy-start(bf16[2,128,1024]{2,1,0:T(8,128)(2,1)S(1)} %collective-permute-done.20.refs_4_) | copy-start | bytes 1572868
  139.0 41.4 %collective-permute-start.24 = (bf16[18,128,128]{2,1,0:T(8,128)(2,1)}, bf16[18,128,128]{2,1,0:T(8,128)(2,1)S(1)}, u32[]{:S(2)}, u32[]{:S(2)}) collective-permute-start(bf16[18,128,128]{2,1,0:T(8,128)(2,1)} %get-tuple-element.136), channel_id=1, source_target_pairs={{4,12},{5,13},{6,14},{7,15},{8,0},{9,1},{10,2},{11,3},{20,28},{21,... | collective-permute-start | bytes 1769480 | tf_op jit(solution)/shard_map/ppermute | solution.py:434
  140.5 1.3 copy-start.14
  140.5 48.5 %collective-permute-start.23 = (bf16[12,128,128]{2,1,0:T(8,128)(2,1)}, bf16[12,128,128]{2,1,0:T(8,128)(2,1)}, u32[]{:S(2)}, u32[]{:S(2)}) collective-permute-start(bf16[12,128,128]{2,1,0:T(8,128)(2,1)} %get-tuple-element.135), channel_id=1, source_target_pairs={{4,12},{5,13},{6,14},{7,15},{8,0},{9,1},{10,2},{11,3},{20,28},{21,... | collective-permute-start | bytes 1179656 | tf_op jit(solution)/shard_map/ppermute | solution.py:434
  141.8 0.9 copy-start.15
  142.7 50.3 %collective-permute-start.17 = (bf16[6,128,128]{2,1,0:T(8,128)(2,1)}, bf16[6,128,128]{2,1,0:T(8,128)(2,1)S(1)}, u32[]{:S(2)}, u32[]{:S(2)}) collective-permute-start(bf16[6,128,128]{2,1,0:T(8,128)(2,1)} %get-tuple-element.125), channel_id=1, source_target_pairs={{4,12},{5,13},{6,14},{7,15},{8,0},{9,1},{10,2},{11,3},{20,28},{21,... | collective-permute-start | bytes 589832 | tf_op jit(solution)/shard_map/ppermute | solution.py:434
  144.1 23.8 %copy-start.2 = (bf16[4,128,1024]{2,1,0:T(8,128)(2,1)S(1)}, bf16[4,128,1024]{2,1,0:T(8,128)(2,1)}, u32[]{:S(2)}) copy-start(bf16[4,128,1024]{2,1,0:T(8,128)(2,1)} %copy-done.1) | copy-start | bytes 3145732

commit v21 on v20

--- a/solution.py
+++ b/solution.py
@@ -10,7 +10,7 @@
 W = 32
 PPD = 16
 REUSE = 3
-SHARES = (30, 9, 6)
+SHARES = (30, 11, 4)
 COLUMNS = 256
 MIB = 1024 * 1024
 GRANT = 36

time: 196 us -> 196 us (level)
  no operation moved by 1% of the time
where the time goes in v21:
time: 196 us
  Pallas kernels  82 us (42%)
  starting transfers between devices  54.3 us (28%)
  waiting for transfers between devices  47.7 us (24%)
  local copies, waits for them, and re-layouts  6.46 us (3%)
  other arithmetic  4.87 us (2%)
    ppermute x26, starting transfers between devices, send(): return lax.ppermute(value, 'tile', pairs)  54.3 us
    ppermute x26, waiting for transfers between devices, send(): return lax.ppermute(value, 'tile', pairs)  47.7 us
    pallas_call x2, Pallas kernels, own_part(): pl.pallas_call(functools.partial(own_kernel, counts, groups, group, not e...  43.9 us
    pallas_call x4, Pallas kernels, far_part(): pl.pallas_call(functools.partial(far_kernel, base, total_count, [segment...  20.2 us
    pallas_call x3, Pallas kernels, tables(): pl.pallas_call(tables_kernel, in_specs=[SMEM] * 2, out_specs=SMEM, out_sh...  12.4 us
    pallas_call x1, Pallas kernels, sort_tiles(): pl.pallas_call(functools.partial(sort_kernel, choices), in_specs=[SMEM] *...  5.37 us
    unnamed x32, local copies, waits for them, and re-layouts  5.18 us
  transfers between devices with their start and end apart: 26, of which 11 were waited for; matrix products, arithmetic and copies ran while one was open for 3% of the time, Pallas kernels for 40%

profile of v21, /device:TPU:0, one launch (start us, length us, event | category | flops | bytes accessed | tf_op | source)
XLA Modules:
  0.0 195.8 jit_solution(10112877421357916576)
XLA Ops:
  0.0 0.7 collective-permute-start
  0.7 0.5 collective-permute-start.3
  1.2 5.4 %collective-permute-start.2 = (bf16[4,128,1024]{2,1,0:T(8,128)(2,1)}, bf16[4,128,1024]{2,1,0:T(8,128)(2,1)}, u32[]{:S(2)}, u32[]{:S(2)}) collective-permute-start(bf16[4,128,1024]{2,1,0:T(8,128)(2,1)} %refs_0_.1), channel_id=1, source_target_pairs={{0,4},{1,5},{2,6},{3,7},{4,0},{5,1},{6,2},{7,3},{8,12},{9,13},{10,... | collective-permute-start | bytes 3145736 | tf_op jit(solution)/shard_map/ppermute | solution.py:434
  6.7 1.5 collective-permute-start.4
  8.2 0.7 pad_add_fusion
  8.9 0.0 collective-permute-start.7
  8.9 4.1 %tables.3.table = s32[273]{0:T(512)} custom-call(s32[96]{0:T(128)} %rows.1, s32[96]{0:T(128)} %cols.3), custom_call_target="tpu_custom_call" | custom-call | tf_op jit(solution)/shard_map/tables/pallas_call | solution.py:88
  13.0 1.2 fusion.6.rows
  14.3 1.9 copy-done
  16.2 0.7 copy-done.7
  16.9 5.4 %sort_tiles.1 = (bf16[4,128,1024]{2,1,0:T(8,128)(2,1)S(1)}, bf16[4,128,1024]{2,1,0:T(8,128)(2,1)S(1)}, bf16[32,128,128]{2,1,0:T(8,128)(2,1)}, bf16[60,128,128]{2...) custom-call(s32[273]{0:T(512)S(1)} %copy-done.7, ...), custom_call_target="tpu_custom_call" | custom-call | tf_op jit(solution)/shard_map/sort_tiles/pallas_call | solution.py:130
  22.2 0.0 collective-permute-done.received
  22.3 0.1 payload.2
  22.3 8.8 %collective-permute-start.1 = (bf16[4,128,1024]{2,1,0:T(8,128)(2,1)S(1)}, bf16[4,128,1024]{2,1,0:T(8,128)(2,1)S(1)}, u32[]{:S(2)}, u32[]{:S(2)}) collective-permute-start(bf16[4,128,1024]{2,1,0:T(8,128)(2,1)S(1)} %payload.2), channel_id=1, source_target_pairs={{4,0},{5,1},{6,2},{7,3},{8,12},{9,13},{10,14},{11,15},{0,8},{1,9},... | collective-permute-start | bytes 3145736 | tf_op jit(solution)/shard_map/ppermute | solution.py:434
  31.1 0.0 collective-permute-done.7
  31.1 0.5 slice_bitcast_fusion
  31.6 0.6 collective-permute-done.4.refs_6_
  32.2 0.4 copy-done.9
  32.6 0.7 collective-permute-start.8
  33.4 0.1 collective-permute-start.6
  33.4 1.6 collective-permute-start.5
  35.0 4.1 %tables.5.far_table.table = s32[273]{0:T(512)} custom-call(s32[96]{0:T(128)} %get-tuple-element.148.rows, s32[96]{0:T(128)} %get-tuple-element.147.cols), custom_call_target="tpu_custom_call" | custom-call | flops 4000000000 | tf_op jit(solution)/shard_map/tables/pallas_call | solution.py:88
  39.2 4.2 %tables.4.own_table = s32[289]{0:T(512)} custom-call(s32[96]{0:T(128)} %fusion.6.rows, s32[96]{0:T(128)} %cols.3), custom_call_target="tpu_custom_call" | custom-call | tf_op jit(solution)/shard_map/tables/pallas_call | solution.py:88
  43.4 1.7 compare_convert_fusion.perm_ref
  45.1 8.0 %collective-permute-done.1.refs_0_ = bf16[4,128,1024]{2,1,0:T(8,128)(2,1)S(1)} collective-permute-done((bf16[4,128,1024]{2,1,0:T(8,128)(2,1)S(1)}, bf16[4,128,1024]{2,1,0:T(8,128)(2,1)S(1)}, u32[]{:S(2)}, u32[]{:S(2)}) %collective-permute-start.1) | collective-permute-done | bytes 1048608 | tf_op jit(solution)/shard_map/ppermute | solution.py:434
  53.1 0.1 broadcast_select_fusion.refs_4_
  53.2 0.0 collective-permute-done.6.refs_3_
  53.2 6.1 %collective-permute-done.5.refs_8_ = bf16[4,128,1024]{2,1,0:T(8,128)(2,1)} collective-permute-done((bf16[4,128,1024]{2,1,0:T(8,128)(2,1)}, bf16[4,128,1024]{2,1,0:T(8,128)(2,1)}, u32[]{:S(2)}, u32[]{:S(2)}) %collective-permute-start.5) | collective-permute-done | bytes 1048608 | tf_op jit(solution)/shard_map/ppermute | solution.py:434
  59.4 0.1 payload.3
  59.5 19.2 %collective-permute-start.9 = (bf16[4,128,1024]{2,1,0:T(8,128)(2,1)S(1)}, bf16[4,128,1024]{2,1,0:T(8,128)(2,1)S(1)}, u32[]{:S(2)}, u32[]{:S(2)}) collective-permute-start(bf16[4,128,1024]{2,1,0:T(8,128)(2,1)S(1)} %payload.3), channel_id=1, source_target_pairs={{4,0},{5,1},{6,2},{7,3},{8,12},{9,13},{10,14},{11,15},{0,8},{1,9},... | collective-permute-start | bytes 3145736 | tf_op jit(solution)/shard_map/ppermute | solution.py:434
  78.7 0.5 collective-permute-start.13
  79.2 1.5 collective-permute-start.10
  80.7 1.3 collective-permute-start.25
  82.0 19.3 %collective-permute-done.9.refs_1_.refs_0_ = bf16[4,128,1024]{2,1,0:T(8,128)(2,1)S(1)} collective-permute-done((bf16[4,128,1024]{2,1,0:T(8,128)(2,1)S(1)}, bf16[4,128,1024]{2,1,0:T(8,128)(2,1)S(1)}, u32[]{:S(2)}, u32[]{:S(2)}) %collective-permute-start.9) | collective-permute-done | bytes 1048608 | tf_op jit(solution)/shard_map/ppermute | solution.py:434
  101.3 5.4 %collective-permute-start.16 = (bf16[32,128,128]{2,1,0:T(8,128)(2,1)}, bf16[32,128,128]{2,1,0:T(8,128)(2,1)S(1)}, u32[]{:S(2)}, u32[]{:S(2)}) collective-permute-start(bf16[32,128,128]{2,1,0:T(8,128)(2,1)} %get-tuple-element.123), channel_id=1, source_target_pairs={{0,8},{1,9},{2,10},{3,11},{12,4},{13,5},{14,6},{15,7},{16,24},{17,... | collective-permute-start | bytes 3145736 | tf_op jit(solution)/shard_map/ppermute | solution.py:434
  106.7 1.1 slice_select_fusion
  107.9 1.0 copy-done.11
  108.8 0.3 copy-done.12
  109.2 1.5 collective-permute-start.14
  110.7 0.5 collective-permute-start.15
  111.2 0.7 stack.89.firsts
  111.9 23.6 %own_part.2 = (f32[16,128,1024]{2,1,0:T(8,128)}, bf16[32,128,1024]{2,1,0:T(8,128)(2,1)}) custom-call(s32[289]{0:T(512)} %tables.4.own_table, s32[273]{0:T(512)} %tables.5.far_table.table, s32[11]{0:T(128)} %stack.89.firsts, bf16[96,128,128]{2,1,0:T(8,128)(2,1)} %tiles_ref.5, bf16[1024,1024]{1,0:T(8,128)(2,1)} %compare_convert_fusion.perm_ref, ...), custom_call_target="tpu_custom_call" | custom-call | tf_op jit(solution)/shard_map/own_part/pallas_call | solution.py:285
  135.4 0.1 collective-permute-start.19
  135.5 0.5 collective-permute-start.20
  136.0 0.1 collective-permute-start.18
  136.1 0.4 collective-permute-start.21
  136.5 1.1 collective-permute-done.19.refs_3_
  137.6 1.3 collective-permute-start.24
  138.9 0.2 collective-permute-done.20.refs_4_
  139.1 0.1 collective-permute-start.22
  139.3 1.4 collective-permute-done.21.refs_7_
  140.6 1.3 collective-permute-start.23
  142.0 0.8 copy-done.15
  142.8 1.3 collective-permute-start.17
  144.1 0.1 stack.99.firsts
  144.2 20.3 %own_part.3 = (f32[16,128,1024]{2,1,0:T(8,128)S(1)}, bf16[32,128,1024]{2,1,0:T(8,128)(2,1)S(1)}) custom-call(s32[289]{0:T(512)S(1)} %copy-done.6, s32[273]{0:T(512)S(1)} %copy-done.5, s32[9]{0:T(128)S(1)} %stack.99.firsts, bf16[96,128,128]{2,1,0:T(8,128)(2,1)} %tiles_ref.5, bf16[1024,1024]{1,0:T(8,128)(2,1)} %compare_convert_fusion.perm_ref, ...), custom_call_target="tpu_custom_call" | custom-call | tf_op jit(solution)/shard_map/own_part/pallas_call | solution.py:285
  164.6 3.3 %collective-permute-done.25.refs_2_ = bf16[60,128,128]{2,1,0:T(8,128)(2,1)} collective-permute-done((bf16[60,128,128]{2,1,0:T(8,128)(2,1)}, bf16[60,128,128]{2,1,0:T(8,128)(2,1)}, u32[]{:S(2)}, u32[]{:S(2)}) %collective-permute-start.25) | collective-permute-done | bytes 1966112 | tf_op jit(solution)/shard_map/ppermute | solution.py:434
  167.9 9.2 %far_part.4 = (f32[128,1024]{1,0:T(8,128)S(1)}, bf16[16,128,1024]{2,1,0:T(8,128)(2,1)}) custom-call(s32[273]{0:T(512)S(1)} %copy-done.5, s32[1]{0:T(128)} %bitcast.chosen.at_end, bf16[4,128,1024]{2,1,0:T(8,128)(2,1)S(1)} %copy-done.2, bf16[4,128,1024]{2,1,0:T(8,128)(2,1)S(1)} %collective-permute-done.9.refs_1_.refs_0_, ...), custom_call_target="tpu_custom_call" | custom-call | tf_op jit(solution)/shard_map/far_part/pallas_call | solution.py:410
  177.1 6.1 %collective-permute-done.24.refs_2_ = bf16[22,128,128]{2,1,0:T(8,128)(2,1)S(1)} collective-permute-done((bf16[22,128,128]{2,1,0:T(8,128)(2,1)}, bf16[22,128,128]{2,1,0:T(8,128)(2,1)S(1)}, u32[]{:S(2)}, u32[]{:S(2)}) %collective-permute-start.24) | collective-permute-done | bytes 720928 | tf_op jit(solution)/shard_map/ppermute | solution.py:434
  183.2 5.0 %far_part.5 = (f32[128,1024]{1,0:T(8,128)S(1)}, bf16[16,128,1024]{2,1,0:T(8,128)(2,1)}) custom-call(s32[273]{0:T(512)S(1)} %copy-done.5, s32[1]{0:T(128)} %bitcast.chosen.at_end, bf16[4,128,1024]{2,1,0:T(8,128)(2,1)S(1)} %collective-permute-done.9.refs_1_.refs_0_, ...), custom_call_target="tpu_custom_call", output_to_operand_aliasing={{1}: (8, {})} | custom-call | tf_op jit(solution)/shard_map/far_part/pallas_call | solution.py:410
  188.2 0.7 collective-permute-done.23.refs_1_
  189.0 3.1 %far_part.6 = (f32[128,1024]{1,0:T(8,128)S(1)}, bf16[16,128,1024]{2,1,0:T(8,128)(2,1)}) custom-call(s32[273]{0:T(512)S(1)} %copy-done.5, s32[1]{0:T(128)} %bitcast.chosen.at_end, bf16[32,128,128]{2,1,0:T(8,128)(2,1)S(1)} %collective-permute-done.16.refs_1_.refs_0_, ...), custom_call_target="tpu_custom_call", output_to_operand_aliasing={{1}: (7, {})} | custom-call | tf_op jit(solution)/shard_map/far_part/pallas_call | solution.py:410
  192.1 0.9 collective-permute-done.17.refs_1_
  193.0 2.8 %far_part.7 = (f32[128,1024]{1,0:T(8,128)}, bf16[16,128,1024]{2,1,0:T(8,128)(2,1)}) custom-call(s32[273]{0:T(512)S(1)} %copy-done.5, s32[1]{0:T(128)} %bitcast.chosen.at_end, bf16[32,128,128]{2,1,0:T(8,128)(2,1)S(1)} %collective-permute-done.16.refs_1_.refs_0_, ...), custom_call_target="tpu_custom_call", output_to_operand_aliasing={{1}: (7, {})} | custom-call | tf_op jit(solution)/shard_map/far_part/pallas_call | solution.py:410
  (42 shorter events, 0.1 us)
Async XLA Ops:
  0.0 22.2 %collective-permute-start = (bf16[4,128,1024]{2,1,0:T(8,128)(2,1)}, bf16[4,128,1024]{2,1,0:T(8,128)(2,1)S(1)}, u32[]{:S(2)}, u32[]{:S(2)}) collective-permute-start(bf16[4,128,1024]{2,1,0:T(8,128)(2,1)} %refs_0_.1), channel_id=1, source_target_pairs={{4,8},{5,9},{6,10},{7,11},{8,4},{9,5},{10,6},{11,7},{20,24},{21,25... | collective-permute-start | bytes 3145736 | tf_op jit(solution)/shard_map/ppermute | solution.py:434
  0.7 30.9 %collective-permute-start.3 = (bf16[4,128,1024]{2,1,0:T(8,128)(2,1)}, bf16[4,128,1024]{2,1,0:T(8,128)(2,1)S(1)}, u32[]{:S(2)}, u32[]{:S(2)}) collective-permute-start(bf16[4,128,1024]{2,1,0:T(8,128)(2,1)} %refs_0_.1), channel_id=1, source_target_pairs={{0,1},{1,0},{2,3},{3,2},{4,5},{5,4},{6,7},{7,6},{8,9},{9,8},{10,11... | collective-permute-start | bytes 3145736 | tf_op jit(solution)/shard_map/ppermute | solution.py:434
  1.2 30.4 %collective-permute-start.2 = (bf16[4,128,1024]{2,1,0:T(8,128)(2,1)}, bf16[4,128,1024]{2,1,0:T(8,128)(2,1)}, u32[]{:S(2)}, u32[]{:S(2)}) collective-permute-start(bf16[4,128,1024]{2,1,0:T(8,128)(2,1)} %refs_0_.1), channel_id=1, source_target_pairs={{0,4},{1,5},{2,6},{3,7},{4,0},{5,1},{6,2},{7,3},{8,12},{9,13},{10,... | collective-permute-start | bytes 3145736 | tf_op jit(solution)/shard_map/ppermute | solution.py:434
  6.7 25.5 %collective-permute-start.4 = (bf16[4,128,1024]{2,1,0:T(8,128)(2,1)}, bf16[4,128,1024]{2,1,0:T(8,128)(2,1)}, u32[]{:S(2)}, u32[]{:S(2)}) collective-permute-start(bf16[4,128,1024]{2,1,0:T(8,128)(2,1)} %refs_0_.1), channel_id=1, source_target_pairs={{0,2},{1,3},{2,0},{3,1},{4,6},{5,7},{6,4},{7,5},{8,10},{9,11},{10,... | collective-permute-start | bytes 3145736 | tf_op jit(solution)/shard_map/ppermute | solution.py:434
  8.9 22.3 %collective-permute-start.7 = (s32[2,96]{1,0:T(2,128)S(1)}, s32[2,96]{1,0:T(2,128)S(1)}, u32[]{:S(2)}, u32[]{:S(2)}) collective-permute-start(s32[2,96]{1,0:T(2,128)S(1)} %pad_add_fusion), channel_id=1, source_target_pairs={{0,8},{1,9},{2,10},{3,11},{4,12},{5,13},{6,14},{7,15},{8,0},{9,1},... | collective-permute-start | bytes 2312 | tf_op jit(solution)/shard_map/ppermute | solution.py:434
  14.3 1.9 copy-start
  16.2 0.7 copy-start.7
  22.2 10.0 %copy-start.3 = (bf16[4,128,1024]{2,1,0:T(8,128)(2,1)}, bf16[4,128,1024]{2,1,0:T(8,128)(2,1)S(1)}, u32[]{:S(2)}) copy-start(bf16[4,128,1024]{2,1,0:T(8,128)(2,1)S(1)} %get-tuple-element.100.tiles_ref) | copy-start | bytes 3145732
  22.3 30.8 %collective-permute-start.1 = (bf16[4,128,1024]{2,1,0:T(8,128)(2,1)S(1)}, bf16[4,128,1024]{2,1,0:T(8,128)(2,1)S(1)}, u32[]{:S(2)}, u32[]{:S(2)}) collective-permute-start(bf16[4,128,1024]{2,1,0:T(8,128)(2,1)S(1)} %payload.2), channel_id=1, source_target_pairs={{4,0},{5,1},{6,2},{7,3},{8,12},{9,13},{10,14},{11,15},{0,8},{1,9},... | collective-permute-start | bytes 3145736 | tf_op jit(solution)/shard_map/ppermute | solution.py:434
  31.6 1.0 copy-start.9
  32.6 26.7 %collective-permute-start.8 = (bf16[4,128,1024]{2,1,0:T(8,128)(2,1)}, bf16[4,128,1024]{2,1,0:T(8,128)(2,1)S(1)}, u32[]{:S(2)}, u32[]{:S(2)}) collective-permute-start(bf16[4,128,1024]{2,1,0:T(8,128)(2,1)} %collective-permute-done.2.refs_2_), channel_id=1, source_target_pairs={{4,8},{5,9},{6,10},{7,11},{8,4},{9,5},{10,6},{11,7},{20,24},{21,25... | collective-permute-start | bytes 3145736 | tf_op jit(solution)/shard_map/ppermute | solution.py:434
  33.4 19.9 %collective-permute-start.6 = (bf16[4,128,1024]{2,1,0:T(8,128)(2,1)}, bf16[4,128,1024]{2,1,0:T(8,128)(2,1)}, u32[]{:S(2)}, u32[]{:S(2)}) collective-permute-start(bf16[4,128,1024]{2,1,0:T(8,128)(2,1)} %collective-permute-done.2.refs_2_), channel_id=1, source_target_pairs={{0,1},{1,0},{2,3},{3,2},{4,5},{5,4},{6,7},{7,6},{8,9},{9,8},{10,11... | collective-permute-start | bytes 3145736 | tf_op jit(solution)/shard_map/ppermute | solution.py:434
  33.4 25.9 %collective-permute-start.5 = (bf16[4,128,1024]{2,1,0:T(8,128)(2,1)}, bf16[4,128,1024]{2,1,0:T(8,128)(2,1)}, u32[]{:S(2)}, u32[]{:S(2)}) collective-permute-start(bf16[4,128,1024]{2,1,0:T(8,128)(2,1)} %collective-permute-done.2.refs_2_), channel_id=1, source_target_pairs={{0,2},{1,3},{2,0},{3,1},{4,6},{5,7},{6,4},{7,5},{8,10},{9,11},{10,... | collective-permute-start | bytes 3145736 | tf_op jit(solution)/shard_map/ppermute | solution.py:434
  43.3 16.0 %copy-start.4 = (bf16[4,128,1024]{2,1,0:T(8,128)(2,1)S(1)}, bf16[4,128,1024]{2,1,0:T(8,128)(2,1)}, u32[]{:S(2)}) copy-start(bf16[4,128,1024]{2,1,0:T(8,128)(2,1)} %copy-done.3) | copy-start | bytes 3145732
  53.1 6.2 %copy-start.1 = (bf16[4,128,1024]{2,1,0:T(8,128)(2,1)}, bf16[4,128,1024]{2,1,0:T(8,128)(2,1)S(1)}, u32[]{:S(2)}) copy-start(bf16[4,128,1024]{2,1,0:T(8,128)(2,1)S(1)} %collective-permute-done.1.refs_0_) | copy-start | bytes 3145732
  53.2 54.6 %copy-start.8 = (bf16[4,128,1024]{2,1,0:T(8,128)(2,1)}, bf16[4,128,1024]{2,1,0:T(8,128)(2,1)S(1)}, u32[]{:S(2)}) copy-start(bf16[4,128,1024]{2,1,0:T(8,128)(2,1)S(1)} %broadcast_select_fusion.refs_4_) | copy-start | bytes 3145732
  59.3 21.4 %collective-permute-start.11 = (bf16[4,128,1024]{2,1,0:T(8,128)(2,1)S(1)}, bf16[4,128,1024]{2,1,0:T(8,128)(2,1)S(1)}, u32[]{:S(2)}, u32[]{:S(2)}) collective-permute-start(bf16[4,128,1024]{2,1,0:T(8,128)(2,1)S(1)} %broadcast_select_fusion.refs_4_), channel_id=1, source_target_pairs={{0,1},{1,0},{2,3},{3,2},{4,5},{5,4},{6,7},{7,6},{8,9},{9,8},{10,11... | collective-permute-start | bytes 3145736 | tf_op jit(solution)/shard_map/ppermute | solution.py:434
  59.5 41.9 %collective-permute-start.9 = (bf16[4,128,1024]{2,1,0:T(8,128)(2,1)S(1)}, bf16[4,128,1024]{2,1,0:T(8,128)(2,1)S(1)}, u32[]{:S(2)}, u32[]{:S(2)}) collective-permute-start(bf16[4,128,1024]{2,1,0:T(8,128)(2,1)S(1)} %payload.3), channel_id=1, source_target_pairs={{4,0},{5,1},{6,2},{7,3},{8,12},{9,13},{10,14},{11,15},{0,8},{1,9},... | collective-permute-start | bytes 3145736 | tf_op jit(solution)/shard_map/ppermute | solution.py:434
  78.7 29.2 %collective-permute-start.12 = (bf16[4,128,1024]{2,1,0:T(8,128)(2,1)}, bf16[4,128,1024]{2,1,0:T(8,128)(2,1)S(1)}, u32[]{:S(2)}, u32[]{:S(2)}) collective-permute-start(bf16[4,128,1024]{2,1,0:T(8,128)(2,1)} %collective-permute-done.4.refs_6_), channel_id=1, source_target_pairs={{0,1},{1,0},{2,3},{3,2},{4,5},{5,4},{6,7},{7,6},{8,9},{9,8},{10,11... | collective-permute-start | bytes 3145736 | tf_op jit(solution)/shard_map/ppermute | solution.py:434
  78.7 29.2 %collective-permute-start.13 = (bf16[4,128,1024]{2,1,0:T(8,128)(2,1)}, bf16[4,128,1024]{2,1,0:T(8,128)(2,1)S(1)}, u32[]{:S(2)}, u32[]{:S(2)}) collective-permute-start(bf16[4,128,1024]{2,1,0:T(8,128)(2,1)} %collective-permute-done.5.refs_8_), channel_id=1, source_target_pairs={{0,1},{1,0},{2,3},{3,2},{4,5},{5,4},{6,7},{7,6},{8,9},{9,8},{10,11... | collective-permute-start | bytes 3145736 | tf_op jit(solution)/shard_map/ppermute | solution.py:434
  79.2 28.7 %collective-permute-start.10 = (bf16[4,128,1024]{2,1,0:T(8,128)(2,1)S(1)}, bf16[4,128,1024]{2,1,0:T(8,128)(2,1)}, u32[]{:S(2)}, u32[]{:S(2)}) collective-permute-start(bf16[4,128,1024]{2,1,0:T(8,128)(2,1)S(1)} %broadcast_select_fusion.refs_4_), channel_id=1, source_target_pairs={{0,2},{1,3},{2,0},{3,1},{4,6},{5,7},{6,4},{7,5},{8,10},{9,11},{10,... | collective-permute-start | bytes 3145736 | tf_op jit(solution)/shard_map/ppermute | solution.py:434
  80.7 1.3 copy-start.10
  80.7 87.2 %collective-permute-start.25 = (bf16[60,128,128]{2,1,0:T(8,128)(2,1)}, bf16[60,128,128]{2,1,0:T(8,128)(2,1)}, u32[]{:S(2)}, u32[]{:S(2)}) collective-permute-start(bf16[60,128,128]{2,1,0:T(8,128)(2,1)} %get-tuple-element.137), channel_id=1, source_target_pairs={{4,12},{5,13},{6,14},{7,15},{8,0},{9,1},{10,2},{11,3},{20,28},{21,... | collective-permute-start | bytes 5898248 | tf_op jit(solution)/shard_map/ppermute | solution.py:434
  101.3 34.8 %collective-permute-start.16 = (bf16[32,128,128]{2,1,0:T(8,128)(2,1)}, bf16[32,128,128]{2,1,0:T(8,128)(2,1)S(1)}, u32[]{:S(2)}, u32[]{:S(2)}) collective-permute-start(bf16[32,128,128]{2,1,0:T(8,128)(2,1)} %get-tuple-element.123), channel_id=1, source_target_pairs={{0,8},{1,9},{2,10},{3,11},{12,4},{13,5},{14,6},{15,7},{16,24},{17,... | collective-permute-start | bytes 3145736 | tf_op jit(solution)/shard_map/ppermute | solution.py:434
  107.8 1.0 copy-start.11
  107.9 1.3 copy-start.12
  109.2 26.3 %collective-permute-start.14 = (bf16[2,128,1024]{2,1,0:T(8,128)(2,1)}, bf16[2,128,1024]{2,1,0:T(8,128)(2,1)}, u32[]{:S(2)}, u32[]{:S(2)}) collective-permute-start(bf16[2,128,1024]{2,1,0:T(8,128)(2,1)} %get-tuple-element.127.refs_1_), channel_id=1, source_target_pairs={{0,2},{1,3},{2,0},{3,1},{4,6},{5,7},{6,4},{7,5},{8,10},{9,11},{10,... | collective-permute-start | bytes 1572872 | tf_op jit(solution)/shard_map/ppermute | solution.py:434
  110.7 24.8 %collective-permute-start.15 = (bf16[2,128,1024]{2,1,0:T(8,128)(2,1)}, bf16[2,128,1024]{2,1,0:T(8,128)(2,1)}, u32[]{:S(2)}, u32[]{:S(2)}) collective-permute-start(bf16[2,128,1024]{2,1,0:T(8,128)(2,1)} %get-tuple-element.128.refs_2_), channel_id=1, source_target_pairs={{0,2},{1,3},{2,0},{3,1},{4,6},{5,7},{6,4},{7,5},{8,10},{9,11},{10,... | collective-permute-start | bytes 1572872 | tf_op jit(solution)/shard_map/ppermute | solution.py:434
  111.9 32.4 %copy-start.5 = (s32[273]{0:T(512)S(1)}, s32[273]{0:T(512)}, u32[]{:S(2)}) copy-start(s32[273]{0:T(512)} %tables.5.far_table.table) | copy-start | bytes 3280
  111.9 32.4 %copy-start.6 = (s32[289]{0:T(512)S(1)}, s32[289]{0:T(512)}, u32[]{:S(2)}) copy-start(s32[289]{0:T(512)} %tables.4.own_table) | copy-start | bytes 3472
  135.4 2.2 %collective-permute-start.19 = (bf16[2,128,1024]{2,1,0:T(8,128)(2,1)}, bf16[2,128,1024]{2,1,0:T(8,128)(2,1)S(1)}, u32[]{:S(2)}, u32[]{:S(2)}) collective-permute-start(bf16[2,128,1024]{2,1,0:T(8,128)(2,1)} %get-tuple-element.127.refs_1_), channel_id=1, source_target_pairs={{0,1},{1,0},{2,3},{3,2},{4,5},{5,4},{6,7},{7,6},{8,9},{9,8},{10,11... | collective-permute-start | bytes 1572872 | tf_op jit(solution)/shard_map/ppermute | solution.py:434
  135.5 3.6 %collective-permute-start.20 = (bf16[2,128,1024]{2,1,0:T(8,128)(2,1)}, bf16[2,128,1024]{2,1,0:T(8,128)(2,1)S(1)}, u32[]{:S(2)}, u32[]{:S(2)}) collective-permute-start(bf16[2,128,1024]{2,1,0:T(8,128)(2,1)} %get-tuple-element.128.refs_2_), channel_id=1, source_target_pairs={{0,1},{1,0},{2,3},{3,2},{4,5},{5,4},{6,7},{7,6},{8,9},{9,8},{10,11... | collective-permute-start | bytes 1572872 | tf_op jit(solution)/shard_map/ppermute | solution.py:434
  136.0 8.2 %collective-permute-start.18 = (bf16[4,128,1024]{2,1,0:T(8,128)(2,1)}, bf16[4,128,1024]{2,1,0:T(8,128)(2,1)}, u32[]{:S(2)}, u32[]{:S(2)}) collective-permute-start(bf16[4,128,1024]{2,1,0:T(8,128)(2,1)} %collective-permute-done.10.refs_10_), channel_id=1, source_target_pairs={{0,1},{1,0},{2,3},{3,2},{4,5},{5,4},{6,7},{7,6},{8,9},{9,8},{10,11... | collective-permute-start | bytes 3145736 | tf_op jit(solution)/shard_map/ppermute | solution.py:434
  136.1 4.5 %collective-permute-start.21 = (bf16[2,128,1024]{2,1,0:T(8,128)(2,1)}, bf16[2,128,1024]{2,1,0:T(8,128)(2,1)S(1)}, u32[]{:S(2)}, u32[]{:S(2)}) collective-permute-start(bf16[2,128,1024]{2,1,0:T(8,128)(2,1)} %collective-permute-done.14.refs_5_), channel_id=1, source_target_pairs={{0,1},{1,0},{2,3},{3,2},{4,5},{5,4},{6,7},{7,6},{8,9},{9,8},{10,11... | collective-permute-start | bytes 1572872 | tf_op jit(solution)/shard_map/ppermute | solution.py:434
  137.6 45.6 %collective-permute-start.24 = (bf16[22,128,128]{2,1,0:T(8,128)(2,1)}, bf16[22,128,128]{2,1,0:T(8,128)(2,1)S(1)}, u32[]{:S(2)}, u32[]{:S(2)}) collective-permute-start(bf16[22,128,128]{2,1,0:T(8,128)(2,1)} %get-tuple-element.136), channel_id=1, source_target_pairs={{4,12},{5,13},{6,14},{7,15},{8,0},{9,1},{10,2},{11,3},{20,28},{21,... | collective-permute-start | bytes 2162696 | tf_op jit(solution)/shard_map/ppermute | solution.py:434
  139.1 2.8 %copy-start.13 = (bf16[2,128,1024]{2,1,0:T(8,128)(2,1)}, bf16[2,128,1024]{2,1,0:T(8,128)(2,1)S(1)}, u32[]{:S(2)}) copy-start(bf16[2,128,1024]{2,1,0:T(8,128)(2,1)S(1)} %collective-permute-done.20.refs_4_) | copy-start | bytes 1572868
  139.1 2.8 %collective-permute-start.22 = (bf16[2,128,1024]{2,1,0:T(8,128)(2,1)}, bf16[2,128,1024]{2,1,0:T(8,128)(2,1)S(1)}, u32[]{:S(2)}, u32[]{:S(2)}) collective-permute-start(bf16[2,128,1024]{2,1,0:T(8,128)(2,1)} %collective-permute-done.15.refs_6_), channel_id=1, source_target_pairs={{0,1},{1,0},{2,3},{3,2},{4,5},{5,4},{6,7},{7,6},{8,9},{9,8},{10,11... | collective-permute-start | bytes 1572872 | tf_op jit(solution)/shard_map/ppermute | solution.py:434
  140.6 1.3 copy-start.14
  140.6 48.3 %collective-permute-start.23 = (bf16[8,128,128]{2,1,0:T(8,128)(2,1)}, bf16[8,128,128]{2,1,0:T(8,128)(2,1)}, u32[]{:S(2)}, u32[]{:S(2)}) collective-permute-start(bf16[8,128,128]{2,1,0:T(8,128)(2,1)} %get-tuple-element.135), channel_id=1, source_target_pairs={{4,12},{5,13},{6,14},{7,15},{8,0},{9,1},{10,2},{11,3},{20,28},{21,... | collective-permute-start | bytes 786440 | tf_op jit(solution)/shard_map/ppermute | solution.py:434
  142.0 0.9 copy-start.15
  142.8 50.2 %collective-permute-start.17 = (bf16[6,128,128]{2,1,0:T(8,128)(2,1)}, bf16[6,128,128]{2,1,0:T(8,128)(2,1)S(1)}, u32[]{:S(2)}, u32[]{:S(2)}) collective-permute-start(bf16[6,128,128]{2,1,0:T(8,128)(2,1)} %get-tuple-element.125), channel_id=1, source_target_pairs={{4,12},{5,13},{6,14},{7,15},{8,0},{9,1},{10,2},{11,3},{20,28},{21,... | collective-permute-start | bytes 589832 | tf_op jit(solution)/shard_map/ppermute | solution.py:434
  144.2 23.7 %copy-start.2 = (bf16[4,128,1024]{2,1,0:T(8,128)(2,1)S(1)}, bf16[4,128,1024]{2,1,0:T(8,128)(2,1)}, u32[]{:S(2)}) copy-start(bf16[4,128,1024]{2,1,0:T(8,128)(2,1)} %copy-done.1) | copy-start | bytes 3145732

commit v22 on v21

--- a/solution.py
+++ b/solution.py
@@ -446,6 +446,7 @@
     from_ends = [(i, i ^ 8) for i in range(16) if i not in centre]
     from_centre = [(i, i ^ 8) for i in centre]
     around = [(i, i ^ 4) for i in centre] + from_ends
+    around_crossed = [(i, i ^ 4) for i in centre] + [(i, i ^ 9) for i, _ in from_ends]
     other_z, other_y, other_core, opposite = (flipped_bit(bit) for bit in (4, 2, 1, 8))
     me = lax.axis_index("tile")
     z = me // 4
@@ -480,7 +481,7 @@
     first = payload_of(at_end, parts[0], first)
     outer = send(first, around)
     near, c_own, y_own, keys, columns, *parts = together(near, c_own, y_own, keys, columns, *parts)
-    second = send(near, across)
+    second = send(jnp.where(in_centre, near, parts[1]), across + [(i, i ^ 1) for i, _ in from_ends])
     y_near = send(near, other_y)
     c_near = send(near, other_core)
     own_table = tables(keys, cols, block_total, 2 * PPD)
@@ -488,8 +489,7 @@
     perm = flip_matrix(columns)
     far_ends = [outer]
     first = jnp.where(in_centre, first, outer)
-    second = payload_of(at_end, parts[1], second)
-    outer = send(second, around)
+    outer = send(second, around_crossed)
     first, y_own, y_near, c_near, perm, *rest = together(
         first, y_own, y_near, c_near, perm, own_table, far_table, *parts[2:]
     )

time: 196 us -> 205 us (1.046)
  waiting for transfers between devices: 47.7 us -> 67.8 us
  starting transfers between devices: 54.3 us -> 39.3 us
  local copies, waits for them, and re-layouts: 6.46 us -> 10.2 us
    ppermute x26, waiting for transfers between devices: 47.7 us -> 67.8 us  [send(): return lax.ppermute(value, 'tile', pairs)]
    ppermute x26, starting transfers between devices: 54.3 us -> 39.3 us  [send(): return lax.ppermute(value, 'tile', pairs)]
    unnamed x32 -> x42, local copies, waits for them, and re-layouts: 5.18 us -> 9.02 us
  transfers between devices with their start and end apart: 26 -> 26, of which waited for: 11 -> 12; matrix products, arithmetic and copies ran while one was open for 3% -> 4% of each run, Pallas kernels for 40% -> 38%
where the time goes in v22:
time: 205 us
  Pallas kernels  81.1 us (40%)
  waiting for transfers between devices  67.8 us (33%)
  starting transfers between devices  39.3 us (19%)
  local copies, waits for them, and re-layouts  10.2 us (5%)
  other arithmetic  6.11 us (3%)
    ppermute x26, waiting for transfers between devices, send(): return lax.ppermute(value, 'tile', pairs)  67.8 us
    pallas_call x2, Pallas kernels, own_part(): pl.pallas_call(functools.partial(own_kernel, counts, groups, group, not e...  44.1 us
    ppermute x26, starting transfers between devices, send(): return lax.ppermute(value, 'tile', pairs)  39.3 us
    pallas_call x4, Pallas kernels, far_part(): pl.pallas_call(functools.partial(far_kernel, base, total_count, [segment...  20.2 us
    pallas_call x3, Pallas kernels, tables(): pl.pallas_call(tables_kernel, in_specs=[SMEM] * 2, out_specs=SMEM, out_sh...  12.4 us
    unnamed x42, local copies, waits for them, and re-layouts  9.02 us
    pallas_call x1, Pallas kernels, sort_tiles(): pl.pallas_call(functools.partial(sort_kernel, choices), in_specs=[SMEM] *...  4.28 us
  transfers between devices with their start and end apart: 26, of which 12 were waited for; matrix products, arithmetic and copies ran while one was open for 4% of the time, Pallas kernels for 38%

profile of v22, /device:TPU:0, one launch (start us, length us, event | category | flops | bytes accessed | tf_op | source)
XLA Modules:
  0.0 204.9 jit_solution(8199169475485779562)
XLA Ops:
  0.0 0.8 collective-permute-start
  0.9 0.5 collective-permute-start.3
  1.4 5.4 %collective-permute-start.2 = (bf16[4,128,1024]{2,1,0:T(8,128)(2,1)}, bf16[4,128,1024]{2,1,0:T(8,128)(2,1)}, u32[]{:S(2)}, u32[]{:S(2)}) collective-permute-start(bf16[4,128,1024]{2,1,0:T(8,128)(2,1)} %refs_0_.1), channel_id=1, source_target_pairs={{0,4},{1,5},{2,6},{3,7},{4,0},{5,1},{6,2},{7,3},{8,12},{9,13},{10,... | collective-permute-start | bytes 3145736 | tf_op jit(solution)/shard_map/ppermute | solution.py:434
  6.8 1.5 collective-permute-start.4
  8.3 4.1 %tables.3.table = s32[273]{0:T(512)} custom-call(s32[96]{0:T(128)} %rows.1, s32[96]{0:T(128)} %cols.3), custom_call_target="tpu_custom_call" | custom-call | tf_op jit(solution)/shard_map/tables/pallas_call | solution.py:88
  12.4 0.0 copy-start
  12.5 1.9 copy-done
  14.3 0.7 copy-done.9
  15.0 4.3 %sort_tiles.1 = (bf16[4,128,1024]{2,1,0:T(8,128)(2,1)S(1)}, bf16[4,128,1024]{2,1,0:T(8,128)(2,1)S(1)}, bf16[32,128,128]{2,1,0:T(8,128)(2,1)S(1)}, bf16[60,128,12...) custom-call(s32[273]{0:T(512)S(1)} %copy-done.9, ...), custom_call_target="tpu_custom_call" | custom-call | tf_op jit(solution)/shard_map/sort_tiles/pallas_call | solution.py:130
  19.3 0.7 copy-done.12
  20.0 0.1 payload.1
  20.1 1.2 copy-done.10
  21.3 10.0 %collective-permute-start.1 = (bf16[4,128,1024]{2,1,0:T(8,128)(2,1)S(1)}, bf16[4,128,1024]{2,1,0:T(8,128)(2,1)S(1)}, u32[]{:S(2)}, u32[]{:S(2)}) collective-permute-start(bf16[4,128,1024]{2,1,0:T(8,128)(2,1)S(1)} %payload.1), channel_id=1, source_target_pairs={{4,0},{5,1},{6,2},{7,3},{8,12},{9,13},{10,14},{11,15},{0,8},{1,9},... | collective-permute-start | bytes 3145736 | tf_op jit(solution)/shard_map/ppermute | solution.py:434
  31.3 0.1 collective-permute-start.7
  31.4 0.6 fusion.6.rows
  32.0 21.0 %collective-permute-done.7 = s32[2,96]{1,0:T(2,128)S(1)} collective-permute-done((s32[2,96]{1,0:T(2,128)S(1)}, s32[2,96]{1,0:T(2,128)S(1)}, u32[]{:S(2)}, u32[]{:S(2)}) %collective-permute-start.7) | collective-permute-done | bytes 800 | tf_op jit(solution)/shard_map/ppermute | solution.py:434
  52.9 0.5 slice_bitcast_fusion
  53.5 0.1 collective-permute-start.6
  53.6 1.6 collective-permute-start.5
  55.1 1.7 broadcast_select_fusion
  56.8 0.2 collective-permute-start.8
  57.0 4.1 %tables.5.far_table.table = s32[273]{0:T(512)} custom-call(s32[96]{0:T(128)} %get-tuple-element.148.rows, s32[96]{0:T(128)} %get-tuple-element.147.cols), custom_call_target="tpu_custom_call" | custom-call | flops 4000000000 | tf_op jit(solution)/shard_map/tables/pallas_call | solution.py:88
  61.1 4.2 %tables.4.own_table = s32[289]{0:T(512)} custom-call(s32[96]{0:T(128)} %fusion.6.rows, s32[96]{0:T(128)} %cols.3), custom_call_target="tpu_custom_call" | custom-call | tf_op jit(solution)/shard_map/tables/pallas_call | solution.py:88
  65.3 1.7 compare_convert_fusion.perm_ref
  67.0 12.4 %collective-permute-done.5.refs_8_ = bf16[4,128,1024]{2,1,0:T(8,128)(2,1)} collective-permute-done((bf16[4,128,1024]{2,1,0:T(8,128)(2,1)}, bf16[4,128,1024]{2,1,0:T(8,128)(2,1)}, u32[]{:S(2)}, u32[]{:S(2)}) %collective-permute-start.5) | collective-permute-done | bytes 1048608 | tf_op jit(solution)/shard_map/ppermute | solution.py:434
  79.5 6.7 %collective-permute-start.9 = (bf16[4,128,1024]{2,1,0:T(8,128)(2,1)}, bf16[4,128,1024]{2,1,0:T(8,128)(2,1)S(1)}, u32[]{:S(2)}, u32[]{:S(2)}) collective-permute-start(bf16[4,128,1024]{2,1,0:T(8,128)(2,1)} %collective-permute-done.8), channel_id=1, source_target_pairs={{4,0},{5,1},{6,2},{7,3},{8,12},{9,13},{10,14},{11,15},{0,9},{1,8},... | collective-permute-start | bytes 3145736 | tf_op jit(solution)/shard_map/ppermute | solution.py:434
  86.2 1.2 collective-permute-start.12
  87.3 0.5 collective-permute-start.10
  87.9 2.4 %collective-permute-start.16 = (bf16[32,128,128]{2,1,0:T(8,128)(2,1)}, bf16[32,128,128]{2,1,0:T(8,128)(2,1)S(1)}, u32[]{:S(2)}, u32[]{:S(2)}) collective-permute-start(bf16[32,128,128]{2,1,0:T(8,128)(2,1)} %copy-done.11), channel_id=1, source_target_pairs={{0,8},{1,9},{2,10},{3,11},{12,4},{13,5},{14,6},{15,7},{16,24},{17,... | collective-permute-start | bytes 3145736 | tf_op jit(solution)/shard_map/ppermute | solution.py:434
  90.2 19.4 %collective-permute-done.9.refs_1_.refs_0_ = bf16[4,128,1024]{2,1,0:T(8,128)(2,1)S(1)} collective-permute-done((bf16[4,128,1024]{2,1,0:T(8,128)(2,1)}, bf16[4,128,1024]{2,1,0:T(8,128)(2,1)S(1)}, u32[]{:S(2)}, u32[]{:S(2)}) %collective-permute-start.9) | collective-permute-done | bytes 1048608 | tf_op jit(solution)/shard_map/ppermute | solution.py:434
  109.6 1.3 collective-permute-start.25
  110.9 2.1 %slice_select_fusion = (bf16[2,128,1024]{2,1,0:T(8,128)(2,1)S(1)}, bf16[2,128,1024]{2,1,0:T(8,128)(2,1)}) fusion(bf16[4,128,1024]{2,1,0:T(8,128)(2,1)S(1)} %collective-permute-done.9.refs_1_.refs_0_, bf16[4,128,1024]{2,1,0:T(8,128)(2,1)} %collective-permute-done.8, pred[]{:T(512)S(6)} %or.6), kind=kLoop, calls=%fused_computation.3 | loop fusion | flops 524288 | bytes 3145729 | tf_op jit(solution)/shard_map/jit(_where)/select_n | solution.py:504
  113.0 0.2 collective-permute-done.10.refs_10_
  113.2 0.8 copy-done.14
  114.0 0.5 collective-permute-start.14
  114.5 1.5 collective-permute-start.15
  116.0 0.6 stack.89.firsts
  116.7 23.3 %own_part.2 = (f32[16,128,1024]{2,1,0:T(8,128)}, bf16[32,128,1024]{2,1,0:T(8,128)(2,1)}) custom-call(s32[289]{0:T(512)} %tables.4.own_table, s32[273]{0:T(512)} %tables.5.far_table.table, s32[11]{0:T(128)} %stack.89.firsts, bf16[96,128,128]{2,1,0:T(8,128)(2,1)} %tiles_ref.5, bf16[1024,1024]{1,0:T(8,128)(2,1)} %compare_convert_fusion.perm_ref, ...), custom_call_target="tpu_custom_call" | custom-call | tf_op jit(solution)/shard_map/own_part/pallas_call | solution.py:285
  140.0 0.4 collective-permute-done.15.refs_6_
  140.4 0.1 collective-permute-start.21
  140.4 0.4 collective-permute-start.22
  140.9 0.1 collective-permute-start.18
  141.0 0.4 collective-permute-start.19
  141.4 1.1 collective-permute-done.21.refs_7_
  142.5 1.3 collective-permute-start.24
  143.8 0.2 collective-permute-done.22.refs_8_
  144.0 0.1 collective-permute-start.20
  144.1 1.4 collective-permute-done.19.refs_3_
  145.5 0.8 copy-done.5
  146.3 1.3 collective-permute-start.23
  147.6 0.8 copy-done.18
  148.4 1.3 collective-permute-start.17
  149.7 0.1 stack.99.firsts
  149.9 1.1 copy-done.4
  151.0 1.0 copy-done.6
  152.0 20.8 %own_part.3 = (f32[16,128,1024]{2,1,0:T(8,128)S(1)}, bf16[32,128,1024]{2,1,0:T(8,128)(2,1)S(1)}) custom-call(s32[289]{0:T(512)S(1)} %copy-done.8, s32[273]{0:T(512)S(1)} %copy-done.7, s32[9]{0:T(128)S(1)} %stack.99.firsts, bf16[96,128,128]{2,1,0:T(8,128)(2,1)} %tiles_ref.5, bf16[1024,1024]{1,0:T(8,128)(2,1)} %compare_convert_fusion.perm_ref, ...), custom_call_target="tpu_custom_call" | custom-call | tf_op jit(solution)/shard_map/own_part/pallas_call | solution.py:285
  172.8 3.7 %collective-permute-done.25.refs_2_ = bf16[60,128,128]{2,1,0:T(8,128)(2,1)} collective-permute-done((bf16[60,128,128]{2,1,0:T(8,128)(2,1)}, bf16[60,128,128]{2,1,0:T(8,128)(2,1)}, u32[]{:S(2)}, u32[]{:S(2)}) %collective-permute-start.25) | collective-permute-done | bytes 1966112 | tf_op jit(solution)/shard_map/ppermute | solution.py:434
  176.5 9.2 %far_part.4 = (f32[128,1024]{1,0:T(8,128)S(1)}, bf16[16,128,1024]{2,1,0:T(8,128)(2,1)}) custom-call(s32[273]{0:T(512)S(1)} %copy-done.7, s32[1]{0:T(128)} %bitcast.chosen.at_end, bf16[4,128,1024]{2,1,0:T(8,128)(2,1)S(1)} %copy-done.2, bf16[4,128,1024]{2,1,0:T(8,128)(2,1)S(1)} %collective-permute-done.9.refs_1_.refs_0_, ...), custom_call_target="tpu_custom_call" | custom-call | tf_op jit(solution)/shard_map/far_part/pallas_call | solution.py:410
  185.7 6.2 %collective-permute-done.24.refs_2_ = bf16[22,128,128]{2,1,0:T(8,128)(2,1)} collective-permute-done((bf16[22,128,128]{2,1,0:T(8,128)(2,1)}, bf16[22,128,128]{2,1,0:T(8,128)(2,1)}, u32[]{:S(2)}, u32[]{:S(2)}) %collective-permute-start.24) | collective-permute-done | bytes 720928 | tf_op jit(solution)/shard_map/ppermute | solution.py:434
  191.9 4.5 %far_part.5 = (f32[128,1024]{1,0:T(8,128)S(1)}, bf16[16,128,1024]{2,1,0:T(8,128)(2,1)}) custom-call(s32[273]{0:T(512)S(1)} %copy-done.7, s32[1]{0:T(128)} %bitcast.chosen.at_end, bf16[4,128,1024]{2,1,0:T(8,128)(2,1)S(1)} %collective-permute-done.9.refs_1_.refs_0_, ...), custom_call_target="tpu_custom_call", output_to_operand_aliasing={{1}: (8, {})} | custom-call | tf_op jit(solution)/shard_map/far_part/pallas_call | solution.py:410
  196.5 1.0 collective-permute-done.23.refs_1_
  197.5 3.3 %far_part.6 = (f32[128,1024]{1,0:T(8,128)S(1)}, bf16[16,128,1024]{2,1,0:T(8,128)(2,1)}) custom-call(s32[273]{0:T(512)S(1)} %copy-done.7, s32[1]{0:T(128)} %bitcast.chosen.at_end, bf16[32,128,128]{2,1,0:T(8,128)(2,1)S(1)} %collective-permute-done.16.refs_1_.refs_0_, ...), custom_call_target="tpu_custom_call", output_to_operand_aliasing={{1}: (7, {})} | custom-call | tf_op jit(solution)/shard_map/far_part/pallas_call | solution.py:410
  200.8 0.9 collective-permute-done.17.refs_1_
  201.7 3.1 %far_part.7 = (f32[128,1024]{1,0:T(8,128)}, bf16[16,128,1024]{2,1,0:T(8,128)(2,1)}) custom-call(s32[273]{0:T(512)S(1)} %copy-done.7, s32[1]{0:T(128)} %bitcast.chosen.at_end, bf16[32,128,128]{2,1,0:T(8,128)(2,1)S(1)} %collective-permute-done.16.refs_1_.refs_0_, ...), custom_call_target="tpu_custom_call", output_to_operand_aliasing={{1}: (7, {})} | custom-call | tf_op jit(solution)/shard_map/far_part/pallas_call | solution.py:410
  (51 shorter events, 0.1 us)
Async XLA Ops:
  0.0 31.3 %copy-start.19 = (s32[96]{0:T(128)S(1)}, s32[96]{0:T(128)}, u32[]{:S(2)}) copy-start(s32[96]{0:T(128)} %cols.3) | copy-start | bytes 1156
  0.0 31.3 %copy-start.20 = (s32[96]{0:T(128)S(1)}, s32[96]{0:T(128)}, u32[]{:S(2)}) copy-start(s32[96]{0:T(128)} %rows.1) | copy-start | bytes 1156
  0.0 20.0 %collective-permute-start = (bf16[4,128,1024]{2,1,0:T(8,128)(2,1)}, bf16[4,128,1024]{2,1,0:T(8,128)(2,1)S(1)}, u32[]{:S(2)}, u32[]{:S(2)}) collective-permute-start(bf16[4,128,1024]{2,1,0:T(8,128)(2,1)} %refs_0_.1), channel_id=1, source_target_pairs={{4,8},{5,9},{6,10},{7,11},{8,4},{9,5},{10,6},{11,7},{20,24},{21,25... | collective-permute-start | bytes 3145736 | tf_op jit(solution)/shard_map/ppermute | solution.py:434
  0.9 52.6 %collective-permute-start.3 = (bf16[4,128,1024]{2,1,0:T(8,128)(2,1)}, bf16[4,128,1024]{2,1,0:T(8,128)(2,1)}, u32[]{:S(2)}, u32[]{:S(2)}) collective-permute-start(bf16[4,128,1024]{2,1,0:T(8,128)(2,1)} %refs_0_.1), channel_id=1, source_target_pairs={{0,1},{1,0},{2,3},{3,2},{4,5},{5,4},{6,7},{7,6},{8,9},{9,8},{10,11... | collective-permute-start | bytes 3145736 | tf_op jit(solution)/shard_map/ppermute | solution.py:434
  1.4 52.1 %collective-permute-start.2 = (bf16[4,128,1024]{2,1,0:T(8,128)(2,1)}, bf16[4,128,1024]{2,1,0:T(8,128)(2,1)}, u32[]{:S(2)}, u32[]{:S(2)}) collective-permute-start(bf16[4,128,1024]{2,1,0:T(8,128)(2,1)} %refs_0_.1), channel_id=1, source_target_pairs={{0,4},{1,5},{2,6},{3,7},{4,0},{5,1},{6,2},{7,3},{8,12},{9,13},{10,... | collective-permute-start | bytes 3145736 | tf_op jit(solution)/shard_map/ppermute | solution.py:434
  6.8 46.7 %collective-permute-start.4 = (bf16[4,128,1024]{2,1,0:T(8,128)(2,1)}, bf16[4,128,1024]{2,1,0:T(8,128)(2,1)}, u32[]{:S(2)}, u32[]{:S(2)}) collective-permute-start(bf16[4,128,1024]{2,1,0:T(8,128)(2,1)} %refs_0_.1), channel_id=1, source_target_pairs={{0,2},{1,3},{2,0},{3,1},{4,6},{5,7},{6,4},{7,5},{8,10},{9,11},{10,... | collective-permute-start | bytes 3145736 | tf_op jit(solution)/shard_map/ppermute | solution.py:434
  12.4 1.9 copy-start
  14.3 0.7 copy-start.9
  19.3 0.7 copy-start.12
  20.0 1.3 copy-start.10
  20.0 11.3 %copy-start.11 = (bf16[32,128,128]{2,1,0:T(8,128)(2,1)}, bf16[32,128,128]{2,1,0:T(8,128)(2,1)S(1)}, u32[]{:S(2)}) copy-start(bf16[32,128,128]{2,1,0:T(8,128)(2,1)S(1)} %get-tuple-element.123) | copy-start | bytes 3145732
  21.3 33.9 %collective-permute-start.1 = (bf16[4,128,1024]{2,1,0:T(8,128)(2,1)S(1)}, bf16[4,128,1024]{2,1,0:T(8,128)(2,1)S(1)}, u32[]{:S(2)}, u32[]{:S(2)}) collective-permute-start(bf16[4,128,1024]{2,1,0:T(8,128)(2,1)S(1)} %payload.1), channel_id=1, source_target_pairs={{4,0},{5,1},{6,2},{7,3},{8,12},{9,13},{10,14},{11,15},{0,8},{1,9},... | collective-permute-start | bytes 3145736 | tf_op jit(solution)/shard_map/ppermute | solution.py:434
  31.3 21.7 %collective-permute-start.7 = (s32[2,96]{1,0:T(2,128)S(1)}, s32[2,96]{1,0:T(2,128)S(1)}, u32[]{:S(2)}, u32[]{:S(2)}) collective-permute-start(s32[2,96]{1,0:T(2,128)S(1)} %pad_add_fusion), channel_id=1, source_target_pairs={{0,8},{1,9},{2,10},{3,11},{4,12},{5,13},{6,14},{7,15},{8,0},{9,1},... | collective-permute-start | bytes 2312 | tf_op jit(solution)/shard_map/ppermute | solution.py:434
  53.5 13.6 %collective-permute-start.6 = (bf16[4,128,1024]{2,1,0:T(8,128)(2,1)}, bf16[4,128,1024]{2,1,0:T(8,128)(2,1)}, u32[]{:S(2)}, u32[]{:S(2)}) collective-permute-start(bf16[4,128,1024]{2,1,0:T(8,128)(2,1)} %collective-permute-done.2.refs_2_), channel_id=1, source_target_pairs={{0,1},{1,0},{2,3},{3,2},{4,5},{5,4},{6,7},{7,6},{8,9},{9,8},{10,11... | collective-permute-start | bytes 3145736 | tf_op jit(solution)/shard_map/ppermute | solution.py:434
  53.6 25.9 %collective-permute-start.5 = (bf16[4,128,1024]{2,1,0:T(8,128)(2,1)}, bf16[4,128,1024]{2,1,0:T(8,128)(2,1)}, u32[]{:S(2)}, u32[]{:S(2)}) collective-permute-start(bf16[4,128,1024]{2,1,0:T(8,128)(2,1)} %collective-permute-done.2.refs_2_), channel_id=1, source_target_pairs={{0,2},{1,3},{2,0},{3,1},{4,6},{5,7},{6,4},{7,5},{8,10},{9,11},{10,... | collective-permute-start | bytes 3145736 | tf_op jit(solution)/shard_map/ppermute | solution.py:434
  55.1 6.0 %copy-start.1 = (bf16[4,128,1024]{2,1,0:T(8,128)(2,1)}, bf16[4,128,1024]{2,1,0:T(8,128)(2,1)S(1)}, u32[]{:S(2)}) copy-start(bf16[4,128,1024]{2,1,0:T(8,128)(2,1)S(1)} %collective-permute-done.1.refs_0_) | copy-start | bytes 3145732
  56.8 22.6 %collective-permute-start.8 = (bf16[4,128,1024]{2,1,0:T(8,128)(2,1)}, bf16[4,128,1024]{2,1,0:T(8,128)(2,1)}, u32[]{:S(2)}, u32[]{:S(2)}) collective-permute-start(bf16[4,128,1024]{2,1,0:T(8,128)(2,1)} %get-tuple-element.149), channel_id=1, source_target_pairs={{4,8},{5,9},{6,10},{7,11},{8,4},{9,5},{10,6},{11,7},{0,1},{1,0},{2... | collective-permute-start | bytes 3145736 | tf_op jit(solution)/shard_map/ppermute | solution.py:434
  79.4 8.4 %collective-permute-start.11 = (bf16[4,128,1024]{2,1,0:T(8,128)(2,1)}, bf16[4,128,1024]{2,1,0:T(8,128)(2,1)}, u32[]{:S(2)}, u32[]{:S(2)}) collective-permute-start(bf16[4,128,1024]{2,1,0:T(8,128)(2,1)} %get-tuple-element.101.refs_4_), channel_id=1, source_target_pairs={{0,1},{1,0},{2,3},{3,2},{4,5},{5,4},{6,7},{7,6},{8,9},{9,8},{10,11... | collective-permute-start | bytes 3145736 | tf_op jit(solution)/shard_map/ppermute | solution.py:434
  79.5 30.2 %collective-permute-start.9 = (bf16[4,128,1024]{2,1,0:T(8,128)(2,1)}, bf16[4,128,1024]{2,1,0:T(8,128)(2,1)S(1)}, u32[]{:S(2)}, u32[]{:S(2)}) collective-permute-start(bf16[4,128,1024]{2,1,0:T(8,128)(2,1)} %collective-permute-done.8), channel_id=1, source_target_pairs={{4,0},{5,1},{6,2},{7,3},{8,12},{9,13},{10,14},{11,15},{0,9},{1,8},... | collective-permute-start | bytes 3145736 | tf_op jit(solution)/shard_map/ppermute | solution.py:434
  86.2 26.9 %collective-permute-start.12 = (bf16[4,128,1024]{2,1,0:T(8,128)(2,1)}, bf16[4,128,1024]{2,1,0:T(8,128)(2,1)S(1)}, u32[]{:S(2)}, u32[]{:S(2)}) collective-permute-start(bf16[4,128,1024]{2,1,0:T(8,128)(2,1)} %collective-permute-done.4.refs_6_), channel_id=1, source_target_pairs={{0,1},{1,0},{2,3},{3,2},{4,5},{5,4},{6,7},{7,6},{8,9},{9,8},{10,11... | collective-permute-start | bytes 3145736 | tf_op jit(solution)/shard_map/ppermute | solution.py:434
  87.3 25.7 %collective-permute-start.13 = (bf16[4,128,1024]{2,1,0:T(8,128)(2,1)}, bf16[4,128,1024]{2,1,0:T(8,128)(2,1)S(1)}, u32[]{:S(2)}, u32[]{:S(2)}) collective-permute-start(bf16[4,128,1024]{2,1,0:T(8,128)(2,1)} %collective-permute-done.5.refs_8_), channel_id=1, source_target_pairs={{0,1},{1,0},{2,3},{3,2},{4,5},{5,4},{6,7},{7,6},{8,9},{9,8},{10,11... | collective-permute-start | bytes 3145736 | tf_op jit(solution)/shard_map/ppermute | solution.py:434
  87.3 25.9 %collective-permute-start.10 = (bf16[4,128,1024]{2,1,0:T(8,128)(2,1)}, bf16[4,128,1024]{2,1,0:T(8,128)(2,1)}, u32[]{:S(2)}, u32[]{:S(2)}) collective-permute-start(bf16[4,128,1024]{2,1,0:T(8,128)(2,1)} %get-tuple-element.101.refs_4_), channel_id=1, source_target_pairs={{0,2},{1,3},{2,0},{3,1},{4,6},{5,7},{6,4},{7,5},{8,10},{9,11},{10,... | collective-permute-start | bytes 3145736 | tf_op jit(solution)/shard_map/ppermute | solution.py:434
  87.9 52.5 %collective-permute-start.16 = (bf16[32,128,128]{2,1,0:T(8,128)(2,1)}, bf16[32,128,128]{2,1,0:T(8,128)(2,1)S(1)}, u32[]{:S(2)}, u32[]{:S(2)}) collective-permute-start(bf16[32,128,128]{2,1,0:T(8,128)(2,1)} %copy-done.11), channel_id=1, source_target_pairs={{0,8},{1,9},{2,10},{3,11},{12,4},{13,5},{14,6},{15,7},{16,24},{17,... | collective-permute-start | bytes 3145736 | tf_op jit(solution)/shard_map/ppermute | solution.py:434
  109.6 66.9 %collective-permute-start.25 = (bf16[60,128,128]{2,1,0:T(8,128)(2,1)}, bf16[60,128,128]{2,1,0:T(8,128)(2,1)}, u32[]{:S(2)}, u32[]{:S(2)}) collective-permute-start(bf16[60,128,128]{2,1,0:T(8,128)(2,1)} %copy-done.10), channel_id=1, source_target_pairs={{4,12},{5,13},{6,14},{7,15},{8,0},{9,1},{10,2},{11,3},{20,28},{21,... | collective-permute-start | bytes 5898248 | tf_op jit(solution)/shard_map/ppermute | solution.py:434
  113.0 31.0 %copy-start.3 = (bf16[2,128,1024]{2,1,0:T(8,128)(2,1)}, bf16[2,128,1024]{2,1,0:T(8,128)(2,1)S(1)}, u32[]{:S(2)}) copy-start(bf16[2,128,1024]{2,1,0:T(8,128)(2,1)S(1)} %get-tuple-element.128.refs_2_) | copy-start | bytes 1572868
  113.0 1.0 copy-start.14
  113.0 1.5 copy-start.15
  114.0 26.0 %collective-permute-start.14 = (bf16[2,128,1024]{2,1,0:T(8,128)(2,1)}, bf16[2,128,1024]{2,1,0:T(8,128)(2,1)}, u32[]{:S(2)}, u32[]{:S(2)}) collective-permute-start(bf16[2,128,1024]{2,1,0:T(8,128)(2,1)} %get-tuple-element.127.refs_1_), channel_id=1, source_target_pairs={{0,2},{1,3},{2,0},{3,1},{4,6},{5,7},{6,4},{7,5},{8,10},{9,11},{10,... | collective-permute-start | bytes 1572872 | tf_op jit(solution)/shard_map/ppermute | solution.py:434
  114.5 25.8 %collective-permute-start.15 = (bf16[2,128,1024]{2,1,0:T(8,128)(2,1)S(1)}, bf16[2,128,1024]{2,1,0:T(8,128)(2,1)}, u32[]{:S(2)}, u32[]{:S(2)}) collective-permute-start(bf16[2,128,1024]{2,1,0:T(8,128)(2,1)S(1)} %get-tuple-element.128.refs_2_), channel_id=1, source_target_pairs={{0,2},{1,3},{2,0},{3,1},{4,6},{5,7},{6,4},{7,5},{8,10},{9,11},{10,... | collective-permute-start | bytes 1572872 | tf_op jit(solution)/shard_map/ppermute | solution.py:434
  116.6 31.8 %copy-start.13 = (bf16[6,128,128]{2,1,0:T(8,128)(2,1)S(1)}, bf16[6,128,128]{2,1,0:T(8,128)(2,1)}, u32[]{:S(2)}) copy-start(bf16[6,128,128]{2,1,0:T(8,128)(2,1)} %copy-done.12) | copy-start | bytes 589828
  116.6 33.2 %copy-start.7 = (s32[273]{0:T(512)S(1)}, s32[273]{0:T(512)}, u32[]{:S(2)}) copy-start(s32[273]{0:T(512)} %tables.5.far_table.table) | copy-start | bytes 3280
  116.6 33.2 %copy-start.8 = (s32[289]{0:T(512)S(1)}, s32[289]{0:T(512)}, u32[]{:S(2)}) copy-start(s32[289]{0:T(512)} %tables.4.own_table) | copy-start | bytes 3472
  140.4 2.1 %collective-permute-start.21 = (bf16[2,128,1024]{2,1,0:T(8,128)(2,1)}, bf16[2,128,1024]{2,1,0:T(8,128)(2,1)S(1)}, u32[]{:S(2)}, u32[]{:S(2)}) collective-permute-start(bf16[2,128,1024]{2,1,0:T(8,128)(2,1)} %collective-permute-done.14.refs_5_), channel_id=1, source_target_pairs={{0,1},{1,0},{2,3},{3,2},{4,5},{5,4},{6,7},{7,6},{8,9},{9,8},{10,11... | collective-permute-start | bytes 1572872 | tf_op jit(solution)/shard_map/ppermute | solution.py:434
  140.4 3.5 %collective-permute-start.22 = (bf16[2,128,1024]{2,1,0:T(8,128)(2,1)}, bf16[2,128,1024]{2,1,0:T(8,128)(2,1)S(1)}, u32[]{:S(2)}, u32[]{:S(2)}) collective-permute-start(bf16[2,128,1024]{2,1,0:T(8,128)(2,1)} %collective-permute-done.15.refs_6_), channel_id=1, source_target_pairs={{0,1},{1,0},{2,3},{3,2},{4,5},{5,4},{6,7},{7,6},{8,9},{9,8},{10,11... | collective-permute-start | bytes 1572872 | tf_op jit(solution)/shard_map/ppermute | solution.py:434
  140.9 9.0 %collective-permute-start.18 = (bf16[4,128,1024]{2,1,0:T(8,128)(2,1)}, bf16[4,128,1024]{2,1,0:T(8,128)(2,1)}, u32[]{:S(2)}, u32[]{:S(2)}) collective-permute-start(bf16[4,128,1024]{2,1,0:T(8,128)(2,1)} %collective-permute-done.10.refs_10_), channel_id=1, source_target_pairs={{0,1},{1,0},{2,3},{3,2},{4,5},{5,4},{6,7},{7,6},{8,9},{9,8},{10,11... | collective-permute-start | bytes 3145736 | tf_op jit(solution)/shard_map/ppermute | solution.py:434
  141.0 4.5 %collective-permute-start.19 = (bf16[2,128,1024]{2,1,0:T(8,128)(2,1)}, bf16[2,128,1024]{2,1,0:T(8,128)(2,1)S(1)}, u32[]{:S(2)}, u32[]{:S(2)}) collective-permute-start(bf16[2,128,1024]{2,1,0:T(8,128)(2,1)} %get-tuple-element.127.refs_1_), channel_id=1, source_target_pairs={{0,1},{1,0},{2,3},{3,2},{4,5},{5,4},{6,7},{7,6},{8,9},{9,8},{10,11... | collective-permute-start | bytes 1572872 | tf_op jit(solution)/shard_map/ppermute | solution.py:434
  142.5 5.1 %copy-start.16 = (bf16[2,128,1024]{2,1,0:T(8,128)(2,1)}, bf16[2,128,1024]{2,1,0:T(8,128)(2,1)S(1)}, u32[]{:S(2)}) copy-start(bf16[2,128,1024]{2,1,0:T(8,128)(2,1)S(1)} %collective-permute-done.21.refs_7_) | copy-start | bytes 1572868
  142.5 49.5 %collective-permute-start.24 = (bf16[22,128,128]{2,1,0:T(8,128)(2,1)}, bf16[22,128,128]{2,1,0:T(8,128)(2,1)}, u32[]{:S(2)}, u32[]{:S(2)}) collective-permute-start(bf16[22,128,128]{2,1,0:T(8,128)(2,1)} %get-tuple-element.136), channel_id=1, source_target_pairs={{4,12},{5,13},{6,14},{7,15},{8,0},{9,1},{10,2},{11,3},{20,28},{21,... | collective-permute-start | bytes 2162696 | tf_op jit(solution)/shard_map/ppermute | solution.py:434
  144.0 3.6 %copy-start.17 = (bf16[2,128,1024]{2,1,0:T(8,128)(2,1)}, bf16[2,128,1024]{2,1,0:T(8,128)(2,1)S(1)}, u32[]{:S(2)}) copy-start(bf16[2,128,1024]{2,1,0:T(8,128)(2,1)S(1)} %collective-permute-done.22.refs_8_) | copy-start | bytes 1572868
  144.0 3.6 %collective-permute-start.20 = (bf16[2,128,1024]{2,1,0:T(8,128)(2,1)S(1)}, bf16[2,128,1024]{2,1,0:T(8,128)(2,1)S(1)}, u32[]{:S(2)}, u32[]{:S(2)}) collective-permute-start(bf16[2,128,1024]{2,1,0:T(8,128)(2,1)S(1)} %get-tuple-element.128.refs_2_), channel_id=1, source_target_pairs={{0,1},{1,0},{2,3},{3,2},{4,5},{5,4},{6,7},{7,6},{8,9},{9,8},{10,11... | collective-permute-start | bytes 1572872 | tf_op jit(solution)/shard_map/ppermute | solution.py:434
  145.5 0.8 copy-start.5
  146.3 51.2 %collective-permute-start.23 = (bf16[8,128,128]{2,1,0:T(8,128)(2,1)S(1)}, bf16[8,128,128]{2,1,0:T(8,128)(2,1)S(1)}, u32[]{:S(2)}, u32[]{:S(2)}) collective-permute-start(bf16[8,128,128]{2,1,0:T(8,128)(2,1)S(1)} %get-tuple-element.135), channel_id=1, source_target_pairs={{4,12},{5,13},{6,14},{7,15},{8,0},{9,1},{10,2},{11,3},{20,28},{21,... | collective-permute-start | bytes 786440 | tf_op jit(solution)/shard_map/ppermute | solution.py:434
  147.6 0.8 copy-start.18
  148.4 53.3 %collective-permute-start.17 = (bf16[6,128,128]{2,1,0:T(8,128)(2,1)S(1)}, bf16[6,128,128]{2,1,0:T(8,128)(2,1)}, u32[]{:S(2)}, u32[]{:S(2)}) collective-permute-start(bf16[6,128,128]{2,1,0:T(8,128)(2,1)S(1)} %copy-done.13), channel_id=1, source_target_pairs={{4,12},{5,13},{6,14},{7,15},{8,0},{9,1},{10,2},{11,3},{20,28},{21,... | collective-permute-start | bytes 589832 | tf_op jit(solution)/shard_map/ppermute | solution.py:434
  149.8 26.7 %copy-start.2 = (bf16[4,128,1024]{2,1,0:T(8,128)(2,1)S(1)}, bf16[4,128,1024]{2,1,0:T(8,128)(2,1)}, u32[]{:S(2)}) copy-start(bf16[4,128,1024]{2,1,0:T(8,128)(2,1)} %copy-done.1) | copy-start | bytes 3145732
  149.8 1.1 copy-start.4
  151.0 1.0 copy-start.6

commit v23 on v21

--- a/solution.py
+++ b/solution.py
@@ -10,7 +10,7 @@
 W = 32
 PPD = 16
 REUSE = 3
-SHARES = (30, 11, 4)
+SHARES = (60, 23, 8)
 COLUMNS = 256
 MIB = 1024 * 1024
 GRANT = 36
@@ -529,7 +529,7 @@
 
 
 def tile_parts(count):
-    sizes = [count * share // 48 for share in SHARES]
+    sizes = [count * share // 96 for share in SHARES]
     return sizes + [count - sum(sizes)]
 
 

time: 196 us -> 196 us (level)
  no operation moved by 1% of the time
where the time goes in v23:
time: 196 us
  Pallas kernels  82.3 us (42%)
  starting transfers between devices  54.3 us (28%)
  waiting for transfers between devices  47.8 us (24%)
  local copies, waits for them, and re-layouts  6.46 us (3%)
  other arithmetic  4.83 us (2%)
    ppermute x26, starting transfers between devices, send(): return lax.ppermute(value, 'tile', pairs)  54.3 us
    ppermute x26, waiting for transfers between devices, send(): return lax.ppermute(value, 'tile', pairs)  47.8 us
    pallas_call x2, Pallas kernels, own_part(): pl.pallas_call(functools.partial(own_kernel, counts, groups, group, not e...  44.2 us
    pallas_call x4, Pallas kernels, far_part(): pl.pallas_call(functools.partial(far_kernel, base, total_count, [segment...  20.2 us
    pallas_call x3, Pallas kernels, tables(): pl.pallas_call(tables_kernel, in_specs=[SMEM] * 2, out_specs=SMEM, out_sh...  12.4 us
    pallas_call x1, Pallas kernels, sort_tiles(): pl.pallas_call(functools.partial(sort_kernel, choices), in_specs=[SMEM] *...  5.39 us
    unnamed x32, local copies, waits for them, and re-layouts  5.18 us
  transfers between devices with their start and end apart: 26, of which 11 were waited for; matrix products, arithmetic and copies ran while one was open for 3% of the time, Pallas kernels for 40%

profile of v23, /device:TPU:0, one launch (start us, length us, event | category | flops | bytes accessed | tf_op | source)
XLA Modules:
  0.0 196.2 jit_solution(13848285760816949672)
XLA Ops:
  0.0 0.7 collective-permute-start
  0.7 0.5 collective-permute-start.3
  1.2 5.4 %collective-permute-start.2 = (bf16[4,128,1024]{2,1,0:T(8,128)(2,1)}, bf16[4,128,1024]{2,1,0:T(8,128)(2,1)}, u32[]{:S(2)}, u32[]{:S(2)}) collective-permute-start(bf16[4,128,1024]{2,1,0:T(8,128)(2,1)} %refs_0_.1), channel_id=1, source_target_pairs={{0,4},{1,5},{2,6},{3,7},{4,0},{5,1},{6,2},{7,3},{8,12},{9,13},{10,... | collective-permute-start | bytes 3145736 | tf_op jit(solution)/shard_map/ppermute | solution.py:434
  6.7 1.5 collective-permute-start.4
  8.2 0.7 pad_add_fusion
  8.9 4.1 %tables.3.table = s32[273]{0:T(512)} custom-call(s32[96]{0:T(128)} %rows.1, s32[96]{0:T(128)} %cols.3), custom_call_target="tpu_custom_call" | custom-call | tf_op jit(solution)/shard_map/tables/pallas_call | solution.py:88
  13.0 1.2 fusion.6.rows
  14.3 1.9 copy-done
  16.1 0.7 copy-done.7
  16.8 5.4 %sort_tiles.1 = (bf16[4,128,1024]{2,1,0:T(8,128)(2,1)S(1)}, bf16[4,128,1024]{2,1,0:T(8,128)(2,1)S(1)}, bf16[32,128,128]{2,1,0:T(8,128)(2,1)}, bf16[60,128,128]{2...) custom-call(s32[273]{0:T(512)S(1)} %copy-done.7, ...), custom_call_target="tpu_custom_call" | custom-call | tf_op jit(solution)/shard_map/sort_tiles/pallas_call | solution.py:130
  22.2 0.1 payload.2
  22.3 8.8 %collective-permute-start.1 = (bf16[4,128,1024]{2,1,0:T(8,128)(2,1)S(1)}, bf16[4,128,1024]{2,1,0:T(8,128)(2,1)S(1)}, u32[]{:S(2)}, u32[]{:S(2)}) collective-permute-start(bf16[4,128,1024]{2,1,0:T(8,128)(2,1)S(1)} %payload.2), channel_id=1, source_target_pairs={{4,0},{5,1},{6,2},{7,3},{8,12},{9,13},{10,14},{11,15},{0,8},{1,9},... | collective-permute-start | bytes 3145736 | tf_op jit(solution)/shard_map/ppermute | solution.py:434
  31.1 0.5 slice_bitcast_fusion
  31.6 0.0 collective-permute-done.2.refs_2_
  31.6 0.6 collective-permute-done.4.refs_6_
  32.2 0.4 copy-done.9
  32.6 0.7 collective-permute-start.8
  33.4 0.1 collective-permute-start.6
  33.4 1.6 collective-permute-start.5
  35.0 4.1 %tables.5.far_table.table = s32[273]{0:T(512)} custom-call(s32[96]{0:T(128)} %get-tuple-element.148.rows, s32[96]{0:T(128)} %get-tuple-element.147.cols), custom_call_target="tpu_custom_call" | custom-call | flops 4000000000 | tf_op jit(solution)/shard_map/tables/pallas_call | solution.py:88
  39.2 4.2 %tables.4.own_table = s32[289]{0:T(512)} custom-call(s32[96]{0:T(128)} %fusion.6.rows, s32[96]{0:T(128)} %cols.3), custom_call_target="tpu_custom_call" | custom-call | tf_op jit(solution)/shard_map/tables/pallas_call | solution.py:88
  43.4 1.7 compare_convert_fusion.perm_ref
  45.1 8.0 %collective-permute-done.1.refs_0_ = bf16[4,128,1024]{2,1,0:T(8,128)(2,1)S(1)} collective-permute-done((bf16[4,128,1024]{2,1,0:T(8,128)(2,1)S(1)}, bf16[4,128,1024]{2,1,0:T(8,128)(2,1)S(1)}, u32[]{:S(2)}, u32[]{:S(2)}) %collective-permute-start.1) | collective-permute-done | bytes 1048608 | tf_op jit(solution)/shard_map/ppermute | solution.py:434
  53.1 0.1 broadcast_select_fusion.refs_4_
  53.2 0.0 collective-permute-done.6.refs_3_
  53.2 6.1 %collective-permute-done.5.refs_8_ = bf16[4,128,1024]{2,1,0:T(8,128)(2,1)} collective-permute-done((bf16[4,128,1024]{2,1,0:T(8,128)(2,1)}, bf16[4,128,1024]{2,1,0:T(8,128)(2,1)}, u32[]{:S(2)}, u32[]{:S(2)}) %collective-permute-start.5) | collective-permute-done | bytes 1048608 | tf_op jit(solution)/shard_map/ppermute | solution.py:434
  59.3 0.0 collective-permute-start.11
  59.3 0.0 collective-permute-done.8.received
  59.4 0.1 payload.3
  59.5 19.2 %collective-permute-start.9 = (bf16[4,128,1024]{2,1,0:T(8,128)(2,1)S(1)}, bf16[4,128,1024]{2,1,0:T(8,128)(2,1)S(1)}, u32[]{:S(2)}, u32[]{:S(2)}) collective-permute-start(bf16[4,128,1024]{2,1,0:T(8,128)(2,1)S(1)} %payload.3), channel_id=1, source_target_pairs={{4,0},{5,1},{6,2},{7,3},{8,12},{9,13},{10,14},{11,15},{0,8},{1,9},... | collective-permute-start | bytes 3145736 | tf_op jit(solution)/shard_map/ppermute | solution.py:434
  78.7 0.5 collective-permute-start.13
  79.2 1.5 collective-permute-start.10
  80.7 1.3 collective-permute-start.25
  82.0 19.3 %collective-permute-done.9.refs_1_.refs_0_ = bf16[4,128,1024]{2,1,0:T(8,128)(2,1)S(1)} collective-permute-done((bf16[4,128,1024]{2,1,0:T(8,128)(2,1)S(1)}, bf16[4,128,1024]{2,1,0:T(8,128)(2,1)S(1)}, u32[]{:S(2)}, u32[]{:S(2)}) %collective-permute-start.9) | collective-permute-done | bytes 1048608 | tf_op jit(solution)/shard_map/ppermute | solution.py:434
  101.3 5.4 %collective-permute-start.16 = (bf16[32,128,128]{2,1,0:T(8,128)(2,1)}, bf16[32,128,128]{2,1,0:T(8,128)(2,1)S(1)}, u32[]{:S(2)}, u32[]{:S(2)}) collective-permute-start(bf16[32,128,128]{2,1,0:T(8,128)(2,1)} %get-tuple-element.123), channel_id=1, source_target_pairs={{0,8},{1,9},{2,10},{3,11},{12,4},{13,5},{14,6},{15,7},{16,24},{17,... | collective-permute-start | bytes 3145736 | tf_op jit(solution)/shard_map/ppermute | solution.py:434
  106.7 1.1 slice_select_fusion
  107.9 1.0 copy-done.11
  108.8 0.3 copy-done.12
  109.1 1.5 collective-permute-start.14
  110.7 0.5 collective-permute-start.15
  111.2 0.7 stack.89.firsts
  111.8 23.9 %own_part.2 = (f32[16,128,1024]{2,1,0:T(8,128)}, bf16[32,128,1024]{2,1,0:T(8,128)(2,1)}) custom-call(s32[289]{0:T(512)} %tables.4.own_table, s32[273]{0:T(512)} %tables.5.far_table.table, s32[11]{0:T(128)} %stack.89.firsts, bf16[96,128,128]{2,1,0:T(8,128)(2,1)} %tiles_ref.5, bf16[1024,1024]{1,0:T(8,128)(2,1)} %compare_convert_fusion.perm_ref, ...), custom_call_target="tpu_custom_call" | custom-call | tf_op jit(solution)/shard_map/own_part/pallas_call | solution.py:285
  135.8 0.1 collective-permute-start.19
  135.8 0.5 collective-permute-start.20
  136.3 0.1 collective-permute-start.18
  136.4 0.4 collective-permute-start.21
  136.8 1.1 collective-permute-done.19.refs_3_
  137.9 1.3 collective-permute-start.24
  139.2 0.2 collective-permute-done.20.refs_4_
  139.4 0.1 collective-permute-start.22
  139.6 1.4 collective-permute-done.21.refs_7_
  140.9 1.3 collective-permute-start.23
  142.3 0.8 copy-done.15
  143.1 1.3 collective-permute-start.17
  144.4 0.1 stack.99.firsts
  144.5 20.3 %own_part.3 = (f32[16,128,1024]{2,1,0:T(8,128)S(1)}, bf16[32,128,1024]{2,1,0:T(8,128)(2,1)S(1)}) custom-call(s32[289]{0:T(512)S(1)} %copy-done.6, s32[273]{0:T(512)S(1)} %copy-done.5, s32[9]{0:T(128)S(1)} %stack.99.firsts, bf16[96,128,128]{2,1,0:T(8,128)(2,1)} %tiles_ref.5, bf16[1024,1024]{1,0:T(8,128)(2,1)} %compare_convert_fusion.perm_ref, ...), custom_call_target="tpu_custom_call" | custom-call | tf_op jit(solution)/shard_map/own_part/pallas_call | solution.py:285
  164.9 3.0 %collective-permute-done.25.refs_2_ = bf16[60,128,128]{2,1,0:T(8,128)(2,1)} collective-permute-done((bf16[60,128,128]{2,1,0:T(8,128)(2,1)}, bf16[60,128,128]{2,1,0:T(8,128)(2,1)}, u32[]{:S(2)}, u32[]{:S(2)}) %collective-permute-start.25) | collective-permute-done | bytes 1966112 | tf_op jit(solution)/shard_map/ppermute | solution.py:434
  167.9 9.2 %far_part.4 = (f32[128,1024]{1,0:T(8,128)S(1)}, bf16[16,128,1024]{2,1,0:T(8,128)(2,1)}) custom-call(s32[273]{0:T(512)S(1)} %copy-done.5, s32[1]{0:T(128)} %bitcast.chosen.at_end, bf16[4,128,1024]{2,1,0:T(8,128)(2,1)S(1)} %copy-done.2, bf16[4,128,1024]{2,1,0:T(8,128)(2,1)S(1)} %collective-permute-done.9.refs_1_.refs_0_, ...), custom_call_target="tpu_custom_call" | custom-call | tf_op jit(solution)/shard_map/far_part/pallas_call | solution.py:410
  177.1 6.8 %collective-permute-done.24.refs_2_ = bf16[23,128,128]{2,1,0:T(8,128)(2,1)S(1)} collective-permute-done((bf16[23,128,128]{2,1,0:T(8,128)(2,1)}, bf16[23,128,128]{2,1,0:T(8,128)(2,1)S(1)}, u32[]{:S(2)}, u32[]{:S(2)}) %collective-permute-start.24) | collective-permute-done | bytes 753696 | tf_op jit(solution)/shard_map/ppermute | solution.py:434
  183.9 4.4 %far_part.5 = (f32[128,1024]{1,0:T(8,128)S(1)}, bf16[16,128,1024]{2,1,0:T(8,128)(2,1)}) custom-call(s32[273]{0:T(512)S(1)} %copy-done.5, s32[1]{0:T(128)} %bitcast.chosen.at_end, bf16[4,128,1024]{2,1,0:T(8,128)(2,1)S(1)} %collective-permute-done.9.refs_1_.refs_0_, ...), custom_call_target="tpu_custom_call", output_to_operand_aliasing={{1}: (8, {})} | custom-call | tf_op jit(solution)/shard_map/far_part/pallas_call | solution.py:410
  188.4 1.3 collective-permute-done.23.refs_1_
  189.7 3.3 %far_part.6 = (f32[128,1024]{1,0:T(8,128)S(1)}, bf16[16,128,1024]{2,1,0:T(8,128)(2,1)}) custom-call(s32[273]{0:T(512)S(1)} %copy-done.5, s32[1]{0:T(128)} %bitcast.chosen.at_end, bf16[32,128,128]{2,1,0:T(8,128)(2,1)S(1)} %collective-permute-done.16.refs_1_.refs_0_, ...), custom_call_target="tpu_custom_call", output_to_operand_aliasing={{1}: (7, {})} | custom-call | tf_op jit(solution)/shard_map/far_part/pallas_call | solution.py:410
  192.9 0.1 collective-permute-done.17.refs_1_
  193.0 3.2 %far_part.7 = (f32[128,1024]{1,0:T(8,128)}, bf16[16,128,1024]{2,1,0:T(8,128)(2,1)}) custom-call(s32[273]{0:T(512)S(1)} %copy-done.5, s32[1]{0:T(128)} %bitcast.chosen.at_end, bf16[32,128,128]{2,1,0:T(8,128)(2,1)S(1)} %collective-permute-done.16.refs_1_.refs_0_, ...), custom_call_target="tpu_custom_call", output_to_operand_aliasing={{1}: (7, {})} | custom-call | tf_op jit(solution)/shard_map/far_part/pallas_call | solution.py:410
  (42 shorter events, 0.1 us)
Async XLA Ops:
  0.0 22.2 %collective-permute-start = (bf16[4,128,1024]{2,1,0:T(8,128)(2,1)}, bf16[4,128,1024]{2,1,0:T(8,128)(2,1)S(1)}, u32[]{:S(2)}, u32[]{:S(2)}) collective-permute-start(bf16[4,128,1024]{2,1,0:T(8,128)(2,1)} %refs_0_.1), channel_id=1, source_target_pairs={{4,8},{5,9},{6,10},{7,11},{8,4},{9,5},{10,6},{11,7},{20,24},{21,25... | collective-permute-start | bytes 3145736 | tf_op jit(solution)/shard_map/ppermute | solution.py:434
  0.7 30.9 %collective-permute-start.3 = (bf16[4,128,1024]{2,1,0:T(8,128)(2,1)}, bf16[4,128,1024]{2,1,0:T(8,128)(2,1)S(1)}, u32[]{:S(2)}, u32[]{:S(2)}) collective-permute-start(bf16[4,128,1024]{2,1,0:T(8,128)(2,1)} %refs_0_.1), channel_id=1, source_target_pairs={{0,1},{1,0},{2,3},{3,2},{4,5},{5,4},{6,7},{7,6},{8,9},{9,8},{10,11... | collective-permute-start | bytes 3145736 | tf_op jit(solution)/shard_map/ppermute | solution.py:434
  1.2 30.4 %collective-permute-start.2 = (bf16[4,128,1024]{2,1,0:T(8,128)(2,1)}, bf16[4,128,1024]{2,1,0:T(8,128)(2,1)}, u32[]{:S(2)}, u32[]{:S(2)}) collective-permute-start(bf16[4,128,1024]{2,1,0:T(8,128)(2,1)} %refs_0_.1), channel_id=1, source_target_pairs={{0,4},{1,5},{2,6},{3,7},{4,0},{5,1},{6,2},{7,3},{8,12},{9,13},{10,... | collective-permute-start | bytes 3145736 | tf_op jit(solution)/shard_map/ppermute | solution.py:434
  6.7 25.5 %collective-permute-start.4 = (bf16[4,128,1024]{2,1,0:T(8,128)(2,1)}, bf16[4,128,1024]{2,1,0:T(8,128)(2,1)}, u32[]{:S(2)}, u32[]{:S(2)}) collective-permute-start(bf16[4,128,1024]{2,1,0:T(8,128)(2,1)} %refs_0_.1), channel_id=1, source_target_pairs={{0,2},{1,3},{2,0},{3,1},{4,6},{5,7},{6,4},{7,5},{8,10},{9,11},{10,... | collective-permute-start | bytes 3145736 | tf_op jit(solution)/shard_map/ppermute | solution.py:434
  8.9 22.3 %collective-permute-start.7 = (s32[2,96]{1,0:T(2,128)S(1)}, s32[2,96]{1,0:T(2,128)S(1)}, u32[]{:S(2)}, u32[]{:S(2)}) collective-permute-start(s32[2,96]{1,0:T(2,128)S(1)} %pad_add_fusion), channel_id=1, source_target_pairs={{0,8},{1,9},{2,10},{3,11},{4,12},{5,13},{6,14},{7,15},{8,0},{9,1},... | collective-permute-start | bytes 2312 | tf_op jit(solution)/shard_map/ppermute | solution.py:434
  14.3 1.9 copy-start
  16.1 0.7 copy-start.7
  22.2 10.0 %copy-start.3 = (bf16[4,128,1024]{2,1,0:T(8,128)(2,1)}, bf16[4,128,1024]{2,1,0:T(8,128)(2,1)S(1)}, u32[]{:S(2)}) copy-start(bf16[4,128,1024]{2,1,0:T(8,128)(2,1)S(1)} %get-tuple-element.100.tiles_ref) | copy-start | bytes 3145732
  22.3 30.8 %collective-permute-start.1 = (bf16[4,128,1024]{2,1,0:T(8,128)(2,1)S(1)}, bf16[4,128,1024]{2,1,0:T(8,128)(2,1)S(1)}, u32[]{:S(2)}, u32[]{:S(2)}) collective-permute-start(bf16[4,128,1024]{2,1,0:T(8,128)(2,1)S(1)} %payload.2), channel_id=1, source_target_pairs={{4,0},{5,1},{6,2},{7,3},{8,12},{9,13},{10,14},{11,15},{0,8},{1,9},... | collective-permute-start | bytes 3145736 | tf_op jit(solution)/shard_map/ppermute | solution.py:434
  31.6 1.0 copy-start.9
  32.6 26.7 %collective-permute-start.8 = (bf16[4,128,1024]{2,1,0:T(8,128)(2,1)}, bf16[4,128,1024]{2,1,0:T(8,128)(2,1)S(1)}, u32[]{:S(2)}, u32[]{:S(2)}) collective-permute-start(bf16[4,128,1024]{2,1,0:T(8,128)(2,1)} %collective-permute-done.2.refs_2_), channel_id=1, source_target_pairs={{4,8},{5,9},{6,10},{7,11},{8,4},{9,5},{10,6},{11,7},{20,24},{21,25... | collective-permute-start | bytes 3145736 | tf_op jit(solution)/shard_map/ppermute | solution.py:434
  33.4 19.9 %collective-permute-start.6 = (bf16[4,128,1024]{2,1,0:T(8,128)(2,1)}, bf16[4,128,1024]{2,1,0:T(8,128)(2,1)}, u32[]{:S(2)}, u32[]{:S(2)}) collective-permute-start(bf16[4,128,1024]{2,1,0:T(8,128)(2,1)} %collective-permute-done.2.refs_2_), channel_id=1, source_target_pairs={{0,1},{1,0},{2,3},{3,2},{4,5},{5,4},{6,7},{7,6},{8,9},{9,8},{10,11... | collective-permute-start | bytes 3145736 | tf_op jit(solution)/shard_map/ppermute | solution.py:434
  33.4 25.9 %collective-permute-start.5 = (bf16[4,128,1024]{2,1,0:T(8,128)(2,1)}, bf16[4,128,1024]{2,1,0:T(8,128)(2,1)}, u32[]{:S(2)}, u32[]{:S(2)}) collective-permute-start(bf16[4,128,1024]{2,1,0:T(8,128)(2,1)} %collective-permute-done.2.refs_2_), channel_id=1, source_target_pairs={{0,2},{1,3},{2,0},{3,1},{4,6},{5,7},{6,4},{7,5},{8,10},{9,11},{10,... | collective-permute-start | bytes 3145736 | tf_op jit(solution)/shard_map/ppermute | solution.py:434
  43.3 16.0 %copy-start.4 = (bf16[4,128,1024]{2,1,0:T(8,128)(2,1)S(1)}, bf16[4,128,1024]{2,1,0:T(8,128)(2,1)}, u32[]{:S(2)}) copy-start(bf16[4,128,1024]{2,1,0:T(8,128)(2,1)} %copy-done.3) | copy-start | bytes 3145732
  53.1 6.2 %copy-start.1 = (bf16[4,128,1024]{2,1,0:T(8,128)(2,1)}, bf16[4,128,1024]{2,1,0:T(8,128)(2,1)S(1)}, u32[]{:S(2)}) copy-start(bf16[4,128,1024]{2,1,0:T(8,128)(2,1)S(1)} %collective-permute-done.1.refs_0_) | copy-start | bytes 3145732
  53.2 54.6 %copy-start.8 = (bf16[4,128,1024]{2,1,0:T(8,128)(2,1)}, bf16[4,128,1024]{2,1,0:T(8,128)(2,1)S(1)}, u32[]{:S(2)}) copy-start(bf16[4,128,1024]{2,1,0:T(8,128)(2,1)S(1)} %broadcast_select_fusion.refs_4_) | copy-start | bytes 3145732
  59.3 21.4 %collective-permute-start.11 = (bf16[4,128,1024]{2,1,0:T(8,128)(2,1)S(1)}, bf16[4,128,1024]{2,1,0:T(8,128)(2,1)S(1)}, u32[]{:S(2)}, u32[]{:S(2)}) collective-permute-start(bf16[4,128,1024]{2,1,0:T(8,128)(2,1)S(1)} %broadcast_select_fusion.refs_4_), channel_id=1, source_target_pairs={{0,1},{1,0},{2,3},{3,2},{4,5},{5,4},{6,7},{7,6},{8,9},{9,8},{10,11... | collective-permute-start | bytes 3145736 | tf_op jit(solution)/shard_map/ppermute | solution.py:434
  59.5 41.9 %collective-permute-start.9 = (bf16[4,128,1024]{2,1,0:T(8,128)(2,1)S(1)}, bf16[4,128,1024]{2,1,0:T(8,128)(2,1)S(1)}, u32[]{:S(2)}, u32[]{:S(2)}) collective-permute-start(bf16[4,128,1024]{2,1,0:T(8,128)(2,1)S(1)} %payload.3), channel_id=1, source_target_pairs={{4,0},{5,1},{6,2},{7,3},{8,12},{9,13},{10,14},{11,15},{0,8},{1,9},... | collective-permute-start | bytes 3145736 | tf_op jit(solution)/shard_map/ppermute | solution.py:434
  78.7 29.1 %collective-permute-start.12 = (bf16[4,128,1024]{2,1,0:T(8,128)(2,1)}, bf16[4,128,1024]{2,1,0:T(8,128)(2,1)S(1)}, u32[]{:S(2)}, u32[]{:S(2)}) collective-permute-start(bf16[4,128,1024]{2,1,0:T(8,128)(2,1)} %collective-permute-done.4.refs_6_), channel_id=1, source_target_pairs={{0,1},{1,0},{2,3},{3,2},{4,5},{5,4},{6,7},{7,6},{8,9},{9,8},{10,11... | collective-permute-start | bytes 3145736 | tf_op jit(solution)/shard_map/ppermute | solution.py:434
  78.7 29.1 %collective-permute-start.13 = (bf16[4,128,1024]{2,1,0:T(8,128)(2,1)}, bf16[4,128,1024]{2,1,0:T(8,128)(2,1)S(1)}, u32[]{:S(2)}, u32[]{:S(2)}) collective-permute-start(bf16[4,128,1024]{2,1,0:T(8,128)(2,1)} %collective-permute-done.5.refs_8_), channel_id=1, source_target_pairs={{0,1},{1,0},{2,3},{3,2},{4,5},{5,4},{6,7},{7,6},{8,9},{9,8},{10,11... | collective-permute-start | bytes 3145736 | tf_op jit(solution)/shard_map/ppermute | solution.py:434
  79.2 28.7 %collective-permute-start.10 = (bf16[4,128,1024]{2,1,0:T(8,128)(2,1)S(1)}, bf16[4,128,1024]{2,1,0:T(8,128)(2,1)}, u32[]{:S(2)}, u32[]{:S(2)}) collective-permute-start(bf16[4,128,1024]{2,1,0:T(8,128)(2,1)S(1)} %broadcast_select_fusion.refs_4_), channel_id=1, source_target_pairs={{0,2},{1,3},{2,0},{3,1},{4,6},{5,7},{6,4},{7,5},{8,10},{9,11},{10,... | collective-permute-start | bytes 3145736 | tf_op jit(solution)/shard_map/ppermute | solution.py:434
  80.7 1.3 copy-start.10
  80.7 87.2 %collective-permute-start.25 = (bf16[60,128,128]{2,1,0:T(8,128)(2,1)}, bf16[60,128,128]{2,1,0:T(8,128)(2,1)}, u32[]{:S(2)}, u32[]{:S(2)}) collective-permute-start(bf16[60,128,128]{2,1,0:T(8,128)(2,1)} %get-tuple-element.137), channel_id=1, source_target_pairs={{4,12},{5,13},{6,14},{7,15},{8,0},{9,1},{10,2},{11,3},{20,28},{21,... | collective-permute-start | bytes 5898248 | tf_op jit(solution)/shard_map/ppermute | solution.py:434
  101.3 35.1 %collective-permute-start.16 = (bf16[32,128,128]{2,1,0:T(8,128)(2,1)}, bf16[32,128,128]{2,1,0:T(8,128)(2,1)S(1)}, u32[]{:S(2)}, u32[]{:S(2)}) collective-permute-start(bf16[32,128,128]{2,1,0:T(8,128)(2,1)} %get-tuple-element.123), channel_id=1, source_target_pairs={{0,8},{1,9},{2,10},{3,11},{12,4},{13,5},{14,6},{15,7},{16,24},{17,... | collective-permute-start | bytes 3145736 | tf_op jit(solution)/shard_map/ppermute | solution.py:434
  107.8 1.0 copy-start.11
  107.8 1.3 copy-start.12
  109.1 26.6 %collective-permute-start.14 = (bf16[2,128,1024]{2,1,0:T(8,128)(2,1)}, bf16[2,128,1024]{2,1,0:T(8,128)(2,1)}, u32[]{:S(2)}, u32[]{:S(2)}) collective-permute-start(bf16[2,128,1024]{2,1,0:T(8,128)(2,1)} %get-tuple-element.127.refs_1_), channel_id=1, source_target_pairs={{0,2},{1,3},{2,0},{3,1},{4,6},{5,7},{6,4},{7,5},{8,10},{9,11},{10,... | collective-permute-start | bytes 1572872 | tf_op jit(solution)/shard_map/ppermute | solution.py:434
  110.7 25.1 %collective-permute-start.15 = (bf16[2,128,1024]{2,1,0:T(8,128)(2,1)}, bf16[2,128,1024]{2,1,0:T(8,128)(2,1)}, u32[]{:S(2)}, u32[]{:S(2)}) collective-permute-start(bf16[2,128,1024]{2,1,0:T(8,128)(2,1)} %get-tuple-element.128.refs_2_), channel_id=1, source_target_pairs={{0,2},{1,3},{2,0},{3,1},{4,6},{5,7},{6,4},{7,5},{8,10},{9,11},{10,... | collective-permute-start | bytes 1572872 | tf_op jit(solution)/shard_map/ppermute | solution.py:434
  111.8 32.7 %copy-start.5 = (s32[273]{0:T(512)S(1)}, s32[273]{0:T(512)}, u32[]{:S(2)}) copy-start(s32[273]{0:T(512)} %tables.5.far_table.table) | copy-start | bytes 3280
  111.8 32.7 %copy-start.6 = (s32[289]{0:T(512)S(1)}, s32[289]{0:T(512)}, u32[]{:S(2)}) copy-start(s32[289]{0:T(512)} %tables.4.own_table) | copy-start | bytes 3472
  135.8 2.2 %collective-permute-start.19 = (bf16[2,128,1024]{2,1,0:T(8,128)(2,1)}, bf16[2,128,1024]{2,1,0:T(8,128)(2,1)S(1)}, u32[]{:S(2)}, u32[]{:S(2)}) collective-permute-start(bf16[2,128,1024]{2,1,0:T(8,128)(2,1)} %get-tuple-element.127.refs_1_), channel_id=1, source_target_pairs={{0,1},{1,0},{2,3},{3,2},{4,5},{5,4},{6,7},{7,6},{8,9},{9,8},{10,11... | collective-permute-start | bytes 1572872 | tf_op jit(solution)/shard_map/ppermute | solution.py:434
  135.8 3.6 %collective-permute-start.20 = (bf16[2,128,1024]{2,1,0:T(8,128)(2,1)}, bf16[2,128,1024]{2,1,0:T(8,128)(2,1)S(1)}, u32[]{:S(2)}, u32[]{:S(2)}) collective-permute-start(bf16[2,128,1024]{2,1,0:T(8,128)(2,1)} %get-tuple-element.128.refs_2_), channel_id=1, source_target_pairs={{0,1},{1,0},{2,3},{3,2},{4,5},{5,4},{6,7},{7,6},{8,9},{9,8},{10,11... | collective-permute-start | bytes 1572872 | tf_op jit(solution)/shard_map/ppermute | solution.py:434
  136.3 8.2 %collective-permute-start.18 = (bf16[4,128,1024]{2,1,0:T(8,128)(2,1)}, bf16[4,128,1024]{2,1,0:T(8,128)(2,1)}, u32[]{:S(2)}, u32[]{:S(2)}) collective-permute-start(bf16[4,128,1024]{2,1,0:T(8,128)(2,1)} %collective-permute-done.10.refs_10_), channel_id=1, source_target_pairs={{0,1},{1,0},{2,3},{3,2},{4,5},{5,4},{6,7},{7,6},{8,9},{9,8},{10,11... | collective-permute-start | bytes 3145736 | tf_op jit(solution)/shard_map/ppermute | solution.py:434
  136.4 4.5 %collective-permute-start.21 = (bf16[2,128,1024]{2,1,0:T(8,128)(2,1)}, bf16[2,128,1024]{2,1,0:T(8,128)(2,1)S(1)}, u32[]{:S(2)}, u32[]{:S(2)}) collective-permute-start(bf16[2,128,1024]{2,1,0:T(8,128)(2,1)} %collective-permute-done.14.refs_5_), channel_id=1, source_target_pairs={{0,1},{1,0},{2,3},{3,2},{4,5},{5,4},{6,7},{7,6},{8,9},{9,8},{10,11... | collective-permute-start | bytes 1572872 | tf_op jit(solution)/shard_map/ppermute | solution.py:434
  137.9 46.0 %collective-permute-start.24 = (bf16[23,128,128]{2,1,0:T(8,128)(2,1)}, bf16[23,128,128]{2,1,0:T(8,128)(2,1)S(1)}, u32[]{:S(2)}, u32[]{:S(2)}) collective-permute-start(bf16[23,128,128]{2,1,0:T(8,128)(2,1)} %get-tuple-element.136), channel_id=1, source_target_pairs={{4,12},{5,13},{6,14},{7,15},{8,0},{9,1},{10,2},{11,3},{20,28},{21,... | collective-permute-start | bytes 2261000 | tf_op jit(solution)/shard_map/ppermute | solution.py:434
  139.4 2.8 %copy-start.13 = (bf16[2,128,1024]{2,1,0:T(8,128)(2,1)}, bf16[2,128,1024]{2,1,0:T(8,128)(2,1)S(1)}, u32[]{:S(2)}) copy-start(bf16[2,128,1024]{2,1,0:T(8,128)(2,1)S(1)} %collective-permute-done.20.refs_4_) | copy-start | bytes 1572868
  139.4 2.8 %collective-permute-start.22 = (bf16[2,128,1024]{2,1,0:T(8,128)(2,1)}, bf16[2,128,1024]{2,1,0:T(8,128)(2,1)S(1)}, u32[]{:S(2)}, u32[]{:S(2)}) collective-permute-start(bf16[2,128,1024]{2,1,0:T(8,128)(2,1)} %collective-permute-done.15.refs_6_), channel_id=1, source_target_pairs={{0,1},{1,0},{2,3},{3,2},{4,5},{5,4},{6,7},{7,6},{8,9},{9,8},{10,11... | collective-permute-start | bytes 1572872 | tf_op jit(solution)/shard_map/ppermute | solution.py:434
  140.9 1.3 copy-start.14
  140.9 48.7 %collective-permute-start.23 = (bf16[8,128,128]{2,1,0:T(8,128)(2,1)}, bf16[8,128,128]{2,1,0:T(8,128)(2,1)}, u32[]{:S(2)}, u32[]{:S(2)}) collective-permute-start(bf16[8,128,128]{2,1,0:T(8,128)(2,1)} %get-tuple-element.135), channel_id=1, source_target_pairs={{4,12},{5,13},{6,14},{7,15},{8,0},{9,1},{10,2},{11,3},{20,28},{21,... | collective-permute-start | bytes 786440 | tf_op jit(solution)/shard_map/ppermute | solution.py:434
  142.3 0.9 copy-start.15
  143.1 49.9 %collective-permute-start.17 = (bf16[5,128,128]{2,1,0:T(8,128)(2,1)}, bf16[5,128,128]{2,1,0:T(8,128)(2,1)S(1)}, u32[]{:S(2)}, u32[]{:S(2)}) collective-permute-start(bf16[5,128,128]{2,1,0:T(8,128)(2,1)} %get-tuple-element.125), channel_id=1, source_target_pairs={{4,12},{5,13},{6,14},{7,15},{8,0},{9,1},{10,2},{11,3},{20,28},{21,... | collective-permute-start | bytes 491528 | tf_op jit(solution)/shard_map/ppermute | solution.py:434
  144.5 23.4 %copy-start.2 = (bf16[4,128,1024]{2,1,0:T(8,128)(2,1)S(1)}, bf16[4,128,1024]{2,1,0:T(8,128)(2,1)}, u32[]{:S(2)}) copy-start(bf16[4,128,1024]{2,1,0:T(8,128)(2,1)} %copy-done.1) | copy-start | bytes 3145732
